TPU v7x, 32 devices: a whole 2x2x4 slice. The times are simulated.
32 devices in a mesh: dp: 4 (over z), seq: 8 (over y, x, core).
Axes of the slice: x: 2, y: 2, z: 4, core: 2. Of those that a mesh axis runs over, the one named last changes fastest.
Arguments:
- query_tiles: bfloat16 [4, 8, 128, 2048], P('dp', 'seq'), may hold values from -20 to 20
- key_tiles: bfloat16 [4, 8, 128, 2048], P('dp', 'seq'), may hold values from -6 to 6
- value_tiles: bfloat16 [4, 8, 128, 2048], P('dp', 'seq'), may hold values from -6 to 6
- attn_grad: bfloat16 [4, 8, 128, 2048], P('dp', 'seq'), may hold values from -6 to 6
- proj_grad: bfloat16 [4, 8, 128, 3072], P('dp', 'seq'), may hold values from -6 to 6
- neighbour: int32 [4, 8], P('dp'), may hold values from 0 to 7, as said below
Outputs:
- query_grad: bfloat16 [4, 8, 128, 2048], P('dp', 'seq')
- key_grad: bfloat16 [4, 8, 128, 2048], P('dp', 'seq')
- value_grad: bfloat16 [4, 8, 128, 2048], P('dp', 'seq')
- update: float32 [2048, 3072], P('dp', 'seq')
Inputs may be any that keep to these rules, and one draw needn't show every extreme that they name: neighbour[v, t] is t - 1 or t + 1; tile 0 names tile 1, tile 1 names tile 0, tile 8 - 2 names tile 8 - 1 and tile 8 - 1 names tile 8 - 2.
All inputs are finite; a program needn't handle non-finite values.
Results may differ from a plain program's by a relative error of at most 0.024.
Values may be sent and summed in bfloat16 or wider, within the bound.
No kernel may reach another device: no remote copies, remote signals or barrier semaphores. Data moves between devices by JAX's collectives and lax.ppermute only.
A program may use at most 128 MiB of HBM per device.

v0:
```python
import jax
import jax.numpy as jnp
from jax import lax
from jax.sharding import PartitionSpec as P

D = 3072
HEAD_DIM = 128
NS_STEPS = 5


coeff_a = 3.4445
coeff_b = -4.775
coeff_c = 2.0315


def padded(cells, sides, width):
    for axis, dim in sides:
        count = lax.axis_size(axis)
        ends = count - 1
        head = lax.slice_in_dim(cells, 0, width, axis=dim)
        tail = lax.slice_in_dim(cells, cells.shape[dim] - width, cells.shape[dim], axis=dim)
        cells = jnp.concatenate(
            [
                lax.ppermute(tail, axis, [(i, (i + 1) % count) for i in range(ends)]),
                cells,
                lax.ppermute(head, axis, [((i + 1) % count, i) for i in range(ends)]),
            ],
            axis=dim,
        )
    return cells


def partner(value, axis, stride):
    mask = 2**stride
    pairs = [(source, source ^ mask) for source in range(lax.axis_size(axis))]
    return lax.ppermute(value, axis, pairs)


def tile_grads(query_rows, key_own, value_own, key_far, value_far, out_grad):
    tile_rows = query_rows.shape[0]
    width = query_rows.shape[1]
    head_count = width // HEAD_DIM
    score_scale = HEAD_DIM ** (-0.5)
    f32 = jnp.float32
    query_h = query_rows.reshape(tile_rows, head_count, HEAD_DIM)
    keys_all = jnp.concatenate([key_own, key_far], 0).reshape(2 * tile_rows, head_count, HEAD_DIM)
    values_all = jnp.concatenate([value_own, value_far], 0).reshape(
        2 * tile_rows, head_count, HEAD_DIM
    )
    grad_h = out_grad.reshape(tile_rows, head_count, HEAD_DIM)
    scores = jnp.einsum("ihd,jhd->hij", query_h, keys_all, preferred_element_type=f32) * score_scale
    row_max = jnp.max(scores, axis=-1, keepdims=True)
    exp_scores = jnp.exp(scores - row_max)
    weights = exp_scores / jnp.sum(exp_scores, axis=-1, keepdims=True)
    weights_b = weights.astype(jnp.bfloat16)
    attended = jnp.einsum("hij,jhd->ihd", weights_b, values_all, preferred_element_type=f32).astype(
        jnp.bfloat16
    )
    row_delta = jnp.sum(grad_h.astype(f32) * attended.astype(f32), axis=-1).T
    dweights = jnp.einsum("ihd,jhd->hij", grad_h, values_all, preferred_element_type=f32)
    dscore_b = (weights * (dweights - row_delta[:, :, None])).astype(jnp.bfloat16)
    query_grad = (
        jnp.einsum("hij,jhd->ihd", dscore_b, keys_all, preferred_element_type=f32) * score_scale
    )
    key_grad = (
        jnp.einsum("hij,ihd->jhd", dscore_b, query_h, preferred_element_type=f32) * score_scale
    )
    value_grad = jnp.einsum("hij,ihd->jhd", weights_b, grad_h, preferred_element_type=f32)
    key_grad = key_grad.reshape(2 * tile_rows, width)
    value_grad = value_grad.reshape(2 * tile_rows, width)
    return (
        query_grad.reshape(tile_rows, width).astype(jnp.bfloat16),
        key_grad[:tile_rows],
        value_grad[:tile_rows],
        key_grad[tile_rows:].astype(jnp.bfloat16),
        value_grad[tile_rows:].astype(jnp.bfloat16),
        attended.reshape(tile_rows, width),
    )


def orthogonalize(grad_rows):
    row_total = grad_rows.shape[0]
    blocks = grad_rows.reshape(row_total // HEAD_DIM, HEAD_DIM, grad_rows.shape[1])
    frob_norm = jnp.sqrt(jnp.sum(blocks * blocks, axis=(1, 2), keepdims=True)) + 1e-07
    iterate = blocks / frob_norm
    best = lax.Precision.HIGHEST
    for turn in range(NS_STEPS):
        gram_matrix = jnp.einsum("hid,hjd->hij", iterate, iterate, precision=best)
        polynomial = coeff_b * gram_matrix + coeff_c * jnp.einsum(
            "hij,hjk->hik", gram_matrix, gram_matrix, precision=best
        )
        iterate = coeff_a * iterate + jnp.einsum(
            "hij,hjd->hid", polynomial, iterate, precision=best
        )
    return (iterate * (0.2 * D**0.5)).reshape(row_total, grad_rows.shape[1])


def split_by_bit(held, bit_value):
    split = held.reshape((2, held.shape[0] // 2) + held.shape[1:])
    kept = lax.dynamic_index_in_dim(split, bit_value, 0, keepdims=False)
    sent = lax.dynamic_index_in_dim(split, 1 - bit_value, 0, keepdims=False)
    return (kept, sent)


def local(query_tiles, key_tiles, value_tiles, attn_grad, proj_grad, neighbour):
    position = lax.axis_index("seq")
    seq_count = lax.axis_size("seq")
    dp_pos = lax.axis_index("dp")
    dp_count = lax.axis_size("dp")
    dp_bits = dp_count.bit_length() - 1
    parity = dp_pos % 2
    targets = neighbour[0]
    tile_ids = lax.iota(jnp.int32, targets.shape[0])
    my_target = jnp.sum(jnp.where(tile_ids == position, targets, 0))
    go_left = my_target < position
    left_sends = jnp.sum(jnp.where((tile_ids == position - 1) & (targets == position), 1, 0)) > 0
    right_sends = jnp.sum(jnp.where((tile_ids == position + 1) & (targets == position), 1, 0)) > 0
    stacked = jnp.concatenate([key_tiles, value_tiles], 0)
    beside_all = padded(stacked, (("seq", 1),), 1)
    remote = jnp.where(go_left, beside_all[:, 0], beside_all[:, 2])
    results = tile_grads(
        query_tiles[0, 0], key_tiles[0, 0], value_tiles[0, 0], remote[0], remote[1], attn_grad[0, 0]
    )
    query_grad, key_own, value_own, key_far, value_far, attended = results
    outgoing = jnp.stack([key_far, value_far])[:, None]
    incoming = padded(outgoing, (("seq", 1),), 1)
    from_left = jnp.where(left_sends, incoming[:, 0].astype(jnp.float32), 0.0)
    from_right = jnp.where(right_sends, incoming[:, 2].astype(jnp.float32), 0.0)
    key_grad = (key_own + from_left[0] + from_right[0]).astype(jnp.bfloat16)
    value_grad = (value_own + from_left[1] + from_right[1]).astype(jnp.bfloat16)
    grad_rows2d = proj_grad[0, 0]
    half = grad_rows2d.shape[1] // 2
    width = attended.shape[1]
    row_block = width // dp_count
    column_width = half // seq_count
    mine_cols = lax.dynamic_slice_in_dim(grad_rows2d, parity * half, half, 1)
    other_cols = lax.dynamic_slice_in_dim(grad_rows2d, (1 - parity) * half, half, 1)
    partner_att, partner_cols = partner((attended, other_cols), "dp", 0)
    pair_att = jnp.concatenate([attended, partner_att], 0)
    pair_grad = jnp.concatenate([mine_cols, partner_cols], 0)
    contract = (((0,), (0,)), ((), ()))
    pair_full = lax.dot_general(pair_att, pair_grad, contract, preferred_element_type=jnp.float32)
    pair_full = lax.optimization_barrier(pair_full.astype(jnp.bfloat16)).astype(jnp.float32)
    held = pair_full.reshape(dp_count // 2, 2, row_block, half)
    for bit in range(dp_bits - 1, 0, -1):
        kept, sent = split_by_bit(held, dp_pos // 2**bit % 2)
        held = kept + partner(sent.astype(jnp.bfloat16), "dp", bit).astype(sent.dtype)
    flat_rows = held[0].transpose(2, 0, 1).reshape(half, 2 * row_block)
    column_sums = lax.psum_scatter(
        flat_rows.astype(jnp.bfloat16), "seq", scatter_dimension=0, tiled=True
    ).astype(jnp.float32)
    pair_blocks = column_sums.reshape(column_width, 2, row_block).transpose(1, 2, 0)
    own_block = lax.dynamic_index_in_dim(pair_blocks, parity, 0, keepdims=False)
    give_block = lax.dynamic_index_in_dim(pair_blocks, 1 - parity, 0, keepdims=False)
    received = partner(give_block.astype(jnp.bfloat16), "dp", 0).astype(give_block.dtype)
    first_half = jnp.where(parity == 0, own_block, received)
    second_half = jnp.where(parity == 0, received, own_block)
    both = jnp.stack([first_half, second_half], 1)
    whole = (
        lax.all_gather(both.astype(jnp.bfloat16), "seq", axis=2, tiled=True)
        .astype(both.dtype)
        .reshape(row_block, 2 * half)
    )
    result = orthogonalize(whole)
    column_count = result.shape[1] // seq_count
    update = lax.dynamic_slice_in_dim(result, position * column_count, column_count, 1)
    return (query_grad[None, None], key_grad[None, None], value_grad[None, None], update)


def solution(mesh):
    placed = (
        P("dp", "seq", None, None),
        P("dp", "seq", None, None),
        P("dp", "seq", None, None),
        P("dp", "seq", None, None),
        P("dp", "seq", None, None),
        P("dp", None),
    )
    return jax.shard_map(
        local,
        mesh=mesh,
        in_specs=placed,
        out_specs=(
            P("dp", "seq", None, None),
            P("dp", "seq", None, None),
            P("dp", "seq", None, None),
            P("dp", "seq"),
        ),
        check_vma=False,
    )
```

profile of v0, /device:TPU:1, one launch (start us, length us, event | category | flops | bytes accessed | tf_op | source)
XLA Modules:
  0.0 421.8 jit_solution(4491370891504538070)
XLA Ops:
  7.2 1.3 copy.105
  8.5 1.3 copy.103
  9.9 1.1 pad_maximum_fusion
  10.9 4.5 %collective-permute-start = (bf16[2,1,128,2048]{2,3,1,0:T(8,128)(2,1)}, bf16[2,1,128,2048]{2,3,1,0:T(8,128)(2,1)S(1)}, u32[]{:S(2)}, u32[]{:S(2)}) collective-permute-start(bf16[2,1,128,2048]{2,3,1,0:T(8,128)(2,1)} %pad_maximum_fusion), channel_id=1, source_target_pairs={{0,1},{1,2},{2,3},{3,4},{4,5},{5,6},{6,7},{8,9},{9,10},{10,11},{11... | collective-permute-start | bytes 3145736 | tf_op jit(solution)/shard_map/ppermute | solution.py:24
  15.4 1.9 collective-permute-start.1
  17.4 2.0 copy.112
  19.4 1.3 copy.141
  20.8 0.8 fusion.33
  22.5 1.0 copy.110
  23.5 4.0 collective-permute-done
  27.5 13.1 %collective-permute-done.1 = bf16[2,1,128,2048]{2,3,1,0:T(8,128)(2,1)} collective-permute-done((bf16[2,1,128,2048]{2,3,1,0:T(8,128)(2,1)}, bf16[2,1,128,2048]{2,3,1,0:T(8,128)(2,1)}, u32[]{:S(2)}, u32[]{:S(2)}) %collective-permute-start.1) | collective-permute-done | bytes 1048608 | tf_op jit(solution)/shard_map/ppermute | solution.py:26
  41.1 0.4 fusion.26
  41.5 1.9 fusion.43
  43.7 2.5 multiply_reduce_fusion.1
  46.2 1.4 collective-permute-start.4
  47.9 15.1 %collective-permute-done.5 = bf16[128,1536]{1,0:T(8,128)(2,1)S(1)} collective-permute-done((bf16[128,1536]{1,0:T(8,128)(2,1)S(1)}, bf16[128,1536]{1,0:T(8,128)(2,1)S(1)}, u32[]{:S(2)}, u32[]{:S(2)}) %collective-permute-start.5) | collective-permute-done | bytes 393248 | tf_op jit(solution)/shard_map/ppermute | solution.py:36
  63.0 1.8 convolution_convert_fusion
  64.8 1.8 convert.20
  66.6 4.5 %copy-done = f32[2,1,2,512,1536]{4,3,2,0,1:T(8,128)} copy-done((f32[2,1,2,512,1536]{4,3,2,0,1:T(8,128)}, f32[2,1,2,512,1536]{4,3,2,0,1:T(8,128)S(1)}, u32[]{:S(2)}) %copy-start) | copy-done | bytes 12582936
  71.1 2.0 fusion.2
  73.1 1.6 collective-permute-start.6
  74.7 116.1 %collective-permute-done.6 = bf16[1,2,512,1536]{3,2,1,0:T(8,128)(2,1)} collective-permute-done((bf16[1,2,512,1536]{3,2,1,0:T(8,128)(2,1)}, bf16[1,2,512,1536]{3,2,1,0:T(8,128)(2,1)}, u32[]{:S(2)}, u32[]{:S(2)}) %collective-permute-start.6) | collective-permute-done | bytes 3145760 | tf_op jit(solution)/shard_map/ppermute | solution.py:36
  190.8 4.8 %fusion.1 = bf16[1,2,512,1536]{3,2,1,0:T(8,128)(2,1)S(1)} fusion(bf16[1,2,512,1536]{3,2,1,0:T(8,128)(2,1)} %collective-permute-done.6, f32[2,1,2,512,1536]{4,3,2,0,1:T(8,128)} %copy-done, s32[]{:T(128)S(6)} %select_n.101), kind=kLoop, calls=%fused_computation.3 | loop fusion | flops 4718592 | bytes 12582916 | tf_op jit(solution)/shard_map/convert_element_type | solution.py:150
  195.6 2.9 copy.137
  198.7 70.7 %reduce-scatter.2.cloned.1.call-done = bf16[192,1024]{1,0:T(8,128)(2,1)} async-done(((bf16[1536,1024]{1,0:T(8,128)(2,1)}), bf16[192,1024]{1,0:T(8,128)(2,1)}) %reduce-scatter.2.cloned.1.call-update) | async-done | bytes 393232 | tf_op jit(solution)/shard_map/reduce_scatter | solution.py:149
  269.4 1.3 reshape.187
  270.7 0.8 convert_bitcast_fusion
  271.6 1.3 collective-permute-start.7
  272.8 4.6 %collective-permute-done.7 = bf16[512,192]{0,1:T(8,128)(2,1)S(1)} collective-permute-done((bf16[512,192]{0,1:T(8,128)(2,1)S(1)}, bf16[512,192]{0,1:T(8,128)(2,1)S(1)}, u32[]{:S(2)}, u32[]{:S(2)}) %collective-permute-start.7) | collective-permute-done | bytes 196640 | tf_op jit(solution)/shard_map/ppermute | solution.py:36
  277.5 0.8 pad_maximum_fusion.7
  278.3 0.4 convolution_bitcast_fusion
  278.9 2.6 fusion.3
  281.5 0.4 multiply_bitcast_fusion
  282.0 0.5 copy-done.8
  282.6 1.0 copy.122
  283.6 2.1 maximum_bitcast_fusion
  285.7 3.4 collective-permute-start.3
  289.2 2.9 collective-permute-start.2
  293.4 2.1 fusion.9
  295.6 1.0 copy.126
  296.9 26.7 %collective-permute-done.3 = bf16[2,1,128,2048]{2,3,1,0:T(8,128)(2,1)} collective-permute-done((bf16[2,1,128,2048]{2,3,1,0:T(8,128)(2,1)}, bf16[2,1,128,2048]{2,3,1,0:T(8,128)(2,1)}, u32[]{:S(2)}, u32[]{:S(2)}) %collective-permute-start.3) | collective-permute-done | bytes 1048608 | tf_op jit(solution)/shard_map/ppermute | solution.py:26
  323.7 1.4 convert_select_fusion
  325.0 1.4 convert_select_fusion.1
  326.4 0.5 fusion.16
  326.9 1.0 copy.127
  327.9 1.0 copy.128
  328.9 6.6 %reshape.188 = f32[4,128,3072]{1,0,2:T(4,128)} reshape(bf16[512,2,1536]{0,2,1:T(8,128)(2,1)} %all-gather.2.cloned.1.call-done) | data formatting | bytes 9437184 | tf_op jit(solution)/shard_map/reshape;reshape | solution.py:83
  335.5 7.8 %copy.138 = f32[4,128,3072]{2,1,0:T(8,128)} copy(f32[4,128,3072]{1,0,2:T(4,128)} %reshape.188) | data formatting | bytes 12582912 | tf_op jit(solution)/shard_map/reshape;reshape | solution.py:83
  343.3 0.7 multiply_reduce_fusion
  344.2 11.3 %fusion.15 = f32[4,128,128]{2,1,0:T(8,128)S(1)} fusion(f32[4,128,3072]{2,1,0:T(8,128)} %copy.138, f32[4]{0:T(128)S(1)} %sqrt_add_fusion), kind=kOutput, calls=%fused_computation.37 | convolution fusion | flops 2417491968 | bytes 6553616 | tf_op jit(solution)/shard_map/hid,hjd->hij/dot_general | solution.py:88
  355.4 0.4 fusion.14
  355.9 6.0 %multiply_add_fusion.3 = f32[4,128,3072]{2,1,0:T(8,128)S(1)} fusion(f32[4,128,128]{2,1,0:T(8,128)S(1)} %fusion.14, f32[4,128,3072]{2,1,0:T(8,128)S(1)} %bitcast.124, f32[4]{0:T(128)S(1)} %sqrt_add_fusion), kind=kOutput, calls=%fused_computation.8 | convolution fusion | flops 2422210560 | bytes 12845072 | tf_op jit(solution)/shard_map/hij,hjd->hid/dot_general | solution.py:92
  361.9 6.2 %fusion.44 = f32[4,128,128]{2,1,0:T(8,128)S(1)} fusion(f32[4,128,3072]{2,1,0:T(8,128)S(1)} %multiply_add_fusion.3), kind=kOutput, calls=%fused_computation.91 | convolution fusion | flops 2415919104 | bytes 6553600 | tf_op jit(solution)/shard_map/hid,hjd->hij/dot_general | solution.py:88
  368.1 0.4 fusion.13
  368.5 6.1 %multiply_add_fusion.2 = f32[4,128,3072]{2,1,0:T(8,128)S(1)} fusion(f32[4,128,3072]{2,1,0:T(8,128)S(1)} %multiply_add_fusion.3, f32[4,128,128]{2,1,0:T(8,128)S(1)} %fusion.13), kind=kOutput, calls=%fused_computation.7 | convolution fusion | flops 2419064832 | bytes 12845056 | tf_op jit(solution)/shard_map/hij,hjd->hid/dot_general | solution.py:92
  374.6 6.0 %fusion.45 = f32[4,128,128]{2,1,0:T(8,128)S(1)} fusion(f32[4,128,3072]{2,1,0:T(8,128)S(1)} %multiply_add_fusion.2), kind=kOutput, calls=%fused_computation.92 | convolution fusion | flops 2415919104 | bytes 6553600 | tf_op jit(solution)/shard_map/hid,hjd->hij/dot_general | solution.py:88
  380.6 0.4 fusion.12
  381.0 6.1 %multiply_add_fusion.1 = f32[4,128,3072]{2,1,0:T(8,128)S(1)} fusion(f32[4,128,3072]{2,1,0:T(8,128)S(1)} %multiply_add_fusion.2, f32[4,128,128]{2,1,0:T(8,128)S(1)} %fusion.12), kind=kOutput, calls=%fused_computation.6 | convolution fusion | flops 2419064832 | bytes 12845056 | tf_op jit(solution)/shard_map/hij,hjd->hid/dot_general | solution.py:92
  387.1 6.0 %fusion.46 = f32[4,128,128]{2,1,0:T(8,128)S(1)} fusion(f32[4,128,3072]{2,1,0:T(8,128)S(1)} %multiply_add_fusion.1), kind=kOutput, calls=%fused_computation.93 | convolution fusion | flops 2415919104 | bytes 6553600 | tf_op jit(solution)/shard_map/hid,hjd->hij/dot_general | solution.py:88
  393.2 0.4 fusion.11
  393.6 6.1 %multiply_add_fusion = f32[4,128,3072]{2,1,0:T(8,128)S(1)} fusion(f32[4,128,3072]{2,1,0:T(8,128)S(1)} %multiply_add_fusion.1, f32[4,128,128]{2,1,0:T(8,128)S(1)} %fusion.11), kind=kOutput, calls=%fused_computation.5 | convolution fusion | flops 2419064832 | bytes 12845056 | tf_op jit(solution)/shard_map/hij,hjd->hid/dot_general | solution.py:92
  399.7 6.1 %fusion.47 = f32[4,128,128]{2,1,0:T(8,128)S(1)} fusion(f32[4,128,3072]{2,1,0:T(8,128)S(1)} %multiply_add_fusion), kind=kOutput, calls=%fused_computation.94 | convolution fusion | flops 2415919104 | bytes 6553600 | tf_op jit(solution)/shard_map/hid,hjd->hij/dot_general | solution.py:88
  406.2 7.3 %add_multiply_fusion = f32[4,128,3072]{2,1,0:T(8,128)S(1)} fusion(f32[4,128,3072]{2,1,0:T(8,128)S(1)} %multiply_add_fusion, f32[4,128,128]{2,1,0:T(8,128)S(1)} %fusion.10), kind=kOutput, calls=%fused_computation.4 | convolution fusion | flops 2420637696 | bytes 12845056 | tf_op jit(solution)/shard_map/hij,hjd->hid/dot_general | solution.py:92
  413.5 1.0 constant_dynamic-slice_fusion
  (56 shorter events, 2.8 us)
Async XLA Ops:
  7.2 13.6 %copy-start.13 = (s32[1,8]{1,0:T(1,128)S(1)}, s32[1,8]{1,0:T(1,128)}, u32[]{:S(2)}) copy-start(s32[1,8]{1,0:T(1,128)} %param.11) | copy-start | bytes 100
  7.2 262.2 %reduce-scatter.2.cloned.1.call-start = ((), (), s32[]{:S(2)}) async-start(), calls=%async_computation.1 | async-start | bytes 3538944 | tf_op jit(solution)/shard_map/reduce_scatter | solution.py:149
  10.9 16.5 %collective-permute-start = (bf16[2,1,128,2048]{2,3,1,0:T(8,128)(2,1)}, bf16[2,1,128,2048]{2,3,1,0:T(8,128)(2,1)S(1)}, u32[]{:S(2)}, u32[]{:S(2)}) collective-permute-start(bf16[2,1,128,2048]{2,3,1,0:T(8,128)(2,1)} %pad_maximum_fusion), channel_id=1, source_target_pairs={{0,1},{1,2},{2,3},{3,4},{4,5},{5,6},{6,7},{8,9},{9,10},{10,11},{11... | collective-permute-start | bytes 3145736 | tf_op jit(solution)/shard_map/ppermute | solution.py:24
  15.4 25.1 %collective-permute-start.1 = (bf16[2,1,128,2048]{2,3,1,0:T(8,128)(2,1)}, bf16[2,1,128,2048]{2,3,1,0:T(8,128)(2,1)}, u32[]{:S(2)}, u32[]{:S(2)}) collective-permute-start(bf16[2,1,128,2048]{2,3,1,0:T(8,128)(2,1)} %pad_maximum_fusion), channel_id=1, source_target_pairs={{1,0},{2,1},{3,2},{4,3},{5,4},{6,5},{7,6},{9,8},{10,9},{11,10},{12... | collective-permute-start | bytes 3145736 | tf_op jit(solution)/shard_map/ppermute | solution.py:26
  20.8 22.6 %copy-start.2 = (bf16[1,1,128,2048]{2,3,1,0:T(8,128)(2,1)}, bf16[1,1,128,2048]{2,3,1,0:T(8,128)(2,1)S(1)}, u32[]{:S(2)}) copy-start(bf16[1,1,128,2048]{2,3,1,0:T(8,128)(2,1)S(1)} %copy.141) | copy-start | bytes 1572868
  22.5 20.9 %copy-start.5 = (bf16[128,16,128]{2,0,1:T(8,128)(2,1)}, bf16[128,16,128]{2,0,1:T(8,128)(2,1)S(1)}, u32[]{:S(2)}) copy-start(bf16[128,16,128]{2,0,1:T(8,128)(2,1)S(1)} %copy.106) | copy-start | bytes 1572868
  40.7 3.0 copy-start.10
  41.0 5.2 %copy-start.6 = (bf16[128,16,128]{2,0,1:T(8,128)(2,1)}, bf16[128,16,128]{2,0,1:T(8,128)(2,1)S(1)}, u32[]{:S(2)}) copy-start(bf16[128,16,128]{2,0,1:T(8,128)(2,1)S(1)} %copy.107) | copy-start | bytes 1572868
  43.4 4.2 %copy-start.9 = (bf16[1,1,128,3072]{3,2,1,0:T(8,128)(2,1)S(1)}, bf16[1,1,128,3072]{3,2,1,0:T(8,128)(2,1)}, u32[]{:S(2)}) copy-start(bf16[1,1,128,3072]{3,2,1,0:T(8,128)(2,1)} %param.10) | copy-start | bytes 2359300
  43.6 2.6 copy-start.12
  46.2 16.8 %collective-permute-start.4 = (bf16[128,2048]{0,1:T(8,128)(2,1)S(1)}, bf16[128,2048]{0,1:T(8,128)(2,1)S(1)}, u32[]{:S(2)}, u32[]{:S(2)}) collective-permute-start(bf16[128,2048]{0,1:T(8,128)(2,1)S(1)} %bitcast.135), channel_id=1, source_target_pairs={{0,8},{8,0},{16,24},{24,16},{1,9},{9,1},{17,25},{25,17},{2,10},{10... | collective-permute-start | bytes 1572872 | tf_op jit(solution)/shard_map/ppermute | solution.py:36
  47.6 15.3 %collective-permute-start.5 = (bf16[128,1536]{1,0:T(8,128)(2,1)S(1)}, bf16[128,1536]{1,0:T(8,128)(2,1)S(1)}, u32[]{:S(2)}, u32[]{:S(2)}) collective-permute-start(bf16[128,1536]{1,0:T(8,128)(2,1)S(1)} %get-tuple-element.32), channel_id=1, source_target_pairs={{0,8},{8,0},{16,24},{24,16},{1,9},{9,1},{17,25},{25,17},{2,10},{10... | collective-permute-start | bytes 1179656 | tf_op jit(solution)/shard_map/ppermute | solution.py:36
  66.6 4.5 %copy-start = (f32[2,1,2,512,1536]{4,3,2,0,1:T(8,128)}, f32[2,1,2,512,1536]{4,3,2,0,1:T(8,128)S(1)}, u32[]{:S(2)}) copy-start(f32[2,1,2,512,1536]{4,3,2,0,1:T(8,128)S(1)} %convert.20) | copy-start | bytes 37748740
  73.1 117.7 %collective-permute-start.6 = (bf16[1,2,512,1536]{3,2,1,0:T(8,128)(2,1)}, bf16[1,2,512,1536]{3,2,1,0:T(8,128)(2,1)}, u32[]{:S(2)}, u32[]{:S(2)}) collective-permute-start(bf16[1,2,512,1536]{3,2,1,0:T(8,128)(2,1)} %fusion.2), channel_id=1, source_target_pairs={{0,16},{8,24},{16,0},{24,8},{1,17},{9,25},{17,1},{25,9},{2,18},{10... | collective-permute-start | bytes 9437192 | tf_op jit(solution)/shard_map/ppermute | solution.py:36
  198.5 79.8 %copy-start.7 = (f32[16,128,256]{1,2,0:T(8,128)S(1)}, f32[16,128,256]{1,2,0:T(8,128)}, u32[]{:S(2)}) copy-start(f32[16,128,256]{1,2,0:T(8,128)} %get-tuple-element.38) | copy-start | bytes 6291460
  198.5 79.8 %copy-start.11 = (bf16[1,1,128,2048]{2,3,1,0:T(8,128)(2,1)S(1)}, bf16[1,1,128,2048]{2,3,1,0:T(8,128)(2,1)}, u32[]{:S(2)}) copy-start(bf16[1,1,128,2048]{2,3,1,0:T(8,128)(2,1)} %copy.112) | copy-start | bytes 1572868
  198.5 130.4 %all-gather.2.cloned.1.call-start = ((), (), s32[]{:S(2)}) async-start(), calls=%async_computation.2 | async-start | bytes 3538944 | tf_op jit(solution)/shard_map/all_gather | solution.py:160
  271.6 5.8 %collective-permute-start.7 = (bf16[512,192]{0,1:T(8,128)(2,1)S(1)}, bf16[512,192]{0,1:T(8,128)(2,1)S(1)}, u32[]{:S(2)}, u32[]{:S(2)}) collective-permute-start(bf16[512,192]{0,1:T(8,128)(2,1)S(1)} %bitcast.141), channel_id=1, source_target_pairs={{0,8},{8,0},{16,24},{24,16},{1,9},{9,1},{17,25},{25,17},{2,10},{10... | collective-permute-start | bytes 589832 | tf_op jit(solution)/shard_map/ppermute | solution.py:36
  278.8 3.2 copy-start.4
  278.8 2.7 copy-start.3
  281.5 1.0 copy-start.8
  285.7 38.0 %collective-permute-start.3 = (bf16[2,1,128,2048]{2,3,1,0:T(8,128)(2,1)}, bf16[2,1,128,2048]{2,3,1,0:T(8,128)(2,1)}, u32[]{:S(2)}, u32[]{:S(2)}) collective-permute-start(bf16[2,1,128,2048]{2,3,1,0:T(8,128)(2,1)} %maximum_bitcast_fusion), channel_id=1, source_target_pairs={{1,0},{2,1},{3,2},{4,3},{5,4},{6,5},{7,6},{9,8},{10,9},{11,10},{12... | collective-permute-start | bytes 3145736 | tf_op jit(solution)/shard_map/ppermute | solution.py:26
  289.2 35.9 %collective-permute-start.2 = (bf16[2,1,128,2048]{2,3,1,0:T(8,128)(2,1)}, bf16[2,1,128,2048]{2,3,1,0:T(8,128)(2,1)}, u32[]{:S(2)}, u32[]{:S(2)}) collective-permute-start(bf16[2,1,128,2048]{2,3,1,0:T(8,128)(2,1)} %maximum_bitcast_fusion), channel_id=1, source_target_pairs={{0,1},{1,2},{2,3},{3,4},{4,5},{5,6},{6,7},{8,9},{9,10},{10,11},{11... | collective-permute-start | bytes 3145736 | tf_op jit(solution)/shard_map/ppermute | solution.py:24
  293.4 33.0 %slice-start.2 = ((f32[256,16,128]{0,2,1:T(8,128)}), f32[128,16,128]{0,2,1:T(8,128)S(1)}, s32[]{:S(2)}) async-start(f32[256,16,128]{0,2,1:T(8,128)} %copy-done.4), calls=%async_computation.5 | async-start | bytes 2097152 | tf_op jit(solution)/shard_map/slice | solution.py:74
  335.5 7.8 %copy-start.1 = (bf16[512,2,1536]{0,2,1:T(8,128)(2,1)S(1)}, bf16[512,2,1536]{0,2,1:T(8,128)(2,1)}, u32[]{:S(2)}) copy-start(bf16[512,2,1536]{0,2,1:T(8,128)(2,1)} %all-gather.2.cloned.1.call-done) | copy-start | bytes 9437188
  343.3 12.5 %slice-start = ((s8[6291456]{0:T(1024)(128)(4,1)}), s8[4194304]{0:T(1024)(128)(4,1)S(1)}, s32[]{:S(2)}) async-start(s8[6291456]{0:T(1024)(128)(4,1)} %bitcast.123), calls=%async_computation.3 | async-start | bytes 8388608
  344.1 11.7 %slice-start.1 = ((s8[6291456]{0:T(1024)(128)(4,1)}), s8[2097152]{0:T(1024)(128)(4,1)S(1)}, s32[]{:S(2)}) async-start(s8[6291456]{0:T(1024)(128)(4,1)} %bitcast.123), calls=%async_computation.4 | async-start | bytes 4194304
Sparse Core Ops, SparseCore 0:
  198.6 70.7 reduce-scatter.1
  278.4 43.4 all-gather.1
where the time goes:
time: 430 us; the launch traced here: 422 us
  waiting for transfers between devices  250 us (58%)
  matrix products  79.6 us (19%)
  local copies, waits for them, and re-layouts  40.1 us (9%)
  starting transfers between devices  17.5 us (4%)
  other arithmetic  17.4 us (4%)
  between operations  16.9 us (4%)
    ppermute x4, waiting for transfers between devices, partner(): return lax.ppermute(value, axis, pairs)  136 us
    reduce_scatter x1, waiting for transfers between devices, local(): lax.psum_scatter(flat_rows.astype(jnp.bfloat16), 'seq', scatter_dimension...  70.7 us
    ppermute x2, waiting for transfers between devices, padded(): lax.ppermute(head, axis, [((i + 1) % count, i) for i in range(ends)])  39.8 us
    dot_general x5, matrix products, orthogonalize(): gram_matrix = jnp.einsum('hid,hjd->hij', iterate, iterate, precision=best)  35.6 us
    dot_general x5, matrix products, orthogonalize(): jnp.einsum('hij,hjd->hid', polynomial, iterate, precision=best)  31.7 us
    another operation x2, local copies, waits for them, and re-layouts, orthogonalize(): grad_rows.reshape(row_total // HEAD_DIM, HEAD_DIM, grad_rows.shape[1])  14.4 us
    unnamed x39, local copies, waits for them, and re-layouts  12.8 us
  transfers between devices with their start and end apart: 10, of which 7 were waited for; matrix products, arithmetic and copies ran while one was open for 5% of the time, Pallas kernels for 0%

commit v1 on v0

v1 whole, which is shorter than its diff:
```python
import functools

import jax
import jax.numpy as jnp
from jax import lax
from jax.experimental import pallas as pl
from jax.experimental.pallas import tpu as pltpu
from jax.sharding import PartitionSpec as P

HEAD_DIM = 128
NS_STEPS = 5
SCALE = HEAD_DIM ** (-0.5)
coeff_a = 3.4445
coeff_b = -4.775
coeff_c = 2.0315
f32 = jnp.float32
bf16 = jnp.bfloat16
VMEM_LIMIT = 48 * 1024 * 1024


def whole(count):
    return [pl.BlockSpec(memory_space=pltpu.VMEM)] * count


def smem():
    return pl.BlockSpec(memory_space=pltpu.SMEM)


def params():
    return pltpu.CompilerParams(vmem_limit_bytes=VMEM_LIMIT)


def cost(flops, moved, exps=0):
    return pl.CostEstimate(flops=int(flops), bytes_accessed=int(moved), transcendentals=int(exps))


def dot_t(a, b):
    return lax.dot_general(a, b, (((1,), (1,)), ((), ())), preferred_element_type=f32)


def dot_n(a, b):
    return lax.dot_general(a, b, (((1,), (0,)), ((), ())), preferred_element_type=f32)


def dot_l(a, b):
    return lax.dot_general(a, b, (((0,), (0,)), ((), ())), preferred_element_type=f32)


def exact(a, b, dims=((1,), (0,))):
    return lax.dot_general(
        a, b, (dims, ((), ())), precision=lax.Precision.HIGHEST, preferred_element_type=f32
    )


class Plan:
    def __init__(self, head_count):
        self.seq = lax.axis_size("seq")
        self.dp = lax.axis_size("dp")
        self.per_target = head_count // self.dp
        self.low = 2
        self.high = self.per_target // 2
        self.col = self.seq // self.per_target
        self.col_bits = self.col.bit_length() - 1

    def row_part(self, place):
        return (place >> (1 + self.col_bits)) * 2 + (place & 1)

    def row_mask(self, part):
        return ((part >> 1) << (1 + self.col_bits)) | (part & 1)

    def col_part(self, place):
        return (place >> 1) & (self.col - 1)

    def high_part(self, place):
        return place >> (1 + self.col_bits)

    def split_place(self, place):
        return place & 1, self.col_part(place), self.high_part(place)


def shift(value, axis, mask):
    return lax.ppermute(value, axis, [(i, i ^ mask) for i in range(lax.axis_size(axis))])


def head_slice(index):
    return pl.ds(pl.multiple_of(index * HEAD_DIM, HEAD_DIM), HEAD_DIM)


def softmax_pair(query, key_own, key_far):
    s_own = dot_t(query, key_own) * SCALE
    s_far = dot_t(query, key_far) * SCALE
    top = jnp.max(jnp.maximum(s_own, s_far), axis=-1, keepdims=True)
    e_own = jnp.exp(s_own - top)
    e_far = jnp.exp(s_far - top)
    inverse = 1.0 / jnp.sum(e_own + e_far, axis=-1, keepdims=True)
    return e_own * inverse, e_far * inverse


def forward_kernel(plan, near_ref, q, ko, vo, kl, vl, kr, vr, *outs):
    place = lax.axis_index("seq")
    layer = lax.axis_index("dp")
    go_left = near_ref[0, place] < place
    mine = plan.row_part(place)
    for j in range(plan.per_target):
        for i in range(plan.dp):
            at = head_slice((layer ^ i) * plan.per_target + (mine ^ j))
            key_far = jnp.where(go_left, kl[:, at], kr[:, at])
            value_far = jnp.where(go_left, vl[:, at], vr[:, at])
            p_own, p_far = softmax_pair(q[:, at], ko[:, at], key_far)
            att = dot_n(p_own.astype(bf16), vo[:, at]) + dot_n(p_far.astype(bf16), value_far)
            outs[j][:, i * HEAD_DIM : (i + 1) * HEAD_DIM] = att.astype(bf16)


def backward_kernel(near_ref, q, ko, vo, kl, vl, kr, vr, g, dq, dko, dvo, dkf, dvf):
    place = lax.axis_index("seq")
    go_left = near_ref[0, place] < place
    for h in range(q.shape[1] // HEAD_DIM):
        at = slice(h * HEAD_DIM, (h + 1) * HEAD_DIM)
        query, key_own, value_own, grad = q[:, at], ko[:, at], vo[:, at], g[:, at]
        key_far = jnp.where(go_left, kl[:, at], kr[:, at])
        value_far = jnp.where(go_left, vl[:, at], vr[:, at])
        p_own, p_far = softmax_pair(query, key_own, key_far)
        pb_own = p_own.astype(bf16)
        pb_far = p_far.astype(bf16)
        att = (dot_n(pb_own, value_own) + dot_n(pb_far, value_far)).astype(bf16)
        delta = jnp.sum(grad.astype(f32) * att.astype(f32), axis=-1, keepdims=True)
        ds_own = (p_own * (dot_t(grad, value_own) - delta)).astype(bf16)
        ds_far = (p_far * (dot_t(grad, value_far) - delta)).astype(bf16)
        dq[:, at] = ((dot_n(ds_own, key_own) + dot_n(ds_far, key_far)) * SCALE).astype(bf16)
        dko[:, at] = dot_l(ds_own, query) * SCALE
        dvo[:, at] = dot_l(pb_own, grad)
        dkf[:, at] = (dot_l(ds_far, query) * SCALE).astype(bf16)
        dvf[:, at] = dot_l(pb_far, grad).astype(bf16)


def combine_kernel(near_ref, dko, dvo, kl, vl, kr, vr, dk, dv):
    place = lax.axis_index("seq")
    last = lax.axis_size("seq") - 1
    before = near_ref[0, jnp.maximum(place - 1, 0)]
    after = near_ref[0, jnp.minimum(place + 1, last)]
    from_left = (place > 0) & (before == place)
    from_right = (place < last) & (after == place)
    for own, left, right, out in ((dko, kl, kr, dk), (dvo, vl, vr, dv)):
        total = own[...] + jnp.where(from_left, left[...].astype(f32), 0.0)
        out[...] = (total + jnp.where(from_right, right[...].astype(f32), 0.0)).astype(bf16)


def product_kernel(plan, *refs):
    att = refs[: plan.seq]
    cols = refs[plan.seq : plan.seq + 2]
    own = refs[plan.seq + 2]
    outs = refs[plan.seq + 3 : plan.seq + 2 + plan.dp]
    turned = refs[plan.seq + 2 + plan.dp :]
    for k in range(plan.seq):
        core, q, high = plan.split_place(k)
        t = high * plan.col + q
        turned[core][:, t * HEAD_DIM : (t + 1) * HEAD_DIM] = att[k][...].T
    tokens = turned[0].shape[1]
    width = own.shape[1]
    step = 512 if width % 512 == 0 else width
    for i in range(plan.dp):
        rows = slice(i * HEAD_DIM, (i + 1) * HEAD_DIM)
        for c in range(0, width, step):
            total = None
            for core in range(2):
                block = cols[core][:, :, :, c : c + step].reshape(tokens, step)
                part = dot_n(turned[core][rows, :], block)
                total = part if total is None else total + part
            if i == 0:
                own[:, c : c + step] = total
            else:
                outs[i - 1][:, c : c + step] = total.astype(bf16)


def gram_kernel(own, *refs):
    *parts, x, gram = refs
    total = own[...]
    for part in parts:
        total = total + part[...].astype(f32)
    x[...] = total
    gram[...] = exact(total, total, ((1,), (1,)))


def polynomial(gram):
    eye = (
        lax.broadcasted_iota(jnp.int32, gram.shape, 0)
        == lax.broadcasted_iota(jnp.int32, gram.shape, 1)
    ).astype(f32)
    square = jnp.sum(jnp.sum(gram * eye, axis=1, keepdims=True), axis=0, keepdims=True)
    inverse = 1.0 / (jnp.sqrt(square) + 1e-07)
    a = gram * inverse * inverse
    p = None
    for turn in range(NS_STEPS):
        q = coeff_a * eye + coeff_b * a + coeff_c * exact(a, a)
        p = q if p is None else exact(q, p)
        if turn + 1 < NS_STEPS:
            a = exact(exact(q, a), q)
    return p, inverse


def update_kernel(plan, factor, x, gram, gram_other, *outs):
    mine = plan.row_part(lax.axis_index("seq"))
    p, inverse = polynomial(gram[...] + gram_other[...])
    p = p * (inverse * factor)
    width = outs[0].shape[1]
    for j in range(plan.per_target):
        if width % HEAD_DIM == 0:
            block = x[:, pl.ds(pl.multiple_of((mine ^ j) * width, width), width)]
        else:
            block = jnp.zeros((HEAD_DIM, width), f32)
            for r in range(plan.per_target):
                part = x[:, r * width : (r + 1) * width]
                block = jnp.where((mine ^ j) == r, part, block)
        outs[j][...] = exact(p, block).astype(outs[j].dtype)


def place_kernel(plan, *refs):
    *parts, out = refs
    mine = plan.row_part(lax.axis_index("seq"))
    for j, part in enumerate(parts):
        at = pl.ds(pl.multiple_of((mine ^ j) * HEAD_DIM, HEAD_DIM), HEAD_DIM)
        out[at, :] = part[...].astype(f32)


def local(query_tiles, key_tiles, value_tiles, attn_grad, proj_grad, neighbour):
    tile, width = query_tiles.shape[2:]
    depth = proj_grad.shape[3]
    head_count = width // HEAD_DIM
    plan = Plan(head_count)
    n, m, per = plan.seq, plan.dp, plan.per_target
    place = lax.axis_index("seq")
    struct = jax.ShapeDtypeStruct
    query, key, value, grad = (
        a.reshape(tile, width) for a in (query_tiles, key_tiles, value_tiles, attn_grad)
    )

    to_right = [(i, i + 1) for i in range(n - 1) if i + 1 != n - 2]
    to_left = [(i + 1, i) for i in range(n - 1) if i != 1]
    key_left = lax.ppermute(key, "seq", to_right)
    key_right = lax.ppermute(key, "seq", to_left)
    value_left = lax.ppermute(value, "seq", to_right)
    value_right = lax.ppermute(value, "seq", to_left)

    slot = depth // n
    view = proj_grad.reshape(tile, plan.high, plan.col, 2, slot)
    mine = plan.col_part(place)
    columns = [lax.dynamic_index_in_dim(view, mine, 2, keepdims=False).reshape(tile, per * slot)]
    for q in range(1, plan.col):
        give = lax.dynamic_index_in_dim(view, mine ^ q, 2, keepdims=False)
        columns.append(shift(give.reshape(tile, per * slot), "seq", q << 1))
    held = jnp.stack(columns)[None]
    bit = 1
    while bit < plan.high:
        other = shift(held, "seq", bit << (1 + plan.col_bits))
        held = jnp.concatenate([held, other], 0)
        bit *= 2
    held_other = shift(held, "seq", 1)

    attended = pl.pallas_call(
        functools.partial(forward_kernel, plan),
        out_shape=[struct((tile, m * HEAD_DIM), bf16)] * per,
        in_specs=[smem()] + whole(7),
        out_specs=whole(per),
        compiler_params=params(),
        cost_estimate=cost(8 * tile * tile * width, 16 * tile * width, 2 * tile * tile * head_count),
        name="attention_forward",
    )(neighbour, query, key, value, key_left, value_left, key_right, value_right)

    rows = [attended[0]] + [shift(attended[plan.row_part(k)], "seq", k) for k in range(1, n)]

    dq, dko, dvo, dkf, dvf = pl.pallas_call(
        backward_kernel,
        out_shape=[
            struct((tile, width), bf16),
            struct((tile, width), f32),
            struct((tile, width), f32),
            struct((tile, width), bf16),
            struct((tile, width), bf16),
        ],
        in_specs=[smem()] + whole(8),
        out_specs=whole(5),
        compiler_params=params(),
        cost_estimate=cost(28 * tile * tile * width, 30 * tile * width, 2 * tile * tile * head_count),
        name="attention_backward",
    )(neighbour, query, key, value, key_left, value_left, key_right, value_right, grad)

    mine_width = per * slot
    own, *sent = pl.pallas_call(
        functools.partial(product_kernel, plan),
        out_shape=[struct((HEAD_DIM, mine_width), f32)]
        + [struct((HEAD_DIM, mine_width), bf16)] * (m - 1),
        in_specs=whole(n + 2),
        out_specs=whole(m),
        scratch_shapes=[pltpu.VMEM((m * HEAD_DIM, n // 2 * tile), bf16)] * 2,
        compiler_params=params(),
        cost_estimate=cost(
            2 * m * HEAD_DIM * n * tile * mine_width, 2 * n * tile * (mine_width + m * HEAD_DIM)
        ),
        name="gradient_product",
    )(*rows, held, held_other)

    came = [shift(part, "dp", i + 1) for i, part in enumerate(sent)]
    x, gram = pl.pallas_call(
        gram_kernel,
        out_shape=[struct((HEAD_DIM, mine_width), f32), struct((HEAD_DIM, HEAD_DIM), f32)],
        in_specs=whole(m),
        out_specs=whole(2),
        compiler_params=params(),
        cost_estimate=cost(12 * HEAD_DIM * HEAD_DIM * mine_width, 14 * HEAD_DIM * mine_width),
        name="gradient_sum",
    )(own, *came)

    gram_other = jnp.zeros_like(gram)
    for b in range(plan.col_bits):
        gram = gram + gram_other
        gram_other = shift(gram, "seq", 2 << b)

    factor = 0.2 * depth**0.5
    pieces = pl.pallas_call(
        functools.partial(update_kernel, plan, factor),
        out_shape=[struct((HEAD_DIM, slot), f32)] + [struct((HEAD_DIM, slot), bf16)] * (per - 1),
        in_specs=whole(3),
        out_specs=whole(per),
        compiler_params=params(),
        cost_estimate=cost(12 * HEAD_DIM * HEAD_DIM * mine_width, 8 * HEAD_DIM * mine_width),
        name="newton_schulz",
    )(x, gram, gram_other)
    pieces = [pieces[0]] + [
        shift(pieces[j], "seq", plan.row_mask(j)) for j in range(1, per)
    ]
    update = pl.pallas_call(
        functools.partial(place_kernel, plan),
        out_shape=struct((per * HEAD_DIM, slot), f32),
        in_specs=whole(per),
        out_specs=pl.BlockSpec(memory_space=pltpu.VMEM),
        compiler_params=params(),
        cost_estimate=cost(1, 8 * per * HEAD_DIM * slot),
        name="update_rows",
    )(*pieces)

    far_right = [(i, i + 1) for i in range(n - 1) if i != 1]
    far_left = [(i + 1, i) for i in range(n - 1) if i + 1 != n - 2]
    far = [lax.ppermute(a, "seq", p) for p in (far_right, far_left) for a in (dkf, dvf)]
    dk, dv = pl.pallas_call(
        combine_kernel,
        out_shape=[struct((tile, width), bf16)] * 2,
        in_specs=[smem()] + whole(6),
        out_specs=whole(2),
        compiler_params=params(),
        cost_estimate=cost(6 * tile * width, 20 * tile * width),
        name="key_value_sum",
    )(neighbour, dko, dvo, far[0], far[1], far[2], far[3])

    shape = query_tiles.shape
    return dq.reshape(shape), dk.reshape(shape), dv.reshape(shape), update


def solution(mesh):
    tiles = P("dp", "seq", None, None)
    return jax.shard_map(
        local,
        mesh=mesh,
        in_specs=(tiles, tiles, tiles, tiles, tiles, P("dp", None)),
        out_specs=(tiles, tiles, tiles, P("dp", "seq")),
        check_vma=False,
    )
```

time: 430 us -> 140 us (0.33); the launches traced: 422 us -> 140 us
  waiting for transfers between devices: 250 us -> 54.3 us
  matrix products: 79.6 us -> 0 us
  local copies, waits for them, and re-layouts: 40.1 us -> 3.65 us
  starting transfers between devices: 17.5 us -> 53.3 us
  Pallas kernels: 0 us -> 27.6 us
  other arithmetic: 17.4 us -> 0.22 us
  between operations: 16.9 us -> 0.9 us
    ppermute x8 -> x25, waiting for transfers between devices: 180 us -> 54.3 us  [the longest x17 48.4 us: shift(): lax.ppermute(value, axis, [(i, i ^ mask) for i in range(lax.axis_size(axi...]
    dot_general x22 -> x0, matrix products: 79.6 us -> none  [the longest x5 35.6 us: orthogonalize(): gram_matrix = jnp.einsum('hid,hjd->hij', iterate, iterate, precision=best)]
    reduce_scatter x1 -> x0, waiting for transfers between devices: 70.7 us -> none  [local(): lax.psum_scatter(flat_rows.astype(jnp.bfloat16), 'seq', scatter_dimension...]
    ppermute x8 -> x25, starting transfers between devices: 17.3 us -> 53.3 us  [the longest x17 35.8 us: shift(): lax.ppermute(value, axis, [(i, i ^ mask) for i in range(lax.axis_size(axi...]
    pallas_call x0 -> x7, Pallas kernels: none -> 27.6 us  [the longest x1 12 us: local(): pl.pallas_call(backward_kernel, out_shape=[struct((tile, width), bf16), s...]
    another operation x3 -> x1, local copies, waits for them, and re-layouts: 15.7 us -> 0.25 us  [local(): held = jnp.stack(columns)[None]]
    unnamed x39 -> x15, local copies, waits for them, and re-layouts: 12.8 us -> 0.59 us
    convert_element_type x3 -> x0, local copies, waits for them, and re-layouts: 5.76 us -> none  [the longest x1 2.91 us: local(): flat_rows.astype(jnp.bfloat16)]
  transfers between devices with their start and end apart: 10 -> 25, of which waited for: 7 -> 11; matrix products, arithmetic and copies ran while one was open for 5% -> 0% of each run, Pallas kernels for 0% -> 18%
where the time goes in v1:
time: 140 us
  waiting for transfers between devices  54.3 us (39%)
  starting transfers between devices  53.3 us (38%)
  Pallas kernels  27.6 us (20%)
  local copies, waits for them, and re-layouts  3.65 us (3%)
    ppermute x17, waiting for transfers between devices, shift(): lax.ppermute(value, axis, [(i, i ^ mask) for i in range(lax.axis_size(axi...  48.4 us
    ppermute x17, starting transfers between devices, shift(): lax.ppermute(value, axis, [(i, i ^ mask) for i in range(lax.axis_size(axi...  35.8 us
    pallas_call x1, Pallas kernels, local(): pl.pallas_call(backward_kernel, out_shape=[struct((tile, width), bf16), s...  12 us
    ppermute x4, starting transfers between devices, local(): lax.ppermute(a, 'seq', p)  8.62 us
    pallas_call x1, Pallas kernels, local(): pl.pallas_call(functools.partial(forward_kernel, plan), out_shape=[struct...  6.18 us
    ppermute x1, waiting for transfers between devices, local(): value_left = lax.ppermute(value, 'seq', to_right)  5.62 us
    pallas_call x1, Pallas kernels, local(): pl.pallas_call(functools.partial(update_kernel, plan, factor), out_shape=...  3.95 us
    ppermute x1, starting transfers between devices, local(): key_left = lax.ppermute(key, 'seq', to_right)  2.96 us
  transfers between devices with their start and end apart: 25, of which 11 were waited for; matrix products, arithmetic and copies ran while one was open for 0% of the time, Pallas kernels for 18%

profile of v1, /device:TPU:1, one launch (start us, length us, event | category | flops | bytes accessed | tf_op | source)
XLA Modules:
  0.0 139.9 jit_solution(2955500650899565168)
XLA Ops:
  0.6 2.6 %reshape.44 = bf16[128,2,2,2,384]{4,3,2,1,0:T(2,128)(2,1)S(1)} reshape(bf16[1,1,128,3072]{3,2,1,0:T(8,128)(2,1)} %param.10) | data formatting | bytes 1572864 | tf_op jit(solution)/shard_map/reshape | solution.py:245
  3.2 0.6 dynamic-slice_bitcast_fusion.1
  3.8 0.2 reshape.45
  4.0 2.1 %collective-permute-start.15 = (bf16[128,1536]{1,0:T(8,128)(2,1)S(1)}, bf16[128,1536]{1,0:T(8,128)(2,1)S(1)}, u32[]{:S(2)}, u32[]{:S(2)}) collective-permute-start(bf16[128,1536]{1,0:T(8,128)(2,1)S(1)} %reshape.45), channel_id=1, source_target_pairs={{0,2},{1,3},{2,0},{3,1},{4,6},{5,7},{6,4},{7,5},{8,10},{9,11},{10,... | collective-permute-start | bytes 1179656 | tf_op jit(solution)/shard_map/ppermute | solution.py:82
  6.1 0.2 stack_reshape.3
  6.4 8.6 %collective-permute-done.15 = bf16[128,1536]{1,0:T(8,128)(2,1)S(1)} collective-permute-done((bf16[128,1536]{1,0:T(8,128)(2,1)S(1)}, bf16[128,1536]{1,0:T(8,128)(2,1)S(1)}, u32[]{:S(2)}, u32[]{:S(2)}) %collective-permute-start.15) | collective-permute-done | bytes 393248 | tf_op jit(solution)/shard_map/ppermute | solution.py:82
  15.0 0.1 maximum_bitcast_fusion
  15.1 0.0 copy-start.1
  15.1 0.0 copy-start.2
  15.1 0.0 copy-start
  15.1 0.0 copy-start.6
  15.1 1.2 collective-permute-start.16
  16.3 16.6 %collective-permute-done.16 = bf16[1,2,128,1536]{3,2,1,0:T(8,128)(2,1)S(1)} collective-permute-done((bf16[1,2,128,1536]{3,2,1,0:T(8,128)(2,1)S(1)}, bf16[1,2,128,1536]{3,2,1,0:T(8,128)(2,1)S(1)}, u32[]{:S(2)}, u32[]{:S(2)}) %collective-permute-start.16) | collective-permute-done | bytes 786464 | tf_op jit(solution)/shard_map/ppermute | solution.py:82
  33.0 0.1 pad_maximum_fusion.refs_8_
  33.1 2.2 %collective-permute-start.17 = (bf16[2,2,128,1536]{3,2,1,0:T(8,128)(2,1)S(1)}, bf16[2,2,128,1536]{3,2,1,0:T(8,128)(2,1)S(1)}, u32[]{:S(2)}, u32[]{:S(2)}) collective-permute-start(bf16[2,2,128,1536]{3,2,1,0:T(8,128)(2,1)S(1)} %pad_maximum_fusion.refs_8_), channel_id=1, source_target_pairs={{0,1},{1,0},{2,3},{3,2},{4,5},{5,4},{6,7},{7,6},{8,9},{9,8},{10,11... | collective-permute-start | bytes 4718600 | tf_op jit(solution)/shard_map/ppermute | solution.py:82
  35.3 3.0 %collective-permute-start = (bf16[128,2048]{1,0:T(8,128)(2,1)S(1)}, bf16[128,2048]{1,0:T(8,128)(2,1)S(1)}, u32[]{:S(2)}, u32[]{:S(2)}) collective-permute-start(bf16[128,2048]{1,0:T(8,128)(2,1)S(1)} %bitcast.22), channel_id=1, source_target_pairs={{0,1},{1,2},{2,3},{3,4},{4,5},{6,7},{8,9},{9,10},{10,11},{11,12},{... | collective-permute-start | bytes 1572872 | tf_op jit(solution)/shard_map/ppermute | solution.py:239
  38.3 2.4 %collective-permute-start.1 = (bf16[128,2048]{1,0:T(8,128)(2,1)S(1)}, bf16[128,2048]{1,0:T(8,128)(2,1)S(1)}, u32[]{:S(2)}, u32[]{:S(2)}) collective-permute-start(bf16[128,2048]{1,0:T(8,128)(2,1)S(1)} %bitcast.26), channel_id=1, source_target_pairs={{0,1},{1,2},{2,3},{3,4},{4,5},{6,7},{8,9},{9,10},{10,11},{11,12},{... | collective-permute-start | bytes 1572872 | tf_op jit(solution)/shard_map/ppermute | solution.py:241
  40.7 2.0 %collective-permute-start.2 = (bf16[128,2048]{1,0:T(8,128)(2,1)S(1)}, bf16[128,2048]{1,0:T(8,128)(2,1)S(1)}, u32[]{:S(2)}, u32[]{:S(2)}) collective-permute-start(bf16[128,2048]{1,0:T(8,128)(2,1)S(1)} %bitcast.23), channel_id=1, source_target_pairs={{1,0},{3,2},{4,3},{5,4},{6,5},{7,6},{9,8},{11,10},{12,11},{13,12},... | collective-permute-start | bytes 1572872 | tf_op jit(solution)/shard_map/ppermute | solution.py:240
  42.7 1.5 %collective-permute-start.3 = (bf16[128,2048]{1,0:T(8,128)(2,1)S(1)}, bf16[128,2048]{1,0:T(8,128)(2,1)S(1)}, u32[]{:S(2)}, u32[]{:S(2)}) collective-permute-start(bf16[128,2048]{1,0:T(8,128)(2,1)S(1)} %bitcast.27), channel_id=1, source_target_pairs={{1,0},{3,2},{4,3},{5,4},{6,5},{7,6},{9,8},{11,10},{12,11},{13,12},... | collective-permute-start | bytes 1572872 | tf_op jit(solution)/shard_map/ppermute | solution.py:242
  44.2 0.2 collective-permute-done.kl
  44.4 5.6 %collective-permute-done.1.vl = bf16[128,2048]{1,0:T(8,128)(2,1)S(1)} collective-permute-done((bf16[128,2048]{1,0:T(8,128)(2,1)S(1)}, bf16[128,2048]{1,0:T(8,128)(2,1)S(1)}, u32[]{:S(2)}, u32[]{:S(2)}) %collective-permute-start.1) | collective-permute-done | bytes 524320 | tf_op jit(solution)/shard_map/ppermute | solution.py:241
  50.0 0.0 collective-permute-done.2.kr
  50.0 0.0 collective-permute-done.3.vr
  50.1 6.2 %attention_forward.1 = (bf16[128,512]{1,0:T(8,128)(2,1)S(1)}, bf16[128,512]{1,0:T(8,128)(2,1)S(1)}, bf16[128,512]{1,0:T(8,128)(2,1)S(1)}, bf16[128,512]{1,0:T(8,128)(2,1)S(1)}) custom-call(s32[1,8]{1,0:T(1,128)S(1)} %copy-done.6, bf16[128,2048]{1,0:T(8,128)(2,1)S(1)} %bitcast.20, bf16[128,2048]{1,0:T(8,128)(2,1)S(1)} %bitcast.24, ...), custom_call_target="tpu_custom_call" | custom-call | flops 268435456 | bytes 4194304 | tf_op jit(solution)/shard_map/attention_forward/pallas_call | solution.py:259
  56.2 0.1 collective-permute-start.8
  56.3 9.0 %collective-permute-start.9 = (bf16[128,512]{1,0:T(8,128)(2,1)S(1)}, bf16[128,512]{1,0:T(8,128)(2,1)S(1)}, u32[]{:S(2)}, u32[]{:S(2)}) collective-permute-start(bf16[128,512]{1,0:T(8,128)(2,1)S(1)} %get-tuple-element.32.refs_0_), channel_id=1, source_target_pairs={{0,2},{1,3},{2,0},{3,1},{4,6},{5,7},{6,4},{7,5},{8,10},{9,11},{10,... | collective-permute-start | bytes 393224 | tf_op jit(solution)/shard_map/ppermute | solution.py:82
  65.3 0.3 collective-permute-start.10
  65.6 0.1 collective-permute-start.11
  65.7 0.0 collective-permute-done.8.refs_1_
  65.7 2.9 %collective-permute-start.13 = (bf16[128,512]{1,0:T(8,128)(2,1)S(1)}, bf16[128,512]{1,0:T(8,128)(2,1)S(1)}, u32[]{:S(2)}, u32[]{:S(2)}) collective-permute-start(bf16[128,512]{1,0:T(8,128)(2,1)S(1)} %get-tuple-element.34), channel_id=1, source_target_pairs={{0,6},{1,7},{2,4},{3,5},{4,2},{5,3},{6,0},{7,1},{8,14},{9,15},{10,... | collective-permute-start | bytes 393224 | tf_op jit(solution)/shard_map/ppermute | solution.py:82
  68.5 0.2 collective-permute-done.9.refs_2_
  68.8 1.5 %collective-permute-start.12 = (bf16[128,512]{1,0:T(8,128)(2,1)S(1)}, bf16[128,512]{1,0:T(8,128)(2,1)S(1)}, u32[]{:S(2)}, u32[]{:S(2)}) collective-permute-start(bf16[128,512]{1,0:T(8,128)(2,1)S(1)} %get-tuple-element.35), channel_id=1, source_target_pairs={{0,5},{1,4},{2,7},{3,6},{4,1},{5,0},{6,3},{7,2},{8,13},{9,12},{10,... | collective-permute-start | bytes 393224 | tf_op jit(solution)/shard_map/ppermute | solution.py:82
  70.2 2.5 %collective-permute-done.10.refs_3_ = bf16[128,512]{1,0:T(8,128)(2,1)S(1)} collective-permute-done((bf16[128,512]{1,0:T(8,128)(2,1)S(1)}, bf16[128,512]{1,0:T(8,128)(2,1)S(1)}, u32[]{:S(2)}, u32[]{:S(2)}) %collective-permute-start.10) | collective-permute-done | bytes 131104 | tf_op jit(solution)/shard_map/ppermute | solution.py:82
  72.7 0.0 collective-permute-start.14
  72.7 0.0 collective-permute-done.11.refs_4_
  72.7 7.2 %collective-permute-done.12.refs_5_ = bf16[128,512]{1,0:T(8,128)(2,1)S(1)} collective-permute-done((bf16[128,512]{1,0:T(8,128)(2,1)S(1)}, bf16[128,512]{1,0:T(8,128)(2,1)S(1)}, u32[]{:S(2)}, u32[]{:S(2)}) %collective-permute-start.12) | collective-permute-done | bytes 131104 | tf_op jit(solution)/shard_map/ppermute | solution.py:82
  79.9 0.0 collective-permute-done.13.refs_6_
  79.9 0.0 collective-permute-done.14.refs_7_
  79.9 0.0 collective-permute-done.17.refs_9_
  80.0 1.8 %gradient_product.1 = (f32[128,1536]{1,0:T(8,128)S(1)}, bf16[128,1536]{1,0:T(8,128)(2,1)S(1)}, bf16[128,1536]{1,0:T(8,128)(2,1)S(1)}, bf16[128,1536]{1,0:T(8,128)(2,1)S(1)}) custom-call(bf16[128,512]{1,0:T(8,128)(2,1)S(1)} %get-tuple-element.32.refs_0_, bf16[128,512]{1,0:T(8,128)(2,1)S(1)} %collective-permute-done.8.refs_1_, ...), custom_call_target="tpu_custom_call" | custom-call | flops 1610612736 | bytes 4194304 | tf_op jit(solution)/shard_map/gradient_product/pallas_call | solution.py:288
  81.8 1.4 collective-permute-start.18
  83.2 2.3 %collective-permute-start.19 = (bf16[128,1536]{1,0:T(8,128)(2,1)S(1)}, bf16[128,1536]{1,0:T(8,128)(2,1)S(1)}, u32[]{:S(2)}, u32[]{:S(2)}) collective-permute-start(bf16[128,1536]{1,0:T(8,128)(2,1)S(1)} %get-tuple-element.38), channel_id=1, source_target_pairs={{0,16},{8,24},{16,0},{24,8},{1,17},{9,25},{17,1},{25,9},{2,18},{10... | collective-permute-start | bytes 1179656 | tf_op jit(solution)/shard_map/ppermute | solution.py:82
  85.5 12.0 %attention_backward.1 = (bf16[128,2048]{1,0:T(8,128)(2,1)}, f32[128,2048]{1,0:T(8,128)}, f32[128,2048]{1,0:T(8,128)}, bf16[128,2048]{1,0:T(8,128)(2,1)S(1)}, bf16[128,2048]{1,0:T(8,128)(2,1)S(1)}) custom-call(s32[1,8]{1,0:T(1,128)S(1)} %copy-done.6, bf16[128,2048]{1,0:T(8,128)(2,1)S(1)} %bitcast.21, bf16[128,2048]{1,0:T(8,128)(2,1)S(1)} %bitcast.25, ...), custom_call_target="tpu_custom_call" | custom-call | flops 939524096 | bytes 7864320 | tf_op jit(solution)/shard_map/attention_backward/pallas_call | solution.py:271
  97.5 1.4 %collective-permute-start.4 = (bf16[128,2048]{1,0:T(8,128)(2,1)S(1)}, bf16[128,2048]{1,0:T(8,128)(2,1)S(1)}, u32[]{:S(2)}, u32[]{:S(2)}) collective-permute-start(bf16[128,2048]{1,0:T(8,128)(2,1)S(1)} %get-tuple-element.28), channel_id=1, source_target_pairs={{0,1},{2,3},{3,4},{4,5},{5,6},{6,7},{8,9},{10,11},{11,12},{12,13},... | collective-permute-start | bytes 1572872 | tf_op jit(solution)/shard_map/ppermute | solution.py:343
  98.9 1.3 collective-permute-start.5
  100.2 0.1 collective-permute-start.20
  100.3 0.0 collective-permute-done.18.refs_0_
  100.3 3.4 %collective-permute-start.6 = (bf16[128,2048]{1,0:T(8,128)(2,1)S(1)}, bf16[128,2048]{1,0:T(8,128)(2,1)S(1)}, u32[]{:S(2)}, u32[]{:S(2)}) collective-permute-start(bf16[128,2048]{1,0:T(8,128)(2,1)S(1)} %get-tuple-element.28), channel_id=1, source_target_pairs={{1,0},{2,1},{3,2},{4,3},{5,4},{7,6},{9,8},{10,9},{11,10},{12,11},{... | collective-permute-start | bytes 1572872 | tf_op jit(solution)/shard_map/ppermute | solution.py:343
  103.7 0.0 collective-permute-done.19.refs_1_
  103.7 2.5 %collective-permute-start.7 = (bf16[128,2048]{1,0:T(8,128)(2,1)S(1)}, bf16[128,2048]{1,0:T(8,128)(2,1)S(1)}, u32[]{:S(2)}, u32[]{:S(2)}) collective-permute-start(bf16[128,2048]{1,0:T(8,128)(2,1)S(1)} %get-tuple-element.29), channel_id=1, source_target_pairs={{1,0},{2,1},{3,2},{4,3},{5,4},{7,6},{9,8},{10,9},{11,10},{12,11},{... | collective-permute-start | bytes 1572872 | tf_op jit(solution)/shard_map/ppermute | solution.py:343
  106.2 5.2 %collective-permute-done.20.refs_2_ = bf16[128,1536]{1,0:T(8,128)(2,1)S(1)} collective-permute-done((bf16[128,1536]{1,0:T(8,128)(2,1)S(1)}, bf16[128,1536]{1,0:T(8,128)(2,1)S(1)}, u32[]{:S(2)}, u32[]{:S(2)}) %collective-permute-start.20) | collective-permute-done | bytes 393248 | tf_op jit(solution)/shard_map/ppermute | solution.py:82
  111.4 0.9 gradient_sum.1
  112.3 5.4 %collective-permute-start.21 = (f32[128,128]{1,0:T(8,128)S(1)}, f32[128,128]{1,0:T(8,128)S(1)}, u32[]{:S(2)}, u32[]{:S(2)}) collective-permute-start(f32[128,128]{1,0:T(8,128)S(1)} %get-tuple-element.41.gram), channel_id=1, source_target_pairs={{0,2},{1,3},{2,0},{3,1},{4,6},{5,7},{6,4},{7,5},{8,10},{9,11},{10,... | collective-permute-start | bytes 196616 | tf_op jit(solution)/shard_map/ppermute | solution.py:82
  117.7 5.0 %collective-permute-done.21.gram_other = f32[128,128]{1,0:T(8,128)S(1)} collective-permute-done((f32[128,128]{1,0:T(8,128)S(1)}, f32[128,128]{1,0:T(8,128)S(1)}, u32[]{:S(2)}, u32[]{:S(2)}) %collective-permute-start.21) | collective-permute-done | bytes 65568 | tf_op jit(solution)/shard_map/ppermute | solution.py:82
  122.7 4.0 %newton_schulz.1 = (f32[128,384]{1,0:T(8,128)S(1)}, bf16[128,384]{1,0:T(8,128)(2,1)S(1)}, bf16[128,384]{1,0:T(8,128)(2,1)S(1)}, bf16[128,384]{1,0:T(8,128)(2,1)S(1)}) custom-call(f32[128,1536]{1,0:T(8,128)S(1)} %get-tuple-element.40.x, f32[128,128]{1,0:T(8,128)S(1)} %get-tuple-element.41.gram, f32[128,128]{1,0:T(8,128)S(1)} %collective-permute-done.21.gram_other), custom_call_target="tpu_custom_call" | custom-call | flops 301989888 | bytes 1572864 | tf_op jit(solution)/shard_map/newton_schulz/pallas_call | solution.py:319
  126.6 5.7 %collective-permute-start.22 = (bf16[128,384]{1,0:T(8,128)(2,1)S(1)}, bf16[128,384]{1,0:T(8,128)(2,1)S(1)}, u32[]{:S(2)}, u32[]{:S(2)}) collective-permute-start(bf16[128,384]{1,0:T(8,128)(2,1)S(1)} %get-tuple-element.43), channel_id=1, source_target_pairs={{0,1},{1,0},{2,3},{3,2},{4,5},{5,4},{6,7},{7,6},{8,9},{9,8},{10,11... | collective-permute-start | bytes 294920 | tf_op jit(solution)/shard_map/ppermute | solution.py:82
  132.3 0.0 collective-permute-done.4.kl
  132.3 0.0 collective-permute-start.23
  132.3 1.7 %collective-permute-start.24 = (bf16[128,384]{1,0:T(8,128)(2,1)S(1)}, bf16[128,384]{1,0:T(8,128)(2,1)S(1)}, u32[]{:S(2)}, u32[]{:S(2)}) collective-permute-start(bf16[128,384]{1,0:T(8,128)(2,1)S(1)} %get-tuple-element.45), channel_id=1, source_target_pairs={{0,5},{1,4},{2,7},{3,6},{4,1},{5,0},{6,3},{7,2},{8,13},{9,12},{10,... | collective-permute-start | bytes 294920 | tf_op jit(solution)/shard_map/ppermute | solution.py:82
  134.1 1.8 %key_value_sum.1 = (bf16[128,2048]{1,0:T(8,128)(2,1)}, bf16[128,2048]{1,0:T(8,128)(2,1)}) custom-call(s32[1,8]{1,0:T(1,128)S(1)} %copy-done.6, f32[128,2048]{1,0:T(8,128)S(1)} %copy-done.3, f32[128,2048]{1,0:T(8,128)S(1)} %copy-done.4, bf16[128,2048]{1,0:T(8,128)(2,1)S(1)} %collective-permute-done.4.kl, bf16[128,2048]{1,0:T(8,128)(2,1)S(1)} %collective-permute-done.5.vl, ...), custom_call_target="tpu_custom_call" | custom-call | flops 1572864 | bytes 5242880 | tf_op jit(solution)/shard_map/key_value_sum/pallas_call | solution.py:344
  135.8 0.0 collective-permute-done.22.refs_1_
  135.9 0.8 collective-permute-done.23.refs_2_
  136.7 2.3 %collective-permute-done.24.refs_3_ = bf16[128,384]{1,0:T(8,128)(2,1)S(1)} collective-permute-done((bf16[128,384]{1,0:T(8,128)(2,1)S(1)}, bf16[128,384]{1,0:T(8,128)(2,1)S(1)}, u32[]{:S(2)}, u32[]{:S(2)}) %collective-permute-start.24) | collective-permute-done | bytes 98336 | tf_op jit(solution)/shard_map/ppermute | solution.py:82
  139.0 0.9 update_rows.1
  (13 shorter events, 0.0 us)
Async XLA Ops:
  4.0 10.9 %collective-permute-start.15 = (bf16[128,1536]{1,0:T(8,128)(2,1)S(1)}, bf16[128,1536]{1,0:T(8,128)(2,1)S(1)}, u32[]{:S(2)}, u32[]{:S(2)}) collective-permute-start(bf16[128,1536]{1,0:T(8,128)(2,1)S(1)} %reshape.45), channel_id=1, source_target_pairs={{0,2},{1,3},{2,0},{3,1},{4,6},{5,7},{6,4},{7,5},{8,10},{9,11},{10,... | collective-permute-start | bytes 1179656 | tf_op jit(solution)/shard_map/ppermute | solution.py:82
  15.1 20.3 %copy-start.1 = (bf16[1,1,128,2048]{3,2,1,0:T(8,128)(2,1)S(1)}, bf16[1,1,128,2048]{3,2,1,0:T(8,128)(2,1)}, u32[]{:S(2)}) copy-start(bf16[1,1,128,2048]{3,2,1,0:T(8,128)(2,1)} %param.7) | copy-start | bytes 1572868
  15.1 23.2 %copy-start.2 = (bf16[1,1,128,2048]{3,2,1,0:T(8,128)(2,1)S(1)}, bf16[1,1,128,2048]{3,2,1,0:T(8,128)(2,1)}, u32[]{:S(2)}) copy-start(bf16[1,1,128,2048]{3,2,1,0:T(8,128)(2,1)} %param.8) | copy-start | bytes 1572868
  15.1 35.0 %copy-start = (bf16[1,1,128,2048]{3,2,1,0:T(8,128)(2,1)S(1)}, bf16[1,1,128,2048]{3,2,1,0:T(8,128)(2,1)}, u32[]{:S(2)}) copy-start(bf16[1,1,128,2048]{3,2,1,0:T(8,128)(2,1)} %param.6) | copy-start | bytes 1572868
  15.1 35.0 %copy-start.6 = (s32[1,8]{1,0:T(1,128)S(1)}, s32[1,8]{1,0:T(1,128)}, u32[]{:S(2)}) copy-start(s32[1,8]{1,0:T(1,128)} %near_ref.5) | copy-start | bytes 100
  15.1 17.9 %collective-permute-start.16 = (bf16[1,2,128,1536]{3,2,1,0:T(8,128)(2,1)S(1)}, bf16[1,2,128,1536]{3,2,1,0:T(8,128)(2,1)S(1)}, u32[]{:S(2)}, u32[]{:S(2)}) collective-permute-start(bf16[1,2,128,1536]{3,2,1,0:T(8,128)(2,1)S(1)} %maximum_bitcast_fusion), channel_id=1, source_target_pairs={{0,4},{1,5},{2,6},{3,7},{4,0},{5,1},{6,2},{7,3},{8,12},{9,13},{10,... | collective-permute-start | bytes 2359304 | tf_op jit(solution)/shard_map/ppermute | solution.py:82
  33.1 46.8 %collective-permute-start.17 = (bf16[2,2,128,1536]{3,2,1,0:T(8,128)(2,1)S(1)}, bf16[2,2,128,1536]{3,2,1,0:T(8,128)(2,1)S(1)}, u32[]{:S(2)}, u32[]{:S(2)}) collective-permute-start(bf16[2,2,128,1536]{3,2,1,0:T(8,128)(2,1)S(1)} %pad_maximum_fusion.refs_8_), channel_id=1, source_target_pairs={{0,1},{1,0},{2,3},{3,2},{4,5},{5,4},{6,7},{7,6},{8,9},{9,8},{10,11... | collective-permute-start | bytes 4718600 | tf_op jit(solution)/shard_map/ppermute | solution.py:82
  35.3 9.1 %collective-permute-start = (bf16[128,2048]{1,0:T(8,128)(2,1)S(1)}, bf16[128,2048]{1,0:T(8,128)(2,1)S(1)}, u32[]{:S(2)}, u32[]{:S(2)}) collective-permute-start(bf16[128,2048]{1,0:T(8,128)(2,1)S(1)} %bitcast.22), channel_id=1, source_target_pairs={{0,1},{1,2},{2,3},{3,4},{4,5},{6,7},{8,9},{9,10},{10,11},{11,12},{... | collective-permute-start | bytes 1572872 | tf_op jit(solution)/shard_map/ppermute | solution.py:239
  38.3 11.7 %collective-permute-start.1 = (bf16[128,2048]{1,0:T(8,128)(2,1)S(1)}, bf16[128,2048]{1,0:T(8,128)(2,1)S(1)}, u32[]{:S(2)}, u32[]{:S(2)}) collective-permute-start(bf16[128,2048]{1,0:T(8,128)(2,1)S(1)} %bitcast.26), channel_id=1, source_target_pairs={{0,1},{1,2},{2,3},{3,4},{4,5},{6,7},{8,9},{9,10},{10,11},{11,12},{... | collective-permute-start | bytes 1572872 | tf_op jit(solution)/shard_map/ppermute | solution.py:241
  40.7 9.3 %collective-permute-start.2 = (bf16[128,2048]{1,0:T(8,128)(2,1)S(1)}, bf16[128,2048]{1,0:T(8,128)(2,1)S(1)}, u32[]{:S(2)}, u32[]{:S(2)}) collective-permute-start(bf16[128,2048]{1,0:T(8,128)(2,1)S(1)} %bitcast.23), channel_id=1, source_target_pairs={{1,0},{3,2},{4,3},{5,4},{6,5},{7,6},{9,8},{11,10},{12,11},{13,12},... | collective-permute-start | bytes 1572872 | tf_op jit(solution)/shard_map/ppermute | solution.py:240
  42.7 7.3 %collective-permute-start.3 = (bf16[128,2048]{1,0:T(8,128)(2,1)S(1)}, bf16[128,2048]{1,0:T(8,128)(2,1)S(1)}, u32[]{:S(2)}, u32[]{:S(2)}) collective-permute-start(bf16[128,2048]{1,0:T(8,128)(2,1)S(1)} %bitcast.27), channel_id=1, source_target_pairs={{1,0},{3,2},{4,3},{5,4},{6,5},{7,6},{9,8},{11,10},{12,11},{13,12},... | collective-permute-start | bytes 1572872 | tf_op jit(solution)/shard_map/ppermute | solution.py:242
  56.2 9.4 %collective-permute-start.8 = (bf16[128,512]{1,0:T(8,128)(2,1)S(1)}, bf16[128,512]{1,0:T(8,128)(2,1)S(1)}, u32[]{:S(2)}, u32[]{:S(2)}) collective-permute-start(bf16[128,512]{1,0:T(8,128)(2,1)S(1)} %get-tuple-element.33), channel_id=1, source_target_pairs={{0,1},{1,0},{2,3},{3,2},{4,5},{5,4},{6,7},{7,6},{8,9},{9,8},{10,11... | collective-permute-start | bytes 393224 | tf_op jit(solution)/shard_map/ppermute | solution.py:82
  56.3 12.5 %collective-permute-start.9 = (bf16[128,512]{1,0:T(8,128)(2,1)S(1)}, bf16[128,512]{1,0:T(8,128)(2,1)S(1)}, u32[]{:S(2)}, u32[]{:S(2)}) collective-permute-start(bf16[128,512]{1,0:T(8,128)(2,1)S(1)} %get-tuple-element.32.refs_0_), channel_id=1, source_target_pairs={{0,2},{1,3},{2,0},{3,1},{4,6},{5,7},{6,4},{7,5},{8,10},{9,11},{10,... | collective-permute-start | bytes 393224 | tf_op jit(solution)/shard_map/ppermute | solution.py:82
  65.3 7.4 %collective-permute-start.10 = (bf16[128,512]{1,0:T(8,128)(2,1)S(1)}, bf16[128,512]{1,0:T(8,128)(2,1)S(1)}, u32[]{:S(2)}, u32[]{:S(2)}) collective-permute-start(bf16[128,512]{1,0:T(8,128)(2,1)S(1)} %get-tuple-element.33), channel_id=1, source_target_pairs={{0,3},{1,2},{2,1},{3,0},{4,7},{5,6},{6,5},{7,4},{8,11},{9,10},{10,... | collective-permute-start | bytes 393224 | tf_op jit(solution)/shard_map/ppermute | solution.py:82
  65.6 7.1 %collective-permute-start.11 = (bf16[128,512]{1,0:T(8,128)(2,1)S(1)}, bf16[128,512]{1,0:T(8,128)(2,1)S(1)}, u32[]{:S(2)}, u32[]{:S(2)}) collective-permute-start(bf16[128,512]{1,0:T(8,128)(2,1)S(1)} %get-tuple-element.34), channel_id=1, source_target_pairs={{0,4},{1,5},{2,6},{3,7},{4,0},{5,1},{6,2},{7,3},{8,12},{9,13},{10,... | collective-permute-start | bytes 393224 | tf_op jit(solution)/shard_map/ppermute | solution.py:82
  65.7 14.3 %collective-permute-start.13 = (bf16[128,512]{1,0:T(8,128)(2,1)S(1)}, bf16[128,512]{1,0:T(8,128)(2,1)S(1)}, u32[]{:S(2)}, u32[]{:S(2)}) collective-permute-start(bf16[128,512]{1,0:T(8,128)(2,1)S(1)} %get-tuple-element.34), channel_id=1, source_target_pairs={{0,6},{1,7},{2,4},{3,5},{4,2},{5,3},{6,0},{7,1},{8,14},{9,15},{10,... | collective-permute-start | bytes 393224 | tf_op jit(solution)/shard_map/ppermute | solution.py:82
  68.8 16.7 %copy-start.5 = (bf16[1,1,128,2048]{3,2,1,0:T(8,128)(2,1)S(1)}, bf16[1,1,128,2048]{3,2,1,0:T(8,128)(2,1)}, u32[]{:S(2)}) copy-start(bf16[1,1,128,2048]{3,2,1,0:T(8,128)(2,1)} %param.9) | copy-start | bytes 1572868
  68.8 11.2 %collective-permute-start.12 = (bf16[128,512]{1,0:T(8,128)(2,1)S(1)}, bf16[128,512]{1,0:T(8,128)(2,1)S(1)}, u32[]{:S(2)}, u32[]{:S(2)}) collective-permute-start(bf16[128,512]{1,0:T(8,128)(2,1)S(1)} %get-tuple-element.35), channel_id=1, source_target_pairs={{0,5},{1,4},{2,7},{3,6},{4,1},{5,0},{6,3},{7,2},{8,13},{9,12},{10,... | collective-permute-start | bytes 393224 | tf_op jit(solution)/shard_map/ppermute | solution.py:82
  72.7 7.3 %collective-permute-start.14 = (bf16[128,512]{1,0:T(8,128)(2,1)S(1)}, bf16[128,512]{1,0:T(8,128)(2,1)S(1)}, u32[]{:S(2)}, u32[]{:S(2)}) collective-permute-start(bf16[128,512]{1,0:T(8,128)(2,1)S(1)} %get-tuple-element.35), channel_id=1, source_target_pairs={{0,7},{1,6},{2,5},{3,4},{4,3},{5,2},{6,1},{7,0},{8,15},{9,14},{10,... | collective-permute-start | bytes 393224 | tf_op jit(solution)/shard_map/ppermute | solution.py:82
  81.8 18.5 %collective-permute-start.18 = (bf16[128,1536]{1,0:T(8,128)(2,1)S(1)}, bf16[128,1536]{1,0:T(8,128)(2,1)S(1)}, u32[]{:S(2)}, u32[]{:S(2)}) collective-permute-start(bf16[128,1536]{1,0:T(8,128)(2,1)S(1)} %get-tuple-element.37), channel_id=1, source_target_pairs={{0,8},{8,0},{16,24},{24,16},{1,9},{9,1},{17,25},{25,17},{2,10},{10... | collective-permute-start | bytes 1179656 | tf_op jit(solution)/shard_map/ppermute | solution.py:82
  83.2 20.6 %collective-permute-start.19 = (bf16[128,1536]{1,0:T(8,128)(2,1)S(1)}, bf16[128,1536]{1,0:T(8,128)(2,1)S(1)}, u32[]{:S(2)}, u32[]{:S(2)}) collective-permute-start(bf16[128,1536]{1,0:T(8,128)(2,1)S(1)} %get-tuple-element.38), channel_id=1, source_target_pairs={{0,16},{8,24},{16,0},{24,8},{1,17},{9,25},{17,1},{25,9},{2,18},{10... | collective-permute-start | bytes 1179656 | tf_op jit(solution)/shard_map/ppermute | solution.py:82
  97.5 36.6 %copy-start.3 = (f32[128,2048]{1,0:T(8,128)S(1)}, f32[128,2048]{1,0:T(8,128)}, u32[]{:S(2)}) copy-start(f32[128,2048]{1,0:T(8,128)} %get-tuple-element.26.dko) | copy-start | bytes 3145732
  97.5 36.6 %copy-start.4 = (f32[128,2048]{1,0:T(8,128)S(1)}, f32[128,2048]{1,0:T(8,128)}, u32[]{:S(2)}) copy-start(f32[128,2048]{1,0:T(8,128)} %get-tuple-element.27.dvo) | copy-start | bytes 3145732
  97.5 34.8 %collective-permute-start.4 = (bf16[128,2048]{1,0:T(8,128)(2,1)S(1)}, bf16[128,2048]{1,0:T(8,128)(2,1)S(1)}, u32[]{:S(2)}, u32[]{:S(2)}) collective-permute-start(bf16[128,2048]{1,0:T(8,128)(2,1)S(1)} %get-tuple-element.28), channel_id=1, source_target_pairs={{0,1},{2,3},{3,4},{4,5},{5,6},{6,7},{8,9},{10,11},{11,12},{12,13},... | collective-permute-start | bytes 1572872 | tf_op jit(solution)/shard_map/ppermute | solution.py:343
  98.9 33.4 %collective-permute-start.5 = (bf16[128,2048]{1,0:T(8,128)(2,1)S(1)}, bf16[128,2048]{1,0:T(8,128)(2,1)S(1)}, u32[]{:S(2)}, u32[]{:S(2)}) collective-permute-start(bf16[128,2048]{1,0:T(8,128)(2,1)S(1)} %get-tuple-element.29), channel_id=1, source_target_pairs={{0,1},{2,3},{3,4},{4,5},{5,6},{6,7},{8,9},{10,11},{11,12},{12,13},... | collective-permute-start | bytes 1572872 | tf_op jit(solution)/shard_map/ppermute | solution.py:343
  100.2 11.2 %collective-permute-start.20 = (bf16[128,1536]{1,0:T(8,128)(2,1)S(1)}, bf16[128,1536]{1,0:T(8,128)(2,1)S(1)}, u32[]{:S(2)}, u32[]{:S(2)}) collective-permute-start(bf16[128,1536]{1,0:T(8,128)(2,1)S(1)} %get-tuple-element.39), channel_id=1, source_target_pairs={{0,24},{8,16},{16,8},{24,0},{1,25},{9,17},{17,9},{25,1},{2,26},{10... | collective-permute-start | bytes 1179656 | tf_op jit(solution)/shard_map/ppermute | solution.py:82
  100.3 33.7 %collective-permute-start.6 = (bf16[128,2048]{1,0:T(8,128)(2,1)S(1)}, bf16[128,2048]{1,0:T(8,128)(2,1)S(1)}, u32[]{:S(2)}, u32[]{:S(2)}) collective-permute-start(bf16[128,2048]{1,0:T(8,128)(2,1)S(1)} %get-tuple-element.28), channel_id=1, source_target_pairs={{1,0},{2,1},{3,2},{4,3},{5,4},{7,6},{9,8},{10,9},{11,10},{12,11},{... | collective-permute-start | bytes 1572872 | tf_op jit(solution)/shard_map/ppermute | solution.py:343
  103.7 30.3 %collective-permute-start.7 = (bf16[128,2048]{1,0:T(8,128)(2,1)S(1)}, bf16[128,2048]{1,0:T(8,128)(2,1)S(1)}, u32[]{:S(2)}, u32[]{:S(2)}) collective-permute-start(bf16[128,2048]{1,0:T(8,128)(2,1)S(1)} %get-tuple-element.29), channel_id=1, source_target_pairs={{1,0},{2,1},{3,2},{4,3},{5,4},{7,6},{9,8},{10,9},{11,10},{12,11},{... | collective-permute-start | bytes 1572872 | tf_op jit(solution)/shard_map/ppermute | solution.py:343
  112.3 10.4 %collective-permute-start.21 = (f32[128,128]{1,0:T(8,128)S(1)}, f32[128,128]{1,0:T(8,128)S(1)}, u32[]{:S(2)}, u32[]{:S(2)}) collective-permute-start(f32[128,128]{1,0:T(8,128)S(1)} %get-tuple-element.41.gram), channel_id=1, source_target_pairs={{0,2},{1,3},{2,0},{3,1},{4,6},{5,7},{6,4},{7,5},{8,10},{9,11},{10,... | collective-permute-start | bytes 196616 | tf_op jit(solution)/shard_map/ppermute | solution.py:82
  126.6 9.2 %collective-permute-start.22 = (bf16[128,384]{1,0:T(8,128)(2,1)S(1)}, bf16[128,384]{1,0:T(8,128)(2,1)S(1)}, u32[]{:S(2)}, u32[]{:S(2)}) collective-permute-start(bf16[128,384]{1,0:T(8,128)(2,1)S(1)} %get-tuple-element.43), channel_id=1, source_target_pairs={{0,1},{1,0},{2,3},{3,2},{4,5},{5,4},{6,7},{7,6},{8,9},{9,8},{10,11... | collective-permute-start | bytes 294920 | tf_op jit(solution)/shard_map/ppermute | solution.py:82
  132.3 4.4 %collective-permute-start.23 = (bf16[128,384]{1,0:T(8,128)(2,1)S(1)}, bf16[128,384]{1,0:T(8,128)(2,1)S(1)}, u32[]{:S(2)}, u32[]{:S(2)}) collective-permute-start(bf16[128,384]{1,0:T(8,128)(2,1)S(1)} %get-tuple-element.44), channel_id=1, source_target_pairs={{0,4},{1,5},{2,6},{3,7},{4,0},{5,1},{6,2},{7,3},{8,12},{9,13},{10,... | collective-permute-start | bytes 294920 | tf_op jit(solution)/shard_map/ppermute | solution.py:82
  132.3 6.6 %collective-permute-start.24 = (bf16[128,384]{1,0:T(8,128)(2,1)S(1)}, bf16[128,384]{1,0:T(8,128)(2,1)S(1)}, u32[]{:S(2)}, u32[]{:S(2)}) collective-permute-start(bf16[128,384]{1,0:T(8,128)(2,1)S(1)} %get-tuple-element.45), channel_id=1, source_target_pairs={{0,5},{1,4},{2,7},{3,6},{4,1},{5,0},{6,3},{7,2},{8,13},{9,12},{10,... | collective-permute-start | bytes 294920 | tf_op jit(solution)/shard_map/ppermute | solution.py:82

commit v2 on v1

v2 whole, which is shorter than its diff:
```python
import functools
import math

import jax
import jax.numpy as jnp
from jax import lax
from jax.experimental import pallas as pl
from jax.experimental.pallas import tpu as pltpu
from jax.sharding import PartitionSpec as P

HEAD_DIM = 128
NS_STEPS = 5
SCALE = HEAD_DIM ** (-0.5)
LOG2E = math.log2(math.e)
GROUP = 4
coeff_a = 3.4445
coeff_b = -4.775
coeff_c = 2.0315
f32 = jnp.float32
bf16 = jnp.bfloat16
VMEM_LIMIT = 48 * 1024 * 1024


def whole(count):
    return [pl.BlockSpec(memory_space=pltpu.VMEM)] * count


def smem():
    return pl.BlockSpec(memory_space=pltpu.SMEM)


def params():
    return pltpu.CompilerParams(vmem_limit_bytes=VMEM_LIMIT)


def cost(flops, moved, exps=0):
    return pl.CostEstimate(flops=int(flops), bytes_accessed=int(moved), transcendentals=int(exps))


def dot_t(a, b):
    return lax.dot_general(a, b, (((1,), (1,)), ((), ())), preferred_element_type=f32)


def dot_n(a, b):
    return lax.dot_general(a, b, (((1,), (0,)), ((), ())), preferred_element_type=f32)


def dot_l(a, b):
    return lax.dot_general(a, b, (((0,), (0,)), ((), ())), preferred_element_type=f32)


def exact(a, b, dims=((1,), (0,))):
    return lax.dot_general(
        a, b, (dims, ((), ())), precision=lax.Precision.HIGHEST, preferred_element_type=f32
    )


class Plan:
    def __init__(self, head_count):
        self.seq = lax.axis_size("seq")
        self.dp = lax.axis_size("dp")
        self.per_target = head_count // self.dp
        self.high = self.per_target // 2
        self.col = self.seq // self.per_target
        self.col_bits = self.col.bit_length() - 1
        self.pairs = self.seq // 2

    def row_part(self, place):
        return (place >> (1 + self.col_bits)) * 2 + (place & 1)

    def row_mask(self, part):
        return ((part >> 1) << (1 + self.col_bits)) | (part & 1)

    def col_part(self, place):
        return (place >> 1) & (self.col - 1)


def after(value, *others):
    return lax.optimization_barrier((value, *others))[0]


def shift(value, axis, mask):
    return lax.ppermute(value, axis, [(i, i ^ mask) for i in range(lax.axis_size(axis))])


def head_slice(index):
    return pl.ds(pl.multiple_of(index * HEAD_DIM, HEAD_DIM), HEAD_DIM)


def softmax_keys(query, keys):
    scores = dot_t(keys, query)
    top = jnp.max(scores, axis=0, keepdims=True)
    powers = jnp.exp2((scores - top) * (SCALE * LOG2E))
    return powers * (1.0 / jnp.sum(powers, axis=0, keepdims=True))


def choose_far(near_ref, left, right, far):
    place = lax.axis_index("seq")
    go_left = near_ref[0, place] < place

    @pl.when(go_left)
    def _():
        far[...] = left[...]

    @pl.when(jnp.logical_not(go_left))
    def _():
        far[...] = right[...]


def forward_kernel(plan, near_ref, q, ko, vo, left, right, keep, give, far):
    layer = lax.axis_index("dp")
    choose_far(near_ref, left, right, far)
    mine = plan.row_part(lax.axis_index("seq"))
    jobs = [(j, i) for j in range(plan.per_target) for i in range(plan.dp)]
    for first in range(0, len(jobs), GROUP):
        group = jobs[first : first + GROUP]
        spots = [head_slice((layer ^ i) * plan.per_target + (mine ^ j)) for j, i in group]
        weights = [
            softmax_keys(q[:, at], jnp.concatenate([ko[:, at], far[0, :, at]], 0)).astype(bf16)
            for at in spots
        ]
        for (j, i), at, p in zip(group, spots, weights, strict=True):
            values = jnp.concatenate([vo[:, at], far[1, :, at]], 0)
            out = give if j & 1 else keep
            out[j >> 1, i * HEAD_DIM : (i + 1) * HEAD_DIM, :] = dot_l(values, p).astype(bf16)


def backward_kernel(near_ref, q, ko, vo, left, right, g, dq, dko, dvo, dfar, far):
    choose_far(near_ref, left, right, far)
    tile = q.shape[0]
    count = q.shape[1] // HEAD_DIM
    for first in range(0, count, GROUP):
        spots = [
            slice(h * HEAD_DIM, (h + 1) * HEAD_DIM)
            for h in range(first, min(first + GROUP, count))
        ]
        weights, slopes = [], []
        for at in spots:
            values = jnp.concatenate([vo[:, at], far[1, :, at]], 0)
            keys = jnp.concatenate([ko[:, at], far[0, :, at]], 0)
            weights.append(softmax_keys(q[:, at], keys))
            slopes.append(dot_t(values, g[:, at]))
        for at, p, dp in zip(spots, weights, slopes, strict=True):
            pb = p.astype(bf16)
            delta = jnp.sum(pb.astype(f32) * dp, axis=0, keepdims=True)
            ds = (p * (dp - delta)).astype(bf16)
            keys = jnp.concatenate([ko[:, at], far[0, :, at]], 0)
            dk = dot_n(ds, q[:, at]) * SCALE
            dv = dot_n(pb, g[:, at])
            dq[:, at] = (dot_l(ds, keys) * SCALE).astype(bf16)
            dko[:, at] = dk[:tile]
            dvo[:, at] = dv[:tile]
            dfar[0, :, at] = dk[tile:].astype(bf16)
            dfar[1, :, at] = dv[tile:].astype(bf16)


def combine_kernel(near_ref, dko, dvo, left, right, dk, dv):
    place = lax.axis_index("seq")
    last = lax.axis_size("seq") - 1
    before = near_ref[0, jnp.maximum(place - 1, 0)]
    beyond = near_ref[0, jnp.minimum(place + 1, last)]
    from_left = (place > 0) & (before == place)
    from_right = (place < last) & (beyond == place)
    for which, (own, out) in enumerate(((dko, dk), (dvo, dv))):
        total = own[...] + jnp.where(from_left, left[which].astype(f32), 0.0)
        out[...] = (total + jnp.where(from_right, right[which].astype(f32), 0.0)).astype(bf16)


def product_kernel(plan, spots, *refs):
    att = refs[: plan.pairs]
    cols = refs[plan.pairs : plan.pairs + 2]
    outs = refs[plan.pairs + 2 : plan.pairs + 2 + len(spots)]
    turned = refs[plan.pairs + 2 + len(spots) :]
    for t in range(plan.pairs):
        for core in range(2):
            turned[core][:, t * HEAD_DIM : (t + 1) * HEAD_DIM] = att[t][core]
    tokens = turned[0].shape[1]
    for (i, start, size), out in zip(spots, outs, strict=True):
        rows = slice(i * HEAD_DIM, (i + 1) * HEAD_DIM)
        step = 256 if size % 256 == 0 else size
        for c in range(0, size, step):
            total = None
            for core in range(2):
                block = cols[core][:, :, start + c : start + c + step].reshape(tokens, step)
                part = dot_n(turned[core][rows, :], block)
                total = part if total is None else total + part
            out[:, c : c + step] = total.astype(out.dtype)


def gram_kernel(starts, own, *refs):
    *parts, x, gram = refs
    x[...] = own[...]
    for start, part in zip(starts, parts, strict=True):
        at = slice(start, start + part.shape[1])
        x[:, at] += part[...].astype(f32)
    gram[...] = exact(x[...], x[...], ((1,), (1,)))


def polynomial(gram):
    eye = (
        lax.broadcasted_iota(jnp.int32, gram.shape, 0)
        == lax.broadcasted_iota(jnp.int32, gram.shape, 1)
    ).astype(f32)
    square = jnp.sum(jnp.sum(gram * eye, axis=1, keepdims=True), axis=0, keepdims=True)
    inverse = 1.0 / (jnp.sqrt(square) + 1e-07)
    a = gram * inverse * inverse
    p = None
    for turn in range(NS_STEPS):
        q = coeff_a * eye + coeff_b * a + coeff_c * exact(a, a)
        p = q if p is None else exact(q, p)
        if turn + 1 < NS_STEPS:
            a = exact(exact(q, a), q)
    return p, inverse


def update_kernel(plan, factor, x, gram, gram_other, *outs):
    mine = plan.row_part(lax.axis_index("seq"))
    p, inverse = polynomial(gram[...] + gram_other[...])
    p = p * (inverse * factor)
    width = outs[0].shape[1]
    for j in range(plan.per_target):
        if width % HEAD_DIM == 0:
            block = x[:, pl.ds(pl.multiple_of((mine ^ j) * width, width), width)]
        else:
            block = jnp.zeros((HEAD_DIM, width), f32)
            for r in range(plan.per_target):
                part = x[:, r * width : (r + 1) * width]
                block = jnp.where((mine ^ j) == r, part, block)
        outs[j][...] = exact(p, block).astype(outs[j].dtype)


def place_kernel(plan, *refs):
    *parts, out = refs
    mine = plan.row_part(lax.axis_index("seq"))
    for j, part in enumerate(parts):
        at = pl.ds(pl.multiple_of((mine ^ j) * HEAD_DIM, HEAD_DIM), HEAD_DIM)
        out[at, :] = part[...].astype(f32)


def local(query_tiles, key_tiles, value_tiles, attn_grad, proj_grad, neighbour):
    tile, width = query_tiles.shape[2:]
    depth = proj_grad.shape[3]
    head_count = width // HEAD_DIM
    plan = Plan(head_count)
    n, m, per = plan.seq, plan.dp, plan.per_target
    place = lax.axis_index("seq")
    struct = jax.ShapeDtypeStruct
    query, key, value, grad = (
        a.reshape(tile, width) for a in (query_tiles, key_tiles, value_tiles, attn_grad)
    )

    to_right = [(i, i + 1) for i in range(n - 1) if i + 1 != n - 2]
    to_left = [(i + 1, i) for i in range(n - 1) if i != 1]
    stacked = jnp.stack([key, value])
    left = lax.ppermute(stacked, "seq", to_right)
    right = lax.ppermute(stacked, "seq", to_left)

    slot = depth // n
    flat = proj_grad.reshape(tile, depth)
    mine = plan.col_part(place)
    mine_width = per * slot

    def column_part(part):
        return jnp.concatenate(
            [
                lax.dynamic_slice_in_dim(flat, (high * plan.col + part) * 2 * slot, 2 * slot, 1)
                for high in range(plan.high)
            ],
            1,
        )

    columns = [column_part(mine)] + [
        shift(column_part(mine ^ (t & (plan.col - 1))), "seq", t << 1)
        for t in range(1, plan.pairs)
    ]

    keep, give = pl.pallas_call(
        functools.partial(forward_kernel, plan),
        out_shape=[struct((plan.high, m * HEAD_DIM, tile), bf16)] * 2,
        in_specs=[smem()] + whole(5),
        out_specs=whole(2),
        scratch_shapes=[pltpu.VMEM((2, tile, width), bf16)],
        compiler_params=params(),
        cost_estimate=cost(8 * tile * tile * width, 16 * tile * width, 2 * tile * tile * head_count),
        name="attention_forward",
    )(neighbour, query, key, value, left, right)

    got = shift(give, "seq", 1)
    rows = [jnp.stack([keep[high], got[high]]) for high in range(plan.high)]
    pairs = [rows[0]] + [
        shift(rows[t >> plan.col_bits], "seq", t << 1) for t in range(1, plan.pairs)
    ]
    held = after(jnp.stack(columns), got)
    held_other = shift(held, "seq", 1)

    dq, dko, dvo, dfar = pl.pallas_call(
        backward_kernel,
        out_shape=[
            struct((tile, width), bf16),
            struct((tile, width), f32),
            struct((tile, width), f32),
            struct((2, tile, width), bf16),
        ],
        in_specs=[smem()] + whole(6),
        out_specs=whole(4),
        scratch_shapes=[pltpu.VMEM((2, tile, width), bf16)],
        compiler_params=params(),
        cost_estimate=cost(28 * tile * tile * width, 30 * tile * width, 2 * tile * tile * head_count),
        name="attention_backward",
    )(neighbour, query, key, value, left, right, grad)

    half = mine_width // 2
    spots = [(0, 0, mine_width), (1, 0, mine_width)]
    spots += [(i, start, half) for i in range(2, m) for start in (0, half)]
    blocks = pl.pallas_call(
        functools.partial(product_kernel, plan, spots),
        out_shape=[
            struct((HEAD_DIM, size), bf16 if i & 1 else f32) for i, start, size in spots
        ],
        in_specs=whole(plan.pairs + 2),
        out_specs=whole(len(spots)),
        scratch_shapes=[pltpu.VMEM((m * HEAD_DIM, plan.pairs * tile), bf16)] * 2,
        compiler_params=params(),
        cost_estimate=cost(
            2 * m * HEAD_DIM * n * tile * mine_width, 2 * n * tile * (mine_width + m * HEAD_DIM)
        ),
        name="gradient_product",
    )(after(pairs[0], dq), *pairs[1:], held, held_other)

    total = dict(zip([spot[:2] for spot in spots], blocks, strict=True))
    came = []
    first_step = []
    bit = 1
    while bit < m:
        for i in range(m - 1, 1, -1):
            if i & -i == bit:
                for start in (0, half):
                    part = shift(total[i, start].astype(bf16), "dp", bit)
                    if bit == 1:
                        first_step.append(part)
                    if i == bit:
                        came.append((start, part))
                    else:
                        total[i ^ bit, start] = total[i ^ bit, start] + part.astype(f32)
        bit *= 2
    came.append((0, shift(after(total[1, 0], *first_step), "dp", 1)))

    x, gram = pl.pallas_call(
        functools.partial(gram_kernel, [start for start, part in came]),
        out_shape=[struct((HEAD_DIM, mine_width), f32), struct((HEAD_DIM, HEAD_DIM), f32)],
        in_specs=whole(1 + len(came)),
        out_specs=whole(2),
        compiler_params=params(),
        cost_estimate=cost(12 * HEAD_DIM * HEAD_DIM * mine_width, 14 * HEAD_DIM * mine_width),
        name="gradient_sum",
    )(total[0, 0], *[part for start, part in came])

    gram_other = jnp.zeros_like(gram)
    for b in range(plan.col_bits):
        gram = gram + gram_other
        gram_other = shift(gram, "seq", 2 << b)

    factor = 0.2 * depth**0.5
    pieces = pl.pallas_call(
        functools.partial(update_kernel, plan, factor),
        out_shape=[struct((HEAD_DIM, slot), f32)] + [struct((HEAD_DIM, slot), bf16)] * (per - 1),
        in_specs=whole(3),
        out_specs=whole(per),
        compiler_params=params(),
        cost_estimate=cost(12 * HEAD_DIM * HEAD_DIM * mine_width, 8 * HEAD_DIM * mine_width),
        name="newton_schulz",
    )(x, gram, gram_other)
    pieces = [pieces[0]] + [
        shift(pieces[j], "seq", plan.row_mask(j)) for j in range(1, per)
    ]
    update = pl.pallas_call(
        functools.partial(place_kernel, plan),
        out_shape=struct((per * HEAD_DIM, slot), f32),
        in_specs=whole(per),
        out_specs=pl.BlockSpec(memory_space=pltpu.VMEM),
        compiler_params=params(),
        cost_estimate=cost(1, 8 * per * HEAD_DIM * slot),
        name="update_rows",
    )(*pieces)

    far_right = [(i, i + 1) for i in range(n - 1) if i != 1]
    far_left = [(i + 1, i) for i in range(n - 1) if i + 1 != n - 2]
    dfar = after(dfar, *first_step)
    dk, dv = pl.pallas_call(
        combine_kernel,
        out_shape=[struct((tile, width), bf16)] * 2,
        in_specs=[smem()] + whole(4),
        out_specs=whole(2),
        compiler_params=params(),
        cost_estimate=cost(6 * tile * width, 20 * tile * width),
        name="key_value_sum",
    )(
        neighbour,
        dko,
        dvo,
        lax.ppermute(dfar, "seq", far_right),
        lax.ppermute(dfar, "seq", far_left),
    )

    shape = query_tiles.shape
    return dq.reshape(shape), dk.reshape(shape), dv.reshape(shape), update


def solution(mesh):
    tiles = P("dp", "seq", None, None)
    return jax.shard_map(
        local,
        mesh=mesh,
        in_specs=(tiles, tiles, tiles, tiles, tiles, P("dp", None)),
        out_specs=(tiles, tiles, tiles, P("dp", "seq")),
        check_vma=False,
    )
```

time: 140 us -> 115 us (0.82)
  starting transfers between devices: 53.3 us -> 30.6 us
  Pallas kernels: 27.6 us -> 18.1 us
  waiting for transfers between devices: 54.3 us -> 60.6 us
  other arithmetic: 0.22 us -> 1.7 us
    ppermute x17, starting transfers between devices: 35.8 us -> 19.1 us  [shift(): lax.ppermute(value, axis, [(i, i ^ mask) for i in range(lax.axis_size(axi...]
    pallas_call x1, Pallas kernels: 12 us -> 4.98 us  [local(): pl.pallas_call(backward_kernel, out_shape=[struct((tile, width), bf16), s...]
    ppermute x8 -> x4, waiting for transfers between devices: 5.82 us -> 12.5 us  [the longest x1 12.5 us: local(): left = lax.ppermute(stacked, 'seq', to_right)]
    ppermute x8 -> x4, starting transfers between devices: 17.5 us -> 11.6 us  [the longest x1 4.28 us: local(): lax.ppermute(dfar, 'seq', far_left)]
    pallas_call x1, Pallas kernels: 6.18 us -> 2.29 us  [local(): pl.pallas_call(functools.partial(forward_kernel, plan), out_shape=[struct...]
    reshape x2 -> x0, local copies, waits for them, and re-layouts: 2.82 us -> none  [the longest x1 2.57 us: local(): view = proj_grad.reshape(tile, plan.high, plan.col, 2, slot)]
    another operation x0 -> x5, other arithmetic: none -> 1.6 us  [the longest x1 1.3 us: local(): stacked = jnp.stack([key, value])]
    pallas_call x2, Pallas kernels: 2.7 us -> 4.1 us  [the longest x1 3.27 us: local(): pl.pallas_call(functools.partial(product_kernel, plan, spots), out_shape=...]
  transfers between devices with their start and end apart: 25 -> 21, of which waited for: 11 -> 13; matrix products, arithmetic and copies ran while one was open for 0% -> 2% of each run, Pallas kernels for 18% -> 11%
where the time goes in v2:
time: 115 us
  waiting for transfers between devices  60.6 us (53%)
  starting transfers between devices  30.6 us (27%)
  Pallas kernels  18.1 us (16%)
  local copies, waits for them, and re-layouts  2.66 us (2%)
  other arithmetic  1.7 us (1%)
    ppermute x17, waiting for transfers between devices, shift(): lax.ppermute(value, axis, [(i, i ^ mask) for i in range(lax.axis_size(axi...  48.2 us
    ppermute x17, starting transfers between devices, shift(): lax.ppermute(value, axis, [(i, i ^ mask) for i in range(lax.axis_size(axi...  19.1 us
    ppermute x1, waiting for transfers between devices, local(): left = lax.ppermute(stacked, 'seq', to_right)  12.5 us
    pallas_call x1, Pallas kernels, local(): pl.pallas_call(backward_kernel, out_shape=[struct((tile, width), bf16), s...  4.98 us
    ppermute x1, starting transfers between devices, local(): lax.ppermute(dfar, 'seq', far_left)  4.28 us
    pallas_call x1, Pallas kernels, local(): pl.pallas_call(functools.partial(update_kernel, plan, factor), out_shape=...  3.97 us
    ppermute x1, starting transfers between devices, local(): left = lax.ppermute(stacked, 'seq', to_right)  3.77 us
    pallas_call x1, Pallas kernels, local(): pl.pallas_call(functools.partial(product_kernel, plan, spots), out_shape=...  3.27 us
  transfers between devices with their start and end apart: 21, of which 13 were waited for; matrix products, arithmetic and copies ran while one was open for 2% of the time, Pallas kernels for 11%

profile of v2, /device:TPU:1, one launch (start us, length us, event | category | flops | bytes accessed | tf_op | source)
XLA Modules:
  0.0 114.6 jit_solution(9538377622372392484)
XLA Ops:
  0.6 1.3 %pad_maximum_fusion.1 = bf16[2,128,2048]{2,1,0:T(8,128)(2,1)S(1)} fusion(bf16[1,128,2048]{2,1,0:T(8,128)(2,1)} %bitcast.25, bf16[1,128,2048]{2,1,0:T(8,128)(2,1)} %bitcast.22), kind=kLoop, calls=%fused_computation.1 | loop fusion | flops 524288 | bytes 2097152 | tf_op jit(solution)/shard_map/stack | solution.py:254
  1.9 2.0 %collective-permute-start.1 = (bf16[2,128,2048]{2,1,0:T(8,128)(2,1)S(1)}, bf16[2,128,2048]{2,1,0:T(8,128)(2,1)S(1)}, u32[]{:S(2)}, u32[]{:S(2)}) collective-permute-start(bf16[2,128,2048]{2,1,0:T(8,128)(2,1)S(1)} %pad_maximum_fusion.1), channel_id=1, source_target_pairs={{1,0},{3,2},{4,3},{5,4},{6,5},{7,6},{9,8},{11,10},{12,11},{13,12},... | collective-permute-start | bytes 3145736 | tf_op jit(solution)/shard_map/ppermute | solution.py:256
  4.0 3.8 %collective-permute-start = (bf16[2,128,2048]{2,1,0:T(8,128)(2,1)S(1)}, bf16[2,128,2048]{2,1,0:T(8,128)(2,1)S(1)}, u32[]{:S(2)}, u32[]{:S(2)}) collective-permute-start(bf16[2,128,2048]{2,1,0:T(8,128)(2,1)S(1)} %pad_maximum_fusion.1), channel_id=1, source_target_pairs={{0,1},{1,2},{2,3},{3,4},{4,5},{6,7},{8,9},{9,10},{10,11},{11,12},{... | collective-permute-start | bytes 3145736 | tf_op jit(solution)/shard_map/ppermute | solution.py:255
  7.8 0.0 copy-start
  7.8 0.0 copy-start.1
  7.8 0.0 copy-start.4
  7.8 0.0 copy-start.6
  7.8 1.4 %dynamic-slice_bitcast_fusion.3 = (bf16[128,768]{1,0:T(8,128)(2,1)S(1)}, bf16[128,768]{1,0:T(8,128)(2,1)S(1)}, bf16[128,768]{1,0:T(8,128)(2,1)S(1)}, bf16[128,768]{1,0:T(8,128)(2,1)S(1)}) fusion(bf16[1,1,128,3072]{3,2,1,0:T(8,128)(2,1)} %param.10, s32[]{:T(128)S(6)} %select_n.16, s32[]{:T(128)S(6)} %select_n.17, s32[]{:T(128)S(6)} %select_n.19, s32[]{:T(128)S(6)} %select_n.18), kind=kLoop, calls=%fused_computation.11 | loop fusion | bytes 1572880 | tf_op jit(solution)/shard_map/dynamic_slice | solution.py:266
  9.2 0.1 fusion
  9.3 0.2 collective-permute-start.7
  9.5 3.8 %collective-permute-start.8 = (bf16[128,1536]{1,0:T(8,128)(2,1)S(1)}, bf16[128,1536]{1,0:T(8,128)(2,1)S(1)}, u32[]{:S(2)}, u32[]{:S(2)}) collective-permute-start(bf16[128,1536]{1,0:T(8,128)(2,1)S(1)} %pad_maximum_fusion.3), channel_id=1, source_target_pairs={{0,6},{1,7},{2,4},{3,5},{4,2},{5,3},{6,0},{7,1},{8,14},{9,15},{10,... | collective-permute-start | bytes 1179656 | tf_op jit(solution)/shard_map/ppermute | solution.py:83
  13.3 0.0 collective-permute-start.6
  13.3 0.0 collective-permute-done.1.right
  13.3 12.5 %collective-permute-done.left = bf16[2,128,2048]{2,1,0:T(8,128)(2,1)S(1)} collective-permute-done((bf16[2,128,2048]{2,1,0:T(8,128)(2,1)S(1)}, bf16[2,128,2048]{2,1,0:T(8,128)(2,1)S(1)}, u32[]{:S(2)}, u32[]{:S(2)}) %collective-permute-start) | collective-permute-done | bytes 1048608 | tf_op jit(solution)/shard_map/ppermute | solution.py:255
  25.8 0.0 copy-done
  25.8 0.0 copy-done.1
  25.8 0.0 copy-done.4
  25.8 0.0 copy-done.6
  25.8 2.3 %attention_forward.1 = (bf16[2,512,128]{2,1,0:T(8,128)(2,1)S(1)}, bf16[2,512,128]{2,1,0:T(8,128)(2,1)S(1)}) custom-call(s32[1,8]{1,0:T(1,128)S(1)} %copy-done.6, bf16[128,2048]{1,0:T(8,128)(2,1)S(1)} %bitcast.28, bf16[128,2048]{1,0:T(8,128)(2,1)S(1)} %bitcast.23, bf16[128,2048]{1,0:T(8,128)(2,1)S(1)} %bitcast.26, ...), custom_call_target="tpu_custom_call" | custom-call | flops 268435456 | bytes 4194304 | tf_op jit(solution)/shard_map/attention_forward/pallas_call | solution.py:277
  28.1 0.0 copy-done.2
  28.1 0.1 collective-permute-start.2
  28.2 9.0 %collective-permute-done.7 = bf16[128,1536]{1,0:T(8,128)(2,1)S(1)} collective-permute-done((bf16[128,1536]{1,0:T(8,128)(2,1)S(1)}, bf16[128,1536]{1,0:T(8,128)(2,1)S(1)}, u32[]{:S(2)}, u32[]{:S(2)}) %collective-permute-start.7) | collective-permute-done | bytes 393248 | tf_op jit(solution)/shard_map/ppermute | solution.py:83
  37.2 0.0 collective-permute-done.8
  37.2 2.3 %collective-permute-done.6 = bf16[128,1536]{1,0:T(8,128)(2,1)S(1)} collective-permute-done((bf16[128,1536]{1,0:T(8,128)(2,1)S(1)}, bf16[128,1536]{1,0:T(8,128)(2,1)S(1)}, u32[]{:S(2)}, u32[]{:S(2)}) %collective-permute-start.6) | collective-permute-done | bytes 393248 | tf_op jit(solution)/shard_map/ppermute | solution.py:83
  39.5 0.2 pad_maximum_fusion.refs_4_
  39.7 0.0 copy-start.5
  39.7 0.0 collective-permute-done.2
  39.7 0.1 collective-permute-start.9
  39.9 0.1 collective-permute-start.3
  40.0 2.4 %collective-permute-start.5 = (bf16[2,512,128]{2,1,0:T(8,128)(2,1)S(1)}, bf16[2,512,128]{2,1,0:T(8,128)(2,1)S(1)}, u32[]{:S(2)}, u32[]{:S(2)}) collective-permute-start(bf16[2,512,128]{2,1,0:T(8,128)(2,1)S(1)} %pad_maximum_fusion.5), channel_id=1, source_target_pairs={{0,6},{1,7},{2,4},{3,5},{4,2},{5,3},{6,0},{7,1},{8,14},{9,15},{10,... | collective-permute-start | bytes 786440 | tf_op jit(solution)/shard_map/ppermute | solution.py:83
  42.4 0.3 collective-permute-start.4
  42.7 5.0 %attention_backward.1 = (bf16[128,2048]{1,0:T(8,128)(2,1)}, f32[128,2048]{1,0:T(8,128)S(1)}, f32[128,2048]{1,0:T(8,128)S(1)}, bf16[2,128,2048]{2,1,0:T(8,128)(2,1)S(1)}) custom-call(s32[1,8]{1,0:T(1,128)S(1)} %copy-done.6, bf16[128,2048]{1,0:T(8,128)(2,1)S(1)} %bitcast.29, bf16[128,2048]{1,0:T(8,128)(2,1)S(1)} %bitcast.24, bf16[128,2048]{1,0:T(8,128)(2,1)S(1)} %bitcast.27, ...), custom_call_target="tpu_custom_call" | custom-call | flops 939524096 | bytes 7864320 | tf_op jit(solution)/shard_map/attention_backward/pallas_call | solution.py:296
  47.7 0.0 collective-permute-done.3.refs_1_
  47.7 6.7 %collective-permute-done.5.refs_3_ = bf16[2,512,128]{2,1,0:T(8,128)(2,1)S(1)} collective-permute-done((bf16[2,512,128]{2,1,0:T(8,128)(2,1)S(1)}, bf16[2,512,128]{2,1,0:T(8,128)(2,1)S(1)}, u32[]{:S(2)}, u32[]{:S(2)}) %collective-permute-start.5) | collective-permute-done | bytes 262176 | tf_op jit(solution)/shard_map/ppermute | solution.py:83
  54.4 0.9 collective-permute-done.4.refs_2_
  55.3 0.0 collective-permute-done.9.refs_5_
  55.3 1.2 %copy-done.7 = bf16[4,128,1536]{2,1,0:T(8,128)(2,1)} copy-done((bf16[4,128,1536]{2,1,0:T(8,128)(2,1)}, bf16[4,128,1536]{2,1,0:T(8,128)(2,1)S(1)}, u32[]{:S(2)}) %copy-start.7) | copy-done | bytes 1572888
  56.5 3.3 %gradient_product.1 = (f32[128,1536]{1,0:T(8,128)S(1)}, bf16[128,1536]{1,0:T(8,128)(2,1)S(1)}, f32[128,768]{1,0:T(8,128)S(1)}, f32[128,768]{1,0:T(8,128)S(1)}, b...) custom-call(bf16[2,512,128]{2,1,0:T(8,128)(2,1)S(1)} %pad_maximum_fusion.4.refs_0_, ...), custom_call_target="tpu_custom_call" | custom-call | flops 1610612736 | bytes 4194304 | tf_op jit(solution)/shard_map/gradient_product/pallas_call | solution.py:315
  59.8 1.4 %collective-permute-start.10 = (bf16[128,768]{1,0:T(8,128)(2,1)S(1)}, bf16[128,768]{1,0:T(8,128)(2,1)S(1)}, u32[]{:S(2)}, u32[]{:S(2)}) collective-permute-start(bf16[128,768]{1,0:T(8,128)(2,1)S(1)} %get-tuple-element.36), channel_id=1, source_target_pairs={{0,8},{8,0},{16,24},{24,16},{1,9},{9,1},{17,25},{25,17},{2,10},{10... | collective-permute-start | bytes 589832 | tf_op jit(solution)/shard_map/ppermute | solution.py:83
  61.1 0.2 collective-permute-start.11
  61.3 3.5 %collective-permute-done.10 = bf16[128,768]{1,0:T(8,128)(2,1)S(1)} collective-permute-done((bf16[128,768]{1,0:T(8,128)(2,1)S(1)}, bf16[128,768]{1,0:T(8,128)(2,1)S(1)}, u32[]{:S(2)}, u32[]{:S(2)}) %collective-permute-start.10) | collective-permute-done | bytes 196640 | tf_op jit(solution)/shard_map/ppermute | solution.py:83
  64.8 4.2 %collective-permute-done.11 = bf16[128,768]{1,0:T(8,128)(2,1)S(1)} collective-permute-done((bf16[128,768]{1,0:T(8,128)(2,1)S(1)}, bf16[128,768]{1,0:T(8,128)(2,1)S(1)}, u32[]{:S(2)}, u32[]{:S(2)}) %collective-permute-start.11) | collective-permute-done | bytes 196640 | tf_op jit(solution)/shard_map/ppermute | solution.py:83
  69.0 4.3 %collective-permute-start.13 = (bf16[2,128,2048]{2,1,0:T(8,128)(2,1)S(1)}, bf16[2,128,2048]{2,1,0:T(8,128)(2,1)S(1)}, u32[]{:S(2)}, u32[]{:S(2)}) collective-permute-start(bf16[2,128,2048]{2,1,0:T(8,128)(2,1)S(1)} %get-tuple-element.38), channel_id=1, source_target_pairs={{1,0},{2,1},{3,2},{4,3},{5,4},{7,6},{9,8},{10,9},{11,10},{12,11},{... | collective-permute-start | bytes 3145736 | tf_op jit(solution)/shard_map/ppermute | solution.py:402
  73.3 1.5 %collective-permute-start.12 = (bf16[2,128,2048]{2,1,0:T(8,128)(2,1)S(1)}, bf16[2,128,2048]{2,1,0:T(8,128)(2,1)S(1)}, u32[]{:S(2)}, u32[]{:S(2)}) collective-permute-start(bf16[2,128,2048]{2,1,0:T(8,128)(2,1)S(1)} %get-tuple-element.38), channel_id=1, source_target_pairs={{0,1},{2,3},{3,4},{4,5},{5,6},{6,7},{8,9},{10,11},{11,12},{12,13},... | collective-permute-start | bytes 3145736 | tf_op jit(solution)/shard_map/ppermute | solution.py:401
  74.8 2.4 %collective-permute-start.14 = (bf16[128,768]{1,0:T(8,128)(2,1)S(1)}, bf16[128,768]{1,0:T(8,128)(2,1)S(1)}, u32[]{:S(2)}, u32[]{:S(2)}) collective-permute-start(bf16[128,768]{1,0:T(8,128)(2,1)S(1)} %add_convert_fusion.1), channel_id=1, source_target_pairs={{0,16},{8,24},{16,0},{24,8},{1,17},{9,25},{17,1},{25,9},{2,18},{10... | collective-permute-start | bytes 589832 | tf_op jit(solution)/shard_map/ppermute | solution.py:83
  77.2 1.3 %collective-permute-start.16 = (bf16[128,1536]{1,0:T(8,128)(2,1)S(1)}, bf16[128,1536]{1,0:T(8,128)(2,1)S(1)}, u32[]{:S(2)}, u32[]{:S(2)}) collective-permute-start(bf16[128,1536]{1,0:T(8,128)(2,1)S(1)} %get-tuple-element.45), channel_id=1, source_target_pairs={{0,8},{8,0},{16,24},{24,16},{1,9},{9,1},{17,25},{25,17},{2,10},{10... | collective-permute-start | bytes 1179656 | tf_op jit(solution)/shard_map/ppermute | solution.py:83
  78.5 0.1 collective-permute-start.15
  78.6 7.1 %collective-permute-done.14.refs_0_ = bf16[128,768]{1,0:T(8,128)(2,1)S(1)} collective-permute-done((bf16[128,768]{1,0:T(8,128)(2,1)S(1)}, bf16[128,768]{1,0:T(8,128)(2,1)S(1)}, u32[]{:S(2)}, u32[]{:S(2)}) %collective-permute-start.14) | collective-permute-done | bytes 196640 | tf_op jit(solution)/shard_map/ppermute | solution.py:83
  85.7 7.1 %collective-permute-done.15.refs_1_ = bf16[128,768]{1,0:T(8,128)(2,1)S(1)} collective-permute-done((bf16[128,768]{1,0:T(8,128)(2,1)S(1)}, bf16[128,768]{1,0:T(8,128)(2,1)S(1)}, u32[]{:S(2)}, u32[]{:S(2)}) %collective-permute-start.15) | collective-permute-done | bytes 196640 | tf_op jit(solution)/shard_map/ppermute | solution.py:83
  92.9 0.8 collective-permute-done.16.refs_2_
  93.6 0.8 gradient_sum.1
  94.5 2.9 %collective-permute-start.17 = (f32[128,128]{1,0:T(8,128)S(1)}, f32[128,128]{1,0:T(8,128)S(1)}, u32[]{:S(2)}, u32[]{:S(2)}) collective-permute-start(f32[128,128]{1,0:T(8,128)S(1)} %get-tuple-element.47.gram), channel_id=1, source_target_pairs={{0,2},{1,3},{2,0},{3,1},{4,6},{5,7},{6,4},{7,5},{8,10},{9,11},{10,... | collective-permute-start | bytes 196616 | tf_op jit(solution)/shard_map/ppermute | solution.py:83
  97.4 1.7 %collective-permute-done.17.gram_other = f32[128,128]{1,0:T(8,128)S(1)} collective-permute-done((f32[128,128]{1,0:T(8,128)S(1)}, f32[128,128]{1,0:T(8,128)S(1)}, u32[]{:S(2)}, u32[]{:S(2)}) %collective-permute-start.17) | collective-permute-done | bytes 65568 | tf_op jit(solution)/shard_map/ppermute | solution.py:83
  99.1 4.0 %newton_schulz.1 = (f32[128,384]{1,0:T(8,128)S(1)}, bf16[128,384]{1,0:T(8,128)(2,1)S(1)}, bf16[128,384]{1,0:T(8,128)(2,1)S(1)}, bf16[128,384]{1,0:T(8,128)(2,1)S(1)}) custom-call(f32[128,1536]{1,0:T(8,128)S(1)} %get-tuple-element.46.x, f32[128,128]{1,0:T(8,128)S(1)} %get-tuple-element.47.gram, f32[128,128]{1,0:T(8,128)S(1)} %collective-permute-done.17.gram_other), custom_call_target="tpu_custom_call" | custom-call | flops 301989888 | bytes 1572864 | tf_op jit(solution)/shard_map/newton_schulz/pallas_call | solution.py:364
  103.0 2.2 %collective-permute-start.18 = (bf16[128,384]{1,0:T(8,128)(2,1)S(1)}, bf16[128,384]{1,0:T(8,128)(2,1)S(1)}, u32[]{:S(2)}, u32[]{:S(2)}) collective-permute-start(bf16[128,384]{1,0:T(8,128)(2,1)S(1)} %get-tuple-element.49), channel_id=1, source_target_pairs={{0,1},{1,0},{2,3},{3,2},{4,5},{5,4},{6,7},{7,6},{8,9},{9,8},{10,11... | collective-permute-start | bytes 294920 | tf_op jit(solution)/shard_map/ppermute | solution.py:83
  105.2 0.1 collective-permute-start.19
  105.3 1.7 %collective-permute-start.20 = (bf16[128,384]{1,0:T(8,128)(2,1)S(1)}, bf16[128,384]{1,0:T(8,128)(2,1)S(1)}, u32[]{:S(2)}, u32[]{:S(2)}) collective-permute-start(bf16[128,384]{1,0:T(8,128)(2,1)S(1)} %get-tuple-element.51), channel_id=1, source_target_pairs={{0,5},{1,4},{2,7},{3,6},{4,1},{5,0},{6,3},{7,2},{8,13},{9,12},{10,... | collective-permute-start | bytes 294920 | tf_op jit(solution)/shard_map/ppermute | solution.py:83
  106.9 0.0 collective-permute-done.18.refs_1_
  106.9 2.7 %collective-permute-done.19.refs_2_ = bf16[128,384]{1,0:T(8,128)(2,1)S(1)} collective-permute-done((bf16[128,384]{1,0:T(8,128)(2,1)S(1)}, bf16[128,384]{1,0:T(8,128)(2,1)S(1)}, u32[]{:S(2)}, u32[]{:S(2)}) %collective-permute-start.19) | collective-permute-done | bytes 98336 | tf_op jit(solution)/shard_map/ppermute | solution.py:83
  109.6 2.3 %collective-permute-done.20.refs_3_ = bf16[128,384]{1,0:T(8,128)(2,1)S(1)} collective-permute-done((bf16[128,384]{1,0:T(8,128)(2,1)S(1)}, bf16[128,384]{1,0:T(8,128)(2,1)S(1)}, u32[]{:S(2)}, u32[]{:S(2)}) %collective-permute-start.20) | collective-permute-done | bytes 98336 | tf_op jit(solution)/shard_map/ppermute | solution.py:83
  111.8 0.9 update_rows.1
  112.8 0.0 collective-permute-done.13.right
  112.8 0.0 collective-permute-done.12.left
  112.8 1.8 %key_value_sum.1 = (bf16[128,2048]{1,0:T(8,128)(2,1)}, bf16[128,2048]{1,0:T(8,128)(2,1)}) custom-call(s32[1,8]{1,0:T(1,128)S(1)} %copy-done.6, f32[128,2048]{1,0:T(8,128)S(1)} %get-tuple-element.29.dko, f32[128,2048]{1,0:T(8,128)S(1)} %get-tuple-element.30.dvo, bf16[2,128,2048]{2,1,0:T(8,128)(2,1)S(1)} %collective-permute-done.12.left, ...), custom_call_target="tpu_custom_call" | custom-call | flops 1572864 | bytes 5242880 | tf_op jit(solution)/shard_map/key_value_sum/pallas_call | solution.py:389
  (12 shorter events, 0.2 us)
Async XLA Ops:
  1.9 11.4 %collective-permute-start.1 = (bf16[2,128,2048]{2,1,0:T(8,128)(2,1)S(1)}, bf16[2,128,2048]{2,1,0:T(8,128)(2,1)S(1)}, u32[]{:S(2)}, u32[]{:S(2)}) collective-permute-start(bf16[2,128,2048]{2,1,0:T(8,128)(2,1)S(1)} %pad_maximum_fusion.1), channel_id=1, source_target_pairs={{1,0},{3,2},{4,3},{5,4},{6,5},{7,6},{9,8},{11,10},{12,11},{13,12},... | collective-permute-start | bytes 3145736 | tf_op jit(solution)/shard_map/ppermute | solution.py:256
  4.0 21.8 %collective-permute-start = (bf16[2,128,2048]{2,1,0:T(8,128)(2,1)S(1)}, bf16[2,128,2048]{2,1,0:T(8,128)(2,1)S(1)}, u32[]{:S(2)}, u32[]{:S(2)}) collective-permute-start(bf16[2,128,2048]{2,1,0:T(8,128)(2,1)S(1)} %pad_maximum_fusion.1), channel_id=1, source_target_pairs={{0,1},{1,2},{2,3},{3,4},{4,5},{6,7},{8,9},{9,10},{10,11},{11,12},{... | collective-permute-start | bytes 3145736 | tf_op jit(solution)/shard_map/ppermute | solution.py:255
  7.8 18.0 %copy-start = (bf16[1,1,128,2048]{3,2,1,0:T(8,128)(2,1)S(1)}, bf16[1,1,128,2048]{3,2,1,0:T(8,128)(2,1)}, u32[]{:S(2)}) copy-start(bf16[1,1,128,2048]{3,2,1,0:T(8,128)(2,1)} %param.7) | copy-start | bytes 1572868
  7.8 18.0 %copy-start.1 = (bf16[1,1,128,2048]{3,2,1,0:T(8,128)(2,1)S(1)}, bf16[1,1,128,2048]{3,2,1,0:T(8,128)(2,1)}, u32[]{:S(2)}) copy-start(bf16[1,1,128,2048]{3,2,1,0:T(8,128)(2,1)} %param.8) | copy-start | bytes 1572868
  7.8 18.0 %copy-start.4 = (bf16[1,1,128,2048]{3,2,1,0:T(8,128)(2,1)S(1)}, bf16[1,1,128,2048]{3,2,1,0:T(8,128)(2,1)}, u32[]{:S(2)}) copy-start(bf16[1,1,128,2048]{3,2,1,0:T(8,128)(2,1)} %param.6) | copy-start | bytes 1572868
  7.8 18.0 %copy-start.6 = (s32[1,8]{1,0:T(1,128)S(1)}, s32[1,8]{1,0:T(1,128)}, u32[]{:S(2)}) copy-start(s32[1,8]{1,0:T(1,128)} %near_ref.5) | copy-start | bytes 100
  9.3 28.0 %collective-permute-start.7 = (bf16[128,1536]{1,0:T(8,128)(2,1)S(1)}, bf16[128,1536]{1,0:T(8,128)(2,1)S(1)}, u32[]{:S(2)}, u32[]{:S(2)}) collective-permute-start(bf16[128,1536]{1,0:T(8,128)(2,1)S(1)} %get-tuple-element.57), channel_id=1, source_target_pairs={{0,4},{1,5},{2,6},{3,7},{4,0},{5,1},{6,2},{7,3},{8,12},{9,13},{10,... | collective-permute-start | bytes 1179656 | tf_op jit(solution)/shard_map/ppermute | solution.py:83
  9.5 27.7 %collective-permute-start.8 = (bf16[128,1536]{1,0:T(8,128)(2,1)S(1)}, bf16[128,1536]{1,0:T(8,128)(2,1)S(1)}, u32[]{:S(2)}, u32[]{:S(2)}) collective-permute-start(bf16[128,1536]{1,0:T(8,128)(2,1)S(1)} %pad_maximum_fusion.3), channel_id=1, source_target_pairs={{0,6},{1,7},{2,4},{3,5},{4,2},{5,3},{6,0},{7,1},{8,14},{9,15},{10,... | collective-permute-start | bytes 1179656 | tf_op jit(solution)/shard_map/ppermute | solution.py:83
  13.3 26.2 %collective-permute-start.6 = (bf16[128,1536]{1,0:T(8,128)(2,1)S(1)}, bf16[128,1536]{1,0:T(8,128)(2,1)S(1)}, u32[]{:S(2)}, u32[]{:S(2)}) collective-permute-start(bf16[128,1536]{1,0:T(8,128)(2,1)S(1)} %pad_maximum_fusion.3), channel_id=1, source_target_pairs={{0,2},{1,3},{2,0},{3,1},{4,6},{5,7},{6,4},{7,5},{8,10},{9,11},{10,... | collective-permute-start | bytes 1179656 | tf_op jit(solution)/shard_map/ppermute | solution.py:83
  13.3 14.8 %copy-start.2 = (bf16[2,128,2048]{2,1,0:T(8,128)(2,1)}, bf16[2,128,2048]{2,1,0:T(8,128)(2,1)S(1)}, u32[]{:S(2)}) copy-start(bf16[2,128,2048]{2,1,0:T(8,128)(2,1)S(1)} %collective-permute-done.1.right) | copy-start | bytes 3145732
  25.8 2.3 %copy-start.3 = (bf16[2,128,2048]{2,1,0:T(8,128)(2,1)}, bf16[2,128,2048]{2,1,0:T(8,128)(2,1)S(1)}, u32[]{:S(2)}) copy-start(bf16[2,128,2048]{2,1,0:T(8,128)(2,1)S(1)} %collective-permute-done.left) | copy-start | bytes 3145732
  28.1 11.6 %collective-permute-start.2 = (bf16[2,512,128]{2,1,0:T(8,128)(2,1)S(1)}, bf16[2,512,128]{2,1,0:T(8,128)(2,1)S(1)}, u32[]{:S(2)}, u32[]{:S(2)}) collective-permute-start(bf16[2,512,128]{2,1,0:T(8,128)(2,1)S(1)} %get-tuple-element.33), channel_id=1, source_target_pairs={{0,1},{1,0},{2,3},{3,2},{4,5},{5,4},{6,7},{7,6},{8,9},{9,8},{10,11... | collective-permute-start | bytes 786440 | tf_op jit(solution)/shard_map/ppermute | solution.py:83
  39.7 3.0 %copy-start.5 = (bf16[1,1,128,2048]{3,2,1,0:T(8,128)(2,1)S(1)}, bf16[1,1,128,2048]{3,2,1,0:T(8,128)(2,1)}, u32[]{:S(2)}) copy-start(bf16[1,1,128,2048]{3,2,1,0:T(8,128)(2,1)} %param.9) | copy-start | bytes 1572868
  39.7 15.6 %collective-permute-start.9 = (bf16[4,128,1536]{2,1,0:T(8,128)(2,1)S(1)}, bf16[4,128,1536]{2,1,0:T(8,128)(2,1)S(1)}, u32[]{:S(2)}, u32[]{:S(2)}) collective-permute-start(bf16[4,128,1536]{2,1,0:T(8,128)(2,1)S(1)} %pad_maximum_fusion.refs_4_), channel_id=1, source_target_pairs={{0,1},{1,0},{2,3},{3,2},{4,5},{5,4},{6,7},{7,6},{8,9},{9,8},{10,11... | collective-permute-start | bytes 4718600 | tf_op jit(solution)/shard_map/ppermute | solution.py:83
  39.9 7.8 %collective-permute-start.3 = (bf16[2,512,128]{2,1,0:T(8,128)(2,1)S(1)}, bf16[2,512,128]{2,1,0:T(8,128)(2,1)S(1)}, u32[]{:S(2)}, u32[]{:S(2)}) collective-permute-start(bf16[2,512,128]{2,1,0:T(8,128)(2,1)S(1)} %pad_maximum_fusion.4.refs_0_), channel_id=1, source_target_pairs={{0,2},{1,3},{2,0},{3,1},{4,6},{5,7},{6,4},{7,5},{8,10},{9,11},{10,... | collective-permute-start | bytes 786440 | tf_op jit(solution)/shard_map/ppermute | solution.py:83
  40.0 14.4 %collective-permute-start.5 = (bf16[2,512,128]{2,1,0:T(8,128)(2,1)S(1)}, bf16[2,512,128]{2,1,0:T(8,128)(2,1)S(1)}, u32[]{:S(2)}, u32[]{:S(2)}) collective-permute-start(bf16[2,512,128]{2,1,0:T(8,128)(2,1)S(1)} %pad_maximum_fusion.5), channel_id=1, source_target_pairs={{0,6},{1,7},{2,4},{3,5},{4,2},{5,3},{6,0},{7,1},{8,14},{9,15},{10,... | collective-permute-start | bytes 786440 | tf_op jit(solution)/shard_map/ppermute | solution.py:83
  42.4 12.9 %collective-permute-start.4 = (bf16[2,512,128]{2,1,0:T(8,128)(2,1)S(1)}, bf16[2,512,128]{2,1,0:T(8,128)(2,1)S(1)}, u32[]{:S(2)}, u32[]{:S(2)}) collective-permute-start(bf16[2,512,128]{2,1,0:T(8,128)(2,1)S(1)} %pad_maximum_fusion.5), channel_id=1, source_target_pairs={{0,4},{1,5},{2,6},{3,7},{4,0},{5,1},{6,2},{7,3},{8,12},{9,13},{10,... | collective-permute-start | bytes 786440 | tf_op jit(solution)/shard_map/ppermute | solution.py:83
  55.3 1.2 %copy-start.7 = (bf16[4,128,1536]{2,1,0:T(8,128)(2,1)}, bf16[4,128,1536]{2,1,0:T(8,128)(2,1)S(1)}, u32[]{:S(2)}) copy-start(bf16[4,128,1536]{2,1,0:T(8,128)(2,1)S(1)} %collective-permute-done.9.refs_5_) | copy-start | bytes 4718596
  59.8 5.0 %collective-permute-start.10 = (bf16[128,768]{1,0:T(8,128)(2,1)S(1)}, bf16[128,768]{1,0:T(8,128)(2,1)S(1)}, u32[]{:S(2)}, u32[]{:S(2)}) collective-permute-start(bf16[128,768]{1,0:T(8,128)(2,1)S(1)} %get-tuple-element.36), channel_id=1, source_target_pairs={{0,8},{8,0},{16,24},{24,16},{1,9},{9,1},{17,25},{25,17},{2,10},{10... | collective-permute-start | bytes 589832 | tf_op jit(solution)/shard_map/ppermute | solution.py:83
  61.1 7.9 %collective-permute-start.11 = (bf16[128,768]{1,0:T(8,128)(2,1)S(1)}, bf16[128,768]{1,0:T(8,128)(2,1)S(1)}, u32[]{:S(2)}, u32[]{:S(2)}) collective-permute-start(bf16[128,768]{1,0:T(8,128)(2,1)S(1)} %get-tuple-element.37), channel_id=1, source_target_pairs={{0,8},{8,0},{16,24},{24,16},{1,9},{9,1},{17,25},{25,17},{2,10},{10... | collective-permute-start | bytes 589832 | tf_op jit(solution)/shard_map/ppermute | solution.py:83
  69.0 43.8 %collective-permute-start.13 = (bf16[2,128,2048]{2,1,0:T(8,128)(2,1)S(1)}, bf16[2,128,2048]{2,1,0:T(8,128)(2,1)S(1)}, u32[]{:S(2)}, u32[]{:S(2)}) collective-permute-start(bf16[2,128,2048]{2,1,0:T(8,128)(2,1)S(1)} %get-tuple-element.38), channel_id=1, source_target_pairs={{1,0},{2,1},{3,2},{4,3},{5,4},{7,6},{9,8},{10,9},{11,10},{12,11},{... | collective-permute-start | bytes 3145736 | tf_op jit(solution)/shard_map/ppermute | solution.py:402
  73.3 39.5 %collective-permute-start.12 = (bf16[2,128,2048]{2,1,0:T(8,128)(2,1)S(1)}, bf16[2,128,2048]{2,1,0:T(8,128)(2,1)S(1)}, u32[]{:S(2)}, u32[]{:S(2)}) collective-permute-start(bf16[2,128,2048]{2,1,0:T(8,128)(2,1)S(1)} %get-tuple-element.38), channel_id=1, source_target_pairs={{0,1},{2,3},{3,4},{4,5},{5,6},{6,7},{8,9},{10,11},{11,12},{12,13},... | collective-permute-start | bytes 3145736 | tf_op jit(solution)/shard_map/ppermute | solution.py:401
  74.8 10.9 %collective-permute-start.14 = (bf16[128,768]{1,0:T(8,128)(2,1)S(1)}, bf16[128,768]{1,0:T(8,128)(2,1)S(1)}, u32[]{:S(2)}, u32[]{:S(2)}) collective-permute-start(bf16[128,768]{1,0:T(8,128)(2,1)S(1)} %add_convert_fusion.1), channel_id=1, source_target_pairs={{0,16},{8,24},{16,0},{24,8},{1,17},{9,25},{17,1},{25,9},{2,18},{10... | collective-permute-start | bytes 589832 | tf_op jit(solution)/shard_map/ppermute | solution.py:83
  77.2 16.5 %collective-permute-start.16 = (bf16[128,1536]{1,0:T(8,128)(2,1)S(1)}, bf16[128,1536]{1,0:T(8,128)(2,1)S(1)}, u32[]{:S(2)}, u32[]{:S(2)}) collective-permute-start(bf16[128,1536]{1,0:T(8,128)(2,1)S(1)} %get-tuple-element.45), channel_id=1, source_target_pairs={{0,8},{8,0},{16,24},{24,16},{1,9},{9,1},{17,25},{25,17},{2,10},{10... | collective-permute-start | bytes 1179656 | tf_op jit(solution)/shard_map/ppermute | solution.py:83
  78.5 14.4 %collective-permute-start.15 = (bf16[128,768]{1,0:T(8,128)(2,1)S(1)}, bf16[128,768]{1,0:T(8,128)(2,1)S(1)}, u32[]{:S(2)}, u32[]{:S(2)}) collective-permute-start(bf16[128,768]{1,0:T(8,128)(2,1)S(1)} %add_convert_fusion), channel_id=1, source_target_pairs={{0,16},{8,24},{16,0},{24,8},{1,17},{9,25},{17,1},{25,9},{2,18},{10... | collective-permute-start | bytes 589832 | tf_op jit(solution)/shard_map/ppermute | solution.py:83
  94.5 4.6 %collective-permute-start.17 = (f32[128,128]{1,0:T(8,128)S(1)}, f32[128,128]{1,0:T(8,128)S(1)}, u32[]{:S(2)}, u32[]{:S(2)}) collective-permute-start(f32[128,128]{1,0:T(8,128)S(1)} %get-tuple-element.47.gram), channel_id=1, source_target_pairs={{0,2},{1,3},{2,0},{3,1},{4,6},{5,7},{6,4},{7,5},{8,10},{9,11},{10,... | collective-permute-start | bytes 196616 | tf_op jit(solution)/shard_map/ppermute | solution.py:83
  103.0 3.9 %collective-permute-start.18 = (bf16[128,384]{1,0:T(8,128)(2,1)S(1)}, bf16[128,384]{1,0:T(8,128)(2,1)S(1)}, u32[]{:S(2)}, u32[]{:S(2)}) collective-permute-start(bf16[128,384]{1,0:T(8,128)(2,1)S(1)} %get-tuple-element.49), channel_id=1, source_target_pairs={{0,1},{1,0},{2,3},{3,2},{4,5},{5,4},{6,7},{7,6},{8,9},{9,8},{10,11... | collective-permute-start | bytes 294920 | tf_op jit(solution)/shard_map/ppermute | solution.py:83
  105.2 4.4 %collective-permute-start.19 = (bf16[128,384]{1,0:T(8,128)(2,1)S(1)}, bf16[128,384]{1,0:T(8,128)(2,1)S(1)}, u32[]{:S(2)}, u32[]{:S(2)}) collective-permute-start(bf16[128,384]{1,0:T(8,128)(2,1)S(1)} %get-tuple-element.50), channel_id=1, source_target_pairs={{0,4},{1,5},{2,6},{3,7},{4,0},{5,1},{6,2},{7,3},{8,12},{9,13},{10,... | collective-permute-start | bytes 294920 | tf_op jit(solution)/shard_map/ppermute | solution.py:83
  105.3 6.6 %collective-permute-start.20 = (bf16[128,384]{1,0:T(8,128)(2,1)S(1)}, bf16[128,384]{1,0:T(8,128)(2,1)S(1)}, u32[]{:S(2)}, u32[]{:S(2)}) collective-permute-start(bf16[128,384]{1,0:T(8,128)(2,1)S(1)} %get-tuple-element.51), channel_id=1, source_target_pairs={{0,5},{1,4},{2,7},{3,6},{4,1},{5,0},{6,3},{7,2},{8,13},{9,12},{10,... | collective-permute-start | bytes 294920 | tf_op jit(solution)/shard_map/ppermute | solution.py:83

commit v3 on v2

--- a/solution.py
+++ b/solution.py
@@ -18,7 +18,7 @@
 coeff_c = 2.0315
 f32 = jnp.float32
 bf16 = jnp.bfloat16
-VMEM_LIMIT = 48 * 1024 * 1024
+VMEM_LIMIT = 24 * 1024 * 1024
 
 
 def whole(count):
@@ -94,22 +94,24 @@
     return powers * (1.0 / jnp.sum(powers, axis=0, keepdims=True))
 
 
-def choose_far(near_ref, left, right, far):
+def choose_far(near_ref, key_left, value_left, key_right, value_right, far):
     place = lax.axis_index("seq")
     go_left = near_ref[0, place] < place
 
     @pl.when(go_left)
     def _():
-        far[...] = left[...]
+        far[0] = key_left[...]
+        far[1] = value_left[...]
 
     @pl.when(jnp.logical_not(go_left))
     def _():
-        far[...] = right[...]
-
-
-def forward_kernel(plan, near_ref, q, ko, vo, left, right, keep, give, far):
+        far[0] = key_right[...]
+        far[1] = value_right[...]
+
+
+def forward_kernel(plan, near_ref, q, ko, vo, kl, vl, kr, vr, keep, give, far):
     layer = lax.axis_index("dp")
-    choose_far(near_ref, left, right, far)
+    choose_far(near_ref, kl, vl, kr, vr, far)
     mine = plan.row_part(lax.axis_index("seq"))
     jobs = [(j, i) for j in range(plan.per_target) for i in range(plan.dp)]
     for first in range(0, len(jobs), GROUP):
@@ -125,8 +127,8 @@
             out[j >> 1, i * HEAD_DIM : (i + 1) * HEAD_DIM, :] = dot_l(values, p).astype(bf16)
 
 
-def backward_kernel(near_ref, q, ko, vo, left, right, g, dq, dko, dvo, dfar, far):
-    choose_far(near_ref, left, right, far)
+def backward_kernel(near_ref, q, ko, vo, kl, vl, kr, vr, g, dq, dko, dvo, dfar, far):
+    choose_far(near_ref, kl, vl, kr, vr, far)
     tile = q.shape[0]
     count = q.shape[1] // HEAD_DIM
     for first in range(0, count, GROUP):
@@ -251,9 +253,11 @@
 
     to_right = [(i, i + 1) for i in range(n - 1) if i + 1 != n - 2]
     to_left = [(i + 1, i) for i in range(n - 1) if i != 1]
-    stacked = jnp.stack([key, value])
-    left = lax.ppermute(stacked, "seq", to_right)
-    right = lax.ppermute(stacked, "seq", to_left)
+    key_left = lax.ppermute(key, "seq", to_right)
+    key_right = lax.ppermute(key, "seq", to_left)
+    value_left = lax.ppermute(value, "seq", to_right)
+    value_right = lax.ppermute(value, "seq", to_left)
+    beside = (key_left, value_left, key_right, value_right)
 
     slot = depth // n
     flat = proj_grad.reshape(tile, depth)
@@ -270,20 +274,20 @@
         )
 
     columns = [column_part(mine)] + [
-        shift(column_part(mine ^ (t & (plan.col - 1))), "seq", t << 1)
+        shift(after(column_part(mine ^ (t & (plan.col - 1))), key_left, key_right), "seq", t << 1)
         for t in range(1, plan.pairs)
     ]
 
     keep, give = pl.pallas_call(
         functools.partial(forward_kernel, plan),
         out_shape=[struct((plan.high, m * HEAD_DIM, tile), bf16)] * 2,
-        in_specs=[smem()] + whole(5),
+        in_specs=[smem()] + whole(7),
         out_specs=whole(2),
         scratch_shapes=[pltpu.VMEM((2, tile, width), bf16)],
         compiler_params=params(),
         cost_estimate=cost(8 * tile * tile * width, 16 * tile * width, 2 * tile * tile * head_count),
         name="attention_forward",
-    )(neighbour, query, key, value, left, right)
+    )(neighbour, query, key, value, *beside)
 
     got = shift(give, "seq", 1)
     rows = [jnp.stack([keep[high], got[high]]) for high in range(plan.high)]
@@ -301,13 +305,13 @@
             struct((tile, width), f32),
             struct((2, tile, width), bf16),
         ],
-        in_specs=[smem()] + whole(6),
+        in_specs=[smem()] + whole(8),
         out_specs=whole(4),
         scratch_shapes=[pltpu.VMEM((2, tile, width), bf16)],
         compiler_params=params(),
         cost_estimate=cost(28 * tile * tile * width, 30 * tile * width, 2 * tile * tile * head_count),
         name="attention_backward",
-    )(neighbour, query, key, value, left, right, grad)
+    )(neighbour, query, key, value, *beside, grad)
 
     half = mine_width // 2
     spots = [(0, 0, mine_width), (1, 0, mine_width)]
@@ -370,22 +374,9 @@
         cost_estimate=cost(12 * HEAD_DIM * HEAD_DIM * mine_width, 8 * HEAD_DIM * mine_width),
         name="newton_schulz",
     )(x, gram, gram_other)
-    pieces = [pieces[0]] + [
-        shift(pieces[j], "seq", plan.row_mask(j)) for j in range(1, per)
-    ]
-    update = pl.pallas_call(
-        functools.partial(place_kernel, plan),
-        out_shape=struct((per * HEAD_DIM, slot), f32),
-        in_specs=whole(per),
-        out_specs=pl.BlockSpec(memory_space=pltpu.VMEM),
-        compiler_params=params(),
-        cost_estimate=cost(1, 8 * per * HEAD_DIM * slot),
-        name="update_rows",
-    )(*pieces)
-
     far_right = [(i, i + 1) for i in range(n - 1) if i != 1]
     far_left = [(i + 1, i) for i in range(n - 1) if i + 1 != n - 2]
-    dfar = after(dfar, *first_step)
+    dfar = after(dfar, total[1, 0])
     dk, dv = pl.pallas_call(
         combine_kernel,
         out_shape=[struct((tile, width), bf16)] * 2,
@@ -402,6 +393,19 @@
         lax.ppermute(dfar, "seq", far_left),
     )
 
+    pieces = [pieces[0]] + [
+        shift(pieces[j], "seq", plan.row_mask(j)) for j in range(1, per)
+    ]
+    update = pl.pallas_call(
+        functools.partial(place_kernel, plan),
+        out_shape=struct((per * HEAD_DIM, slot), f32),
+        in_specs=whole(per),
+        out_specs=pl.BlockSpec(memory_space=pltpu.VMEM),
+        compiler_params=params(),
+        cost_estimate=cost(1, 8 * per * HEAD_DIM * slot),
+        name="update_rows",
+    )(after(pieces[0], dk), *pieces[1:])
+
     shape = query_tiles.shape
     return dq.reshape(shape), dk.reshape(shape), dv.reshape(shape), update
 

time: 115 us -> 107 us (0.930)
  waiting for transfers between devices: 60.6 us -> 51.8 us
  starting transfers between devices: 30.6 us -> 36.4 us
  Pallas kernels: 18.1 us -> 15.5 us
  other arithmetic: 1.7 us -> 0.42 us
  local copies, waits for them, and re-layouts: 2.66 us -> 1.45 us
    ppermute x2 -> x4, waiting for transfers between devices: 12.5 us -> 0.57 us  [the longest x1 0.53 us: local(): key_left = lax.ppermute(key, 'seq', to_right)]
    ppermute x2 -> x4, starting transfers between devices: 5.8 us -> 10.1 us  [the longest x1 3.81 us: local(): key_left = lax.ppermute(key, 'seq', to_right)]
    ppermute x17, waiting for transfers between devices: 48.2 us -> 51.2 us  [shift(): lax.ppermute(value, axis, [(i, i ^ mask) for i in range(lax.axis_size(axi...]
    ppermute x17, starting transfers between devices: 19.1 us -> 21.2 us  [shift(): lax.ppermute(value, axis, [(i, i ^ mask) for i in range(lax.axis_size(axi...]
    pallas_call x1, Pallas kernels: 3.27 us -> 1.88 us  [local(): pl.pallas_call(functools.partial(product_kernel, plan, spots), out_shape=...]
    another operation x1 -> x0, other arithmetic: 1.3 us -> none  [local(): stacked = jnp.stack([key, value])]
    unnamed x16 -> x10, local copies, waits for them, and re-layouts: 1.24 us -> 0.02 us
  transfers between devices with their start and end apart: 21 -> 23, of which waited for: 13 -> 12; matrix products, arithmetic and copies ran while one was open for 2% -> 2% of each run, Pallas kernels for 11% -> 12%
where the time goes in v3:
time: 107 us
  waiting for transfers between devices  51.8 us (48%)
  starting transfers between devices  36.4 us (34%)
  Pallas kernels  15.5 us (14%)
  local copies, waits for them, and re-layouts  1.45 us (1%)
    ppermute x17, waiting for transfers between devices, shift(): lax.ppermute(value, axis, [(i, i ^ mask) for i in range(lax.axis_size(axi...  51.2 us
    ppermute x17, starting transfers between devices, shift(): lax.ppermute(value, axis, [(i, i ^ mask) for i in range(lax.axis_size(axi...  21.2 us
    pallas_call x1, Pallas kernels, local(): pl.pallas_call(functools.partial(update_kernel, plan, factor), out_shape=...  3.93 us
    pallas_call x1, Pallas kernels, local(): pl.pallas_call(backward_kernel, out_shape=[struct((tile, width), bf16), s...  3.9 us
    ppermute x1, starting transfers between devices, local(): key_left = lax.ppermute(key, 'seq', to_right)  3.81 us
    ppermute x1, starting transfers between devices, local(): lax.ppermute(dfar, 'seq', far_left)  3.62 us
    ppermute x1, starting transfers between devices, local(): value_left = lax.ppermute(value, 'seq', to_right)  3 us
    pallas_call x1, Pallas kernels, local(): pl.pallas_call(functools.partial(forward_kernel, plan), out_shape=[struct...  2.29 us
  transfers between devices with their start and end apart: 23, of which 12 were waited for; matrix products, arithmetic and copies ran while one was open for 2% of the time, Pallas kernels for 12%

profile of v3, /device:TPU:1, one launch (start us, length us, event | category | flops | bytes accessed | tf_op | source)
XLA Modules:
  0.0 106.6 jit_solution(1827765586592494702)
XLA Ops:
  0.6 2.0 %collective-permute-start.2 = (bf16[128,2048]{1,0:T(8,128)(2,1)}, bf16[128,2048]{1,0:T(8,128)(2,1)S(1)}, u32[]{:S(2)}, u32[]{:S(2)}) collective-permute-start(bf16[128,2048]{1,0:T(8,128)(2,1)} %bitcast.22), channel_id=1, source_target_pairs={{1,0},{3,2},{4,3},{5,4},{6,5},{7,6},{9,8},{11,10},{12,11},{13,12},... | collective-permute-start | bytes 1572872 | tf_op jit(solution)/shard_map/ppermute | solution.py:257
  2.6 3.8 %collective-permute-start = (bf16[128,2048]{1,0:T(8,128)(2,1)}, bf16[128,2048]{1,0:T(8,128)(2,1)S(1)}, u32[]{:S(2)}, u32[]{:S(2)}) collective-permute-start(bf16[128,2048]{1,0:T(8,128)(2,1)} %bitcast.23), channel_id=1, source_target_pairs={{0,1},{1,2},{2,3},{3,4},{4,5},{6,7},{8,9},{9,10},{10,11},{11,12},{... | collective-permute-start | bytes 1572872 | tf_op jit(solution)/shard_map/ppermute | solution.py:256
  6.4 1.3 %collective-permute-start.3 = (bf16[128,2048]{1,0:T(8,128)(2,1)}, bf16[128,2048]{1,0:T(8,128)(2,1)S(1)}, u32[]{:S(2)}, u32[]{:S(2)}) collective-permute-start(bf16[128,2048]{1,0:T(8,128)(2,1)} %bitcast.26), channel_id=1, source_target_pairs={{1,0},{3,2},{4,3},{5,4},{6,5},{7,6},{9,8},{11,10},{12,11},{13,12},... | collective-permute-start | bytes 1572872 | tf_op jit(solution)/shard_map/ppermute | solution.py:259
  7.8 3.0 %collective-permute-start.1 = (bf16[128,2048]{1,0:T(8,128)(2,1)}, bf16[128,2048]{1,0:T(8,128)(2,1)S(1)}, u32[]{:S(2)}, u32[]{:S(2)}) collective-permute-start(bf16[128,2048]{1,0:T(8,128)(2,1)} %bitcast.27), channel_id=1, source_target_pairs={{0,1},{1,2},{2,3},{3,4},{4,5},{6,7},{8,9},{9,10},{10,11},{11,12},{... | collective-permute-start | bytes 1572872 | tf_op jit(solution)/shard_map/ppermute | solution.py:258
  10.8 0.0 copy-start
  10.8 0.0 copy-start.1
  10.8 0.0 copy-start.2
  10.8 0.0 copy-start.4
  10.8 1.4 %dynamic-slice_bitcast_fusion.3 = (bf16[128,768]{1,0:T(8,128)(2,1)S(1)}, bf16[128,768]{1,0:T(8,128)(2,1)S(1)}, bf16[128,768]{1,0:T(8,128)(2,1)S(1)}, bf16[128,768]{1,0:T(8,128)(2,1)S(1)}) fusion(bf16[1,1,128,3072]{3,2,1,0:T(8,128)(2,1)} %param.10, s32[]{:T(128)S(6)} %select_n.16, s32[]{:T(128)S(6)} %select_n.17, s32[]{:T(128)S(6)} %select_n.19, s32[]{:T(128)S(6)} %select_n.18), kind=kLoop, calls=%fused_computation.10 | loop fusion | bytes 1572880 | tf_op jit(solution)/shard_map/dynamic_slice | solution.py:270
  12.3 0.1 fusion
  12.3 0.0 collective-permute-done.2.kr
  12.3 0.5 collective-permute-done.kl
  12.9 0.9 collective-permute-start.9
  13.7 4.7 %collective-permute-start.10 = (bf16[128,1536]{1,0:T(8,128)(2,1)S(1)}, bf16[128,1536]{1,0:T(8,128)(2,1)S(1)}, u32[]{:S(2)}, u32[]{:S(2)}) collective-permute-start(bf16[128,1536]{1,0:T(8,128)(2,1)S(1)} %pad_maximum_fusion.2), channel_id=1, source_target_pairs={{0,6},{1,7},{2,4},{3,5},{4,2},{5,3},{6,0},{7,1},{8,14},{9,15},{10,... | collective-permute-start | bytes 1179656 | tf_op jit(solution)/shard_map/ppermute | solution.py:83
  18.4 0.0 collective-permute-start.8
  18.4 0.0 collective-permute-done.3.vr
  18.4 0.0 collective-permute-done.1.vl
  18.5 0.0 copy-done
  18.5 0.0 copy-done.1
  18.5 0.0 copy-done.4
  18.5 2.3 %attention_forward.1 = (bf16[2,512,128]{2,1,0:T(8,128)(2,1)S(1)}, bf16[2,512,128]{2,1,0:T(8,128)(2,1)S(1)}) custom-call(s32[1,8]{1,0:T(1,128)S(1)} %copy-done.4, bf16[128,2048]{1,0:T(8,128)(2,1)S(1)} %bitcast.20, bf16[128,2048]{1,0:T(8,128)(2,1)S(1)} %bitcast.24, bf16[128,2048]{1,0:T(8,128)(2,1)S(1)} %bitcast.28, ...), custom_call_target="tpu_custom_call" | custom-call | flops 268435456 | bytes 4194304 | tf_op jit(solution)/shard_map/attention_forward/pallas_call | solution.py:281
  20.8 1.2 %collective-permute-start.4 = (bf16[2,512,128]{2,1,0:T(8,128)(2,1)S(1)}, bf16[2,512,128]{2,1,0:T(8,128)(2,1)S(1)}, u32[]{:S(2)}, u32[]{:S(2)}) collective-permute-start(bf16[2,512,128]{2,1,0:T(8,128)(2,1)S(1)} %get-tuple-element.36), channel_id=1, source_target_pairs={{0,1},{1,0},{2,3},{3,2},{4,5},{5,4},{6,7},{7,6},{8,9},{9,8},{10,11... | collective-permute-start | bytes 786440 | tf_op jit(solution)/shard_map/ppermute | solution.py:83
  22.0 14.6 %collective-permute-done.9 = bf16[128,1536]{1,0:T(8,128)(2,1)S(1)} collective-permute-done((bf16[128,1536]{1,0:T(8,128)(2,1)S(1)}, bf16[128,1536]{1,0:T(8,128)(2,1)S(1)}, u32[]{:S(2)}, u32[]{:S(2)}) %collective-permute-start.9) | collective-permute-done | bytes 393248 | tf_op jit(solution)/shard_map/ppermute | solution.py:83
  36.6 0.0 collective-permute-done.10
  36.6 2.6 %collective-permute-done.8 = bf16[128,1536]{1,0:T(8,128)(2,1)S(1)} collective-permute-done((bf16[128,1536]{1,0:T(8,128)(2,1)S(1)}, bf16[128,1536]{1,0:T(8,128)(2,1)S(1)}, u32[]{:S(2)}, u32[]{:S(2)}) %collective-permute-start.8) | collective-permute-done | bytes 393248 | tf_op jit(solution)/shard_map/ppermute | solution.py:83
  39.3 0.2 pad_maximum_fusion.refs_4_
  39.5 0.0 copy-start.3
  39.5 0.0 collective-permute-done.4
  39.5 0.1 collective-permute-start.11
  39.7 0.1 collective-permute-start.5
  39.8 2.2 %collective-permute-start.7 = (bf16[2,512,128]{2,1,0:T(8,128)(2,1)S(1)}, bf16[2,512,128]{2,1,0:T(8,128)(2,1)S(1)}, u32[]{:S(2)}, u32[]{:S(2)}) collective-permute-start(bf16[2,512,128]{2,1,0:T(8,128)(2,1)S(1)} %pad_maximum_fusion.4), channel_id=1, source_target_pairs={{0,6},{1,7},{2,4},{3,5},{4,2},{5,3},{6,0},{7,1},{8,14},{9,15},{10,... | collective-permute-start | bytes 786440 | tf_op jit(solution)/shard_map/ppermute | solution.py:83
  42.0 0.5 collective-permute-start.6
  42.5 3.9 %attention_backward.1 = (bf16[128,2048]{1,0:T(8,128)(2,1)}, f32[128,2048]{1,0:T(8,128)S(1)}, f32[128,2048]{1,0:T(8,128)S(1)}, bf16[2,128,2048]{2,1,0:T(8,128)(2,1)S(1)}) custom-call(s32[1,8]{1,0:T(1,128)S(1)} %copy-done.4, bf16[128,2048]{1,0:T(8,128)(2,1)S(1)} %bitcast.21, bf16[128,2048]{1,0:T(8,128)(2,1)S(1)} %bitcast.25, bf16[128,2048]{1,0:T(8,128)(2,1)S(1)} %bitcast.29, ...), custom_call_target="tpu_custom_call" | custom-call | flops 939524096 | bytes 7864320 | tf_op jit(solution)/shard_map/attention_backward/pallas_call | solution.py:300
  46.4 0.7 collective-permute-done.5.refs_1_
  47.1 6.9 %collective-permute-done.7.refs_3_ = bf16[2,512,128]{2,1,0:T(8,128)(2,1)S(1)} collective-permute-done((bf16[2,512,128]{2,1,0:T(8,128)(2,1)S(1)}, bf16[2,512,128]{2,1,0:T(8,128)(2,1)S(1)}, u32[]{:S(2)}, u32[]{:S(2)}) %collective-permute-start.7) | collective-permute-done | bytes 262176 | tf_op jit(solution)/shard_map/ppermute | solution.py:83
  54.0 0.9 collective-permute-done.6.refs_2_
  54.9 0.0 collective-permute-done.11.refs_5_
  54.9 1.9 %gradient_product.1 = (f32[128,1536]{1,0:T(8,128)S(1)}, bf16[128,1536]{1,0:T(8,128)(2,1)S(1)}, f32[128,768]{1,0:T(8,128)S(1)}, f32[128,768]{1,0:T(8,128)S(1)}, b...) custom-call(bf16[2,512,128]{2,1,0:T(8,128)(2,1)S(1)} %pad_maximum_fusion.3.refs_0_, ...), custom_call_target="tpu_custom_call" | custom-call | flops 1610612736 | bytes 4194304 | tf_op jit(solution)/shard_map/gradient_product/pallas_call | solution.py:319
  56.8 1.4 %collective-permute-start.14 = (bf16[128,768]{1,0:T(8,128)(2,1)S(1)}, bf16[128,768]{1,0:T(8,128)(2,1)S(1)}, u32[]{:S(2)}, u32[]{:S(2)}) collective-permute-start(bf16[128,768]{1,0:T(8,128)(2,1)S(1)} %get-tuple-element.47), channel_id=1, source_target_pairs={{0,8},{8,0},{16,24},{24,16},{1,9},{9,1},{17,25},{25,17},{2,10},{10... | collective-permute-start | bytes 589832 | tf_op jit(solution)/shard_map/ppermute | solution.py:83
  58.1 3.6 %collective-permute-start.13 = (bf16[2,128,2048]{2,1,0:T(8,128)(2,1)S(1)}, bf16[2,128,2048]{2,1,0:T(8,128)(2,1)S(1)}, u32[]{:S(2)}, u32[]{:S(2)}) collective-permute-start(bf16[2,128,2048]{2,1,0:T(8,128)(2,1)S(1)} %get-tuple-element.42), channel_id=1, source_target_pairs={{1,0},{2,1},{3,2},{4,3},{5,4},{7,6},{9,8},{10,9},{11,10},{12,11},{... | collective-permute-start | bytes 3145736 | tf_op jit(solution)/shard_map/ppermute | solution.py:393
  61.7 1.5 %collective-permute-start.12 = (bf16[2,128,2048]{2,1,0:T(8,128)(2,1)S(1)}, bf16[2,128,2048]{2,1,0:T(8,128)(2,1)S(1)}, u32[]{:S(2)}, u32[]{:S(2)}) collective-permute-start(bf16[2,128,2048]{2,1,0:T(8,128)(2,1)S(1)} %get-tuple-element.42), channel_id=1, source_target_pairs={{0,1},{2,3},{3,4},{4,5},{5,6},{6,7},{8,9},{10,11},{11,12},{12,13},... | collective-permute-start | bytes 3145736 | tf_op jit(solution)/shard_map/ppermute | solution.py:392
  63.2 0.2 collective-permute-start.16
  63.5 0.0 collective-permute-done.14
  63.5 2.4 %collective-permute-start.15 = (bf16[128,768]{1,0:T(8,128)(2,1)S(1)}, bf16[128,768]{1,0:T(8,128)(2,1)S(1)}, u32[]{:S(2)}, u32[]{:S(2)}) collective-permute-start(bf16[128,768]{1,0:T(8,128)(2,1)S(1)} %add_convert_fusion.1), channel_id=1, source_target_pairs={{0,16},{8,24},{16,0},{24,8},{1,17},{9,25},{17,1},{25,9},{2,18},{10... | collective-permute-start | bytes 589832 | tf_op jit(solution)/shard_map/ppermute | solution.py:83
  65.9 7.2 %collective-permute-done.16 = bf16[128,768]{1,0:T(8,128)(2,1)S(1)} collective-permute-done((bf16[128,768]{1,0:T(8,128)(2,1)S(1)}, bf16[128,768]{1,0:T(8,128)(2,1)S(1)}, u32[]{:S(2)}, u32[]{:S(2)}) %collective-permute-start.16) | collective-permute-done | bytes 196640 | tf_op jit(solution)/shard_map/ppermute | solution.py:83
  73.1 0.0 collective-permute-start.18
  73.1 0.1 collective-permute-start.17
  73.2 0.0 collective-permute-done.15.refs_0_
  73.2 11.0 %collective-permute-done.17.refs_1_ = bf16[128,768]{1,0:T(8,128)(2,1)S(1)} collective-permute-done((bf16[128,768]{1,0:T(8,128)(2,1)S(1)}, bf16[128,768]{1,0:T(8,128)(2,1)S(1)}, u32[]{:S(2)}, u32[]{:S(2)}) %collective-permute-start.17) | collective-permute-done | bytes 196640 | tf_op jit(solution)/shard_map/ppermute | solution.py:83
  84.2 2.5 %collective-permute-done.18.refs_2_ = bf16[128,1536]{1,0:T(8,128)(2,1)S(1)} collective-permute-done((bf16[128,1536]{1,0:T(8,128)(2,1)S(1)}, bf16[128,1536]{1,0:T(8,128)(2,1)S(1)}, u32[]{:S(2)}, u32[]{:S(2)}) %collective-permute-start.18) | collective-permute-done | bytes 393248 | tf_op jit(solution)/shard_map/ppermute | solution.py:83
  86.7 0.8 gradient_sum.1
  87.6 3.9 %collective-permute-start.19 = (f32[128,128]{1,0:T(8,128)S(1)}, f32[128,128]{1,0:T(8,128)S(1)}, u32[]{:S(2)}, u32[]{:S(2)}) collective-permute-start(f32[128,128]{1,0:T(8,128)S(1)} %get-tuple-element.52.gram), channel_id=1, source_target_pairs={{0,2},{1,3},{2,0},{3,1},{4,6},{5,7},{6,4},{7,5},{8,10},{9,11},{10,... | collective-permute-start | bytes 196616 | tf_op jit(solution)/shard_map/ppermute | solution.py:83
  91.4 1.7 %collective-permute-done.19.gram_other = f32[128,128]{1,0:T(8,128)S(1)} collective-permute-done((f32[128,128]{1,0:T(8,128)S(1)}, f32[128,128]{1,0:T(8,128)S(1)}, u32[]{:S(2)}, u32[]{:S(2)}) %collective-permute-start.19) | collective-permute-done | bytes 65568 | tf_op jit(solution)/shard_map/ppermute | solution.py:83
  93.1 3.9 %newton_schulz.1 = (f32[128,384]{1,0:T(8,128)S(1)}, bf16[128,384]{1,0:T(8,128)(2,1)S(1)}, bf16[128,384]{1,0:T(8,128)(2,1)S(1)}, bf16[128,384]{1,0:T(8,128)(2,1)S(1)}) custom-call(f32[128,1536]{1,0:T(8,128)S(1)} %get-tuple-element.51.x, f32[128,128]{1,0:T(8,128)S(1)} %get-tuple-element.52.gram, f32[128,128]{1,0:T(8,128)S(1)} %collective-permute-done.19.gram_other), custom_call_target="tpu_custom_call" | custom-call | flops 301989888 | bytes 1572864 | tf_op jit(solution)/shard_map/newton_schulz/pallas_call | solution.py:368
  97.0 2.0 %collective-permute-start.20 = (bf16[128,384]{1,0:T(8,128)(2,1)S(1)}, bf16[128,384]{1,0:T(8,128)(2,1)S(1)}, u32[]{:S(2)}, u32[]{:S(2)}) collective-permute-start(bf16[128,384]{1,0:T(8,128)(2,1)S(1)} %get-tuple-element.55), channel_id=1, source_target_pairs={{0,1},{1,0},{2,3},{3,2},{4,5},{5,4},{6,7},{7,6},{8,9},{9,8},{10,11... | collective-permute-start | bytes 294920 | tf_op jit(solution)/shard_map/ppermute | solution.py:83
  99.0 0.6 collective-permute-start.21
  99.6 1.1 %collective-permute-start.22 = (bf16[128,384]{1,0:T(8,128)(2,1)S(1)}, bf16[128,384]{1,0:T(8,128)(2,1)S(1)}, u32[]{:S(2)}, u32[]{:S(2)}) collective-permute-start(bf16[128,384]{1,0:T(8,128)(2,1)S(1)} %get-tuple-element.57), channel_id=1, source_target_pairs={{0,5},{1,4},{2,7},{3,6},{4,1},{5,0},{6,3},{7,2},{8,13},{9,12},{10,... | collective-permute-start | bytes 294920 | tf_op jit(solution)/shard_map/ppermute | solution.py:83
  100.7 0.0 collective-permute-done.13.right
  100.7 0.0 collective-permute-done.12.left
  100.7 1.8 %key_value_sum.1 = (bf16[128,2048]{1,0:T(8,128)(2,1)}, bf16[128,2048]{1,0:T(8,128)(2,1)}) custom-call(s32[1,8]{1,0:T(1,128)S(1)} %copy-done.4, f32[128,2048]{1,0:T(8,128)S(1)} %get-tuple-element.32.dko, f32[128,2048]{1,0:T(8,128)S(1)} %get-tuple-element.33.dvo, bf16[2,128,2048]{2,1,0:T(8,128)(2,1)S(1)} %collective-permute-done.12.left, ...), custom_call_target="tpu_custom_call" | custom-call | flops 1572864 | bytes 5242880 | tf_op jit(solution)/shard_map/key_value_sum/pallas_call | solution.py:380
  102.5 0.0 collective-permute-done.20.refs_1_
  102.5 0.9 collective-permute-done.21.refs_2_
  103.4 2.3 %collective-permute-done.22.refs_3_ = bf16[128,384]{1,0:T(8,128)(2,1)S(1)} collective-permute-done((bf16[128,384]{1,0:T(8,128)(2,1)S(1)}, bf16[128,384]{1,0:T(8,128)(2,1)S(1)}, u32[]{:S(2)}, u32[]{:S(2)}) %collective-permute-start.22) | collective-permute-done | bytes 98336 | tf_op jit(solution)/shard_map/ppermute | solution.py:83
  105.6 0.9 update_rows.1
  (9 shorter events, 0.2 us)
Async XLA Ops:
  0.6 11.7 %collective-permute-start.2 = (bf16[128,2048]{1,0:T(8,128)(2,1)}, bf16[128,2048]{1,0:T(8,128)(2,1)S(1)}, u32[]{:S(2)}, u32[]{:S(2)}) collective-permute-start(bf16[128,2048]{1,0:T(8,128)(2,1)} %bitcast.22), channel_id=1, source_target_pairs={{1,0},{3,2},{4,3},{5,4},{6,5},{7,6},{9,8},{11,10},{12,11},{13,12},... | collective-permute-start | bytes 1572872 | tf_op jit(solution)/shard_map/ppermute | solution.py:257
  2.6 10.2 %collective-permute-start = (bf16[128,2048]{1,0:T(8,128)(2,1)}, bf16[128,2048]{1,0:T(8,128)(2,1)S(1)}, u32[]{:S(2)}, u32[]{:S(2)}) collective-permute-start(bf16[128,2048]{1,0:T(8,128)(2,1)} %bitcast.23), channel_id=1, source_target_pairs={{0,1},{1,2},{2,3},{3,4},{4,5},{6,7},{8,9},{9,10},{10,11},{11,12},{... | collective-permute-start | bytes 1572872 | tf_op jit(solution)/shard_map/ppermute | solution.py:256
  6.4 12.0 %collective-permute-start.3 = (bf16[128,2048]{1,0:T(8,128)(2,1)}, bf16[128,2048]{1,0:T(8,128)(2,1)S(1)}, u32[]{:S(2)}, u32[]{:S(2)}) collective-permute-start(bf16[128,2048]{1,0:T(8,128)(2,1)} %bitcast.26), channel_id=1, source_target_pairs={{1,0},{3,2},{4,3},{5,4},{6,5},{7,6},{9,8},{11,10},{12,11},{13,12},... | collective-permute-start | bytes 1572872 | tf_op jit(solution)/shard_map/ppermute | solution.py:259
  7.8 10.7 %collective-permute-start.1 = (bf16[128,2048]{1,0:T(8,128)(2,1)}, bf16[128,2048]{1,0:T(8,128)(2,1)S(1)}, u32[]{:S(2)}, u32[]{:S(2)}) collective-permute-start(bf16[128,2048]{1,0:T(8,128)(2,1)} %bitcast.27), channel_id=1, source_target_pairs={{0,1},{1,2},{2,3},{3,4},{4,5},{6,7},{8,9},{9,10},{10,11},{11,12},{... | collective-permute-start | bytes 1572872 | tf_op jit(solution)/shard_map/ppermute | solution.py:258
  10.8 7.7 %copy-start = (bf16[1,1,128,2048]{3,2,1,0:T(8,128)(2,1)S(1)}, bf16[1,1,128,2048]{3,2,1,0:T(8,128)(2,1)}, u32[]{:S(2)}) copy-start(bf16[1,1,128,2048]{3,2,1,0:T(8,128)(2,1)} %param.6) | copy-start | bytes 1572868
  10.8 7.7 %copy-start.1 = (bf16[1,1,128,2048]{3,2,1,0:T(8,128)(2,1)S(1)}, bf16[1,1,128,2048]{3,2,1,0:T(8,128)(2,1)}, u32[]{:S(2)}) copy-start(bf16[1,1,128,2048]{3,2,1,0:T(8,128)(2,1)} %param.7) | copy-start | bytes 1572868
  10.8 7.7 %copy-start.2 = (bf16[1,1,128,2048]{3,2,1,0:T(8,128)(2,1)S(1)}, bf16[1,1,128,2048]{3,2,1,0:T(8,128)(2,1)}, u32[]{:S(2)}) copy-start(bf16[1,1,128,2048]{3,2,1,0:T(8,128)(2,1)} %param.8) | copy-start | bytes 1572868
  10.8 7.7 %copy-start.4 = (s32[1,8]{1,0:T(1,128)S(1)}, s32[1,8]{1,0:T(1,128)}, u32[]{:S(2)}) copy-start(s32[1,8]{1,0:T(1,128)} %near_ref.5) | copy-start | bytes 100
  12.9 23.8 %collective-permute-start.9 = (bf16[128,1536]{1,0:T(8,128)(2,1)S(1)}, bf16[128,1536]{1,0:T(8,128)(2,1)S(1)}, u32[]{:S(2)}, u32[]{:S(2)}) collective-permute-start(bf16[128,1536]{1,0:T(8,128)(2,1)S(1)} %get-tuple-element.39), channel_id=1, source_target_pairs={{0,4},{1,5},{2,6},{3,7},{4,0},{5,1},{6,2},{7,3},{8,12},{9,13},{10,... | collective-permute-start | bytes 1179656 | tf_op jit(solution)/shard_map/ppermute | solution.py:83
  13.7 22.9 %collective-permute-start.10 = (bf16[128,1536]{1,0:T(8,128)(2,1)S(1)}, bf16[128,1536]{1,0:T(8,128)(2,1)S(1)}, u32[]{:S(2)}, u32[]{:S(2)}) collective-permute-start(bf16[128,1536]{1,0:T(8,128)(2,1)S(1)} %pad_maximum_fusion.2), channel_id=1, source_target_pairs={{0,6},{1,7},{2,4},{3,5},{4,2},{5,3},{6,0},{7,1},{8,14},{9,15},{10,... | collective-permute-start | bytes 1179656 | tf_op jit(solution)/shard_map/ppermute | solution.py:83
  18.4 20.8 %collective-permute-start.8 = (bf16[128,1536]{1,0:T(8,128)(2,1)S(1)}, bf16[128,1536]{1,0:T(8,128)(2,1)S(1)}, u32[]{:S(2)}, u32[]{:S(2)}) collective-permute-start(bf16[128,1536]{1,0:T(8,128)(2,1)S(1)} %pad_maximum_fusion.2), channel_id=1, source_target_pairs={{0,2},{1,3},{2,0},{3,1},{4,6},{5,7},{6,4},{7,5},{8,10},{9,11},{10,... | collective-permute-start | bytes 1179656 | tf_op jit(solution)/shard_map/ppermute | solution.py:83
  20.8 18.7 %collective-permute-start.4 = (bf16[2,512,128]{2,1,0:T(8,128)(2,1)S(1)}, bf16[2,512,128]{2,1,0:T(8,128)(2,1)S(1)}, u32[]{:S(2)}, u32[]{:S(2)}) collective-permute-start(bf16[2,512,128]{2,1,0:T(8,128)(2,1)S(1)} %get-tuple-element.36), channel_id=1, source_target_pairs={{0,1},{1,0},{2,3},{3,2},{4,5},{5,4},{6,7},{7,6},{8,9},{9,8},{10,11... | collective-permute-start | bytes 786440 | tf_op jit(solution)/shard_map/ppermute | solution.py:83
  39.5 3.0 %copy-start.3 = (bf16[1,1,128,2048]{3,2,1,0:T(8,128)(2,1)S(1)}, bf16[1,1,128,2048]{3,2,1,0:T(8,128)(2,1)}, u32[]{:S(2)}) copy-start(bf16[1,1,128,2048]{3,2,1,0:T(8,128)(2,1)} %param.9) | copy-start | bytes 1572868
  39.5 15.4 %collective-permute-start.11 = (bf16[4,128,1536]{2,1,0:T(8,128)(2,1)S(1)}, bf16[4,128,1536]{2,1,0:T(8,128)(2,1)S(1)}, u32[]{:S(2)}, u32[]{:S(2)}) collective-permute-start(bf16[4,128,1536]{2,1,0:T(8,128)(2,1)S(1)} %pad_maximum_fusion.refs_4_), channel_id=1, source_target_pairs={{0,1},{1,0},{2,3},{3,2},{4,5},{5,4},{6,7},{7,6},{8,9},{9,8},{10,11... | collective-permute-start | bytes 4718600 | tf_op jit(solution)/shard_map/ppermute | solution.py:83
  39.7 7.4 %collective-permute-start.5 = (bf16[2,512,128]{2,1,0:T(8,128)(2,1)S(1)}, bf16[2,512,128]{2,1,0:T(8,128)(2,1)S(1)}, u32[]{:S(2)}, u32[]{:S(2)}) collective-permute-start(bf16[2,512,128]{2,1,0:T(8,128)(2,1)S(1)} %pad_maximum_fusion.3.refs_0_), channel_id=1, source_target_pairs={{0,2},{1,3},{2,0},{3,1},{4,6},{5,7},{6,4},{7,5},{8,10},{9,11},{10,... | collective-permute-start | bytes 786440 | tf_op jit(solution)/shard_map/ppermute | solution.py:83
  39.8 14.2 %collective-permute-start.7 = (bf16[2,512,128]{2,1,0:T(8,128)(2,1)S(1)}, bf16[2,512,128]{2,1,0:T(8,128)(2,1)S(1)}, u32[]{:S(2)}, u32[]{:S(2)}) collective-permute-start(bf16[2,512,128]{2,1,0:T(8,128)(2,1)S(1)} %pad_maximum_fusion.4), channel_id=1, source_target_pairs={{0,6},{1,7},{2,4},{3,5},{4,2},{5,3},{6,0},{7,1},{8,14},{9,15},{10,... | collective-permute-start | bytes 786440 | tf_op jit(solution)/shard_map/ppermute | solution.py:83
  42.0 12.9 %collective-permute-start.6 = (bf16[2,512,128]{2,1,0:T(8,128)(2,1)S(1)}, bf16[2,512,128]{2,1,0:T(8,128)(2,1)S(1)}, u32[]{:S(2)}, u32[]{:S(2)}) collective-permute-start(bf16[2,512,128]{2,1,0:T(8,128)(2,1)S(1)} %pad_maximum_fusion.4), channel_id=1, source_target_pairs={{0,4},{1,5},{2,6},{3,7},{4,0},{5,1},{6,2},{7,3},{8,12},{9,13},{10,... | collective-permute-start | bytes 786440 | tf_op jit(solution)/shard_map/ppermute | solution.py:83
  56.8 6.7 %collective-permute-start.14 = (bf16[128,768]{1,0:T(8,128)(2,1)S(1)}, bf16[128,768]{1,0:T(8,128)(2,1)S(1)}, u32[]{:S(2)}, u32[]{:S(2)}) collective-permute-start(bf16[128,768]{1,0:T(8,128)(2,1)S(1)} %get-tuple-element.47), channel_id=1, source_target_pairs={{0,8},{8,0},{16,24},{24,16},{1,9},{9,1},{17,25},{25,17},{2,10},{10... | collective-permute-start | bytes 589832 | tf_op jit(solution)/shard_map/ppermute | solution.py:83
  58.1 42.6 %collective-permute-start.13 = (bf16[2,128,2048]{2,1,0:T(8,128)(2,1)S(1)}, bf16[2,128,2048]{2,1,0:T(8,128)(2,1)S(1)}, u32[]{:S(2)}, u32[]{:S(2)}) collective-permute-start(bf16[2,128,2048]{2,1,0:T(8,128)(2,1)S(1)} %get-tuple-element.42), channel_id=1, source_target_pairs={{1,0},{2,1},{3,2},{4,3},{5,4},{7,6},{9,8},{10,9},{11,10},{12,11},{... | collective-permute-start | bytes 3145736 | tf_op jit(solution)/shard_map/ppermute | solution.py:393
  61.7 39.0 %collective-permute-start.12 = (bf16[2,128,2048]{2,1,0:T(8,128)(2,1)S(1)}, bf16[2,128,2048]{2,1,0:T(8,128)(2,1)S(1)}, u32[]{:S(2)}, u32[]{:S(2)}) collective-permute-start(bf16[2,128,2048]{2,1,0:T(8,128)(2,1)S(1)} %get-tuple-element.42), channel_id=1, source_target_pairs={{0,1},{2,3},{3,4},{4,5},{5,6},{6,7},{8,9},{10,11},{11,12},{12,13},... | collective-permute-start | bytes 3145736 | tf_op jit(solution)/shard_map/ppermute | solution.py:392
  63.2 9.8 %collective-permute-start.16 = (bf16[128,768]{1,0:T(8,128)(2,1)S(1)}, bf16[128,768]{1,0:T(8,128)(2,1)S(1)}, u32[]{:S(2)}, u32[]{:S(2)}) collective-permute-start(bf16[128,768]{1,0:T(8,128)(2,1)S(1)} %get-tuple-element.49), channel_id=1, source_target_pairs={{0,8},{8,0},{16,24},{24,16},{1,9},{9,1},{17,25},{25,17},{2,10},{10... | collective-permute-start | bytes 589832 | tf_op jit(solution)/shard_map/ppermute | solution.py:83
  63.5 9.7 %collective-permute-start.15 = (bf16[128,768]{1,0:T(8,128)(2,1)S(1)}, bf16[128,768]{1,0:T(8,128)(2,1)S(1)}, u32[]{:S(2)}, u32[]{:S(2)}) collective-permute-start(bf16[128,768]{1,0:T(8,128)(2,1)S(1)} %add_convert_fusion.1), channel_id=1, source_target_pairs={{0,16},{8,24},{16,0},{24,8},{1,17},{9,25},{17,1},{25,9},{2,18},{10... | collective-permute-start | bytes 589832 | tf_op jit(solution)/shard_map/ppermute | solution.py:83
  73.1 13.7 %collective-permute-start.18 = (bf16[128,1536]{1,0:T(8,128)(2,1)S(1)}, bf16[128,1536]{1,0:T(8,128)(2,1)S(1)}, u32[]{:S(2)}, u32[]{:S(2)}) collective-permute-start(bf16[128,1536]{1,0:T(8,128)(2,1)S(1)} %get-tuple-element.50), channel_id=1, source_target_pairs={{0,8},{8,0},{16,24},{24,16},{1,9},{9,1},{17,25},{25,17},{2,10},{10... | collective-permute-start | bytes 1179656 | tf_op jit(solution)/shard_map/ppermute | solution.py:83
  73.1 11.1 %collective-permute-start.17 = (bf16[128,768]{1,0:T(8,128)(2,1)S(1)}, bf16[128,768]{1,0:T(8,128)(2,1)S(1)}, u32[]{:S(2)}, u32[]{:S(2)}) collective-permute-start(bf16[128,768]{1,0:T(8,128)(2,1)S(1)} %add_convert_fusion), channel_id=1, source_target_pairs={{0,16},{8,24},{16,0},{24,8},{1,17},{9,25},{17,1},{25,9},{2,18},{10... | collective-permute-start | bytes 589832 | tf_op jit(solution)/shard_map/ppermute | solution.py:83
  87.6 5.5 %collective-permute-start.19 = (f32[128,128]{1,0:T(8,128)S(1)}, f32[128,128]{1,0:T(8,128)S(1)}, u32[]{:S(2)}, u32[]{:S(2)}) collective-permute-start(f32[128,128]{1,0:T(8,128)S(1)} %get-tuple-element.52.gram), channel_id=1, source_target_pairs={{0,2},{1,3},{2,0},{3,1},{4,6},{5,7},{6,4},{7,5},{8,10},{9,11},{10,... | collective-permute-start | bytes 196616 | tf_op jit(solution)/shard_map/ppermute | solution.py:83
  97.0 5.5 %collective-permute-start.20 = (bf16[128,384]{1,0:T(8,128)(2,1)S(1)}, bf16[128,384]{1,0:T(8,128)(2,1)S(1)}, u32[]{:S(2)}, u32[]{:S(2)}) collective-permute-start(bf16[128,384]{1,0:T(8,128)(2,1)S(1)} %get-tuple-element.55), channel_id=1, source_target_pairs={{0,1},{1,0},{2,3},{3,2},{4,5},{5,4},{6,7},{7,6},{8,9},{9,8},{10,11... | collective-permute-start | bytes 294920 | tf_op jit(solution)/shard_map/ppermute | solution.py:83
  99.0 4.4 %collective-permute-start.21 = (bf16[128,384]{1,0:T(8,128)(2,1)S(1)}, bf16[128,384]{1,0:T(8,128)(2,1)S(1)}, u32[]{:S(2)}, u32[]{:S(2)}) collective-permute-start(bf16[128,384]{1,0:T(8,128)(2,1)S(1)} %get-tuple-element.56), channel_id=1, source_target_pairs={{0,4},{1,5},{2,6},{3,7},{4,0},{5,1},{6,2},{7,3},{8,12},{9,13},{10,... | collective-permute-start | bytes 294920 | tf_op jit(solution)/shard_map/ppermute | solution.py:83
  99.6 6.0 %collective-permute-start.22 = (bf16[128,384]{1,0:T(8,128)(2,1)S(1)}, bf16[128,384]{1,0:T(8,128)(2,1)S(1)}, u32[]{:S(2)}, u32[]{:S(2)}) collective-permute-start(bf16[128,384]{1,0:T(8,128)(2,1)S(1)} %get-tuple-element.57), channel_id=1, source_target_pairs={{0,5},{1,4},{2,7},{3,6},{4,1},{5,0},{6,3},{7,2},{8,13},{9,12},{10,... | collective-permute-start | bytes 294920 | tf_op jit(solution)/shard_map/ppermute | solution.py:83

commit v4 on v3

--- a/solution.py
+++ b/solution.py
@@ -94,24 +94,24 @@
     return powers * (1.0 / jnp.sum(powers, axis=0, keepdims=True))
 
 
-def choose_far(near_ref, key_left, value_left, key_right, value_right, far):
+def choose_far(near_ref, key_mate, value_mate, key_next, value_next, far):
     place = lax.axis_index("seq")
-    go_left = near_ref[0, place] < place
-
-    @pl.when(go_left)
+    is_mate = near_ref[0, place] == (place ^ 1)
+
+    @pl.when(is_mate)
     def _():
-        far[0] = key_left[...]
-        far[1] = value_left[...]
-
-    @pl.when(jnp.logical_not(go_left))
+        far[0] = key_mate[...]
+        far[1] = value_mate[...]
+
+    @pl.when(jnp.logical_not(is_mate))
     def _():
-        far[0] = key_right[...]
-        far[1] = value_right[...]
-
-
-def forward_kernel(plan, near_ref, q, ko, vo, kl, vl, kr, vr, keep, give, far):
+        far[0] = key_next[...]
+        far[1] = value_next[...]
+
+
+def forward_kernel(plan, near_ref, q, ko, vo, km, vm, kn, vn, out, far):
     layer = lax.axis_index("dp")
-    choose_far(near_ref, kl, vl, kr, vr, far)
+    choose_far(near_ref, km, vm, kn, vn, far)
     mine = plan.row_part(lax.axis_index("seq"))
     jobs = [(j, i) for j in range(plan.per_target) for i in range(plan.dp)]
     for first in range(0, len(jobs), GROUP):
@@ -123,12 +123,12 @@
         ]
         for (j, i), at, p in zip(group, spots, weights, strict=True):
             values = jnp.concatenate([vo[:, at], far[1, :, at]], 0)
-            out = give if j & 1 else keep
-            out[j >> 1, i * HEAD_DIM : (i + 1) * HEAD_DIM, :] = dot_l(values, p).astype(bf16)
-
-
-def backward_kernel(near_ref, q, ko, vo, kl, vl, kr, vr, g, dq, dko, dvo, dfar, far):
-    choose_far(near_ref, kl, vl, kr, vr, far)
+            rows = slice(i * HEAD_DIM, (i + 1) * HEAD_DIM)
+            out[j >> 1, j & 1, rows, :] = dot_l(values, p).astype(bf16)
+
+
+def backward_kernel(near_ref, q, ko, vo, km, vm, kn, vn, g, dq, dko, dvo, dfar, far):
+    choose_far(near_ref, km, vm, kn, vn, far)
     tile = q.shape[0]
     count = q.shape[1] // HEAD_DIM
     for first in range(0, count, GROUP):
@@ -156,45 +156,58 @@
             dfar[1, :, at] = dv[tile:].astype(bf16)
 
 
-def combine_kernel(near_ref, dko, dvo, left, right, dk, dv):
+def combine_kernel(near_ref, dko, dvo, mate, beyond, dk, dv):
     place = lax.axis_index("seq")
     last = lax.axis_size("seq") - 1
-    before = near_ref[0, jnp.maximum(place - 1, 0)]
-    beyond = near_ref[0, jnp.minimum(place + 1, last)]
-    from_left = (place > 0) & (before == place)
-    from_right = (place < last) & (beyond == place)
+    other = place + 2 * (place & 1) - 1
+    inside = (other >= 0) & (other <= last)
+    from_mate = near_ref[0, place ^ 1] == place
+    from_other = inside & (near_ref[0, jnp.clip(other, 0, last)] == place)
     for which, (own, out) in enumerate(((dko, dk), (dvo, dv))):
-        total = own[...] + jnp.where(from_left, left[which].astype(f32), 0.0)
-        out[...] = (total + jnp.where(from_right, right[which].astype(f32), 0.0)).astype(bf16)
-
-
-def product_kernel(plan, spots, *refs):
+        total = own[...] + jnp.where(from_mate, mate[which].astype(f32), 0.0)
+        out[...] = (total + jnp.where(from_other, beyond[which].astype(f32), 0.0)).astype(bf16)
+
+
+def product_kernel(plan, layers, *refs):
     att = refs[: plan.pairs]
-    cols = refs[plan.pairs : plan.pairs + 2]
-    outs = refs[plan.pairs + 2 : plan.pairs + 2 + len(spots)]
-    turned = refs[plan.pairs + 2 + len(spots) :]
+    cols, *outs, for_mate, gathered = refs[plan.pairs :]
     for t in range(plan.pairs):
+        at = slice(t * HEAD_DIM, (t + 1) * HEAD_DIM)
         for core in range(2):
-            turned[core][:, t * HEAD_DIM : (t + 1) * HEAD_DIM] = att[t][core]
-    tokens = turned[0].shape[1]
-    for (i, start, size), out in zip(spots, outs, strict=True):
-        rows = slice(i * HEAD_DIM, (i + 1) * HEAD_DIM)
-        step = 256 if size % 256 == 0 else size
-        for c in range(0, size, step):
-            total = None
-            for core in range(2):
-                block = cols[core][:, :, start + c : start + c + step].reshape(tokens, step)
-                part = dot_n(turned[core][rows, :], block)
-                total = part if total is None else total + part
-            out[:, c : c + step] = total.astype(out.dtype)
-
-
-def gram_kernel(starts, own, *refs):
+            for n, i in enumerate(layers):
+                block = att[t][core, i * HEAD_DIM : (i + 1) * HEAD_DIM, :]
+                gathered[core, n * HEAD_DIM : (n + 1) * HEAD_DIM, at] = block
+    tokens, width = gathered.shape[2], cols.shape[2]
+    step = 512 if width % 512 == 0 else width
+    for c in range(0, width, step):
+        block = cols[:, :, c : c + step].reshape(tokens, step)
+        for n, out in enumerate(outs):
+            rows = slice(n * HEAD_DIM, (n + 1) * HEAD_DIM)
+            out[:, c : c + step] = dot_n(gathered[0, rows, :], block)
+            for_mate[n, :, c : c + step] = dot_n(gathered[1, rows, :], block).astype(bf16)
+
+
+def piece(ref, lead, start, size):
+    at = slice(start, start + size)
+    return (ref[:, at] if lead is None else ref[lead, :, at]).astype(f32)
+
+
+def sum_kernel(spots, start, *refs):
+    *parts, out = refs
+    size = out.shape[1]
+    total = None
+    for (lead, first), part in zip(spots, parts, strict=True):
+        value = piece(part, lead, start - first, size)
+        total = value if total is None else total + value
+    out[...] = total.astype(bf16)
+
+
+def gram_kernel(spots, own, *refs):
     *parts, x, gram = refs
     x[...] = own[...]
-    for start, part in zip(starts, parts, strict=True):
-        at = slice(start, start + part.shape[1])
-        x[:, at] += part[...].astype(f32)
+    for (lead, first), part in zip(spots, parts, strict=True):
+        size = part.shape[-1]
+        x[:, first : first + size] += piece(part, lead, 0, size)
     gram[...] = exact(x[...], x[...], ((1,), (1,)))
 
 
@@ -251,13 +264,15 @@
         a.reshape(tile, width) for a in (query_tiles, key_tiles, value_tiles, attn_grad)
     )
 
-    to_right = [(i, i + 1) for i in range(n - 1) if i + 1 != n - 2]
-    to_left = [(i + 1, i) for i in range(n - 1) if i != 1]
-    key_left = lax.ppermute(key, "seq", to_right)
-    key_right = lax.ppermute(key, "seq", to_left)
-    value_left = lax.ppermute(value, "seq", to_right)
-    value_right = lax.ppermute(value, "seq", to_left)
-    beside = (key_left, value_left, key_right, value_right)
+    steps = [(i, i + 1) for i in range(1, n - 1, 2)]
+    back = [(j, i) for i, j in steps]
+    takes = [(i, j) for i, j in steps if j != n - 2] + [(j, i) for j, i in back if i != 1]
+    gives = [(i, j) for i, j in steps if i != 1] + [(j, i) for j, i in back if j != n - 2]
+    key_next = lax.ppermute(key, "seq", takes)
+    value_next = lax.ppermute(value, "seq", takes)
+    key_mate = shift(key, "seq", 1)
+    value_mate = shift(value, "seq", 1)
+    beside = (key_mate, value_mate, key_next, value_next)
 
     slot = depth // n
     flat = proj_grad.reshape(tile, depth)
@@ -273,29 +288,36 @@
             1,
         )
 
-    columns = [column_part(mine)] + [
-        shift(after(column_part(mine ^ (t & (plan.col - 1))), key_left, key_right), "seq", t << 1)
-        for t in range(1, plan.pairs)
+    own_columns = column_part(mine)
+    columns = [own_columns] + [
+        shift(after(column_part(mine ^ q), key_next, key_mate), "seq", q << 1)
+        for q in range(1, plan.col)
     ]
-
-    keep, give = pl.pallas_call(
+    high_columns = [
+        shift(after(own_columns, key_next, key_mate), "seq", high << (1 + plan.col_bits))
+        for high in range(1, plan.high)
+    ]
+
+    attended = pl.pallas_call(
         functools.partial(forward_kernel, plan),
-        out_shape=[struct((plan.high, m * HEAD_DIM, tile), bf16)] * 2,
+        out_shape=struct((plan.high, 2, m * HEAD_DIM, tile), bf16),
         in_specs=[smem()] + whole(7),
-        out_specs=whole(2),
+        out_specs=pl.BlockSpec(memory_space=pltpu.VMEM),
         scratch_shapes=[pltpu.VMEM((2, tile, width), bf16)],
         compiler_params=params(),
         cost_estimate=cost(8 * tile * tile * width, 16 * tile * width, 2 * tile * tile * head_count),
         name="attention_forward",
     )(neighbour, query, key, value, *beside)
 
-    got = shift(give, "seq", 1)
-    rows = [jnp.stack([keep[high], got[high]]) for high in range(plan.high)]
-    pairs = [rows[0]] + [
-        shift(rows[t >> plan.col_bits], "seq", t << 1) for t in range(1, plan.pairs)
+    pairs = [attended[0]] + [
+        shift(attended[t >> plan.col_bits], "seq", t << 1) for t in range(1, plan.pairs)
     ]
-    held = after(jnp.stack(columns), got)
-    held_other = shift(held, "seq", 1)
+    through = after(jnp.stack(columns[1:]), attended)
+    held = [jnp.stack(columns)]
+    for high in range(1, plan.high):
+        rest = shift(through, "seq", high << (1 + plan.col_bits))
+        held.append(jnp.concatenate([high_columns[high - 1][None], rest], 0))
+    held = jnp.concatenate(held, 0)
 
     dq, dko, dvo, dfar = pl.pallas_call(
         backward_kernel,
@@ -311,53 +333,73 @@
         compiler_params=params(),
         cost_estimate=cost(28 * tile * tile * width, 30 * tile * width, 2 * tile * tile * head_count),
         name="attention_backward",
-    )(neighbour, query, key, value, *beside, grad)
+    )(neighbour, query, key, value, *beside, after(grad, attended))
+
+    def product(name, layers, *operands):
+        *blocks, for_mate = pl.pallas_call(
+            functools.partial(product_kernel, plan, layers),
+            out_shape=[struct((HEAD_DIM, mine_width), f32)] * len(layers)
+            + [struct((len(layers), HEAD_DIM, mine_width), bf16)],
+            in_specs=whole(plan.pairs + 1),
+            out_specs=whole(len(layers) + 1),
+            scratch_shapes=[pltpu.VMEM((2, len(layers) * HEAD_DIM, plan.pairs * tile), bf16)],
+            compiler_params=params(),
+            cost_estimate=cost(
+                2 * len(layers) * HEAD_DIM * n * tile * mine_width, n * tile * mine_width
+            ),
+            name=name,
+        )(*operands)
+        mate = shift(for_mate, "seq", 1)
+        return {i: [(block, None, 0), (mate, k, 0)] for k, (i, block) in enumerate(zip(layers, blocks))}
+
+    def added(parts, start, size):
+        return pl.pallas_call(
+            functools.partial(sum_kernel, [spot for _, *spot in parts], start),
+            out_shape=struct((HEAD_DIM, size), bf16),
+            in_specs=whole(len(parts)),
+            out_specs=pl.BlockSpec(memory_space=pltpu.VMEM),
+            compiler_params=params(),
+            cost_estimate=cost(len(parts) * HEAD_DIM * size, 4 * len(parts) * HEAD_DIM * size),
+            name="block_sum",
+        )(*[array for array, *_ in parts])
+
+    leading = [i for i in range(m - 1, 1, -1) if i & 1]
+    blocks = product("product_first", leading, after(pairs[0], dq), *pairs[1:], held)
+    first_block = blocks[leading[0]][0][0]
+    blocks |= product(
+        "product_rest",
+        [i for i in range(m) if i not in leading],
+        after(pairs[0], first_block),
+        *pairs[1:],
+        held,
+    )
 
     half = mine_width // 2
-    spots = [(0, 0, mine_width), (1, 0, mine_width)]
-    spots += [(i, start, half) for i in range(2, m) for start in (0, half)]
-    blocks = pl.pallas_call(
-        functools.partial(product_kernel, plan, spots),
-        out_shape=[
-            struct((HEAD_DIM, size), bf16 if i & 1 else f32) for i, start, size in spots
-        ],
-        in_specs=whole(plan.pairs + 2),
-        out_specs=whole(len(spots)),
-        scratch_shapes=[pltpu.VMEM((m * HEAD_DIM, plan.pairs * tile), bf16)] * 2,
-        compiler_params=params(),
-        cost_estimate=cost(
-            2 * m * HEAD_DIM * n * tile * mine_width, 2 * n * tile * (mine_width + m * HEAD_DIM)
-        ),
-        name="gradient_product",
-    )(after(pairs[0], dq), *pairs[1:], held, held_other)
-
-    total = dict(zip([spot[:2] for spot in spots], blocks, strict=True))
-    came = []
     first_step = []
+    extra = {(i, start): [] for i in range(m) for start in (0, half)}
     bit = 1
     while bit < m:
         for i in range(m - 1, 1, -1):
             if i & -i == bit:
                 for start in (0, half):
-                    part = shift(total[i, start].astype(bf16), "dp", bit)
+                    part = shift(added(blocks[i] + extra[i, start], start, half), "dp", bit)
                     if bit == 1:
                         first_step.append(part)
-                    if i == bit:
-                        came.append((start, part))
-                    else:
-                        total[i ^ bit, start] = total[i ^ bit, start] + part.astype(f32)
+                    extra[i ^ bit, start].append((part, None, start))
         bit *= 2
-    came.append((0, shift(after(total[1, 0], *first_step), "dp", 1)))
+    near = shift(after(added(blocks[1], 0, mine_width), *first_step), "dp", 1)
+    own = blocks[0][0][0]
+    came = [blocks[0][1], (near, None, 0)] + extra[0, 0] + extra[0, half]
 
     x, gram = pl.pallas_call(
-        functools.partial(gram_kernel, [start for start, part in came]),
+        functools.partial(gram_kernel, [spot for _, *spot in came]),
         out_shape=[struct((HEAD_DIM, mine_width), f32), struct((HEAD_DIM, HEAD_DIM), f32)],
         in_specs=whole(1 + len(came)),
         out_specs=whole(2),
         compiler_params=params(),
         cost_estimate=cost(12 * HEAD_DIM * HEAD_DIM * mine_width, 14 * HEAD_DIM * mine_width),
         name="gradient_sum",
-    )(total[0, 0], *[part for start, part in came])
+    )(own, *[array for array, *_ in came])
 
     gram_other = jnp.zeros_like(gram)
     for b in range(plan.col_bits):
@@ -374,9 +416,7 @@
         cost_estimate=cost(12 * HEAD_DIM * HEAD_DIM * mine_width, 8 * HEAD_DIM * mine_width),
         name="newton_schulz",
     )(x, gram, gram_other)
-    far_right = [(i, i + 1) for i in range(n - 1) if i != 1]
-    far_left = [(i + 1, i) for i in range(n - 1) if i + 1 != n - 2]
-    dfar = after(dfar, total[1, 0])
+    dfar = after(dfar, own)
     dk, dv = pl.pallas_call(
         combine_kernel,
         out_shape=[struct((tile, width), bf16)] * 2,
@@ -389,8 +429,8 @@
         neighbour,
         dko,
         dvo,
-        lax.ppermute(dfar, "seq", far_right),
-        lax.ppermute(dfar, "seq", far_left),
+        shift(dfar, "seq", 1),
+        lax.ppermute(dfar, "seq", gives),
     )
 
     pieces = [pieces[0]] + [

time: 107 us -> 105 us (0.981)
  starting transfers between devices: 36.4 us -> 30.3 us
  waiting for transfers between devices: 51.8 us -> 56 us
    ppermute x6 -> x3, starting transfers between devices: 15.2 us -> 9.49 us  [the longest x1 4.54 us: local(): key_next = lax.ppermute(key, 'seq', takes)]
    ppermute x6 -> x3, waiting for transfers between devices: 0.58 us -> 6 us  [the longest x1 4.75 us: local(): value_next = lax.ppermute(value, 'seq', takes)]
    ppermute x17 -> x20, waiting for transfers between devices: 51.2 us -> 50 us  [shift(): lax.ppermute(value, axis, [(i, i ^ mask) for i in range(lax.axis_size(axi...]
    pallas_call x3 -> x9, Pallas kernels: 4.97 us -> 5.38 us  [the longest x1 2.29 us: local(): pl.pallas_call(functools.partial(forward_kernel, plan), out_shape=struct(...]
    ppermute x17 -> x20, starting transfers between devices: 21.2 us -> 20.8 us  [shift(): lax.ppermute(value, axis, [(i, i ^ mask) for i in range(lax.axis_size(axi...]
  transfers between devices with their start and end apart: 23 -> 23, of which waited for: 12 -> 14; matrix products, arithmetic and copies ran while one was open for 2% -> 2% of each run, Pallas kernels for 12% -> 12%
where the time goes in v4:
time: 105 us
  waiting for transfers between devices  56 us (53%)
  starting transfers between devices  30.3 us (29%)
  Pallas kernels  16 us (15%)
  local copies, waits for them, and re-layouts  1.44 us (1%)
    ppermute x20, waiting for transfers between devices, shift(): lax.ppermute(value, axis, [(i, i ^ mask) for i in range(lax.axis_size(axi...  50 us
    ppermute x20, starting transfers between devices, shift(): lax.ppermute(value, axis, [(i, i ^ mask) for i in range(lax.axis_size(axi...  20.8 us
    ppermute x1, waiting for transfers between devices, local(): value_next = lax.ppermute(value, 'seq', takes)  4.75 us
    ppermute x1, starting transfers between devices, local(): key_next = lax.ppermute(key, 'seq', takes)  4.54 us
    pallas_call x1, Pallas kernels, local(): pl.pallas_call(functools.partial(update_kernel, plan, factor), out_shape=...  3.95 us
    pallas_call x1, Pallas kernels, local(): pl.pallas_call(backward_kernel, out_shape=[struct((tile, width), bf16), s...  3.9 us
    ppermute x1, starting transfers between devices, local(): value_next = lax.ppermute(value, 'seq', takes)  3.49 us
    pallas_call x1, Pallas kernels, local(): pl.pallas_call(functools.partial(forward_kernel, plan), out_shape=struct(...  2.29 us
  transfers between devices with their start and end apart: 23, of which 14 were waited for; matrix products, arithmetic and copies ran while one was open for 2% of the time, Pallas kernels for 12%

profile of v4, /device:TPU:1, one launch (start us, length us, event | category | flops | bytes accessed | tf_op | source)
XLA Modules:
  0.0 104.8 jit_solution(6454898823425294706)
XLA Ops:
  0.6 4.5 %collective-permute-start.2 = (bf16[128,2048]{1,0:T(8,128)(2,1)}, bf16[128,2048]{1,0:T(8,128)(2,1)S(1)}, u32[]{:S(2)}, u32[]{:S(2)}) collective-permute-start(bf16[128,2048]{1,0:T(8,128)(2,1)} %bitcast.25), channel_id=1, source_target_pairs={{1,2},{3,4},{4,3},{6,5},{9,10},{11,12},{12,11},{14,13},{17,18},{19... | collective-permute-start | bytes 1572872 | tf_op jit(solution)/shard_map/ppermute | solution.py:271
  5.2 0.1 collective-permute-start
  5.3 3.5 %collective-permute-start.3 = (bf16[128,2048]{1,0:T(8,128)(2,1)}, bf16[128,2048]{1,0:T(8,128)(2,1)S(1)}, u32[]{:S(2)}, u32[]{:S(2)}) collective-permute-start(bf16[128,2048]{1,0:T(8,128)(2,1)} %bitcast.29), channel_id=1, source_target_pairs={{1,2},{3,4},{4,3},{6,5},{9,10},{11,12},{12,11},{14,13},{17,18},{19... | collective-permute-start | bytes 1572872 | tf_op jit(solution)/shard_map/ppermute | solution.py:272
  8.8 0.1 collective-permute-start.1
  8.8 0.0 copy-start
  8.9 0.0 copy-start.1
  8.9 0.0 copy-start.2
  8.9 1.4 %dynamic-slice_bitcast_fusion.3 = (bf16[128,768]{1,0:T(8,128)(2,1)S(1)}, bf16[128,768]{1,0:T(8,128)(2,1)S(1)}, bf16[128,768]{1,0:T(8,128)(2,1)S(1)}, bf16[128,768]{1,0:T(8,128)(2,1)S(1)}) fusion(bf16[1,1,128,3072]{3,2,1,0:T(8,128)(2,1)} %param.10, s32[]{:T(128)S(6)} %select_n.12, s32[]{:T(128)S(6)} %select_n.13, s32[]{:T(128)S(6)} %select_n.15, s32[]{:T(128)S(6)} %select_n.14), kind=kLoop, calls=%fused_computation.8 | loop fusion | bytes 1572880 | tf_op jit(solution)/shard_map/dynamic_slice | solution.py:285
  10.3 1.3 %collective-permute-done.2.kn = bf16[128,2048]{1,0:T(8,128)(2,1)S(1)} collective-permute-done((bf16[128,2048]{1,0:T(8,128)(2,1)}, bf16[128,2048]{1,0:T(8,128)(2,1)S(1)}, u32[]{:S(2)}, u32[]{:S(2)}) %collective-permute-start.2) | collective-permute-done | bytes 524320 | tf_op jit(solution)/shard_map/ppermute | solution.py:271
  11.6 0.0 collective-permute-done.km
  11.6 2.7 %collective-permute-start.7 = (bf16[128,1536]{1,0:T(8,128)(2,1)S(1)}, bf16[128,1536]{1,0:T(8,128)(2,1)S(1)}, u32[]{:S(2)}, u32[]{:S(2)}) collective-permute-start(bf16[128,1536]{1,0:T(8,128)(2,1)S(1)} %pad_maximum_fusion.2), channel_id=1, source_target_pairs={{0,2},{1,3},{2,0},{3,1},{4,6},{5,7},{6,4},{7,5},{8,10},{9,11},{10,... | collective-permute-start | bytes 1179656 | tf_op jit(solution)/shard_map/ppermute | solution.py:83
  14.3 0.1 fusion
  14.3 0.1 collective-permute-start.8
  14.4 4.7 %collective-permute-done.3.vn = bf16[128,2048]{1,0:T(8,128)(2,1)S(1)} collective-permute-done((bf16[128,2048]{1,0:T(8,128)(2,1)}, bf16[128,2048]{1,0:T(8,128)(2,1)S(1)}, u32[]{:S(2)}, u32[]{:S(2)}) %collective-permute-start.3) | collective-permute-done | bytes 524320 | tf_op jit(solution)/shard_map/ppermute | solution.py:272
  19.2 0.0 collective-permute-done.1.vm
  19.2 0.0 copy-start.3
  19.2 2.3 %attention_forward.1 = bf16[2,2,512,128]{3,2,1,0:T(8,128)(2,1)S(1)} custom-call(s32[1,8]{1,0:T(1,128)S(1)} %copy-done.4, bf16[128,2048]{1,0:T(8,128)(2,1)S(1)} %bitcast.23, bf16[128,2048]{1,0:T(8,128)(2,1)S(1)} %bitcast.27, bf16[128,2048]{1,0:T(8,128)(2,1)S(1)} %bitcast.31, bf16[128,2048]{1,0:T(8,128)(2,1)S(1)} %collective-permute-done.km, ...), custom_call_target="tpu_custom_call" | custom-call | flops 268435456 | bytes 4194304 | tf_op jit(solution)/shard_map/attention_forward/pallas_call | solution.py:301
  21.5 5.7 %collective-permute-done.7 = bf16[128,1536]{1,0:T(8,128)(2,1)S(1)} collective-permute-done((bf16[128,1536]{1,0:T(8,128)(2,1)S(1)}, bf16[128,1536]{1,0:T(8,128)(2,1)S(1)}, u32[]{:S(2)}, u32[]{:S(2)}) %collective-permute-start.7) | collective-permute-done | bytes 393248 | tf_op jit(solution)/shard_map/ppermute | solution.py:83
  27.2 0.0 collective-permute-start.9
  27.2 1.8 %collective-permute-start.6 = (bf16[2,512,128]{2,1,0:T(8,128)(2,1)S(1)}, bf16[2,512,128]{2,1,0:T(8,128)(2,1)S(1)}, u32[]{:S(2)}, u32[]{:S(2)}) collective-permute-start(bf16[2,512,128]{2,1,0:T(8,128)(2,1)S(1)} %get-tuple-element.62), channel_id=1, source_target_pairs={{0,6},{1,7},{2,4},{3,5},{4,2},{5,3},{6,0},{7,1},{8,14},{9,15},{10,... | collective-permute-start | bytes 786440 | tf_op jit(solution)/shard_map/ppermute | solution.py:83
  29.0 0.0 collective-permute-start.5
  29.0 0.9 collective-permute-start.4
  29.9 3.9 %attention_backward.1 = (bf16[128,2048]{1,0:T(8,128)(2,1)}, f32[128,2048]{1,0:T(8,128)S(1)}, f32[128,2048]{1,0:T(8,128)S(1)}, bf16[2,128,2048]{2,1,0:T(8,128)(2,1)S(1)}) custom-call(s32[1,8]{1,0:T(1,128)S(1)} %copy-done.4, bf16[128,2048]{1,0:T(8,128)(2,1)S(1)} %bitcast.24, bf16[128,2048]{1,0:T(8,128)(2,1)S(1)} %bitcast.28, bf16[128,2048]{1,0:T(8,128)(2,1)S(1)} %bitcast.32, ...), custom_call_target="tpu_custom_call" | custom-call | flops 939524096 | bytes 7864320 | tf_op jit(solution)/shard_map/attention_backward/pallas_call | solution.py:322
  33.8 0.0 collective-permute-done.8
  33.8 10.1 %collective-permute-done.9 = bf16[1,128,1536]{2,1,0:T(8,128)(2,1)S(1)} collective-permute-done((bf16[1,128,1536]{2,1,0:T(8,128)(2,1)S(1)}, bf16[1,128,1536]{2,1,0:T(8,128)(2,1)S(1)}, u32[]{:S(2)}, u32[]{:S(2)}) %collective-permute-start.9) | collective-permute-done | bytes 393248 | tf_op jit(solution)/shard_map/ppermute | solution.py:83
  43.9 0.2 pad_maximum_fusion.refs_4_
  44.1 0.0 collective-permute-done.6.refs_3_
  44.1 4.8 %collective-permute-done.5.refs_2_ = bf16[2,512,128]{2,1,0:T(8,128)(2,1)S(1)} collective-permute-done((bf16[2,512,128]{2,1,0:T(8,128)(2,1)S(1)}, bf16[2,512,128]{2,1,0:T(8,128)(2,1)S(1)}, u32[]{:S(2)}, u32[]{:S(2)}) %collective-permute-start.5) | collective-permute-done | bytes 262176 | tf_op jit(solution)/shard_map/ppermute | solution.py:83
  48.9 0.0 collective-permute-done.4.refs_1_
  48.9 0.6 product_first.1
  49.5 1.4 %product_rest.1 = (f32[128,1536]{1,0:T(8,128)S(1)}, f32[128,1536]{1,0:T(8,128)S(1)}, f32[128,1536]{1,0:T(8,128)S(1)}, bf16[3,128,1536]{2,1,0:T(8,128)(2,1)S(1)}) custom-call(bf16[2,512,128]{2,1,0:T(8,128)(2,1)S(1)} %get-tuple-element.41.refs_0_, bf16[2,512,128]{2,1,0:T(8,128)(2,1)S(1)} %collective-permute-done.4.refs_1_, ...), custom_call_target="tpu_custom_call" | custom-call | flops 1207959552 | bytes 1572864 | tf_op jit(solution)/shard_map/product_rest/pallas_call | solution.py:339
  51.0 0.5 collective-permute-start.12
  51.4 0.1 collective-permute-start.13
  51.5 1.5 %collective-permute-start.11 = (bf16[2,128,2048]{2,1,0:T(8,128)(2,1)S(1)}, bf16[2,128,2048]{2,1,0:T(8,128)(2,1)S(1)}, u32[]{:S(2)}, u32[]{:S(2)}) collective-permute-start(bf16[2,128,2048]{2,1,0:T(8,128)(2,1)S(1)} %get-tuple-element.43), channel_id=1, source_target_pairs={{3,4},{5,6},{2,1},{4,3},{11,12},{13,14},{10,9},{12,11},{19,20},{21... | collective-permute-start | bytes 3145736 | tf_op jit(solution)/shard_map/ppermute | solution.py:433
  53.0 0.1 collective-permute-start.10
  53.1 1.4 %collective-permute-done.13.refs_1_ = bf16[1,128,1536]{2,1,0:T(8,128)(2,1)S(1)} collective-permute-done((bf16[1,128,1536]{2,1,0:T(8,128)(2,1)S(1)}, bf16[1,128,1536]{2,1,0:T(8,128)(2,1)S(1)}, u32[]{:S(2)}, u32[]{:S(2)}) %collective-permute-start.13) | collective-permute-done | bytes 393248 | tf_op jit(solution)/shard_map/ppermute | solution.py:83
  54.5 1.4 %collective-permute-start.14 = (bf16[128,768]{1,0:T(8,128)(2,1)S(1)}, bf16[128,768]{1,0:T(8,128)(2,1)S(1)}, u32[]{:S(2)}, u32[]{:S(2)}) collective-permute-start(bf16[128,768]{1,0:T(8,128)(2,1)S(1)} %block_sum.6), channel_id=1, source_target_pairs={{0,8},{8,0},{16,24},{24,16},{1,9},{9,1},{17,25},{25,17},{2,10},{10... | collective-permute-start | bytes 589832 | tf_op jit(solution)/shard_map/ppermute | solution.py:83
  55.9 0.3 collective-permute-start.15
  56.1 0.0 collective-permute-done.12.refs_1_.refs_0_
  56.2 0.1 block_sum.5
  56.2 4.5 %collective-permute-done.14.refs_2_ = bf16[128,768]{1,0:T(8,128)(2,1)S(1)} collective-permute-done((bf16[128,768]{1,0:T(8,128)(2,1)S(1)}, bf16[128,768]{1,0:T(8,128)(2,1)S(1)}, u32[]{:S(2)}, u32[]{:S(2)}) %collective-permute-start.14) | collective-permute-done | bytes 196640 | tf_op jit(solution)/shard_map/ppermute | solution.py:83
  60.7 4.2 %collective-permute-done.15.refs_2_ = bf16[128,768]{1,0:T(8,128)(2,1)S(1)} collective-permute-done((bf16[128,768]{1,0:T(8,128)(2,1)S(1)}, bf16[128,768]{1,0:T(8,128)(2,1)S(1)}, u32[]{:S(2)}, u32[]{:S(2)}) %collective-permute-start.15) | collective-permute-done | bytes 196640 | tf_op jit(solution)/shard_map/ppermute | solution.py:83
  64.9 1.3 %collective-permute-start.16 = (bf16[128,1536]{1,0:T(8,128)(2,1)S(1)}, bf16[128,1536]{1,0:T(8,128)(2,1)S(1)}, u32[]{:S(2)}, u32[]{:S(2)}) collective-permute-start(bf16[128,1536]{1,0:T(8,128)(2,1)S(1)} %block_sum.5), channel_id=1, source_target_pairs={{0,8},{8,0},{16,24},{24,16},{1,9},{9,1},{17,25},{25,17},{2,10},{10... | collective-permute-start | bytes 1179656 | tf_op jit(solution)/shard_map/ppermute | solution.py:83
  66.2 0.1 block_sum.8
  66.2 2.4 %collective-permute-start.17 = (bf16[128,768]{1,0:T(8,128)(2,1)S(1)}, bf16[128,768]{1,0:T(8,128)(2,1)S(1)}, u32[]{:S(2)}, u32[]{:S(2)}) collective-permute-start(bf16[128,768]{1,0:T(8,128)(2,1)S(1)} %block_sum.8), channel_id=1, source_target_pairs={{0,16},{8,24},{16,0},{24,8},{1,17},{9,25},{17,1},{25,9},{2,18},{10... | collective-permute-start | bytes 589832 | tf_op jit(solution)/shard_map/ppermute | solution.py:83
  68.6 0.1 block_sum.9
  68.7 0.1 collective-permute-start.18
  68.8 8.8 %collective-permute-done.17.refs_2_ = bf16[128,768]{1,0:T(8,128)(2,1)S(1)} collective-permute-done((bf16[128,768]{1,0:T(8,128)(2,1)S(1)}, bf16[128,768]{1,0:T(8,128)(2,1)S(1)}, u32[]{:S(2)}, u32[]{:S(2)}) %collective-permute-start.17) | collective-permute-done | bytes 196640 | tf_op jit(solution)/shard_map/ppermute | solution.py:83
  77.6 4.3 %collective-permute-done.18.refs_3_ = bf16[128,768]{1,0:T(8,128)(2,1)S(1)} collective-permute-done((bf16[128,768]{1,0:T(8,128)(2,1)S(1)}, bf16[128,768]{1,0:T(8,128)(2,1)S(1)}, u32[]{:S(2)}, u32[]{:S(2)}) %collective-permute-start.18) | collective-permute-done | bytes 196640 | tf_op jit(solution)/shard_map/ppermute | solution.py:83
  81.9 0.6 collective-permute-done.16.refs_1_
  82.5 0.8 gradient_sum.1
  83.3 1.1 %collective-permute-start.19 = (f32[128,128]{1,0:T(8,128)S(1)}, f32[128,128]{1,0:T(8,128)S(1)}, u32[]{:S(2)}, u32[]{:S(2)}) collective-permute-start(f32[128,128]{1,0:T(8,128)S(1)} %get-tuple-element.52.gram), channel_id=1, source_target_pairs={{0,2},{1,3},{2,0},{3,1},{4,6},{5,7},{6,4},{7,5},{8,10},{9,11},{10,... | collective-permute-start | bytes 196616 | tf_op jit(solution)/shard_map/ppermute | solution.py:83
  84.4 2.3 %collective-permute-done.19.gram_other = f32[128,128]{1,0:T(8,128)S(1)} collective-permute-done((f32[128,128]{1,0:T(8,128)S(1)}, f32[128,128]{1,0:T(8,128)S(1)}, u32[]{:S(2)}, u32[]{:S(2)}) %collective-permute-start.19) | collective-permute-done | bytes 65568 | tf_op jit(solution)/shard_map/ppermute | solution.py:83
  86.8 4.0 %newton_schulz.1 = (f32[128,384]{1,0:T(8,128)S(1)}, bf16[128,384]{1,0:T(8,128)(2,1)S(1)}, bf16[128,384]{1,0:T(8,128)(2,1)S(1)}, bf16[128,384]{1,0:T(8,128)(2,1)S(1)}) custom-call(f32[128,1536]{1,0:T(8,128)S(1)} %get-tuple-element.51.x, f32[128,128]{1,0:T(8,128)S(1)} %get-tuple-element.52.gram, f32[128,128]{1,0:T(8,128)S(1)} %collective-permute-done.19.gram_other), custom_call_target="tpu_custom_call" | custom-call | flops 301989888 | bytes 1572864 | tf_op jit(solution)/shard_map/newton_schulz/pallas_call | solution.py:410
  90.7 5.6 %collective-permute-start.20 = (bf16[128,384]{1,0:T(8,128)(2,1)S(1)}, bf16[128,384]{1,0:T(8,128)(2,1)S(1)}, u32[]{:S(2)}, u32[]{:S(2)}) collective-permute-start(bf16[128,384]{1,0:T(8,128)(2,1)S(1)} %get-tuple-element.55), channel_id=1, source_target_pairs={{0,1},{1,0},{2,3},{3,2},{4,5},{5,4},{6,7},{7,6},{8,9},{9,8},{10,11... | collective-permute-start | bytes 294920 | tf_op jit(solution)/shard_map/ppermute | solution.py:83
  96.4 2.3 %collective-permute-start.21 = (bf16[128,384]{1,0:T(8,128)(2,1)S(1)}, bf16[128,384]{1,0:T(8,128)(2,1)S(1)}, u32[]{:S(2)}, u32[]{:S(2)}) collective-permute-start(bf16[128,384]{1,0:T(8,128)(2,1)S(1)} %get-tuple-element.56), channel_id=1, source_target_pairs={{0,4},{1,5},{2,6},{3,7},{4,0},{5,1},{6,2},{7,3},{8,12},{9,13},{10,... | collective-permute-start | bytes 294920 | tf_op jit(solution)/shard_map/ppermute | solution.py:83
  98.7 0.0 collective-permute-start.22
  98.8 0.0 collective-permute-done.11.beyond
  98.8 0.0 collective-permute-done.10.mate
  98.8 1.8 %key_value_sum.1 = (bf16[128,2048]{1,0:T(8,128)(2,1)}, bf16[128,2048]{1,0:T(8,128)(2,1)}) custom-call(s32[1,8]{1,0:T(1,128)S(1)} %copy-done.4, f32[128,2048]{1,0:T(8,128)S(1)} %get-tuple-element.33.dko, f32[128,2048]{1,0:T(8,128)S(1)} %get-tuple-element.34.dvo, bf16[2,128,2048]{2,1,0:T(8,128)(2,1)S(1)} %collective-permute-done.10.mate, ...), custom_call_target="tpu_custom_call" | custom-call | flops 1572864 | bytes 5242880 | tf_op jit(solution)/shard_map/key_value_sum/pallas_call | solution.py:420
  100.6 0.0 collective-permute-done.20.refs_1_
  100.6 1.2 %collective-permute-done.21.refs_2_ = bf16[128,384]{1,0:T(8,128)(2,1)S(1)} collective-permute-done((bf16[128,384]{1,0:T(8,128)(2,1)S(1)}, bf16[128,384]{1,0:T(8,128)(2,1)S(1)}, u32[]{:S(2)}, u32[]{:S(2)}) %collective-permute-start.21) | collective-permute-done | bytes 98336 | tf_op jit(solution)/shard_map/ppermute | solution.py:83
  101.8 2.1 %collective-permute-done.22.refs_3_ = bf16[128,384]{1,0:T(8,128)(2,1)S(1)} collective-permute-done((bf16[128,384]{1,0:T(8,128)(2,1)S(1)}, bf16[128,384]{1,0:T(8,128)(2,1)S(1)}, u32[]{:S(2)}, u32[]{:S(2)}) %collective-permute-start.22) | collective-permute-done | bytes 98336 | tf_op jit(solution)/shard_map/ppermute | solution.py:83
  103.9 0.9 update_rows.1
  (10 shorter events, 0.1 us)
Async XLA Ops:
  0.6 10.9 %collective-permute-start.2 = (bf16[128,2048]{1,0:T(8,128)(2,1)}, bf16[128,2048]{1,0:T(8,128)(2,1)S(1)}, u32[]{:S(2)}, u32[]{:S(2)}) collective-permute-start(bf16[128,2048]{1,0:T(8,128)(2,1)} %bitcast.25), channel_id=1, source_target_pairs={{1,2},{3,4},{4,3},{6,5},{9,10},{11,12},{12,11},{14,13},{17,18},{19... | collective-permute-start | bytes 1572872 | tf_op jit(solution)/shard_map/ppermute | solution.py:271
  5.2 6.4 %collective-permute-start = (bf16[128,2048]{1,0:T(8,128)(2,1)}, bf16[128,2048]{1,0:T(8,128)(2,1)S(1)}, u32[]{:S(2)}, u32[]{:S(2)}) collective-permute-start(bf16[128,2048]{1,0:T(8,128)(2,1)} %bitcast.26), channel_id=1, source_target_pairs={{0,1},{1,0},{2,3},{3,2},{4,5},{5,4},{6,7},{7,6},{8,9},{9,8},{10,11... | collective-permute-start | bytes 1572872 | tf_op jit(solution)/shard_map/ppermute | solution.py:83
  5.3 13.9 %collective-permute-start.3 = (bf16[128,2048]{1,0:T(8,128)(2,1)}, bf16[128,2048]{1,0:T(8,128)(2,1)S(1)}, u32[]{:S(2)}, u32[]{:S(2)}) collective-permute-start(bf16[128,2048]{1,0:T(8,128)(2,1)} %bitcast.29), channel_id=1, source_target_pairs={{1,2},{3,4},{4,3},{6,5},{9,10},{11,12},{12,11},{14,13},{17,18},{19... | collective-permute-start | bytes 1572872 | tf_op jit(solution)/shard_map/ppermute | solution.py:272
  8.8 10.4 %collective-permute-start.1 = (bf16[128,2048]{1,0:T(8,128)(2,1)}, bf16[128,2048]{1,0:T(8,128)(2,1)S(1)}, u32[]{:S(2)}, u32[]{:S(2)}) collective-permute-start(bf16[128,2048]{1,0:T(8,128)(2,1)} %bitcast.30), channel_id=1, source_target_pairs={{0,1},{1,0},{2,3},{3,2},{4,5},{5,4},{6,7},{7,6},{8,9},{9,8},{10,11... | collective-permute-start | bytes 1572872 | tf_op jit(solution)/shard_map/ppermute | solution.py:83
  8.8 10.3 %copy-start = (bf16[1,1,128,2048]{3,2,1,0:T(8,128)(2,1)S(1)}, bf16[1,1,128,2048]{3,2,1,0:T(8,128)(2,1)}, u32[]{:S(2)}) copy-start(bf16[1,1,128,2048]{3,2,1,0:T(8,128)(2,1)} %param.6) | copy-start | bytes 1572868
  8.9 10.3 %copy-start.1 = (bf16[1,1,128,2048]{3,2,1,0:T(8,128)(2,1)S(1)}, bf16[1,1,128,2048]{3,2,1,0:T(8,128)(2,1)}, u32[]{:S(2)}) copy-start(bf16[1,1,128,2048]{3,2,1,0:T(8,128)(2,1)} %param.7) | copy-start | bytes 1572868
  8.9 10.3 %copy-start.2 = (bf16[1,1,128,2048]{3,2,1,0:T(8,128)(2,1)S(1)}, bf16[1,1,128,2048]{3,2,1,0:T(8,128)(2,1)}, u32[]{:S(2)}) copy-start(bf16[1,1,128,2048]{3,2,1,0:T(8,128)(2,1)} %param.8) | copy-start | bytes 1572868
  8.9 10.3 %copy-start.4 = (s32[1,8]{1,0:T(1,128)S(1)}, s32[1,8]{1,0:T(1,128)}, u32[]{:S(2)}) copy-start(s32[1,8]{1,0:T(1,128)} %near_ref.5) | copy-start | bytes 100
  11.6 15.6 %collective-permute-start.7 = (bf16[128,1536]{1,0:T(8,128)(2,1)S(1)}, bf16[128,1536]{1,0:T(8,128)(2,1)S(1)}, u32[]{:S(2)}, u32[]{:S(2)}) collective-permute-start(bf16[128,1536]{1,0:T(8,128)(2,1)S(1)} %pad_maximum_fusion.2), channel_id=1, source_target_pairs={{0,2},{1,3},{2,0},{3,1},{4,6},{5,7},{6,4},{7,5},{8,10},{9,11},{10,... | collective-permute-start | bytes 1179656 | tf_op jit(solution)/shard_map/ppermute | solution.py:83
  14.3 19.5 %collective-permute-start.8 = (bf16[128,1536]{1,0:T(8,128)(2,1)S(1)}, bf16[128,1536]{1,0:T(8,128)(2,1)S(1)}, u32[]{:S(2)}, u32[]{:S(2)}) collective-permute-start(bf16[128,1536]{1,0:T(8,128)(2,1)S(1)} %get-tuple-element.38), channel_id=1, source_target_pairs={{0,4},{1,5},{2,6},{3,7},{4,0},{5,1},{6,2},{7,3},{8,12},{9,13},{10,... | collective-permute-start | bytes 1179656 | tf_op jit(solution)/shard_map/ppermute | solution.py:83
  19.2 10.7 %copy-start.3 = (bf16[1,1,128,2048]{3,2,1,0:T(8,128)(2,1)S(1)}, bf16[1,1,128,2048]{3,2,1,0:T(8,128)(2,1)}, u32[]{:S(2)}) copy-start(bf16[1,1,128,2048]{3,2,1,0:T(8,128)(2,1)} %param.9) | copy-start | bytes 1572868
  27.2 16.7 %collective-permute-start.9 = (bf16[1,128,1536]{2,1,0:T(8,128)(2,1)S(1)}, bf16[1,128,1536]{2,1,0:T(8,128)(2,1)S(1)}, u32[]{:S(2)}, u32[]{:S(2)}) collective-permute-start(bf16[1,128,1536]{2,1,0:T(8,128)(2,1)S(1)} %bitcast.34), channel_id=1, source_target_pairs={{0,4},{1,5},{2,6},{3,7},{4,0},{5,1},{6,2},{7,3},{8,12},{9,13},{10,... | collective-permute-start | bytes 1179656 | tf_op jit(solution)/shard_map/ppermute | solution.py:83
  27.2 16.9 %collective-permute-start.6 = (bf16[2,512,128]{2,1,0:T(8,128)(2,1)S(1)}, bf16[2,512,128]{2,1,0:T(8,128)(2,1)S(1)}, u32[]{:S(2)}, u32[]{:S(2)}) collective-permute-start(bf16[2,512,128]{2,1,0:T(8,128)(2,1)S(1)} %get-tuple-element.62), channel_id=1, source_target_pairs={{0,6},{1,7},{2,4},{3,5},{4,2},{5,3},{6,0},{7,1},{8,14},{9,15},{10,... | collective-permute-start | bytes 786440 | tf_op jit(solution)/shard_map/ppermute | solution.py:83
  29.0 19.9 %collective-permute-start.5 = (bf16[2,512,128]{2,1,0:T(8,128)(2,1)S(1)}, bf16[2,512,128]{2,1,0:T(8,128)(2,1)S(1)}, u32[]{:S(2)}, u32[]{:S(2)}) collective-permute-start(bf16[2,512,128]{2,1,0:T(8,128)(2,1)S(1)} %get-tuple-element.62), channel_id=1, source_target_pairs={{0,4},{1,5},{2,6},{3,7},{4,0},{5,1},{6,2},{7,3},{8,12},{9,13},{10,... | collective-permute-start | bytes 786440 | tf_op jit(solution)/shard_map/ppermute | solution.py:83
  29.0 19.9 %collective-permute-start.4 = (bf16[2,512,128]{2,1,0:T(8,128)(2,1)S(1)}, bf16[2,512,128]{2,1,0:T(8,128)(2,1)S(1)}, u32[]{:S(2)}, u32[]{:S(2)}) collective-permute-start(bf16[2,512,128]{2,1,0:T(8,128)(2,1)S(1)} %get-tuple-element.41.refs_0_), channel_id=1, source_target_pairs={{0,2},{1,3},{2,0},{3,1},{4,6},{5,7},{6,4},{7,5},{8,10},{9,11},{10,... | collective-permute-start | bytes 786440 | tf_op jit(solution)/shard_map/ppermute | solution.py:83
  51.0 5.2 %collective-permute-start.12 = (bf16[3,128,1536]{2,1,0:T(8,128)(2,1)S(1)}, bf16[3,128,1536]{2,1,0:T(8,128)(2,1)S(1)}, u32[]{:S(2)}, u32[]{:S(2)}) collective-permute-start(bf16[3,128,1536]{2,1,0:T(8,128)(2,1)S(1)} %get-tuple-element.46), channel_id=1, source_target_pairs={{0,1},{1,0},{2,3},{3,2},{4,5},{5,4},{6,7},{7,6},{8,9},{9,8},{10,11... | collective-permute-start | bytes 3538952 | tf_op jit(solution)/shard_map/ppermute | solution.py:83
  51.4 3.0 %collective-permute-start.13 = (bf16[1,128,1536]{2,1,0:T(8,128)(2,1)S(1)}, bf16[1,128,1536]{2,1,0:T(8,128)(2,1)S(1)}, u32[]{:S(2)}, u32[]{:S(2)}) collective-permute-start(bf16[1,128,1536]{2,1,0:T(8,128)(2,1)S(1)} %get-tuple-element.48), channel_id=1, source_target_pairs={{0,1},{1,0},{2,3},{3,2},{4,5},{5,4},{6,7},{7,6},{8,9},{9,8},{10,11... | collective-permute-start | bytes 1179656 | tf_op jit(solution)/shard_map/ppermute | solution.py:83
  51.5 47.2 %collective-permute-start.11 = (bf16[2,128,2048]{2,1,0:T(8,128)(2,1)S(1)}, bf16[2,128,2048]{2,1,0:T(8,128)(2,1)S(1)}, u32[]{:S(2)}, u32[]{:S(2)}) collective-permute-start(bf16[2,128,2048]{2,1,0:T(8,128)(2,1)S(1)} %get-tuple-element.43), channel_id=1, source_target_pairs={{3,4},{5,6},{2,1},{4,3},{11,12},{13,14},{10,9},{12,11},{19,20},{21... | collective-permute-start | bytes 3145736 | tf_op jit(solution)/shard_map/ppermute | solution.py:433
  53.0 45.8 %collective-permute-start.10 = (bf16[2,128,2048]{2,1,0:T(8,128)(2,1)S(1)}, bf16[2,128,2048]{2,1,0:T(8,128)(2,1)S(1)}, u32[]{:S(2)}, u32[]{:S(2)}) collective-permute-start(bf16[2,128,2048]{2,1,0:T(8,128)(2,1)S(1)} %get-tuple-element.43), channel_id=1, source_target_pairs={{0,1},{1,0},{2,3},{3,2},{4,5},{5,4},{6,7},{7,6},{8,9},{9,8},{10,11... | collective-permute-start | bytes 3145736 | tf_op jit(solution)/shard_map/ppermute | solution.py:83
  54.5 6.2 %collective-permute-start.14 = (bf16[128,768]{1,0:T(8,128)(2,1)S(1)}, bf16[128,768]{1,0:T(8,128)(2,1)S(1)}, u32[]{:S(2)}, u32[]{:S(2)}) collective-permute-start(bf16[128,768]{1,0:T(8,128)(2,1)S(1)} %block_sum.6), channel_id=1, source_target_pairs={{0,8},{8,0},{16,24},{24,16},{1,9},{9,1},{17,25},{25,17},{2,10},{10... | collective-permute-start | bytes 589832 | tf_op jit(solution)/shard_map/ppermute | solution.py:83
  55.9 9.0 %collective-permute-start.15 = (bf16[128,768]{1,0:T(8,128)(2,1)S(1)}, bf16[128,768]{1,0:T(8,128)(2,1)S(1)}, u32[]{:S(2)}, u32[]{:S(2)}) collective-permute-start(bf16[128,768]{1,0:T(8,128)(2,1)S(1)} %block_sum.7), channel_id=1, source_target_pairs={{0,8},{8,0},{16,24},{24,16},{1,9},{9,1},{17,25},{25,17},{2,10},{10... | collective-permute-start | bytes 589832 | tf_op jit(solution)/shard_map/ppermute | solution.py:83
  64.9 17.6 %collective-permute-start.16 = (bf16[128,1536]{1,0:T(8,128)(2,1)S(1)}, bf16[128,1536]{1,0:T(8,128)(2,1)S(1)}, u32[]{:S(2)}, u32[]{:S(2)}) collective-permute-start(bf16[128,1536]{1,0:T(8,128)(2,1)S(1)} %block_sum.5), channel_id=1, source_target_pairs={{0,8},{8,0},{16,24},{24,16},{1,9},{9,1},{17,25},{25,17},{2,10},{10... | collective-permute-start | bytes 1179656 | tf_op jit(solution)/shard_map/ppermute | solution.py:83
  66.2 11.4 %collective-permute-start.17 = (bf16[128,768]{1,0:T(8,128)(2,1)S(1)}, bf16[128,768]{1,0:T(8,128)(2,1)S(1)}, u32[]{:S(2)}, u32[]{:S(2)}) collective-permute-start(bf16[128,768]{1,0:T(8,128)(2,1)S(1)} %block_sum.8), channel_id=1, source_target_pairs={{0,16},{8,24},{16,0},{24,8},{1,17},{9,25},{17,1},{25,9},{2,18},{10... | collective-permute-start | bytes 589832 | tf_op jit(solution)/shard_map/ppermute | solution.py:83
  68.7 13.2 %collective-permute-start.18 = (bf16[128,768]{1,0:T(8,128)(2,1)S(1)}, bf16[128,768]{1,0:T(8,128)(2,1)S(1)}, u32[]{:S(2)}, u32[]{:S(2)}) collective-permute-start(bf16[128,768]{1,0:T(8,128)(2,1)S(1)} %block_sum.9), channel_id=1, source_target_pairs={{0,16},{8,24},{16,0},{24,8},{1,17},{9,25},{17,1},{25,9},{2,18},{10... | collective-permute-start | bytes 589832 | tf_op jit(solution)/shard_map/ppermute | solution.py:83
  83.3 3.5 %collective-permute-start.19 = (f32[128,128]{1,0:T(8,128)S(1)}, f32[128,128]{1,0:T(8,128)S(1)}, u32[]{:S(2)}, u32[]{:S(2)}) collective-permute-start(f32[128,128]{1,0:T(8,128)S(1)} %get-tuple-element.52.gram), channel_id=1, source_target_pairs={{0,2},{1,3},{2,0},{3,1},{4,6},{5,7},{6,4},{7,5},{8,10},{9,11},{10,... | collective-permute-start | bytes 196616 | tf_op jit(solution)/shard_map/ppermute | solution.py:83
  90.7 9.8 %collective-permute-start.20 = (bf16[128,384]{1,0:T(8,128)(2,1)S(1)}, bf16[128,384]{1,0:T(8,128)(2,1)S(1)}, u32[]{:S(2)}, u32[]{:S(2)}) collective-permute-start(bf16[128,384]{1,0:T(8,128)(2,1)S(1)} %get-tuple-element.55), channel_id=1, source_target_pairs={{0,1},{1,0},{2,3},{3,2},{4,5},{5,4},{6,7},{7,6},{8,9},{9,8},{10,11... | collective-permute-start | bytes 294920 | tf_op jit(solution)/shard_map/ppermute | solution.py:83
  96.4 5.4 %collective-permute-start.21 = (bf16[128,384]{1,0:T(8,128)(2,1)S(1)}, bf16[128,384]{1,0:T(8,128)(2,1)S(1)}, u32[]{:S(2)}, u32[]{:S(2)}) collective-permute-start(bf16[128,384]{1,0:T(8,128)(2,1)S(1)} %get-tuple-element.56), channel_id=1, source_target_pairs={{0,4},{1,5},{2,6},{3,7},{4,0},{5,1},{6,2},{7,3},{8,12},{9,13},{10,... | collective-permute-start | bytes 294920 | tf_op jit(solution)/shard_map/ppermute | solution.py:83
  98.7 5.2 %collective-permute-start.22 = (bf16[128,384]{1,0:T(8,128)(2,1)S(1)}, bf16[128,384]{1,0:T(8,128)(2,1)S(1)}, u32[]{:S(2)}, u32[]{:S(2)}) collective-permute-start(bf16[128,384]{1,0:T(8,128)(2,1)S(1)} %get-tuple-element.57), channel_id=1, source_target_pairs={{0,5},{1,4},{2,7},{3,6},{4,1},{5,0},{6,3},{7,2},{8,13},{9,12},{10,... | collective-permute-start | bytes 294920 | tf_op jit(solution)/shard_map/ppermute | solution.py:83

commit v5 on v4

--- a/solution.py
+++ b/solution.py
@@ -290,7 +290,7 @@
 
     own_columns = column_part(mine)
     columns = [own_columns] + [
-        shift(after(column_part(mine ^ q), key_next, key_mate), "seq", q << 1)
+        shift(column_part(mine ^ q), "seq", q << 1)
         for q in range(1, plan.col)
     ]
     high_columns = [
@@ -309,9 +309,11 @@
         name="attention_forward",
     )(neighbour, query, key, value, *beside)
 
-    pairs = [attended[0]] + [
-        shift(attended[t >> plan.col_bits], "seq", t << 1) for t in range(1, plan.pairs)
-    ]
+    pairs = [attended[0]] + [shift(attended[0], "seq", q << 1) for q in range(1, plan.col)]
+    for high in range(1, plan.high):
+        came_high = shift(attended[high], "seq", high << (1 + plan.col_bits))
+        pairs.append(came_high)
+        pairs += [shift(came_high, "seq", q << 1) for q in range(1, plan.col)]
     through = after(jnp.stack(columns[1:]), attended)
     held = [jnp.stack(columns)]
     for high in range(1, plan.high):
@@ -374,22 +376,18 @@
         held,
     )
 
-    half = mine_width // 2
-    first_step = []
-    extra = {(i, start): [] for i in range(m) for start in (0, half)}
+    extra = {i: [] for i in range(m)}
+    sent = []
     bit = 1
     while bit < m:
         for i in range(m - 1, 1, -1):
             if i & -i == bit:
-                for start in (0, half):
-                    part = shift(added(blocks[i] + extra[i, start], start, half), "dp", bit)
-                    if bit == 1:
-                        first_step.append(part)
-                    extra[i ^ bit, start].append((part, None, start))
+                sent.append(added(blocks[i] + extra[i], 0, mine_width))
+                extra[i ^ bit].append((shift(sent[-1], "dp", bit), None, 0))
         bit *= 2
-    near = shift(after(added(blocks[1], 0, mine_width), *first_step), "dp", 1)
+    near = shift(after(added(blocks[1], 0, mine_width), sent[-1]), "dp", 1)
     own = blocks[0][0][0]
-    came = [blocks[0][1], (near, None, 0)] + extra[0, 0] + extra[0, half]
+    came = [blocks[0][1], (near, None, 0)] + extra[0]
 
     x, gram = pl.pallas_call(
         functools.partial(gram_kernel, [spot for _, *spot in came]),

time: 105 us -> 108 us (1.029)
  waiting for transfers between devices: 56 us -> 57.7 us
    ppermute x1, waiting for transfers between devices: 4.75 us -> 7.69 us  [local(): value_next = lax.ppermute(value, 'seq', takes)]
    ppermute x20 -> x18, starting transfers between devices: 20.8 us -> 21.6 us  [shift(): lax.ppermute(value, axis, [(i, i ^ mask) for i in range(lax.axis_size(axi...]
    ppermute x20 -> x18, waiting for transfers between devices: 50 us -> 49.4 us  [shift(): lax.ppermute(value, axis, [(i, i ^ mask) for i in range(lax.axis_size(axi...]
  transfers between devices with their start and end apart: 23 -> 21, of which waited for: 14 -> 11; matrix products, arithmetic and copies ran while one was open for 2% -> 2% of each run, Pallas kernels for 12% -> 12%
where the time goes in v5:
time: 108 us
  waiting for transfers between devices  57.7 us (53%)
  starting transfers between devices  31.1 us (29%)
  Pallas kernels  16.1 us (15%)
  local copies, waits for them, and re-layouts  1.44 us (1%)
    ppermute x18, waiting for transfers between devices, shift(): lax.ppermute(value, axis, [(i, i ^ mask) for i in range(lax.axis_size(axi...  49.4 us
    ppermute x18, starting transfers between devices, shift(): lax.ppermute(value, axis, [(i, i ^ mask) for i in range(lax.axis_size(axi...  21.6 us
    ppermute x1, waiting for transfers between devices, local(): value_next = lax.ppermute(value, 'seq', takes)  7.69 us
    ppermute x1, starting transfers between devices, local(): key_next = lax.ppermute(key, 'seq', takes)  4.54 us
    pallas_call x1, Pallas kernels, local(): pl.pallas_call(functools.partial(update_kernel, plan, factor), out_shape=...  3.93 us
    pallas_call x1, Pallas kernels, local(): pl.pallas_call(backward_kernel, out_shape=[struct((tile, width), bf16), s...  3.91 us
    ppermute x1, starting transfers between devices, local(): value_next = lax.ppermute(value, 'seq', takes)  3.49 us
    pallas_call x1, Pallas kernels, local(): pl.pallas_call(functools.partial(forward_kernel, plan), out_shape=struct(...  2.29 us
  transfers between devices with their start and end apart: 21, of which 11 were waited for; matrix products, arithmetic and copies ran while one was open for 2% of the time, Pallas kernels for 12%

profile of v5, /device:TPU:1, one launch (start us, length us, event | category | flops | bytes accessed | tf_op | source)
XLA Modules:
  0.0 107.5 jit_solution(328205696227506943)
XLA Ops:
  0.6 4.5 %collective-permute-start.2 = (bf16[128,2048]{1,0:T(8,128)(2,1)}, bf16[128,2048]{1,0:T(8,128)(2,1)S(1)}, u32[]{:S(2)}, u32[]{:S(2)}) collective-permute-start(bf16[128,2048]{1,0:T(8,128)(2,1)} %bitcast.25), channel_id=1, source_target_pairs={{1,2},{3,4},{4,3},{6,5},{9,10},{11,12},{12,11},{14,13},{17,18},{19... | collective-permute-start | bytes 1572872 | tf_op jit(solution)/shard_map/ppermute | solution.py:271
  5.2 0.1 collective-permute-start
  5.3 3.5 %collective-permute-start.3 = (bf16[128,2048]{1,0:T(8,128)(2,1)}, bf16[128,2048]{1,0:T(8,128)(2,1)S(1)}, u32[]{:S(2)}, u32[]{:S(2)}) collective-permute-start(bf16[128,2048]{1,0:T(8,128)(2,1)} %bitcast.29), channel_id=1, source_target_pairs={{1,2},{3,4},{4,3},{6,5},{9,10},{11,12},{12,11},{14,13},{17,18},{19... | collective-permute-start | bytes 1572872 | tf_op jit(solution)/shard_map/ppermute | solution.py:272
  8.8 0.1 collective-permute-start.1
  8.8 0.0 copy-start
  8.9 0.0 copy-start.1
  8.9 0.0 copy-start.2
  8.9 0.0 copy-start.4
  8.9 1.4 %dynamic-slice_bitcast_fusion.3 = (bf16[128,768]{1,0:T(8,128)(2,1)S(1)}, bf16[128,768]{1,0:T(8,128)(2,1)S(1)}, bf16[128,768]{1,0:T(8,128)(2,1)S(1)}, bf16[128,768]{1,0:T(8,128)(2,1)S(1)}) fusion(bf16[1,1,128,3072]{3,2,1,0:T(8,128)(2,1)} %param.10, s32[]{:T(128)S(6)} %select_n.12, s32[]{:T(128)S(6)} %select_n.13, s32[]{:T(128)S(6)} %select_n.15, s32[]{:T(128)S(6)} %select_n.14), kind=kLoop, calls=%fused_computation.8 | loop fusion | bytes 1572880 | tf_op jit(solution)/shard_map/dynamic_slice | solution.py:285
  10.3 0.5 collective-permute-start.7
  10.9 0.1 fusion
  10.9 0.7 collective-permute-done.2.kn
  11.6 0.0 collective-permute-done.km
  11.6 2.1 %collective-permute-start.8 = (bf16[128,1536]{1,0:T(8,128)(2,1)S(1)}, bf16[128,1536]{1,0:T(8,128)(2,1)S(1)}, u32[]{:S(2)}, u32[]{:S(2)}) collective-permute-start(bf16[128,1536]{1,0:T(8,128)(2,1)S(1)} %get-tuple-element.36), channel_id=1, source_target_pairs={{0,4},{1,5},{2,6},{3,7},{4,0},{5,1},{6,2},{7,3},{8,12},{9,13},{10,... | collective-permute-start | bytes 1179656 | tf_op jit(solution)/shard_map/ppermute | solution.py:83
  13.7 7.7 %collective-permute-done.3.vn = bf16[128,2048]{1,0:T(8,128)(2,1)S(1)} collective-permute-done((bf16[128,2048]{1,0:T(8,128)(2,1)}, bf16[128,2048]{1,0:T(8,128)(2,1)S(1)}, u32[]{:S(2)}, u32[]{:S(2)}) %collective-permute-start.3) | collective-permute-done | bytes 524320 | tf_op jit(solution)/shard_map/ppermute | solution.py:272
  21.4 0.0 collective-permute-done.1.vm
  21.4 0.0 copy-done
  21.4 0.0 copy-done.2
  21.4 0.0 copy-start.3
  21.4 2.3 %attention_forward.1 = bf16[2,2,512,128]{3,2,1,0:T(8,128)(2,1)S(1)} custom-call(s32[1,8]{1,0:T(1,128)S(1)} %copy-done.4, bf16[128,2048]{1,0:T(8,128)(2,1)S(1)} %bitcast.23, bf16[128,2048]{1,0:T(8,128)(2,1)S(1)} %bitcast.27, bf16[128,2048]{1,0:T(8,128)(2,1)S(1)} %bitcast.31, bf16[128,2048]{1,0:T(8,128)(2,1)S(1)} %collective-permute-done.km, ...), custom_call_target="tpu_custom_call" | custom-call | flops 268435456 | bytes 4194304 | tf_op jit(solution)/shard_map/attention_forward/pallas_call | solution.py:301
  23.7 3.4 %collective-permute-done.7 = bf16[128,1536]{1,0:T(8,128)(2,1)S(1)} collective-permute-done((bf16[128,1536]{1,0:T(8,128)(2,1)S(1)}, bf16[128,1536]{1,0:T(8,128)(2,1)S(1)}, u32[]{:S(2)}, u32[]{:S(2)}) %collective-permute-start.7) | collective-permute-done | bytes 393248 | tf_op jit(solution)/shard_map/ppermute | solution.py:83
  27.2 0.0 collective-permute-start.9
  27.2 1.5 %collective-permute-start.5 = (bf16[2,512,128]{2,1,0:T(8,128)(2,1)S(1)}, bf16[2,512,128]{2,1,0:T(8,128)(2,1)S(1)}, u32[]{:S(2)}, u32[]{:S(2)}) collective-permute-start(bf16[2,512,128]{2,1,0:T(8,128)(2,1)S(1)} %get-tuple-element.60), channel_id=1, source_target_pairs={{0,4},{1,5},{2,6},{3,7},{4,0},{5,1},{6,2},{7,3},{8,12},{9,13},{10,... | collective-permute-start | bytes 786440 | tf_op jit(solution)/shard_map/ppermute | solution.py:83
  28.7 0.5 collective-permute-start.4
  29.3 0.0 copy-done.3
  29.3 3.9 %attention_backward.1 = (bf16[128,2048]{1,0:T(8,128)(2,1)}, f32[128,2048]{1,0:T(8,128)S(1)}, f32[128,2048]{1,0:T(8,128)S(1)}, bf16[2,128,2048]{2,1,0:T(8,128)(2,1)S(1)}) custom-call(s32[1,8]{1,0:T(1,128)S(1)} %copy-done.4, bf16[128,2048]{1,0:T(8,128)(2,1)S(1)} %bitcast.24, bf16[128,2048]{1,0:T(8,128)(2,1)S(1)} %bitcast.28, bf16[128,2048]{1,0:T(8,128)(2,1)S(1)} %bitcast.32, ...), custom_call_target="tpu_custom_call" | custom-call | flops 939524096 | bytes 7864320 | tf_op jit(solution)/shard_map/attention_backward/pallas_call | solution.py:324
  33.2 10.1 %collective-permute-done.5.refs_2_ = bf16[2,512,128]{2,1,0:T(8,128)(2,1)S(1)} collective-permute-done((bf16[2,512,128]{2,1,0:T(8,128)(2,1)S(1)}, bf16[2,512,128]{2,1,0:T(8,128)(2,1)S(1)}, u32[]{:S(2)}, u32[]{:S(2)}) %collective-permute-start.5) | collective-permute-done | bytes 262176 | tf_op jit(solution)/shard_map/ppermute | solution.py:83
  43.3 0.9 collective-permute-start.6
  44.2 0.0 collective-permute-done.8
  44.2 0.0 collective-permute-done.9
  44.2 0.2 pad_maximum_fusion.refs_4_
  44.4 0.0 collective-permute-done.4.refs_1_
  44.4 6.4 %collective-permute-done.6.refs_3_ = bf16[2,512,128]{2,1,0:T(8,128)(2,1)S(1)} collective-permute-done((bf16[2,512,128]{2,1,0:T(8,128)(2,1)S(1)}, bf16[2,512,128]{2,1,0:T(8,128)(2,1)S(1)}, u32[]{:S(2)}, u32[]{:S(2)}) %collective-permute-start.6) | collective-permute-done | bytes 262176 | tf_op jit(solution)/shard_map/ppermute | solution.py:83
  50.8 0.6 product_first.1
  51.4 1.4 %product_rest.1 = (f32[128,1536]{1,0:T(8,128)S(1)}, f32[128,1536]{1,0:T(8,128)S(1)}, f32[128,1536]{1,0:T(8,128)S(1)}, bf16[3,128,1536]{2,1,0:T(8,128)(2,1)S(1)}) custom-call(bf16[2,512,128]{2,1,0:T(8,128)(2,1)S(1)} %get-tuple-element.39.refs_0_, bf16[2,512,128]{2,1,0:T(8,128)(2,1)S(1)} %collective-permute-done.4.refs_1_, ...), custom_call_target="tpu_custom_call" | custom-call | flops 1207959552 | bytes 1572864 | tf_op jit(solution)/shard_map/product_rest/pallas_call | solution.py:341
  52.8 1.3 %collective-permute-start.12 = (bf16[3,128,1536]{2,1,0:T(8,128)(2,1)S(1)}, bf16[3,128,1536]{2,1,0:T(8,128)(2,1)S(1)}, u32[]{:S(2)}, u32[]{:S(2)}) collective-permute-start(bf16[3,128,1536]{2,1,0:T(8,128)(2,1)S(1)} %get-tuple-element.44), channel_id=1, source_target_pairs={{0,1},{1,0},{2,3},{3,2},{4,5},{5,4},{6,7},{7,6},{8,9},{9,8},{10,11... | collective-permute-start | bytes 3538952 | tf_op jit(solution)/shard_map/ppermute | solution.py:83
  54.1 0.1 collective-permute-start.13
  54.2 1.5 %collective-permute-start.11 = (bf16[2,128,2048]{2,1,0:T(8,128)(2,1)S(1)}, bf16[2,128,2048]{2,1,0:T(8,128)(2,1)S(1)}, u32[]{:S(2)}, u32[]{:S(2)}) collective-permute-start(bf16[2,128,2048]{2,1,0:T(8,128)(2,1)S(1)} %get-tuple-element.41), channel_id=1, source_target_pairs={{3,4},{5,6},{2,1},{4,3},{11,12},{13,14},{10,9},{12,11},{19,20},{21... | collective-permute-start | bytes 3145736 | tf_op jit(solution)/shard_map/ppermute | solution.py:431
  55.7 0.1 collective-permute-start.10
  55.8 1.4 %collective-permute-done.13.refs_1_ = bf16[1,128,1536]{2,1,0:T(8,128)(2,1)S(1)} collective-permute-done((bf16[1,128,1536]{2,1,0:T(8,128)(2,1)S(1)}, bf16[1,128,1536]{2,1,0:T(8,128)(2,1)S(1)}, u32[]{:S(2)}, u32[]{:S(2)}) %collective-permute-start.13) | collective-permute-done | bytes 393248 | tf_op jit(solution)/shard_map/ppermute | solution.py:83
  57.2 0.1 block_sum.4
  57.3 1.4 %collective-permute-start.14 = (bf16[128,1536]{1,0:T(8,128)(2,1)S(1)}, bf16[128,1536]{1,0:T(8,128)(2,1)S(1)}, u32[]{:S(2)}, u32[]{:S(2)}) collective-permute-start(bf16[128,1536]{1,0:T(8,128)(2,1)S(1)} %block_sum.4), channel_id=1, source_target_pairs={{0,8},{8,0},{16,24},{24,16},{1,9},{9,1},{17,25},{25,17},{2,10},{10... | collective-permute-start | bytes 1179656 | tf_op jit(solution)/shard_map/ppermute | solution.py:83
  58.6 0.0 collective-permute-done.12.refs_1_.refs_0_
  58.6 0.1 block_sum.3
  58.7 9.0 %collective-permute-done.14.refs_2_ = bf16[128,1536]{1,0:T(8,128)(2,1)S(1)} collective-permute-done((bf16[128,1536]{1,0:T(8,128)(2,1)S(1)}, bf16[128,1536]{1,0:T(8,128)(2,1)S(1)}, u32[]{:S(2)}, u32[]{:S(2)}) %collective-permute-start.14) | collective-permute-done | bytes 393248 | tf_op jit(solution)/shard_map/ppermute | solution.py:83
  67.7 0.2 block_sum.5
  67.8 1.4 %collective-permute-start.15 = (bf16[128,1536]{1,0:T(8,128)(2,1)S(1)}, bf16[128,1536]{1,0:T(8,128)(2,1)S(1)}, u32[]{:S(2)}, u32[]{:S(2)}) collective-permute-start(bf16[128,1536]{1,0:T(8,128)(2,1)S(1)} %block_sum.3), channel_id=1, source_target_pairs={{0,8},{8,0},{16,24},{24,16},{1,9},{9,1},{17,25},{25,17},{2,10},{10... | collective-permute-start | bytes 1179656 | tf_op jit(solution)/shard_map/ppermute | solution.py:83
  69.2 2.3 %collective-permute-start.16 = (bf16[128,1536]{1,0:T(8,128)(2,1)S(1)}, bf16[128,1536]{1,0:T(8,128)(2,1)S(1)}, u32[]{:S(2)}, u32[]{:S(2)}) collective-permute-start(bf16[128,1536]{1,0:T(8,128)(2,1)S(1)} %block_sum.5), channel_id=1, source_target_pairs={{0,16},{8,24},{16,0},{24,8},{1,17},{9,25},{17,1},{25,9},{2,18},{10... | collective-permute-start | bytes 1179656 | tf_op jit(solution)/shard_map/ppermute | solution.py:83
  71.5 14.1 %collective-permute-done.15.refs_1_ = bf16[128,1536]{1,0:T(8,128)(2,1)S(1)} collective-permute-done((bf16[128,1536]{1,0:T(8,128)(2,1)S(1)}, bf16[128,1536]{1,0:T(8,128)(2,1)S(1)}, u32[]{:S(2)}, u32[]{:S(2)}) %collective-permute-start.15) | collective-permute-done | bytes 393248 | tf_op jit(solution)/shard_map/ppermute | solution.py:83
  85.6 0.0 collective-permute-done.16.refs_2_
  85.6 0.9 gradient_sum.1
  86.5 1.7 %collective-permute-start.17 = (f32[128,128]{1,0:T(8,128)S(1)}, f32[128,128]{1,0:T(8,128)S(1)}, u32[]{:S(2)}, u32[]{:S(2)}) collective-permute-start(f32[128,128]{1,0:T(8,128)S(1)} %get-tuple-element.50.gram), channel_id=1, source_target_pairs={{0,2},{1,3},{2,0},{3,1},{4,6},{5,7},{6,4},{7,5},{8,10},{9,11},{10,... | collective-permute-start | bytes 196616 | tf_op jit(solution)/shard_map/ppermute | solution.py:83
  88.2 1.7 %collective-permute-done.17.gram_other = f32[128,128]{1,0:T(8,128)S(1)} collective-permute-done((f32[128,128]{1,0:T(8,128)S(1)}, f32[128,128]{1,0:T(8,128)S(1)}, u32[]{:S(2)}, u32[]{:S(2)}) %collective-permute-start.17) | collective-permute-done | bytes 65568 | tf_op jit(solution)/shard_map/ppermute | solution.py:83
  89.8 3.9 %newton_schulz.1 = (f32[128,384]{1,0:T(8,128)S(1)}, bf16[128,384]{1,0:T(8,128)(2,1)S(1)}, bf16[128,384]{1,0:T(8,128)(2,1)S(1)}, bf16[128,384]{1,0:T(8,128)(2,1)S(1)}) custom-call(f32[128,1536]{1,0:T(8,128)S(1)} %get-tuple-element.49.x, f32[128,128]{1,0:T(8,128)S(1)} %get-tuple-element.50.gram, f32[128,128]{1,0:T(8,128)S(1)} %collective-permute-done.17.gram_other), custom_call_target="tpu_custom_call" | custom-call | flops 301989888 | bytes 1572864 | tf_op jit(solution)/shard_map/newton_schulz/pallas_call | solution.py:408
  93.8 5.5 %collective-permute-start.18 = (bf16[128,384]{1,0:T(8,128)(2,1)S(1)}, bf16[128,384]{1,0:T(8,128)(2,1)S(1)}, u32[]{:S(2)}, u32[]{:S(2)}) collective-permute-start(bf16[128,384]{1,0:T(8,128)(2,1)S(1)} %get-tuple-element.53), channel_id=1, source_target_pairs={{0,1},{1,0},{2,3},{3,2},{4,5},{5,4},{6,7},{7,6},{8,9},{9,8},{10,11... | collective-permute-start | bytes 294920 | tf_op jit(solution)/shard_map/ppermute | solution.py:83
  99.3 2.1 %collective-permute-start.19 = (bf16[128,384]{1,0:T(8,128)(2,1)S(1)}, bf16[128,384]{1,0:T(8,128)(2,1)S(1)}, u32[]{:S(2)}, u32[]{:S(2)}) collective-permute-start(bf16[128,384]{1,0:T(8,128)(2,1)S(1)} %get-tuple-element.54), channel_id=1, source_target_pairs={{0,4},{1,5},{2,6},{3,7},{4,0},{5,1},{6,2},{7,3},{8,12},{9,13},{10,... | collective-permute-start | bytes 294920 | tf_op jit(solution)/shard_map/ppermute | solution.py:83
  101.4 0.0 collective-permute-start.20
  101.4 0.0 collective-permute-done.11.beyond
  101.4 0.0 collective-permute-done.10.mate
  101.4 1.8 %key_value_sum.1 = (bf16[128,2048]{1,0:T(8,128)(2,1)}, bf16[128,2048]{1,0:T(8,128)(2,1)}) custom-call(s32[1,8]{1,0:T(1,128)S(1)} %copy-done.4, f32[128,2048]{1,0:T(8,128)S(1)} %get-tuple-element.32.dko, f32[128,2048]{1,0:T(8,128)S(1)} %get-tuple-element.33.dvo, bf16[2,128,2048]{2,1,0:T(8,128)(2,1)S(1)} %collective-permute-done.10.mate, ...), custom_call_target="tpu_custom_call" | custom-call | flops 1572864 | bytes 5242880 | tf_op jit(solution)/shard_map/key_value_sum/pallas_call | solution.py:418
  103.3 0.0 collective-permute-done.18.refs_1_
  103.3 1.2 %collective-permute-done.19.refs_2_ = bf16[128,384]{1,0:T(8,128)(2,1)S(1)} collective-permute-done((bf16[128,384]{1,0:T(8,128)(2,1)S(1)}, bf16[128,384]{1,0:T(8,128)(2,1)S(1)}, u32[]{:S(2)}, u32[]{:S(2)}) %collective-permute-start.19) | collective-permute-done | bytes 98336 | tf_op jit(solution)/shard_map/ppermute | solution.py:83
  104.5 2.1 %collective-permute-done.20.refs_3_ = bf16[128,384]{1,0:T(8,128)(2,1)S(1)} collective-permute-done((bf16[128,384]{1,0:T(8,128)(2,1)S(1)}, bf16[128,384]{1,0:T(8,128)(2,1)S(1)}, u32[]{:S(2)}, u32[]{:S(2)}) %collective-permute-start.20) | collective-permute-done | bytes 98336 | tf_op jit(solution)/shard_map/ppermute | solution.py:83
  106.6 0.9 update_rows.1
  (4 shorter events, 0.1 us)
Async XLA Ops:
  0.6 10.9 %collective-permute-start.2 = (bf16[128,2048]{1,0:T(8,128)(2,1)}, bf16[128,2048]{1,0:T(8,128)(2,1)S(1)}, u32[]{:S(2)}, u32[]{:S(2)}) collective-permute-start(bf16[128,2048]{1,0:T(8,128)(2,1)} %bitcast.25), channel_id=1, source_target_pairs={{1,2},{3,4},{4,3},{6,5},{9,10},{11,12},{12,11},{14,13},{17,18},{19... | collective-permute-start | bytes 1572872 | tf_op jit(solution)/shard_map/ppermute | solution.py:271
  5.2 6.4 %collective-permute-start = (bf16[128,2048]{1,0:T(8,128)(2,1)}, bf16[128,2048]{1,0:T(8,128)(2,1)S(1)}, u32[]{:S(2)}, u32[]{:S(2)}) collective-permute-start(bf16[128,2048]{1,0:T(8,128)(2,1)} %bitcast.26), channel_id=1, source_target_pairs={{0,1},{1,0},{2,3},{3,2},{4,5},{5,4},{6,7},{7,6},{8,9},{9,8},{10,11... | collective-permute-start | bytes 1572872 | tf_op jit(solution)/shard_map/ppermute | solution.py:83
  5.3 16.1 %collective-permute-start.3 = (bf16[128,2048]{1,0:T(8,128)(2,1)}, bf16[128,2048]{1,0:T(8,128)(2,1)S(1)}, u32[]{:S(2)}, u32[]{:S(2)}) collective-permute-start(bf16[128,2048]{1,0:T(8,128)(2,1)} %bitcast.29), channel_id=1, source_target_pairs={{1,2},{3,4},{4,3},{6,5},{9,10},{11,12},{12,11},{14,13},{17,18},{19... | collective-permute-start | bytes 1572872 | tf_op jit(solution)/shard_map/ppermute | solution.py:272
  8.8 12.6 %collective-permute-start.1 = (bf16[128,2048]{1,0:T(8,128)(2,1)}, bf16[128,2048]{1,0:T(8,128)(2,1)S(1)}, u32[]{:S(2)}, u32[]{:S(2)}) collective-permute-start(bf16[128,2048]{1,0:T(8,128)(2,1)} %bitcast.30), channel_id=1, source_target_pairs={{0,1},{1,0},{2,3},{3,2},{4,5},{5,4},{6,7},{7,6},{8,9},{9,8},{10,11... | collective-permute-start | bytes 1572872 | tf_op jit(solution)/shard_map/ppermute | solution.py:83
  8.8 12.6 %copy-start = (bf16[1,1,128,2048]{3,2,1,0:T(8,128)(2,1)S(1)}, bf16[1,1,128,2048]{3,2,1,0:T(8,128)(2,1)}, u32[]{:S(2)}) copy-start(bf16[1,1,128,2048]{3,2,1,0:T(8,128)(2,1)} %param.6) | copy-start | bytes 1572868
  8.9 12.5 %copy-start.1 = (bf16[1,1,128,2048]{3,2,1,0:T(8,128)(2,1)S(1)}, bf16[1,1,128,2048]{3,2,1,0:T(8,128)(2,1)}, u32[]{:S(2)}) copy-start(bf16[1,1,128,2048]{3,2,1,0:T(8,128)(2,1)} %param.7) | copy-start | bytes 1572868
  8.9 12.5 %copy-start.2 = (bf16[1,1,128,2048]{3,2,1,0:T(8,128)(2,1)S(1)}, bf16[1,1,128,2048]{3,2,1,0:T(8,128)(2,1)}, u32[]{:S(2)}) copy-start(bf16[1,1,128,2048]{3,2,1,0:T(8,128)(2,1)} %param.8) | copy-start | bytes 1572868
  8.9 12.5 %copy-start.4 = (s32[1,8]{1,0:T(1,128)S(1)}, s32[1,8]{1,0:T(1,128)}, u32[]{:S(2)}) copy-start(s32[1,8]{1,0:T(1,128)} %near_ref.5) | copy-start | bytes 100
  10.3 16.8 %collective-permute-start.7 = (bf16[128,1536]{1,0:T(8,128)(2,1)S(1)}, bf16[128,1536]{1,0:T(8,128)(2,1)S(1)}, u32[]{:S(2)}, u32[]{:S(2)}) collective-permute-start(bf16[128,1536]{1,0:T(8,128)(2,1)S(1)} %pad_maximum_fusion.2), channel_id=1, source_target_pairs={{0,2},{1,3},{2,0},{3,1},{4,6},{5,7},{6,4},{7,5},{8,10},{9,11},{10,... | collective-permute-start | bytes 1179656 | tf_op jit(solution)/shard_map/ppermute | solution.py:83
  11.6 32.6 %collective-permute-start.8 = (bf16[128,1536]{1,0:T(8,128)(2,1)S(1)}, bf16[128,1536]{1,0:T(8,128)(2,1)S(1)}, u32[]{:S(2)}, u32[]{:S(2)}) collective-permute-start(bf16[128,1536]{1,0:T(8,128)(2,1)S(1)} %get-tuple-element.36), channel_id=1, source_target_pairs={{0,4},{1,5},{2,6},{3,7},{4,0},{5,1},{6,2},{7,3},{8,12},{9,13},{10,... | collective-permute-start | bytes 1179656 | tf_op jit(solution)/shard_map/ppermute | solution.py:83
  21.4 7.9 %copy-start.3 = (bf16[1,1,128,2048]{3,2,1,0:T(8,128)(2,1)S(1)}, bf16[1,1,128,2048]{3,2,1,0:T(8,128)(2,1)}, u32[]{:S(2)}) copy-start(bf16[1,1,128,2048]{3,2,1,0:T(8,128)(2,1)} %param.9) | copy-start | bytes 1572868
  27.2 17.0 %collective-permute-start.9 = (bf16[1,128,1536]{2,1,0:T(8,128)(2,1)S(1)}, bf16[1,128,1536]{2,1,0:T(8,128)(2,1)S(1)}, u32[]{:S(2)}, u32[]{:S(2)}) collective-permute-start(bf16[1,128,1536]{2,1,0:T(8,128)(2,1)S(1)} %bitcast.34), channel_id=1, source_target_pairs={{0,4},{1,5},{2,6},{3,7},{4,0},{5,1},{6,2},{7,3},{8,12},{9,13},{10,... | collective-permute-start | bytes 1179656 | tf_op jit(solution)/shard_map/ppermute | solution.py:83
  27.2 16.1 %collective-permute-start.5 = (bf16[2,512,128]{2,1,0:T(8,128)(2,1)S(1)}, bf16[2,512,128]{2,1,0:T(8,128)(2,1)S(1)}, u32[]{:S(2)}, u32[]{:S(2)}) collective-permute-start(bf16[2,512,128]{2,1,0:T(8,128)(2,1)S(1)} %get-tuple-element.60), channel_id=1, source_target_pairs={{0,4},{1,5},{2,6},{3,7},{4,0},{5,1},{6,2},{7,3},{8,12},{9,13},{10,... | collective-permute-start | bytes 786440 | tf_op jit(solution)/shard_map/ppermute | solution.py:83
  28.7 15.7 %collective-permute-start.4 = (bf16[2,512,128]{2,1,0:T(8,128)(2,1)S(1)}, bf16[2,512,128]{2,1,0:T(8,128)(2,1)S(1)}, u32[]{:S(2)}, u32[]{:S(2)}) collective-permute-start(bf16[2,512,128]{2,1,0:T(8,128)(2,1)S(1)} %get-tuple-element.39.refs_0_), channel_id=1, source_target_pairs={{0,2},{1,3},{2,0},{3,1},{4,6},{5,7},{6,4},{7,5},{8,10},{9,11},{10,... | collective-permute-start | bytes 786440 | tf_op jit(solution)/shard_map/ppermute | solution.py:83
  43.3 7.5 %collective-permute-start.6 = (bf16[2,512,128]{2,1,0:T(8,128)(2,1)S(1)}, bf16[2,512,128]{2,1,0:T(8,128)(2,1)S(1)}, u32[]{:S(2)}, u32[]{:S(2)}) collective-permute-start(bf16[2,512,128]{2,1,0:T(8,128)(2,1)S(1)} %collective-permute-done.5.refs_2_), channel_id=1, source_target_pairs={{0,2},{1,3},{2,0},{3,1},{4,6},{5,7},{6,4},{7,5},{8,10},{9,11},{10,... | collective-permute-start | bytes 786440 | tf_op jit(solution)/shard_map/ppermute | solution.py:83
  52.8 5.8 %collective-permute-start.12 = (bf16[3,128,1536]{2,1,0:T(8,128)(2,1)S(1)}, bf16[3,128,1536]{2,1,0:T(8,128)(2,1)S(1)}, u32[]{:S(2)}, u32[]{:S(2)}) collective-permute-start(bf16[3,128,1536]{2,1,0:T(8,128)(2,1)S(1)} %get-tuple-element.44), channel_id=1, source_target_pairs={{0,1},{1,0},{2,3},{3,2},{4,5},{5,4},{6,7},{7,6},{8,9},{9,8},{10,11... | collective-permute-start | bytes 3538952 | tf_op jit(solution)/shard_map/ppermute | solution.py:83
  54.1 3.0 %collective-permute-start.13 = (bf16[1,128,1536]{2,1,0:T(8,128)(2,1)S(1)}, bf16[1,128,1536]{2,1,0:T(8,128)(2,1)S(1)}, u32[]{:S(2)}, u32[]{:S(2)}) collective-permute-start(bf16[1,128,1536]{2,1,0:T(8,128)(2,1)S(1)} %get-tuple-element.47), channel_id=1, source_target_pairs={{0,1},{1,0},{2,3},{3,2},{4,5},{5,4},{6,7},{7,6},{8,9},{9,8},{10,11... | collective-permute-start | bytes 1179656 | tf_op jit(solution)/shard_map/ppermute | solution.py:83
  54.2 47.2 %collective-permute-start.11 = (bf16[2,128,2048]{2,1,0:T(8,128)(2,1)S(1)}, bf16[2,128,2048]{2,1,0:T(8,128)(2,1)S(1)}, u32[]{:S(2)}, u32[]{:S(2)}) collective-permute-start(bf16[2,128,2048]{2,1,0:T(8,128)(2,1)S(1)} %get-tuple-element.41), channel_id=1, source_target_pairs={{3,4},{5,6},{2,1},{4,3},{11,12},{13,14},{10,9},{12,11},{19,20},{21... | collective-permute-start | bytes 3145736 | tf_op jit(solution)/shard_map/ppermute | solution.py:431
  55.7 45.7 %collective-permute-start.10 = (bf16[2,128,2048]{2,1,0:T(8,128)(2,1)S(1)}, bf16[2,128,2048]{2,1,0:T(8,128)(2,1)S(1)}, u32[]{:S(2)}, u32[]{:S(2)}) collective-permute-start(bf16[2,128,2048]{2,1,0:T(8,128)(2,1)S(1)} %get-tuple-element.41), channel_id=1, source_target_pairs={{0,1},{1,0},{2,3},{3,2},{4,5},{5,4},{6,7},{7,6},{8,9},{9,8},{10,11... | collective-permute-start | bytes 3145736 | tf_op jit(solution)/shard_map/ppermute | solution.py:83
  57.3 10.4 %collective-permute-start.14 = (bf16[128,1536]{1,0:T(8,128)(2,1)S(1)}, bf16[128,1536]{1,0:T(8,128)(2,1)S(1)}, u32[]{:S(2)}, u32[]{:S(2)}) collective-permute-start(bf16[128,1536]{1,0:T(8,128)(2,1)S(1)} %block_sum.4), channel_id=1, source_target_pairs={{0,8},{8,0},{16,24},{24,16},{1,9},{9,1},{17,25},{25,17},{2,10},{10... | collective-permute-start | bytes 1179656 | tf_op jit(solution)/shard_map/ppermute | solution.py:83
  67.8 17.8 %collective-permute-start.15 = (bf16[128,1536]{1,0:T(8,128)(2,1)S(1)}, bf16[128,1536]{1,0:T(8,128)(2,1)S(1)}, u32[]{:S(2)}, u32[]{:S(2)}) collective-permute-start(bf16[128,1536]{1,0:T(8,128)(2,1)S(1)} %block_sum.3), channel_id=1, source_target_pairs={{0,8},{8,0},{16,24},{24,16},{1,9},{9,1},{17,25},{25,17},{2,10},{10... | collective-permute-start | bytes 1179656 | tf_op jit(solution)/shard_map/ppermute | solution.py:83
  69.2 16.4 %collective-permute-start.16 = (bf16[128,1536]{1,0:T(8,128)(2,1)S(1)}, bf16[128,1536]{1,0:T(8,128)(2,1)S(1)}, u32[]{:S(2)}, u32[]{:S(2)}) collective-permute-start(bf16[128,1536]{1,0:T(8,128)(2,1)S(1)} %block_sum.5), channel_id=1, source_target_pairs={{0,16},{8,24},{16,0},{24,8},{1,17},{9,25},{17,1},{25,9},{2,18},{10... | collective-permute-start | bytes 1179656 | tf_op jit(solution)/shard_map/ppermute | solution.py:83
  86.5 3.4 %collective-permute-start.17 = (f32[128,128]{1,0:T(8,128)S(1)}, f32[128,128]{1,0:T(8,128)S(1)}, u32[]{:S(2)}, u32[]{:S(2)}) collective-permute-start(f32[128,128]{1,0:T(8,128)S(1)} %get-tuple-element.50.gram), channel_id=1, source_target_pairs={{0,2},{1,3},{2,0},{3,1},{4,6},{5,7},{6,4},{7,5},{8,10},{9,11},{10,... | collective-permute-start | bytes 196616 | tf_op jit(solution)/shard_map/ppermute | solution.py:83
  93.8 9.5 %collective-permute-start.18 = (bf16[128,384]{1,0:T(8,128)(2,1)S(1)}, bf16[128,384]{1,0:T(8,128)(2,1)S(1)}, u32[]{:S(2)}, u32[]{:S(2)}) collective-permute-start(bf16[128,384]{1,0:T(8,128)(2,1)S(1)} %get-tuple-element.53), channel_id=1, source_target_pairs={{0,1},{1,0},{2,3},{3,2},{4,5},{5,4},{6,7},{7,6},{8,9},{9,8},{10,11... | collective-permute-start | bytes 294920 | tf_op jit(solution)/shard_map/ppermute | solution.py:83
  99.3 5.2 %collective-permute-start.19 = (bf16[128,384]{1,0:T(8,128)(2,1)S(1)}, bf16[128,384]{1,0:T(8,128)(2,1)S(1)}, u32[]{:S(2)}, u32[]{:S(2)}) collective-permute-start(bf16[128,384]{1,0:T(8,128)(2,1)S(1)} %get-tuple-element.54), channel_id=1, source_target_pairs={{0,4},{1,5},{2,6},{3,7},{4,0},{5,1},{6,2},{7,3},{8,12},{9,13},{10,... | collective-permute-start | bytes 294920 | tf_op jit(solution)/shard_map/ppermute | solution.py:83
  101.4 5.2 %collective-permute-start.20 = (bf16[128,384]{1,0:T(8,128)(2,1)S(1)}, bf16[128,384]{1,0:T(8,128)(2,1)S(1)}, u32[]{:S(2)}, u32[]{:S(2)}) collective-permute-start(bf16[128,384]{1,0:T(8,128)(2,1)S(1)} %get-tuple-element.55), channel_id=1, source_target_pairs={{0,5},{1,4},{2,7},{3,6},{4,1},{5,0},{6,3},{7,2},{8,13},{9,12},{10,... | collective-permute-start | bytes 294920 | tf_op jit(solution)/shard_map/ppermute | solution.py:83

commit v6 on v5

--- a/solution.py
+++ b/solution.py
@@ -290,11 +290,11 @@
 
     own_columns = column_part(mine)
     columns = [own_columns] + [
-        shift(column_part(mine ^ q), "seq", q << 1)
+        shift(after(column_part(mine ^ q), key_next, value_next), "seq", q << 1)
         for q in range(1, plan.col)
     ]
     high_columns = [
-        shift(after(own_columns, key_next, key_mate), "seq", high << (1 + plan.col_bits))
+        shift(after(own_columns, key_next, value_next), "seq", high << (1 + plan.col_bits))
         for high in range(1, plan.high)
     ]
 
@@ -385,7 +385,9 @@
                 sent.append(added(blocks[i] + extra[i], 0, mine_width))
                 extra[i ^ bit].append((shift(sent[-1], "dp", bit), None, 0))
         bit *= 2
-    near = shift(after(added(blocks[1], 0, mine_width), sent[-1]), "dp", 1)
+    near = added(blocks[1], 0, mine_width)
+    dfar = after(dfar, near)
+    near = shift(after(near, sent[-1]), "dp", 1)
     own = blocks[0][0][0]
     came = [blocks[0][1], (near, None, 0)] + extra[0]
 
@@ -414,7 +416,6 @@
         cost_estimate=cost(12 * HEAD_DIM * HEAD_DIM * mine_width, 8 * HEAD_DIM * mine_width),
         name="newton_schulz",
     )(x, gram, gram_other)
-    dfar = after(dfar, own)
     dk, dv = pl.pallas_call(
         combine_kernel,
         out_shape=[struct((tile, width), bf16)] * 2,

time: 108 us -> 113 us (1.046)
  waiting for transfers between devices: 57.7 us -> 60.7 us
  starting transfers between devices: 31.1 us -> 32.8 us
    ppermute x18, starting transfers between devices: 21.6 us -> 25.5 us  [shift(): lax.ppermute(value, axis, [(i, i ^ mask) for i in range(lax.axis_size(axi...]
    ppermute x18, waiting for transfers between devices: 49.4 us -> 52 us  [shift(): lax.ppermute(value, axis, [(i, i ^ mask) for i in range(lax.axis_size(axi...]
    ppermute x1, waiting for transfers between devices: 0.66 us -> 3.04 us  [local(): key_next = lax.ppermute(key, 'seq', takes)]
    ppermute x1, starting transfers between devices: 3.49 us -> 1.32 us  [local(): value_next = lax.ppermute(value, 'seq', takes)]
    ppermute x1, waiting for transfers between devices: 7.69 us -> 5.62 us  [local(): value_next = lax.ppermute(value, 'seq', takes)]
where the time goes in v6:
time: 113 us; the launch traced here: 112 us
  waiting for transfers between devices  60.7 us (54%)
  starting transfers between devices  32.8 us (29%)
  Pallas kernels  16.1 us (14%)
  local copies, waits for them, and re-layouts  1.45 us (1%)
    ppermute x18, waiting for transfers between devices, shift(): lax.ppermute(value, axis, [(i, i ^ mask) for i in range(lax.axis_size(axi...  52 us
    ppermute x18, starting transfers between devices, shift(): lax.ppermute(value, axis, [(i, i ^ mask) for i in range(lax.axis_size(axi...  25.5 us
    ppermute x1, waiting for transfers between devices, local(): value_next = lax.ppermute(value, 'seq', takes)  5.62 us
    ppermute x1, starting transfers between devices, local(): key_next = lax.ppermute(key, 'seq', takes)  4.54 us
    pallas_call x1, Pallas kernels, local(): pl.pallas_call(functools.partial(update_kernel, plan, factor), out_shape=...  3.95 us
    pallas_call x1, Pallas kernels, local(): pl.pallas_call(backward_kernel, out_shape=[struct((tile, width), bf16), s...  3.9 us
    ppermute x1, waiting for transfers between devices, local(): key_next = lax.ppermute(key, 'seq', takes)  3.04 us
    pallas_call x1, Pallas kernels, local(): pl.pallas_call(functools.partial(forward_kernel, plan), out_shape=struct(...  2.29 us
  transfers between devices with their start and end apart: 21, of which 11 were waited for; matrix products, arithmetic and copies ran while one was open for 2% of the time, Pallas kernels for 12%

profile of v6, /device:TPU:1, one launch (start us, length us, event | category | flops | bytes accessed | tf_op | source)
XLA Modules:
  0.0 112.2 jit_solution(15867841620454317711)
XLA Ops:
  0.6 4.5 %collective-permute-start.2 = (bf16[128,2048]{1,0:T(8,128)(2,1)}, bf16[128,2048]{1,0:T(8,128)(2,1)S(1)}, u32[]{:S(2)}, u32[]{:S(2)}) collective-permute-start(bf16[128,2048]{1,0:T(8,128)(2,1)} %bitcast.25), channel_id=1, source_target_pairs={{1,2},{3,4},{4,3},{6,5},{9,10},{11,12},{12,11},{14,13},{17,18},{19... | collective-permute-start | bytes 1572872 | tf_op jit(solution)/shard_map/ppermute | solution.py:271
  5.2 1.3 %collective-permute-start.3 = (bf16[128,2048]{1,0:T(8,128)(2,1)}, bf16[128,2048]{1,0:T(8,128)(2,1)S(1)}, u32[]{:S(2)}, u32[]{:S(2)}) collective-permute-start(bf16[128,2048]{1,0:T(8,128)(2,1)} %bitcast.29), channel_id=1, source_target_pairs={{1,2},{3,4},{4,3},{6,5},{9,10},{11,12},{12,11},{14,13},{17,18},{19... | collective-permute-start | bytes 1572872 | tf_op jit(solution)/shard_map/ppermute | solution.py:272
  6.5 0.1 collective-permute-start
  6.6 0.5 collective-permute-start.1
  7.1 0.0 copy-start
  7.1 0.0 copy-start.1
  7.1 1.4 %dynamic-slice_bitcast_fusion.3 = (bf16[128,768]{1,0:T(8,128)(2,1)S(1)}, bf16[128,768]{1,0:T(8,128)(2,1)S(1)}, bf16[128,768]{1,0:T(8,128)(2,1)S(1)}, bf16[128,768]{1,0:T(8,128)(2,1)S(1)}) fusion(bf16[1,1,128,3072]{3,2,1,0:T(8,128)(2,1)} %param.10, s32[]{:T(128)S(6)} %select_n.12, s32[]{:T(128)S(6)} %select_n.13, s32[]{:T(128)S(6)} %select_n.15, s32[]{:T(128)S(6)} %select_n.14), kind=kLoop, calls=%fused_computation.8 | loop fusion | bytes 1572880 | tf_op jit(solution)/shard_map/dynamic_slice | solution.py:285
  8.5 3.0 %collective-permute-done.2.kn = bf16[128,2048]{1,0:T(8,128)(2,1)S(1)} collective-permute-done((bf16[128,2048]{1,0:T(8,128)(2,1)}, bf16[128,2048]{1,0:T(8,128)(2,1)S(1)}, u32[]{:S(2)}, u32[]{:S(2)}) %collective-permute-start.2) | collective-permute-done | bytes 524320 | tf_op jit(solution)/shard_map/ppermute | solution.py:271
  11.6 5.6 %collective-permute-done.3.vn = bf16[128,2048]{1,0:T(8,128)(2,1)S(1)} collective-permute-done((bf16[128,2048]{1,0:T(8,128)(2,1)}, bf16[128,2048]{1,0:T(8,128)(2,1)S(1)}, u32[]{:S(2)}, u32[]{:S(2)}) %collective-permute-start.3) | collective-permute-done | bytes 524320 | tf_op jit(solution)/shard_map/ppermute | solution.py:272
  17.2 2.7 %collective-permute-start.7 = (bf16[128,1536]{1,0:T(8,128)(2,1)S(1)}, bf16[128,1536]{1,0:T(8,128)(2,1)S(1)}, u32[]{:S(2)}, u32[]{:S(2)}) collective-permute-start(bf16[128,1536]{1,0:T(8,128)(2,1)S(1)} %pad_maximum_fusion.2), channel_id=1, source_target_pairs={{0,2},{1,3},{2,0},{3,1},{4,6},{5,7},{6,4},{7,5},{8,10},{9,11},{10,... | collective-permute-start | bytes 1179656 | tf_op jit(solution)/shard_map/ppermute | solution.py:83
  19.9 0.1 fusion
  20.0 0.1 collective-permute-start.8
  20.0 0.0 collective-permute-done.km
  20.0 0.0 collective-permute-done.1.vm
  20.1 0.0 copy-done
  20.1 0.0 copy-done.1
  20.1 0.0 copy-done.2
  20.1 0.0 copy-done.4
  20.1 0.0 copy-start.3
  20.1 2.3 %attention_forward.1 = bf16[2,2,512,128]{3,2,1,0:T(8,128)(2,1)S(1)} custom-call(s32[1,8]{1,0:T(1,128)S(1)} %copy-done.4, bf16[128,2048]{1,0:T(8,128)(2,1)S(1)} %bitcast.23, bf16[128,2048]{1,0:T(8,128)(2,1)S(1)} %bitcast.27, bf16[128,2048]{1,0:T(8,128)(2,1)S(1)} %bitcast.31, bf16[128,2048]{1,0:T(8,128)(2,1)S(1)} %collective-permute-done.km, ...), custom_call_target="tpu_custom_call" | custom-call | flops 268435456 | bytes 4194304 | tf_op jit(solution)/shard_map/attention_forward/pallas_call | solution.py:301
  22.4 7.1 %collective-permute-done.7 = bf16[128,1536]{1,0:T(8,128)(2,1)S(1)} collective-permute-done((bf16[128,1536]{1,0:T(8,128)(2,1)S(1)}, bf16[128,1536]{1,0:T(8,128)(2,1)S(1)}, u32[]{:S(2)}, u32[]{:S(2)}) %collective-permute-start.7) | collective-permute-done | bytes 393248 | tf_op jit(solution)/shard_map/ppermute | solution.py:83
  29.5 0.0 collective-permute-start.9
  29.6 1.5 %collective-permute-start.5 = (bf16[2,512,128]{2,1,0:T(8,128)(2,1)S(1)}, bf16[2,512,128]{2,1,0:T(8,128)(2,1)S(1)}, u32[]{:S(2)}, u32[]{:S(2)}) collective-permute-start(bf16[2,512,128]{2,1,0:T(8,128)(2,1)S(1)} %get-tuple-element.62), channel_id=1, source_target_pairs={{0,4},{1,5},{2,6},{3,7},{4,0},{5,1},{6,2},{7,3},{8,12},{9,13},{10,... | collective-permute-start | bytes 786440 | tf_op jit(solution)/shard_map/ppermute | solution.py:83
  31.1 1.3 %collective-permute-start.4 = (bf16[2,512,128]{2,1,0:T(8,128)(2,1)S(1)}, bf16[2,512,128]{2,1,0:T(8,128)(2,1)S(1)}, u32[]{:S(2)}, u32[]{:S(2)}) collective-permute-start(bf16[2,512,128]{2,1,0:T(8,128)(2,1)S(1)} %get-tuple-element.41.refs_0_), channel_id=1, source_target_pairs={{0,2},{1,3},{2,0},{3,1},{4,6},{5,7},{6,4},{7,5},{8,10},{9,11},{10,... | collective-permute-start | bytes 786440 | tf_op jit(solution)/shard_map/ppermute | solution.py:83
  32.4 0.0 copy-done.3
  32.4 3.9 %attention_backward.1 = (bf16[128,2048]{1,0:T(8,128)(2,1)}, f32[128,2048]{1,0:T(8,128)S(1)}, f32[128,2048]{1,0:T(8,128)S(1)}, bf16[2,128,2048]{2,1,0:T(8,128)(2,1)S(1)}) custom-call(s32[1,8]{1,0:T(1,128)S(1)} %copy-done.4, bf16[128,2048]{1,0:T(8,128)(2,1)S(1)} %bitcast.24, bf16[128,2048]{1,0:T(8,128)(2,1)S(1)} %bitcast.28, bf16[128,2048]{1,0:T(8,128)(2,1)S(1)} %bitcast.32, ...), custom_call_target="tpu_custom_call" | custom-call | flops 939524096 | bytes 7864320 | tf_op jit(solution)/shard_map/attention_backward/pallas_call | solution.py:324
  36.3 9.2 %collective-permute-done.5.refs_2_ = bf16[2,512,128]{2,1,0:T(8,128)(2,1)S(1)} collective-permute-done((bf16[2,512,128]{2,1,0:T(8,128)(2,1)S(1)}, bf16[2,512,128]{2,1,0:T(8,128)(2,1)S(1)}, u32[]{:S(2)}, u32[]{:S(2)}) %collective-permute-start.5) | collective-permute-done | bytes 262176 | tf_op jit(solution)/shard_map/ppermute | solution.py:83
  45.5 0.9 collective-permute-start.6
  46.4 0.0 collective-permute-done.8
  46.4 0.0 collective-permute-done.9
  46.4 0.2 pad_maximum_fusion.refs_4_
  46.6 0.0 collective-permute-done.4.refs_1_
  46.7 5.5 %collective-permute-done.6.refs_3_ = bf16[2,512,128]{2,1,0:T(8,128)(2,1)S(1)} collective-permute-done((bf16[2,512,128]{2,1,0:T(8,128)(2,1)S(1)}, bf16[2,512,128]{2,1,0:T(8,128)(2,1)S(1)}, u32[]{:S(2)}, u32[]{:S(2)}) %collective-permute-start.6) | collective-permute-done | bytes 262176 | tf_op jit(solution)/shard_map/ppermute | solution.py:83
  52.1 0.6 product_first.1
  52.7 1.4 %product_rest.1 = (f32[128,1536]{1,0:T(8,128)S(1)}, f32[128,1536]{1,0:T(8,128)S(1)}, f32[128,1536]{1,0:T(8,128)S(1)}, bf16[3,128,1536]{2,1,0:T(8,128)(2,1)S(1)}) custom-call(bf16[2,512,128]{2,1,0:T(8,128)(2,1)S(1)} %get-tuple-element.41.refs_0_, bf16[2,512,128]{2,1,0:T(8,128)(2,1)S(1)} %collective-permute-done.4.refs_1_, ...), custom_call_target="tpu_custom_call" | custom-call | flops 1207959552 | bytes 1572864 | tf_op jit(solution)/shard_map/product_rest/pallas_call | solution.py:341
  54.1 2.2 %collective-permute-start.10 = (bf16[3,128,1536]{2,1,0:T(8,128)(2,1)S(1)}, bf16[3,128,1536]{2,1,0:T(8,128)(2,1)S(1)}, u32[]{:S(2)}, u32[]{:S(2)}) collective-permute-start(bf16[3,128,1536]{2,1,0:T(8,128)(2,1)S(1)} %get-tuple-element.43), channel_id=1, source_target_pairs={{0,1},{1,0},{2,3},{3,2},{4,5},{5,4},{6,7},{7,6},{8,9},{9,8},{10,11... | collective-permute-start | bytes 3538952 | tf_op jit(solution)/shard_map/ppermute | solution.py:83
  56.3 0.1 collective-permute-start.13
  56.4 2.4 %collective-permute-done.10.refs_1_.refs_0_ = bf16[3,128,1536]{2,1,0:T(8,128)(2,1)S(1)} collective-permute-done((bf16[3,128,1536]{2,1,0:T(8,128)(2,1)S(1)}, bf16[3,128,1536]{2,1,0:T(8,128)(2,1)S(1)}, u32[]{:S(2)}, u32[]{:S(2)}) %collective-permute-start.10) | collective-permute-done | bytes 1179680 | tf_op jit(solution)/shard_map/ppermute | solution.py:83
  58.8 0.1 block_sum.3
  58.9 1.5 %collective-permute-start.12 = (bf16[2,128,2048]{2,1,0:T(8,128)(2,1)S(1)}, bf16[2,128,2048]{2,1,0:T(8,128)(2,1)S(1)}, u32[]{:S(2)}, u32[]{:S(2)}) collective-permute-start(bf16[2,128,2048]{2,1,0:T(8,128)(2,1)S(1)} %get-tuple-element.44), channel_id=1, source_target_pairs={{3,4},{5,6},{2,1},{4,3},{11,12},{13,14},{10,9},{12,11},{19,20},{21... | collective-permute-start | bytes 3145736 | tf_op jit(solution)/shard_map/ppermute | solution.py:432
  60.3 0.1 collective-permute-start.11
  60.4 0.0 collective-permute-done.13.refs_1_
  60.4 0.1 block_sum.4
  60.5 1.4 %collective-permute-start.14 = (bf16[128,1536]{1,0:T(8,128)(2,1)S(1)}, bf16[128,1536]{1,0:T(8,128)(2,1)S(1)}, u32[]{:S(2)}, u32[]{:S(2)}) collective-permute-start(bf16[128,1536]{1,0:T(8,128)(2,1)S(1)} %block_sum.4), channel_id=1, source_target_pairs={{0,8},{8,0},{16,24},{24,16},{1,9},{9,1},{17,25},{25,17},{2,10},{10... | collective-permute-start | bytes 1179656 | tf_op jit(solution)/shard_map/ppermute | solution.py:83
  61.9 8.9 %collective-permute-done.14.refs_2_ = bf16[128,1536]{1,0:T(8,128)(2,1)S(1)} collective-permute-done((bf16[128,1536]{1,0:T(8,128)(2,1)S(1)}, bf16[128,1536]{1,0:T(8,128)(2,1)S(1)}, u32[]{:S(2)}, u32[]{:S(2)}) %collective-permute-start.14) | collective-permute-done | bytes 393248 | tf_op jit(solution)/shard_map/ppermute | solution.py:83
  70.8 0.2 block_sum.5
  70.9 1.4 %collective-permute-start.15 = (bf16[128,1536]{1,0:T(8,128)(2,1)S(1)}, bf16[128,1536]{1,0:T(8,128)(2,1)S(1)}, u32[]{:S(2)}, u32[]{:S(2)}) collective-permute-start(bf16[128,1536]{1,0:T(8,128)(2,1)S(1)} %block_sum.3), channel_id=1, source_target_pairs={{0,8},{8,0},{16,24},{24,16},{1,9},{9,1},{17,25},{25,17},{2,10},{10... | collective-permute-start | bytes 1179656 | tf_op jit(solution)/shard_map/ppermute | solution.py:83
  72.3 2.3 %collective-permute-start.16 = (bf16[128,1536]{1,0:T(8,128)(2,1)S(1)}, bf16[128,1536]{1,0:T(8,128)(2,1)S(1)}, u32[]{:S(2)}, u32[]{:S(2)}) collective-permute-start(bf16[128,1536]{1,0:T(8,128)(2,1)S(1)} %block_sum.5), channel_id=1, source_target_pairs={{0,16},{8,24},{16,0},{24,8},{1,17},{9,25},{17,1},{25,9},{2,18},{10... | collective-permute-start | bytes 1179656 | tf_op jit(solution)/shard_map/ppermute | solution.py:83
  74.6 14.0 %collective-permute-done.15.refs_1_ = bf16[128,1536]{1,0:T(8,128)(2,1)S(1)} collective-permute-done((bf16[128,1536]{1,0:T(8,128)(2,1)S(1)}, bf16[128,1536]{1,0:T(8,128)(2,1)S(1)}, u32[]{:S(2)}, u32[]{:S(2)}) %collective-permute-start.15) | collective-permute-done | bytes 393248 | tf_op jit(solution)/shard_map/ppermute | solution.py:83
  88.6 0.0 collective-permute-done.16.refs_2_
  88.6 0.9 gradient_sum.1
  89.5 3.7 %collective-permute-start.17 = (f32[128,128]{1,0:T(8,128)S(1)}, f32[128,128]{1,0:T(8,128)S(1)}, u32[]{:S(2)}, u32[]{:S(2)}) collective-permute-start(f32[128,128]{1,0:T(8,128)S(1)} %get-tuple-element.52.gram), channel_id=1, source_target_pairs={{0,2},{1,3},{2,0},{3,1},{4,6},{5,7},{6,4},{7,5},{8,10},{9,11},{10,... | collective-permute-start | bytes 196616 | tf_op jit(solution)/shard_map/ppermute | solution.py:83
  93.1 1.7 %collective-permute-done.17.gram_other = f32[128,128]{1,0:T(8,128)S(1)} collective-permute-done((f32[128,128]{1,0:T(8,128)S(1)}, f32[128,128]{1,0:T(8,128)S(1)}, u32[]{:S(2)}, u32[]{:S(2)}) %collective-permute-start.17) | collective-permute-done | bytes 65568 | tf_op jit(solution)/shard_map/ppermute | solution.py:83
  94.8 4.0 %newton_schulz.1 = (f32[128,384]{1,0:T(8,128)S(1)}, bf16[128,384]{1,0:T(8,128)(2,1)S(1)}, bf16[128,384]{1,0:T(8,128)(2,1)S(1)}, bf16[128,384]{1,0:T(8,128)(2,1)S(1)}) custom-call(f32[128,1536]{1,0:T(8,128)S(1)} %get-tuple-element.51.x, f32[128,128]{1,0:T(8,128)S(1)} %get-tuple-element.52.gram, f32[128,128]{1,0:T(8,128)S(1)} %collective-permute-done.17.gram_other), custom_call_target="tpu_custom_call" | custom-call | flops 301989888 | bytes 1572864 | tf_op jit(solution)/shard_map/newton_schulz/pallas_call | solution.py:410
  98.7 5.0 %collective-permute-start.18 = (bf16[128,384]{1,0:T(8,128)(2,1)S(1)}, bf16[128,384]{1,0:T(8,128)(2,1)S(1)}, u32[]{:S(2)}, u32[]{:S(2)}) collective-permute-start(bf16[128,384]{1,0:T(8,128)(2,1)S(1)} %get-tuple-element.55), channel_id=1, source_target_pairs={{0,1},{1,0},{2,3},{3,2},{4,5},{5,4},{6,7},{7,6},{8,9},{9,8},{10,11... | collective-permute-start | bytes 294920 | tf_op jit(solution)/shard_map/ppermute | solution.py:83
  103.7 2.4 %collective-permute-start.19 = (bf16[128,384]{1,0:T(8,128)(2,1)S(1)}, bf16[128,384]{1,0:T(8,128)(2,1)S(1)}, u32[]{:S(2)}, u32[]{:S(2)}) collective-permute-start(bf16[128,384]{1,0:T(8,128)(2,1)S(1)} %get-tuple-element.56), channel_id=1, source_target_pairs={{0,4},{1,5},{2,6},{3,7},{4,0},{5,1},{6,2},{7,3},{8,12},{9,13},{10,... | collective-permute-start | bytes 294920 | tf_op jit(solution)/shard_map/ppermute | solution.py:83
  106.1 0.0 collective-permute-start.20
  106.1 0.0 collective-permute-done.12.beyond
  106.1 0.0 collective-permute-done.11.mate
  106.2 1.8 %key_value_sum.1 = (bf16[128,2048]{1,0:T(8,128)(2,1)}, bf16[128,2048]{1,0:T(8,128)(2,1)}) custom-call(s32[1,8]{1,0:T(1,128)S(1)} %copy-done.4, f32[128,2048]{1,0:T(8,128)S(1)} %get-tuple-element.33.dko, f32[128,2048]{1,0:T(8,128)S(1)} %get-tuple-element.34.dvo, bf16[2,128,2048]{2,1,0:T(8,128)(2,1)S(1)} %collective-permute-done.11.mate, ...), custom_call_target="tpu_custom_call" | custom-call | flops 1572864 | bytes 5242880 | tf_op jit(solution)/shard_map/key_value_sum/pallas_call | solution.py:419
  108.0 0.0 collective-permute-done.18.refs_1_
  108.0 1.2 %collective-permute-done.19.refs_2_ = bf16[128,384]{1,0:T(8,128)(2,1)S(1)} collective-permute-done((bf16[128,384]{1,0:T(8,128)(2,1)S(1)}, bf16[128,384]{1,0:T(8,128)(2,1)S(1)}, u32[]{:S(2)}, u32[]{:S(2)}) %collective-permute-start.19) | collective-permute-done | bytes 98336 | tf_op jit(solution)/shard_map/ppermute | solution.py:83
  109.2 2.1 %collective-permute-done.20.refs_3_ = bf16[128,384]{1,0:T(8,128)(2,1)S(1)} collective-permute-done((bf16[128,384]{1,0:T(8,128)(2,1)S(1)}, bf16[128,384]{1,0:T(8,128)(2,1)S(1)}, u32[]{:S(2)}, u32[]{:S(2)}) %collective-permute-start.20) | collective-permute-done | bytes 98336 | tf_op jit(solution)/shard_map/ppermute | solution.py:83
  111.3 0.9 update_rows.1
  (4 shorter events, 0.1 us)
Async XLA Ops:
  0.6 10.9 %collective-permute-start.2 = (bf16[128,2048]{1,0:T(8,128)(2,1)}, bf16[128,2048]{1,0:T(8,128)(2,1)S(1)}, u32[]{:S(2)}, u32[]{:S(2)}) collective-permute-start(bf16[128,2048]{1,0:T(8,128)(2,1)} %bitcast.25), channel_id=1, source_target_pairs={{1,2},{3,4},{4,3},{6,5},{9,10},{11,12},{12,11},{14,13},{17,18},{19... | collective-permute-start | bytes 1572872 | tf_op jit(solution)/shard_map/ppermute | solution.py:271
  5.2 12.0 %collective-permute-start.3 = (bf16[128,2048]{1,0:T(8,128)(2,1)}, bf16[128,2048]{1,0:T(8,128)(2,1)S(1)}, u32[]{:S(2)}, u32[]{:S(2)}) collective-permute-start(bf16[128,2048]{1,0:T(8,128)(2,1)} %bitcast.29), channel_id=1, source_target_pairs={{1,2},{3,4},{4,3},{6,5},{9,10},{11,12},{12,11},{14,13},{17,18},{19... | collective-permute-start | bytes 1572872 | tf_op jit(solution)/shard_map/ppermute | solution.py:272
  6.5 13.5 %collective-permute-start = (bf16[128,2048]{1,0:T(8,128)(2,1)}, bf16[128,2048]{1,0:T(8,128)(2,1)S(1)}, u32[]{:S(2)}, u32[]{:S(2)}) collective-permute-start(bf16[128,2048]{1,0:T(8,128)(2,1)} %bitcast.26), channel_id=1, source_target_pairs={{0,1},{1,0},{2,3},{3,2},{4,5},{5,4},{6,7},{7,6},{8,9},{9,8},{10,11... | collective-permute-start | bytes 1572872 | tf_op jit(solution)/shard_map/ppermute | solution.py:83
  6.6 13.5 %collective-permute-start.1 = (bf16[128,2048]{1,0:T(8,128)(2,1)}, bf16[128,2048]{1,0:T(8,128)(2,1)S(1)}, u32[]{:S(2)}, u32[]{:S(2)}) collective-permute-start(bf16[128,2048]{1,0:T(8,128)(2,1)} %bitcast.30), channel_id=1, source_target_pairs={{0,1},{1,0},{2,3},{3,2},{4,5},{5,4},{6,7},{7,6},{8,9},{9,8},{10,11... | collective-permute-start | bytes 1572872 | tf_op jit(solution)/shard_map/ppermute | solution.py:83
  7.1 13.0 %copy-start = (bf16[1,1,128,2048]{3,2,1,0:T(8,128)(2,1)S(1)}, bf16[1,1,128,2048]{3,2,1,0:T(8,128)(2,1)}, u32[]{:S(2)}) copy-start(bf16[1,1,128,2048]{3,2,1,0:T(8,128)(2,1)} %param.6) | copy-start | bytes 1572868
  7.1 13.0 %copy-start.1 = (bf16[1,1,128,2048]{3,2,1,0:T(8,128)(2,1)S(1)}, bf16[1,1,128,2048]{3,2,1,0:T(8,128)(2,1)}, u32[]{:S(2)}) copy-start(bf16[1,1,128,2048]{3,2,1,0:T(8,128)(2,1)} %param.7) | copy-start | bytes 1572868
  7.1 13.0 %copy-start.2 = (bf16[1,1,128,2048]{3,2,1,0:T(8,128)(2,1)S(1)}, bf16[1,1,128,2048]{3,2,1,0:T(8,128)(2,1)}, u32[]{:S(2)}) copy-start(bf16[1,1,128,2048]{3,2,1,0:T(8,128)(2,1)} %param.8) | copy-start | bytes 1572868
  7.1 13.0 %copy-start.4 = (s32[1,8]{1,0:T(1,128)S(1)}, s32[1,8]{1,0:T(1,128)}, u32[]{:S(2)}) copy-start(s32[1,8]{1,0:T(1,128)} %near_ref.5) | copy-start | bytes 100
  17.2 12.3 %collective-permute-start.7 = (bf16[128,1536]{1,0:T(8,128)(2,1)S(1)}, bf16[128,1536]{1,0:T(8,128)(2,1)S(1)}, u32[]{:S(2)}, u32[]{:S(2)}) collective-permute-start(bf16[128,1536]{1,0:T(8,128)(2,1)S(1)} %pad_maximum_fusion.2), channel_id=1, source_target_pairs={{0,2},{1,3},{2,0},{3,1},{4,6},{5,7},{6,4},{7,5},{8,10},{9,11},{10,... | collective-permute-start | bytes 1179656 | tf_op jit(solution)/shard_map/ppermute | solution.py:83
  20.0 26.5 %collective-permute-start.8 = (bf16[128,1536]{1,0:T(8,128)(2,1)S(1)}, bf16[128,1536]{1,0:T(8,128)(2,1)S(1)}, u32[]{:S(2)}, u32[]{:S(2)}) collective-permute-start(bf16[128,1536]{1,0:T(8,128)(2,1)S(1)} %get-tuple-element.38), channel_id=1, source_target_pairs={{0,4},{1,5},{2,6},{3,7},{4,0},{5,1},{6,2},{7,3},{8,12},{9,13},{10,... | collective-permute-start | bytes 1179656 | tf_op jit(solution)/shard_map/ppermute | solution.py:83
  20.1 12.3 %copy-start.3 = (bf16[1,1,128,2048]{3,2,1,0:T(8,128)(2,1)S(1)}, bf16[1,1,128,2048]{3,2,1,0:T(8,128)(2,1)}, u32[]{:S(2)}) copy-start(bf16[1,1,128,2048]{3,2,1,0:T(8,128)(2,1)} %param.9) | copy-start | bytes 1572868
  29.5 16.9 %collective-permute-start.9 = (bf16[1,128,1536]{2,1,0:T(8,128)(2,1)S(1)}, bf16[1,128,1536]{2,1,0:T(8,128)(2,1)S(1)}, u32[]{:S(2)}, u32[]{:S(2)}) collective-permute-start(bf16[1,128,1536]{2,1,0:T(8,128)(2,1)S(1)} %bitcast.34), channel_id=1, source_target_pairs={{0,4},{1,5},{2,6},{3,7},{4,0},{5,1},{6,2},{7,3},{8,12},{9,13},{10,... | collective-permute-start | bytes 1179656 | tf_op jit(solution)/shard_map/ppermute | solution.py:83
  29.6 15.9 %collective-permute-start.5 = (bf16[2,512,128]{2,1,0:T(8,128)(2,1)S(1)}, bf16[2,512,128]{2,1,0:T(8,128)(2,1)S(1)}, u32[]{:S(2)}, u32[]{:S(2)}) collective-permute-start(bf16[2,512,128]{2,1,0:T(8,128)(2,1)S(1)} %get-tuple-element.62), channel_id=1, source_target_pairs={{0,4},{1,5},{2,6},{3,7},{4,0},{5,1},{6,2},{7,3},{8,12},{9,13},{10,... | collective-permute-start | bytes 786440 | tf_op jit(solution)/shard_map/ppermute | solution.py:83
  31.1 15.6 %collective-permute-start.4 = (bf16[2,512,128]{2,1,0:T(8,128)(2,1)S(1)}, bf16[2,512,128]{2,1,0:T(8,128)(2,1)S(1)}, u32[]{:S(2)}, u32[]{:S(2)}) collective-permute-start(bf16[2,512,128]{2,1,0:T(8,128)(2,1)S(1)} %get-tuple-element.41.refs_0_), channel_id=1, source_target_pairs={{0,2},{1,3},{2,0},{3,1},{4,6},{5,7},{6,4},{7,5},{8,10},{9,11},{10,... | collective-permute-start | bytes 786440 | tf_op jit(solution)/shard_map/ppermute | solution.py:83
  45.5 6.6 %collective-permute-start.6 = (bf16[2,512,128]{2,1,0:T(8,128)(2,1)S(1)}, bf16[2,512,128]{2,1,0:T(8,128)(2,1)S(1)}, u32[]{:S(2)}, u32[]{:S(2)}) collective-permute-start(bf16[2,512,128]{2,1,0:T(8,128)(2,1)S(1)} %collective-permute-done.5.refs_2_), channel_id=1, source_target_pairs={{0,2},{1,3},{2,0},{3,1},{4,6},{5,7},{6,4},{7,5},{8,10},{9,11},{10,... | collective-permute-start | bytes 786440 | tf_op jit(solution)/shard_map/ppermute | solution.py:83
  54.1 4.6 %collective-permute-start.10 = (bf16[3,128,1536]{2,1,0:T(8,128)(2,1)S(1)}, bf16[3,128,1536]{2,1,0:T(8,128)(2,1)S(1)}, u32[]{:S(2)}, u32[]{:S(2)}) collective-permute-start(bf16[3,128,1536]{2,1,0:T(8,128)(2,1)S(1)} %get-tuple-element.43), channel_id=1, source_target_pairs={{0,1},{1,0},{2,3},{3,2},{4,5},{5,4},{6,7},{7,6},{8,9},{9,8},{10,11... | collective-permute-start | bytes 3538952 | tf_op jit(solution)/shard_map/ppermute | solution.py:83
  56.3 4.1 %collective-permute-start.13 = (bf16[1,128,1536]{2,1,0:T(8,128)(2,1)S(1)}, bf16[1,128,1536]{2,1,0:T(8,128)(2,1)S(1)}, u32[]{:S(2)}, u32[]{:S(2)}) collective-permute-start(bf16[1,128,1536]{2,1,0:T(8,128)(2,1)S(1)} %get-tuple-element.49), channel_id=1, source_target_pairs={{0,1},{1,0},{2,3},{3,2},{4,5},{5,4},{6,7},{7,6},{8,9},{9,8},{10,11... | collective-permute-start | bytes 1179656 | tf_op jit(solution)/shard_map/ppermute | solution.py:83
  58.9 47.3 %collective-permute-start.12 = (bf16[2,128,2048]{2,1,0:T(8,128)(2,1)S(1)}, bf16[2,128,2048]{2,1,0:T(8,128)(2,1)S(1)}, u32[]{:S(2)}, u32[]{:S(2)}) collective-permute-start(bf16[2,128,2048]{2,1,0:T(8,128)(2,1)S(1)} %get-tuple-element.44), channel_id=1, source_target_pairs={{3,4},{5,6},{2,1},{4,3},{11,12},{13,14},{10,9},{12,11},{19,20},{21... | collective-permute-start | bytes 3145736 | tf_op jit(solution)/shard_map/ppermute | solution.py:432
  60.3 45.8 %collective-permute-start.11 = (bf16[2,128,2048]{2,1,0:T(8,128)(2,1)S(1)}, bf16[2,128,2048]{2,1,0:T(8,128)(2,1)S(1)}, u32[]{:S(2)}, u32[]{:S(2)}) collective-permute-start(bf16[2,128,2048]{2,1,0:T(8,128)(2,1)S(1)} %get-tuple-element.44), channel_id=1, source_target_pairs={{0,1},{1,0},{2,3},{3,2},{4,5},{5,4},{6,7},{7,6},{8,9},{9,8},{10,11... | collective-permute-start | bytes 3145736 | tf_op jit(solution)/shard_map/ppermute | solution.py:83
  60.5 10.3 %collective-permute-start.14 = (bf16[128,1536]{1,0:T(8,128)(2,1)S(1)}, bf16[128,1536]{1,0:T(8,128)(2,1)S(1)}, u32[]{:S(2)}, u32[]{:S(2)}) collective-permute-start(bf16[128,1536]{1,0:T(8,128)(2,1)S(1)} %block_sum.4), channel_id=1, source_target_pairs={{0,8},{8,0},{16,24},{24,16},{1,9},{9,1},{17,25},{25,17},{2,10},{10... | collective-permute-start | bytes 1179656 | tf_op jit(solution)/shard_map/ppermute | solution.py:83
  70.9 17.7 %collective-permute-start.15 = (bf16[128,1536]{1,0:T(8,128)(2,1)S(1)}, bf16[128,1536]{1,0:T(8,128)(2,1)S(1)}, u32[]{:S(2)}, u32[]{:S(2)}) collective-permute-start(bf16[128,1536]{1,0:T(8,128)(2,1)S(1)} %block_sum.3), channel_id=1, source_target_pairs={{0,8},{8,0},{16,24},{24,16},{1,9},{9,1},{17,25},{25,17},{2,10},{10... | collective-permute-start | bytes 1179656 | tf_op jit(solution)/shard_map/ppermute | solution.py:83
  72.3 16.3 %collective-permute-start.16 = (bf16[128,1536]{1,0:T(8,128)(2,1)S(1)}, bf16[128,1536]{1,0:T(8,128)(2,1)S(1)}, u32[]{:S(2)}, u32[]{:S(2)}) collective-permute-start(bf16[128,1536]{1,0:T(8,128)(2,1)S(1)} %block_sum.5), channel_id=1, source_target_pairs={{0,16},{8,24},{16,0},{24,8},{1,17},{9,25},{17,1},{25,9},{2,18},{10... | collective-permute-start | bytes 1179656 | tf_op jit(solution)/shard_map/ppermute | solution.py:83
  89.5 5.3 %collective-permute-start.17 = (f32[128,128]{1,0:T(8,128)S(1)}, f32[128,128]{1,0:T(8,128)S(1)}, u32[]{:S(2)}, u32[]{:S(2)}) collective-permute-start(f32[128,128]{1,0:T(8,128)S(1)} %get-tuple-element.52.gram), channel_id=1, source_target_pairs={{0,2},{1,3},{2,0},{3,1},{4,6},{5,7},{6,4},{7,5},{8,10},{9,11},{10,... | collective-permute-start | bytes 196616 | tf_op jit(solution)/shard_map/ppermute | solution.py:83
  98.7 9.3 %collective-permute-start.18 = (bf16[128,384]{1,0:T(8,128)(2,1)S(1)}, bf16[128,384]{1,0:T(8,128)(2,1)S(1)}, u32[]{:S(2)}, u32[]{:S(2)}) collective-permute-start(bf16[128,384]{1,0:T(8,128)(2,1)S(1)} %get-tuple-element.55), channel_id=1, source_target_pairs={{0,1},{1,0},{2,3},{3,2},{4,5},{5,4},{6,7},{7,6},{8,9},{9,8},{10,11... | collective-permute-start | bytes 294920 | tf_op jit(solution)/shard_map/ppermute | solution.py:83
  103.7 5.5 %collective-permute-start.19 = (bf16[128,384]{1,0:T(8,128)(2,1)S(1)}, bf16[128,384]{1,0:T(8,128)(2,1)S(1)}, u32[]{:S(2)}, u32[]{:S(2)}) collective-permute-start(bf16[128,384]{1,0:T(8,128)(2,1)S(1)} %get-tuple-element.56), channel_id=1, source_target_pairs={{0,4},{1,5},{2,6},{3,7},{4,0},{5,1},{6,2},{7,3},{8,12},{9,13},{10,... | collective-permute-start | bytes 294920 | tf_op jit(solution)/shard_map/ppermute | solution.py:83
  106.1 5.2 %collective-permute-start.20 = (bf16[128,384]{1,0:T(8,128)(2,1)S(1)}, bf16[128,384]{1,0:T(8,128)(2,1)S(1)}, u32[]{:S(2)}, u32[]{:S(2)}) collective-permute-start(bf16[128,384]{1,0:T(8,128)(2,1)S(1)} %get-tuple-element.57), channel_id=1, source_target_pairs={{0,5},{1,4},{2,7},{3,6},{4,1},{5,0},{6,3},{7,2},{8,13},{9,12},{10,... | collective-permute-start | bytes 294920 | tf_op jit(solution)/shard_map/ppermute | solution.py:83

commit v7 on v6

--- a/solution.py
+++ b/solution.py
@@ -313,29 +313,17 @@
     for high in range(1, plan.high):
         came_high = shift(attended[high], "seq", high << (1 + plan.col_bits))
         pairs.append(came_high)
-        pairs += [shift(came_high, "seq", q << 1) for q in range(1, plan.col)]
+        there = after(came_high, *pairs[1 : plan.col])
+        pairs += [shift(there, "seq", q << 1) for q in range(1, plan.col)]
+
     through = after(jnp.stack(columns[1:]), attended)
     held = [jnp.stack(columns)]
     for high in range(1, plan.high):
-        rest = shift(through, "seq", high << (1 + plan.col_bits))
+        rest = jnp.concatenate(
+            [shift(part, "seq", high << (1 + plan.col_bits)) for part in jnp.split(through, 2, 2)], 2
+        )
         held.append(jnp.concatenate([high_columns[high - 1][None], rest], 0))
     held = jnp.concatenate(held, 0)
-
-    dq, dko, dvo, dfar = pl.pallas_call(
-        backward_kernel,
-        out_shape=[
-            struct((tile, width), bf16),
-            struct((tile, width), f32),
-            struct((tile, width), f32),
-            struct((2, tile, width), bf16),
-        ],
-        in_specs=[smem()] + whole(8),
-        out_specs=whole(4),
-        scratch_shapes=[pltpu.VMEM((2, tile, width), bf16)],
-        compiler_params=params(),
-        cost_estimate=cost(28 * tile * tile * width, 30 * tile * width, 2 * tile * tile * head_count),
-        name="attention_backward",
-    )(neighbour, query, key, value, *beside, after(grad, attended))
 
     def product(name, layers, *operands):
         *blocks, for_mate = pl.pallas_call(
@@ -366,7 +354,7 @@
         )(*[array for array, *_ in parts])
 
     leading = [i for i in range(m - 1, 1, -1) if i & 1]
-    blocks = product("product_first", leading, after(pairs[0], dq), *pairs[1:], held)
+    blocks = product("product_first", leading, *pairs, held)
     first_block = blocks[leading[0]][0][0]
     blocks |= product(
         "product_rest",
@@ -385,11 +373,25 @@
                 sent.append(added(blocks[i] + extra[i], 0, mine_width))
                 extra[i ^ bit].append((shift(sent[-1], "dp", bit), None, 0))
         bit *= 2
-    near = added(blocks[1], 0, mine_width)
-    dfar = after(dfar, near)
-    near = shift(after(near, sent[-1]), "dp", 1)
+    near = shift(after(added(blocks[1], 0, mine_width), sent[-1]), "dp", 1)
     own = blocks[0][0][0]
     came = [blocks[0][1], (near, None, 0)] + extra[0]
+
+    dq, dko, dvo, dfar = pl.pallas_call(
+        backward_kernel,
+        out_shape=[
+            struct((tile, width), bf16),
+            struct((tile, width), f32),
+            struct((tile, width), f32),
+            struct((2, tile, width), bf16),
+        ],
+        in_specs=[smem()] + whole(8),
+        out_specs=whole(4),
+        scratch_shapes=[pltpu.VMEM((2, tile, width), bf16)],
+        compiler_params=params(),
+        cost_estimate=cost(28 * tile * tile * width, 30 * tile * width, 2 * tile * tile * head_count),
+        name="attention_backward",
+    )(neighbour, query, key, value, *beside, after(grad, *pairs[plan.col :: plan.col]))
 
     x, gram = pl.pallas_call(
         functools.partial(gram_kernel, [spot for _, *spot in came]),
@@ -416,6 +418,7 @@
         cost_estimate=cost(12 * HEAD_DIM * HEAD_DIM * mine_width, 8 * HEAD_DIM * mine_width),
         name="newton_schulz",
     )(x, gram, gram_other)
+    dfar = after(dfar, sent[-1])
     dk, dv = pl.pallas_call(
         combine_kernel,
         out_shape=[struct((tile, width), bf16)] * 2,

time: 113 us -> 106 us (0.938)
  starting transfers between devices: 32.8 us -> 27.5 us
    ppermute x18 -> x19, starting transfers between devices: 25.5 us -> 20.1 us  [shift(): lax.ppermute(value, axis, [(i, i ^ mask) for i in range(lax.axis_size(axi...]
    ppermute x18 -> x19, waiting for transfers between devices: 52 us -> 51.1 us  [shift(): lax.ppermute(value, axis, [(i, i ^ mask) for i in range(lax.axis_size(axi...]
  transfers between devices with their start and end apart: 21 -> 22, of which waited for: 11 -> 13; matrix products, arithmetic and copies ran while one was open for 2% -> 2% of each run, Pallas kernels for 12% -> 12%
where the time goes in v7:
time: 106 us
  waiting for transfers between devices  59.8 us (56%)
  starting transfers between devices  27.5 us (26%)
  Pallas kernels  16 us (15%)
  local copies, waits for them, and re-layouts  1.47 us (1%)
    ppermute x19, waiting for transfers between devices, shift(): lax.ppermute(value, axis, [(i, i ^ mask) for i in range(lax.axis_size(axi...  51.1 us
    ppermute x19, starting transfers between devices, shift(): lax.ppermute(value, axis, [(i, i ^ mask) for i in range(lax.axis_size(axi...  20.1 us
    ppermute x1, waiting for transfers between devices, local(): value_next = lax.ppermute(value, 'seq', takes)  5.62 us
    ppermute x1, starting transfers between devices, local(): key_next = lax.ppermute(key, 'seq', takes)  4.54 us
    pallas_call x1, Pallas kernels, local(): pl.pallas_call(functools.partial(update_kernel, plan, factor), out_shape=...  3.95 us
    pallas_call x1, Pallas kernels, local(): pl.pallas_call(backward_kernel, out_shape=[struct((tile, width), bf16), s...  3.9 us
    ppermute x1, waiting for transfers between devices, local(): key_next = lax.ppermute(key, 'seq', takes)  3.04 us
    pallas_call x1, Pallas kernels, local(): pl.pallas_call(functools.partial(forward_kernel, plan), out_shape=struct(...  2.29 us
  transfers between devices with their start and end apart: 22, of which 13 were waited for; matrix products, arithmetic and copies ran while one was open for 2% of the time, Pallas kernels for 12%

profile of v7, /device:TPU:1, one launch (start us, length us, event | category | flops | bytes accessed | tf_op | source)
XLA Modules:
  0.0 105.8 jit_solution(2796622509095991056)
XLA Ops:
  0.6 4.5 %collective-permute-start.2 = (bf16[128,2048]{1,0:T(8,128)(2,1)}, bf16[128,2048]{1,0:T(8,128)(2,1)S(1)}, u32[]{:S(2)}, u32[]{:S(2)}) collective-permute-start(bf16[128,2048]{1,0:T(8,128)(2,1)} %bitcast.25), channel_id=1, source_target_pairs={{1,2},{3,4},{4,3},{6,5},{9,10},{11,12},{12,11},{14,13},{17,18},{19... | collective-permute-start | bytes 1572872 | tf_op jit(solution)/shard_map/ppermute | solution.py:271
  5.2 1.3 %collective-permute-start.3 = (bf16[128,2048]{1,0:T(8,128)(2,1)}, bf16[128,2048]{1,0:T(8,128)(2,1)S(1)}, u32[]{:S(2)}, u32[]{:S(2)}) collective-permute-start(bf16[128,2048]{1,0:T(8,128)(2,1)} %bitcast.29), channel_id=1, source_target_pairs={{1,2},{3,4},{4,3},{6,5},{9,10},{11,12},{12,11},{14,13},{17,18},{19... | collective-permute-start | bytes 1572872 | tf_op jit(solution)/shard_map/ppermute | solution.py:272
  6.5 0.1 collective-permute-start
  6.6 0.5 collective-permute-start.1
  7.1 1.4 %dynamic-slice_bitcast_fusion.3 = (bf16[128,768]{1,0:T(8,128)(2,1)S(1)}, bf16[128,768]{1,0:T(8,128)(2,1)S(1)}, bf16[128,768]{1,0:T(8,128)(2,1)S(1)}, bf16[128,768]{1,0:T(8,128)(2,1)S(1)}) fusion(bf16[1,1,128,3072]{3,2,1,0:T(8,128)(2,1)} %param.10, s32[]{:T(128)S(6)} %select_n.12, s32[]{:T(128)S(6)} %select_n.13, s32[]{:T(128)S(6)} %select_n.15, s32[]{:T(128)S(6)} %select_n.14), kind=kLoop, calls=%fused_computation.8 | loop fusion | bytes 1572880 | tf_op jit(solution)/shard_map/dynamic_slice | solution.py:285
  8.5 3.0 %collective-permute-done.2.kn = bf16[128,2048]{1,0:T(8,128)(2,1)S(1)} collective-permute-done((bf16[128,2048]{1,0:T(8,128)(2,1)}, bf16[128,2048]{1,0:T(8,128)(2,1)S(1)}, u32[]{:S(2)}, u32[]{:S(2)}) %collective-permute-start.2) | collective-permute-done | bytes 524320 | tf_op jit(solution)/shard_map/ppermute | solution.py:271
  11.6 5.6 %collective-permute-done.3.vn = bf16[128,2048]{1,0:T(8,128)(2,1)S(1)} collective-permute-done((bf16[128,2048]{1,0:T(8,128)(2,1)}, bf16[128,2048]{1,0:T(8,128)(2,1)S(1)}, u32[]{:S(2)}, u32[]{:S(2)}) %collective-permute-start.3) | collective-permute-done | bytes 524320 | tf_op jit(solution)/shard_map/ppermute | solution.py:272
  17.2 2.7 %collective-permute-start.7 = (bf16[128,1536]{1,0:T(8,128)(2,1)S(1)}, bf16[128,1536]{1,0:T(8,128)(2,1)S(1)}, u32[]{:S(2)}, u32[]{:S(2)}) collective-permute-start(bf16[128,1536]{1,0:T(8,128)(2,1)S(1)} %pad_maximum_fusion.1), channel_id=1, source_target_pairs={{0,2},{1,3},{2,0},{3,1},{4,6},{5,7},{6,4},{7,5},{8,10},{9,11},{10,... | collective-permute-start | bytes 1179656 | tf_op jit(solution)/shard_map/ppermute | solution.py:83
  19.9 0.1 fusion
  20.0 0.0 collective-permute-done.km
  20.0 0.0 collective-permute-done.1.vm
  20.0 0.0 copy-done
  20.0 0.0 copy-done.1
  20.0 0.0 copy-done.2
  20.0 0.0 copy-done.4
  20.0 2.3 %attention_forward.1 = bf16[2,2,512,128]{3,2,1,0:T(8,128)(2,1)S(1)} custom-call(s32[1,8]{1,0:T(1,128)S(1)} %copy-done.4, bf16[128,2048]{1,0:T(8,128)(2,1)S(1)} %bitcast.23, bf16[128,2048]{1,0:T(8,128)(2,1)S(1)} %bitcast.27, bf16[128,2048]{1,0:T(8,128)(2,1)S(1)} %bitcast.31, bf16[128,2048]{1,0:T(8,128)(2,1)S(1)} %collective-permute-done.km, ...), custom_call_target="tpu_custom_call" | custom-call | flops 268435456 | bytes 4194304 | tf_op jit(solution)/shard_map/attention_forward/pallas_call | solution.py:301
  22.4 0.1 collective-permute-start.4
  22.4 0.9 collective-permute-start.5
  23.3 0.6 collective-permute-start.8
  23.9 5.7 %collective-permute-done.7 = bf16[128,1536]{1,0:T(8,128)(2,1)S(1)} collective-permute-done((bf16[128,1536]{1,0:T(8,128)(2,1)S(1)}, bf16[128,1536]{1,0:T(8,128)(2,1)S(1)}, u32[]{:S(2)}, u32[]{:S(2)}) %collective-permute-start.7) | collective-permute-done | bytes 393248 | tf_op jit(solution)/shard_map/ppermute | solution.py:83
  29.6 0.1 collective-permute-start.9
  29.7 1.5 %collective-permute-start.10 = (bf16[1,128,768]{2,1,0:T(8,128)(2,1)S(1)}, bf16[1,128,768]{2,1,0:T(8,128)(2,1)S(1)}, u32[]{:S(2)}, u32[]{:S(2)}) collective-permute-start(bf16[1,128,768]{2,1,0:T(8,128)(2,1)S(1)} %get-tuple-element.67), channel_id=1, source_target_pairs={{0,4},{1,5},{2,6},{3,7},{4,0},{5,1},{6,2},{7,3},{8,12},{9,13},{10,... | collective-permute-start | bytes 589832 | tf_op jit(solution)/shard_map/ppermute | solution.py:83
  31.1 0.0 collective-permute-done.4.refs_2_
  31.1 4.0 %collective-permute-done.5.refs_1_ = bf16[2,512,128]{2,1,0:T(8,128)(2,1)S(1)} collective-permute-done((bf16[2,512,128]{2,1,0:T(8,128)(2,1)S(1)}, bf16[2,512,128]{2,1,0:T(8,128)(2,1)S(1)}, u32[]{:S(2)}, u32[]{:S(2)}) %collective-permute-start.5) | collective-permute-done | bytes 262176 | tf_op jit(solution)/shard_map/ppermute | solution.py:83
  35.1 1.3 %collective-permute-start.6 = (bf16[2,512,128]{2,1,0:T(8,128)(2,1)S(1)}, bf16[2,512,128]{2,1,0:T(8,128)(2,1)S(1)}, u32[]{:S(2)}, u32[]{:S(2)}) collective-permute-start(bf16[2,512,128]{2,1,0:T(8,128)(2,1)S(1)} %collective-permute-done.4.refs_2_), channel_id=1, source_target_pairs={{0,2},{1,3},{2,0},{3,1},{4,6},{5,7},{6,4},{7,5},{8,10},{9,11},{10,... | collective-permute-start | bytes 786440 | tf_op jit(solution)/shard_map/ppermute | solution.py:83
  36.4 2.3 %collective-permute-done.8 = bf16[128,1536]{1,0:T(8,128)(2,1)S(1)} collective-permute-done((bf16[128,1536]{1,0:T(8,128)(2,1)S(1)}, bf16[128,1536]{1,0:T(8,128)(2,1)S(1)}, u32[]{:S(2)}, u32[]{:S(2)}) %collective-permute-start.8) | collective-permute-done | bytes 393248 | tf_op jit(solution)/shard_map/ppermute | solution.py:83
  38.7 4.2 %collective-permute-done.9 = bf16[1,128,768]{2,1,0:T(8,128)(2,1)S(1)} collective-permute-done((bf16[1,128,768]{2,1,0:T(8,128)(2,1)S(1)}, bf16[1,128,768]{2,1,0:T(8,128)(2,1)S(1)}, u32[]{:S(2)}, u32[]{:S(2)}) %collective-permute-start.9) | collective-permute-done | bytes 196640 | tf_op jit(solution)/shard_map/ppermute | solution.py:83
  42.9 4.2 %collective-permute-done.10 = bf16[1,128,768]{2,1,0:T(8,128)(2,1)S(1)} collective-permute-done((bf16[1,128,768]{2,1,0:T(8,128)(2,1)S(1)}, bf16[1,128,768]{2,1,0:T(8,128)(2,1)S(1)}, u32[]{:S(2)}, u32[]{:S(2)}) %collective-permute-start.10) | collective-permute-done | bytes 196640 | tf_op jit(solution)/shard_map/ppermute | solution.py:83
  47.2 0.1 maximum_maximum_fusion.refs_4_
  47.3 0.0 collective-permute-done.6.refs_3_
  47.3 0.6 product_first.1
  47.9 1.4 %product_rest.1 = (f32[128,1536]{1,0:T(8,128)S(1)}, f32[128,1536]{1,0:T(8,128)S(1)}, f32[128,1536]{1,0:T(8,128)S(1)}, bf16[3,128,1536]{2,1,0:T(8,128)(2,1)S(1)}) custom-call(bf16[2,512,128]{2,1,0:T(8,128)(2,1)S(1)} %get-tuple-element.41.refs_0_, bf16[2,512,128]{2,1,0:T(8,128)(2,1)S(1)} %collective-permute-done.5.refs_1_, ...), custom_call_target="tpu_custom_call" | custom-call | flops 1207959552 | bytes 1572864 | tf_op jit(solution)/shard_map/product_rest/pallas_call | solution.py:329
  49.3 0.0 copy-start.3
  49.3 0.9 collective-permute-start.11
  50.2 0.1 collective-permute-start.12
  50.3 3.0 %collective-permute-done.12.refs_1_ = bf16[1,128,1536]{2,1,0:T(8,128)(2,1)S(1)} collective-permute-done((bf16[1,128,1536]{2,1,0:T(8,128)(2,1)S(1)}, bf16[1,128,1536]{2,1,0:T(8,128)(2,1)S(1)}, u32[]{:S(2)}, u32[]{:S(2)}) %collective-permute-start.12) | collective-permute-done | bytes 393248 | tf_op jit(solution)/shard_map/ppermute | solution.py:83
  53.3 0.1 block_sum.3
  53.4 1.4 %collective-permute-start.13 = (bf16[128,1536]{1,0:T(8,128)(2,1)S(1)}, bf16[128,1536]{1,0:T(8,128)(2,1)S(1)}, u32[]{:S(2)}, u32[]{:S(2)}) collective-permute-start(bf16[128,1536]{1,0:T(8,128)(2,1)S(1)} %block_sum.3), channel_id=1, source_target_pairs={{0,8},{8,0},{16,24},{24,16},{1,9},{9,1},{17,25},{25,17},{2,10},{10... | collective-permute-start | bytes 1179656 | tf_op jit(solution)/shard_map/ppermute | solution.py:83
  54.7 0.0 copy-done.3
  54.7 3.9 %attention_backward.1 = (bf16[128,2048]{1,0:T(8,128)(2,1)}, f32[128,2048]{1,0:T(8,128)S(1)}, f32[128,2048]{1,0:T(8,128)S(1)}, bf16[2,128,2048]{2,1,0:T(8,128)(2,1)S(1)}) custom-call(s32[1,8]{1,0:T(1,128)S(1)} %copy-done.4, bf16[128,2048]{1,0:T(8,128)(2,1)S(1)} %bitcast.24, bf16[128,2048]{1,0:T(8,128)(2,1)S(1)} %bitcast.28, bf16[128,2048]{1,0:T(8,128)(2,1)S(1)} %bitcast.32, ...), custom_call_target="tpu_custom_call" | custom-call | flops 939524096 | bytes 7864320 | tf_op jit(solution)/shard_map/attention_backward/pallas_call | solution.py:380
  58.6 5.1 %collective-permute-done.13.refs_2_ = bf16[128,1536]{1,0:T(8,128)(2,1)S(1)} collective-permute-done((bf16[128,1536]{1,0:T(8,128)(2,1)S(1)}, bf16[128,1536]{1,0:T(8,128)(2,1)S(1)}, u32[]{:S(2)}, u32[]{:S(2)}) %collective-permute-start.13) | collective-permute-done | bytes 393248 | tf_op jit(solution)/shard_map/ppermute | solution.py:83
  63.8 0.0 collective-permute-done.11.refs_1_.refs_0_
  63.8 0.1 block_sum.4
  63.9 1.5 %collective-permute-start.15 = (bf16[2,128,2048]{2,1,0:T(8,128)(2,1)S(1)}, bf16[2,128,2048]{2,1,0:T(8,128)(2,1)S(1)}, u32[]{:S(2)}, u32[]{:S(2)}) collective-permute-start(bf16[2,128,2048]{2,1,0:T(8,128)(2,1)S(1)} %get-tuple-element.45), channel_id=1, source_target_pairs={{3,4},{5,6},{2,1},{4,3},{11,12},{13,14},{10,9},{12,11},{19,20},{21... | collective-permute-start | bytes 3145736 | tf_op jit(solution)/shard_map/ppermute | solution.py:435
  65.4 0.7 collective-permute-start.14
  66.1 0.1 block_sum.5
  66.2 1.4 %collective-permute-start.16 = (bf16[128,1536]{1,0:T(8,128)(2,1)S(1)}, bf16[128,1536]{1,0:T(8,128)(2,1)S(1)}, u32[]{:S(2)}, u32[]{:S(2)}) collective-permute-start(bf16[128,1536]{1,0:T(8,128)(2,1)S(1)} %block_sum.5), channel_id=1, source_target_pairs={{0,8},{8,0},{16,24},{24,16},{1,9},{9,1},{17,25},{25,17},{2,10},{10... | collective-permute-start | bytes 1179656 | tf_op jit(solution)/shard_map/ppermute | solution.py:83
  67.5 2.3 %collective-permute-start.17 = (bf16[128,1536]{1,0:T(8,128)(2,1)S(1)}, bf16[128,1536]{1,0:T(8,128)(2,1)S(1)}, u32[]{:S(2)}, u32[]{:S(2)}) collective-permute-start(bf16[128,1536]{1,0:T(8,128)(2,1)S(1)} %block_sum.4), channel_id=1, source_target_pairs={{0,16},{8,24},{16,0},{24,8},{1,17},{9,25},{17,1},{25,9},{2,18},{10... | collective-permute-start | bytes 1179656 | tf_op jit(solution)/shard_map/ppermute | solution.py:83
  69.9 15.4 %collective-permute-done.16.refs_1_ = bf16[128,1536]{1,0:T(8,128)(2,1)S(1)} collective-permute-done((bf16[128,1536]{1,0:T(8,128)(2,1)S(1)}, bf16[128,1536]{1,0:T(8,128)(2,1)S(1)}, u32[]{:S(2)}, u32[]{:S(2)}) %collective-permute-start.16) | collective-permute-done | bytes 393248 | tf_op jit(solution)/shard_map/ppermute | solution.py:83
  85.3 0.0 collective-permute-done.17.refs_2_
  85.3 0.9 gradient_sum.1
  86.2 1.8 %collective-permute-start.18 = (f32[128,128]{1,0:T(8,128)S(1)}, f32[128,128]{1,0:T(8,128)S(1)}, u32[]{:S(2)}, u32[]{:S(2)}) collective-permute-start(f32[128,128]{1,0:T(8,128)S(1)} %get-tuple-element.52.gram), channel_id=1, source_target_pairs={{0,2},{1,3},{2,0},{3,1},{4,6},{5,7},{6,4},{7,5},{8,10},{9,11},{10,... | collective-permute-start | bytes 196616 | tf_op jit(solution)/shard_map/ppermute | solution.py:83
  87.9 4.0 %collective-permute-done.18.gram_other = f32[128,128]{1,0:T(8,128)S(1)} collective-permute-done((f32[128,128]{1,0:T(8,128)S(1)}, f32[128,128]{1,0:T(8,128)S(1)}, u32[]{:S(2)}, u32[]{:S(2)}) %collective-permute-start.18) | collective-permute-done | bytes 65568 | tf_op jit(solution)/shard_map/ppermute | solution.py:83
  91.9 4.0 %newton_schulz.1 = (f32[128,384]{1,0:T(8,128)S(1)}, bf16[128,384]{1,0:T(8,128)(2,1)S(1)}, bf16[128,384]{1,0:T(8,128)(2,1)S(1)}, bf16[128,384]{1,0:T(8,128)(2,1)S(1)}) custom-call(f32[128,1536]{1,0:T(8,128)S(1)} %get-tuple-element.51.x, f32[128,128]{1,0:T(8,128)S(1)} %get-tuple-element.52.gram, f32[128,128]{1,0:T(8,128)S(1)} %collective-permute-done.18.gram_other), custom_call_target="tpu_custom_call" | custom-call | flops 301989888 | bytes 1572864 | tf_op jit(solution)/shard_map/newton_schulz/pallas_call | solution.py:412
  95.9 2.3 %collective-permute-start.19 = (bf16[128,384]{1,0:T(8,128)(2,1)S(1)}, bf16[128,384]{1,0:T(8,128)(2,1)S(1)}, u32[]{:S(2)}, u32[]{:S(2)}) collective-permute-start(bf16[128,384]{1,0:T(8,128)(2,1)S(1)} %get-tuple-element.55), channel_id=1, source_target_pairs={{0,1},{1,0},{2,3},{3,2},{4,5},{5,4},{6,7},{7,6},{8,9},{9,8},{10,11... | collective-permute-start | bytes 294920 | tf_op jit(solution)/shard_map/ppermute | solution.py:83
  98.2 1.5 %collective-permute-start.20 = (bf16[128,384]{1,0:T(8,128)(2,1)S(1)}, bf16[128,384]{1,0:T(8,128)(2,1)S(1)}, u32[]{:S(2)}, u32[]{:S(2)}) collective-permute-start(bf16[128,384]{1,0:T(8,128)(2,1)S(1)} %get-tuple-element.56), channel_id=1, source_target_pairs={{0,4},{1,5},{2,6},{3,7},{4,0},{5,1},{6,2},{7,3},{8,12},{9,13},{10,... | collective-permute-start | bytes 294920 | tf_op jit(solution)/shard_map/ppermute | solution.py:83
  99.7 0.2 collective-permute-start.21
  99.9 0.0 collective-permute-done.15.beyond
  99.9 0.0 collective-permute-done.14.mate
  99.9 1.8 %key_value_sum.1 = (bf16[128,2048]{1,0:T(8,128)(2,1)}, bf16[128,2048]{1,0:T(8,128)(2,1)}) custom-call(s32[1,8]{1,0:T(1,128)S(1)} %copy-done.4, f32[128,2048]{1,0:T(8,128)S(1)} %get-tuple-element.33.dko, f32[128,2048]{1,0:T(8,128)S(1)} %get-tuple-element.34.dvo, bf16[2,128,2048]{2,1,0:T(8,128)(2,1)S(1)} %collective-permute-done.14.mate, ...), custom_call_target="tpu_custom_call" | custom-call | flops 1572864 | bytes 5242880 | tf_op jit(solution)/shard_map/key_value_sum/pallas_call | solution.py:422
  101.7 0.0 collective-permute-done.19.refs_1_
  101.7 0.9 collective-permute-done.20.refs_2_
  102.6 2.3 %collective-permute-done.21.refs_3_ = bf16[128,384]{1,0:T(8,128)(2,1)S(1)} collective-permute-done((bf16[128,384]{1,0:T(8,128)(2,1)S(1)}, bf16[128,384]{1,0:T(8,128)(2,1)S(1)}, u32[]{:S(2)}, u32[]{:S(2)}) %collective-permute-start.21) | collective-permute-done | bytes 98336 | tf_op jit(solution)/shard_map/ppermute | solution.py:83
  104.9 0.9 update_rows.1
  (7 shorter events, 0.1 us)
Async XLA Ops:
  0.6 10.9 %collective-permute-start.2 = (bf16[128,2048]{1,0:T(8,128)(2,1)}, bf16[128,2048]{1,0:T(8,128)(2,1)S(1)}, u32[]{:S(2)}, u32[]{:S(2)}) collective-permute-start(bf16[128,2048]{1,0:T(8,128)(2,1)} %bitcast.25), channel_id=1, source_target_pairs={{1,2},{3,4},{4,3},{6,5},{9,10},{11,12},{12,11},{14,13},{17,18},{19... | collective-permute-start | bytes 1572872 | tf_op jit(solution)/shard_map/ppermute | solution.py:271
  5.2 12.0 %collective-permute-start.3 = (bf16[128,2048]{1,0:T(8,128)(2,1)}, bf16[128,2048]{1,0:T(8,128)(2,1)S(1)}, u32[]{:S(2)}, u32[]{:S(2)}) collective-permute-start(bf16[128,2048]{1,0:T(8,128)(2,1)} %bitcast.29), channel_id=1, source_target_pairs={{1,2},{3,4},{4,3},{6,5},{9,10},{11,12},{12,11},{14,13},{17,18},{19... | collective-permute-start | bytes 1572872 | tf_op jit(solution)/shard_map/ppermute | solution.py:272
  6.5 13.5 %collective-permute-start = (bf16[128,2048]{1,0:T(8,128)(2,1)}, bf16[128,2048]{1,0:T(8,128)(2,1)S(1)}, u32[]{:S(2)}, u32[]{:S(2)}) collective-permute-start(bf16[128,2048]{1,0:T(8,128)(2,1)} %bitcast.26), channel_id=1, source_target_pairs={{0,1},{1,0},{2,3},{3,2},{4,5},{5,4},{6,7},{7,6},{8,9},{9,8},{10,11... | collective-permute-start | bytes 1572872 | tf_op jit(solution)/shard_map/ppermute | solution.py:83
  6.6 13.4 %collective-permute-start.1 = (bf16[128,2048]{1,0:T(8,128)(2,1)}, bf16[128,2048]{1,0:T(8,128)(2,1)S(1)}, u32[]{:S(2)}, u32[]{:S(2)}) collective-permute-start(bf16[128,2048]{1,0:T(8,128)(2,1)} %bitcast.30), channel_id=1, source_target_pairs={{0,1},{1,0},{2,3},{3,2},{4,5},{5,4},{6,7},{7,6},{8,9},{9,8},{10,11... | collective-permute-start | bytes 1572872 | tf_op jit(solution)/shard_map/ppermute | solution.py:83
  7.1 12.9 %copy-start = (bf16[1,1,128,2048]{3,2,1,0:T(8,128)(2,1)S(1)}, bf16[1,1,128,2048]{3,2,1,0:T(8,128)(2,1)}, u32[]{:S(2)}) copy-start(bf16[1,1,128,2048]{3,2,1,0:T(8,128)(2,1)} %param.6) | copy-start | bytes 1572868
  7.1 12.9 %copy-start.1 = (bf16[1,1,128,2048]{3,2,1,0:T(8,128)(2,1)S(1)}, bf16[1,1,128,2048]{3,2,1,0:T(8,128)(2,1)}, u32[]{:S(2)}) copy-start(bf16[1,1,128,2048]{3,2,1,0:T(8,128)(2,1)} %param.7) | copy-start | bytes 1572868
  7.1 12.9 %copy-start.2 = (bf16[1,1,128,2048]{3,2,1,0:T(8,128)(2,1)S(1)}, bf16[1,1,128,2048]{3,2,1,0:T(8,128)(2,1)}, u32[]{:S(2)}) copy-start(bf16[1,1,128,2048]{3,2,1,0:T(8,128)(2,1)} %param.8) | copy-start | bytes 1572868
  7.1 12.9 %copy-start.4 = (s32[1,8]{1,0:T(1,128)S(1)}, s32[1,8]{1,0:T(1,128)}, u32[]{:S(2)}) copy-start(s32[1,8]{1,0:T(1,128)} %near_ref.5) | copy-start | bytes 100
  17.2 12.4 %collective-permute-start.7 = (bf16[128,1536]{1,0:T(8,128)(2,1)S(1)}, bf16[128,1536]{1,0:T(8,128)(2,1)S(1)}, u32[]{:S(2)}, u32[]{:S(2)}) collective-permute-start(bf16[128,1536]{1,0:T(8,128)(2,1)S(1)} %pad_maximum_fusion.1), channel_id=1, source_target_pairs={{0,2},{1,3},{2,0},{3,1},{4,6},{5,7},{6,4},{7,5},{8,10},{9,11},{10,... | collective-permute-start | bytes 1179656 | tf_op jit(solution)/shard_map/ppermute | solution.py:83
  22.4 8.8 %collective-permute-start.4 = (bf16[2,512,128]{2,1,0:T(8,128)(2,1)S(1)}, bf16[2,512,128]{2,1,0:T(8,128)(2,1)S(1)}, u32[]{:S(2)}, u32[]{:S(2)}) collective-permute-start(bf16[2,512,128]{2,1,0:T(8,128)(2,1)S(1)} %get-tuple-element.63), channel_id=1, source_target_pairs={{0,4},{1,5},{2,6},{3,7},{4,0},{5,1},{6,2},{7,3},{8,12},{9,13},{10,... | collective-permute-start | bytes 786440 | tf_op jit(solution)/shard_map/ppermute | solution.py:83
  22.4 12.7 %collective-permute-start.5 = (bf16[2,512,128]{2,1,0:T(8,128)(2,1)S(1)}, bf16[2,512,128]{2,1,0:T(8,128)(2,1)S(1)}, u32[]{:S(2)}, u32[]{:S(2)}) collective-permute-start(bf16[2,512,128]{2,1,0:T(8,128)(2,1)S(1)} %get-tuple-element.41.refs_0_), channel_id=1, source_target_pairs={{0,2},{1,3},{2,0},{3,1},{4,6},{5,7},{6,4},{7,5},{8,10},{9,11},{10,... | collective-permute-start | bytes 786440 | tf_op jit(solution)/shard_map/ppermute | solution.py:83
  23.3 15.4 %collective-permute-start.8 = (bf16[128,1536]{1,0:T(8,128)(2,1)S(1)}, bf16[128,1536]{1,0:T(8,128)(2,1)S(1)}, u32[]{:S(2)}, u32[]{:S(2)}) collective-permute-start(bf16[128,1536]{1,0:T(8,128)(2,1)S(1)} %get-tuple-element.38), channel_id=1, source_target_pairs={{0,4},{1,5},{2,6},{3,7},{4,0},{5,1},{6,2},{7,3},{8,12},{9,13},{10,... | collective-permute-start | bytes 1179656 | tf_op jit(solution)/shard_map/ppermute | solution.py:83
  29.6 13.3 %collective-permute-start.9 = (bf16[1,128,768]{2,1,0:T(8,128)(2,1)S(1)}, bf16[1,128,768]{2,1,0:T(8,128)(2,1)S(1)}, u32[]{:S(2)}, u32[]{:S(2)}) collective-permute-start(bf16[1,128,768]{2,1,0:T(8,128)(2,1)S(1)} %get-tuple-element.66), channel_id=1, source_target_pairs={{0,4},{1,5},{2,6},{3,7},{4,0},{5,1},{6,2},{7,3},{8,12},{9,13},{10,... | collective-permute-start | bytes 589832 | tf_op jit(solution)/shard_map/ppermute | solution.py:83
  29.7 17.5 %collective-permute-start.10 = (bf16[1,128,768]{2,1,0:T(8,128)(2,1)S(1)}, bf16[1,128,768]{2,1,0:T(8,128)(2,1)S(1)}, u32[]{:S(2)}, u32[]{:S(2)}) collective-permute-start(bf16[1,128,768]{2,1,0:T(8,128)(2,1)S(1)} %get-tuple-element.67), channel_id=1, source_target_pairs={{0,4},{1,5},{2,6},{3,7},{4,0},{5,1},{6,2},{7,3},{8,12},{9,13},{10,... | collective-permute-start | bytes 589832 | tf_op jit(solution)/shard_map/ppermute | solution.py:83
  35.1 12.1 %collective-permute-start.6 = (bf16[2,512,128]{2,1,0:T(8,128)(2,1)S(1)}, bf16[2,512,128]{2,1,0:T(8,128)(2,1)S(1)}, u32[]{:S(2)}, u32[]{:S(2)}) collective-permute-start(bf16[2,512,128]{2,1,0:T(8,128)(2,1)S(1)} %collective-permute-done.4.refs_2_), channel_id=1, source_target_pairs={{0,2},{1,3},{2,0},{3,1},{4,6},{5,7},{6,4},{7,5},{8,10},{9,11},{10,... | collective-permute-start | bytes 786440 | tf_op jit(solution)/shard_map/ppermute | solution.py:83
  49.3 5.4 %copy-start.3 = (bf16[1,1,128,2048]{3,2,1,0:T(8,128)(2,1)S(1)}, bf16[1,1,128,2048]{3,2,1,0:T(8,128)(2,1)}, u32[]{:S(2)}) copy-start(bf16[1,1,128,2048]{3,2,1,0:T(8,128)(2,1)} %param.9) | copy-start | bytes 1572868
  49.3 14.4 %collective-permute-start.11 = (bf16[3,128,1536]{2,1,0:T(8,128)(2,1)S(1)}, bf16[3,128,1536]{2,1,0:T(8,128)(2,1)S(1)}, u32[]{:S(2)}, u32[]{:S(2)}) collective-permute-start(bf16[3,128,1536]{2,1,0:T(8,128)(2,1)S(1)} %get-tuple-element.43), channel_id=1, source_target_pairs={{0,1},{1,0},{2,3},{3,2},{4,5},{5,4},{6,7},{7,6},{8,9},{9,8},{10,11... | collective-permute-start | bytes 3538952 | tf_op jit(solution)/shard_map/ppermute | solution.py:83
  50.2 3.0 %collective-permute-start.12 = (bf16[1,128,1536]{2,1,0:T(8,128)(2,1)S(1)}, bf16[1,128,1536]{2,1,0:T(8,128)(2,1)S(1)}, u32[]{:S(2)}, u32[]{:S(2)}) collective-permute-start(bf16[1,128,1536]{2,1,0:T(8,128)(2,1)S(1)} %get-tuple-element.44), channel_id=1, source_target_pairs={{0,1},{1,0},{2,3},{3,2},{4,5},{5,4},{6,7},{7,6},{8,9},{9,8},{10,11... | collective-permute-start | bytes 1179656 | tf_op jit(solution)/shard_map/ppermute | solution.py:83
  53.4 10.4 %collective-permute-start.13 = (bf16[128,1536]{1,0:T(8,128)(2,1)S(1)}, bf16[128,1536]{1,0:T(8,128)(2,1)S(1)}, u32[]{:S(2)}, u32[]{:S(2)}) collective-permute-start(bf16[128,1536]{1,0:T(8,128)(2,1)S(1)} %block_sum.3), channel_id=1, source_target_pairs={{0,8},{8,0},{16,24},{24,16},{1,9},{9,1},{17,25},{25,17},{2,10},{10... | collective-permute-start | bytes 1179656 | tf_op jit(solution)/shard_map/ppermute | solution.py:83
  63.9 36.1 %collective-permute-start.15 = (bf16[2,128,2048]{2,1,0:T(8,128)(2,1)S(1)}, bf16[2,128,2048]{2,1,0:T(8,128)(2,1)S(1)}, u32[]{:S(2)}, u32[]{:S(2)}) collective-permute-start(bf16[2,128,2048]{2,1,0:T(8,128)(2,1)S(1)} %get-tuple-element.45), channel_id=1, source_target_pairs={{3,4},{5,6},{2,1},{4,3},{11,12},{13,14},{10,9},{12,11},{19,20},{21... | collective-permute-start | bytes 3145736 | tf_op jit(solution)/shard_map/ppermute | solution.py:435
  65.4 34.6 %collective-permute-start.14 = (bf16[2,128,2048]{2,1,0:T(8,128)(2,1)S(1)}, bf16[2,128,2048]{2,1,0:T(8,128)(2,1)S(1)}, u32[]{:S(2)}, u32[]{:S(2)}) collective-permute-start(bf16[2,128,2048]{2,1,0:T(8,128)(2,1)S(1)} %get-tuple-element.45), channel_id=1, source_target_pairs={{0,1},{1,0},{2,3},{3,2},{4,5},{5,4},{6,7},{7,6},{8,9},{9,8},{10,11... | collective-permute-start | bytes 3145736 | tf_op jit(solution)/shard_map/ppermute | solution.py:83
  66.2 19.1 %collective-permute-start.16 = (bf16[128,1536]{1,0:T(8,128)(2,1)S(1)}, bf16[128,1536]{1,0:T(8,128)(2,1)S(1)}, u32[]{:S(2)}, u32[]{:S(2)}) collective-permute-start(bf16[128,1536]{1,0:T(8,128)(2,1)S(1)} %block_sum.5), channel_id=1, source_target_pairs={{0,8},{8,0},{16,24},{24,16},{1,9},{9,1},{17,25},{25,17},{2,10},{10... | collective-permute-start | bytes 1179656 | tf_op jit(solution)/shard_map/ppermute | solution.py:83
  67.5 17.7 %collective-permute-start.17 = (bf16[128,1536]{1,0:T(8,128)(2,1)S(1)}, bf16[128,1536]{1,0:T(8,128)(2,1)S(1)}, u32[]{:S(2)}, u32[]{:S(2)}) collective-permute-start(bf16[128,1536]{1,0:T(8,128)(2,1)S(1)} %block_sum.4), channel_id=1, source_target_pairs={{0,16},{8,24},{16,0},{24,8},{1,17},{9,25},{17,1},{25,9},{2,18},{10... | collective-permute-start | bytes 1179656 | tf_op jit(solution)/shard_map/ppermute | solution.py:83
  86.2 5.8 %collective-permute-start.18 = (f32[128,128]{1,0:T(8,128)S(1)}, f32[128,128]{1,0:T(8,128)S(1)}, u32[]{:S(2)}, u32[]{:S(2)}) collective-permute-start(f32[128,128]{1,0:T(8,128)S(1)} %get-tuple-element.52.gram), channel_id=1, source_target_pairs={{0,2},{1,3},{2,0},{3,1},{4,6},{5,7},{6,4},{7,5},{8,10},{9,11},{10,... | collective-permute-start | bytes 196616 | tf_op jit(solution)/shard_map/ppermute | solution.py:83
  95.9 5.8 %collective-permute-start.19 = (bf16[128,384]{1,0:T(8,128)(2,1)S(1)}, bf16[128,384]{1,0:T(8,128)(2,1)S(1)}, u32[]{:S(2)}, u32[]{:S(2)}) collective-permute-start(bf16[128,384]{1,0:T(8,128)(2,1)S(1)} %get-tuple-element.55), channel_id=1, source_target_pairs={{0,1},{1,0},{2,3},{3,2},{4,5},{5,4},{6,7},{7,6},{8,9},{9,8},{10,11... | collective-permute-start | bytes 294920 | tf_op jit(solution)/shard_map/ppermute | solution.py:83
  98.2 4.4 %collective-permute-start.20 = (bf16[128,384]{1,0:T(8,128)(2,1)S(1)}, bf16[128,384]{1,0:T(8,128)(2,1)S(1)}, u32[]{:S(2)}, u32[]{:S(2)}) collective-permute-start(bf16[128,384]{1,0:T(8,128)(2,1)S(1)} %get-tuple-element.56), channel_id=1, source_target_pairs={{0,4},{1,5},{2,6},{3,7},{4,0},{5,1},{6,2},{7,3},{8,12},{9,13},{10,... | collective-permute-start | bytes 294920 | tf_op jit(solution)/shard_map/ppermute | solution.py:83
  99.7 5.2 %collective-permute-start.21 = (bf16[128,384]{1,0:T(8,128)(2,1)S(1)}, bf16[128,384]{1,0:T(8,128)(2,1)S(1)}, u32[]{:S(2)}, u32[]{:S(2)}) collective-permute-start(bf16[128,384]{1,0:T(8,128)(2,1)S(1)} %get-tuple-element.57), channel_id=1, source_target_pairs={{0,5},{1,4},{2,7},{3,6},{4,1},{5,0},{6,3},{7,2},{8,13},{9,12},{10,... | collective-permute-start | bytes 294920 | tf_op jit(solution)/shard_map/ppermute | solution.py:83

commit v8 on v7

--- a/solution.py
+++ b/solution.py
@@ -127,7 +127,7 @@
             out[j >> 1, j & 1, rows, :] = dot_l(values, p).astype(bf16)
 
 
-def backward_kernel(near_ref, q, ko, vo, km, vm, kn, vn, g, dq, dko, dvo, dfar, far):
+def backward_kernel(near_ref, q, ko, vo, km, vm, kn, vn, g, dq, dko, dvo, dkf, dvf, dfar, far):
     choose_far(near_ref, km, vm, kn, vn, far)
     tile = q.shape[0]
     count = q.shape[1] // HEAD_DIM
@@ -152,20 +152,22 @@
             dq[:, at] = (dot_l(ds, keys) * SCALE).astype(bf16)
             dko[:, at] = dk[:tile]
             dvo[:, at] = dv[:tile]
-            dfar[0, :, at] = dk[tile:].astype(bf16)
-            dfar[1, :, at] = dv[tile:].astype(bf16)
-
-
-def combine_kernel(near_ref, dko, dvo, mate, beyond, dk, dv):
+            for which, (one, term) in enumerate(((dkf, dk), (dvf, dv))):
+                rounded = term[tile:].astype(bf16)
+                one[:, at] = rounded
+                dfar[which, :, at] = rounded
+
+
+def combine_kernel(near_ref, dko, dvo, mate, kn, vn, dk, dv):
     place = lax.axis_index("seq")
     last = lax.axis_size("seq") - 1
     other = place + 2 * (place & 1) - 1
     inside = (other >= 0) & (other <= last)
     from_mate = near_ref[0, place ^ 1] == place
     from_other = inside & (near_ref[0, jnp.clip(other, 0, last)] == place)
-    for which, (own, out) in enumerate(((dko, dk), (dvo, dv))):
+    for which, (own, beyond, out) in enumerate(((dko, kn, dk), (dvo, vn, dv))):
         total = own[...] + jnp.where(from_mate, mate[which].astype(f32), 0.0)
-        out[...] = (total + jnp.where(from_other, beyond[which].astype(f32), 0.0)).astype(bf16)
+        out[...] = (total + jnp.where(from_other, beyond[...].astype(f32), 0.0)).astype(bf16)
 
 
 def product_kernel(plan, layers, *refs):
@@ -353,16 +355,31 @@
             name="block_sum",
         )(*[array for array, *_ in parts])
 
-    leading = [i for i in range(m - 1, 1, -1) if i & 1]
-    blocks = product("product_first", leading, *pairs, held)
-    first_block = blocks[leading[0]][0][0]
-    blocks |= product(
-        "product_rest",
-        [i for i in range(m) if i not in leading],
-        after(pairs[0], first_block),
-        *pairs[1:],
-        held,
-    )
+    first = [i for i in range(m - 1, 1, -1) if i & 1]
+    middle = [i for i in range(m - 1, 1, -1) if not i & 1]
+    blocks = product("product_first", first, *pairs, held)
+    going = {i: added(blocks[i], 0, mine_width) for i in first}
+    blocks |= product("product_middle", middle, after(pairs[0], *going.values()), *pairs[1:], held)
+
+    dq, dko, dvo, dkf, dvf, dfar = pl.pallas_call(
+        backward_kernel,
+        out_shape=[
+            struct((tile, width), bf16),
+            struct((tile, width), f32),
+            struct((tile, width), f32),
+            struct((tile, width), bf16),
+            struct((tile, width), bf16),
+            struct((2, tile, width), bf16),
+        ],
+        in_specs=[smem()] + whole(8),
+        out_specs=whole(6),
+        scratch_shapes=[pltpu.VMEM((2, tile, width), bf16)],
+        compiler_params=params(),
+        cost_estimate=cost(28 * tile * tile * width, 30 * tile * width, 2 * tile * tile * head_count),
+        name="attention_backward",
+    )(neighbour, query, key, value, *beside, after(grad, *going.values()))
+
+    blocks |= product("product_last", [1, 0], after(pairs[0], dq), *pairs[1:], held)
 
     extra = {i: [] for i in range(m)}
     sent = []
@@ -370,28 +387,16 @@
     while bit < m:
         for i in range(m - 1, 1, -1):
             if i & -i == bit:
-                sent.append(added(blocks[i] + extra[i], 0, mine_width))
+                if bit == 1:
+                    sent.append(going[i])
+                else:
+                    (block, *where), *others = blocks[i] + extra[i]
+                    sent.append(added([(after(block, dq), *where)] + others, 0, mine_width))
                 extra[i ^ bit].append((shift(sent[-1], "dp", bit), None, 0))
         bit *= 2
     near = shift(after(added(blocks[1], 0, mine_width), sent[-1]), "dp", 1)
     own = blocks[0][0][0]
     came = [blocks[0][1], (near, None, 0)] + extra[0]
-
-    dq, dko, dvo, dfar = pl.pallas_call(
-        backward_kernel,
-        out_shape=[
-            struct((tile, width), bf16),
-            struct((tile, width), f32),
-            struct((tile, width), f32),
-            struct((2, tile, width), bf16),
-        ],
-        in_specs=[smem()] + whole(8),
-        out_specs=whole(4),
-        scratch_shapes=[pltpu.VMEM((2, tile, width), bf16)],
-        compiler_params=params(),
-        cost_estimate=cost(28 * tile * tile * width, 30 * tile * width, 2 * tile * tile * head_count),
-        name="attention_backward",
-    )(neighbour, query, key, value, *beside, after(grad, *pairs[plan.col :: plan.col]))
 
     x, gram = pl.pallas_call(
         functools.partial(gram_kernel, [spot for _, *spot in came]),
@@ -418,11 +423,11 @@
         cost_estimate=cost(12 * HEAD_DIM * HEAD_DIM * mine_width, 8 * HEAD_DIM * mine_width),
         name="newton_schulz",
     )(x, gram, gram_other)
-    dfar = after(dfar, sent[-1])
+    dkf, dvf, dfar = (after(part, sent[-1]) for part in (dkf, dvf, dfar))
     dk, dv = pl.pallas_call(
         combine_kernel,
         out_shape=[struct((tile, width), bf16)] * 2,
-        in_specs=[smem()] + whole(4),
+        in_specs=[smem()] + whole(5),
         out_specs=whole(2),
         compiler_params=params(),
         cost_estimate=cost(6 * tile * width, 20 * tile * width),
@@ -432,7 +437,8 @@
         dko,
         dvo,
         shift(dfar, "seq", 1),
-        lax.ppermute(dfar, "seq", gives),
+        lax.ppermute(dkf, "seq", gives),
+        lax.ppermute(dvf, "seq", gives),
     )
 
     pieces = [pieces[0]] + [

time: 106 us -> 103 us (0.972)
  waiting for transfers between devices: 59.8 us -> 54.5 us
  starting transfers between devices: 27.5 us -> 29.7 us
    ppermute x19 -> x20, waiting for transfers between devices: 51.1 us -> 45.8 us  [shift(): lax.ppermute(value, axis, [(i, i ^ mask) for i in range(lax.axis_size(axi...]
    ppermute x1 -> x2, starting transfers between devices: 1.47 us -> 2.74 us  [the longest x1 1.46 us: local(): lax.ppermute(dvf, 'seq', gives)]
    ppermute x19 -> x20, starting transfers between devices: 20.1 us -> 21.1 us  [shift(): lax.ppermute(value, axis, [(i, i ^ mask) for i in range(lax.axis_size(axi...]
    pallas_call x2 -> x3, Pallas kernels: 2.01 us -> 2.21 us  [product(): pl.pallas_call(functools.partial(product_kernel, plan, layers), out_shape...]
  transfers between devices with their start and end apart: 22 -> 24, of which waited for: 13 -> 14; matrix products, arithmetic and copies ran while one was open for 2% -> 2% of each run, Pallas kernels for 12% -> 14%
where the time goes in v8:
time: 103 us
  waiting for transfers between devices  54.5 us (53%)
  starting transfers between devices  29.7 us (29%)
  Pallas kernels  16.3 us (16%)
  local copies, waits for them, and re-layouts  1.47 us (1%)
    ppermute x20, waiting for transfers between devices, shift(): lax.ppermute(value, axis, [(i, i ^ mask) for i in range(lax.axis_size(axi...  45.8 us
    ppermute x20, starting transfers between devices, shift(): lax.ppermute(value, axis, [(i, i ^ mask) for i in range(lax.axis_size(axi...  21.1 us
    ppermute x1, waiting for transfers between devices, local(): value_next = lax.ppermute(value, 'seq', takes)  5.62 us
    ppermute x1, starting transfers between devices, local(): key_next = lax.ppermute(key, 'seq', takes)  4.54 us
    pallas_call x1, Pallas kernels, local(): pl.pallas_call(backward_kernel, out_shape=[struct((tile, width), bf16), s...  4.05 us
    pallas_call x1, Pallas kernels, local(): pl.pallas_call(functools.partial(update_kernel, plan, factor), out_shape=...  3.97 us
    ppermute x1, waiting for transfers between devices, local(): key_next = lax.ppermute(key, 'seq', takes)  3.04 us
    pallas_call x1, Pallas kernels, local(): pl.pallas_call(functools.partial(forward_kernel, plan), out_shape=struct(...  2.29 us
  transfers between devices with their start and end apart: 24, of which 14 were waited for; matrix products, arithmetic and copies ran while one was open for 2% of the time, Pallas kernels for 14%

profile of v8, /device:TPU:1, one launch (start us, length us, event | category | flops | bytes accessed | tf_op | source)
XLA Modules:
  0.0 103.0 jit_solution(15700702966156663400)
XLA Ops:
  0.6 4.5 %collective-permute-start.2 = (bf16[128,2048]{1,0:T(8,128)(2,1)}, bf16[128,2048]{1,0:T(8,128)(2,1)S(1)}, u32[]{:S(2)}, u32[]{:S(2)}) collective-permute-start(bf16[128,2048]{1,0:T(8,128)(2,1)} %bitcast.25), channel_id=1, source_target_pairs={{1,2},{3,4},{4,3},{6,5},{9,10},{11,12},{12,11},{14,13},{17,18},{19... | collective-permute-start | bytes 1572872 | tf_op jit(solution)/shard_map/ppermute | solution.py:273
  5.2 1.3 %collective-permute-start.3 = (bf16[128,2048]{1,0:T(8,128)(2,1)}, bf16[128,2048]{1,0:T(8,128)(2,1)S(1)}, u32[]{:S(2)}, u32[]{:S(2)}) collective-permute-start(bf16[128,2048]{1,0:T(8,128)(2,1)} %bitcast.29), channel_id=1, source_target_pairs={{1,2},{3,4},{4,3},{6,5},{9,10},{11,12},{12,11},{14,13},{17,18},{19... | collective-permute-start | bytes 1572872 | tf_op jit(solution)/shard_map/ppermute | solution.py:274
  6.5 0.1 collective-permute-start
  6.6 0.5 collective-permute-start.1
  7.1 1.4 %dynamic-slice_bitcast_fusion.3 = (bf16[128,768]{1,0:T(8,128)(2,1)S(1)}, bf16[128,768]{1,0:T(8,128)(2,1)S(1)}, bf16[128,768]{1,0:T(8,128)(2,1)S(1)}, bf16[128,768]{1,0:T(8,128)(2,1)S(1)}) fusion(bf16[1,1,128,3072]{3,2,1,0:T(8,128)(2,1)} %param.10, s32[]{:T(128)S(6)} %select_n.12, s32[]{:T(128)S(6)} %select_n.13, s32[]{:T(128)S(6)} %select_n.15, s32[]{:T(128)S(6)} %select_n.14), kind=kLoop, calls=%fused_computation.8 | loop fusion | bytes 1572880 | tf_op jit(solution)/shard_map/dynamic_slice | solution.py:287
  8.5 3.0 %collective-permute-done.2.kn = bf16[128,2048]{1,0:T(8,128)(2,1)S(1)} collective-permute-done((bf16[128,2048]{1,0:T(8,128)(2,1)}, bf16[128,2048]{1,0:T(8,128)(2,1)S(1)}, u32[]{:S(2)}, u32[]{:S(2)}) %collective-permute-start.2) | collective-permute-done | bytes 524320 | tf_op jit(solution)/shard_map/ppermute | solution.py:273
  11.6 5.6 %collective-permute-done.3.vn = bf16[128,2048]{1,0:T(8,128)(2,1)S(1)} collective-permute-done((bf16[128,2048]{1,0:T(8,128)(2,1)}, bf16[128,2048]{1,0:T(8,128)(2,1)S(1)}, u32[]{:S(2)}, u32[]{:S(2)}) %collective-permute-start.3) | collective-permute-done | bytes 524320 | tf_op jit(solution)/shard_map/ppermute | solution.py:274
  17.2 2.7 %collective-permute-start.7 = (bf16[128,1536]{1,0:T(8,128)(2,1)S(1)}, bf16[128,1536]{1,0:T(8,128)(2,1)S(1)}, u32[]{:S(2)}, u32[]{:S(2)}) collective-permute-start(bf16[128,1536]{1,0:T(8,128)(2,1)S(1)} %pad_maximum_fusion.1), channel_id=1, source_target_pairs={{0,2},{1,3},{2,0},{3,1},{4,6},{5,7},{6,4},{7,5},{8,10},{9,11},{10,... | collective-permute-start | bytes 1179656 | tf_op jit(solution)/shard_map/ppermute | solution.py:83
  19.9 0.1 fusion
  20.0 0.0 collective-permute-done.km
  20.0 0.0 collective-permute-done.1.vm
  20.0 2.3 %attention_forward.1 = bf16[2,2,512,128]{3,2,1,0:T(8,128)(2,1)S(1)} custom-call(s32[1,8]{1,0:T(1,128)S(1)} %copy-done.4, bf16[128,2048]{1,0:T(8,128)(2,1)S(1)} %bitcast.23, bf16[128,2048]{1,0:T(8,128)(2,1)S(1)} %bitcast.27, bf16[128,2048]{1,0:T(8,128)(2,1)S(1)} %bitcast.31, bf16[128,2048]{1,0:T(8,128)(2,1)S(1)} %collective-permute-done.km, ...), custom_call_target="tpu_custom_call" | custom-call | flops 268435456 | bytes 4194304 | tf_op jit(solution)/shard_map/attention_forward/pallas_call | solution.py:303
  22.4 0.1 collective-permute-start.4
  22.4 0.9 collective-permute-start.5
  23.3 0.6 collective-permute-start.8
  24.0 5.6 %collective-permute-done.7 = bf16[128,1536]{1,0:T(8,128)(2,1)S(1)} collective-permute-done((bf16[128,1536]{1,0:T(8,128)(2,1)S(1)}, bf16[128,1536]{1,0:T(8,128)(2,1)S(1)}, u32[]{:S(2)}, u32[]{:S(2)}) %collective-permute-start.7) | collective-permute-done | bytes 393248 | tf_op jit(solution)/shard_map/ppermute | solution.py:83
  29.6 0.1 collective-permute-start.10
  29.7 1.5 %collective-permute-start.9 = (bf16[1,128,768]{2,1,0:T(8,128)(2,1)S(1)}, bf16[1,128,768]{2,1,0:T(8,128)(2,1)S(1)}, u32[]{:S(2)}, u32[]{:S(2)}) collective-permute-start(bf16[1,128,768]{2,1,0:T(8,128)(2,1)S(1)} %get-tuple-element.80), channel_id=1, source_target_pairs={{0,4},{1,5},{2,6},{3,7},{4,0},{5,1},{6,2},{7,3},{8,12},{9,13},{10,... | collective-permute-start | bytes 589832 | tf_op jit(solution)/shard_map/ppermute | solution.py:83
  31.1 4.0 %collective-permute-done.4.refs_1_ = bf16[2,512,128]{2,1,0:T(8,128)(2,1)S(1)} collective-permute-done((bf16[2,512,128]{2,1,0:T(8,128)(2,1)S(1)}, bf16[2,512,128]{2,1,0:T(8,128)(2,1)S(1)}, u32[]{:S(2)}, u32[]{:S(2)}) %collective-permute-start.4) | collective-permute-done | bytes 262176 | tf_op jit(solution)/shard_map/ppermute | solution.py:83
  35.1 0.0 collective-permute-done.5.refs_2_
  35.1 1.3 %collective-permute-start.6 = (bf16[2,512,128]{2,1,0:T(8,128)(2,1)S(1)}, bf16[2,512,128]{2,1,0:T(8,128)(2,1)S(1)}, u32[]{:S(2)}, u32[]{:S(2)}) collective-permute-start(bf16[2,512,128]{2,1,0:T(8,128)(2,1)S(1)} %collective-permute-done.5.refs_2_), channel_id=1, source_target_pairs={{0,2},{1,3},{2,0},{3,1},{4,6},{5,7},{6,4},{7,5},{8,10},{9,11},{10,... | collective-permute-start | bytes 786440 | tf_op jit(solution)/shard_map/ppermute | solution.py:83
  36.4 1.4 %collective-permute-done.8 = bf16[128,1536]{1,0:T(8,128)(2,1)S(1)} collective-permute-done((bf16[128,1536]{1,0:T(8,128)(2,1)S(1)}, bf16[128,1536]{1,0:T(8,128)(2,1)S(1)}, u32[]{:S(2)}, u32[]{:S(2)}) %collective-permute-start.8) | collective-permute-done | bytes 393248 | tf_op jit(solution)/shard_map/ppermute | solution.py:83
  37.8 4.2 %collective-permute-done.10 = bf16[1,128,768]{2,1,0:T(8,128)(2,1)S(1)} collective-permute-done((bf16[1,128,768]{2,1,0:T(8,128)(2,1)S(1)}, bf16[1,128,768]{2,1,0:T(8,128)(2,1)S(1)}, u32[]{:S(2)}, u32[]{:S(2)}) %collective-permute-start.10) | collective-permute-done | bytes 196640 | tf_op jit(solution)/shard_map/ppermute | solution.py:83
  42.0 4.2 %collective-permute-done.9 = bf16[1,128,768]{2,1,0:T(8,128)(2,1)S(1)} collective-permute-done((bf16[1,128,768]{2,1,0:T(8,128)(2,1)S(1)}, bf16[1,128,768]{2,1,0:T(8,128)(2,1)S(1)}, u32[]{:S(2)}, u32[]{:S(2)}) %collective-permute-start.9) | collective-permute-done | bytes 196640 | tf_op jit(solution)/shard_map/ppermute | solution.py:83
  46.2 0.1 maximum_maximum_fusion.refs_4_
  46.4 0.0 collective-permute-done.6.refs_3_
  46.4 0.6 product_first.1
  47.0 1.9 %collective-permute-start.11 = (bf16[1,128,1536]{2,1,0:T(8,128)(2,1)S(1)}, bf16[1,128,1536]{2,1,0:T(8,128)(2,1)S(1)}, u32[]{:S(2)}, u32[]{:S(2)}) collective-permute-start(bf16[1,128,1536]{2,1,0:T(8,128)(2,1)S(1)} %get-tuple-element.43), channel_id=1, source_target_pairs={{0,1},{1,0},{2,3},{3,2},{4,5},{5,4},{6,7},{7,6},{8,9},{9,8},{10,11... | collective-permute-start | bytes 1179656 | tf_op jit(solution)/shard_map/ppermute | solution.py:83
  48.9 1.3 %collective-permute-done.11.refs_1_ = bf16[1,128,1536]{2,1,0:T(8,128)(2,1)S(1)} collective-permute-done((bf16[1,128,1536]{2,1,0:T(8,128)(2,1)S(1)}, bf16[1,128,1536]{2,1,0:T(8,128)(2,1)S(1)}, u32[]{:S(2)}, u32[]{:S(2)}) %collective-permute-start.11) | collective-permute-done | bytes 393248 | tf_op jit(solution)/shard_map/ppermute | solution.py:83
  50.2 0.1 block_sum.3
  50.3 0.0 copy-start.3
  50.3 1.4 %collective-permute-start.13 = (bf16[128,1536]{1,0:T(8,128)(2,1)S(1)}, bf16[128,1536]{1,0:T(8,128)(2,1)S(1)}, u32[]{:S(2)}, u32[]{:S(2)}) collective-permute-start(bf16[128,1536]{1,0:T(8,128)(2,1)S(1)} %block_sum.3), channel_id=1, source_target_pairs={{0,8},{8,0},{16,24},{24,16},{1,9},{9,1},{17,25},{25,17},{2,10},{10... | collective-permute-start | bytes 1179656 | tf_op jit(solution)/shard_map/ppermute | solution.py:83
  51.7 0.6 product_middle.1
  52.3 0.7 collective-permute-start.12
  53.0 4.0 %attention_backward.1 = (bf16[128,2048]{1,0:T(8,128)(2,1)}, f32[128,2048]{1,0:T(8,128)S(1)}, f32[128,2048]{1,0:T(8,128)S(1)}, bf16[128,2048]{1,0:T(8,128)(2,1)S(...) custom-call(s32[1,8]{1,0:T(1,128)S(1)} %copy-done.4, bf16[128,2048]{1,0:T(8,128)(2,1)S(1)} %bitcast.24, ...), custom_call_target="tpu_custom_call" | custom-call | flops 939524096 | bytes 7864320 | tf_op jit(solution)/shard_map/attention_backward/pallas_call | solution.py:364
  57.1 1.0 product_last.1
  58.1 0.1 collective-permute-start.17
  58.2 0.0 collective-permute-done.12.refs_1_
  58.2 2.5 %collective-permute-done.13.refs_2_ = bf16[128,1536]{1,0:T(8,128)(2,1)S(1)} collective-permute-done((bf16[128,1536]{1,0:T(8,128)(2,1)S(1)}, bf16[128,1536]{1,0:T(8,128)(2,1)S(1)}, u32[]{:S(2)}, u32[]{:S(2)}) %collective-permute-start.13) | collective-permute-done | bytes 393248 | tf_op jit(solution)/shard_map/ppermute | solution.py:83
  60.7 0.1 block_sum.4
  60.8 1.3 %collective-permute-start.14 = (bf16[2,128,2048]{2,1,0:T(8,128)(2,1)S(1)}, bf16[2,128,2048]{2,1,0:T(8,128)(2,1)S(1)}, u32[]{:S(2)}, u32[]{:S(2)}) collective-permute-start(bf16[2,128,2048]{2,1,0:T(8,128)(2,1)S(1)} %get-tuple-element.53), channel_id=1, source_target_pairs={{0,1},{1,0},{2,3},{3,2},{4,5},{5,4},{6,7},{7,6},{8,9},{9,8},{10,11... | collective-permute-start | bytes 3145736 | tf_op jit(solution)/shard_map/ppermute | solution.py:83
  62.1 1.3 %collective-permute-start.15 = (bf16[128,2048]{1,0:T(8,128)(2,1)S(1)}, bf16[128,2048]{1,0:T(8,128)(2,1)S(1)}, u32[]{:S(2)}, u32[]{:S(2)}) collective-permute-start(bf16[128,2048]{1,0:T(8,128)(2,1)S(1)} %get-tuple-element.55), channel_id=1, source_target_pairs={{3,4},{5,6},{2,1},{4,3},{11,12},{13,14},{10,9},{12,11},{19,20},{21... | collective-permute-start | bytes 1572872 | tf_op jit(solution)/shard_map/ppermute | solution.py:440
  63.4 2.4 %collective-permute-start.19 = (bf16[128,1536]{1,0:T(8,128)(2,1)S(1)}, bf16[128,1536]{1,0:T(8,128)(2,1)S(1)}, u32[]{:S(2)}, u32[]{:S(2)}) collective-permute-start(bf16[128,1536]{1,0:T(8,128)(2,1)S(1)} %block_sum.4), channel_id=1, source_target_pairs={{0,16},{8,24},{16,0},{24,8},{1,17},{9,25},{17,1},{25,9},{2,18},{10... | collective-permute-start | bytes 1179656 | tf_op jit(solution)/shard_map/ppermute | solution.py:83
  65.8 0.0 collective-permute-done.17.refs_1_.refs_0_
  65.8 0.1 block_sum.5
  65.9 1.4 %collective-permute-start.18 = (bf16[128,1536]{1,0:T(8,128)(2,1)S(1)}, bf16[128,1536]{1,0:T(8,128)(2,1)S(1)}, u32[]{:S(2)}, u32[]{:S(2)}) collective-permute-start(bf16[128,1536]{1,0:T(8,128)(2,1)S(1)} %block_sum.5), channel_id=1, source_target_pairs={{0,8},{8,0},{16,24},{24,16},{1,9},{9,1},{17,25},{25,17},{2,10},{10... | collective-permute-start | bytes 1179656 | tf_op jit(solution)/shard_map/ppermute | solution.py:83
  67.2 1.5 %collective-permute-start.16 = (bf16[128,2048]{1,0:T(8,128)(2,1)S(1)}, bf16[128,2048]{1,0:T(8,128)(2,1)S(1)}, u32[]{:S(2)}, u32[]{:S(2)}) collective-permute-start(bf16[128,2048]{1,0:T(8,128)(2,1)S(1)} %get-tuple-element.57), channel_id=1, source_target_pairs={{3,4},{5,6},{2,1},{4,3},{11,12},{13,14},{10,9},{12,11},{19,20},{21... | collective-permute-start | bytes 1572872 | tf_op jit(solution)/shard_map/ppermute | solution.py:441
  68.7 15.1 %collective-permute-done.19.refs_2_ = bf16[128,1536]{1,0:T(8,128)(2,1)S(1)} collective-permute-done((bf16[128,1536]{1,0:T(8,128)(2,1)S(1)}, bf16[128,1536]{1,0:T(8,128)(2,1)S(1)}, u32[]{:S(2)}, u32[]{:S(2)}) %collective-permute-start.19) | collective-permute-done | bytes 393248 | tf_op jit(solution)/shard_map/ppermute | solution.py:83
  83.7 0.4 collective-permute-done.18.refs_1_
  84.2 0.8 gradient_sum.1
  85.0 2.0 %collective-permute-start.20 = (f32[128,128]{1,0:T(8,128)S(1)}, f32[128,128]{1,0:T(8,128)S(1)}, u32[]{:S(2)}, u32[]{:S(2)}) collective-permute-start(f32[128,128]{1,0:T(8,128)S(1)} %get-tuple-element.66.gram), channel_id=1, source_target_pairs={{0,2},{1,3},{2,0},{3,1},{4,6},{5,7},{6,4},{7,5},{8,10},{9,11},{10,... | collective-permute-start | bytes 196616 | tf_op jit(solution)/shard_map/ppermute | solution.py:83
  87.1 3.9 %collective-permute-done.20.gram_other = f32[128,128]{1,0:T(8,128)S(1)} collective-permute-done((f32[128,128]{1,0:T(8,128)S(1)}, f32[128,128]{1,0:T(8,128)S(1)}, u32[]{:S(2)}, u32[]{:S(2)}) %collective-permute-start.20) | collective-permute-done | bytes 65568 | tf_op jit(solution)/shard_map/ppermute | solution.py:83
  90.9 4.0 %newton_schulz.1 = (f32[128,384]{1,0:T(8,128)S(1)}, bf16[128,384]{1,0:T(8,128)(2,1)S(1)}, bf16[128,384]{1,0:T(8,128)(2,1)S(1)}, bf16[128,384]{1,0:T(8,128)(2,1)S(1)}) custom-call(f32[128,1536]{1,0:T(8,128)S(1)} %get-tuple-element.65.x, f32[128,128]{1,0:T(8,128)S(1)} %get-tuple-element.66.gram, f32[128,128]{1,0:T(8,128)S(1)} %collective-permute-done.20.gram_other), custom_call_target="tpu_custom_call" | custom-call | flops 301989888 | bytes 1572864 | tf_op jit(solution)/shard_map/newton_schulz/pallas_call | solution.py:417
  94.9 0.6 collective-permute-start.21
  95.5 0.4 collective-permute-start.22
  95.9 0.0 collective-permute-done.15.kn
  95.9 1.3 %collective-permute-start.23 = (bf16[128,384]{1,0:T(8,128)(2,1)S(1)}, bf16[128,384]{1,0:T(8,128)(2,1)S(1)}, u32[]{:S(2)}, u32[]{:S(2)}) collective-permute-start(bf16[128,384]{1,0:T(8,128)(2,1)S(1)} %get-tuple-element.71), channel_id=1, source_target_pairs={{0,5},{1,4},{2,7},{3,6},{4,1},{5,0},{6,3},{7,2},{8,13},{9,12},{10,... | collective-permute-start | bytes 294920 | tf_op jit(solution)/shard_map/ppermute | solution.py:83
  97.2 0.0 collective-permute-done.16.vn
  97.2 0.0 collective-permute-done.14.mate
  97.2 1.8 %key_value_sum.1 = (bf16[128,2048]{1,0:T(8,128)(2,1)}, bf16[128,2048]{1,0:T(8,128)(2,1)}) custom-call(s32[1,8]{1,0:T(1,128)S(1)} %copy-done.4, f32[128,2048]{1,0:T(8,128)S(1)} %get-tuple-element.46.dko, f32[128,2048]{1,0:T(8,128)S(1)} %get-tuple-element.47.dvo, bf16[2,128,2048]{2,1,0:T(8,128)(2,1)S(1)} %collective-permute-done.14.mate, ...), custom_call_target="tpu_custom_call" | custom-call | flops 1572864 | bytes 5242880 | tf_op jit(solution)/shard_map/key_value_sum/pallas_call | solution.py:427
  99.0 0.0 collective-permute-done.21.refs_1_
  99.0 0.8 collective-permute-done.22.refs_2_
  99.8 2.3 %collective-permute-done.23.refs_3_ = bf16[128,384]{1,0:T(8,128)(2,1)S(1)} collective-permute-done((bf16[128,384]{1,0:T(8,128)(2,1)S(1)}, bf16[128,384]{1,0:T(8,128)(2,1)S(1)}, u32[]{:S(2)}, u32[]{:S(2)}) %collective-permute-start.23) | collective-permute-done | bytes 98336 | tf_op jit(solution)/shard_map/ppermute | solution.py:83
  102.1 0.9 update_rows.1
  (12 shorter events, 0.1 us)
Async XLA Ops:
  0.6 10.9 %collective-permute-start.2 = (bf16[128,2048]{1,0:T(8,128)(2,1)}, bf16[128,2048]{1,0:T(8,128)(2,1)S(1)}, u32[]{:S(2)}, u32[]{:S(2)}) collective-permute-start(bf16[128,2048]{1,0:T(8,128)(2,1)} %bitcast.25), channel_id=1, source_target_pairs={{1,2},{3,4},{4,3},{6,5},{9,10},{11,12},{12,11},{14,13},{17,18},{19... | collective-permute-start | bytes 1572872 | tf_op jit(solution)/shard_map/ppermute | solution.py:273
  5.2 12.0 %collective-permute-start.3 = (bf16[128,2048]{1,0:T(8,128)(2,1)}, bf16[128,2048]{1,0:T(8,128)(2,1)S(1)}, u32[]{:S(2)}, u32[]{:S(2)}) collective-permute-start(bf16[128,2048]{1,0:T(8,128)(2,1)} %bitcast.29), channel_id=1, source_target_pairs={{1,2},{3,4},{4,3},{6,5},{9,10},{11,12},{12,11},{14,13},{17,18},{19... | collective-permute-start | bytes 1572872 | tf_op jit(solution)/shard_map/ppermute | solution.py:274
  6.5 13.5 %collective-permute-start = (bf16[128,2048]{1,0:T(8,128)(2,1)}, bf16[128,2048]{1,0:T(8,128)(2,1)S(1)}, u32[]{:S(2)}, u32[]{:S(2)}) collective-permute-start(bf16[128,2048]{1,0:T(8,128)(2,1)} %bitcast.26), channel_id=1, source_target_pairs={{0,1},{1,0},{2,3},{3,2},{4,5},{5,4},{6,7},{7,6},{8,9},{9,8},{10,11... | collective-permute-start | bytes 1572872 | tf_op jit(solution)/shard_map/ppermute | solution.py:83
  6.6 13.4 %collective-permute-start.1 = (bf16[128,2048]{1,0:T(8,128)(2,1)}, bf16[128,2048]{1,0:T(8,128)(2,1)S(1)}, u32[]{:S(2)}, u32[]{:S(2)}) collective-permute-start(bf16[128,2048]{1,0:T(8,128)(2,1)} %bitcast.30), channel_id=1, source_target_pairs={{0,1},{1,0},{2,3},{3,2},{4,5},{5,4},{6,7},{7,6},{8,9},{9,8},{10,11... | collective-permute-start | bytes 1572872 | tf_op jit(solution)/shard_map/ppermute | solution.py:83
  7.1 12.9 %copy-start = (bf16[1,1,128,2048]{3,2,1,0:T(8,128)(2,1)S(1)}, bf16[1,1,128,2048]{3,2,1,0:T(8,128)(2,1)}, u32[]{:S(2)}) copy-start(bf16[1,1,128,2048]{3,2,1,0:T(8,128)(2,1)} %param.6) | copy-start | bytes 1572868
  7.1 12.9 %copy-start.1 = (bf16[1,1,128,2048]{3,2,1,0:T(8,128)(2,1)S(1)}, bf16[1,1,128,2048]{3,2,1,0:T(8,128)(2,1)}, u32[]{:S(2)}) copy-start(bf16[1,1,128,2048]{3,2,1,0:T(8,128)(2,1)} %param.7) | copy-start | bytes 1572868
  7.1 12.9 %copy-start.2 = (bf16[1,1,128,2048]{3,2,1,0:T(8,128)(2,1)S(1)}, bf16[1,1,128,2048]{3,2,1,0:T(8,128)(2,1)}, u32[]{:S(2)}) copy-start(bf16[1,1,128,2048]{3,2,1,0:T(8,128)(2,1)} %param.8) | copy-start | bytes 1572868
  7.1 12.9 %copy-start.4 = (s32[1,8]{1,0:T(1,128)S(1)}, s32[1,8]{1,0:T(1,128)}, u32[]{:S(2)}) copy-start(s32[1,8]{1,0:T(1,128)} %near_ref.5) | copy-start | bytes 100
  17.2 12.4 %collective-permute-start.7 = (bf16[128,1536]{1,0:T(8,128)(2,1)S(1)}, bf16[128,1536]{1,0:T(8,128)(2,1)S(1)}, u32[]{:S(2)}, u32[]{:S(2)}) collective-permute-start(bf16[128,1536]{1,0:T(8,128)(2,1)S(1)} %pad_maximum_fusion.1), channel_id=1, source_target_pairs={{0,2},{1,3},{2,0},{3,1},{4,6},{5,7},{6,4},{7,5},{8,10},{9,11},{10,... | collective-permute-start | bytes 1179656 | tf_op jit(solution)/shard_map/ppermute | solution.py:83
  22.4 12.8 %collective-permute-start.4 = (bf16[2,512,128]{2,1,0:T(8,128)(2,1)S(1)}, bf16[2,512,128]{2,1,0:T(8,128)(2,1)S(1)}, u32[]{:S(2)}, u32[]{:S(2)}) collective-permute-start(bf16[2,512,128]{2,1,0:T(8,128)(2,1)S(1)} %get-tuple-element.60.refs_0_), channel_id=1, source_target_pairs={{0,2},{1,3},{2,0},{3,1},{4,6},{5,7},{6,4},{7,5},{8,10},{9,11},{10,... | collective-permute-start | bytes 786440 | tf_op jit(solution)/shard_map/ppermute | solution.py:83
  22.4 12.7 %collective-permute-start.5 = (bf16[2,512,128]{2,1,0:T(8,128)(2,1)S(1)}, bf16[2,512,128]{2,1,0:T(8,128)(2,1)S(1)}, u32[]{:S(2)}, u32[]{:S(2)}) collective-permute-start(bf16[2,512,128]{2,1,0:T(8,128)(2,1)S(1)} %get-tuple-element.76), channel_id=1, source_target_pairs={{0,4},{1,5},{2,6},{3,7},{4,0},{5,1},{6,2},{7,3},{8,12},{9,13},{10,... | collective-permute-start | bytes 786440 | tf_op jit(solution)/shard_map/ppermute | solution.py:83
  23.3 14.5 %collective-permute-start.8 = (bf16[128,1536]{1,0:T(8,128)(2,1)S(1)}, bf16[128,1536]{1,0:T(8,128)(2,1)S(1)}, u32[]{:S(2)}, u32[]{:S(2)}) collective-permute-start(bf16[128,1536]{1,0:T(8,128)(2,1)S(1)} %get-tuple-element.40), channel_id=1, source_target_pairs={{0,4},{1,5},{2,6},{3,7},{4,0},{5,1},{6,2},{7,3},{8,12},{9,13},{10,... | collective-permute-start | bytes 1179656 | tf_op jit(solution)/shard_map/ppermute | solution.py:83
  29.6 12.4 %collective-permute-start.10 = (bf16[1,128,768]{2,1,0:T(8,128)(2,1)S(1)}, bf16[1,128,768]{2,1,0:T(8,128)(2,1)S(1)}, u32[]{:S(2)}, u32[]{:S(2)}) collective-permute-start(bf16[1,128,768]{2,1,0:T(8,128)(2,1)S(1)} %get-tuple-element.81), channel_id=1, source_target_pairs={{0,4},{1,5},{2,6},{3,7},{4,0},{5,1},{6,2},{7,3},{8,12},{9,13},{10,... | collective-permute-start | bytes 589832 | tf_op jit(solution)/shard_map/ppermute | solution.py:83
  29.7 16.6 %collective-permute-start.9 = (bf16[1,128,768]{2,1,0:T(8,128)(2,1)S(1)}, bf16[1,128,768]{2,1,0:T(8,128)(2,1)S(1)}, u32[]{:S(2)}, u32[]{:S(2)}) collective-permute-start(bf16[1,128,768]{2,1,0:T(8,128)(2,1)S(1)} %get-tuple-element.80), channel_id=1, source_target_pairs={{0,4},{1,5},{2,6},{3,7},{4,0},{5,1},{6,2},{7,3},{8,12},{9,13},{10,... | collective-permute-start | bytes 589832 | tf_op jit(solution)/shard_map/ppermute | solution.py:83
  35.1 11.2 %collective-permute-start.6 = (bf16[2,512,128]{2,1,0:T(8,128)(2,1)S(1)}, bf16[2,512,128]{2,1,0:T(8,128)(2,1)S(1)}, u32[]{:S(2)}, u32[]{:S(2)}) collective-permute-start(bf16[2,512,128]{2,1,0:T(8,128)(2,1)S(1)} %collective-permute-done.5.refs_2_), channel_id=1, source_target_pairs={{0,2},{1,3},{2,0},{3,1},{4,6},{5,7},{6,4},{7,5},{8,10},{9,11},{10,... | collective-permute-start | bytes 786440 | tf_op jit(solution)/shard_map/ppermute | solution.py:83
  47.0 3.2 %collective-permute-start.11 = (bf16[1,128,1536]{2,1,0:T(8,128)(2,1)S(1)}, bf16[1,128,1536]{2,1,0:T(8,128)(2,1)S(1)}, u32[]{:S(2)}, u32[]{:S(2)}) collective-permute-start(bf16[1,128,1536]{2,1,0:T(8,128)(2,1)S(1)} %get-tuple-element.43), channel_id=1, source_target_pairs={{0,1},{1,0},{2,3},{3,2},{4,5},{5,4},{6,7},{7,6},{8,9},{9,8},{10,11... | collective-permute-start | bytes 1179656 | tf_op jit(solution)/shard_map/ppermute | solution.py:83
  50.3 2.7 %copy-start.3 = (bf16[1,1,128,2048]{3,2,1,0:T(8,128)(2,1)S(1)}, bf16[1,1,128,2048]{3,2,1,0:T(8,128)(2,1)}, u32[]{:S(2)}) copy-start(bf16[1,1,128,2048]{3,2,1,0:T(8,128)(2,1)} %param.9) | copy-start | bytes 1572868
  50.3 10.4 %collective-permute-start.13 = (bf16[128,1536]{1,0:T(8,128)(2,1)S(1)}, bf16[128,1536]{1,0:T(8,128)(2,1)S(1)}, u32[]{:S(2)}, u32[]{:S(2)}) collective-permute-start(bf16[128,1536]{1,0:T(8,128)(2,1)S(1)} %block_sum.3), channel_id=1, source_target_pairs={{0,8},{8,0},{16,24},{24,16},{1,9},{9,1},{17,25},{25,17},{2,10},{10... | collective-permute-start | bytes 1179656 | tf_op jit(solution)/shard_map/ppermute | solution.py:83
  52.3 5.9 %collective-permute-start.12 = (bf16[1,128,1536]{2,1,0:T(8,128)(2,1)S(1)}, bf16[1,128,1536]{2,1,0:T(8,128)(2,1)S(1)}, u32[]{:S(2)}, u32[]{:S(2)}) collective-permute-start(bf16[1,128,1536]{2,1,0:T(8,128)(2,1)S(1)} %get-tuple-element.52), channel_id=1, source_target_pairs={{0,1},{1,0},{2,3},{3,2},{4,5},{5,4},{6,7},{7,6},{8,9},{9,8},{10,11... | collective-permute-start | bytes 1179656 | tf_op jit(solution)/shard_map/ppermute | solution.py:83
  58.1 7.7 %collective-permute-start.17 = (bf16[2,128,1536]{2,1,0:T(8,128)(2,1)S(1)}, bf16[2,128,1536]{2,1,0:T(8,128)(2,1)S(1)}, u32[]{:S(2)}, u32[]{:S(2)}) collective-permute-start(bf16[2,128,1536]{2,1,0:T(8,128)(2,1)S(1)} %get-tuple-element.62), channel_id=1, source_target_pairs={{0,1},{1,0},{2,3},{3,2},{4,5},{5,4},{6,7},{7,6},{8,9},{9,8},{10,11... | collective-permute-start | bytes 2359304 | tf_op jit(solution)/shard_map/ppermute | solution.py:83
  60.8 36.3 %collective-permute-start.14 = (bf16[2,128,2048]{2,1,0:T(8,128)(2,1)S(1)}, bf16[2,128,2048]{2,1,0:T(8,128)(2,1)S(1)}, u32[]{:S(2)}, u32[]{:S(2)}) collective-permute-start(bf16[2,128,2048]{2,1,0:T(8,128)(2,1)S(1)} %get-tuple-element.53), channel_id=1, source_target_pairs={{0,1},{1,0},{2,3},{3,2},{4,5},{5,4},{6,7},{7,6},{8,9},{9,8},{10,11... | collective-permute-start | bytes 3145736 | tf_op jit(solution)/shard_map/ppermute | solution.py:83
  62.1 33.8 %collective-permute-start.15 = (bf16[128,2048]{1,0:T(8,128)(2,1)S(1)}, bf16[128,2048]{1,0:T(8,128)(2,1)S(1)}, u32[]{:S(2)}, u32[]{:S(2)}) collective-permute-start(bf16[128,2048]{1,0:T(8,128)(2,1)S(1)} %get-tuple-element.55), channel_id=1, source_target_pairs={{3,4},{5,6},{2,1},{4,3},{11,12},{13,14},{10,9},{12,11},{19,20},{21... | collective-permute-start | bytes 1572872 | tf_op jit(solution)/shard_map/ppermute | solution.py:440
  63.4 20.3 %collective-permute-start.19 = (bf16[128,1536]{1,0:T(8,128)(2,1)S(1)}, bf16[128,1536]{1,0:T(8,128)(2,1)S(1)}, u32[]{:S(2)}, u32[]{:S(2)}) collective-permute-start(bf16[128,1536]{1,0:T(8,128)(2,1)S(1)} %block_sum.4), channel_id=1, source_target_pairs={{0,16},{8,24},{16,0},{24,8},{1,17},{9,25},{17,1},{25,9},{2,18},{10... | collective-permute-start | bytes 1179656 | tf_op jit(solution)/shard_map/ppermute | solution.py:83
  65.9 18.3 %collective-permute-start.18 = (bf16[128,1536]{1,0:T(8,128)(2,1)S(1)}, bf16[128,1536]{1,0:T(8,128)(2,1)S(1)}, u32[]{:S(2)}, u32[]{:S(2)}) collective-permute-start(bf16[128,1536]{1,0:T(8,128)(2,1)S(1)} %block_sum.5), channel_id=1, source_target_pairs={{0,8},{8,0},{16,24},{24,16},{1,9},{9,1},{17,25},{25,17},{2,10},{10... | collective-permute-start | bytes 1179656 | tf_op jit(solution)/shard_map/ppermute | solution.py:83
  67.2 29.9 %collective-permute-start.16 = (bf16[128,2048]{1,0:T(8,128)(2,1)S(1)}, bf16[128,2048]{1,0:T(8,128)(2,1)S(1)}, u32[]{:S(2)}, u32[]{:S(2)}) collective-permute-start(bf16[128,2048]{1,0:T(8,128)(2,1)S(1)} %get-tuple-element.57), channel_id=1, source_target_pairs={{3,4},{5,6},{2,1},{4,3},{11,12},{13,14},{10,9},{12,11},{19,20},{21... | collective-permute-start | bytes 1572872 | tf_op jit(solution)/shard_map/ppermute | solution.py:441
  85.0 5.9 %collective-permute-start.20 = (f32[128,128]{1,0:T(8,128)S(1)}, f32[128,128]{1,0:T(8,128)S(1)}, u32[]{:S(2)}, u32[]{:S(2)}) collective-permute-start(f32[128,128]{1,0:T(8,128)S(1)} %get-tuple-element.66.gram), channel_id=1, source_target_pairs={{0,2},{1,3},{2,0},{3,1},{4,6},{5,7},{6,4},{7,5},{8,10},{9,11},{10,... | collective-permute-start | bytes 196616 | tf_op jit(solution)/shard_map/ppermute | solution.py:83
  94.9 4.1 %collective-permute-start.21 = (bf16[128,384]{1,0:T(8,128)(2,1)S(1)}, bf16[128,384]{1,0:T(8,128)(2,1)S(1)}, u32[]{:S(2)}, u32[]{:S(2)}) collective-permute-start(bf16[128,384]{1,0:T(8,128)(2,1)S(1)} %get-tuple-element.69), channel_id=1, source_target_pairs={{0,1},{1,0},{2,3},{3,2},{4,5},{5,4},{6,7},{7,6},{8,9},{9,8},{10,11... | collective-permute-start | bytes 294920 | tf_op jit(solution)/shard_map/ppermute | solution.py:83
  95.5 4.4 %collective-permute-start.22 = (bf16[128,384]{1,0:T(8,128)(2,1)S(1)}, bf16[128,384]{1,0:T(8,128)(2,1)S(1)}, u32[]{:S(2)}, u32[]{:S(2)}) collective-permute-start(bf16[128,384]{1,0:T(8,128)(2,1)S(1)} %get-tuple-element.70), channel_id=1, source_target_pairs={{0,4},{1,5},{2,6},{3,7},{4,0},{5,1},{6,2},{7,3},{8,12},{9,13},{10,... | collective-permute-start | bytes 294920 | tf_op jit(solution)/shard_map/ppermute | solution.py:83
  95.9 6.2 %collective-permute-start.23 = (bf16[128,384]{1,0:T(8,128)(2,1)S(1)}, bf16[128,384]{1,0:T(8,128)(2,1)S(1)}, u32[]{:S(2)}, u32[]{:S(2)}) collective-permute-start(bf16[128,384]{1,0:T(8,128)(2,1)S(1)} %get-tuple-element.71), channel_id=1, source_target_pairs={{0,5},{1,4},{2,7},{3,6},{4,1},{5,0},{6,3},{7,2},{8,13},{9,12},{10,... | collective-permute-start | bytes 294920 | tf_op jit(solution)/shard_map/ppermute | solution.py:83

commit v9 on v8

--- a/solution.py
+++ b/solution.py
@@ -318,7 +318,7 @@
         there = after(came_high, *pairs[1 : plan.col])
         pairs += [shift(there, "seq", q << 1) for q in range(1, plan.col)]
 
-    through = after(jnp.stack(columns[1:]), attended)
+    through = after(jnp.stack(columns[1:]), attended, *high_columns)
     held = [jnp.stack(columns)]
     for high in range(1, plan.high):
         rest = jnp.concatenate(
@@ -379,7 +379,8 @@
         name="attention_backward",
     )(neighbour, query, key, value, *beside, after(grad, *going.values()))
 
-    blocks |= product("product_last", [1, 0], after(pairs[0], dq), *pairs[1:], held)
+    blocks |= product("product_near", [1], after(pairs[0], dq), *pairs[1:], held)
+    blocks |= product("product_own", [0], after(pairs[0], dq), *pairs[1:], held)
 
     extra = {i: [] for i in range(m)}
     sent = []
@@ -394,7 +395,7 @@
                     sent.append(added([(after(block, dq), *where)] + others, 0, mine_width))
                 extra[i ^ bit].append((shift(sent[-1], "dp", bit), None, 0))
         bit *= 2
-    near = shift(after(added(blocks[1], 0, mine_width), sent[-1]), "dp", 1)
+    near = shift(after(added(blocks[1], 0, mine_width), sent[-1], blocks[0][1][0]), "dp", 1)
     own = blocks[0][0][0]
     came = [blocks[0][1], (near, None, 0)] + extra[0]
 
@@ -452,7 +453,7 @@
         compiler_params=params(),
         cost_estimate=cost(1, 8 * per * HEAD_DIM * slot),
         name="update_rows",
-    )(after(pieces[0], dk), *pieces[1:])
+    )(*pieces)
 
     shape = query_tiles.shape
     return dq.reshape(shape), dk.reshape(shape), dv.reshape(shape), update

time: 103 us -> 108 us (1.049)
  waiting for transfers between devices: 54.5 us -> 61.9 us
  starting transfers between devices: 29.7 us -> 26.5 us
    ppermute x20 -> x21, waiting for transfers between devices: 45.8 us -> 55 us  [shift(): lax.ppermute(value, axis, [(i, i ^ mask) for i in range(lax.axis_size(axi...]
    ppermute x20 -> x21, starting transfers between devices: 21.1 us -> 15.8 us  [shift(): lax.ppermute(value, axis, [(i, i ^ mask) for i in range(lax.axis_size(axi...]
    ppermute x1, starting transfers between devices: 1.32 us -> 3.49 us  [local(): value_next = lax.ppermute(value, 'seq', takes)]
    ppermute x1, waiting for transfers between devices: 3.04 us -> 1.27 us  [local(): key_next = lax.ppermute(key, 'seq', takes)]
    pallas_call x3 -> x4, Pallas kernels: 2.21 us -> 2.38 us  [product(): pl.pallas_call(functools.partial(product_kernel, plan, layers), out_shape...]
  transfers between devices with their start and end apart: 24 -> 25, of which waited for: 14 -> 15; matrix products, arithmetic and copies ran while one was open for 2% -> 2% of each run, Pallas kernels for 14% -> 12%
where the time goes in v9:
time: 108 us; the launch traced here: 107 us
  waiting for transfers between devices  61.9 us (57%)
  starting transfers between devices  26.5 us (25%)
  Pallas kernels  16.5 us (15%)
  local copies, waits for them, and re-layouts  1.47 us (1%)
    ppermute x21, waiting for transfers between devices, shift(): lax.ppermute(value, axis, [(i, i ^ mask) for i in range(lax.axis_size(axi...  55 us
    ppermute x21, starting transfers between devices, shift(): lax.ppermute(value, axis, [(i, i ^ mask) for i in range(lax.axis_size(axi...  15.8 us
    ppermute x1, waiting for transfers between devices, local(): value_next = lax.ppermute(value, 'seq', takes)  5.62 us
    ppermute x1, starting transfers between devices, local(): key_next = lax.ppermute(key, 'seq', takes)  4.49 us
    pallas_call x1, Pallas kernels, local(): pl.pallas_call(backward_kernel, out_shape=[struct((tile, width), bf16), s...  3.96 us
    pallas_call x1, Pallas kernels, local(): pl.pallas_call(functools.partial(update_kernel, plan, factor), out_shape=...  3.94 us
    ppermute x1, starting transfers between devices, local(): value_next = lax.ppermute(value, 'seq', takes)  3.49 us
    pallas_call x4, Pallas kernels, product(): pl.pallas_call(functools.partial(product_kernel, plan, layers), out_shape...  2.38 us
  transfers between devices with their start and end apart: 25, of which 15 were waited for; matrix products, arithmetic and copies ran while one was open for 2% of the time, Pallas kernels for 12%

profile of v9, /device:TPU:1, one launch (start us, length us, event | category | flops | bytes accessed | tf_op | source)
XLA Modules:
  0.0 107.5 jit_solution(8681200343650129612)
XLA Ops:
  0.6 0.1 collective-permute-start
  0.8 4.5 %collective-permute-start.2 = (bf16[128,2048]{1,0:T(8,128)(2,1)}, bf16[128,2048]{1,0:T(8,128)(2,1)S(1)}, u32[]{:S(2)}, u32[]{:S(2)}) collective-permute-start(bf16[128,2048]{1,0:T(8,128)(2,1)} %bitcast.26), channel_id=1, source_target_pairs={{1,2},{3,4},{4,3},{6,5},{9,10},{11,12},{12,11},{14,13},{17,18},{19... | collective-permute-start | bytes 1572872 | tf_op jit(solution)/shard_map/ppermute | solution.py:273
  5.3 0.1 collective-permute-start.1
  5.3 3.5 %collective-permute-start.3 = (bf16[128,2048]{1,0:T(8,128)(2,1)}, bf16[128,2048]{1,0:T(8,128)(2,1)S(1)}, u32[]{:S(2)}, u32[]{:S(2)}) collective-permute-start(bf16[128,2048]{1,0:T(8,128)(2,1)} %bitcast.30), channel_id=1, source_target_pairs={{1,2},{3,4},{4,3},{6,5},{9,10},{11,12},{12,11},{14,13},{17,18},{19... | collective-permute-start | bytes 1572872 | tf_op jit(solution)/shard_map/ppermute | solution.py:274
  8.9 1.4 %dynamic-slice_bitcast_fusion.3 = (bf16[128,768]{1,0:T(8,128)(2,1)S(1)}, bf16[128,768]{1,0:T(8,128)(2,1)S(1)}, bf16[128,768]{1,0:T(8,128)(2,1)S(1)}, bf16[128,768]{1,0:T(8,128)(2,1)S(1)}) fusion(bf16[1,1,128,3072]{3,2,1,0:T(8,128)(2,1)} %param.10, s32[]{:T(128)S(6)} %select_n.12, s32[]{:T(128)S(6)} %select_n.13, s32[]{:T(128)S(6)} %select_n.15, s32[]{:T(128)S(6)} %select_n.14), kind=kLoop, calls=%fused_computation.8 | loop fusion | bytes 1572880 | tf_op jit(solution)/shard_map/dynamic_slice | solution.py:287
  10.3 0.1 fusion
  10.4 1.3 %collective-permute-done.2.kn = bf16[128,2048]{1,0:T(8,128)(2,1)S(1)} collective-permute-done((bf16[128,2048]{1,0:T(8,128)(2,1)}, bf16[128,2048]{1,0:T(8,128)(2,1)S(1)}, u32[]{:S(2)}, u32[]{:S(2)}) %collective-permute-start.2) | collective-permute-done | bytes 524320 | tf_op jit(solution)/shard_map/ppermute | solution.py:273
  11.6 5.6 %collective-permute-done.3.vn = bf16[128,2048]{1,0:T(8,128)(2,1)S(1)} collective-permute-done((bf16[128,2048]{1,0:T(8,128)(2,1)}, bf16[128,2048]{1,0:T(8,128)(2,1)S(1)}, u32[]{:S(2)}, u32[]{:S(2)}) %collective-permute-start.3) | collective-permute-done | bytes 524320 | tf_op jit(solution)/shard_map/ppermute | solution.py:274
  17.3 3.4 %collective-permute-start.7 = (bf16[128,1536]{1,0:T(8,128)(2,1)S(1)}, bf16[128,1536]{1,0:T(8,128)(2,1)S(1)}, u32[]{:S(2)}, u32[]{:S(2)}) collective-permute-start(bf16[128,1536]{1,0:T(8,128)(2,1)S(1)} %pad_maximum_fusion.1), channel_id=1, source_target_pairs={{0,2},{1,3},{2,0},{3,1},{4,6},{5,7},{6,4},{7,5},{8,10},{9,11},{10,... | collective-permute-start | bytes 1179656 | tf_op jit(solution)/shard_map/ppermute | solution.py:83
  20.6 0.0 collective-permute-start.8
  20.6 0.0 collective-permute-done.km
  20.6 0.0 collective-permute-done.1.vm
  20.7 2.3 %attention_forward.1 = bf16[2,2,512,128]{3,2,1,0:T(8,128)(2,1)S(1)} custom-call(s32[1,8]{1,0:T(1,128)S(1)} %copy-done.4, bf16[128,2048]{1,0:T(8,128)(2,1)S(1)} %bitcast.23, bf16[128,2048]{1,0:T(8,128)(2,1)S(1)} %bitcast.27, bf16[128,2048]{1,0:T(8,128)(2,1)S(1)} %bitcast.31, bf16[128,2048]{1,0:T(8,128)(2,1)S(1)} %collective-permute-done.km, ...), custom_call_target="tpu_custom_call" | custom-call | flops 268435456 | bytes 4194304 | tf_op jit(solution)/shard_map/attention_forward/pallas_call | solution.py:303
  23.0 0.9 collective-permute-start.4
  24.0 0.7 collective-permute-start.5
  24.6 5.6 %collective-permute-done.7 = bf16[128,1536]{1,0:T(8,128)(2,1)S(1)} collective-permute-done((bf16[128,1536]{1,0:T(8,128)(2,1)S(1)}, bf16[128,1536]{1,0:T(8,128)(2,1)S(1)}, u32[]{:S(2)}, u32[]{:S(2)}) %collective-permute-start.7) | collective-permute-done | bytes 393248 | tf_op jit(solution)/shard_map/ppermute | solution.py:83
  30.3 1.5 %collective-permute-done.8 = bf16[128,1536]{1,0:T(8,128)(2,1)S(1)} collective-permute-done((bf16[128,1536]{1,0:T(8,128)(2,1)S(1)}, bf16[128,1536]{1,0:T(8,128)(2,1)S(1)}, u32[]{:S(2)}, u32[]{:S(2)}) %collective-permute-start.8) | collective-permute-done | bytes 393248 | tf_op jit(solution)/shard_map/ppermute | solution.py:83
  31.8 0.1 collective-permute-start.10
  31.9 1.5 %collective-permute-start.9 = (bf16[1,128,768]{2,1,0:T(8,128)(2,1)S(1)}, bf16[1,128,768]{2,1,0:T(8,128)(2,1)S(1)}, u32[]{:S(2)}, u32[]{:S(2)}) collective-permute-start(bf16[1,128,768]{2,1,0:T(8,128)(2,1)S(1)} %get-tuple-element.80), channel_id=1, source_target_pairs={{0,4},{1,5},{2,6},{3,7},{4,0},{5,1},{6,2},{7,3},{8,12},{9,13},{10,... | collective-permute-start | bytes 589832 | tf_op jit(solution)/shard_map/ppermute | solution.py:83
  33.3 1.9 %collective-permute-done.4.refs_1_ = bf16[2,512,128]{2,1,0:T(8,128)(2,1)S(1)} collective-permute-done((bf16[2,512,128]{2,1,0:T(8,128)(2,1)S(1)}, bf16[2,512,128]{2,1,0:T(8,128)(2,1)S(1)}, u32[]{:S(2)}, u32[]{:S(2)}) %collective-permute-start.4) | collective-permute-done | bytes 262176 | tf_op jit(solution)/shard_map/ppermute | solution.py:83
  35.2 2.2 %collective-permute-done.5.refs_2_ = bf16[2,512,128]{2,1,0:T(8,128)(2,1)S(1)} collective-permute-done((bf16[2,512,128]{2,1,0:T(8,128)(2,1)S(1)}, bf16[2,512,128]{2,1,0:T(8,128)(2,1)S(1)}, u32[]{:S(2)}, u32[]{:S(2)}) %collective-permute-start.5) | collective-permute-done | bytes 262176 | tf_op jit(solution)/shard_map/ppermute | solution.py:83
  37.4 0.0 collective-permute-start.6
  37.4 4.2 %collective-permute-done.10 = bf16[1,128,768]{2,1,0:T(8,128)(2,1)S(1)} collective-permute-done((bf16[1,128,768]{2,1,0:T(8,128)(2,1)S(1)}, bf16[1,128,768]{2,1,0:T(8,128)(2,1)S(1)}, u32[]{:S(2)}, u32[]{:S(2)}) %collective-permute-start.10) | collective-permute-done | bytes 196640 | tf_op jit(solution)/shard_map/ppermute | solution.py:83
  41.6 4.1 %collective-permute-done.9 = bf16[1,128,768]{2,1,0:T(8,128)(2,1)S(1)} collective-permute-done((bf16[1,128,768]{2,1,0:T(8,128)(2,1)S(1)}, bf16[1,128,768]{2,1,0:T(8,128)(2,1)S(1)}, u32[]{:S(2)}, u32[]{:S(2)}) %collective-permute-start.9) | collective-permute-done | bytes 196640 | tf_op jit(solution)/shard_map/ppermute | solution.py:83
  45.7 0.1 maximum_maximum_fusion.refs_4_
  45.8 0.0 collective-permute-done.6.refs_3_
  45.8 0.6 product_first.1
  46.4 0.4 collective-permute-start.11
  46.8 1.4 %collective-permute-done.11.refs_1_ = bf16[1,128,1536]{2,1,0:T(8,128)(2,1)S(1)} collective-permute-done((bf16[1,128,1536]{2,1,0:T(8,128)(2,1)S(1)}, bf16[1,128,1536]{2,1,0:T(8,128)(2,1)S(1)}, u32[]{:S(2)}, u32[]{:S(2)}) %collective-permute-start.11) | collective-permute-done | bytes 393248 | tf_op jit(solution)/shard_map/ppermute | solution.py:83
  48.2 0.1 block_sum.3
  48.3 0.0 copy-start.3
  48.3 0.6 product_middle.1
  48.9 0.4 collective-permute-start.12
  49.2 1.3 %collective-permute-start.13 = (bf16[128,1536]{1,0:T(8,128)(2,1)S(1)}, bf16[128,1536]{1,0:T(8,128)(2,1)S(1)}, u32[]{:S(2)}, u32[]{:S(2)}) collective-permute-start(bf16[128,1536]{1,0:T(8,128)(2,1)S(1)} %block_sum.3), channel_id=1, source_target_pairs={{0,8},{8,0},{16,24},{24,16},{1,9},{9,1},{17,25},{25,17},{2,10},{10... | collective-permute-start | bytes 1179656 | tf_op jit(solution)/shard_map/ppermute | solution.py:83
  50.5 4.0 %attention_backward.1 = (bf16[128,2048]{1,0:T(8,128)(2,1)}, f32[128,2048]{1,0:T(8,128)S(1)}, f32[128,2048]{1,0:T(8,128)S(1)}, bf16[128,2048]{1,0:T(8,128)(2,1)S(...) custom-call(s32[1,8]{1,0:T(1,128)S(1)} %copy-done.4, bf16[128,2048]{1,0:T(8,128)(2,1)S(1)} %bitcast.24, ...), custom_call_target="tpu_custom_call" | custom-call | flops 939524096 | bytes 7864320 | tf_op jit(solution)/shard_map/attention_backward/pallas_call | solution.py:364
  54.5 0.6 product_near.1
  55.1 0.6 collective-permute-start.18
  55.7 0.6 product_own.1
  56.3 0.1 collective-permute-start.17
  56.3 0.0 collective-permute-done.12.refs_1_
  56.4 3.4 %collective-permute-done.13.refs_2_ = bf16[128,1536]{1,0:T(8,128)(2,1)S(1)} collective-permute-done((bf16[128,1536]{1,0:T(8,128)(2,1)S(1)}, bf16[128,1536]{1,0:T(8,128)(2,1)S(1)}, u32[]{:S(2)}, u32[]{:S(2)}) %collective-permute-start.13) | collective-permute-done | bytes 393248 | tf_op jit(solution)/shard_map/ppermute | solution.py:83
  59.7 0.1 block_sum.4
  59.9 1.1 %collective-permute-start.14 = (bf16[2,128,2048]{2,1,0:T(8,128)(2,1)S(1)}, bf16[2,128,2048]{2,1,0:T(8,128)(2,1)S(1)}, u32[]{:S(2)}, u32[]{:S(2)}) collective-permute-start(bf16[2,128,2048]{2,1,0:T(8,128)(2,1)S(1)} %get-tuple-element.53), channel_id=1, source_target_pairs={{0,1},{1,0},{2,3},{3,2},{4,5},{5,4},{6,7},{7,6},{8,9},{9,8},{10,11... | collective-permute-start | bytes 3145736 | tf_op jit(solution)/shard_map/ppermute | solution.py:83
  61.0 0.0 collective-permute-done.18.refs_1_
  61.0 0.1 block_sum.5
  61.1 0.0 collective-permute-done.17.refs_0_
  61.1 1.4 %collective-permute-start.19 = (bf16[128,1536]{1,0:T(8,128)(2,1)S(1)}, bf16[128,1536]{1,0:T(8,128)(2,1)S(1)}, u32[]{:S(2)}, u32[]{:S(2)}) collective-permute-start(bf16[128,1536]{1,0:T(8,128)(2,1)S(1)} %block_sum.5), channel_id=1, source_target_pairs={{0,8},{8,0},{16,24},{24,16},{1,9},{9,1},{17,25},{25,17},{2,10},{10... | collective-permute-start | bytes 1179656 | tf_op jit(solution)/shard_map/ppermute | solution.py:83
  62.4 2.3 %collective-permute-start.20 = (bf16[128,1536]{1,0:T(8,128)(2,1)S(1)}, bf16[128,1536]{1,0:T(8,128)(2,1)S(1)}, u32[]{:S(2)}, u32[]{:S(2)}) collective-permute-start(bf16[128,1536]{1,0:T(8,128)(2,1)S(1)} %block_sum.4), channel_id=1, source_target_pairs={{0,16},{8,24},{16,0},{24,8},{1,17},{9,25},{17,1},{25,9},{2,18},{10... | collective-permute-start | bytes 1179656 | tf_op jit(solution)/shard_map/ppermute | solution.py:83
  64.7 1.3 %collective-permute-start.15 = (bf16[128,2048]{1,0:T(8,128)(2,1)S(1)}, bf16[128,2048]{1,0:T(8,128)(2,1)S(1)}, u32[]{:S(2)}, u32[]{:S(2)}) collective-permute-start(bf16[128,2048]{1,0:T(8,128)(2,1)S(1)} %get-tuple-element.55), channel_id=1, source_target_pairs={{3,4},{5,6},{2,1},{4,3},{11,12},{13,14},{10,9},{12,11},{19,20},{21... | collective-permute-start | bytes 1572872 | tf_op jit(solution)/shard_map/ppermute | solution.py:441
  66.0 1.5 %collective-permute-start.16 = (bf16[128,2048]{1,0:T(8,128)(2,1)S(1)}, bf16[128,2048]{1,0:T(8,128)(2,1)S(1)}, u32[]{:S(2)}, u32[]{:S(2)}) collective-permute-start(bf16[128,2048]{1,0:T(8,128)(2,1)S(1)} %get-tuple-element.57), channel_id=1, source_target_pairs={{3,4},{5,6},{2,1},{4,3},{11,12},{13,14},{10,9},{12,11},{19,20},{21... | collective-permute-start | bytes 1572872 | tf_op jit(solution)/shard_map/ppermute | solution.py:442
  67.5 12.7 %collective-permute-done.19.refs_1_ = bf16[128,1536]{1,0:T(8,128)(2,1)S(1)} collective-permute-done((bf16[128,1536]{1,0:T(8,128)(2,1)S(1)}, bf16[128,1536]{1,0:T(8,128)(2,1)S(1)}, u32[]{:S(2)}, u32[]{:S(2)}) %collective-permute-start.19) | collective-permute-done | bytes 393248 | tf_op jit(solution)/shard_map/ppermute | solution.py:83
  80.2 0.0 collective-permute-done.20.refs_2_
  80.2 0.9 gradient_sum.1
  81.0 0.3 collective-permute-start.21
  81.3 12.1 %collective-permute-done.21.gram_other = f32[128,128]{1,0:T(8,128)S(1)} collective-permute-done((f32[128,128]{1,0:T(8,128)S(1)}, f32[128,128]{1,0:T(8,128)S(1)}, u32[]{:S(2)}, u32[]{:S(2)}) %collective-permute-start.21) | collective-permute-done | bytes 65568 | tf_op jit(solution)/shard_map/ppermute | solution.py:83
  93.5 3.9 %newton_schulz.1 = (f32[128,384]{1,0:T(8,128)S(1)}, bf16[128,384]{1,0:T(8,128)(2,1)S(1)}, bf16[128,384]{1,0:T(8,128)(2,1)S(1)}, bf16[128,384]{1,0:T(8,128)(2,1)S(1)}) custom-call(f32[128,1536]{1,0:T(8,128)S(1)} %get-tuple-element.66.x, f32[128,128]{1,0:T(8,128)S(1)} %get-tuple-element.67.gram, f32[128,128]{1,0:T(8,128)S(1)} %collective-permute-done.21.gram_other), custom_call_target="tpu_custom_call" | custom-call | flops 301989888 | bytes 1572864 | tf_op jit(solution)/shard_map/newton_schulz/pallas_call | solution.py:418
  97.4 0.6 collective-permute-start.22
  98.1 0.9 collective-permute-done.22.refs_1_
  99.0 0.8 collective-permute-start.24
  99.8 2.7 %collective-permute-done.23.refs_2_ = bf16[128,384]{1,0:T(8,128)(2,1)S(1)} collective-permute-done((bf16[128,384]{1,0:T(8,128)(2,1)S(1)}, bf16[128,384]{1,0:T(8,128)(2,1)S(1)}, u32[]{:S(2)}, u32[]{:S(2)}) %collective-permute-start.23) | collective-permute-done | bytes 98336 | tf_op jit(solution)/shard_map/ppermute | solution.py:83
  102.4 2.3 %collective-permute-done.24.refs_3_ = bf16[128,384]{1,0:T(8,128)(2,1)S(1)} collective-permute-done((bf16[128,384]{1,0:T(8,128)(2,1)S(1)}, bf16[128,384]{1,0:T(8,128)(2,1)S(1)}, u32[]{:S(2)}, u32[]{:S(2)}) %collective-permute-start.24) | collective-permute-done | bytes 98336 | tf_op jit(solution)/shard_map/ppermute | solution.py:83
  104.7 0.9 update_rows.1
  105.6 0.0 collective-permute-done.15.kn
  105.7 1.8 %key_value_sum.1 = (bf16[128,2048]{1,0:T(8,128)(2,1)}, bf16[128,2048]{1,0:T(8,128)(2,1)}) custom-call(s32[1,8]{1,0:T(1,128)S(1)} %copy-done.4, f32[128,2048]{1,0:T(8,128)S(1)} %get-tuple-element.46.dko, f32[128,2048]{1,0:T(8,128)S(1)} %get-tuple-element.47.dvo, bf16[2,128,2048]{2,1,0:T(8,128)(2,1)S(1)} %collective-permute-done.14.mate, ...), custom_call_target="tpu_custom_call" | custom-call | flops 1572864 | bytes 5242880 | tf_op jit(solution)/shard_map/key_value_sum/pallas_call | solution.py:428
  (15 shorter events, 0.1 us)
Async XLA Ops:
  0.6 20.0 %collective-permute-start = (bf16[128,2048]{1,0:T(8,128)(2,1)}, bf16[128,2048]{1,0:T(8,128)(2,1)S(1)}, u32[]{:S(2)}, u32[]{:S(2)}) collective-permute-start(bf16[128,2048]{1,0:T(8,128)(2,1)} %bitcast.25), channel_id=1, source_target_pairs={{0,1},{1,0},{2,3},{3,2},{4,5},{5,4},{6,7},{7,6},{8,9},{9,8},{10,11... | collective-permute-start | bytes 1572872 | tf_op jit(solution)/shard_map/ppermute | solution.py:83
  0.8 10.9 %collective-permute-start.2 = (bf16[128,2048]{1,0:T(8,128)(2,1)}, bf16[128,2048]{1,0:T(8,128)(2,1)S(1)}, u32[]{:S(2)}, u32[]{:S(2)}) collective-permute-start(bf16[128,2048]{1,0:T(8,128)(2,1)} %bitcast.26), channel_id=1, source_target_pairs={{1,2},{3,4},{4,3},{6,5},{9,10},{11,12},{12,11},{14,13},{17,18},{19... | collective-permute-start | bytes 1572872 | tf_op jit(solution)/shard_map/ppermute | solution.py:273
  5.3 15.4 %collective-permute-start.1 = (bf16[128,2048]{1,0:T(8,128)(2,1)}, bf16[128,2048]{1,0:T(8,128)(2,1)S(1)}, u32[]{:S(2)}, u32[]{:S(2)}) collective-permute-start(bf16[128,2048]{1,0:T(8,128)(2,1)} %bitcast.29), channel_id=1, source_target_pairs={{0,1},{1,0},{2,3},{3,2},{4,5},{5,4},{6,7},{7,6},{8,9},{9,8},{10,11... | collective-permute-start | bytes 1572872 | tf_op jit(solution)/shard_map/ppermute | solution.py:83
  5.3 11.9 %collective-permute-start.3 = (bf16[128,2048]{1,0:T(8,128)(2,1)}, bf16[128,2048]{1,0:T(8,128)(2,1)S(1)}, u32[]{:S(2)}, u32[]{:S(2)}) collective-permute-start(bf16[128,2048]{1,0:T(8,128)(2,1)} %bitcast.30), channel_id=1, source_target_pairs={{1,2},{3,4},{4,3},{6,5},{9,10},{11,12},{12,11},{14,13},{17,18},{19... | collective-permute-start | bytes 1572872 | tf_op jit(solution)/shard_map/ppermute | solution.py:274
  8.8 11.8 %copy-start = (bf16[1,1,128,2048]{3,2,1,0:T(8,128)(2,1)S(1)}, bf16[1,1,128,2048]{3,2,1,0:T(8,128)(2,1)}, u32[]{:S(2)}) copy-start(bf16[1,1,128,2048]{3,2,1,0:T(8,128)(2,1)} %param.6) | copy-start | bytes 1572868
  8.9 11.8 %copy-start.1 = (bf16[1,1,128,2048]{3,2,1,0:T(8,128)(2,1)S(1)}, bf16[1,1,128,2048]{3,2,1,0:T(8,128)(2,1)}, u32[]{:S(2)}) copy-start(bf16[1,1,128,2048]{3,2,1,0:T(8,128)(2,1)} %param.7) | copy-start | bytes 1572868
  8.9 11.8 %copy-start.2 = (bf16[1,1,128,2048]{3,2,1,0:T(8,128)(2,1)S(1)}, bf16[1,1,128,2048]{3,2,1,0:T(8,128)(2,1)}, u32[]{:S(2)}) copy-start(bf16[1,1,128,2048]{3,2,1,0:T(8,128)(2,1)} %param.8) | copy-start | bytes 1572868
  8.9 11.8 %copy-start.4 = (s32[1,8]{1,0:T(1,128)S(1)}, s32[1,8]{1,0:T(1,128)}, u32[]{:S(2)}) copy-start(s32[1,8]{1,0:T(1,128)} %near_ref.5) | copy-start | bytes 100
  17.3 13.0 %collective-permute-start.7 = (bf16[128,1536]{1,0:T(8,128)(2,1)S(1)}, bf16[128,1536]{1,0:T(8,128)(2,1)S(1)}, u32[]{:S(2)}, u32[]{:S(2)}) collective-permute-start(bf16[128,1536]{1,0:T(8,128)(2,1)S(1)} %pad_maximum_fusion.1), channel_id=1, source_target_pairs={{0,2},{1,3},{2,0},{3,1},{4,6},{5,7},{6,4},{7,5},{8,10},{9,11},{10,... | collective-permute-start | bytes 1179656 | tf_op jit(solution)/shard_map/ppermute | solution.py:83
  20.6 11.1 %collective-permute-start.8 = (bf16[128,1536]{1,0:T(8,128)(2,1)S(1)}, bf16[128,1536]{1,0:T(8,128)(2,1)S(1)}, u32[]{:S(2)}, u32[]{:S(2)}) collective-permute-start(bf16[128,1536]{1,0:T(8,128)(2,1)S(1)} %get-tuple-element.40), channel_id=1, source_target_pairs={{0,4},{1,5},{2,6},{3,7},{4,0},{5,1},{6,2},{7,3},{8,12},{9,13},{10,... | collective-permute-start | bytes 1179656 | tf_op jit(solution)/shard_map/ppermute | solution.py:83
  23.0 12.2 %collective-permute-start.4 = (bf16[2,512,128]{2,1,0:T(8,128)(2,1)S(1)}, bf16[2,512,128]{2,1,0:T(8,128)(2,1)S(1)}, u32[]{:S(2)}, u32[]{:S(2)}) collective-permute-start(bf16[2,512,128]{2,1,0:T(8,128)(2,1)S(1)} %get-tuple-element.60.refs_0_), channel_id=1, source_target_pairs={{0,2},{1,3},{2,0},{3,1},{4,6},{5,7},{6,4},{7,5},{8,10},{9,11},{10,... | collective-permute-start | bytes 786440 | tf_op jit(solution)/shard_map/ppermute | solution.py:83
  24.0 13.4 %collective-permute-start.5 = (bf16[2,512,128]{2,1,0:T(8,128)(2,1)S(1)}, bf16[2,512,128]{2,1,0:T(8,128)(2,1)S(1)}, u32[]{:S(2)}, u32[]{:S(2)}) collective-permute-start(bf16[2,512,128]{2,1,0:T(8,128)(2,1)S(1)} %get-tuple-element.76), channel_id=1, source_target_pairs={{0,4},{1,5},{2,6},{3,7},{4,0},{5,1},{6,2},{7,3},{8,12},{9,13},{10,... | collective-permute-start | bytes 786440 | tf_op jit(solution)/shard_map/ppermute | solution.py:83
  31.8 9.8 %collective-permute-start.10 = (bf16[1,128,768]{2,1,0:T(8,128)(2,1)S(1)}, bf16[1,128,768]{2,1,0:T(8,128)(2,1)S(1)}, u32[]{:S(2)}, u32[]{:S(2)}) collective-permute-start(bf16[1,128,768]{2,1,0:T(8,128)(2,1)S(1)} %get-tuple-element.81), channel_id=1, source_target_pairs={{0,4},{1,5},{2,6},{3,7},{4,0},{5,1},{6,2},{7,3},{8,12},{9,13},{10,... | collective-permute-start | bytes 589832 | tf_op jit(solution)/shard_map/ppermute | solution.py:83
  31.9 13.8 %collective-permute-start.9 = (bf16[1,128,768]{2,1,0:T(8,128)(2,1)S(1)}, bf16[1,128,768]{2,1,0:T(8,128)(2,1)S(1)}, u32[]{:S(2)}, u32[]{:S(2)}) collective-permute-start(bf16[1,128,768]{2,1,0:T(8,128)(2,1)S(1)} %get-tuple-element.80), channel_id=1, source_target_pairs={{0,4},{1,5},{2,6},{3,7},{4,0},{5,1},{6,2},{7,3},{8,12},{9,13},{10,... | collective-permute-start | bytes 589832 | tf_op jit(solution)/shard_map/ppermute | solution.py:83
  37.4 8.4 %collective-permute-start.6 = (bf16[2,512,128]{2,1,0:T(8,128)(2,1)S(1)}, bf16[2,512,128]{2,1,0:T(8,128)(2,1)S(1)}, u32[]{:S(2)}, u32[]{:S(2)}) collective-permute-start(bf16[2,512,128]{2,1,0:T(8,128)(2,1)S(1)} %collective-permute-done.5.refs_2_), channel_id=1, source_target_pairs={{0,2},{1,3},{2,0},{3,1},{4,6},{5,7},{6,4},{7,5},{8,10},{9,11},{10,... | collective-permute-start | bytes 786440 | tf_op jit(solution)/shard_map/ppermute | solution.py:83
  46.4 1.8 %collective-permute-start.11 = (bf16[1,128,1536]{2,1,0:T(8,128)(2,1)S(1)}, bf16[1,128,1536]{2,1,0:T(8,128)(2,1)S(1)}, u32[]{:S(2)}, u32[]{:S(2)}) collective-permute-start(bf16[1,128,1536]{2,1,0:T(8,128)(2,1)S(1)} %get-tuple-element.43), channel_id=1, source_target_pairs={{0,1},{1,0},{2,3},{3,2},{4,5},{5,4},{6,7},{7,6},{8,9},{9,8},{10,11... | collective-permute-start | bytes 1179656 | tf_op jit(solution)/shard_map/ppermute | solution.py:83
  48.3 2.3 %copy-start.3 = (bf16[1,1,128,2048]{3,2,1,0:T(8,128)(2,1)S(1)}, bf16[1,1,128,2048]{3,2,1,0:T(8,128)(2,1)}, u32[]{:S(2)}) copy-start(bf16[1,1,128,2048]{3,2,1,0:T(8,128)(2,1)} %param.9) | copy-start | bytes 1572868
  48.9 7.5 %collective-permute-start.12 = (bf16[1,128,1536]{2,1,0:T(8,128)(2,1)S(1)}, bf16[1,128,1536]{2,1,0:T(8,128)(2,1)S(1)}, u32[]{:S(2)}, u32[]{:S(2)}) collective-permute-start(bf16[1,128,1536]{2,1,0:T(8,128)(2,1)S(1)} %get-tuple-element.52), channel_id=1, source_target_pairs={{0,1},{1,0},{2,3},{3,2},{4,5},{5,4},{6,7},{7,6},{8,9},{9,8},{10,11... | collective-permute-start | bytes 1179656 | tf_op jit(solution)/shard_map/ppermute | solution.py:83
  49.2 10.5 %collective-permute-start.13 = (bf16[128,1536]{1,0:T(8,128)(2,1)S(1)}, bf16[128,1536]{1,0:T(8,128)(2,1)S(1)}, u32[]{:S(2)}, u32[]{:S(2)}) collective-permute-start(bf16[128,1536]{1,0:T(8,128)(2,1)S(1)} %block_sum.3), channel_id=1, source_target_pairs={{0,8},{8,0},{16,24},{24,16},{1,9},{9,1},{17,25},{25,17},{2,10},{10... | collective-permute-start | bytes 1179656 | tf_op jit(solution)/shard_map/ppermute | solution.py:83
  55.1 5.9 %collective-permute-start.18 = (bf16[1,128,1536]{2,1,0:T(8,128)(2,1)S(1)}, bf16[1,128,1536]{2,1,0:T(8,128)(2,1)S(1)}, u32[]{:S(2)}, u32[]{:S(2)}) collective-permute-start(bf16[1,128,1536]{2,1,0:T(8,128)(2,1)S(1)} %get-tuple-element.64), channel_id=1, source_target_pairs={{0,1},{1,0},{2,3},{3,2},{4,5},{5,4},{6,7},{7,6},{8,9},{9,8},{10,11... | collective-permute-start | bytes 1179656 | tf_op jit(solution)/shard_map/ppermute | solution.py:83
  56.3 4.8 %collective-permute-start.17 = (bf16[1,128,1536]{2,1,0:T(8,128)(2,1)S(1)}, bf16[1,128,1536]{2,1,0:T(8,128)(2,1)S(1)}, u32[]{:S(2)}, u32[]{:S(2)}) collective-permute-start(bf16[1,128,1536]{2,1,0:T(8,128)(2,1)S(1)} %get-tuple-element.62), channel_id=1, source_target_pairs={{0,1},{1,0},{2,3},{3,2},{4,5},{5,4},{6,7},{7,6},{8,9},{9,8},{10,11... | collective-permute-start | bytes 1179656 | tf_op jit(solution)/shard_map/ppermute | solution.py:83
  59.9 45.8 %collective-permute-start.14 = (bf16[2,128,2048]{2,1,0:T(8,128)(2,1)S(1)}, bf16[2,128,2048]{2,1,0:T(8,128)(2,1)S(1)}, u32[]{:S(2)}, u32[]{:S(2)}) collective-permute-start(bf16[2,128,2048]{2,1,0:T(8,128)(2,1)S(1)} %get-tuple-element.53), channel_id=1, source_target_pairs={{0,1},{1,0},{2,3},{3,2},{4,5},{5,4},{6,7},{7,6},{8,9},{9,8},{10,11... | collective-permute-start | bytes 3145736 | tf_op jit(solution)/shard_map/ppermute | solution.py:83
  61.1 19.1 %collective-permute-start.19 = (bf16[128,1536]{1,0:T(8,128)(2,1)S(1)}, bf16[128,1536]{1,0:T(8,128)(2,1)S(1)}, u32[]{:S(2)}, u32[]{:S(2)}) collective-permute-start(bf16[128,1536]{1,0:T(8,128)(2,1)S(1)} %block_sum.5), channel_id=1, source_target_pairs={{0,8},{8,0},{16,24},{24,16},{1,9},{9,1},{17,25},{25,17},{2,10},{10... | collective-permute-start | bytes 1179656 | tf_op jit(solution)/shard_map/ppermute | solution.py:83
  62.4 17.7 %collective-permute-start.20 = (bf16[128,1536]{1,0:T(8,128)(2,1)S(1)}, bf16[128,1536]{1,0:T(8,128)(2,1)S(1)}, u32[]{:S(2)}, u32[]{:S(2)}) collective-permute-start(bf16[128,1536]{1,0:T(8,128)(2,1)S(1)} %block_sum.4), channel_id=1, source_target_pairs={{0,16},{8,24},{16,0},{24,8},{1,17},{9,25},{17,1},{25,9},{2,18},{10... | collective-permute-start | bytes 1179656 | tf_op jit(solution)/shard_map/ppermute | solution.py:83
  64.7 40.9 %collective-permute-start.15 = (bf16[128,2048]{1,0:T(8,128)(2,1)S(1)}, bf16[128,2048]{1,0:T(8,128)(2,1)S(1)}, u32[]{:S(2)}, u32[]{:S(2)}) collective-permute-start(bf16[128,2048]{1,0:T(8,128)(2,1)S(1)} %get-tuple-element.55), channel_id=1, source_target_pairs={{3,4},{5,6},{2,1},{4,3},{11,12},{13,14},{10,9},{12,11},{19,20},{21... | collective-permute-start | bytes 1572872 | tf_op jit(solution)/shard_map/ppermute | solution.py:441
  66.0 39.6 %collective-permute-start.16 = (bf16[128,2048]{1,0:T(8,128)(2,1)S(1)}, bf16[128,2048]{1,0:T(8,128)(2,1)S(1)}, u32[]{:S(2)}, u32[]{:S(2)}) collective-permute-start(bf16[128,2048]{1,0:T(8,128)(2,1)S(1)} %get-tuple-element.57), channel_id=1, source_target_pairs={{3,4},{5,6},{2,1},{4,3},{11,12},{13,14},{10,9},{12,11},{19,20},{21... | collective-permute-start | bytes 1572872 | tf_op jit(solution)/shard_map/ppermute | solution.py:442
  81.0 12.4 %collective-permute-start.21 = (f32[128,128]{1,0:T(8,128)S(1)}, f32[128,128]{1,0:T(8,128)S(1)}, u32[]{:S(2)}, u32[]{:S(2)}) collective-permute-start(f32[128,128]{1,0:T(8,128)S(1)} %get-tuple-element.67.gram), channel_id=1, source_target_pairs={{0,2},{1,3},{2,0},{3,1},{4,6},{5,7},{6,4},{7,5},{8,10},{9,11},{10,... | collective-permute-start | bytes 196616 | tf_op jit(solution)/shard_map/ppermute | solution.py:83
  97.4 1.6 %collective-permute-start.22 = (bf16[128,384]{1,0:T(8,128)(2,1)S(1)}, bf16[128,384]{1,0:T(8,128)(2,1)S(1)}, u32[]{:S(2)}, u32[]{:S(2)}) collective-permute-start(bf16[128,384]{1,0:T(8,128)(2,1)S(1)} %get-tuple-element.69), channel_id=1, source_target_pairs={{0,1},{1,0},{2,3},{3,2},{4,5},{5,4},{6,7},{7,6},{8,9},{9,8},{10,11... | collective-permute-start | bytes 294920 | tf_op jit(solution)/shard_map/ppermute | solution.py:83
  98.1 4.4 %collective-permute-start.23 = (bf16[128,384]{1,0:T(8,128)(2,1)S(1)}, bf16[128,384]{1,0:T(8,128)(2,1)S(1)}, u32[]{:S(2)}, u32[]{:S(2)}) collective-permute-start(bf16[128,384]{1,0:T(8,128)(2,1)S(1)} %get-tuple-element.70), channel_id=1, source_target_pairs={{0,4},{1,5},{2,6},{3,7},{4,0},{5,1},{6,2},{7,3},{8,12},{9,13},{10,... | collective-permute-start | bytes 294920 | tf_op jit(solution)/shard_map/ppermute | solution.py:83
  99.0 5.7 %collective-permute-start.24 = (bf16[128,384]{1,0:T(8,128)(2,1)S(1)}, bf16[128,384]{1,0:T(8,128)(2,1)S(1)}, u32[]{:S(2)}, u32[]{:S(2)}) collective-permute-start(bf16[128,384]{1,0:T(8,128)(2,1)S(1)} %get-tuple-element.71), channel_id=1, source_target_pairs={{0,5},{1,4},{2,7},{3,6},{4,1},{5,0},{6,3},{7,2},{8,13},{9,12},{10,... | collective-permute-start | bytes 294920 | tf_op jit(solution)/shard_map/ppermute | solution.py:83

commit v10 on v9

--- a/solution.py
+++ b/solution.py
@@ -320,12 +320,31 @@
 
     through = after(jnp.stack(columns[1:]), attended, *high_columns)
     held = [jnp.stack(columns)]
+    late = []
     for high in range(1, plan.high):
-        rest = jnp.concatenate(
-            [shift(part, "seq", high << (1 + plan.col_bits)) for part in jnp.split(through, 2, 2)], 2
-        )
+        halves = [shift(part, "seq", high << (1 + plan.col_bits)) for part in jnp.split(through, 2, 2)]
+        late.append(halves[0])
+        rest = jnp.concatenate(halves, 2)
         held.append(jnp.concatenate([high_columns[high - 1][None], rest], 0))
     held = jnp.concatenate(held, 0)
+
+    dq, dko, dvo, dkf, dvf, dfar = pl.pallas_call(
+        backward_kernel,
+        out_shape=[
+            struct((tile, width), bf16),
+            struct((tile, width), f32),
+            struct((tile, width), f32),
+            struct((tile, width), bf16),
+            struct((tile, width), bf16),
+            struct((2, tile, width), bf16),
+        ],
+        in_specs=[smem()] + whole(8),
+        out_specs=whole(6),
+        scratch_shapes=[pltpu.VMEM((2, tile, width), bf16)],
+        compiler_params=params(),
+        cost_estimate=cost(28 * tile * tile * width, 30 * tile * width, 2 * tile * tile * head_count),
+        name="attention_backward",
+    )(neighbour, query, key, value, *beside, after(grad, *late))
 
     def product(name, layers, *operands):
         *blocks, for_mate = pl.pallas_call(
@@ -357,27 +376,9 @@
 
     first = [i for i in range(m - 1, 1, -1) if i & 1]
     middle = [i for i in range(m - 1, 1, -1) if not i & 1]
-    blocks = product("product_first", first, *pairs, held)
+    blocks = product("product_first", first, after(pairs[0], dq), *pairs[1:], held)
     going = {i: added(blocks[i], 0, mine_width) for i in first}
     blocks |= product("product_middle", middle, after(pairs[0], *going.values()), *pairs[1:], held)
-
-    dq, dko, dvo, dkf, dvf, dfar = pl.pallas_call(
-        backward_kernel,
-        out_shape=[
-            struct((tile, width), bf16),
-            struct((tile, width), f32),
-            struct((tile, width), f32),
-            struct((tile, width), bf16),
-            struct((tile, width), bf16),
-            struct((2, tile, width), bf16),
-        ],
-        in_specs=[smem()] + whole(8),
-        out_specs=whole(6),
-        scratch_shapes=[pltpu.VMEM((2, tile, width), bf16)],
-        compiler_params=params(),
-        cost_estimate=cost(28 * tile * tile * width, 30 * tile * width, 2 * tile * tile * head_count),
-        name="attention_backward",
-    )(neighbour, query, key, value, *beside, after(grad, *going.values()))
 
     blocks |= product("product_near", [1], after(pairs[0], dq), *pairs[1:], held)
     blocks |= product("product_own", [0], after(pairs[0], dq), *pairs[1:], held)
@@ -399,6 +400,26 @@
     own = blocks[0][0][0]
     came = [blocks[0][1], (near, None, 0)] + extra[0]
 
+    far = [
+        shift(after(dfar, dq), "seq", 1),
+        lax.ppermute(after(dkf, dq), "seq", gives),
+        lax.ppermute(after(dvf, dq), "seq", gives),
+    ]
+    dk, dv = pl.pallas_call(
+        combine_kernel,
+        out_shape=[struct((tile, width), bf16)] * 2,
+        in_specs=[smem()] + whole(5),
+        out_specs=whole(2),
+        compiler_params=params(),
+        cost_estimate=cost(6 * tile * width, 20 * tile * width),
+        name="key_value_sum",
+    )(
+        neighbour,
+        dko,
+        dvo,
+        *far,
+    )
+
     x, gram = pl.pallas_call(
         functools.partial(gram_kernel, [spot for _, *spot in came]),
         out_shape=[struct((HEAD_DIM, mine_width), f32), struct((HEAD_DIM, HEAD_DIM), f32)],
@@ -423,25 +444,7 @@
         compiler_params=params(),
         cost_estimate=cost(12 * HEAD_DIM * HEAD_DIM * mine_width, 8 * HEAD_DIM * mine_width),
         name="newton_schulz",
-    )(x, gram, gram_other)
-    dkf, dvf, dfar = (after(part, sent[-1]) for part in (dkf, dvf, dfar))
-    dk, dv = pl.pallas_call(
-        combine_kernel,
-        out_shape=[struct((tile, width), bf16)] * 2,
-        in_specs=[smem()] + whole(5),
-        out_specs=whole(2),
-        compiler_params=params(),
-        cost_estimate=cost(6 * tile * width, 20 * tile * width),
-        name="key_value_sum",
-    )(
-        neighbour,
-        dko,
-        dvo,
-        shift(dfar, "seq", 1),
-        lax.ppermute(dkf, "seq", gives),
-        lax.ppermute(dvf, "seq", gives),
-    )
-
+    )(after(x, dk), gram, gram_other)
     pieces = [pieces[0]] + [
         shift(pieces[j], "seq", plan.row_mask(j)) for j in range(1, per)
     ]

time: 108 us -> 98.3 us (0.910)
  waiting for transfers between devices: 61.9 us -> 47.4 us
  starting transfers between devices: 26.5 us -> 31.5 us
    ppermute x21, waiting for transfers between devices: 55 us -> 39.2 us  [shift(): lax.ppermute(value, axis, [(i, i ^ mask) for i in range(lax.axis_size(axi...]
    ppermute x21, starting transfers between devices: 15.8 us -> 20.7 us  [shift(): lax.ppermute(value, axis, [(i, i ^ mask) for i in range(lax.axis_size(axi...]
    ppermute x2, waiting for transfers between devices: 0.01 us -> 1.33 us  [the longest x1 1.32 us: local(): lax.ppermute(after(dvf, dq), 'seq', gives)]
  transfers between devices with their start and end apart: 25 -> 25, of which waited for: 15 -> 14; matrix products, arithmetic and copies ran while one was open for 2% -> 2% of each run, Pallas kernels for 12% -> 11%
where the time goes in v10:
time: 98.3 us; the launch traced here: 97.9 us
  waiting for transfers between devices  47.4 us (48%)
  starting transfers between devices  31.5 us (32%)
  Pallas kernels  16.5 us (17%)
  local copies, waits for them, and re-layouts  1.47 us (1%)
    ppermute x21, waiting for transfers between devices, shift(): lax.ppermute(value, axis, [(i, i ^ mask) for i in range(lax.axis_size(axi...  39.2 us
    ppermute x21, starting transfers between devices, shift(): lax.ppermute(value, axis, [(i, i ^ mask) for i in range(lax.axis_size(axi...  20.7 us
    ppermute x1, waiting for transfers between devices, local(): value_next = lax.ppermute(value, 'seq', takes)  5.62 us
    ppermute x1, starting transfers between devices, local(): key_next = lax.ppermute(key, 'seq', takes)  4.49 us
    pallas_call x1, Pallas kernels, local(): pl.pallas_call(backward_kernel, out_shape=[struct((tile, width), bf16), s...  3.98 us
    pallas_call x1, Pallas kernels, local(): pl.pallas_call(functools.partial(update_kernel, plan, factor), out_shape=...  3.95 us
    ppermute x1, starting transfers between devices, local(): value_next = lax.ppermute(value, 'seq', takes)  3.49 us
    pallas_call x4, Pallas kernels, product(): pl.pallas_call(functools.partial(product_kernel, plan, layers), out_shape...  2.38 us
  transfers between devices with their start and end apart: 25, of which 14 were waited for; matrix products, arithmetic and copies ran while one was open for 2% of the time, Pallas kernels for 11%

profile of v10, /device:TPU:1, one launch (start us, length us, event | category | flops | bytes accessed | tf_op | source)
XLA Modules:
  0.0 97.9 jit_solution(13230050534383010862)
XLA Ops:
  0.6 0.1 collective-permute-start
  0.8 4.5 %collective-permute-start.2 = (bf16[128,2048]{1,0:T(8,128)(2,1)}, bf16[128,2048]{1,0:T(8,128)(2,1)S(1)}, u32[]{:S(2)}, u32[]{:S(2)}) collective-permute-start(bf16[128,2048]{1,0:T(8,128)(2,1)} %bitcast.26), channel_id=1, source_target_pairs={{1,2},{3,4},{4,3},{6,5},{9,10},{11,12},{12,11},{14,13},{17,18},{19... | collective-permute-start | bytes 1572872 | tf_op jit(solution)/shard_map/ppermute | solution.py:273
  5.3 0.1 collective-permute-start.1
  5.3 3.5 %collective-permute-start.3 = (bf16[128,2048]{1,0:T(8,128)(2,1)}, bf16[128,2048]{1,0:T(8,128)(2,1)S(1)}, u32[]{:S(2)}, u32[]{:S(2)}) collective-permute-start(bf16[128,2048]{1,0:T(8,128)(2,1)} %bitcast.30), channel_id=1, source_target_pairs={{1,2},{3,4},{4,3},{6,5},{9,10},{11,12},{12,11},{14,13},{17,18},{19... | collective-permute-start | bytes 1572872 | tf_op jit(solution)/shard_map/ppermute | solution.py:274
  8.9 1.4 %dynamic-slice_bitcast_fusion.1 = (bf16[128,768]{1,0:T(8,128)(2,1)S(1)}, bf16[128,768]{1,0:T(8,128)(2,1)S(1)}, bf16[128,768]{1,0:T(8,128)(2,1)S(1)}, bf16[128,768]{1,0:T(8,128)(2,1)S(1)}) fusion(bf16[1,1,128,3072]{3,2,1,0:T(8,128)(2,1)} %param.10, s32[]{:T(128)S(6)} %select_n.14, s32[]{:T(128)S(6)} %select_n.13, s32[]{:T(128)S(6)} %select_n.12, s32[]{:T(128)S(6)} %select_n.15), kind=kLoop, calls=%fused_computation.6 | loop fusion | bytes 1572880 | tf_op jit(solution)/shard_map/dynamic_slice | solution.py:287
  10.3 0.1 fusion
  10.4 1.3 %collective-permute-done.2.kn = bf16[128,2048]{1,0:T(8,128)(2,1)S(1)} collective-permute-done((bf16[128,2048]{1,0:T(8,128)(2,1)}, bf16[128,2048]{1,0:T(8,128)(2,1)S(1)}, u32[]{:S(2)}, u32[]{:S(2)}) %collective-permute-start.2) | collective-permute-done | bytes 524320 | tf_op jit(solution)/shard_map/ppermute | solution.py:273
  11.6 5.6 %collective-permute-done.3.vn = bf16[128,2048]{1,0:T(8,128)(2,1)S(1)} collective-permute-done((bf16[128,2048]{1,0:T(8,128)(2,1)}, bf16[128,2048]{1,0:T(8,128)(2,1)S(1)}, u32[]{:S(2)}, u32[]{:S(2)}) %collective-permute-start.3) | collective-permute-done | bytes 524320 | tf_op jit(solution)/shard_map/ppermute | solution.py:274
  17.3 3.4 %collective-permute-start.4 = (bf16[128,1536]{1,0:T(8,128)(2,1)S(1)}, bf16[128,1536]{1,0:T(8,128)(2,1)S(1)}, u32[]{:S(2)}, u32[]{:S(2)}) collective-permute-start(bf16[128,1536]{1,0:T(8,128)(2,1)S(1)} %pad_maximum_fusion), channel_id=1, source_target_pairs={{0,2},{1,3},{2,0},{3,1},{4,6},{5,7},{6,4},{7,5},{8,10},{9,11},{10,... | collective-permute-start | bytes 1179656 | tf_op jit(solution)/shard_map/ppermute | solution.py:83
  20.6 0.0 collective-permute-start.5
  20.6 0.0 collective-permute-done.km
  20.7 2.3 %attention_forward.1 = bf16[2,2,512,128]{3,2,1,0:T(8,128)(2,1)S(1)} custom-call(s32[1,8]{1,0:T(1,128)S(1)} %copy-done.4, bf16[128,2048]{1,0:T(8,128)(2,1)S(1)} %bitcast.23, bf16[128,2048]{1,0:T(8,128)(2,1)S(1)} %bitcast.27, bf16[128,2048]{1,0:T(8,128)(2,1)S(1)} %bitcast.31, bf16[128,2048]{1,0:T(8,128)(2,1)S(1)} %collective-permute-done.km, ...), custom_call_target="tpu_custom_call" | custom-call | flops 268435456 | bytes 4194304 | tf_op jit(solution)/shard_map/attention_forward/pallas_call | solution.py:303
  23.0 0.0 copy-start.3
  23.0 0.9 collective-permute-start.10
  24.0 0.7 collective-permute-start.11
  24.6 5.6 %collective-permute-done.4 = bf16[128,1536]{1,0:T(8,128)(2,1)S(1)} collective-permute-done((bf16[128,1536]{1,0:T(8,128)(2,1)S(1)}, bf16[128,1536]{1,0:T(8,128)(2,1)S(1)}, u32[]{:S(2)}, u32[]{:S(2)}) %collective-permute-start.4) | collective-permute-done | bytes 393248 | tf_op jit(solution)/shard_map/ppermute | solution.py:83
  30.3 1.5 %collective-permute-done.5 = bf16[128,1536]{1,0:T(8,128)(2,1)S(1)} collective-permute-done((bf16[128,1536]{1,0:T(8,128)(2,1)S(1)}, bf16[128,1536]{1,0:T(8,128)(2,1)S(1)}, u32[]{:S(2)}, u32[]{:S(2)}) %collective-permute-start.5) | collective-permute-done | bytes 393248 | tf_op jit(solution)/shard_map/ppermute | solution.py:83
  31.8 0.1 collective-permute-start.6
  31.9 1.5 %collective-permute-start.13 = (bf16[1,128,768]{2,1,0:T(8,128)(2,1)S(1)}, bf16[1,128,768]{2,1,0:T(8,128)(2,1)S(1)}, u32[]{:S(2)}, u32[]{:S(2)}) collective-permute-start(bf16[1,128,768]{2,1,0:T(8,128)(2,1)S(1)} %get-tuple-element.82), channel_id=1, source_target_pairs={{0,4},{1,5},{2,6},{3,7},{4,0},{5,1},{6,2},{7,3},{8,12},{9,13},{10,... | collective-permute-start | bytes 589832 | tf_op jit(solution)/shard_map/ppermute | solution.py:83
  33.3 1.9 %collective-permute-done.10.refs_1_ = bf16[2,512,128]{2,1,0:T(8,128)(2,1)S(1)} collective-permute-done((bf16[2,512,128]{2,1,0:T(8,128)(2,1)S(1)}, bf16[2,512,128]{2,1,0:T(8,128)(2,1)S(1)}, u32[]{:S(2)}, u32[]{:S(2)}) %collective-permute-start.10) | collective-permute-done | bytes 262176 | tf_op jit(solution)/shard_map/ppermute | solution.py:83
  35.2 2.2 %collective-permute-done.11.refs_2_ = bf16[2,512,128]{2,1,0:T(8,128)(2,1)S(1)} collective-permute-done((bf16[2,512,128]{2,1,0:T(8,128)(2,1)S(1)}, bf16[2,512,128]{2,1,0:T(8,128)(2,1)S(1)}, u32[]{:S(2)}, u32[]{:S(2)}) %collective-permute-start.11) | collective-permute-done | bytes 262176 | tf_op jit(solution)/shard_map/ppermute | solution.py:83
  37.4 4.2 %collective-permute-done.6 = bf16[1,128,768]{2,1,0:T(8,128)(2,1)S(1)} collective-permute-done((bf16[1,128,768]{2,1,0:T(8,128)(2,1)S(1)}, bf16[1,128,768]{2,1,0:T(8,128)(2,1)S(1)}, u32[]{:S(2)}, u32[]{:S(2)}) %collective-permute-start.6) | collective-permute-done | bytes 196640 | tf_op jit(solution)/shard_map/ppermute | solution.py:83
  41.6 4.0 %attention_backward.1 = (bf16[128,2048]{1,0:T(8,128)(2,1)}, f32[128,2048]{1,0:T(8,128)S(1)}, f32[128,2048]{1,0:T(8,128)S(1)}, bf16[128,2048]{1,0:T(8,128)(2,1)S(...) custom-call(s32[1,8]{1,0:T(1,128)S(1)} %copy-done.4, bf16[128,2048]{1,0:T(8,128)(2,1)S(1)} %bitcast.24, ...), custom_call_target="tpu_custom_call" | custom-call | flops 939524096 | bytes 7864320 | tf_op jit(solution)/shard_map/attention_backward/pallas_call | solution.py:331
  45.6 0.1 collective-permute-done.13
  45.7 0.1 maximum_maximum_fusion.refs_4_
  45.8 0.0 collective-permute-done.12.refs_3_
  45.8 0.6 product_first.1
  46.4 0.4 collective-permute-start.16
  46.8 0.2 collective-permute-start.7
  47.0 0.6 product_near.1
  47.6 0.4 collective-permute-start.15
  47.9 0.3 collective-permute-done.16.refs_1_
  48.2 0.1 block_sum.4
  48.3 1.4 %collective-permute-start.18 = (bf16[128,1536]{1,0:T(8,128)(2,1)S(1)}, bf16[128,1536]{1,0:T(8,128)(2,1)S(1)}, u32[]{:S(2)}, u32[]{:S(2)}) collective-permute-start(bf16[128,1536]{1,0:T(8,128)(2,1)S(1)} %block_sum.4), channel_id=1, source_target_pairs={{0,8},{8,0},{16,24},{24,16},{1,9},{9,1},{17,25},{25,17},{2,10},{10... | collective-permute-start | bytes 1179656 | tf_op jit(solution)/shard_map/ppermute | solution.py:83
  49.6 0.6 product_middle.1
  50.2 0.6 collective-permute-start.17
  50.9 0.6 product_own.1
  51.5 0.1 collective-permute-start.14
  51.6 1.3 %collective-permute-start.8 = (bf16[128,2048]{1,0:T(8,128)(2,1)S(1)}, bf16[128,2048]{1,0:T(8,128)(2,1)S(1)}, u32[]{:S(2)}, u32[]{:S(2)}) collective-permute-start(bf16[128,2048]{1,0:T(8,128)(2,1)S(1)} %get-tuple-element.49), channel_id=1, source_target_pairs={{3,4},{5,6},{2,1},{4,3},{11,12},{13,14},{10,9},{12,11},{19,20},{21... | collective-permute-start | bytes 1572872 | tf_op jit(solution)/shard_map/ppermute | solution.py:405
  52.9 0.0 collective-permute-done.17.refs_1_
  52.9 1.5 %collective-permute-start.9 = (bf16[128,2048]{1,0:T(8,128)(2,1)S(1)}, bf16[128,2048]{1,0:T(8,128)(2,1)S(1)}, u32[]{:S(2)}, u32[]{:S(2)}) collective-permute-start(bf16[128,2048]{1,0:T(8,128)(2,1)S(1)} %get-tuple-element.51), channel_id=1, source_target_pairs={{3,4},{5,6},{2,1},{4,3},{11,12},{13,14},{10,9},{12,11},{19,20},{21... | collective-permute-start | bytes 1572872 | tf_op jit(solution)/shard_map/ppermute | solution.py:406
  54.4 0.1 block_sum.3
  54.5 4.3 %collective-permute-done.18.refs_2_ = bf16[128,1536]{1,0:T(8,128)(2,1)S(1)} collective-permute-done((bf16[128,1536]{1,0:T(8,128)(2,1)S(1)}, bf16[128,1536]{1,0:T(8,128)(2,1)S(1)}, u32[]{:S(2)}, u32[]{:S(2)}) %collective-permute-start.18) | collective-permute-done | bytes 393248 | tf_op jit(solution)/shard_map/ppermute | solution.py:83
  58.8 0.1 block_sum.5
  58.9 0.0 collective-permute-done.14.refs_0_
  58.9 1.4 %collective-permute-start.19 = (bf16[128,1536]{1,0:T(8,128)(2,1)S(1)}, bf16[128,1536]{1,0:T(8,128)(2,1)S(1)}, u32[]{:S(2)}, u32[]{:S(2)}) collective-permute-start(bf16[128,1536]{1,0:T(8,128)(2,1)S(1)} %block_sum.3), channel_id=1, source_target_pairs={{0,8},{8,0},{16,24},{24,16},{1,9},{9,1},{17,25},{25,17},{2,10},{10... | collective-permute-start | bytes 1179656 | tf_op jit(solution)/shard_map/ppermute | solution.py:83
  60.3 2.3 %collective-permute-start.20 = (bf16[128,1536]{1,0:T(8,128)(2,1)S(1)}, bf16[128,1536]{1,0:T(8,128)(2,1)S(1)}, u32[]{:S(2)}, u32[]{:S(2)}) collective-permute-start(bf16[128,1536]{1,0:T(8,128)(2,1)S(1)} %block_sum.5), channel_id=1, source_target_pairs={{0,16},{8,24},{16,0},{24,8},{1,17},{9,25},{17,1},{25,9},{2,18},{10... | collective-permute-start | bytes 1179656 | tf_op jit(solution)/shard_map/ppermute | solution.py:83
  62.6 14.2 %collective-permute-done.19.refs_1_ = bf16[128,1536]{1,0:T(8,128)(2,1)S(1)} collective-permute-done((bf16[128,1536]{1,0:T(8,128)(2,1)S(1)}, bf16[128,1536]{1,0:T(8,128)(2,1)S(1)}, u32[]{:S(2)}, u32[]{:S(2)}) %collective-permute-start.19) | collective-permute-done | bytes 393248 | tf_op jit(solution)/shard_map/ppermute | solution.py:83
  76.8 0.0 collective-permute-done.20.refs_2_
  76.8 0.8 gradient_sum.1
  77.6 0.3 collective-permute-start.21
  77.9 0.0 collective-permute-done.8.kn
  77.9 1.3 %collective-permute-done.9.vn = bf16[128,2048]{1,0:T(8,128)(2,1)S(1)} collective-permute-done((bf16[128,2048]{1,0:T(8,128)(2,1)S(1)}, bf16[128,2048]{1,0:T(8,128)(2,1)S(1)}, u32[]{:S(2)}, u32[]{:S(2)}) %collective-permute-start.9) | collective-permute-done | bytes 524320 | tf_op jit(solution)/shard_map/ppermute | solution.py:406
  79.2 0.0 collective-permute-done.7.mate
  79.2 1.8 %key_value_sum.1 = (bf16[128,2048]{1,0:T(8,128)(2,1)}, bf16[128,2048]{1,0:T(8,128)(2,1)}) custom-call(s32[1,8]{1,0:T(1,128)S(1)} %copy-done.4, f32[128,2048]{1,0:T(8,128)S(1)} %get-tuple-element.44.dko, f32[128,2048]{1,0:T(8,128)S(1)} %get-tuple-element.45.dvo, bf16[2,128,2048]{2,1,0:T(8,128)(2,1)S(1)} %collective-permute-done.7.mate, ...), custom_call_target="tpu_custom_call" | custom-call | flops 1572864 | bytes 5242880 | tf_op jit(solution)/shard_map/key_value_sum/pallas_call | solution.py:408
  81.0 0.0 collective-permute-done.21.gram_other
  81.0 4.0 %newton_schulz.1 = (f32[128,384]{1,0:T(8,128)S(1)}, bf16[128,384]{1,0:T(8,128)(2,1)S(1)}, bf16[128,384]{1,0:T(8,128)(2,1)S(1)}, bf16[128,384]{1,0:T(8,128)(2,1)S(1)}) custom-call(f32[128,1536]{1,0:T(8,128)S(1)} %get-tuple-element.68.x, f32[128,128]{1,0:T(8,128)S(1)} %get-tuple-element.69.gram, f32[128,128]{1,0:T(8,128)S(1)} %collective-permute-done.21.gram_other), custom_call_target="tpu_custom_call" | custom-call | flops 301989888 | bytes 1572864 | tf_op jit(solution)/shard_map/newton_schulz/pallas_call | solution.py:439
  85.0 5.4 %collective-permute-start.22 = (bf16[128,384]{1,0:T(8,128)(2,1)S(1)}, bf16[128,384]{1,0:T(8,128)(2,1)S(1)}, u32[]{:S(2)}, u32[]{:S(2)}) collective-permute-start(bf16[128,384]{1,0:T(8,128)(2,1)S(1)} %get-tuple-element.71), channel_id=1, source_target_pairs={{0,1},{1,0},{2,3},{3,2},{4,5},{5,4},{6,7},{7,6},{8,9},{9,8},{10,11... | collective-permute-start | bytes 294920 | tf_op jit(solution)/shard_map/ppermute | solution.py:83
  90.3 0.4 collective-permute-start.23
  90.8 1.3 %collective-permute-start.24 = (bf16[128,384]{1,0:T(8,128)(2,1)S(1)}, bf16[128,384]{1,0:T(8,128)(2,1)S(1)}, u32[]{:S(2)}, u32[]{:S(2)}) collective-permute-start(bf16[128,384]{1,0:T(8,128)(2,1)S(1)} %get-tuple-element.73), channel_id=1, source_target_pairs={{0,5},{1,4},{2,7},{3,6},{4,1},{5,0},{6,3},{7,2},{8,13},{9,12},{10,... | collective-permute-start | bytes 294920 | tf_op jit(solution)/shard_map/ppermute | solution.py:83
  92.1 0.0 collective-permute-done.22.refs_1_
  92.1 2.7 %collective-permute-done.23.refs_2_ = bf16[128,384]{1,0:T(8,128)(2,1)S(1)} collective-permute-done((bf16[128,384]{1,0:T(8,128)(2,1)S(1)}, bf16[128,384]{1,0:T(8,128)(2,1)S(1)}, u32[]{:S(2)}, u32[]{:S(2)}) %collective-permute-start.23) | collective-permute-done | bytes 98336 | tf_op jit(solution)/shard_map/ppermute | solution.py:83
  94.7 2.3 %collective-permute-done.24.refs_3_ = bf16[128,384]{1,0:T(8,128)(2,1)S(1)} collective-permute-done((bf16[128,384]{1,0:T(8,128)(2,1)S(1)}, bf16[128,384]{1,0:T(8,128)(2,1)S(1)}, u32[]{:S(2)}, u32[]{:S(2)}) %collective-permute-start.24) | collective-permute-done | bytes 98336 | tf_op jit(solution)/shard_map/ppermute | solution.py:83
  97.0 0.9 update_rows.1
  (15 shorter events, 0.1 us)
Async XLA Ops:
  0.6 20.0 %collective-permute-start = (bf16[128,2048]{1,0:T(8,128)(2,1)}, bf16[128,2048]{1,0:T(8,128)(2,1)S(1)}, u32[]{:S(2)}, u32[]{:S(2)}) collective-permute-start(bf16[128,2048]{1,0:T(8,128)(2,1)} %bitcast.25), channel_id=1, source_target_pairs={{0,1},{1,0},{2,3},{3,2},{4,5},{5,4},{6,7},{7,6},{8,9},{9,8},{10,11... | collective-permute-start | bytes 1572872 | tf_op jit(solution)/shard_map/ppermute | solution.py:83
  0.8 10.9 %collective-permute-start.2 = (bf16[128,2048]{1,0:T(8,128)(2,1)}, bf16[128,2048]{1,0:T(8,128)(2,1)S(1)}, u32[]{:S(2)}, u32[]{:S(2)}) collective-permute-start(bf16[128,2048]{1,0:T(8,128)(2,1)} %bitcast.26), channel_id=1, source_target_pairs={{1,2},{3,4},{4,3},{6,5},{9,10},{11,12},{12,11},{14,13},{17,18},{19... | collective-permute-start | bytes 1572872 | tf_op jit(solution)/shard_map/ppermute | solution.py:273
  5.3 15.4 %collective-permute-start.1 = (bf16[128,2048]{1,0:T(8,128)(2,1)}, bf16[128,2048]{1,0:T(8,128)(2,1)S(1)}, u32[]{:S(2)}, u32[]{:S(2)}) collective-permute-start(bf16[128,2048]{1,0:T(8,128)(2,1)} %bitcast.29), channel_id=1, source_target_pairs={{0,1},{1,0},{2,3},{3,2},{4,5},{5,4},{6,7},{7,6},{8,9},{9,8},{10,11... | collective-permute-start | bytes 1572872 | tf_op jit(solution)/shard_map/ppermute | solution.py:83
  5.3 11.9 %collective-permute-start.3 = (bf16[128,2048]{1,0:T(8,128)(2,1)}, bf16[128,2048]{1,0:T(8,128)(2,1)S(1)}, u32[]{:S(2)}, u32[]{:S(2)}) collective-permute-start(bf16[128,2048]{1,0:T(8,128)(2,1)} %bitcast.30), channel_id=1, source_target_pairs={{1,2},{3,4},{4,3},{6,5},{9,10},{11,12},{12,11},{14,13},{17,18},{19... | collective-permute-start | bytes 1572872 | tf_op jit(solution)/shard_map/ppermute | solution.py:274
  8.8 11.8 %copy-start = (bf16[1,1,128,2048]{3,2,1,0:T(8,128)(2,1)S(1)}, bf16[1,1,128,2048]{3,2,1,0:T(8,128)(2,1)}, u32[]{:S(2)}) copy-start(bf16[1,1,128,2048]{3,2,1,0:T(8,128)(2,1)} %param.6) | copy-start | bytes 1572868
  8.9 11.8 %copy-start.1 = (bf16[1,1,128,2048]{3,2,1,0:T(8,128)(2,1)S(1)}, bf16[1,1,128,2048]{3,2,1,0:T(8,128)(2,1)}, u32[]{:S(2)}) copy-start(bf16[1,1,128,2048]{3,2,1,0:T(8,128)(2,1)} %param.7) | copy-start | bytes 1572868
  8.9 11.8 %copy-start.2 = (bf16[1,1,128,2048]{3,2,1,0:T(8,128)(2,1)S(1)}, bf16[1,1,128,2048]{3,2,1,0:T(8,128)(2,1)}, u32[]{:S(2)}) copy-start(bf16[1,1,128,2048]{3,2,1,0:T(8,128)(2,1)} %param.8) | copy-start | bytes 1572868
  8.9 11.8 %copy-start.4 = (s32[1,8]{1,0:T(1,128)S(1)}, s32[1,8]{1,0:T(1,128)}, u32[]{:S(2)}) copy-start(s32[1,8]{1,0:T(1,128)} %near_ref.5) | copy-start | bytes 100
  17.3 13.0 %collective-permute-start.4 = (bf16[128,1536]{1,0:T(8,128)(2,1)S(1)}, bf16[128,1536]{1,0:T(8,128)(2,1)S(1)}, u32[]{:S(2)}, u32[]{:S(2)}) collective-permute-start(bf16[128,1536]{1,0:T(8,128)(2,1)S(1)} %pad_maximum_fusion), channel_id=1, source_target_pairs={{0,2},{1,3},{2,0},{3,1},{4,6},{5,7},{6,4},{7,5},{8,10},{9,11},{10,... | collective-permute-start | bytes 1179656 | tf_op jit(solution)/shard_map/ppermute | solution.py:83
  20.6 11.1 %collective-permute-start.5 = (bf16[128,1536]{1,0:T(8,128)(2,1)S(1)}, bf16[128,1536]{1,0:T(8,128)(2,1)S(1)}, u32[]{:S(2)}, u32[]{:S(2)}) collective-permute-start(bf16[128,1536]{1,0:T(8,128)(2,1)S(1)} %get-tuple-element.40), channel_id=1, source_target_pairs={{0,4},{1,5},{2,6},{3,7},{4,0},{5,1},{6,2},{7,3},{8,12},{9,13},{10,... | collective-permute-start | bytes 1179656 | tf_op jit(solution)/shard_map/ppermute | solution.py:83
  23.0 18.6 %copy-start.3 = (bf16[1,1,128,2048]{3,2,1,0:T(8,128)(2,1)S(1)}, bf16[1,1,128,2048]{3,2,1,0:T(8,128)(2,1)}, u32[]{:S(2)}) copy-start(bf16[1,1,128,2048]{3,2,1,0:T(8,128)(2,1)} %param.9) | copy-start | bytes 1572868
  23.0 12.2 %collective-permute-start.10 = (bf16[2,512,128]{2,1,0:T(8,128)(2,1)S(1)}, bf16[2,512,128]{2,1,0:T(8,128)(2,1)S(1)}, u32[]{:S(2)}, u32[]{:S(2)}) collective-permute-start(bf16[2,512,128]{2,1,0:T(8,128)(2,1)S(1)} %get-tuple-element.62.refs_0_), channel_id=1, source_target_pairs={{0,2},{1,3},{2,0},{3,1},{4,6},{5,7},{6,4},{7,5},{8,10},{9,11},{10,... | collective-permute-start | bytes 786440 | tf_op jit(solution)/shard_map/ppermute | solution.py:83
  24.0 13.4 %collective-permute-start.11 = (bf16[2,512,128]{2,1,0:T(8,128)(2,1)S(1)}, bf16[2,512,128]{2,1,0:T(8,128)(2,1)S(1)}, u32[]{:S(2)}, u32[]{:S(2)}) collective-permute-start(bf16[2,512,128]{2,1,0:T(8,128)(2,1)S(1)} %get-tuple-element.78), channel_id=1, source_target_pairs={{0,4},{1,5},{2,6},{3,7},{4,0},{5,1},{6,2},{7,3},{8,12},{9,13},{10,... | collective-permute-start | bytes 786440 | tf_op jit(solution)/shard_map/ppermute | solution.py:83
  31.8 9.8 %collective-permute-start.6 = (bf16[1,128,768]{2,1,0:T(8,128)(2,1)S(1)}, bf16[1,128,768]{2,1,0:T(8,128)(2,1)S(1)}, u32[]{:S(2)}, u32[]{:S(2)}) collective-permute-start(bf16[1,128,768]{2,1,0:T(8,128)(2,1)S(1)} %get-tuple-element.83), channel_id=1, source_target_pairs={{0,4},{1,5},{2,6},{3,7},{4,0},{5,1},{6,2},{7,3},{8,12},{9,13},{10,... | collective-permute-start | bytes 589832 | tf_op jit(solution)/shard_map/ppermute | solution.py:83
  31.9 13.8 %collective-permute-start.13 = (bf16[1,128,768]{2,1,0:T(8,128)(2,1)S(1)}, bf16[1,128,768]{2,1,0:T(8,128)(2,1)S(1)}, u32[]{:S(2)}, u32[]{:S(2)}) collective-permute-start(bf16[1,128,768]{2,1,0:T(8,128)(2,1)S(1)} %get-tuple-element.82), channel_id=1, source_target_pairs={{0,4},{1,5},{2,6},{3,7},{4,0},{5,1},{6,2},{7,3},{8,12},{9,13},{10,... | collective-permute-start | bytes 589832 | tf_op jit(solution)/shard_map/ppermute | solution.py:83
  37.4 8.4 %collective-permute-start.12 = (bf16[2,512,128]{2,1,0:T(8,128)(2,1)S(1)}, bf16[2,512,128]{2,1,0:T(8,128)(2,1)S(1)}, u32[]{:S(2)}, u32[]{:S(2)}) collective-permute-start(bf16[2,512,128]{2,1,0:T(8,128)(2,1)S(1)} %collective-permute-done.11.refs_2_), channel_id=1, source_target_pairs={{0,2},{1,3},{2,0},{3,1},{4,6},{5,7},{6,4},{7,5},{8,10},{9,11},{10,... | collective-permute-start | bytes 786440 | tf_op jit(solution)/shard_map/ppermute | solution.py:83
  46.4 1.8 %collective-permute-start.16 = (bf16[1,128,1536]{2,1,0:T(8,128)(2,1)S(1)}, bf16[1,128,1536]{2,1,0:T(8,128)(2,1)S(1)}, u32[]{:S(2)}, u32[]{:S(2)}) collective-permute-start(bf16[1,128,1536]{2,1,0:T(8,128)(2,1)S(1)} %get-tuple-element.61), channel_id=1, source_target_pairs={{0,1},{1,0},{2,3},{3,2},{4,5},{5,4},{6,7},{7,6},{8,9},{9,8},{10,11... | collective-permute-start | bytes 1179656 | tf_op jit(solution)/shard_map/ppermute | solution.py:83
  46.8 32.4 %collective-permute-start.7 = (bf16[2,128,2048]{2,1,0:T(8,128)(2,1)S(1)}, bf16[2,128,2048]{2,1,0:T(8,128)(2,1)S(1)}, u32[]{:S(2)}, u32[]{:S(2)}) collective-permute-start(bf16[2,128,2048]{2,1,0:T(8,128)(2,1)S(1)} %get-tuple-element.47), channel_id=1, source_target_pairs={{0,1},{1,0},{2,3},{3,2},{4,5},{5,4},{6,7},{7,6},{8,9},{9,8},{10,11... | collective-permute-start | bytes 3145736 | tf_op jit(solution)/shard_map/ppermute | solution.py:83
  47.6 4.0 %collective-permute-start.15 = (bf16[1,128,1536]{2,1,0:T(8,128)(2,1)S(1)}, bf16[1,128,1536]{2,1,0:T(8,128)(2,1)S(1)}, u32[]{:S(2)}, u32[]{:S(2)}) collective-permute-start(bf16[1,128,1536]{2,1,0:T(8,128)(2,1)S(1)} %get-tuple-element.59), channel_id=1, source_target_pairs={{0,1},{1,0},{2,3},{3,2},{4,5},{5,4},{6,7},{7,6},{8,9},{9,8},{10,11... | collective-permute-start | bytes 1179656 | tf_op jit(solution)/shard_map/ppermute | solution.py:83
  48.3 10.5 %collective-permute-start.18 = (bf16[128,1536]{1,0:T(8,128)(2,1)S(1)}, bf16[128,1536]{1,0:T(8,128)(2,1)S(1)}, u32[]{:S(2)}, u32[]{:S(2)}) collective-permute-start(bf16[128,1536]{1,0:T(8,128)(2,1)S(1)} %block_sum.4), channel_id=1, source_target_pairs={{0,8},{8,0},{16,24},{24,16},{1,9},{9,1},{17,25},{25,17},{2,10},{10... | collective-permute-start | bytes 1179656 | tf_op jit(solution)/shard_map/ppermute | solution.py:83
  50.2 2.6 %collective-permute-start.17 = (bf16[1,128,1536]{2,1,0:T(8,128)(2,1)S(1)}, bf16[1,128,1536]{2,1,0:T(8,128)(2,1)S(1)}, u32[]{:S(2)}, u32[]{:S(2)}) collective-permute-start(bf16[1,128,1536]{2,1,0:T(8,128)(2,1)S(1)} %get-tuple-element.65), channel_id=1, source_target_pairs={{0,1},{1,0},{2,3},{3,2},{4,5},{5,4},{6,7},{7,6},{8,9},{9,8},{10,11... | collective-permute-start | bytes 1179656 | tf_op jit(solution)/shard_map/ppermute | solution.py:83
  51.5 7.4 %collective-permute-start.14 = (bf16[1,128,1536]{2,1,0:T(8,128)(2,1)S(1)}, bf16[1,128,1536]{2,1,0:T(8,128)(2,1)S(1)}, u32[]{:S(2)}, u32[]{:S(2)}) collective-permute-start(bf16[1,128,1536]{2,1,0:T(8,128)(2,1)S(1)} %get-tuple-element.57), channel_id=1, source_target_pairs={{0,1},{1,0},{2,3},{3,2},{4,5},{5,4},{6,7},{7,6},{8,9},{9,8},{10,11... | collective-permute-start | bytes 1179656 | tf_op jit(solution)/shard_map/ppermute | solution.py:83
  51.6 26.3 %collective-permute-start.8 = (bf16[128,2048]{1,0:T(8,128)(2,1)S(1)}, bf16[128,2048]{1,0:T(8,128)(2,1)S(1)}, u32[]{:S(2)}, u32[]{:S(2)}) collective-permute-start(bf16[128,2048]{1,0:T(8,128)(2,1)S(1)} %get-tuple-element.49), channel_id=1, source_target_pairs={{3,4},{5,6},{2,1},{4,3},{11,12},{13,14},{10,9},{12,11},{19,20},{21... | collective-permute-start | bytes 1572872 | tf_op jit(solution)/shard_map/ppermute | solution.py:405
  52.9 26.3 %collective-permute-start.9 = (bf16[128,2048]{1,0:T(8,128)(2,1)S(1)}, bf16[128,2048]{1,0:T(8,128)(2,1)S(1)}, u32[]{:S(2)}, u32[]{:S(2)}) collective-permute-start(bf16[128,2048]{1,0:T(8,128)(2,1)S(1)} %get-tuple-element.51), channel_id=1, source_target_pairs={{3,4},{5,6},{2,1},{4,3},{11,12},{13,14},{10,9},{12,11},{19,20},{21... | collective-permute-start | bytes 1572872 | tf_op jit(solution)/shard_map/ppermute | solution.py:406
  58.9 17.9 %collective-permute-start.19 = (bf16[128,1536]{1,0:T(8,128)(2,1)S(1)}, bf16[128,1536]{1,0:T(8,128)(2,1)S(1)}, u32[]{:S(2)}, u32[]{:S(2)}) collective-permute-start(bf16[128,1536]{1,0:T(8,128)(2,1)S(1)} %block_sum.3), channel_id=1, source_target_pairs={{0,8},{8,0},{16,24},{24,16},{1,9},{9,1},{17,25},{25,17},{2,10},{10... | collective-permute-start | bytes 1179656 | tf_op jit(solution)/shard_map/ppermute | solution.py:83
  60.3 16.5 %collective-permute-start.20 = (bf16[128,1536]{1,0:T(8,128)(2,1)S(1)}, bf16[128,1536]{1,0:T(8,128)(2,1)S(1)}, u32[]{:S(2)}, u32[]{:S(2)}) collective-permute-start(bf16[128,1536]{1,0:T(8,128)(2,1)S(1)} %block_sum.5), channel_id=1, source_target_pairs={{0,16},{8,24},{16,0},{24,8},{1,17},{9,25},{17,1},{25,9},{2,18},{10... | collective-permute-start | bytes 1179656 | tf_op jit(solution)/shard_map/ppermute | solution.py:83
  77.6 3.4 %collective-permute-start.21 = (f32[128,128]{1,0:T(8,128)S(1)}, f32[128,128]{1,0:T(8,128)S(1)}, u32[]{:S(2)}, u32[]{:S(2)}) collective-permute-start(f32[128,128]{1,0:T(8,128)S(1)} %get-tuple-element.69.gram), channel_id=1, source_target_pairs={{0,2},{1,3},{2,0},{3,1},{4,6},{5,7},{6,4},{7,5},{8,10},{9,11},{10,... | collective-permute-start | bytes 196616 | tf_op jit(solution)/shard_map/ppermute | solution.py:83
  85.0 7.1 %collective-permute-start.22 = (bf16[128,384]{1,0:T(8,128)(2,1)S(1)}, bf16[128,384]{1,0:T(8,128)(2,1)S(1)}, u32[]{:S(2)}, u32[]{:S(2)}) collective-permute-start(bf16[128,384]{1,0:T(8,128)(2,1)S(1)} %get-tuple-element.71), channel_id=1, source_target_pairs={{0,1},{1,0},{2,3},{3,2},{4,5},{5,4},{6,7},{7,6},{8,9},{9,8},{10,11... | collective-permute-start | bytes 294920 | tf_op jit(solution)/shard_map/ppermute | solution.py:83
  90.3 4.4 %collective-permute-start.23 = (bf16[128,384]{1,0:T(8,128)(2,1)S(1)}, bf16[128,384]{1,0:T(8,128)(2,1)S(1)}, u32[]{:S(2)}, u32[]{:S(2)}) collective-permute-start(bf16[128,384]{1,0:T(8,128)(2,1)S(1)} %get-tuple-element.72), channel_id=1, source_target_pairs={{0,4},{1,5},{2,6},{3,7},{4,0},{5,1},{6,2},{7,3},{8,12},{9,13},{10,... | collective-permute-start | bytes 294920 | tf_op jit(solution)/shard_map/ppermute | solution.py:83
  90.8 6.2 %collective-permute-start.24 = (bf16[128,384]{1,0:T(8,128)(2,1)S(1)}, bf16[128,384]{1,0:T(8,128)(2,1)S(1)}, u32[]{:S(2)}, u32[]{:S(2)}) collective-permute-start(bf16[128,384]{1,0:T(8,128)(2,1)S(1)} %get-tuple-element.73), channel_id=1, source_target_pairs={{0,5},{1,4},{2,7},{3,6},{4,1},{5,0},{6,3},{7,2},{8,13},{9,12},{10,... | collective-permute-start | bytes 294920 | tf_op jit(solution)/shard_map/ppermute | solution.py:83

commit v11 on v10

--- a/solution.py
+++ b/solution.py
@@ -311,14 +311,15 @@
         name="attention_forward",
     )(neighbour, query, key, value, *beside)
 
+    by_high = [attended[0]] + [
+        shift(attended[high], "seq", high << (1 + plan.col_bits)) for high in range(1, plan.high)
+    ]
     pairs = [attended[0]] + [shift(attended[0], "seq", q << 1) for q in range(1, plan.col)]
-    for high in range(1, plan.high):
-        came_high = shift(attended[high], "seq", high << (1 + plan.col_bits))
-        pairs.append(came_high)
+    for came_high in by_high[1:]:
         there = after(came_high, *pairs[1 : plan.col])
-        pairs += [shift(there, "seq", q << 1) for q in range(1, plan.col)]
-
-    through = after(jnp.stack(columns[1:]), attended, *high_columns)
+        pairs += [came_high] + [shift(there, "seq", q << 1) for q in range(1, plan.col)]
+
+    through = lax.optimization_barrier((attended, *high_columns, jnp.stack(columns[1:])))[-1]
     held = [jnp.stack(columns)]
     late = []
     for high in range(1, plan.high):
@@ -396,15 +397,18 @@
                     sent.append(added([(after(block, dq), *where)] + others, 0, mine_width))
                 extra[i ^ bit].append((shift(sent[-1], "dp", bit), None, 0))
         bit *= 2
-    near = shift(after(added(blocks[1], 0, mine_width), sent[-1], blocks[0][1][0]), "dp", 1)
-    own = blocks[0][0][0]
-    came = [blocks[0][1], (near, None, 0)] + extra[0]
-
     far = [
         shift(after(dfar, dq), "seq", 1),
         lax.ppermute(after(dkf, dq), "seq", gives),
         lax.ppermute(after(dvf, dq), "seq", gives),
     ]
+    own = blocks[0][0][0]
+    came = [blocks[0][1]] + extra[0]
+    parts = 1
+    size = mine_width // parts
+    for start in range(0, mine_width, size):
+        near = after(added(blocks[1], start, size), sent[-1], blocks[0][1][0], far[0])
+        came.append((shift(near, "dp", 1), None, start))
     dk, dv = pl.pallas_call(
         combine_kernel,
         out_shape=[struct((tile, width), bf16)] * 2,

time: 98.3 us -> 97 us (0.987)
  waiting for transfers between devices: 47.4 us -> 43 us
  starting transfers between devices: 31.5 us -> 34.4 us
    ppermute x21, waiting for transfers between devices: 39.2 us -> 36.1 us  [shift(): lax.ppermute(value, axis, [(i, i ^ mask) for i in range(lax.axis_size(axi...]
    ppermute x21, starting transfers between devices: 20.7 us -> 23.6 us  [shift(): lax.ppermute(value, axis, [(i, i ^ mask) for i in range(lax.axis_size(axi...]
    ppermute x1, waiting for transfers between devices: 1.32 us -> 0.01 us  [local(): lax.ppermute(after(dvf, dq), 'seq', gives)]
  transfers between devices with their start and end apart: 25 -> 25, of which waited for: 14 -> 12; matrix products, arithmetic and copies ran while one was open for 2% -> 2% of each run, Pallas kernels for 11% -> 12%
where the time goes in v11:
time: 97 us; the launch traced here: 96.5 us
  waiting for transfers between devices  43 us (44%)
  starting transfers between devices  34.4 us (35%)
  Pallas kernels  16.5 us (17%)
  local copies, waits for them, and re-layouts  1.47 us (2%)
    ppermute x21, waiting for transfers between devices, shift(): lax.ppermute(value, axis, [(i, i ^ mask) for i in range(lax.axis_size(axi...  36.1 us
    ppermute x21, starting transfers between devices, shift(): lax.ppermute(value, axis, [(i, i ^ mask) for i in range(lax.axis_size(axi...  23.6 us
    ppermute x1, waiting for transfers between devices, local(): value_next = lax.ppermute(value, 'seq', takes)  5.62 us
    ppermute x1, starting transfers between devices, local(): key_next = lax.ppermute(key, 'seq', takes)  4.49 us
    pallas_call x1, Pallas kernels, local(): pl.pallas_call(backward_kernel, out_shape=[struct((tile, width), bf16), s...  3.98 us
    pallas_call x1, Pallas kernels, local(): pl.pallas_call(functools.partial(update_kernel, plan, factor), out_shape=...  3.97 us
    ppermute x1, starting transfers between devices, local(): value_next = lax.ppermute(value, 'seq', takes)  3.49 us
    pallas_call x4, Pallas kernels, product(): pl.pallas_call(functools.partial(product_kernel, plan, layers), out_shape...  2.39 us
  transfers between devices with their start and end apart: 25, of which 12 were waited for; matrix products, arithmetic and copies ran while one was open for 2% of the time, Pallas kernels for 12%

profile of v11, /device:TPU:1, one launch (start us, length us, event | category | flops | bytes accessed | tf_op | source)
XLA Modules:
  0.0 96.5 jit_solution(755811436388997603)
XLA Ops:
  0.6 0.1 collective-permute-start
  0.8 4.5 %collective-permute-start.2 = (bf16[128,2048]{1,0:T(8,128)(2,1)}, bf16[128,2048]{1,0:T(8,128)(2,1)S(1)}, u32[]{:S(2)}, u32[]{:S(2)}) collective-permute-start(bf16[128,2048]{1,0:T(8,128)(2,1)} %bitcast.26), channel_id=1, source_target_pairs={{1,2},{3,4},{4,3},{6,5},{9,10},{11,12},{12,11},{14,13},{17,18},{19... | collective-permute-start | bytes 1572872 | tf_op jit(solution)/shard_map/ppermute | solution.py:273
  5.3 0.1 collective-permute-start.1
  5.3 3.5 %collective-permute-start.3 = (bf16[128,2048]{1,0:T(8,128)(2,1)}, bf16[128,2048]{1,0:T(8,128)(2,1)S(1)}, u32[]{:S(2)}, u32[]{:S(2)}) collective-permute-start(bf16[128,2048]{1,0:T(8,128)(2,1)} %bitcast.30), channel_id=1, source_target_pairs={{1,2},{3,4},{4,3},{6,5},{9,10},{11,12},{12,11},{14,13},{17,18},{19... | collective-permute-start | bytes 1572872 | tf_op jit(solution)/shard_map/ppermute | solution.py:274
  8.9 1.4 %dynamic-slice_bitcast_fusion.1 = (bf16[128,768]{1,0:T(8,128)(2,1)S(1)}, bf16[128,768]{1,0:T(8,128)(2,1)S(1)}, bf16[128,768]{1,0:T(8,128)(2,1)S(1)}, bf16[128,768]{1,0:T(8,128)(2,1)S(1)}) fusion(bf16[1,1,128,3072]{3,2,1,0:T(8,128)(2,1)} %param.10, s32[]{:T(128)S(6)} %select_n.14, s32[]{:T(128)S(6)} %select_n.13, s32[]{:T(128)S(6)} %select_n.12, s32[]{:T(128)S(6)} %select_n.15), kind=kLoop, calls=%fused_computation.6 | loop fusion | bytes 1572880 | tf_op jit(solution)/shard_map/dynamic_slice | solution.py:287
  10.3 0.1 fusion
  10.4 1.3 %collective-permute-done.2.kn = bf16[128,2048]{1,0:T(8,128)(2,1)S(1)} collective-permute-done((bf16[128,2048]{1,0:T(8,128)(2,1)}, bf16[128,2048]{1,0:T(8,128)(2,1)S(1)}, u32[]{:S(2)}, u32[]{:S(2)}) %collective-permute-start.2) | collective-permute-done | bytes 524320 | tf_op jit(solution)/shard_map/ppermute | solution.py:273
  11.6 5.6 %collective-permute-done.3.vn = bf16[128,2048]{1,0:T(8,128)(2,1)S(1)} collective-permute-done((bf16[128,2048]{1,0:T(8,128)(2,1)}, bf16[128,2048]{1,0:T(8,128)(2,1)S(1)}, u32[]{:S(2)}, u32[]{:S(2)}) %collective-permute-start.3) | collective-permute-done | bytes 524320 | tf_op jit(solution)/shard_map/ppermute | solution.py:274
  17.3 2.8 %collective-permute-start.4 = (bf16[128,1536]{1,0:T(8,128)(2,1)S(1)}, bf16[128,1536]{1,0:T(8,128)(2,1)S(1)}, u32[]{:S(2)}, u32[]{:S(2)}) collective-permute-start(bf16[128,1536]{1,0:T(8,128)(2,1)S(1)} %get-tuple-element.39), channel_id=1, source_target_pairs={{0,4},{1,5},{2,6},{3,7},{4,0},{5,1},{6,2},{7,3},{8,12},{9,13},{10,... | collective-permute-start | bytes 1179656 | tf_op jit(solution)/shard_map/ppermute | solution.py:83
  20.1 0.6 collective-permute-start.5
  20.6 0.0 collective-permute-done.km
  20.6 0.0 collective-permute-done.1.vm
  20.7 2.3 %attention_forward.1 = bf16[2,2,512,128]{3,2,1,0:T(8,128)(2,1)S(1)} custom-call(s32[1,8]{1,0:T(1,128)S(1)} %copy-done.4, bf16[128,2048]{1,0:T(8,128)(2,1)S(1)} %bitcast.23, bf16[128,2048]{1,0:T(8,128)(2,1)S(1)} %bitcast.27, bf16[128,2048]{1,0:T(8,128)(2,1)S(1)} %bitcast.31, bf16[128,2048]{1,0:T(8,128)(2,1)S(1)} %collective-permute-done.km, ...), custom_call_target="tpu_custom_call" | custom-call | flops 268435456 | bytes 4194304 | tf_op jit(solution)/shard_map/attention_forward/pallas_call | solution.py:303
  23.0 0.0 copy-start.3
  23.0 1.0 collective-permute-start.10
  24.0 0.7 collective-permute-start.11
  24.6 4.3 %collective-permute-done.4 = bf16[128,1536]{1,0:T(8,128)(2,1)S(1)} collective-permute-done((bf16[128,1536]{1,0:T(8,128)(2,1)S(1)}, bf16[128,1536]{1,0:T(8,128)(2,1)S(1)}, u32[]{:S(2)}, u32[]{:S(2)}) %collective-permute-start.4) | collective-permute-done | bytes 393248 | tf_op jit(solution)/shard_map/ppermute | solution.py:83
  28.9 0.8 collective-permute-done.5
  29.8 1.6 %collective-permute-start.6 = (bf16[1,128,768]{2,1,0:T(8,128)(2,1)S(1)}, bf16[1,128,768]{2,1,0:T(8,128)(2,1)S(1)}, u32[]{:S(2)}, u32[]{:S(2)}) collective-permute-start(bf16[1,128,768]{2,1,0:T(8,128)(2,1)S(1)} %get-tuple-element.83), channel_id=1, source_target_pairs={{0,4},{1,5},{2,6},{3,7},{4,0},{5,1},{6,2},{7,3},{8,12},{9,13},{10,... | collective-permute-start | bytes 589832 | tf_op jit(solution)/shard_map/ppermute | solution.py:83
  31.4 0.1 collective-permute-start.13
  31.5 3.9 %collective-permute-done.10.refs_1_ = bf16[2,512,128]{2,1,0:T(8,128)(2,1)S(1)} collective-permute-done((bf16[2,512,128]{2,1,0:T(8,128)(2,1)S(1)}, bf16[2,512,128]{2,1,0:T(8,128)(2,1)S(1)}, u32[]{:S(2)}, u32[]{:S(2)}) %collective-permute-start.10) | collective-permute-done | bytes 262176 | tf_op jit(solution)/shard_map/ppermute | solution.py:83
  35.4 1.9 %collective-permute-start.12 = (bf16[2,512,128]{2,1,0:T(8,128)(2,1)S(1)}, bf16[2,512,128]{2,1,0:T(8,128)(2,1)S(1)}, u32[]{:S(2)}, u32[]{:S(2)}) collective-permute-start(bf16[2,512,128]{2,1,0:T(8,128)(2,1)S(1)} %collective-permute-done.11.refs_2_), channel_id=1, source_target_pairs={{0,2},{1,3},{2,0},{3,1},{4,6},{5,7},{6,4},{7,5},{8,10},{9,11},{10,... | collective-permute-start | bytes 786440 | tf_op jit(solution)/shard_map/ppermute | solution.py:83
  37.3 1.3 %collective-permute-done.6 = bf16[1,128,768]{2,1,0:T(8,128)(2,1)S(1)} collective-permute-done((bf16[1,128,768]{2,1,0:T(8,128)(2,1)S(1)}, bf16[1,128,768]{2,1,0:T(8,128)(2,1)S(1)}, u32[]{:S(2)}, u32[]{:S(2)}) %collective-permute-start.6) | collective-permute-done | bytes 196640 | tf_op jit(solution)/shard_map/ppermute | solution.py:83
  38.6 4.0 %attention_backward.1 = (bf16[128,2048]{1,0:T(8,128)(2,1)}, f32[128,2048]{1,0:T(8,128)S(1)}, f32[128,2048]{1,0:T(8,128)S(1)}, bf16[128,2048]{1,0:T(8,128)(2,1)S(...) custom-call(s32[1,8]{1,0:T(1,128)S(1)} %copy-done.4, bf16[128,2048]{1,0:T(8,128)(2,1)S(1)} %bitcast.24, ...), custom_call_target="tpu_custom_call" | custom-call | flops 939524096 | bytes 7864320 | tf_op jit(solution)/shard_map/attention_backward/pallas_call | solution.py:332
  42.6 2.4 %collective-permute-start.7 = (bf16[2,128,2048]{2,1,0:T(8,128)(2,1)S(1)}, bf16[2,128,2048]{2,1,0:T(8,128)(2,1)S(1)}, u32[]{:S(2)}, u32[]{:S(2)}) collective-permute-start(bf16[2,128,2048]{2,1,0:T(8,128)(2,1)S(1)} %get-tuple-element.47), channel_id=1, source_target_pairs={{0,1},{1,0},{2,3},{3,2},{4,5},{5,4},{6,7},{7,6},{8,9},{9,8},{10,11... | collective-permute-start | bytes 3145736 | tf_op jit(solution)/shard_map/ppermute | solution.py:83
  44.9 0.1 maximum_maximum_fusion.refs_4_
  45.1 0.0 collective-permute-done.12.refs_3_
  45.1 0.6 product_first.1
  45.7 0.1 collective-permute-start.15
  45.8 0.6 product_near.1
  46.4 0.6 collective-permute-start.19
  46.9 0.8 collective-permute-done.15.refs_1_
  47.8 0.1 block_sum.3
  47.9 1.4 %collective-permute-start.17 = (bf16[128,1536]{1,0:T(8,128)(2,1)S(1)}, bf16[128,1536]{1,0:T(8,128)(2,1)S(1)}, u32[]{:S(2)}, u32[]{:S(2)}) collective-permute-start(bf16[128,1536]{1,0:T(8,128)(2,1)S(1)} %block_sum.3), channel_id=1, source_target_pairs={{0,8},{8,0},{16,24},{24,16},{1,9},{9,1},{17,25},{25,17},{2,10},{10... | collective-permute-start | bytes 1179656 | tf_op jit(solution)/shard_map/ppermute | solution.py:83
  49.2 0.6 product_middle.1
  49.8 0.7 collective-permute-start.16
  50.5 0.6 product_own.1
  51.1 0.1 collective-permute-start.14
  51.2 0.0 collective-permute-done.19.refs_1_
  51.2 1.3 %collective-permute-start.8 = (bf16[128,2048]{1,0:T(8,128)(2,1)S(1)}, bf16[128,2048]{1,0:T(8,128)(2,1)S(1)}, u32[]{:S(2)}, u32[]{:S(2)}) collective-permute-start(bf16[128,2048]{1,0:T(8,128)(2,1)S(1)} %get-tuple-element.49), channel_id=1, source_target_pairs={{3,4},{5,6},{2,1},{4,3},{11,12},{13,14},{10,9},{12,11},{19,20},{21... | collective-permute-start | bytes 1572872 | tf_op jit(solution)/shard_map/ppermute | solution.py:402
  52.5 0.0 collective-permute-done.16.refs_1_
  52.5 1.5 %collective-permute-start.9 = (bf16[128,2048]{1,0:T(8,128)(2,1)S(1)}, bf16[128,2048]{1,0:T(8,128)(2,1)S(1)}, u32[]{:S(2)}, u32[]{:S(2)}) collective-permute-start(bf16[128,2048]{1,0:T(8,128)(2,1)S(1)} %get-tuple-element.51), channel_id=1, source_target_pairs={{3,4},{5,6},{2,1},{4,3},{11,12},{13,14},{10,9},{12,11},{19,20},{21... | collective-permute-start | bytes 1572872 | tf_op jit(solution)/shard_map/ppermute | solution.py:403
  54.0 0.1 block_sum.5
  54.1 4.1 %collective-permute-done.17.refs_2_ = bf16[128,1536]{1,0:T(8,128)(2,1)S(1)} collective-permute-done((bf16[128,1536]{1,0:T(8,128)(2,1)S(1)}, bf16[128,1536]{1,0:T(8,128)(2,1)S(1)}, u32[]{:S(2)}, u32[]{:S(2)}) %collective-permute-start.17) | collective-permute-done | bytes 393248 | tf_op jit(solution)/shard_map/ppermute | solution.py:83
  58.2 0.1 block_sum.4
  58.4 2.4 %collective-permute-start.18 = (bf16[128,1536]{1,0:T(8,128)(2,1)S(1)}, bf16[128,1536]{1,0:T(8,128)(2,1)S(1)}, u32[]{:S(2)}, u32[]{:S(2)}) collective-permute-start(bf16[128,1536]{1,0:T(8,128)(2,1)S(1)} %block_sum.4), channel_id=1, source_target_pairs={{0,16},{8,24},{16,0},{24,8},{1,17},{9,25},{17,1},{25,9},{2,18},{10... | collective-permute-start | bytes 1179656 | tf_op jit(solution)/shard_map/ppermute | solution.py:83
  60.7 0.0 collective-permute-done.14.refs_0_
  60.7 1.3 %collective-permute-start.20 = (bf16[128,1536]{1,0:T(8,128)(2,1)S(1)}, bf16[128,1536]{1,0:T(8,128)(2,1)S(1)}, u32[]{:S(2)}, u32[]{:S(2)}) collective-permute-start(bf16[128,1536]{1,0:T(8,128)(2,1)S(1)} %block_sum.5), channel_id=1, source_target_pairs={{0,8},{8,0},{16,24},{24,16},{1,9},{9,1},{17,25},{25,17},{2,10},{10... | collective-permute-start | bytes 1179656 | tf_op jit(solution)/shard_map/ppermute | solution.py:83
  62.0 15.7 %collective-permute-done.18.refs_1_ = bf16[128,1536]{1,0:T(8,128)(2,1)S(1)} collective-permute-done((bf16[128,1536]{1,0:T(8,128)(2,1)S(1)}, bf16[128,1536]{1,0:T(8,128)(2,1)S(1)}, u32[]{:S(2)}, u32[]{:S(2)}) %collective-permute-start.18) | collective-permute-done | bytes 393248 | tf_op jit(solution)/shard_map/ppermute | solution.py:83
  77.8 0.0 collective-permute-done.20.refs_2_
  77.8 0.8 gradient_sum.1
  78.6 1.3 %collective-permute-start.21 = (f32[128,128]{1,0:T(8,128)S(1)}, f32[128,128]{1,0:T(8,128)S(1)}, u32[]{:S(2)}, u32[]{:S(2)}) collective-permute-start(f32[128,128]{1,0:T(8,128)S(1)} %get-tuple-element.69.gram), channel_id=1, source_target_pairs={{0,2},{1,3},{2,0},{3,1},{4,6},{5,7},{6,4},{7,5},{8,10},{9,11},{10,... | collective-permute-start | bytes 196616 | tf_op jit(solution)/shard_map/ppermute | solution.py:83
  79.9 0.0 collective-permute-done.8.kn
  79.9 0.0 collective-permute-done.9.vn
  79.9 1.8 %key_value_sum.1 = (bf16[128,2048]{1,0:T(8,128)(2,1)}, bf16[128,2048]{1,0:T(8,128)(2,1)}) custom-call(s32[1,8]{1,0:T(1,128)S(1)} %copy-done.4, f32[128,2048]{1,0:T(8,128)S(1)} %get-tuple-element.44.dko, f32[128,2048]{1,0:T(8,128)S(1)} %get-tuple-element.45.dvo, bf16[2,128,2048]{2,1,0:T(8,128)(2,1)S(1)} %collective-permute-done.7.mate, ...), custom_call_target="tpu_custom_call" | custom-call | flops 1572864 | bytes 5242880 | tf_op jit(solution)/shard_map/key_value_sum/pallas_call | solution.py:412
  81.7 0.1 collective-permute-done.21.gram_other
  81.8 4.0 %newton_schulz.1 = (f32[128,384]{1,0:T(8,128)S(1)}, bf16[128,384]{1,0:T(8,128)(2,1)S(1)}, bf16[128,384]{1,0:T(8,128)(2,1)S(1)}, bf16[128,384]{1,0:T(8,128)(2,1)S(1)}) custom-call(f32[128,1536]{1,0:T(8,128)S(1)} %get-tuple-element.68.x, f32[128,128]{1,0:T(8,128)S(1)} %get-tuple-element.69.gram, f32[128,128]{1,0:T(8,128)S(1)} %collective-permute-done.21.gram_other), custom_call_target="tpu_custom_call" | custom-call | flops 301989888 | bytes 1572864 | tf_op jit(solution)/shard_map/newton_schulz/pallas_call | solution.py:443
  85.7 3.0 %collective-permute-start.22 = (bf16[128,384]{1,0:T(8,128)(2,1)S(1)}, bf16[128,384]{1,0:T(8,128)(2,1)S(1)}, u32[]{:S(2)}, u32[]{:S(2)}) collective-permute-start(bf16[128,384]{1,0:T(8,128)(2,1)S(1)} %get-tuple-element.71), channel_id=1, source_target_pairs={{0,1},{1,0},{2,3},{3,2},{4,5},{5,4},{6,7},{7,6},{8,9},{9,8},{10,11... | collective-permute-start | bytes 294920 | tf_op jit(solution)/shard_map/ppermute | solution.py:83
  88.8 1.6 %collective-permute-start.23 = (bf16[128,384]{1,0:T(8,128)(2,1)S(1)}, bf16[128,384]{1,0:T(8,128)(2,1)S(1)}, u32[]{:S(2)}, u32[]{:S(2)}) collective-permute-start(bf16[128,384]{1,0:T(8,128)(2,1)S(1)} %get-tuple-element.72), channel_id=1, source_target_pairs={{0,4},{1,5},{2,6},{3,7},{4,0},{5,1},{6,2},{7,3},{8,12},{9,13},{10,... | collective-permute-start | bytes 294920 | tf_op jit(solution)/shard_map/ppermute | solution.py:83
  90.4 0.1 collective-permute-start.24
  90.5 0.0 collective-permute-done.22.refs_1_
  90.5 2.9 %collective-permute-done.23.refs_2_ = bf16[128,384]{1,0:T(8,128)(2,1)S(1)} collective-permute-done((bf16[128,384]{1,0:T(8,128)(2,1)S(1)}, bf16[128,384]{1,0:T(8,128)(2,1)S(1)}, u32[]{:S(2)}, u32[]{:S(2)}) %collective-permute-start.23) | collective-permute-done | bytes 98336 | tf_op jit(solution)/shard_map/ppermute | solution.py:83
  93.4 2.2 %collective-permute-done.24.refs_3_ = bf16[128,384]{1,0:T(8,128)(2,1)S(1)} collective-permute-done((bf16[128,384]{1,0:T(8,128)(2,1)S(1)}, bf16[128,384]{1,0:T(8,128)(2,1)S(1)}, u32[]{:S(2)}, u32[]{:S(2)}) %collective-permute-start.24) | collective-permute-done | bytes 98336 | tf_op jit(solution)/shard_map/ppermute | solution.py:83
  95.5 0.9 update_rows.1
  (15 shorter events, 0.1 us)
Async XLA Ops:
  0.6 20.0 %collective-permute-start = (bf16[128,2048]{1,0:T(8,128)(2,1)}, bf16[128,2048]{1,0:T(8,128)(2,1)S(1)}, u32[]{:S(2)}, u32[]{:S(2)}) collective-permute-start(bf16[128,2048]{1,0:T(8,128)(2,1)} %bitcast.25), channel_id=1, source_target_pairs={{0,1},{1,0},{2,3},{3,2},{4,5},{5,4},{6,7},{7,6},{8,9},{9,8},{10,11... | collective-permute-start | bytes 1572872 | tf_op jit(solution)/shard_map/ppermute | solution.py:83
  0.8 10.9 %collective-permute-start.2 = (bf16[128,2048]{1,0:T(8,128)(2,1)}, bf16[128,2048]{1,0:T(8,128)(2,1)S(1)}, u32[]{:S(2)}, u32[]{:S(2)}) collective-permute-start(bf16[128,2048]{1,0:T(8,128)(2,1)} %bitcast.26), channel_id=1, source_target_pairs={{1,2},{3,4},{4,3},{6,5},{9,10},{11,12},{12,11},{14,13},{17,18},{19... | collective-permute-start | bytes 1572872 | tf_op jit(solution)/shard_map/ppermute | solution.py:273
  5.3 15.4 %collective-permute-start.1 = (bf16[128,2048]{1,0:T(8,128)(2,1)}, bf16[128,2048]{1,0:T(8,128)(2,1)S(1)}, u32[]{:S(2)}, u32[]{:S(2)}) collective-permute-start(bf16[128,2048]{1,0:T(8,128)(2,1)} %bitcast.29), channel_id=1, source_target_pairs={{0,1},{1,0},{2,3},{3,2},{4,5},{5,4},{6,7},{7,6},{8,9},{9,8},{10,11... | collective-permute-start | bytes 1572872 | tf_op jit(solution)/shard_map/ppermute | solution.py:83
  5.3 11.9 %collective-permute-start.3 = (bf16[128,2048]{1,0:T(8,128)(2,1)}, bf16[128,2048]{1,0:T(8,128)(2,1)S(1)}, u32[]{:S(2)}, u32[]{:S(2)}) collective-permute-start(bf16[128,2048]{1,0:T(8,128)(2,1)} %bitcast.30), channel_id=1, source_target_pairs={{1,2},{3,4},{4,3},{6,5},{9,10},{11,12},{12,11},{14,13},{17,18},{19... | collective-permute-start | bytes 1572872 | tf_op jit(solution)/shard_map/ppermute | solution.py:274
  8.8 11.8 %copy-start = (bf16[1,1,128,2048]{3,2,1,0:T(8,128)(2,1)S(1)}, bf16[1,1,128,2048]{3,2,1,0:T(8,128)(2,1)}, u32[]{:S(2)}) copy-start(bf16[1,1,128,2048]{3,2,1,0:T(8,128)(2,1)} %param.6) | copy-start | bytes 1572868
  8.9 11.8 %copy-start.1 = (bf16[1,1,128,2048]{3,2,1,0:T(8,128)(2,1)S(1)}, bf16[1,1,128,2048]{3,2,1,0:T(8,128)(2,1)}, u32[]{:S(2)}) copy-start(bf16[1,1,128,2048]{3,2,1,0:T(8,128)(2,1)} %param.7) | copy-start | bytes 1572868
  8.9 11.8 %copy-start.2 = (bf16[1,1,128,2048]{3,2,1,0:T(8,128)(2,1)S(1)}, bf16[1,1,128,2048]{3,2,1,0:T(8,128)(2,1)}, u32[]{:S(2)}) copy-start(bf16[1,1,128,2048]{3,2,1,0:T(8,128)(2,1)} %param.8) | copy-start | bytes 1572868
  8.9 11.8 %copy-start.4 = (s32[1,8]{1,0:T(1,128)S(1)}, s32[1,8]{1,0:T(1,128)}, u32[]{:S(2)}) copy-start(s32[1,8]{1,0:T(1,128)} %near_ref.5) | copy-start | bytes 100
  17.3 11.7 %collective-permute-start.4 = (bf16[128,1536]{1,0:T(8,128)(2,1)S(1)}, bf16[128,1536]{1,0:T(8,128)(2,1)S(1)}, u32[]{:S(2)}, u32[]{:S(2)}) collective-permute-start(bf16[128,1536]{1,0:T(8,128)(2,1)S(1)} %get-tuple-element.39), channel_id=1, source_target_pairs={{0,4},{1,5},{2,6},{3,7},{4,0},{5,1},{6,2},{7,3},{8,12},{9,13},{10,... | collective-permute-start | bytes 1179656 | tf_op jit(solution)/shard_map/ppermute | solution.py:83
  20.1 9.7 %collective-permute-start.5 = (bf16[128,1536]{1,0:T(8,128)(2,1)S(1)}, bf16[128,1536]{1,0:T(8,128)(2,1)S(1)}, u32[]{:S(2)}, u32[]{:S(2)}) collective-permute-start(bf16[128,1536]{1,0:T(8,128)(2,1)S(1)} %pad_maximum_fusion.1), channel_id=1, source_target_pairs={{0,2},{1,3},{2,0},{3,1},{4,6},{5,7},{6,4},{7,5},{8,10},{9,11},{10,... | collective-permute-start | bytes 1179656 | tf_op jit(solution)/shard_map/ppermute | solution.py:83
  23.0 15.6 %copy-start.3 = (bf16[1,1,128,2048]{3,2,1,0:T(8,128)(2,1)S(1)}, bf16[1,1,128,2048]{3,2,1,0:T(8,128)(2,1)}, u32[]{:S(2)}) copy-start(bf16[1,1,128,2048]{3,2,1,0:T(8,128)(2,1)} %param.9) | copy-start | bytes 1572868
  23.0 12.4 %collective-permute-start.10 = (bf16[2,512,128]{2,1,0:T(8,128)(2,1)S(1)}, bf16[2,512,128]{2,1,0:T(8,128)(2,1)S(1)}, u32[]{:S(2)}, u32[]{:S(2)}) collective-permute-start(bf16[2,512,128]{2,1,0:T(8,128)(2,1)S(1)} %get-tuple-element.60.refs_0_), channel_id=1, source_target_pairs={{0,2},{1,3},{2,0},{3,1},{4,6},{5,7},{6,4},{7,5},{8,10},{9,11},{10,... | collective-permute-start | bytes 786440 | tf_op jit(solution)/shard_map/ppermute | solution.py:83
  24.0 11.4 %collective-permute-start.11 = (bf16[2,512,128]{2,1,0:T(8,128)(2,1)S(1)}, bf16[2,512,128]{2,1,0:T(8,128)(2,1)S(1)}, u32[]{:S(2)}, u32[]{:S(2)}) collective-permute-start(bf16[2,512,128]{2,1,0:T(8,128)(2,1)S(1)} %get-tuple-element.78), channel_id=1, source_target_pairs={{0,4},{1,5},{2,6},{3,7},{4,0},{5,1},{6,2},{7,3},{8,12},{9,13},{10,... | collective-permute-start | bytes 786440 | tf_op jit(solution)/shard_map/ppermute | solution.py:83
  29.8 8.8 %collective-permute-start.6 = (bf16[1,128,768]{2,1,0:T(8,128)(2,1)S(1)}, bf16[1,128,768]{2,1,0:T(8,128)(2,1)S(1)}, u32[]{:S(2)}, u32[]{:S(2)}) collective-permute-start(bf16[1,128,768]{2,1,0:T(8,128)(2,1)S(1)} %get-tuple-element.83), channel_id=1, source_target_pairs={{0,4},{1,5},{2,6},{3,7},{4,0},{5,1},{6,2},{7,3},{8,12},{9,13},{10,... | collective-permute-start | bytes 589832 | tf_op jit(solution)/shard_map/ppermute | solution.py:83
  31.4 13.5 %collective-permute-start.13 = (bf16[1,128,768]{2,1,0:T(8,128)(2,1)S(1)}, bf16[1,128,768]{2,1,0:T(8,128)(2,1)S(1)}, u32[]{:S(2)}, u32[]{:S(2)}) collective-permute-start(bf16[1,128,768]{2,1,0:T(8,128)(2,1)S(1)} %get-tuple-element.82), channel_id=1, source_target_pairs={{0,4},{1,5},{2,6},{3,7},{4,0},{5,1},{6,2},{7,3},{8,12},{9,13},{10,... | collective-permute-start | bytes 589832 | tf_op jit(solution)/shard_map/ppermute | solution.py:83
  35.4 9.7 %collective-permute-start.12 = (bf16[2,512,128]{2,1,0:T(8,128)(2,1)S(1)}, bf16[2,512,128]{2,1,0:T(8,128)(2,1)S(1)}, u32[]{:S(2)}, u32[]{:S(2)}) collective-permute-start(bf16[2,512,128]{2,1,0:T(8,128)(2,1)S(1)} %collective-permute-done.11.refs_2_), channel_id=1, source_target_pairs={{0,2},{1,3},{2,0},{3,1},{4,6},{5,7},{6,4},{7,5},{8,10},{9,11},{10,... | collective-permute-start | bytes 786440 | tf_op jit(solution)/shard_map/ppermute | solution.py:83
  42.6 18.2 %collective-permute-start.7 = (bf16[2,128,2048]{2,1,0:T(8,128)(2,1)S(1)}, bf16[2,128,2048]{2,1,0:T(8,128)(2,1)S(1)}, u32[]{:S(2)}, u32[]{:S(2)}) collective-permute-start(bf16[2,128,2048]{2,1,0:T(8,128)(2,1)S(1)} %get-tuple-element.47), channel_id=1, source_target_pairs={{0,1},{1,0},{2,3},{3,2},{4,5},{5,4},{6,7},{7,6},{8,9},{9,8},{10,11... | collective-permute-start | bytes 3145736 | tf_op jit(solution)/shard_map/ppermute | solution.py:83
  45.7 2.1 %collective-permute-start.15 = (bf16[1,128,1536]{2,1,0:T(8,128)(2,1)S(1)}, bf16[1,128,1536]{2,1,0:T(8,128)(2,1)S(1)}, u32[]{:S(2)}, u32[]{:S(2)}) collective-permute-start(bf16[1,128,1536]{2,1,0:T(8,128)(2,1)S(1)} %get-tuple-element.59), channel_id=1, source_target_pairs={{0,1},{1,0},{2,3},{3,2},{4,5},{5,4},{6,7},{7,6},{8,9},{9,8},{10,11... | collective-permute-start | bytes 1179656 | tf_op jit(solution)/shard_map/ppermute | solution.py:83
  46.4 4.8 %collective-permute-start.19 = (bf16[1,128,1536]{2,1,0:T(8,128)(2,1)S(1)}, bf16[1,128,1536]{2,1,0:T(8,128)(2,1)S(1)}, u32[]{:S(2)}, u32[]{:S(2)}) collective-permute-start(bf16[1,128,1536]{2,1,0:T(8,128)(2,1)S(1)} %get-tuple-element.65), channel_id=1, source_target_pairs={{0,1},{1,0},{2,3},{3,2},{4,5},{5,4},{6,7},{7,6},{8,9},{9,8},{10,11... | collective-permute-start | bytes 1179656 | tf_op jit(solution)/shard_map/ppermute | solution.py:83
  47.9 10.4 %collective-permute-start.17 = (bf16[128,1536]{1,0:T(8,128)(2,1)S(1)}, bf16[128,1536]{1,0:T(8,128)(2,1)S(1)}, u32[]{:S(2)}, u32[]{:S(2)}) collective-permute-start(bf16[128,1536]{1,0:T(8,128)(2,1)S(1)} %block_sum.3), channel_id=1, source_target_pairs={{0,8},{8,0},{16,24},{24,16},{1,9},{9,1},{17,25},{25,17},{2,10},{10... | collective-permute-start | bytes 1179656 | tf_op jit(solution)/shard_map/ppermute | solution.py:83
  49.8 2.7 %collective-permute-start.16 = (bf16[1,128,1536]{2,1,0:T(8,128)(2,1)S(1)}, bf16[1,128,1536]{2,1,0:T(8,128)(2,1)S(1)}, u32[]{:S(2)}, u32[]{:S(2)}) collective-permute-start(bf16[1,128,1536]{2,1,0:T(8,128)(2,1)S(1)} %get-tuple-element.63), channel_id=1, source_target_pairs={{0,1},{1,0},{2,3},{3,2},{4,5},{5,4},{6,7},{7,6},{8,9},{9,8},{10,11... | collective-permute-start | bytes 1179656 | tf_op jit(solution)/shard_map/ppermute | solution.py:83
  51.1 9.6 %collective-permute-start.14 = (bf16[1,128,1536]{2,1,0:T(8,128)(2,1)S(1)}, bf16[1,128,1536]{2,1,0:T(8,128)(2,1)S(1)}, u32[]{:S(2)}, u32[]{:S(2)}) collective-permute-start(bf16[1,128,1536]{2,1,0:T(8,128)(2,1)S(1)} %get-tuple-element.57), channel_id=1, source_target_pairs={{0,1},{1,0},{2,3},{3,2},{4,5},{5,4},{6,7},{7,6},{8,9},{9,8},{10,11... | collective-permute-start | bytes 1179656 | tf_op jit(solution)/shard_map/ppermute | solution.py:83
  51.2 28.6 %collective-permute-start.8 = (bf16[128,2048]{1,0:T(8,128)(2,1)S(1)}, bf16[128,2048]{1,0:T(8,128)(2,1)S(1)}, u32[]{:S(2)}, u32[]{:S(2)}) collective-permute-start(bf16[128,2048]{1,0:T(8,128)(2,1)S(1)} %get-tuple-element.49), channel_id=1, source_target_pairs={{3,4},{5,6},{2,1},{4,3},{11,12},{13,14},{10,9},{12,11},{19,20},{21... | collective-permute-start | bytes 1572872 | tf_op jit(solution)/shard_map/ppermute | solution.py:402
  52.5 27.3 %collective-permute-start.9 = (bf16[128,2048]{1,0:T(8,128)(2,1)S(1)}, bf16[128,2048]{1,0:T(8,128)(2,1)S(1)}, u32[]{:S(2)}, u32[]{:S(2)}) collective-permute-start(bf16[128,2048]{1,0:T(8,128)(2,1)S(1)} %get-tuple-element.51), channel_id=1, source_target_pairs={{3,4},{5,6},{2,1},{4,3},{11,12},{13,14},{10,9},{12,11},{19,20},{21... | collective-permute-start | bytes 1572872 | tf_op jit(solution)/shard_map/ppermute | solution.py:403
  58.4 19.4 %collective-permute-start.18 = (bf16[128,1536]{1,0:T(8,128)(2,1)S(1)}, bf16[128,1536]{1,0:T(8,128)(2,1)S(1)}, u32[]{:S(2)}, u32[]{:S(2)}) collective-permute-start(bf16[128,1536]{1,0:T(8,128)(2,1)S(1)} %block_sum.4), channel_id=1, source_target_pairs={{0,16},{8,24},{16,0},{24,8},{1,17},{9,25},{17,1},{25,9},{2,18},{10... | collective-permute-start | bytes 1179656 | tf_op jit(solution)/shard_map/ppermute | solution.py:83
  60.7 17.0 %collective-permute-start.20 = (bf16[128,1536]{1,0:T(8,128)(2,1)S(1)}, bf16[128,1536]{1,0:T(8,128)(2,1)S(1)}, u32[]{:S(2)}, u32[]{:S(2)}) collective-permute-start(bf16[128,1536]{1,0:T(8,128)(2,1)S(1)} %block_sum.5), channel_id=1, source_target_pairs={{0,8},{8,0},{16,24},{24,16},{1,9},{9,1},{17,25},{25,17},{2,10},{10... | collective-permute-start | bytes 1179656 | tf_op jit(solution)/shard_map/ppermute | solution.py:83
  78.6 3.2 %collective-permute-start.21 = (f32[128,128]{1,0:T(8,128)S(1)}, f32[128,128]{1,0:T(8,128)S(1)}, u32[]{:S(2)}, u32[]{:S(2)}) collective-permute-start(f32[128,128]{1,0:T(8,128)S(1)} %get-tuple-element.69.gram), channel_id=1, source_target_pairs={{0,2},{1,3},{2,0},{3,1},{4,6},{5,7},{6,4},{7,5},{8,10},{9,11},{10,... | collective-permute-start | bytes 196616 | tf_op jit(solution)/shard_map/ppermute | solution.py:83
  85.7 4.7 %collective-permute-start.22 = (bf16[128,384]{1,0:T(8,128)(2,1)S(1)}, bf16[128,384]{1,0:T(8,128)(2,1)S(1)}, u32[]{:S(2)}, u32[]{:S(2)}) collective-permute-start(bf16[128,384]{1,0:T(8,128)(2,1)S(1)} %get-tuple-element.71), channel_id=1, source_target_pairs={{0,1},{1,0},{2,3},{3,2},{4,5},{5,4},{6,7},{7,6},{8,9},{9,8},{10,11... | collective-permute-start | bytes 294920 | tf_op jit(solution)/shard_map/ppermute | solution.py:83
  88.8 4.6 %collective-permute-start.23 = (bf16[128,384]{1,0:T(8,128)(2,1)S(1)}, bf16[128,384]{1,0:T(8,128)(2,1)S(1)}, u32[]{:S(2)}, u32[]{:S(2)}) collective-permute-start(bf16[128,384]{1,0:T(8,128)(2,1)S(1)} %get-tuple-element.72), channel_id=1, source_target_pairs={{0,4},{1,5},{2,6},{3,7},{4,0},{5,1},{6,2},{7,3},{8,12},{9,13},{10,... | collective-permute-start | bytes 294920 | tf_op jit(solution)/shard_map/ppermute | solution.py:83
  90.4 5.1 %collective-permute-start.24 = (bf16[128,384]{1,0:T(8,128)(2,1)S(1)}, bf16[128,384]{1,0:T(8,128)(2,1)S(1)}, u32[]{:S(2)}, u32[]{:S(2)}) collective-permute-start(bf16[128,384]{1,0:T(8,128)(2,1)S(1)} %get-tuple-element.73), channel_id=1, source_target_pairs={{0,5},{1,4},{2,7},{3,6},{4,1},{5,0},{6,3},{7,2},{8,13},{9,12},{10,... | collective-permute-start | bytes 294920 | tf_op jit(solution)/shard_map/ppermute | solution.py:83

commit v12 on v11

--- a/solution.py
+++ b/solution.py
@@ -296,7 +296,7 @@
         for q in range(1, plan.col)
     ]
     high_columns = [
-        shift(after(own_columns, key_next, value_next), "seq", high << (1 + plan.col_bits))
+        shift(after(own_columns, key_next), "seq", high << (1 + plan.col_bits))
         for high in range(1, plan.high)
     ]
 

time: 97 us -> 95.2 us (0.981)
  waiting for transfers between devices: 43 us -> 39.8 us
  starting transfers between devices: 34.4 us -> 35.9 us
    ppermute x1, waiting for transfers between devices: 5.62 us -> 2.83 us  [local(): value_next = lax.ppermute(value, 'seq', takes)]
    ppermute x21, starting transfers between devices: 23.6 us -> 25.1 us  [shift(): lax.ppermute(value, axis, [(i, i ^ mask) for i in range(lax.axis_size(axi...]
  transfers between devices with their start and end apart: 25 -> 25, of which waited for: 12 -> 11; matrix products, arithmetic and copies ran while one was open for 2% -> 2% of each run, Pallas kernels for 12% -> 12%
where the time goes in v12:
time: 95.2 us; the launch traced here: 94.8 us
  waiting for transfers between devices  39.8 us (42%)
  starting transfers between devices  35.9 us (38%)
  Pallas kernels  16.5 us (17%)
  local copies, waits for them, and re-layouts  1.47 us (2%)
    ppermute x21, waiting for transfers between devices, shift(): lax.ppermute(value, axis, [(i, i ^ mask) for i in range(lax.axis_size(axi...  35.7 us
    ppermute x21, starting transfers between devices, shift(): lax.ppermute(value, axis, [(i, i ^ mask) for i in range(lax.axis_size(axi...  25.1 us
    ppermute x1, starting transfers between devices, local(): key_next = lax.ppermute(key, 'seq', takes)  4.49 us
    pallas_call x1, Pallas kernels, local(): pl.pallas_call(backward_kernel, out_shape=[struct((tile, width), bf16), s...  3.99 us
    pallas_call x1, Pallas kernels, local(): pl.pallas_call(functools.partial(update_kernel, plan, factor), out_shape=...  3.97 us
    ppermute x1, starting transfers between devices, local(): value_next = lax.ppermute(value, 'seq', takes)  3.49 us
    ppermute x1, waiting for transfers between devices, local(): value_next = lax.ppermute(value, 'seq', takes)  2.83 us
    pallas_call x4, Pallas kernels, product(): pl.pallas_call(functools.partial(product_kernel, plan, layers), out_shape...  2.39 us
  transfers between devices with their start and end apart: 25, of which 11 were waited for; matrix products, arithmetic and copies ran while one was open for 2% of the time, Pallas kernels for 12%

profile of v12, /device:TPU:1, one launch (start us, length us, event | category | flops | bytes accessed | tf_op | source)
XLA Modules:
  0.0 94.8 jit_solution(7837325245877205252)
XLA Ops:
  0.6 0.1 collective-permute-start
  0.8 4.5 %collective-permute-start.2 = (bf16[128,2048]{1,0:T(8,128)(2,1)}, bf16[128,2048]{1,0:T(8,128)(2,1)S(1)}, u32[]{:S(2)}, u32[]{:S(2)}) collective-permute-start(bf16[128,2048]{1,0:T(8,128)(2,1)} %bitcast.26), channel_id=1, source_target_pairs={{1,2},{3,4},{4,3},{6,5},{9,10},{11,12},{12,11},{14,13},{17,18},{19... | collective-permute-start | bytes 1572872 | tf_op jit(solution)/shard_map/ppermute | solution.py:273
  5.3 0.1 collective-permute-start.1
  5.3 3.5 %collective-permute-start.3 = (bf16[128,2048]{1,0:T(8,128)(2,1)}, bf16[128,2048]{1,0:T(8,128)(2,1)S(1)}, u32[]{:S(2)}, u32[]{:S(2)}) collective-permute-start(bf16[128,2048]{1,0:T(8,128)(2,1)} %bitcast.30), channel_id=1, source_target_pairs={{1,2},{3,4},{4,3},{6,5},{9,10},{11,12},{12,11},{14,13},{17,18},{19... | collective-permute-start | bytes 1572872 | tf_op jit(solution)/shard_map/ppermute | solution.py:274
  8.9 1.4 %dynamic-slice_bitcast_fusion.1 = (bf16[128,768]{1,0:T(8,128)(2,1)S(1)}, bf16[128,768]{1,0:T(8,128)(2,1)S(1)}, bf16[128,768]{1,0:T(8,128)(2,1)S(1)}, bf16[128,768]{1,0:T(8,128)(2,1)S(1)}) fusion(bf16[1,1,128,3072]{3,2,1,0:T(8,128)(2,1)} %param.10, s32[]{:T(128)S(6)} %select_n.14, s32[]{:T(128)S(6)} %select_n.13, s32[]{:T(128)S(6)} %select_n.12, s32[]{:T(128)S(6)} %select_n.15), kind=kLoop, calls=%fused_computation.6 | loop fusion | bytes 1572880 | tf_op jit(solution)/shard_map/dynamic_slice | solution.py:287
  10.3 0.1 fusion
  10.4 1.3 %collective-permute-done.2.kn = bf16[128,2048]{1,0:T(8,128)(2,1)S(1)} collective-permute-done((bf16[128,2048]{1,0:T(8,128)(2,1)}, bf16[128,2048]{1,0:T(8,128)(2,1)S(1)}, u32[]{:S(2)}, u32[]{:S(2)}) %collective-permute-start.2) | collective-permute-done | bytes 524320 | tf_op jit(solution)/shard_map/ppermute | solution.py:273
  11.6 2.8 %collective-permute-start.4 = (bf16[128,1536]{1,0:T(8,128)(2,1)S(1)}, bf16[128,1536]{1,0:T(8,128)(2,1)S(1)}, u32[]{:S(2)}, u32[]{:S(2)}) collective-permute-start(bf16[128,1536]{1,0:T(8,128)(2,1)S(1)} %get-tuple-element.39), channel_id=1, source_target_pairs={{0,4},{1,5},{2,6},{3,7},{4,0},{5,1},{6,2},{7,3},{8,12},{9,13},{10,... | collective-permute-start | bytes 1179656 | tf_op jit(solution)/shard_map/ppermute | solution.py:83
  14.4 2.8 %collective-permute-done.3.vn = bf16[128,2048]{1,0:T(8,128)(2,1)S(1)} collective-permute-done((bf16[128,2048]{1,0:T(8,128)(2,1)}, bf16[128,2048]{1,0:T(8,128)(2,1)S(1)}, u32[]{:S(2)}, u32[]{:S(2)}) %collective-permute-start.3) | collective-permute-done | bytes 524320 | tf_op jit(solution)/shard_map/ppermute | solution.py:274
  17.3 3.5 %collective-permute-start.5 = (bf16[128,1536]{1,0:T(8,128)(2,1)S(1)}, bf16[128,1536]{1,0:T(8,128)(2,1)S(1)}, u32[]{:S(2)}, u32[]{:S(2)}) collective-permute-start(bf16[128,1536]{1,0:T(8,128)(2,1)S(1)} %pad_maximum_fusion.1), channel_id=1, source_target_pairs={{0,2},{1,3},{2,0},{3,1},{4,6},{5,7},{6,4},{7,5},{8,10},{9,11},{10,... | collective-permute-start | bytes 1179656 | tf_op jit(solution)/shard_map/ppermute | solution.py:83
  20.7 0.0 collective-permute-done.km
  20.7 0.0 collective-permute-done.1.vm
  20.8 2.3 %attention_forward.1 = bf16[2,2,512,128]{3,2,1,0:T(8,128)(2,1)S(1)} custom-call(s32[1,8]{1,0:T(1,128)S(1)} %copy-done.4, bf16[128,2048]{1,0:T(8,128)(2,1)S(1)} %bitcast.23, bf16[128,2048]{1,0:T(8,128)(2,1)S(1)} %bitcast.27, bf16[128,2048]{1,0:T(8,128)(2,1)S(1)} %bitcast.31, bf16[128,2048]{1,0:T(8,128)(2,1)S(1)} %collective-permute-done.km, ...), custom_call_target="tpu_custom_call" | custom-call | flops 268435456 | bytes 4194304 | tf_op jit(solution)/shard_map/attention_forward/pallas_call | solution.py:303
  23.1 0.0 copy-start.3
  23.1 0.1 collective-permute-start.10
  23.2 0.8 collective-permute-start.11
  24.0 2.4 %collective-permute-done.4 = bf16[128,1536]{1,0:T(8,128)(2,1)S(1)} collective-permute-done((bf16[128,1536]{1,0:T(8,128)(2,1)S(1)}, bf16[128,1536]{1,0:T(8,128)(2,1)S(1)}, u32[]{:S(2)}, u32[]{:S(2)}) %collective-permute-start.4) | collective-permute-done | bytes 393248 | tf_op jit(solution)/shard_map/ppermute | solution.py:83
  26.4 4.0 %collective-permute-done.5 = bf16[128,1536]{1,0:T(8,128)(2,1)S(1)} collective-permute-done((bf16[128,1536]{1,0:T(8,128)(2,1)S(1)}, bf16[128,1536]{1,0:T(8,128)(2,1)S(1)}, u32[]{:S(2)}, u32[]{:S(2)}) %collective-permute-start.5) | collective-permute-done | bytes 393248 | tf_op jit(solution)/shard_map/ppermute | solution.py:83
  30.4 0.1 collective-permute-start.6
  30.5 1.5 %collective-permute-start.13 = (bf16[1,128,768]{2,1,0:T(8,128)(2,1)S(1)}, bf16[1,128,768]{2,1,0:T(8,128)(2,1)S(1)}, u32[]{:S(2)}, u32[]{:S(2)}) collective-permute-start(bf16[1,128,768]{2,1,0:T(8,128)(2,1)S(1)} %get-tuple-element.82), channel_id=1, source_target_pairs={{0,4},{1,5},{2,6},{3,7},{4,0},{5,1},{6,2},{7,3},{8,12},{9,13},{10,... | collective-permute-start | bytes 589832 | tf_op jit(solution)/shard_map/ppermute | solution.py:83
  31.9 3.3 %collective-permute-done.10.refs_1_ = bf16[2,512,128]{2,1,0:T(8,128)(2,1)S(1)} collective-permute-done((bf16[2,512,128]{2,1,0:T(8,128)(2,1)S(1)}, bf16[2,512,128]{2,1,0:T(8,128)(2,1)S(1)}, u32[]{:S(2)}, u32[]{:S(2)}) %collective-permute-start.10) | collective-permute-done | bytes 262176 | tf_op jit(solution)/shard_map/ppermute | solution.py:83
  35.2 0.0 collective-permute-done.11.refs_2_
  35.2 1.7 %collective-permute-start.12 = (bf16[2,512,128]{2,1,0:T(8,128)(2,1)S(1)}, bf16[2,512,128]{2,1,0:T(8,128)(2,1)S(1)}, u32[]{:S(2)}, u32[]{:S(2)}) collective-permute-start(bf16[2,512,128]{2,1,0:T(8,128)(2,1)S(1)} %collective-permute-done.11.refs_2_), channel_id=1, source_target_pairs={{0,2},{1,3},{2,0},{3,1},{4,6},{5,7},{6,4},{7,5},{8,10},{9,11},{10,... | collective-permute-start | bytes 786440 | tf_op jit(solution)/shard_map/ppermute | solution.py:83
  37.0 0.0 collective-permute-done.6
  37.0 4.0 %attention_backward.1 = (bf16[128,2048]{1,0:T(8,128)(2,1)}, f32[128,2048]{1,0:T(8,128)S(1)}, f32[128,2048]{1,0:T(8,128)S(1)}, bf16[128,2048]{1,0:T(8,128)(2,1)S(...) custom-call(s32[1,8]{1,0:T(1,128)S(1)} %copy-done.4, bf16[128,2048]{1,0:T(8,128)(2,1)S(1)} %bitcast.24, ...), custom_call_target="tpu_custom_call" | custom-call | flops 939524096 | bytes 7864320 | tf_op jit(solution)/shard_map/attention_backward/pallas_call | solution.py:332
  41.0 2.0 %collective-permute-start.7 = (bf16[2,128,2048]{2,1,0:T(8,128)(2,1)S(1)}, bf16[2,128,2048]{2,1,0:T(8,128)(2,1)S(1)}, u32[]{:S(2)}, u32[]{:S(2)}) collective-permute-start(bf16[2,128,2048]{2,1,0:T(8,128)(2,1)S(1)} %get-tuple-element.47), channel_id=1, source_target_pairs={{0,1},{1,0},{2,3},{3,2},{4,5},{5,4},{6,7},{7,6},{8,9},{9,8},{10,11... | collective-permute-start | bytes 3145736 | tf_op jit(solution)/shard_map/ppermute | solution.py:83
  42.9 0.1 maximum_maximum_fusion.refs_4_
  43.1 0.6 collective-permute-done.12.refs_3_
  43.7 0.6 product_first.1
  44.3 0.6 collective-permute-start.15
  44.9 0.6 product_near.1
  45.5 0.1 collective-permute-start.19
  45.6 0.7 collective-permute-done.15.refs_1_
  46.3 0.1 block_sum.3
  46.3 1.4 %collective-permute-start.17 = (bf16[128,1536]{1,0:T(8,128)(2,1)S(1)}, bf16[128,1536]{1,0:T(8,128)(2,1)S(1)}, u32[]{:S(2)}, u32[]{:S(2)}) collective-permute-start(bf16[128,1536]{1,0:T(8,128)(2,1)S(1)} %block_sum.3), channel_id=1, source_target_pairs={{0,8},{8,0},{16,24},{24,16},{1,9},{9,1},{17,25},{25,17},{2,10},{10... | collective-permute-start | bytes 1179656 | tf_op jit(solution)/shard_map/ppermute | solution.py:83
  47.7 0.6 product_middle.1
  48.3 0.7 collective-permute-start.16
  49.0 0.6 product_own.1
  49.6 0.1 collective-permute-start.14
  49.7 0.0 collective-permute-done.19.refs_1_
  49.7 1.3 %collective-permute-start.8 = (bf16[128,2048]{1,0:T(8,128)(2,1)S(1)}, bf16[128,2048]{1,0:T(8,128)(2,1)S(1)}, u32[]{:S(2)}, u32[]{:S(2)}) collective-permute-start(bf16[128,2048]{1,0:T(8,128)(2,1)S(1)} %get-tuple-element.49), channel_id=1, source_target_pairs={{3,4},{5,6},{2,1},{4,3},{11,12},{13,14},{10,9},{12,11},{19,20},{21... | collective-permute-start | bytes 1572872 | tf_op jit(solution)/shard_map/ppermute | solution.py:402
  51.0 1.5 %collective-permute-start.9 = (bf16[128,2048]{1,0:T(8,128)(2,1)S(1)}, bf16[128,2048]{1,0:T(8,128)(2,1)S(1)}, u32[]{:S(2)}, u32[]{:S(2)}) collective-permute-start(bf16[128,2048]{1,0:T(8,128)(2,1)S(1)} %get-tuple-element.51), channel_id=1, source_target_pairs={{3,4},{5,6},{2,1},{4,3},{11,12},{13,14},{10,9},{12,11},{19,20},{21... | collective-permute-start | bytes 1572872 | tf_op jit(solution)/shard_map/ppermute | solution.py:403
  52.5 0.1 block_sum.5
  52.6 4.1 %collective-permute-done.17.refs_2_ = bf16[128,1536]{1,0:T(8,128)(2,1)S(1)} collective-permute-done((bf16[128,1536]{1,0:T(8,128)(2,1)S(1)}, bf16[128,1536]{1,0:T(8,128)(2,1)S(1)}, u32[]{:S(2)}, u32[]{:S(2)}) %collective-permute-start.17) | collective-permute-done | bytes 393248 | tf_op jit(solution)/shard_map/ppermute | solution.py:83
  56.7 0.1 block_sum.4
  56.8 2.4 %collective-permute-start.18 = (bf16[128,1536]{1,0:T(8,128)(2,1)S(1)}, bf16[128,1536]{1,0:T(8,128)(2,1)S(1)}, u32[]{:S(2)}, u32[]{:S(2)}) collective-permute-start(bf16[128,1536]{1,0:T(8,128)(2,1)S(1)} %block_sum.4), channel_id=1, source_target_pairs={{0,16},{8,24},{16,0},{24,8},{1,17},{9,25},{17,1},{25,9},{2,18},{10... | collective-permute-start | bytes 1179656 | tf_op jit(solution)/shard_map/ppermute | solution.py:83
  59.2 0.0 collective-permute-done.14.refs_0_
  59.2 0.0 collective-permute-done.7.mate
  59.2 1.3 %collective-permute-start.20 = (bf16[128,1536]{1,0:T(8,128)(2,1)S(1)}, bf16[128,1536]{1,0:T(8,128)(2,1)S(1)}, u32[]{:S(2)}, u32[]{:S(2)}) collective-permute-start(bf16[128,1536]{1,0:T(8,128)(2,1)S(1)} %block_sum.5), channel_id=1, source_target_pairs={{0,8},{8,0},{16,24},{24,16},{1,9},{9,1},{17,25},{25,17},{2,10},{10... | collective-permute-start | bytes 1179656 | tf_op jit(solution)/shard_map/ppermute | solution.py:83
  60.5 15.7 %collective-permute-done.18.refs_1_ = bf16[128,1536]{1,0:T(8,128)(2,1)S(1)} collective-permute-done((bf16[128,1536]{1,0:T(8,128)(2,1)S(1)}, bf16[128,1536]{1,0:T(8,128)(2,1)S(1)}, u32[]{:S(2)}, u32[]{:S(2)}) %collective-permute-start.18) | collective-permute-done | bytes 393248 | tf_op jit(solution)/shard_map/ppermute | solution.py:83
  76.2 0.0 collective-permute-done.20.refs_2_
  76.2 0.8 gradient_sum.1
  77.1 1.5 %collective-permute-start.21 = (f32[128,128]{1,0:T(8,128)S(1)}, f32[128,128]{1,0:T(8,128)S(1)}, u32[]{:S(2)}, u32[]{:S(2)}) collective-permute-start(f32[128,128]{1,0:T(8,128)S(1)} %get-tuple-element.69.gram), channel_id=1, source_target_pairs={{0,2},{1,3},{2,0},{3,1},{4,6},{5,7},{6,4},{7,5},{8,10},{9,11},{10,... | collective-permute-start | bytes 196616 | tf_op jit(solution)/shard_map/ppermute | solution.py:83
  78.6 0.0 collective-permute-done.8.kn
  78.6 0.0 collective-permute-done.9.vn
  78.6 1.8 %key_value_sum.1 = (bf16[128,2048]{1,0:T(8,128)(2,1)}, bf16[128,2048]{1,0:T(8,128)(2,1)}) custom-call(s32[1,8]{1,0:T(1,128)S(1)} %copy-done.4, f32[128,2048]{1,0:T(8,128)S(1)} %get-tuple-element.44.dko, f32[128,2048]{1,0:T(8,128)S(1)} %get-tuple-element.45.dvo, bf16[2,128,2048]{2,1,0:T(8,128)(2,1)S(1)} %collective-permute-done.7.mate, ...), custom_call_target="tpu_custom_call" | custom-call | flops 1572864 | bytes 5242880 | tf_op jit(solution)/shard_map/key_value_sum/pallas_call | solution.py:412
  80.4 4.0 %newton_schulz.1 = (f32[128,384]{1,0:T(8,128)S(1)}, bf16[128,384]{1,0:T(8,128)(2,1)S(1)}, bf16[128,384]{1,0:T(8,128)(2,1)S(1)}, bf16[128,384]{1,0:T(8,128)(2,1)S(1)}) custom-call(f32[128,1536]{1,0:T(8,128)S(1)} %get-tuple-element.68.x, f32[128,128]{1,0:T(8,128)S(1)} %get-tuple-element.69.gram, f32[128,128]{1,0:T(8,128)S(1)} %collective-permute-done.21.gram_other), custom_call_target="tpu_custom_call" | custom-call | flops 301989888 | bytes 1572864 | tf_op jit(solution)/shard_map/newton_schulz/pallas_call | solution.py:443
  84.4 2.9 %collective-permute-start.22 = (bf16[128,384]{1,0:T(8,128)(2,1)S(1)}, bf16[128,384]{1,0:T(8,128)(2,1)S(1)}, u32[]{:S(2)}, u32[]{:S(2)}) collective-permute-start(bf16[128,384]{1,0:T(8,128)(2,1)S(1)} %get-tuple-element.71), channel_id=1, source_target_pairs={{0,1},{1,0},{2,3},{3,2},{4,5},{5,4},{6,7},{7,6},{8,9},{9,8},{10,11... | collective-permute-start | bytes 294920 | tf_op jit(solution)/shard_map/ppermute | solution.py:83
  87.2 1.3 %collective-permute-start.23 = (bf16[128,384]{1,0:T(8,128)(2,1)S(1)}, bf16[128,384]{1,0:T(8,128)(2,1)S(1)}, u32[]{:S(2)}, u32[]{:S(2)}) collective-permute-start(bf16[128,384]{1,0:T(8,128)(2,1)S(1)} %get-tuple-element.72), channel_id=1, source_target_pairs={{0,4},{1,5},{2,6},{3,7},{4,0},{5,1},{6,2},{7,3},{8,12},{9,13},{10,... | collective-permute-start | bytes 294920 | tf_op jit(solution)/shard_map/ppermute | solution.py:83
  88.6 0.4 collective-permute-start.24
  89.0 0.0 collective-permute-done.22.refs_1_
  89.0 2.7 %collective-permute-done.23.refs_2_ = bf16[128,384]{1,0:T(8,128)(2,1)S(1)} collective-permute-done((bf16[128,384]{1,0:T(8,128)(2,1)S(1)}, bf16[128,384]{1,0:T(8,128)(2,1)S(1)}, u32[]{:S(2)}, u32[]{:S(2)}) %collective-permute-start.23) | collective-permute-done | bytes 98336 | tf_op jit(solution)/shard_map/ppermute | solution.py:83
  91.6 2.3 %collective-permute-done.24.refs_3_ = bf16[128,384]{1,0:T(8,128)(2,1)S(1)} collective-permute-done((bf16[128,384]{1,0:T(8,128)(2,1)S(1)}, bf16[128,384]{1,0:T(8,128)(2,1)S(1)}, u32[]{:S(2)}, u32[]{:S(2)}) %collective-permute-start.24) | collective-permute-done | bytes 98336 | tf_op jit(solution)/shard_map/ppermute | solution.py:83
  93.9 0.9 update_rows.1
  (15 shorter events, 0.1 us)
Async XLA Ops:
  0.6 20.1 %collective-permute-start = (bf16[128,2048]{1,0:T(8,128)(2,1)}, bf16[128,2048]{1,0:T(8,128)(2,1)S(1)}, u32[]{:S(2)}, u32[]{:S(2)}) collective-permute-start(bf16[128,2048]{1,0:T(8,128)(2,1)} %bitcast.25), channel_id=1, source_target_pairs={{0,1},{1,0},{2,3},{3,2},{4,5},{5,4},{6,7},{7,6},{8,9},{9,8},{10,11... | collective-permute-start | bytes 1572872 | tf_op jit(solution)/shard_map/ppermute | solution.py:83
  0.8 10.9 %collective-permute-start.2 = (bf16[128,2048]{1,0:T(8,128)(2,1)}, bf16[128,2048]{1,0:T(8,128)(2,1)S(1)}, u32[]{:S(2)}, u32[]{:S(2)}) collective-permute-start(bf16[128,2048]{1,0:T(8,128)(2,1)} %bitcast.26), channel_id=1, source_target_pairs={{1,2},{3,4},{4,3},{6,5},{9,10},{11,12},{12,11},{14,13},{17,18},{19... | collective-permute-start | bytes 1572872 | tf_op jit(solution)/shard_map/ppermute | solution.py:273
  5.3 15.5 %collective-permute-start.1 = (bf16[128,2048]{1,0:T(8,128)(2,1)}, bf16[128,2048]{1,0:T(8,128)(2,1)S(1)}, u32[]{:S(2)}, u32[]{:S(2)}) collective-permute-start(bf16[128,2048]{1,0:T(8,128)(2,1)} %bitcast.29), channel_id=1, source_target_pairs={{0,1},{1,0},{2,3},{3,2},{4,5},{5,4},{6,7},{7,6},{8,9},{9,8},{10,11... | collective-permute-start | bytes 1572872 | tf_op jit(solution)/shard_map/ppermute | solution.py:83
  5.3 11.9 %collective-permute-start.3 = (bf16[128,2048]{1,0:T(8,128)(2,1)}, bf16[128,2048]{1,0:T(8,128)(2,1)S(1)}, u32[]{:S(2)}, u32[]{:S(2)}) collective-permute-start(bf16[128,2048]{1,0:T(8,128)(2,1)} %bitcast.30), channel_id=1, source_target_pairs={{1,2},{3,4},{4,3},{6,5},{9,10},{11,12},{12,11},{14,13},{17,18},{19... | collective-permute-start | bytes 1572872 | tf_op jit(solution)/shard_map/ppermute | solution.py:274
  8.8 11.9 %copy-start = (bf16[1,1,128,2048]{3,2,1,0:T(8,128)(2,1)S(1)}, bf16[1,1,128,2048]{3,2,1,0:T(8,128)(2,1)}, u32[]{:S(2)}) copy-start(bf16[1,1,128,2048]{3,2,1,0:T(8,128)(2,1)} %param.6) | copy-start | bytes 1572868
  8.9 11.9 %copy-start.1 = (bf16[1,1,128,2048]{3,2,1,0:T(8,128)(2,1)S(1)}, bf16[1,1,128,2048]{3,2,1,0:T(8,128)(2,1)}, u32[]{:S(2)}) copy-start(bf16[1,1,128,2048]{3,2,1,0:T(8,128)(2,1)} %param.7) | copy-start | bytes 1572868
  8.9 11.9 %copy-start.2 = (bf16[1,1,128,2048]{3,2,1,0:T(8,128)(2,1)S(1)}, bf16[1,1,128,2048]{3,2,1,0:T(8,128)(2,1)}, u32[]{:S(2)}) copy-start(bf16[1,1,128,2048]{3,2,1,0:T(8,128)(2,1)} %param.8) | copy-start | bytes 1572868
  8.9 11.9 %copy-start.4 = (s32[1,8]{1,0:T(1,128)S(1)}, s32[1,8]{1,0:T(1,128)}, u32[]{:S(2)}) copy-start(s32[1,8]{1,0:T(1,128)} %near_ref.5) | copy-start | bytes 100
  11.6 14.8 %collective-permute-start.4 = (bf16[128,1536]{1,0:T(8,128)(2,1)S(1)}, bf16[128,1536]{1,0:T(8,128)(2,1)S(1)}, u32[]{:S(2)}, u32[]{:S(2)}) collective-permute-start(bf16[128,1536]{1,0:T(8,128)(2,1)S(1)} %get-tuple-element.39), channel_id=1, source_target_pairs={{0,4},{1,5},{2,6},{3,7},{4,0},{5,1},{6,2},{7,3},{8,12},{9,13},{10,... | collective-permute-start | bytes 1179656 | tf_op jit(solution)/shard_map/ppermute | solution.py:83
  17.3 13.1 %collective-permute-start.5 = (bf16[128,1536]{1,0:T(8,128)(2,1)S(1)}, bf16[128,1536]{1,0:T(8,128)(2,1)S(1)}, u32[]{:S(2)}, u32[]{:S(2)}) collective-permute-start(bf16[128,1536]{1,0:T(8,128)(2,1)S(1)} %pad_maximum_fusion.1), channel_id=1, source_target_pairs={{0,2},{1,3},{2,0},{3,1},{4,6},{5,7},{6,4},{7,5},{8,10},{9,11},{10,... | collective-permute-start | bytes 1179656 | tf_op jit(solution)/shard_map/ppermute | solution.py:83
  23.1 13.9 %copy-start.3 = (bf16[1,1,128,2048]{3,2,1,0:T(8,128)(2,1)S(1)}, bf16[1,1,128,2048]{3,2,1,0:T(8,128)(2,1)}, u32[]{:S(2)}) copy-start(bf16[1,1,128,2048]{3,2,1,0:T(8,128)(2,1)} %param.9) | copy-start | bytes 1572868
  23.1 12.1 %collective-permute-start.10 = (bf16[2,512,128]{2,1,0:T(8,128)(2,1)S(1)}, bf16[2,512,128]{2,1,0:T(8,128)(2,1)S(1)}, u32[]{:S(2)}, u32[]{:S(2)}) collective-permute-start(bf16[2,512,128]{2,1,0:T(8,128)(2,1)S(1)} %get-tuple-element.60.refs_0_), channel_id=1, source_target_pairs={{0,2},{1,3},{2,0},{3,1},{4,6},{5,7},{6,4},{7,5},{8,10},{9,11},{10,... | collective-permute-start | bytes 786440 | tf_op jit(solution)/shard_map/ppermute | solution.py:83
  23.2 12.0 %collective-permute-start.11 = (bf16[2,512,128]{2,1,0:T(8,128)(2,1)S(1)}, bf16[2,512,128]{2,1,0:T(8,128)(2,1)S(1)}, u32[]{:S(2)}, u32[]{:S(2)}) collective-permute-start(bf16[2,512,128]{2,1,0:T(8,128)(2,1)S(1)} %get-tuple-element.78), channel_id=1, source_target_pairs={{0,4},{1,5},{2,6},{3,7},{4,0},{5,1},{6,2},{7,3},{8,12},{9,13},{10,... | collective-permute-start | bytes 786440 | tf_op jit(solution)/shard_map/ppermute | solution.py:83
  30.4 6.6 %collective-permute-start.6 = (bf16[1,128,768]{2,1,0:T(8,128)(2,1)S(1)}, bf16[1,128,768]{2,1,0:T(8,128)(2,1)S(1)}, u32[]{:S(2)}, u32[]{:S(2)}) collective-permute-start(bf16[1,128,768]{2,1,0:T(8,128)(2,1)S(1)} %get-tuple-element.83), channel_id=1, source_target_pairs={{0,4},{1,5},{2,6},{3,7},{4,0},{5,1},{6,2},{7,3},{8,12},{9,13},{10,... | collective-permute-start | bytes 589832 | tf_op jit(solution)/shard_map/ppermute | solution.py:83
  30.5 12.5 %collective-permute-start.13 = (bf16[1,128,768]{2,1,0:T(8,128)(2,1)S(1)}, bf16[1,128,768]{2,1,0:T(8,128)(2,1)S(1)}, u32[]{:S(2)}, u32[]{:S(2)}) collective-permute-start(bf16[1,128,768]{2,1,0:T(8,128)(2,1)S(1)} %get-tuple-element.82), channel_id=1, source_target_pairs={{0,4},{1,5},{2,6},{3,7},{4,0},{5,1},{6,2},{7,3},{8,12},{9,13},{10,... | collective-permute-start | bytes 589832 | tf_op jit(solution)/shard_map/ppermute | solution.py:83
  35.2 8.5 %collective-permute-start.12 = (bf16[2,512,128]{2,1,0:T(8,128)(2,1)S(1)}, bf16[2,512,128]{2,1,0:T(8,128)(2,1)S(1)}, u32[]{:S(2)}, u32[]{:S(2)}) collective-permute-start(bf16[2,512,128]{2,1,0:T(8,128)(2,1)S(1)} %collective-permute-done.11.refs_2_), channel_id=1, source_target_pairs={{0,2},{1,3},{2,0},{3,1},{4,6},{5,7},{6,4},{7,5},{8,10},{9,11},{10,... | collective-permute-start | bytes 786440 | tf_op jit(solution)/shard_map/ppermute | solution.py:83
  41.0 18.2 %collective-permute-start.7 = (bf16[2,128,2048]{2,1,0:T(8,128)(2,1)S(1)}, bf16[2,128,2048]{2,1,0:T(8,128)(2,1)S(1)}, u32[]{:S(2)}, u32[]{:S(2)}) collective-permute-start(bf16[2,128,2048]{2,1,0:T(8,128)(2,1)S(1)} %get-tuple-element.47), channel_id=1, source_target_pairs={{0,1},{1,0},{2,3},{3,2},{4,5},{5,4},{6,7},{7,6},{8,9},{9,8},{10,11... | collective-permute-start | bytes 3145736 | tf_op jit(solution)/shard_map/ppermute | solution.py:83
  44.3 1.9 %collective-permute-start.15 = (bf16[1,128,1536]{2,1,0:T(8,128)(2,1)S(1)}, bf16[1,128,1536]{2,1,0:T(8,128)(2,1)S(1)}, u32[]{:S(2)}, u32[]{:S(2)}) collective-permute-start(bf16[1,128,1536]{2,1,0:T(8,128)(2,1)S(1)} %get-tuple-element.59), channel_id=1, source_target_pairs={{0,1},{1,0},{2,3},{3,2},{4,5},{5,4},{6,7},{7,6},{8,9},{9,8},{10,11... | collective-permute-start | bytes 1179656 | tf_op jit(solution)/shard_map/ppermute | solution.py:83
  45.5 4.2 %collective-permute-start.19 = (bf16[1,128,1536]{2,1,0:T(8,128)(2,1)S(1)}, bf16[1,128,1536]{2,1,0:T(8,128)(2,1)S(1)}, u32[]{:S(2)}, u32[]{:S(2)}) collective-permute-start(bf16[1,128,1536]{2,1,0:T(8,128)(2,1)S(1)} %get-tuple-element.65), channel_id=1, source_target_pairs={{0,1},{1,0},{2,3},{3,2},{4,5},{5,4},{6,7},{7,6},{8,9},{9,8},{10,11... | collective-permute-start | bytes 1179656 | tf_op jit(solution)/shard_map/ppermute | solution.py:83
  46.3 10.4 %collective-permute-start.17 = (bf16[128,1536]{1,0:T(8,128)(2,1)S(1)}, bf16[128,1536]{1,0:T(8,128)(2,1)S(1)}, u32[]{:S(2)}, u32[]{:S(2)}) collective-permute-start(bf16[128,1536]{1,0:T(8,128)(2,1)S(1)} %block_sum.3), channel_id=1, source_target_pairs={{0,8},{8,0},{16,24},{24,16},{1,9},{9,1},{17,25},{25,17},{2,10},{10... | collective-permute-start | bytes 1179656 | tf_op jit(solution)/shard_map/ppermute | solution.py:83
  48.3 2.7 %collective-permute-start.16 = (bf16[1,128,1536]{2,1,0:T(8,128)(2,1)S(1)}, bf16[1,128,1536]{2,1,0:T(8,128)(2,1)S(1)}, u32[]{:S(2)}, u32[]{:S(2)}) collective-permute-start(bf16[1,128,1536]{2,1,0:T(8,128)(2,1)S(1)} %get-tuple-element.63), channel_id=1, source_target_pairs={{0,1},{1,0},{2,3},{3,2},{4,5},{5,4},{6,7},{7,6},{8,9},{9,8},{10,11... | collective-permute-start | bytes 1179656 | tf_op jit(solution)/shard_map/ppermute | solution.py:83
  49.6 9.6 %collective-permute-start.14 = (bf16[1,128,1536]{2,1,0:T(8,128)(2,1)S(1)}, bf16[1,128,1536]{2,1,0:T(8,128)(2,1)S(1)}, u32[]{:S(2)}, u32[]{:S(2)}) collective-permute-start(bf16[1,128,1536]{2,1,0:T(8,128)(2,1)S(1)} %get-tuple-element.57), channel_id=1, source_target_pairs={{0,1},{1,0},{2,3},{3,2},{4,5},{5,4},{6,7},{7,6},{8,9},{9,8},{10,11... | collective-permute-start | bytes 1179656 | tf_op jit(solution)/shard_map/ppermute | solution.py:83
  49.7 28.9 %collective-permute-start.8 = (bf16[128,2048]{1,0:T(8,128)(2,1)S(1)}, bf16[128,2048]{1,0:T(8,128)(2,1)S(1)}, u32[]{:S(2)}, u32[]{:S(2)}) collective-permute-start(bf16[128,2048]{1,0:T(8,128)(2,1)S(1)} %get-tuple-element.49), channel_id=1, source_target_pairs={{3,4},{5,6},{2,1},{4,3},{11,12},{13,14},{10,9},{12,11},{19,20},{21... | collective-permute-start | bytes 1572872 | tf_op jit(solution)/shard_map/ppermute | solution.py:402
  51.0 27.6 %collective-permute-start.9 = (bf16[128,2048]{1,0:T(8,128)(2,1)S(1)}, bf16[128,2048]{1,0:T(8,128)(2,1)S(1)}, u32[]{:S(2)}, u32[]{:S(2)}) collective-permute-start(bf16[128,2048]{1,0:T(8,128)(2,1)S(1)} %get-tuple-element.51), channel_id=1, source_target_pairs={{3,4},{5,6},{2,1},{4,3},{11,12},{13,14},{10,9},{12,11},{19,20},{21... | collective-permute-start | bytes 1572872 | tf_op jit(solution)/shard_map/ppermute | solution.py:403
  56.8 19.4 %collective-permute-start.18 = (bf16[128,1536]{1,0:T(8,128)(2,1)S(1)}, bf16[128,1536]{1,0:T(8,128)(2,1)S(1)}, u32[]{:S(2)}, u32[]{:S(2)}) collective-permute-start(bf16[128,1536]{1,0:T(8,128)(2,1)S(1)} %block_sum.4), channel_id=1, source_target_pairs={{0,16},{8,24},{16,0},{24,8},{1,17},{9,25},{17,1},{25,9},{2,18},{10... | collective-permute-start | bytes 1179656 | tf_op jit(solution)/shard_map/ppermute | solution.py:83
  59.2 17.0 %collective-permute-start.20 = (bf16[128,1536]{1,0:T(8,128)(2,1)S(1)}, bf16[128,1536]{1,0:T(8,128)(2,1)S(1)}, u32[]{:S(2)}, u32[]{:S(2)}) collective-permute-start(bf16[128,1536]{1,0:T(8,128)(2,1)S(1)} %block_sum.5), channel_id=1, source_target_pairs={{0,8},{8,0},{16,24},{24,16},{1,9},{9,1},{17,25},{25,17},{2,10},{10... | collective-permute-start | bytes 1179656 | tf_op jit(solution)/shard_map/ppermute | solution.py:83
  77.1 3.3 %collective-permute-start.21 = (f32[128,128]{1,0:T(8,128)S(1)}, f32[128,128]{1,0:T(8,128)S(1)}, u32[]{:S(2)}, u32[]{:S(2)}) collective-permute-start(f32[128,128]{1,0:T(8,128)S(1)} %get-tuple-element.69.gram), channel_id=1, source_target_pairs={{0,2},{1,3},{2,0},{3,1},{4,6},{5,7},{6,4},{7,5},{8,10},{9,11},{10,... | collective-permute-start | bytes 196616 | tf_op jit(solution)/shard_map/ppermute | solution.py:83
  84.4 4.6 %collective-permute-start.22 = (bf16[128,384]{1,0:T(8,128)(2,1)S(1)}, bf16[128,384]{1,0:T(8,128)(2,1)S(1)}, u32[]{:S(2)}, u32[]{:S(2)}) collective-permute-start(bf16[128,384]{1,0:T(8,128)(2,1)S(1)} %get-tuple-element.71), channel_id=1, source_target_pairs={{0,1},{1,0},{2,3},{3,2},{4,5},{5,4},{6,7},{7,6},{8,9},{9,8},{10,11... | collective-permute-start | bytes 294920 | tf_op jit(solution)/shard_map/ppermute | solution.py:83
  87.2 4.4 %collective-permute-start.23 = (bf16[128,384]{1,0:T(8,128)(2,1)S(1)}, bf16[128,384]{1,0:T(8,128)(2,1)S(1)}, u32[]{:S(2)}, u32[]{:S(2)}) collective-permute-start(bf16[128,384]{1,0:T(8,128)(2,1)S(1)} %get-tuple-element.72), channel_id=1, source_target_pairs={{0,4},{1,5},{2,6},{3,7},{4,0},{5,1},{6,2},{7,3},{8,12},{9,13},{10,... | collective-permute-start | bytes 294920 | tf_op jit(solution)/shard_map/ppermute | solution.py:83
  88.6 5.3 %collective-permute-start.24 = (bf16[128,384]{1,0:T(8,128)(2,1)S(1)}, bf16[128,384]{1,0:T(8,128)(2,1)S(1)}, u32[]{:S(2)}, u32[]{:S(2)}) collective-permute-start(bf16[128,384]{1,0:T(8,128)(2,1)S(1)} %get-tuple-element.73), channel_id=1, source_target_pairs={{0,5},{1,4},{2,7},{3,6},{4,1},{5,0},{6,3},{7,2},{8,13},{9,12},{10,... | collective-permute-start | bytes 294920 | tf_op jit(solution)/shard_map/ppermute | solution.py:83

commit v13 on v12

--- a/solution.py
+++ b/solution.py
@@ -296,7 +296,7 @@
         for q in range(1, plan.col)
     ]
     high_columns = [
-        shift(after(own_columns, key_next), "seq", high << (1 + plan.col_bits))
+        shift(own_columns, "seq", high << (1 + plan.col_bits))
         for high in range(1, plan.high)
     ]
 
@@ -318,16 +318,6 @@
     for came_high in by_high[1:]:
         there = after(came_high, *pairs[1 : plan.col])
         pairs += [came_high] + [shift(there, "seq", q << 1) for q in range(1, plan.col)]
-
-    through = lax.optimization_barrier((attended, *high_columns, jnp.stack(columns[1:])))[-1]
-    held = [jnp.stack(columns)]
-    late = []
-    for high in range(1, plan.high):
-        halves = [shift(part, "seq", high << (1 + plan.col_bits)) for part in jnp.split(through, 2, 2)]
-        late.append(halves[0])
-        rest = jnp.concatenate(halves, 2)
-        held.append(jnp.concatenate([high_columns[high - 1][None], rest], 0))
-    held = jnp.concatenate(held, 0)
 
     dq, dko, dvo, dkf, dvf, dfar = pl.pallas_call(
         backward_kernel,
@@ -343,9 +333,19 @@
         out_specs=whole(6),
         scratch_shapes=[pltpu.VMEM((2, tile, width), bf16)],
         compiler_params=params(),
-        cost_estimate=cost(28 * tile * tile * width, 30 * tile * width, 2 * tile * tile * head_count),
+        cost_estimate=cost(1, 1),
         name="attention_backward",
-    )(neighbour, query, key, value, *beside, after(grad, *late))
+    )(neighbour, query, key, value, *beside, after(grad, attended))
+
+    through = lax.optimization_barrier((dq, *high_columns, jnp.stack(columns[1:])))[-1]
+    held = [jnp.stack(columns)]
+    late = []
+    for high in range(1, plan.high):
+        halves = [shift(part, "seq", high << (1 + plan.col_bits)) for part in jnp.split(through, 2, 2)]
+        late.append(halves[0])
+        rest = jnp.concatenate(halves, 2)
+        held.append(jnp.concatenate([high_columns[high - 1][None], rest], 0))
+    held = jnp.concatenate(held, 0)
 
     def product(name, layers, *operands):
         *blocks, for_mate = pl.pallas_call(

time: 95.2 us -> 95.2 us (level)
  waiting for transfers between devices: 39.8 us -> 43.2 us
  starting transfers between devices: 35.9 us -> 32.5 us
    ppermute x21, starting transfers between devices: 25.1 us -> 21.8 us  [shift(): lax.ppermute(value, axis, [(i, i ^ mask) for i in range(lax.axis_size(axi...]
    ppermute x1, waiting for transfers between devices: 2.83 us -> 5.62 us  [local(): value_next = lax.ppermute(value, 'seq', takes)]
where the time goes in v13:
time: 95.2 us; the launch traced here: 94.8 us
  waiting for transfers between devices  43.2 us (45%)
  starting transfers between devices  32.5 us (34%)
  Pallas kernels  16.5 us (17%)
  local copies, waits for them, and re-layouts  1.47 us (2%)
    ppermute x21, waiting for transfers between devices, shift(): lax.ppermute(value, axis, [(i, i ^ mask) for i in range(lax.axis_size(axi...  36.4 us
    ppermute x21, starting transfers between devices, shift(): lax.ppermute(value, axis, [(i, i ^ mask) for i in range(lax.axis_size(axi...  21.8 us
    ppermute x1, waiting for transfers between devices, local(): value_next = lax.ppermute(value, 'seq', takes)  5.62 us
    ppermute x1, starting transfers between devices, local(): key_next = lax.ppermute(key, 'seq', takes)  4.49 us
    pallas_call x1, Pallas kernels, local(): pl.pallas_call(backward_kernel, out_shape=[struct((tile, width), bf16), s...  3.98 us
    pallas_call x1, Pallas kernels, local(): pl.pallas_call(functools.partial(update_kernel, plan, factor), out_shape=...  3.97 us
    ppermute x1, starting transfers between devices, local(): value_next = lax.ppermute(value, 'seq', takes)  3.49 us
    pallas_call x4, Pallas kernels, product(): pl.pallas_call(functools.partial(product_kernel, plan, layers), out_shape...  2.37 us
  transfers between devices with their start and end apart: 25, of which 11 were waited for; matrix products, arithmetic and copies ran while one was open for 2% of the time, Pallas kernels for 12%

profile of v13, /device:TPU:1, one launch (start us, length us, event | category | flops | bytes accessed | tf_op | source)
XLA Modules:
  0.0 94.8 jit_solution(9013149269875105838)
XLA Ops:
  0.6 0.1 collective-permute-start
  0.8 4.5 %collective-permute-start.2 = (bf16[128,2048]{1,0:T(8,128)(2,1)}, bf16[128,2048]{1,0:T(8,128)(2,1)S(1)}, u32[]{:S(2)}, u32[]{:S(2)}) collective-permute-start(bf16[128,2048]{1,0:T(8,128)(2,1)} %bitcast.26), channel_id=1, source_target_pairs={{1,2},{3,4},{4,3},{6,5},{9,10},{11,12},{12,11},{14,13},{17,18},{19... | collective-permute-start | bytes 1572872 | tf_op jit(solution)/shard_map/ppermute | solution.py:273
  5.3 0.1 collective-permute-start.1
  5.3 3.5 %collective-permute-start.3 = (bf16[128,2048]{1,0:T(8,128)(2,1)}, bf16[128,2048]{1,0:T(8,128)(2,1)S(1)}, u32[]{:S(2)}, u32[]{:S(2)}) collective-permute-start(bf16[128,2048]{1,0:T(8,128)(2,1)} %bitcast.30), channel_id=1, source_target_pairs={{1,2},{3,4},{4,3},{6,5},{9,10},{11,12},{12,11},{14,13},{17,18},{19... | collective-permute-start | bytes 1572872 | tf_op jit(solution)/shard_map/ppermute | solution.py:274
  8.9 1.4 %dynamic-slice_bitcast_fusion.1 = (bf16[128,768]{1,0:T(8,128)(2,1)S(1)}, bf16[128,768]{1,0:T(8,128)(2,1)S(1)}, bf16[128,768]{1,0:T(8,128)(2,1)S(1)}, bf16[128,768]{1,0:T(8,128)(2,1)S(1)}) fusion(bf16[1,1,128,3072]{3,2,1,0:T(8,128)(2,1)} %param.10, s32[]{:T(128)S(6)} %select_n.14, s32[]{:T(128)S(6)} %select_n.13, s32[]{:T(128)S(6)} %select_n.12, s32[]{:T(128)S(6)} %select_n.15), kind=kLoop, calls=%fused_computation.6 | loop fusion | bytes 1572880 | tf_op jit(solution)/shard_map/dynamic_slice | solution.py:287
  10.3 0.1 fusion
  10.3 0.1 collective-permute-start.11
  10.5 1.2 %collective-permute-done.2.kn = bf16[128,2048]{1,0:T(8,128)(2,1)S(1)} collective-permute-done((bf16[128,2048]{1,0:T(8,128)(2,1)}, bf16[128,2048]{1,0:T(8,128)(2,1)S(1)}, u32[]{:S(2)}, u32[]{:S(2)}) %collective-permute-start.2) | collective-permute-done | bytes 524320 | tf_op jit(solution)/shard_map/ppermute | solution.py:273
  11.6 5.6 %collective-permute-done.3.vn = bf16[128,2048]{1,0:T(8,128)(2,1)S(1)} collective-permute-done((bf16[128,2048]{1,0:T(8,128)(2,1)}, bf16[128,2048]{1,0:T(8,128)(2,1)S(1)}, u32[]{:S(2)}, u32[]{:S(2)}) %collective-permute-start.3) | collective-permute-done | bytes 524320 | tf_op jit(solution)/shard_map/ppermute | solution.py:274
  17.3 3.5 %collective-permute-start.10 = (bf16[128,1536]{1,0:T(8,128)(2,1)S(1)}, bf16[128,1536]{1,0:T(8,128)(2,1)S(1)}, u32[]{:S(2)}, u32[]{:S(2)}) collective-permute-start(bf16[128,1536]{1,0:T(8,128)(2,1)S(1)} %pad_maximum_fusion.1), channel_id=1, source_target_pairs={{0,2},{1,3},{2,0},{3,1},{4,6},{5,7},{6,4},{7,5},{8,10},{9,11},{10,... | collective-permute-start | bytes 1179656 | tf_op jit(solution)/shard_map/ppermute | solution.py:83
  20.7 0.0 collective-permute-done.km
  20.7 0.0 collective-permute-done.1.vm
  20.8 0.0 copy-start.3
  20.8 2.3 %attention_forward.1 = bf16[2,2,512,128]{3,2,1,0:T(8,128)(2,1)S(1)} custom-call(s32[1,8]{1,0:T(1,128)S(1)} %copy-done.4, bf16[128,2048]{1,0:T(8,128)(2,1)S(1)} %bitcast.23, bf16[128,2048]{1,0:T(8,128)(2,1)S(1)} %bitcast.27, bf16[128,2048]{1,0:T(8,128)(2,1)S(1)} %bitcast.31, bf16[128,2048]{1,0:T(8,128)(2,1)S(1)} %collective-permute-done.km, ...), custom_call_target="tpu_custom_call" | custom-call | flops 268435456 | bytes 4194304 | tf_op jit(solution)/shard_map/attention_forward/pallas_call | solution.py:303
  23.1 0.1 collective-permute-start.7
  23.2 0.8 collective-permute-start.8
  24.0 4.0 %attention_backward.1 = (bf16[128,2048]{1,0:T(8,128)(2,1)}, f32[128,2048]{1,0:T(8,128)S(1)}, f32[128,2048]{1,0:T(8,128)S(1)}, bf16[128,2048]{1,0:T(8,128)(2,1)S(...) custom-call(s32[1,8]{1,0:T(1,128)S(1)} %copy-done.4, bf16[128,2048]{1,0:T(8,128)(2,1)S(1)} %bitcast.24, ...), custom_call_target="tpu_custom_call" | custom-call | flops 1 | bytes 1 | tf_op jit(solution)/shard_map/attention_backward/pallas_call | solution.py:322
  28.0 0.0 collective-permute-done.11
  28.0 2.4 %collective-permute-done.10 = bf16[128,1536]{1,0:T(8,128)(2,1)S(1)} collective-permute-done((bf16[128,1536]{1,0:T(8,128)(2,1)S(1)}, bf16[128,1536]{1,0:T(8,128)(2,1)S(1)}, u32[]{:S(2)}, u32[]{:S(2)}) %collective-permute-start.10) | collective-permute-done | bytes 393248 | tf_op jit(solution)/shard_map/ppermute | solution.py:83
  30.4 0.1 collective-permute-start.13
  30.5 1.5 %collective-permute-start.12 = (bf16[1,128,768]{2,1,0:T(8,128)(2,1)S(1)}, bf16[1,128,768]{2,1,0:T(8,128)(2,1)S(1)}, u32[]{:S(2)}, u32[]{:S(2)}) collective-permute-start(bf16[1,128,768]{2,1,0:T(8,128)(2,1)S(1)} %get-tuple-element.80), channel_id=1, source_target_pairs={{0,4},{1,5},{2,6},{3,7},{4,0},{5,1},{6,2},{7,3},{8,12},{9,13},{10,... | collective-permute-start | bytes 589832 | tf_op jit(solution)/shard_map/ppermute | solution.py:83
  31.9 1.3 %collective-permute-start.4 = (bf16[2,128,2048]{2,1,0:T(8,128)(2,1)S(1)}, bf16[2,128,2048]{2,1,0:T(8,128)(2,1)S(1)}, u32[]{:S(2)}, u32[]{:S(2)}) collective-permute-start(bf16[2,128,2048]{2,1,0:T(8,128)(2,1)S(1)} %get-tuple-element.43), channel_id=1, source_target_pairs={{0,1},{1,0},{2,3},{3,2},{4,5},{5,4},{6,7},{7,6},{8,9},{9,8},{10,11... | collective-permute-start | bytes 3145736 | tf_op jit(solution)/shard_map/ppermute | solution.py:83
  33.3 2.0 %collective-permute-done.7.refs_1_ = bf16[2,512,128]{2,1,0:T(8,128)(2,1)S(1)} collective-permute-done((bf16[2,512,128]{2,1,0:T(8,128)(2,1)S(1)}, bf16[2,512,128]{2,1,0:T(8,128)(2,1)S(1)}, u32[]{:S(2)}, u32[]{:S(2)}) %collective-permute-start.7) | collective-permute-done | bytes 262176 | tf_op jit(solution)/shard_map/ppermute | solution.py:83
  35.2 0.0 collective-permute-done.8.refs_2_
  35.2 1.7 %collective-permute-start.9 = (bf16[2,512,128]{2,1,0:T(8,128)(2,1)S(1)}, bf16[2,512,128]{2,1,0:T(8,128)(2,1)S(1)}, u32[]{:S(2)}, u32[]{:S(2)}) collective-permute-start(bf16[2,512,128]{2,1,0:T(8,128)(2,1)S(1)} %collective-permute-done.8.refs_2_), channel_id=1, source_target_pairs={{0,2},{1,3},{2,0},{3,1},{4,6},{5,7},{6,4},{7,5},{8,10},{9,11},{10,... | collective-permute-start | bytes 786440 | tf_op jit(solution)/shard_map/ppermute | solution.py:83
  37.0 0.0 collective-permute-done.13
  37.0 3.5 %collective-permute-done.12 = bf16[1,128,768]{2,1,0:T(8,128)(2,1)S(1)} collective-permute-done((bf16[1,128,768]{2,1,0:T(8,128)(2,1)S(1)}, bf16[1,128,768]{2,1,0:T(8,128)(2,1)S(1)}, u32[]{:S(2)}, u32[]{:S(2)}) %collective-permute-start.12) | collective-permute-done | bytes 196640 | tf_op jit(solution)/shard_map/ppermute | solution.py:83
  40.4 0.1 maximum_maximum_fusion.refs_4_
  40.6 3.1 %collective-permute-done.9.refs_3_ = bf16[2,512,128]{2,1,0:T(8,128)(2,1)S(1)} collective-permute-done((bf16[2,512,128]{2,1,0:T(8,128)(2,1)S(1)}, bf16[2,512,128]{2,1,0:T(8,128)(2,1)S(1)}, u32[]{:S(2)}, u32[]{:S(2)}) %collective-permute-start.9) | collective-permute-done | bytes 262176 | tf_op jit(solution)/shard_map/ppermute | solution.py:83
  43.7 0.6 product_first.1
  44.3 0.6 collective-permute-start.15
  44.9 0.6 product_near.1
  45.5 0.1 collective-permute-start.19
  45.6 0.7 collective-permute-done.15.refs_1_
  46.3 0.1 block_sum.3
  46.3 1.4 %collective-permute-start.17 = (bf16[128,1536]{1,0:T(8,128)(2,1)S(1)}, bf16[128,1536]{1,0:T(8,128)(2,1)S(1)}, u32[]{:S(2)}, u32[]{:S(2)}) collective-permute-start(bf16[128,1536]{1,0:T(8,128)(2,1)S(1)} %block_sum.3), channel_id=1, source_target_pairs={{0,8},{8,0},{16,24},{24,16},{1,9},{9,1},{17,25},{25,17},{2,10},{10... | collective-permute-start | bytes 1179656 | tf_op jit(solution)/shard_map/ppermute | solution.py:83
  47.7 0.6 product_middle.1
  48.3 0.7 collective-permute-start.16
  49.0 0.6 product_own.1
  49.6 0.1 collective-permute-start.14
  49.7 0.0 collective-permute-done.19.refs_1_
  49.7 1.3 %collective-permute-start.5 = (bf16[128,2048]{1,0:T(8,128)(2,1)S(1)}, bf16[128,2048]{1,0:T(8,128)(2,1)S(1)}, u32[]{:S(2)}, u32[]{:S(2)}) collective-permute-start(bf16[128,2048]{1,0:T(8,128)(2,1)S(1)} %get-tuple-element.45), channel_id=1, source_target_pairs={{3,4},{5,6},{2,1},{4,3},{11,12},{13,14},{10,9},{12,11},{19,20},{21... | collective-permute-start | bytes 1572872 | tf_op jit(solution)/shard_map/ppermute | solution.py:402
  51.0 0.0 collective-permute-done.16.refs_1_
  51.0 1.5 %collective-permute-start.6 = (bf16[128,2048]{1,0:T(8,128)(2,1)S(1)}, bf16[128,2048]{1,0:T(8,128)(2,1)S(1)}, u32[]{:S(2)}, u32[]{:S(2)}) collective-permute-start(bf16[128,2048]{1,0:T(8,128)(2,1)S(1)} %get-tuple-element.47), channel_id=1, source_target_pairs={{3,4},{5,6},{2,1},{4,3},{11,12},{13,14},{10,9},{12,11},{19,20},{21... | collective-permute-start | bytes 1572872 | tf_op jit(solution)/shard_map/ppermute | solution.py:403
  52.5 0.1 block_sum.5
  52.6 4.1 %collective-permute-done.17.refs_2_ = bf16[128,1536]{1,0:T(8,128)(2,1)S(1)} collective-permute-done((bf16[128,1536]{1,0:T(8,128)(2,1)S(1)}, bf16[128,1536]{1,0:T(8,128)(2,1)S(1)}, u32[]{:S(2)}, u32[]{:S(2)}) %collective-permute-start.17) | collective-permute-done | bytes 393248 | tf_op jit(solution)/shard_map/ppermute | solution.py:83
  56.7 0.1 block_sum.4
  56.8 2.4 %collective-permute-start.18 = (bf16[128,1536]{1,0:T(8,128)(2,1)S(1)}, bf16[128,1536]{1,0:T(8,128)(2,1)S(1)}, u32[]{:S(2)}, u32[]{:S(2)}) collective-permute-start(bf16[128,1536]{1,0:T(8,128)(2,1)S(1)} %block_sum.4), channel_id=1, source_target_pairs={{0,16},{8,24},{16,0},{24,8},{1,17},{9,25},{17,1},{25,9},{2,18},{10... | collective-permute-start | bytes 1179656 | tf_op jit(solution)/shard_map/ppermute | solution.py:83
  59.2 0.0 collective-permute-done.14.refs_0_
  59.2 1.3 %collective-permute-start.20 = (bf16[128,1536]{1,0:T(8,128)(2,1)S(1)}, bf16[128,1536]{1,0:T(8,128)(2,1)S(1)}, u32[]{:S(2)}, u32[]{:S(2)}) collective-permute-start(bf16[128,1536]{1,0:T(8,128)(2,1)S(1)} %block_sum.5), channel_id=1, source_target_pairs={{0,8},{8,0},{16,24},{24,16},{1,9},{9,1},{17,25},{25,17},{2,10},{10... | collective-permute-start | bytes 1179656 | tf_op jit(solution)/shard_map/ppermute | solution.py:83
  60.5 15.7 %collective-permute-done.18.refs_1_ = bf16[128,1536]{1,0:T(8,128)(2,1)S(1)} collective-permute-done((bf16[128,1536]{1,0:T(8,128)(2,1)S(1)}, bf16[128,1536]{1,0:T(8,128)(2,1)S(1)}, u32[]{:S(2)}, u32[]{:S(2)}) %collective-permute-start.18) | collective-permute-done | bytes 393248 | tf_op jit(solution)/shard_map/ppermute | solution.py:83
  76.2 0.8 gradient_sum.1
  77.1 1.5 %collective-permute-start.21 = (f32[128,128]{1,0:T(8,128)S(1)}, f32[128,128]{1,0:T(8,128)S(1)}, u32[]{:S(2)}, u32[]{:S(2)}) collective-permute-start(f32[128,128]{1,0:T(8,128)S(1)} %get-tuple-element.67.gram), channel_id=1, source_target_pairs={{0,2},{1,3},{2,0},{3,1},{4,6},{5,7},{6,4},{7,5},{8,10},{9,11},{10,... | collective-permute-start | bytes 196616 | tf_op jit(solution)/shard_map/ppermute | solution.py:83
  78.6 0.0 collective-permute-done.5.kn
  78.6 0.0 collective-permute-done.6.vn
  78.6 1.8 %key_value_sum.1 = (bf16[128,2048]{1,0:T(8,128)(2,1)}, bf16[128,2048]{1,0:T(8,128)(2,1)}) custom-call(s32[1,8]{1,0:T(1,128)S(1)} %copy-done.4, f32[128,2048]{1,0:T(8,128)S(1)} %get-tuple-element.40.dko, f32[128,2048]{1,0:T(8,128)S(1)} %get-tuple-element.41.dvo, bf16[2,128,2048]{2,1,0:T(8,128)(2,1)S(1)} %collective-permute-done.4.mate, ...), custom_call_target="tpu_custom_call" | custom-call | flops 1572864 | bytes 5242880 | tf_op jit(solution)/shard_map/key_value_sum/pallas_call | solution.py:412
  80.4 4.0 %newton_schulz.1 = (f32[128,384]{1,0:T(8,128)S(1)}, bf16[128,384]{1,0:T(8,128)(2,1)S(1)}, bf16[128,384]{1,0:T(8,128)(2,1)S(1)}, bf16[128,384]{1,0:T(8,128)(2,1)S(1)}) custom-call(f32[128,1536]{1,0:T(8,128)S(1)} %get-tuple-element.66.x, f32[128,128]{1,0:T(8,128)S(1)} %get-tuple-element.67.gram, f32[128,128]{1,0:T(8,128)S(1)} %collective-permute-done.21.gram_other), custom_call_target="tpu_custom_call" | custom-call | flops 301989888 | bytes 1572864 | tf_op jit(solution)/shard_map/newton_schulz/pallas_call | solution.py:443
  84.4 2.9 %collective-permute-start.22 = (bf16[128,384]{1,0:T(8,128)(2,1)S(1)}, bf16[128,384]{1,0:T(8,128)(2,1)S(1)}, u32[]{:S(2)}, u32[]{:S(2)}) collective-permute-start(bf16[128,384]{1,0:T(8,128)(2,1)S(1)} %get-tuple-element.69), channel_id=1, source_target_pairs={{0,1},{1,0},{2,3},{3,2},{4,5},{5,4},{6,7},{7,6},{8,9},{9,8},{10,11... | collective-permute-start | bytes 294920 | tf_op jit(solution)/shard_map/ppermute | solution.py:83
  87.2 0.1 collective-permute-start.23
  87.3 1.6 %collective-permute-start.24 = (bf16[128,384]{1,0:T(8,128)(2,1)S(1)}, bf16[128,384]{1,0:T(8,128)(2,1)S(1)}, u32[]{:S(2)}, u32[]{:S(2)}) collective-permute-start(bf16[128,384]{1,0:T(8,128)(2,1)S(1)} %get-tuple-element.71), channel_id=1, source_target_pairs={{0,5},{1,4},{2,7},{3,6},{4,1},{5,0},{6,3},{7,2},{8,13},{9,12},{10,... | collective-permute-start | bytes 294920 | tf_op jit(solution)/shard_map/ppermute | solution.py:83
  89.0 0.0 collective-permute-done.22.refs_1_
  89.0 2.7 %collective-permute-done.23.refs_2_ = bf16[128,384]{1,0:T(8,128)(2,1)S(1)} collective-permute-done((bf16[128,384]{1,0:T(8,128)(2,1)S(1)}, bf16[128,384]{1,0:T(8,128)(2,1)S(1)}, u32[]{:S(2)}, u32[]{:S(2)}) %collective-permute-start.23) | collective-permute-done | bytes 98336 | tf_op jit(solution)/shard_map/ppermute | solution.py:83
  91.6 2.3 %collective-permute-done.24.refs_3_ = bf16[128,384]{1,0:T(8,128)(2,1)S(1)} collective-permute-done((bf16[128,384]{1,0:T(8,128)(2,1)S(1)}, bf16[128,384]{1,0:T(8,128)(2,1)S(1)}, u32[]{:S(2)}, u32[]{:S(2)}) %collective-permute-start.24) | collective-permute-done | bytes 98336 | tf_op jit(solution)/shard_map/ppermute | solution.py:83
  93.9 0.9 update_rows.1
  (15 shorter events, 0.1 us)
Async XLA Ops:
  0.6 20.1 %collective-permute-start = (bf16[128,2048]{1,0:T(8,128)(2,1)}, bf16[128,2048]{1,0:T(8,128)(2,1)S(1)}, u32[]{:S(2)}, u32[]{:S(2)}) collective-permute-start(bf16[128,2048]{1,0:T(8,128)(2,1)} %bitcast.25), channel_id=1, source_target_pairs={{0,1},{1,0},{2,3},{3,2},{4,5},{5,4},{6,7},{7,6},{8,9},{9,8},{10,11... | collective-permute-start | bytes 1572872 | tf_op jit(solution)/shard_map/ppermute | solution.py:83
  0.8 10.9 %collective-permute-start.2 = (bf16[128,2048]{1,0:T(8,128)(2,1)}, bf16[128,2048]{1,0:T(8,128)(2,1)S(1)}, u32[]{:S(2)}, u32[]{:S(2)}) collective-permute-start(bf16[128,2048]{1,0:T(8,128)(2,1)} %bitcast.26), channel_id=1, source_target_pairs={{1,2},{3,4},{4,3},{6,5},{9,10},{11,12},{12,11},{14,13},{17,18},{19... | collective-permute-start | bytes 1572872 | tf_op jit(solution)/shard_map/ppermute | solution.py:273
  5.3 15.5 %collective-permute-start.1 = (bf16[128,2048]{1,0:T(8,128)(2,1)}, bf16[128,2048]{1,0:T(8,128)(2,1)S(1)}, u32[]{:S(2)}, u32[]{:S(2)}) collective-permute-start(bf16[128,2048]{1,0:T(8,128)(2,1)} %bitcast.29), channel_id=1, source_target_pairs={{0,1},{1,0},{2,3},{3,2},{4,5},{5,4},{6,7},{7,6},{8,9},{9,8},{10,11... | collective-permute-start | bytes 1572872 | tf_op jit(solution)/shard_map/ppermute | solution.py:83
  5.3 11.9 %collective-permute-start.3 = (bf16[128,2048]{1,0:T(8,128)(2,1)}, bf16[128,2048]{1,0:T(8,128)(2,1)S(1)}, u32[]{:S(2)}, u32[]{:S(2)}) collective-permute-start(bf16[128,2048]{1,0:T(8,128)(2,1)} %bitcast.30), channel_id=1, source_target_pairs={{1,2},{3,4},{4,3},{6,5},{9,10},{11,12},{12,11},{14,13},{17,18},{19... | collective-permute-start | bytes 1572872 | tf_op jit(solution)/shard_map/ppermute | solution.py:274
  8.8 11.9 %copy-start = (bf16[1,1,128,2048]{3,2,1,0:T(8,128)(2,1)S(1)}, bf16[1,1,128,2048]{3,2,1,0:T(8,128)(2,1)}, u32[]{:S(2)}) copy-start(bf16[1,1,128,2048]{3,2,1,0:T(8,128)(2,1)} %param.6) | copy-start | bytes 1572868
  8.9 11.9 %copy-start.1 = (bf16[1,1,128,2048]{3,2,1,0:T(8,128)(2,1)S(1)}, bf16[1,1,128,2048]{3,2,1,0:T(8,128)(2,1)}, u32[]{:S(2)}) copy-start(bf16[1,1,128,2048]{3,2,1,0:T(8,128)(2,1)} %param.7) | copy-start | bytes 1572868
  8.9 11.9 %copy-start.2 = (bf16[1,1,128,2048]{3,2,1,0:T(8,128)(2,1)S(1)}, bf16[1,1,128,2048]{3,2,1,0:T(8,128)(2,1)}, u32[]{:S(2)}) copy-start(bf16[1,1,128,2048]{3,2,1,0:T(8,128)(2,1)} %param.8) | copy-start | bytes 1572868
  8.9 11.9 %copy-start.4 = (s32[1,8]{1,0:T(1,128)S(1)}, s32[1,8]{1,0:T(1,128)}, u32[]{:S(2)}) copy-start(s32[1,8]{1,0:T(1,128)} %near_ref.5) | copy-start | bytes 100
  10.3 17.6 %collective-permute-start.11 = (bf16[128,1536]{1,0:T(8,128)(2,1)S(1)}, bf16[128,1536]{1,0:T(8,128)(2,1)S(1)}, u32[]{:S(2)}, u32[]{:S(2)}) collective-permute-start(bf16[128,1536]{1,0:T(8,128)(2,1)S(1)} %get-tuple-element.79), channel_id=1, source_target_pairs={{0,4},{1,5},{2,6},{3,7},{4,0},{5,1},{6,2},{7,3},{8,12},{9,13},{10,... | collective-permute-start | bytes 1179656 | tf_op jit(solution)/shard_map/ppermute | solution.py:83
  17.3 13.1 %collective-permute-start.10 = (bf16[128,1536]{1,0:T(8,128)(2,1)S(1)}, bf16[128,1536]{1,0:T(8,128)(2,1)S(1)}, u32[]{:S(2)}, u32[]{:S(2)}) collective-permute-start(bf16[128,1536]{1,0:T(8,128)(2,1)S(1)} %pad_maximum_fusion.1), channel_id=1, source_target_pairs={{0,2},{1,3},{2,0},{3,1},{4,6},{5,7},{6,4},{7,5},{8,10},{9,11},{10,... | collective-permute-start | bytes 1179656 | tf_op jit(solution)/shard_map/ppermute | solution.py:83
  20.8 3.2 %copy-start.3 = (bf16[1,1,128,2048]{3,2,1,0:T(8,128)(2,1)S(1)}, bf16[1,1,128,2048]{3,2,1,0:T(8,128)(2,1)}, u32[]{:S(2)}) copy-start(bf16[1,1,128,2048]{3,2,1,0:T(8,128)(2,1)} %param.9) | copy-start | bytes 1572868
  23.1 12.1 %collective-permute-start.7 = (bf16[2,512,128]{2,1,0:T(8,128)(2,1)S(1)}, bf16[2,512,128]{2,1,0:T(8,128)(2,1)S(1)}, u32[]{:S(2)}, u32[]{:S(2)}) collective-permute-start(bf16[2,512,128]{2,1,0:T(8,128)(2,1)S(1)} %get-tuple-element.58.refs_0_), channel_id=1, source_target_pairs={{0,2},{1,3},{2,0},{3,1},{4,6},{5,7},{6,4},{7,5},{8,10},{9,11},{10,... | collective-permute-start | bytes 786440 | tf_op jit(solution)/shard_map/ppermute | solution.py:83
  23.2 12.0 %collective-permute-start.8 = (bf16[2,512,128]{2,1,0:T(8,128)(2,1)S(1)}, bf16[2,512,128]{2,1,0:T(8,128)(2,1)S(1)}, u32[]{:S(2)}, u32[]{:S(2)}) collective-permute-start(bf16[2,512,128]{2,1,0:T(8,128)(2,1)S(1)} %get-tuple-element.76), channel_id=1, source_target_pairs={{0,4},{1,5},{2,6},{3,7},{4,0},{5,1},{6,2},{7,3},{8,12},{9,13},{10,... | collective-permute-start | bytes 786440 | tf_op jit(solution)/shard_map/ppermute | solution.py:83
  30.4 6.6 %collective-permute-start.13 = (bf16[1,128,768]{2,1,0:T(8,128)(2,1)S(1)}, bf16[1,128,768]{2,1,0:T(8,128)(2,1)S(1)}, u32[]{:S(2)}, u32[]{:S(2)}) collective-permute-start(bf16[1,128,768]{2,1,0:T(8,128)(2,1)S(1)} %get-tuple-element.81), channel_id=1, source_target_pairs={{0,4},{1,5},{2,6},{3,7},{4,0},{5,1},{6,2},{7,3},{8,12},{9,13},{10,... | collective-permute-start | bytes 589832 | tf_op jit(solution)/shard_map/ppermute | solution.py:83
  30.5 10.0 %collective-permute-start.12 = (bf16[1,128,768]{2,1,0:T(8,128)(2,1)S(1)}, bf16[1,128,768]{2,1,0:T(8,128)(2,1)S(1)}, u32[]{:S(2)}, u32[]{:S(2)}) collective-permute-start(bf16[1,128,768]{2,1,0:T(8,128)(2,1)S(1)} %get-tuple-element.80), channel_id=1, source_target_pairs={{0,4},{1,5},{2,6},{3,7},{4,0},{5,1},{6,2},{7,3},{8,12},{9,13},{10,... | collective-permute-start | bytes 589832 | tf_op jit(solution)/shard_map/ppermute | solution.py:83
  31.9 27.3 %collective-permute-start.4 = (bf16[2,128,2048]{2,1,0:T(8,128)(2,1)S(1)}, bf16[2,128,2048]{2,1,0:T(8,128)(2,1)S(1)}, u32[]{:S(2)}, u32[]{:S(2)}) collective-permute-start(bf16[2,128,2048]{2,1,0:T(8,128)(2,1)S(1)} %get-tuple-element.43), channel_id=1, source_target_pairs={{0,1},{1,0},{2,3},{3,2},{4,5},{5,4},{6,7},{7,6},{8,9},{9,8},{10,11... | collective-permute-start | bytes 3145736 | tf_op jit(solution)/shard_map/ppermute | solution.py:83
  35.2 8.5 %collective-permute-start.9 = (bf16[2,512,128]{2,1,0:T(8,128)(2,1)S(1)}, bf16[2,512,128]{2,1,0:T(8,128)(2,1)S(1)}, u32[]{:S(2)}, u32[]{:S(2)}) collective-permute-start(bf16[2,512,128]{2,1,0:T(8,128)(2,1)S(1)} %collective-permute-done.8.refs_2_), channel_id=1, source_target_pairs={{0,2},{1,3},{2,0},{3,1},{4,6},{5,7},{6,4},{7,5},{8,10},{9,11},{10,... | collective-permute-start | bytes 786440 | tf_op jit(solution)/shard_map/ppermute | solution.py:83
  44.3 1.9 %collective-permute-start.15 = (bf16[1,128,1536]{2,1,0:T(8,128)(2,1)S(1)}, bf16[1,128,1536]{2,1,0:T(8,128)(2,1)S(1)}, u32[]{:S(2)}, u32[]{:S(2)}) collective-permute-start(bf16[1,128,1536]{2,1,0:T(8,128)(2,1)S(1)} %get-tuple-element.57), channel_id=1, source_target_pairs={{0,1},{1,0},{2,3},{3,2},{4,5},{5,4},{6,7},{7,6},{8,9},{9,8},{10,11... | collective-permute-start | bytes 1179656 | tf_op jit(solution)/shard_map/ppermute | solution.py:83
  45.5 4.2 %collective-permute-start.19 = (bf16[1,128,1536]{2,1,0:T(8,128)(2,1)S(1)}, bf16[1,128,1536]{2,1,0:T(8,128)(2,1)S(1)}, u32[]{:S(2)}, u32[]{:S(2)}) collective-permute-start(bf16[1,128,1536]{2,1,0:T(8,128)(2,1)S(1)} %get-tuple-element.63), channel_id=1, source_target_pairs={{0,1},{1,0},{2,3},{3,2},{4,5},{5,4},{6,7},{7,6},{8,9},{9,8},{10,11... | collective-permute-start | bytes 1179656 | tf_op jit(solution)/shard_map/ppermute | solution.py:83
  46.3 10.4 %collective-permute-start.17 = (bf16[128,1536]{1,0:T(8,128)(2,1)S(1)}, bf16[128,1536]{1,0:T(8,128)(2,1)S(1)}, u32[]{:S(2)}, u32[]{:S(2)}) collective-permute-start(bf16[128,1536]{1,0:T(8,128)(2,1)S(1)} %block_sum.3), channel_id=1, source_target_pairs={{0,8},{8,0},{16,24},{24,16},{1,9},{9,1},{17,25},{25,17},{2,10},{10... | collective-permute-start | bytes 1179656 | tf_op jit(solution)/shard_map/ppermute | solution.py:83
  48.3 2.7 %collective-permute-start.16 = (bf16[1,128,1536]{2,1,0:T(8,128)(2,1)S(1)}, bf16[1,128,1536]{2,1,0:T(8,128)(2,1)S(1)}, u32[]{:S(2)}, u32[]{:S(2)}) collective-permute-start(bf16[1,128,1536]{2,1,0:T(8,128)(2,1)S(1)} %get-tuple-element.61), channel_id=1, source_target_pairs={{0,1},{1,0},{2,3},{3,2},{4,5},{5,4},{6,7},{7,6},{8,9},{9,8},{10,11... | collective-permute-start | bytes 1179656 | tf_op jit(solution)/shard_map/ppermute | solution.py:83
  49.6 9.6 %collective-permute-start.14 = (bf16[1,128,1536]{2,1,0:T(8,128)(2,1)S(1)}, bf16[1,128,1536]{2,1,0:T(8,128)(2,1)S(1)}, u32[]{:S(2)}, u32[]{:S(2)}) collective-permute-start(bf16[1,128,1536]{2,1,0:T(8,128)(2,1)S(1)} %get-tuple-element.55), channel_id=1, source_target_pairs={{0,1},{1,0},{2,3},{3,2},{4,5},{5,4},{6,7},{7,6},{8,9},{9,8},{10,11... | collective-permute-start | bytes 1179656 | tf_op jit(solution)/shard_map/ppermute | solution.py:83
  49.7 28.9 %collective-permute-start.5 = (bf16[128,2048]{1,0:T(8,128)(2,1)S(1)}, bf16[128,2048]{1,0:T(8,128)(2,1)S(1)}, u32[]{:S(2)}, u32[]{:S(2)}) collective-permute-start(bf16[128,2048]{1,0:T(8,128)(2,1)S(1)} %get-tuple-element.45), channel_id=1, source_target_pairs={{3,4},{5,6},{2,1},{4,3},{11,12},{13,14},{10,9},{12,11},{19,20},{21... | collective-permute-start | bytes 1572872 | tf_op jit(solution)/shard_map/ppermute | solution.py:402
  51.0 27.6 %collective-permute-start.6 = (bf16[128,2048]{1,0:T(8,128)(2,1)S(1)}, bf16[128,2048]{1,0:T(8,128)(2,1)S(1)}, u32[]{:S(2)}, u32[]{:S(2)}) collective-permute-start(bf16[128,2048]{1,0:T(8,128)(2,1)S(1)} %get-tuple-element.47), channel_id=1, source_target_pairs={{3,4},{5,6},{2,1},{4,3},{11,12},{13,14},{10,9},{12,11},{19,20},{21... | collective-permute-start | bytes 1572872 | tf_op jit(solution)/shard_map/ppermute | solution.py:403
  56.8 19.4 %collective-permute-start.18 = (bf16[128,1536]{1,0:T(8,128)(2,1)S(1)}, bf16[128,1536]{1,0:T(8,128)(2,1)S(1)}, u32[]{:S(2)}, u32[]{:S(2)}) collective-permute-start(bf16[128,1536]{1,0:T(8,128)(2,1)S(1)} %block_sum.4), channel_id=1, source_target_pairs={{0,16},{8,24},{16,0},{24,8},{1,17},{9,25},{17,1},{25,9},{2,18},{10... | collective-permute-start | bytes 1179656 | tf_op jit(solution)/shard_map/ppermute | solution.py:83
  59.2 17.0 %collective-permute-start.20 = (bf16[128,1536]{1,0:T(8,128)(2,1)S(1)}, bf16[128,1536]{1,0:T(8,128)(2,1)S(1)}, u32[]{:S(2)}, u32[]{:S(2)}) collective-permute-start(bf16[128,1536]{1,0:T(8,128)(2,1)S(1)} %block_sum.5), channel_id=1, source_target_pairs={{0,8},{8,0},{16,24},{24,16},{1,9},{9,1},{17,25},{25,17},{2,10},{10... | collective-permute-start | bytes 1179656 | tf_op jit(solution)/shard_map/ppermute | solution.py:83
  77.1 3.4 %collective-permute-start.21 = (f32[128,128]{1,0:T(8,128)S(1)}, f32[128,128]{1,0:T(8,128)S(1)}, u32[]{:S(2)}, u32[]{:S(2)}) collective-permute-start(f32[128,128]{1,0:T(8,128)S(1)} %get-tuple-element.67.gram), channel_id=1, source_target_pairs={{0,2},{1,3},{2,0},{3,1},{4,6},{5,7},{6,4},{7,5},{8,10},{9,11},{10,... | collective-permute-start | bytes 196616 | tf_op jit(solution)/shard_map/ppermute | solution.py:83
  84.4 4.6 %collective-permute-start.22 = (bf16[128,384]{1,0:T(8,128)(2,1)S(1)}, bf16[128,384]{1,0:T(8,128)(2,1)S(1)}, u32[]{:S(2)}, u32[]{:S(2)}) collective-permute-start(bf16[128,384]{1,0:T(8,128)(2,1)S(1)} %get-tuple-element.69), channel_id=1, source_target_pairs={{0,1},{1,0},{2,3},{3,2},{4,5},{5,4},{6,7},{7,6},{8,9},{9,8},{10,11... | collective-permute-start | bytes 294920 | tf_op jit(solution)/shard_map/ppermute | solution.py:83
  87.2 4.4 %collective-permute-start.23 = (bf16[128,384]{1,0:T(8,128)(2,1)S(1)}, bf16[128,384]{1,0:T(8,128)(2,1)S(1)}, u32[]{:S(2)}, u32[]{:S(2)}) collective-permute-start(bf16[128,384]{1,0:T(8,128)(2,1)S(1)} %get-tuple-element.70), channel_id=1, source_target_pairs={{0,4},{1,5},{2,6},{3,7},{4,0},{5,1},{6,2},{7,3},{8,12},{9,13},{10,... | collective-permute-start | bytes 294920 | tf_op jit(solution)/shard_map/ppermute | solution.py:83
  87.3 6.6 %collective-permute-start.24 = (bf16[128,384]{1,0:T(8,128)(2,1)S(1)}, bf16[128,384]{1,0:T(8,128)(2,1)S(1)}, u32[]{:S(2)}, u32[]{:S(2)}) collective-permute-start(bf16[128,384]{1,0:T(8,128)(2,1)S(1)} %get-tuple-element.71), channel_id=1, source_target_pairs={{0,5},{1,4},{2,7},{3,6},{4,1},{5,0},{6,3},{7,2},{8,13},{9,12},{10,... | collective-permute-start | bytes 294920 | tf_op jit(solution)/shard_map/ppermute | solution.py:83

commit v14 on v13

--- a/solution.py
+++ b/solution.py
@@ -170,14 +170,16 @@
         out[...] = (total + jnp.where(from_other, beyond[...].astype(f32), 0.0)).astype(bf16)
 
 
-def product_kernel(plan, layers, *refs):
-    att = refs[: plan.pairs]
-    cols, *outs, for_mate, gathered = refs[plan.pairs :]
-    for t in range(plan.pairs):
+def product_kernel(counts, layers, *refs):
+    att = list(refs[: sum(counts)])
+    cols, *outs, for_mate, gathered = refs[sum(counts) :]
+    for t, count in enumerate(counts):
         at = slice(t * HEAD_DIM, (t + 1) * HEAD_DIM)
+        parts, att = att[:count], att[count:]
         for core in range(2):
+            part, row = (parts[0], core) if count == 1 else (parts[core], 0)
             for n, i in enumerate(layers):
-                block = att[t][core, i * HEAD_DIM : (i + 1) * HEAD_DIM, :]
+                block = part[row, i * HEAD_DIM : (i + 1) * HEAD_DIM, :]
                 gathered[core, n * HEAD_DIM : (n + 1) * HEAD_DIM, at] = block
     tokens, width = gathered.shape[2], cols.shape[2]
     step = 512 if width % 512 == 0 else width
@@ -314,10 +316,17 @@
     by_high = [attended[0]] + [
         shift(attended[high], "seq", high << (1 + plan.col_bits)) for high in range(1, plan.high)
     ]
-    pairs = [attended[0]] + [shift(attended[0], "seq", q << 1) for q in range(1, plan.col)]
+    pairs = [(attended[0],)] + [
+        (shift(attended[0], "seq", q << 1),) for q in range(1, plan.col)
+    ]
     for came_high in by_high[1:]:
-        there = after(came_high, *pairs[1 : plan.col])
-        pairs += [came_high] + [shift(there, "seq", q << 1) for q in range(1, plan.col)]
+        pairs.append((came_high,))
+        pairs += [
+            tuple(shift(came_high[core : core + 1], "seq", q << 1) for core in range(2))
+            for q in range(1, plan.col)
+        ]
+    counts = [len(pair) for pair in pairs]
+    pairs = [part for pair in pairs for part in pair]
 
     dq, dko, dvo, dkf, dvf, dfar = pl.pallas_call(
         backward_kernel,
@@ -349,10 +358,10 @@
 
     def product(name, layers, *operands):
         *blocks, for_mate = pl.pallas_call(
-            functools.partial(product_kernel, plan, layers),
+            functools.partial(product_kernel, counts, layers),
             out_shape=[struct((HEAD_DIM, mine_width), f32)] * len(layers)
             + [struct((len(layers), HEAD_DIM, mine_width), bf16)],
-            in_specs=whole(plan.pairs + 1),
+            in_specs=whole(len(pairs) + 1),
             out_specs=whole(len(layers) + 1),
             scratch_shapes=[pltpu.VMEM((2, len(layers) * HEAD_DIM, plan.pairs * tile), bf16)],
             compiler_params=params(),
@@ -398,7 +407,7 @@
                 extra[i ^ bit].append((shift(sent[-1], "dp", bit), None, 0))
         bit *= 2
     far = [
-        shift(after(dfar, dq), "seq", 1),
+        shift(after(dfar, dq, *late), "seq", 1),
         lax.ppermute(after(dkf, dq), "seq", gives),
         lax.ppermute(after(dvf, dq), "seq", gives),
     ]

time: 95.2 us -> 93.3 us (0.980)
  waiting for transfers between devices: 43.2 us -> 38.2 us
  starting transfers between devices: 32.5 us -> 35.6 us
    ppermute x21 -> x22, waiting for transfers between devices: 36.4 us -> 31.4 us  [shift(): lax.ppermute(value, axis, [(i, i ^ mask) for i in range(lax.axis_size(axi...]
    ppermute x21 -> x22, starting transfers between devices: 21.8 us -> 24.9 us  [shift(): lax.ppermute(value, axis, [(i, i ^ mask) for i in range(lax.axis_size(axi...]
  transfers between devices with their start and end apart: 25 -> 26, of which waited for: 11 -> 12; matrix products, arithmetic and copies ran while one was open for 2% -> 2% of each run, Pallas kernels for 12% -> 12%
where the time goes in v14:
time: 93.3 us; the launch traced here: 92.9 us
  waiting for transfers between devices  38.2 us (41%)
  starting transfers between devices  35.6 us (38%)
  Pallas kernels  16.5 us (18%)
  local copies, waits for them, and re-layouts  1.49 us (2%)
    ppermute x22, waiting for transfers between devices, shift(): lax.ppermute(value, axis, [(i, i ^ mask) for i in range(lax.axis_size(axi...  31.4 us
    ppermute x22, starting transfers between devices, shift(): lax.ppermute(value, axis, [(i, i ^ mask) for i in range(lax.axis_size(axi...  24.9 us
    ppermute x1, waiting for transfers between devices, local(): value_next = lax.ppermute(value, 'seq', takes)  5.62 us
    ppermute x1, starting transfers between devices, local(): key_next = lax.ppermute(key, 'seq', takes)  4.49 us
    pallas_call x1, Pallas kernels, local(): pl.pallas_call(backward_kernel, out_shape=[struct((tile, width), bf16), s...  3.98 us
    pallas_call x1, Pallas kernels, local(): pl.pallas_call(functools.partial(update_kernel, plan, factor), out_shape=...  3.94 us
    ppermute x1, starting transfers between devices, local(): value_next = lax.ppermute(value, 'seq', takes)  3.49 us
    pallas_call x4, Pallas kernels, product(): pl.pallas_call(functools.partial(product_kernel, counts, layers), out_sha...  2.38 us
  transfers between devices with their start and end apart: 26, of which 12 were waited for; matrix products, arithmetic and copies ran while one was open for 2% of the time, Pallas kernels for 12%

profile of v14, /device:TPU:1, one launch (start us, length us, event | category | flops | bytes accessed | tf_op | source)
XLA Modules:
  0.0 92.9 jit_solution(5089910184331931161)
XLA Ops:
  0.6 0.1 collective-permute-start
  0.8 4.5 %collective-permute-start.2 = (bf16[128,2048]{1,0:T(8,128)(2,1)}, bf16[128,2048]{1,0:T(8,128)(2,1)S(1)}, u32[]{:S(2)}, u32[]{:S(2)}) collective-permute-start(bf16[128,2048]{1,0:T(8,128)(2,1)} %bitcast.26), channel_id=1, source_target_pairs={{1,2},{3,4},{4,3},{6,5},{9,10},{11,12},{12,11},{14,13},{17,18},{19... | collective-permute-start | bytes 1572872 | tf_op jit(solution)/shard_map/ppermute | solution.py:275
  5.3 0.1 collective-permute-start.1
  5.3 3.5 %collective-permute-start.3 = (bf16[128,2048]{1,0:T(8,128)(2,1)}, bf16[128,2048]{1,0:T(8,128)(2,1)S(1)}, u32[]{:S(2)}, u32[]{:S(2)}) collective-permute-start(bf16[128,2048]{1,0:T(8,128)(2,1)} %bitcast.30), channel_id=1, source_target_pairs={{1,2},{3,4},{4,3},{6,5},{9,10},{11,12},{12,11},{14,13},{17,18},{19... | collective-permute-start | bytes 1572872 | tf_op jit(solution)/shard_map/ppermute | solution.py:276
  8.9 1.4 %dynamic-slice_bitcast_fusion.1 = (bf16[128,768]{1,0:T(8,128)(2,1)S(1)}, bf16[128,768]{1,0:T(8,128)(2,1)S(1)}, bf16[128,768]{1,0:T(8,128)(2,1)S(1)}, bf16[128,768]{1,0:T(8,128)(2,1)S(1)}) fusion(bf16[1,1,128,3072]{3,2,1,0:T(8,128)(2,1)} %param.10, s32[]{:T(128)S(6)} %select_n.14, s32[]{:T(128)S(6)} %select_n.13, s32[]{:T(128)S(6)} %select_n.12, s32[]{:T(128)S(6)} %select_n.15), kind=kLoop, calls=%fused_computation.6 | loop fusion | bytes 1572880 | tf_op jit(solution)/shard_map/dynamic_slice | solution.py:289
  10.3 0.1 fusion
  10.3 0.1 collective-permute-start.4
  10.5 1.2 %collective-permute-done.2.kn = bf16[128,2048]{1,0:T(8,128)(2,1)S(1)} collective-permute-done((bf16[128,2048]{1,0:T(8,128)(2,1)}, bf16[128,2048]{1,0:T(8,128)(2,1)S(1)}, u32[]{:S(2)}, u32[]{:S(2)}) %collective-permute-start.2) | collective-permute-done | bytes 524320 | tf_op jit(solution)/shard_map/ppermute | solution.py:275
  11.6 5.6 %collective-permute-done.3.vn = bf16[128,2048]{1,0:T(8,128)(2,1)S(1)} collective-permute-done((bf16[128,2048]{1,0:T(8,128)(2,1)}, bf16[128,2048]{1,0:T(8,128)(2,1)S(1)}, u32[]{:S(2)}, u32[]{:S(2)}) %collective-permute-start.3) | collective-permute-done | bytes 524320 | tf_op jit(solution)/shard_map/ppermute | solution.py:276
  17.3 3.5 %collective-permute-start.5 = (bf16[128,1536]{1,0:T(8,128)(2,1)S(1)}, bf16[128,1536]{1,0:T(8,128)(2,1)S(1)}, u32[]{:S(2)}, u32[]{:S(2)}) collective-permute-start(bf16[128,1536]{1,0:T(8,128)(2,1)S(1)} %pad_maximum_fusion.1), channel_id=1, source_target_pairs={{0,2},{1,3},{2,0},{3,1},{4,6},{5,7},{6,4},{7,5},{8,10},{9,11},{10,... | collective-permute-start | bytes 1179656 | tf_op jit(solution)/shard_map/ppermute | solution.py:83
  20.7 0.0 collective-permute-done.km
  20.8 0.0 copy-start.3
  20.8 2.3 %attention_forward.1 = bf16[2,2,512,128]{3,2,1,0:T(8,128)(2,1)S(1)} custom-call(s32[1,8]{1,0:T(1,128)S(1)} %copy-done.4, bf16[128,2048]{1,0:T(8,128)(2,1)S(1)} %bitcast.23, bf16[128,2048]{1,0:T(8,128)(2,1)S(1)} %bitcast.27, bf16[128,2048]{1,0:T(8,128)(2,1)S(1)} %bitcast.31, bf16[128,2048]{1,0:T(8,128)(2,1)S(1)} %collective-permute-done.km, ...), custom_call_target="tpu_custom_call" | custom-call | flops 268435456 | bytes 4194304 | tf_op jit(solution)/shard_map/attention_forward/pallas_call | solution.py:305
  23.1 0.1 collective-permute-start.11
  23.2 0.8 collective-permute-start.10
  24.0 4.0 %attention_backward.1 = (bf16[128,2048]{1,0:T(8,128)(2,1)}, f32[128,2048]{1,0:T(8,128)S(1)}, f32[128,2048]{1,0:T(8,128)S(1)}, bf16[128,2048]{1,0:T(8,128)(2,1)S(...) custom-call(s32[1,8]{1,0:T(1,128)S(1)} %copy-done.4, bf16[128,2048]{1,0:T(8,128)(2,1)S(1)} %bitcast.24, ...), custom_call_target="tpu_custom_call" | custom-call | flops 1 | bytes 1 | tf_op jit(solution)/shard_map/attention_backward/pallas_call | solution.py:331
  28.0 2.4 %collective-permute-done.5 = bf16[128,1536]{1,0:T(8,128)(2,1)S(1)} collective-permute-done((bf16[128,1536]{1,0:T(8,128)(2,1)S(1)}, bf16[128,1536]{1,0:T(8,128)(2,1)S(1)}, u32[]{:S(2)}, u32[]{:S(2)}) %collective-permute-start.5) | collective-permute-done | bytes 393248 | tf_op jit(solution)/shard_map/ppermute | solution.py:83
  30.4 0.1 collective-permute-start.6
  30.5 1.5 %collective-permute-start.14 = (bf16[1,128,768]{2,1,0:T(8,128)(2,1)S(1)}, bf16[1,128,768]{2,1,0:T(8,128)(2,1)S(1)}, u32[]{:S(2)}, u32[]{:S(2)}) collective-permute-start(bf16[1,128,768]{2,1,0:T(8,128)(2,1)S(1)} %get-tuple-element.78), channel_id=1, source_target_pairs={{0,4},{1,5},{2,6},{3,7},{4,0},{5,1},{6,2},{7,3},{8,12},{9,13},{10,... | collective-permute-start | bytes 589832 | tf_op jit(solution)/shard_map/ppermute | solution.py:83
  31.9 0.1 collective-permute-done.11.refs_2_
  32.1 3.0 %collective-permute-start.12 = (bf16[1,512,128]{2,1,0:T(8,128)(2,1)S(1)}, bf16[1,512,128]{2,1,0:T(8,128)(2,1)S(1)}, u32[]{:S(2)}, u32[]{:S(2)}) collective-permute-start(bf16[1,512,128]{2,1,0:T(8,128)(2,1)S(1)} %get-tuple-element.81), channel_id=1, source_target_pairs={{0,2},{1,3},{2,0},{3,1},{4,6},{5,7},{6,4},{7,5},{8,10},{9,11},{10,... | collective-permute-start | bytes 393224 | tf_op jit(solution)/shard_map/ppermute | solution.py:83
  35.1 0.1 collective-permute-start.13
  35.2 1.0 %collective-permute-done.6 = bf16[1,128,768]{2,1,0:T(8,128)(2,1)S(1)} collective-permute-done((bf16[1,128,768]{2,1,0:T(8,128)(2,1)S(1)}, bf16[1,128,768]{2,1,0:T(8,128)(2,1)S(1)}, u32[]{:S(2)}, u32[]{:S(2)}) %collective-permute-start.6) | collective-permute-done | bytes 196640 | tf_op jit(solution)/shard_map/ppermute | solution.py:83
  36.2 2.7 %collective-permute-start.7 = (bf16[2,128,2048]{2,1,0:T(8,128)(2,1)S(1)}, bf16[2,128,2048]{2,1,0:T(8,128)(2,1)S(1)}, u32[]{:S(2)}, u32[]{:S(2)}) collective-permute-start(bf16[2,128,2048]{2,1,0:T(8,128)(2,1)S(1)} %get-tuple-element.44), channel_id=1, source_target_pairs={{0,1},{1,0},{2,3},{3,2},{4,5},{5,4},{6,7},{7,6},{8,9},{9,8},{10,11... | collective-permute-start | bytes 3145736 | tf_op jit(solution)/shard_map/ppermute | solution.py:83
  38.9 1.5 %collective-permute-done.14 = bf16[1,128,768]{2,1,0:T(8,128)(2,1)S(1)} collective-permute-done((bf16[1,128,768]{2,1,0:T(8,128)(2,1)S(1)}, bf16[1,128,768]{2,1,0:T(8,128)(2,1)S(1)}, u32[]{:S(2)}, u32[]{:S(2)}) %collective-permute-start.14) | collective-permute-done | bytes 196640 | tf_op jit(solution)/shard_map/ppermute | solution.py:83
  40.4 0.1 maximum_maximum_fusion.refs_5_
  40.6 0.0 collective-permute-done.10.refs_1_
  40.6 0.9 %collective-permute-done.13.refs_4_ = bf16[1,512,128]{2,1,0:T(8,128)(2,1)S(1)} collective-permute-done((bf16[1,512,128]{2,1,0:T(8,128)(2,1)S(1)}, bf16[1,512,128]{2,1,0:T(8,128)(2,1)S(1)}, u32[]{:S(2)}, u32[]{:S(2)}) %collective-permute-start.13) | collective-permute-done | bytes 131104 | tf_op jit(solution)/shard_map/ppermute | solution.py:83
  41.5 0.6 product_first.1
  42.1 0.9 collective-permute-start.16
  43.0 0.6 product_near.1
  43.6 0.1 collective-permute-start.20
  43.7 0.7 collective-permute-done.16.refs_1_
  44.4 0.1 block_sum.3
  44.4 1.4 %collective-permute-start.18 = (bf16[128,1536]{1,0:T(8,128)(2,1)S(1)}, bf16[128,1536]{1,0:T(8,128)(2,1)S(1)}, u32[]{:S(2)}, u32[]{:S(2)}) collective-permute-start(bf16[128,1536]{1,0:T(8,128)(2,1)S(1)} %block_sum.3), channel_id=1, source_target_pairs={{0,8},{8,0},{16,24},{24,16},{1,9},{9,1},{17,25},{25,17},{2,10},{10... | collective-permute-start | bytes 1179656 | tf_op jit(solution)/shard_map/ppermute | solution.py:83
  45.8 0.6 product_middle.1
  46.4 0.7 collective-permute-start.17
  47.1 0.6 product_own.1
  47.7 0.1 collective-permute-start.15
  47.8 0.0 collective-permute-done.20.refs_1_
  47.8 1.3 %collective-permute-start.8 = (bf16[128,2048]{1,0:T(8,128)(2,1)S(1)}, bf16[128,2048]{1,0:T(8,128)(2,1)S(1)}, u32[]{:S(2)}, u32[]{:S(2)}) collective-permute-start(bf16[128,2048]{1,0:T(8,128)(2,1)S(1)} %get-tuple-element.46), channel_id=1, source_target_pairs={{3,4},{5,6},{2,1},{4,3},{11,12},{13,14},{10,9},{12,11},{19,20},{21... | collective-permute-start | bytes 1572872 | tf_op jit(solution)/shard_map/ppermute | solution.py:411
  49.1 1.5 %collective-permute-start.9 = (bf16[128,2048]{1,0:T(8,128)(2,1)S(1)}, bf16[128,2048]{1,0:T(8,128)(2,1)S(1)}, u32[]{:S(2)}, u32[]{:S(2)}) collective-permute-start(bf16[128,2048]{1,0:T(8,128)(2,1)S(1)} %get-tuple-element.48), channel_id=1, source_target_pairs={{3,4},{5,6},{2,1},{4,3},{11,12},{13,14},{10,9},{12,11},{19,20},{21... | collective-permute-start | bytes 1572872 | tf_op jit(solution)/shard_map/ppermute | solution.py:412
  50.6 0.1 block_sum.5
  50.7 4.1 %collective-permute-done.18.refs_2_ = bf16[128,1536]{1,0:T(8,128)(2,1)S(1)} collective-permute-done((bf16[128,1536]{1,0:T(8,128)(2,1)S(1)}, bf16[128,1536]{1,0:T(8,128)(2,1)S(1)}, u32[]{:S(2)}, u32[]{:S(2)}) %collective-permute-start.18) | collective-permute-done | bytes 393248 | tf_op jit(solution)/shard_map/ppermute | solution.py:83
  54.8 0.1 block_sum.4
  55.0 2.4 %collective-permute-start.19 = (bf16[128,1536]{1,0:T(8,128)(2,1)S(1)}, bf16[128,1536]{1,0:T(8,128)(2,1)S(1)}, u32[]{:S(2)}, u32[]{:S(2)}) collective-permute-start(bf16[128,1536]{1,0:T(8,128)(2,1)S(1)} %block_sum.4), channel_id=1, source_target_pairs={{0,16},{8,24},{16,0},{24,8},{1,17},{9,25},{17,1},{25,9},{2,18},{10... | collective-permute-start | bytes 1179656 | tf_op jit(solution)/shard_map/ppermute | solution.py:83
  57.3 0.0 collective-permute-done.15.refs_0_
  57.3 0.0 collective-permute-done.7.mate
  57.3 1.3 %collective-permute-start.21 = (bf16[128,1536]{1,0:T(8,128)(2,1)S(1)}, bf16[128,1536]{1,0:T(8,128)(2,1)S(1)}, u32[]{:S(2)}, u32[]{:S(2)}) collective-permute-start(bf16[128,1536]{1,0:T(8,128)(2,1)S(1)} %block_sum.5), channel_id=1, source_target_pairs={{0,8},{8,0},{16,24},{24,16},{1,9},{9,1},{17,25},{25,17},{2,10},{10... | collective-permute-start | bytes 1179656 | tf_op jit(solution)/shard_map/ppermute | solution.py:83
  58.6 15.7 %collective-permute-done.19.refs_1_ = bf16[128,1536]{1,0:T(8,128)(2,1)S(1)} collective-permute-done((bf16[128,1536]{1,0:T(8,128)(2,1)S(1)}, bf16[128,1536]{1,0:T(8,128)(2,1)S(1)}, u32[]{:S(2)}, u32[]{:S(2)}) %collective-permute-start.19) | collective-permute-done | bytes 393248 | tf_op jit(solution)/shard_map/ppermute | solution.py:83
  74.4 0.0 collective-permute-done.21.refs_2_
  74.4 0.8 gradient_sum.1
  75.2 1.7 %collective-permute-start.22 = (f32[128,128]{1,0:T(8,128)S(1)}, f32[128,128]{1,0:T(8,128)S(1)}, u32[]{:S(2)}, u32[]{:S(2)}) collective-permute-start(f32[128,128]{1,0:T(8,128)S(1)} %get-tuple-element.65.gram), channel_id=1, source_target_pairs={{0,2},{1,3},{2,0},{3,1},{4,6},{5,7},{6,4},{7,5},{8,10},{9,11},{10,... | collective-permute-start | bytes 196616 | tf_op jit(solution)/shard_map/ppermute | solution.py:83
  76.9 0.0 collective-permute-done.8.kn
  76.9 0.0 collective-permute-done.9.vn
  76.9 1.8 %key_value_sum.1 = (bf16[128,2048]{1,0:T(8,128)(2,1)}, bf16[128,2048]{1,0:T(8,128)(2,1)}) custom-call(s32[1,8]{1,0:T(1,128)S(1)} %copy-done.4, f32[128,2048]{1,0:T(8,128)S(1)} %get-tuple-element.39.dko, f32[128,2048]{1,0:T(8,128)S(1)} %get-tuple-element.40.dvo, bf16[2,128,2048]{2,1,0:T(8,128)(2,1)S(1)} %collective-permute-done.7.mate, ...), custom_call_target="tpu_custom_call" | custom-call | flops 1572864 | bytes 5242880 | tf_op jit(solution)/shard_map/key_value_sum/pallas_call | solution.py:421
  78.7 3.9 %newton_schulz.1 = (f32[128,384]{1,0:T(8,128)S(1)}, bf16[128,384]{1,0:T(8,128)(2,1)S(1)}, bf16[128,384]{1,0:T(8,128)(2,1)S(1)}, bf16[128,384]{1,0:T(8,128)(2,1)S(1)}) custom-call(f32[128,1536]{1,0:T(8,128)S(1)} %get-tuple-element.64.x, f32[128,128]{1,0:T(8,128)S(1)} %get-tuple-element.65.gram, f32[128,128]{1,0:T(8,128)S(1)} %collective-permute-done.22.gram_other), custom_call_target="tpu_custom_call" | custom-call | flops 301989888 | bytes 1572864 | tf_op jit(solution)/shard_map/newton_schulz/pallas_call | solution.py:452
  82.7 2.7 %collective-permute-start.23 = (bf16[128,384]{1,0:T(8,128)(2,1)S(1)}, bf16[128,384]{1,0:T(8,128)(2,1)S(1)}, u32[]{:S(2)}, u32[]{:S(2)}) collective-permute-start(bf16[128,384]{1,0:T(8,128)(2,1)S(1)} %get-tuple-element.67), channel_id=1, source_target_pairs={{0,1},{1,0},{2,3},{3,2},{4,5},{5,4},{6,7},{7,6},{8,9},{9,8},{10,11... | collective-permute-start | bytes 294920 | tf_op jit(solution)/shard_map/ppermute | solution.py:83
  85.4 1.0 %collective-permute-start.24 = (bf16[128,384]{1,0:T(8,128)(2,1)S(1)}, bf16[128,384]{1,0:T(8,128)(2,1)S(1)}, u32[]{:S(2)}, u32[]{:S(2)}) collective-permute-start(bf16[128,384]{1,0:T(8,128)(2,1)S(1)} %get-tuple-element.68), channel_id=1, source_target_pairs={{0,4},{1,5},{2,6},{3,7},{4,0},{5,1},{6,2},{7,3},{8,12},{9,13},{10,... | collective-permute-start | bytes 294920 | tf_op jit(solution)/shard_map/ppermute | solution.py:83
  86.4 0.7 collective-permute-start.25
  87.1 0.0 collective-permute-done.23.refs_1_
  87.1 2.7 %collective-permute-done.24.refs_2_ = bf16[128,384]{1,0:T(8,128)(2,1)S(1)} collective-permute-done((bf16[128,384]{1,0:T(8,128)(2,1)S(1)}, bf16[128,384]{1,0:T(8,128)(2,1)S(1)}, u32[]{:S(2)}, u32[]{:S(2)}) %collective-permute-start.24) | collective-permute-done | bytes 98336 | tf_op jit(solution)/shard_map/ppermute | solution.py:83
  89.7 2.3 %collective-permute-done.25.refs_3_ = bf16[128,384]{1,0:T(8,128)(2,1)S(1)} collective-permute-done((bf16[128,384]{1,0:T(8,128)(2,1)S(1)}, bf16[128,384]{1,0:T(8,128)(2,1)S(1)}, u32[]{:S(2)}, u32[]{:S(2)}) %collective-permute-start.25) | collective-permute-done | bytes 98336 | tf_op jit(solution)/shard_map/ppermute | solution.py:83
  92.0 0.9 %update_rows.1 = f32[512,384]{1,0:T(8,128)} custom-call(f32[128,384]{1,0:T(8,128)S(1)} %get-tuple-element.66.refs_0_, bf16[128,384]{1,0:T(8,128)(2,1)S(1)} %collective-permute-done.23.refs_1_, bf16[128,384]{1,0:T(8,128)(2,1)S(1)} %collective-permute-done.24.refs_2_, bf16[128,384]{1,0:T(8,128)(2,1)S(1)} %collective-permute-done.25.refs_3_), custom_call_target="tpu_custom_call" | custom-call | flops 1 | bytes 1572864 | tf_op jit(solution)/shard_map/update_rows/pallas_call | solution.py:464
  (18 shorter events, 0.1 us)
Async XLA Ops:
  0.6 20.1 %collective-permute-start = (bf16[128,2048]{1,0:T(8,128)(2,1)}, bf16[128,2048]{1,0:T(8,128)(2,1)S(1)}, u32[]{:S(2)}, u32[]{:S(2)}) collective-permute-start(bf16[128,2048]{1,0:T(8,128)(2,1)} %bitcast.25), channel_id=1, source_target_pairs={{0,1},{1,0},{2,3},{3,2},{4,5},{5,4},{6,7},{7,6},{8,9},{9,8},{10,11... | collective-permute-start | bytes 1572872 | tf_op jit(solution)/shard_map/ppermute | solution.py:83
  0.8 10.9 %collective-permute-start.2 = (bf16[128,2048]{1,0:T(8,128)(2,1)}, bf16[128,2048]{1,0:T(8,128)(2,1)S(1)}, u32[]{:S(2)}, u32[]{:S(2)}) collective-permute-start(bf16[128,2048]{1,0:T(8,128)(2,1)} %bitcast.26), channel_id=1, source_target_pairs={{1,2},{3,4},{4,3},{6,5},{9,10},{11,12},{12,11},{14,13},{17,18},{19... | collective-permute-start | bytes 1572872 | tf_op jit(solution)/shard_map/ppermute | solution.py:275
  5.3 15.5 %collective-permute-start.1 = (bf16[128,2048]{1,0:T(8,128)(2,1)}, bf16[128,2048]{1,0:T(8,128)(2,1)S(1)}, u32[]{:S(2)}, u32[]{:S(2)}) collective-permute-start(bf16[128,2048]{1,0:T(8,128)(2,1)} %bitcast.29), channel_id=1, source_target_pairs={{0,1},{1,0},{2,3},{3,2},{4,5},{5,4},{6,7},{7,6},{8,9},{9,8},{10,11... | collective-permute-start | bytes 1572872 | tf_op jit(solution)/shard_map/ppermute | solution.py:83
  5.3 11.9 %collective-permute-start.3 = (bf16[128,2048]{1,0:T(8,128)(2,1)}, bf16[128,2048]{1,0:T(8,128)(2,1)S(1)}, u32[]{:S(2)}, u32[]{:S(2)}) collective-permute-start(bf16[128,2048]{1,0:T(8,128)(2,1)} %bitcast.30), channel_id=1, source_target_pairs={{1,2},{3,4},{4,3},{6,5},{9,10},{11,12},{12,11},{14,13},{17,18},{19... | collective-permute-start | bytes 1572872 | tf_op jit(solution)/shard_map/ppermute | solution.py:276
  8.8 11.9 %copy-start = (bf16[1,1,128,2048]{3,2,1,0:T(8,128)(2,1)S(1)}, bf16[1,1,128,2048]{3,2,1,0:T(8,128)(2,1)}, u32[]{:S(2)}) copy-start(bf16[1,1,128,2048]{3,2,1,0:T(8,128)(2,1)} %param.6) | copy-start | bytes 1572868
  8.9 11.9 %copy-start.1 = (bf16[1,1,128,2048]{3,2,1,0:T(8,128)(2,1)S(1)}, bf16[1,1,128,2048]{3,2,1,0:T(8,128)(2,1)}, u32[]{:S(2)}) copy-start(bf16[1,1,128,2048]{3,2,1,0:T(8,128)(2,1)} %param.7) | copy-start | bytes 1572868
  8.9 11.9 %copy-start.2 = (bf16[1,1,128,2048]{3,2,1,0:T(8,128)(2,1)S(1)}, bf16[1,1,128,2048]{3,2,1,0:T(8,128)(2,1)}, u32[]{:S(2)}) copy-start(bf16[1,1,128,2048]{3,2,1,0:T(8,128)(2,1)} %param.8) | copy-start | bytes 1572868
  8.9 11.9 %copy-start.4 = (s32[1,8]{1,0:T(1,128)S(1)}, s32[1,8]{1,0:T(1,128)}, u32[]{:S(2)}) copy-start(s32[1,8]{1,0:T(1,128)} %near_ref.5) | copy-start | bytes 100
  10.3 17.6 %collective-permute-start.4 = (bf16[128,1536]{1,0:T(8,128)(2,1)S(1)}, bf16[128,1536]{1,0:T(8,128)(2,1)S(1)}, u32[]{:S(2)}, u32[]{:S(2)}) collective-permute-start(bf16[128,1536]{1,0:T(8,128)(2,1)S(1)} %get-tuple-element.77), channel_id=1, source_target_pairs={{0,4},{1,5},{2,6},{3,7},{4,0},{5,1},{6,2},{7,3},{8,12},{9,13},{10,... | collective-permute-start | bytes 1179656 | tf_op jit(solution)/shard_map/ppermute | solution.py:83
  17.3 13.1 %collective-permute-start.5 = (bf16[128,1536]{1,0:T(8,128)(2,1)S(1)}, bf16[128,1536]{1,0:T(8,128)(2,1)S(1)}, u32[]{:S(2)}, u32[]{:S(2)}) collective-permute-start(bf16[128,1536]{1,0:T(8,128)(2,1)S(1)} %pad_maximum_fusion.1), channel_id=1, source_target_pairs={{0,2},{1,3},{2,0},{3,1},{4,6},{5,7},{6,4},{7,5},{8,10},{9,11},{10,... | collective-permute-start | bytes 1179656 | tf_op jit(solution)/shard_map/ppermute | solution.py:83
  20.8 3.2 %copy-start.3 = (bf16[1,1,128,2048]{3,2,1,0:T(8,128)(2,1)S(1)}, bf16[1,1,128,2048]{3,2,1,0:T(8,128)(2,1)}, u32[]{:S(2)}) copy-start(bf16[1,1,128,2048]{3,2,1,0:T(8,128)(2,1)} %param.9) | copy-start | bytes 1572868
  23.1 8.9 %collective-permute-start.11 = (bf16[2,512,128]{2,1,0:T(8,128)(2,1)S(1)}, bf16[2,512,128]{2,1,0:T(8,128)(2,1)S(1)}, u32[]{:S(2)}, u32[]{:S(2)}) collective-permute-start(bf16[2,512,128]{2,1,0:T(8,128)(2,1)S(1)} %get-tuple-element.74), channel_id=1, source_target_pairs={{0,4},{1,5},{2,6},{3,7},{4,0},{5,1},{6,2},{7,3},{8,12},{9,13},{10,... | collective-permute-start | bytes 786440 | tf_op jit(solution)/shard_map/ppermute | solution.py:83
  23.2 17.4 %collective-permute-start.10 = (bf16[2,512,128]{2,1,0:T(8,128)(2,1)S(1)}, bf16[2,512,128]{2,1,0:T(8,128)(2,1)S(1)}, u32[]{:S(2)}, u32[]{:S(2)}) collective-permute-start(bf16[2,512,128]{2,1,0:T(8,128)(2,1)S(1)} %get-tuple-element.56.refs_0_), channel_id=1, source_target_pairs={{0,2},{1,3},{2,0},{3,1},{4,6},{5,7},{6,4},{7,5},{8,10},{9,11},{10,... | collective-permute-start | bytes 786440 | tf_op jit(solution)/shard_map/ppermute | solution.py:83
  30.4 5.8 %collective-permute-start.6 = (bf16[1,128,768]{2,1,0:T(8,128)(2,1)S(1)}, bf16[1,128,768]{2,1,0:T(8,128)(2,1)S(1)}, u32[]{:S(2)}, u32[]{:S(2)}) collective-permute-start(bf16[1,128,768]{2,1,0:T(8,128)(2,1)S(1)} %get-tuple-element.79), channel_id=1, source_target_pairs={{0,4},{1,5},{2,6},{3,7},{4,0},{5,1},{6,2},{7,3},{8,12},{9,13},{10,... | collective-permute-start | bytes 589832 | tf_op jit(solution)/shard_map/ppermute | solution.py:83
  30.5 10.0 %collective-permute-start.14 = (bf16[1,128,768]{2,1,0:T(8,128)(2,1)S(1)}, bf16[1,128,768]{2,1,0:T(8,128)(2,1)S(1)}, u32[]{:S(2)}, u32[]{:S(2)}) collective-permute-start(bf16[1,128,768]{2,1,0:T(8,128)(2,1)S(1)} %get-tuple-element.78), channel_id=1, source_target_pairs={{0,4},{1,5},{2,6},{3,7},{4,0},{5,1},{6,2},{7,3},{8,12},{9,13},{10,... | collective-permute-start | bytes 589832 | tf_op jit(solution)/shard_map/ppermute | solution.py:83
  32.1 8.5 %collective-permute-start.12 = (bf16[1,512,128]{2,1,0:T(8,128)(2,1)S(1)}, bf16[1,512,128]{2,1,0:T(8,128)(2,1)S(1)}, u32[]{:S(2)}, u32[]{:S(2)}) collective-permute-start(bf16[1,512,128]{2,1,0:T(8,128)(2,1)S(1)} %get-tuple-element.81), channel_id=1, source_target_pairs={{0,2},{1,3},{2,0},{3,1},{4,6},{5,7},{6,4},{7,5},{8,10},{9,11},{10,... | collective-permute-start | bytes 393224 | tf_op jit(solution)/shard_map/ppermute | solution.py:83
  35.1 6.4 %collective-permute-start.13 = (bf16[1,512,128]{2,1,0:T(8,128)(2,1)S(1)}, bf16[1,512,128]{2,1,0:T(8,128)(2,1)S(1)}, u32[]{:S(2)}, u32[]{:S(2)}) collective-permute-start(bf16[1,512,128]{2,1,0:T(8,128)(2,1)S(1)} %get-tuple-element.80), channel_id=1, source_target_pairs={{0,2},{1,3},{2,0},{3,1},{4,6},{5,7},{6,4},{7,5},{8,10},{9,11},{10,... | collective-permute-start | bytes 393224 | tf_op jit(solution)/shard_map/ppermute | solution.py:83
  36.2 21.1 %collective-permute-start.7 = (bf16[2,128,2048]{2,1,0:T(8,128)(2,1)S(1)}, bf16[2,128,2048]{2,1,0:T(8,128)(2,1)S(1)}, u32[]{:S(2)}, u32[]{:S(2)}) collective-permute-start(bf16[2,128,2048]{2,1,0:T(8,128)(2,1)S(1)} %get-tuple-element.44), channel_id=1, source_target_pairs={{0,1},{1,0},{2,3},{3,2},{4,5},{5,4},{6,7},{7,6},{8,9},{9,8},{10,11... | collective-permute-start | bytes 3145736 | tf_op jit(solution)/shard_map/ppermute | solution.py:83
  42.1 2.2 %collective-permute-start.16 = (bf16[1,128,1536]{2,1,0:T(8,128)(2,1)S(1)}, bf16[1,128,1536]{2,1,0:T(8,128)(2,1)S(1)}, u32[]{:S(2)}, u32[]{:S(2)}) collective-permute-start(bf16[1,128,1536]{2,1,0:T(8,128)(2,1)S(1)} %get-tuple-element.55), channel_id=1, source_target_pairs={{0,1},{1,0},{2,3},{3,2},{4,5},{5,4},{6,7},{7,6},{8,9},{9,8},{10,11... | collective-permute-start | bytes 1179656 | tf_op jit(solution)/shard_map/ppermute | solution.py:83
  43.6 4.2 %collective-permute-start.20 = (bf16[1,128,1536]{2,1,0:T(8,128)(2,1)S(1)}, bf16[1,128,1536]{2,1,0:T(8,128)(2,1)S(1)}, u32[]{:S(2)}, u32[]{:S(2)}) collective-permute-start(bf16[1,128,1536]{2,1,0:T(8,128)(2,1)S(1)} %get-tuple-element.61), channel_id=1, source_target_pairs={{0,1},{1,0},{2,3},{3,2},{4,5},{5,4},{6,7},{7,6},{8,9},{9,8},{10,11... | collective-permute-start | bytes 1179656 | tf_op jit(solution)/shard_map/ppermute | solution.py:83
  44.4 10.4 %collective-permute-start.18 = (bf16[128,1536]{1,0:T(8,128)(2,1)S(1)}, bf16[128,1536]{1,0:T(8,128)(2,1)S(1)}, u32[]{:S(2)}, u32[]{:S(2)}) collective-permute-start(bf16[128,1536]{1,0:T(8,128)(2,1)S(1)} %block_sum.3), channel_id=1, source_target_pairs={{0,8},{8,0},{16,24},{24,16},{1,9},{9,1},{17,25},{25,17},{2,10},{10... | collective-permute-start | bytes 1179656 | tf_op jit(solution)/shard_map/ppermute | solution.py:83
  46.4 2.7 %collective-permute-start.17 = (bf16[1,128,1536]{2,1,0:T(8,128)(2,1)S(1)}, bf16[1,128,1536]{2,1,0:T(8,128)(2,1)S(1)}, u32[]{:S(2)}, u32[]{:S(2)}) collective-permute-start(bf16[1,128,1536]{2,1,0:T(8,128)(2,1)S(1)} %get-tuple-element.59), channel_id=1, source_target_pairs={{0,1},{1,0},{2,3},{3,2},{4,5},{5,4},{6,7},{7,6},{8,9},{9,8},{10,11... | collective-permute-start | bytes 1179656 | tf_op jit(solution)/shard_map/ppermute | solution.py:83
  47.7 9.6 %collective-permute-start.15 = (bf16[1,128,1536]{2,1,0:T(8,128)(2,1)S(1)}, bf16[1,128,1536]{2,1,0:T(8,128)(2,1)S(1)}, u32[]{:S(2)}, u32[]{:S(2)}) collective-permute-start(bf16[1,128,1536]{2,1,0:T(8,128)(2,1)S(1)} %get-tuple-element.53), channel_id=1, source_target_pairs={{0,1},{1,0},{2,3},{3,2},{4,5},{5,4},{6,7},{7,6},{8,9},{9,8},{10,11... | collective-permute-start | bytes 1179656 | tf_op jit(solution)/shard_map/ppermute | solution.py:83
  47.8 29.1 %collective-permute-start.8 = (bf16[128,2048]{1,0:T(8,128)(2,1)S(1)}, bf16[128,2048]{1,0:T(8,128)(2,1)S(1)}, u32[]{:S(2)}, u32[]{:S(2)}) collective-permute-start(bf16[128,2048]{1,0:T(8,128)(2,1)S(1)} %get-tuple-element.46), channel_id=1, source_target_pairs={{3,4},{5,6},{2,1},{4,3},{11,12},{13,14},{10,9},{12,11},{19,20},{21... | collective-permute-start | bytes 1572872 | tf_op jit(solution)/shard_map/ppermute | solution.py:411
  49.1 27.7 %collective-permute-start.9 = (bf16[128,2048]{1,0:T(8,128)(2,1)S(1)}, bf16[128,2048]{1,0:T(8,128)(2,1)S(1)}, u32[]{:S(2)}, u32[]{:S(2)}) collective-permute-start(bf16[128,2048]{1,0:T(8,128)(2,1)S(1)} %get-tuple-element.48), channel_id=1, source_target_pairs={{3,4},{5,6},{2,1},{4,3},{11,12},{13,14},{10,9},{12,11},{19,20},{21... | collective-permute-start | bytes 1572872 | tf_op jit(solution)/shard_map/ppermute | solution.py:412
  55.0 19.4 %collective-permute-start.19 = (bf16[128,1536]{1,0:T(8,128)(2,1)S(1)}, bf16[128,1536]{1,0:T(8,128)(2,1)S(1)}, u32[]{:S(2)}, u32[]{:S(2)}) collective-permute-start(bf16[128,1536]{1,0:T(8,128)(2,1)S(1)} %block_sum.4), channel_id=1, source_target_pairs={{0,16},{8,24},{16,0},{24,8},{1,17},{9,25},{17,1},{25,9},{2,18},{10... | collective-permute-start | bytes 1179656 | tf_op jit(solution)/shard_map/ppermute | solution.py:83
  57.3 17.0 %collective-permute-start.21 = (bf16[128,1536]{1,0:T(8,128)(2,1)S(1)}, bf16[128,1536]{1,0:T(8,128)(2,1)S(1)}, u32[]{:S(2)}, u32[]{:S(2)}) collective-permute-start(bf16[128,1536]{1,0:T(8,128)(2,1)S(1)} %block_sum.5), channel_id=1, source_target_pairs={{0,8},{8,0},{16,24},{24,16},{1,9},{9,1},{17,25},{25,17},{2,10},{10... | collective-permute-start | bytes 1179656 | tf_op jit(solution)/shard_map/ppermute | solution.py:83
  75.2 3.5 %collective-permute-start.22 = (f32[128,128]{1,0:T(8,128)S(1)}, f32[128,128]{1,0:T(8,128)S(1)}, u32[]{:S(2)}, u32[]{:S(2)}) collective-permute-start(f32[128,128]{1,0:T(8,128)S(1)} %get-tuple-element.65.gram), channel_id=1, source_target_pairs={{0,2},{1,3},{2,0},{3,1},{4,6},{5,7},{6,4},{7,5},{8,10},{9,11},{10,... | collective-permute-start | bytes 196616 | tf_op jit(solution)/shard_map/ppermute | solution.py:83
  82.7 4.4 %collective-permute-start.23 = (bf16[128,384]{1,0:T(8,128)(2,1)S(1)}, bf16[128,384]{1,0:T(8,128)(2,1)S(1)}, u32[]{:S(2)}, u32[]{:S(2)}) collective-permute-start(bf16[128,384]{1,0:T(8,128)(2,1)S(1)} %get-tuple-element.67), channel_id=1, source_target_pairs={{0,1},{1,0},{2,3},{3,2},{4,5},{5,4},{6,7},{7,6},{8,9},{9,8},{10,11... | collective-permute-start | bytes 294920 | tf_op jit(solution)/shard_map/ppermute | solution.py:83
  85.4 4.4 %collective-permute-start.24 = (bf16[128,384]{1,0:T(8,128)(2,1)S(1)}, bf16[128,384]{1,0:T(8,128)(2,1)S(1)}, u32[]{:S(2)}, u32[]{:S(2)}) collective-permute-start(bf16[128,384]{1,0:T(8,128)(2,1)S(1)} %get-tuple-element.68), channel_id=1, source_target_pairs={{0,4},{1,5},{2,6},{3,7},{4,0},{5,1},{6,2},{7,3},{8,12},{9,13},{10,... | collective-permute-start | bytes 294920 | tf_op jit(solution)/shard_map/ppermute | solution.py:83
  86.4 5.6 %collective-permute-start.25 = (bf16[128,384]{1,0:T(8,128)(2,1)S(1)}, bf16[128,384]{1,0:T(8,128)(2,1)S(1)}, u32[]{:S(2)}, u32[]{:S(2)}) collective-permute-start(bf16[128,384]{1,0:T(8,128)(2,1)S(1)} %get-tuple-element.69), channel_id=1, source_target_pairs={{0,5},{1,4},{2,7},{3,6},{4,1},{5,0},{6,3},{7,2},{8,13},{9,12},{10,... | collective-permute-start | bytes 294920 | tf_op jit(solution)/shard_map/ppermute | solution.py:83

commit v15 on v14

--- a/solution.py
+++ b/solution.py
@@ -53,6 +53,26 @@
     return lax.dot_general(
         a, b, (dims, ((), ())), precision=lax.Precision.HIGHEST, preferred_element_type=f32
     )
+
+
+def parts_of(value):
+    high = value.astype(bf16)
+    rest = value - high.astype(f32)
+    middle = rest.astype(bf16)
+    return high, middle, (rest - middle.astype(f32)).astype(bf16)
+
+
+def square_dot(a, b):
+    a_high, a_middle, a_low = a
+    b_high, b_middle, b_low = b
+    size = a_high.shape[0]
+    left = jnp.concatenate([a_high, a_middle], 1)
+    right = jnp.concatenate(
+        [jnp.concatenate([b_high, b_high], 0), jnp.concatenate([b_middle, b_middle], 0)], 1
+    )
+    wide = dot_n(left, right)
+    small = dot_n(jnp.concatenate([a_high, a_low], 1), jnp.concatenate([b_low, b_high], 0))
+    return wide[:, :size] + (wide[:, size:] + small)
 
 
 class Plan:
@@ -225,10 +245,12 @@
     a = gram * inverse * inverse
     p = None
     for turn in range(NS_STEPS):
-        q = coeff_a * eye + coeff_b * a + coeff_c * exact(a, a)
-        p = q if p is None else exact(q, p)
+        a_parts = parts_of(a)
+        q = coeff_a * eye + coeff_b * a + coeff_c * square_dot(a_parts, a_parts)
+        q_parts = parts_of(q)
+        p = q if p is None else square_dot(q_parts, parts_of(p))
         if turn + 1 < NS_STEPS:
-            a = exact(exact(q, a), q)
+            a = square_dot(parts_of(square_dot(q_parts, a_parts)), q_parts)
     return p, inverse
 
 
@@ -274,10 +296,6 @@
     gives = [(i, j) for i, j in steps if i != 1] + [(j, i) for j, i in back if j != n - 2]
     key_next = lax.ppermute(key, "seq", takes)
     value_next = lax.ppermute(value, "seq", takes)
-    key_mate = shift(key, "seq", 1)
-    value_mate = shift(value, "seq", 1)
-    beside = (key_mate, value_mate, key_next, value_next)
-
     slot = depth // n
     flat = proj_grad.reshape(tile, depth)
     mine = plan.col_part(place)
@@ -293,6 +311,9 @@
         )
 
     own_columns = column_part(mine)
+    key_mate = shift(after(key, own_columns), "seq", 1)
+    value_mate = shift(after(value, own_columns), "seq", 1)
+    beside = (key_mate, value_mate, key_next, value_next)
     columns = [own_columns] + [
         shift(after(column_part(mine ^ q), key_next, value_next), "seq", q << 1)
         for q in range(1, plan.col)

time: 93.3 us -> 92.3 us (0.989)
  waiting for transfers between devices: 38.2 us -> 36.1 us
  starting transfers between devices: 35.6 us -> 37.4 us
    ppermute x22, starting transfers between devices: 24.9 us -> 28.6 us  [shift(): lax.ppermute(value, axis, [(i, i ^ mask) for i in range(lax.axis_size(axi...]
    ppermute x1, starting transfers between devices: 3.49 us -> 1.32 us  [local(): value_next = lax.ppermute(value, 'seq', takes)]
    ppermute x1, waiting for transfers between devices: 1.19 us -> 0.09 us  [local(): key_next = lax.ppermute(key, 'seq', takes)]
    ppermute x22, waiting for transfers between devices: 31.4 us -> 30.4 us  [shift(): lax.ppermute(value, axis, [(i, i ^ mask) for i in range(lax.axis_size(axi...]
  transfers between devices with their start and end apart: 26 -> 26, of which waited for: 12 -> 12; matrix products, arithmetic and copies ran while one was open for 2% -> 2% of each run, Pallas kernels for 12% -> 13%
where the time goes in v15:
time: 92.3 us; the launch traced here: 91.7 us
  starting transfers between devices  37.4 us (41%)
  waiting for transfers between devices  36.1 us (39%)
  Pallas kernels  15.7 us (17%)
  local copies, waits for them, and re-layouts  1.43 us (2%)
    ppermute x22, waiting for transfers between devices, shift(): lax.ppermute(value, axis, [(i, i ^ mask) for i in range(lax.axis_size(axi...  30.4 us
    ppermute x22, starting transfers between devices, shift(): lax.ppermute(value, axis, [(i, i ^ mask) for i in range(lax.axis_size(axi...  28.6 us
    ppermute x1, waiting for transfers between devices, local(): value_next = lax.ppermute(value, 'seq', takes)  5.62 us
    ppermute x1, starting transfers between devices, local(): key_next = lax.ppermute(key, 'seq', takes)  4.67 us
    pallas_call x1, Pallas kernels, local(): pl.pallas_call(backward_kernel, out_shape=[struct((tile, width), bf16), s...  3.97 us
    pallas_call x1, Pallas kernels, local(): pl.pallas_call(functools.partial(update_kernel, plan, factor), out_shape=...  3.15 us
    pallas_call x4, Pallas kernels, product(): pl.pallas_call(functools.partial(product_kernel, counts, layers), out_sha...  2.38 us
    pallas_call x1, Pallas kernels, local(): pl.pallas_call(functools.partial(forward_kernel, plan), out_shape=struct(...  2.3 us
  transfers between devices with their start and end apart: 26, of which 12 were waited for; matrix products, arithmetic and copies ran while one was open for 2% of the time, Pallas kernels for 13%

profile of v15, /device:TPU:1, one launch (start us, length us, event | category | flops | bytes accessed | tf_op | source)
XLA Modules:
  0.0 91.7 jit_solution(15310864460902253811)
XLA Ops:
  0.7 4.7 %collective-permute-start.2 = (bf16[128,2048]{1,0:T(8,128)(2,1)}, bf16[128,2048]{1,0:T(8,128)(2,1)S(1)}, u32[]{:S(2)}, u32[]{:S(2)}) collective-permute-start(bf16[128,2048]{1,0:T(8,128)(2,1)} %bitcast.25), channel_id=1, source_target_pairs={{1,2},{3,4},{4,3},{6,5},{9,10},{11,12},{12,11},{14,13},{17,18},{19... | collective-permute-start | bytes 1572872 | tf_op jit(solution)/shard_map/ppermute | solution.py:297
  5.3 1.3 %collective-permute-start.3 = (bf16[128,2048]{1,0:T(8,128)(2,1)}, bf16[128,2048]{1,0:T(8,128)(2,1)S(1)}, u32[]{:S(2)}, u32[]{:S(2)}) collective-permute-start(bf16[128,2048]{1,0:T(8,128)(2,1)} %bitcast.29), channel_id=1, source_target_pairs={{1,2},{3,4},{4,3},{6,5},{9,10},{11,12},{12,11},{14,13},{17,18},{19... | collective-permute-start | bytes 1572872 | tf_op jit(solution)/shard_map/ppermute | solution.py:298
  6.7 1.3 %dynamic-slice_bitcast_fusion.1 = (bf16[128,768]{1,0:T(8,128)(2,1)S(1)}, bf16[128,768]{1,0:T(8,128)(2,1)S(1)}, bf16[128,768]{1,0:T(8,128)(2,1)S(1)}, bf16[128,768]{1,0:T(8,128)(2,1)S(1)}) fusion(bf16[1,1,128,3072]{3,2,1,0:T(8,128)(2,1)} %param.10, s32[]{:T(128)S(6)} %select_n.14, s32[]{:T(128)S(6)} %select_n.13, s32[]{:T(128)S(6)} %select_n.12, s32[]{:T(128)S(6)} %select_n.15), kind=kLoop, calls=%fused_computation.6 | loop fusion | bytes 1572880 | tf_op jit(solution)/shard_map/dynamic_slice | solution.py:307
  8.0 0.1 fusion
  8.1 0.1 collective-permute-start
  8.2 0.5 collective-permute-start.1
  8.7 2.9 %collective-permute-start.4 = (bf16[128,1536]{1,0:T(8,128)(2,1)S(1)}, bf16[128,1536]{1,0:T(8,128)(2,1)S(1)}, u32[]{:S(2)}, u32[]{:S(2)}) collective-permute-start(bf16[128,1536]{1,0:T(8,128)(2,1)S(1)} %get-tuple-element.81), channel_id=1, source_target_pairs={{0,4},{1,5},{2,6},{3,7},{4,0},{5,1},{6,2},{7,3},{8,12},{9,13},{10,... | collective-permute-start | bytes 1179656 | tf_op jit(solution)/shard_map/ppermute | solution.py:103
  11.6 0.1 collective-permute-done.2.kn
  11.7 5.6 %collective-permute-done.3.vn = bf16[128,2048]{1,0:T(8,128)(2,1)S(1)} collective-permute-done((bf16[128,2048]{1,0:T(8,128)(2,1)}, bf16[128,2048]{1,0:T(8,128)(2,1)S(1)}, u32[]{:S(2)}, u32[]{:S(2)}) %collective-permute-start.3) | collective-permute-done | bytes 524320 | tf_op jit(solution)/shard_map/ppermute | solution.py:298
  17.3 2.8 %collective-permute-start.5 = (bf16[128,1536]{1,0:T(8,128)(2,1)S(1)}, bf16[128,1536]{1,0:T(8,128)(2,1)S(1)}, u32[]{:S(2)}, u32[]{:S(2)}) collective-permute-start(bf16[128,1536]{1,0:T(8,128)(2,1)S(1)} %pad_maximum_fusion.1), channel_id=1, source_target_pairs={{0,2},{1,3},{2,0},{3,1},{4,6},{5,7},{6,4},{7,5},{8,10},{9,11},{10,... | collective-permute-start | bytes 1179656 | tf_op jit(solution)/shard_map/ppermute | solution.py:103
  20.2 0.0 collective-permute-done.km
  20.2 0.0 collective-permute-done.1.vm
  20.2 0.0 copy-start.3
  20.2 2.3 %attention_forward.1 = bf16[2,2,512,128]{3,2,1,0:T(8,128)(2,1)S(1)} custom-call(s32[1,8]{1,0:T(1,128)S(1)} %copy-done.4, bf16[128,2048]{1,0:T(8,128)(2,1)S(1)} %bitcast.23, bf16[128,2048]{1,0:T(8,128)(2,1)S(1)} %bitcast.27, bf16[128,2048]{1,0:T(8,128)(2,1)S(1)} %bitcast.31, bf16[128,2048]{1,0:T(8,128)(2,1)S(1)} %collective-permute-done.km, ...), custom_call_target="tpu_custom_call" | custom-call | flops 268435456 | bytes 4194304 | tf_op jit(solution)/shard_map/attention_forward/pallas_call | solution.py:326
  22.5 0.1 collective-permute-start.11
  22.6 0.8 collective-permute-start.10
  23.4 4.0 %attention_backward.1 = (bf16[128,2048]{1,0:T(8,128)(2,1)}, f32[128,2048]{1,0:T(8,128)S(1)}, f32[128,2048]{1,0:T(8,128)S(1)}, bf16[128,2048]{1,0:T(8,128)(2,1)S(...) custom-call(s32[1,8]{1,0:T(1,128)S(1)} %copy-done.4, bf16[128,2048]{1,0:T(8,128)(2,1)S(1)} %bitcast.24, ...), custom_call_target="tpu_custom_call" | custom-call | flops 1 | bytes 1 | tf_op jit(solution)/shard_map/attention_backward/pallas_call | solution.py:352
  27.4 0.0 collective-permute-done.4
  27.4 2.5 %collective-permute-done.5 = bf16[128,1536]{1,0:T(8,128)(2,1)S(1)} collective-permute-done((bf16[128,1536]{1,0:T(8,128)(2,1)S(1)}, bf16[128,1536]{1,0:T(8,128)(2,1)S(1)}, u32[]{:S(2)}, u32[]{:S(2)}) %collective-permute-start.5) | collective-permute-done | bytes 393248 | tf_op jit(solution)/shard_map/ppermute | solution.py:103
  29.9 0.1 collective-permute-start.6
  29.9 1.5 %collective-permute-start.14 = (bf16[1,128,768]{2,1,0:T(8,128)(2,1)S(1)}, bf16[1,128,768]{2,1,0:T(8,128)(2,1)S(1)}, u32[]{:S(2)}, u32[]{:S(2)}) collective-permute-start(bf16[1,128,768]{2,1,0:T(8,128)(2,1)S(1)} %get-tuple-element.82), channel_id=1, source_target_pairs={{0,4},{1,5},{2,6},{3,7},{4,0},{5,1},{6,2},{7,3},{8,12},{9,13},{10,... | collective-permute-start | bytes 589832 | tf_op jit(solution)/shard_map/ppermute | solution.py:103
  31.4 0.7 collective-permute-done.11.refs_2_
  32.1 2.3 %collective-permute-start.12 = (bf16[1,512,128]{2,1,0:T(8,128)(2,1)S(1)}, bf16[1,512,128]{2,1,0:T(8,128)(2,1)S(1)}, u32[]{:S(2)}, u32[]{:S(2)}) collective-permute-start(bf16[1,512,128]{2,1,0:T(8,128)(2,1)S(1)} %get-tuple-element.85), channel_id=1, source_target_pairs={{0,2},{1,3},{2,0},{3,1},{4,6},{5,7},{6,4},{7,5},{8,10},{9,11},{10,... | collective-permute-start | bytes 393224 | tf_op jit(solution)/shard_map/ppermute | solution.py:103
  34.4 0.1 collective-permute-start.13
  34.5 0.5 collective-permute-done.6
  35.0 4.1 %collective-permute-start.7 = (bf16[2,128,2048]{2,1,0:T(8,128)(2,1)S(1)}, bf16[2,128,2048]{2,1,0:T(8,128)(2,1)S(1)}, u32[]{:S(2)}, u32[]{:S(2)}) collective-permute-start(bf16[2,128,2048]{2,1,0:T(8,128)(2,1)S(1)} %get-tuple-element.48), channel_id=1, source_target_pairs={{0,1},{1,0},{2,3},{3,2},{4,5},{5,4},{6,7},{7,6},{8,9},{9,8},{10,11... | collective-permute-start | bytes 3145736 | tf_op jit(solution)/shard_map/ppermute | solution.py:103
  39.1 0.1 collective-permute-done.14
  39.2 0.1 maximum_maximum_fusion.refs_5_
  39.4 0.0 collective-permute-done.10.refs_1_
  39.4 1.0 %collective-permute-done.13.refs_4_ = bf16[1,512,128]{2,1,0:T(8,128)(2,1)S(1)} collective-permute-done((bf16[1,512,128]{2,1,0:T(8,128)(2,1)S(1)}, bf16[1,512,128]{2,1,0:T(8,128)(2,1)S(1)}, u32[]{:S(2)}, u32[]{:S(2)}) %collective-permute-start.13) | collective-permute-done | bytes 131104 | tf_op jit(solution)/shard_map/ppermute | solution.py:103
  40.4 0.6 product_first.1
  41.0 1.4 %collective-permute-start.16 = (bf16[1,128,1536]{2,1,0:T(8,128)(2,1)S(1)}, bf16[1,128,1536]{2,1,0:T(8,128)(2,1)S(1)}, u32[]{:S(2)}, u32[]{:S(2)}) collective-permute-start(bf16[1,128,1536]{2,1,0:T(8,128)(2,1)S(1)} %get-tuple-element.59), channel_id=1, source_target_pairs={{0,1},{1,0},{2,3},{3,2},{4,5},{5,4},{6,7},{7,6},{8,9},{9,8},{10,11... | collective-permute-start | bytes 1179656 | tf_op jit(solution)/shard_map/ppermute | solution.py:103
  42.4 0.6 product_near.1
  43.0 0.1 collective-permute-start.20
  43.0 0.7 collective-permute-done.16.refs_1_
  43.7 0.1 block_sum.3
  43.8 1.4 %collective-permute-start.18 = (bf16[128,1536]{1,0:T(8,128)(2,1)S(1)}, bf16[128,1536]{1,0:T(8,128)(2,1)S(1)}, u32[]{:S(2)}, u32[]{:S(2)}) collective-permute-start(bf16[128,1536]{1,0:T(8,128)(2,1)S(1)} %block_sum.3), channel_id=1, source_target_pairs={{0,8},{8,0},{16,24},{24,16},{1,9},{9,1},{17,25},{25,17},{2,10},{10... | collective-permute-start | bytes 1179656 | tf_op jit(solution)/shard_map/ppermute | solution.py:103
  45.1 0.6 product_middle.1
  45.7 0.7 collective-permute-start.17
  46.5 0.6 product_own.1
  47.1 0.1 collective-permute-start.15
  47.1 0.0 collective-permute-done.20.refs_1_
  47.2 1.3 %collective-permute-start.8 = (bf16[128,2048]{1,0:T(8,128)(2,1)S(1)}, bf16[128,2048]{1,0:T(8,128)(2,1)S(1)}, u32[]{:S(2)}, u32[]{:S(2)}) collective-permute-start(bf16[128,2048]{1,0:T(8,128)(2,1)S(1)} %get-tuple-element.50), channel_id=1, source_target_pairs={{3,4},{5,6},{2,1},{4,3},{11,12},{13,14},{10,9},{12,11},{19,20},{21... | collective-permute-start | bytes 1572872 | tf_op jit(solution)/shard_map/ppermute | solution.py:432
  48.5 0.0 collective-permute-done.17.refs_1_
  48.5 1.5 %collective-permute-start.9 = (bf16[128,2048]{1,0:T(8,128)(2,1)S(1)}, bf16[128,2048]{1,0:T(8,128)(2,1)S(1)}, u32[]{:S(2)}, u32[]{:S(2)}) collective-permute-start(bf16[128,2048]{1,0:T(8,128)(2,1)S(1)} %get-tuple-element.52), channel_id=1, source_target_pairs={{3,4},{5,6},{2,1},{4,3},{11,12},{13,14},{10,9},{12,11},{19,20},{21... | collective-permute-start | bytes 1572872 | tf_op jit(solution)/shard_map/ppermute | solution.py:433
  49.9 0.1 block_sum.5
  50.1 4.1 %collective-permute-done.18.refs_2_ = bf16[128,1536]{1,0:T(8,128)(2,1)S(1)} collective-permute-done((bf16[128,1536]{1,0:T(8,128)(2,1)S(1)}, bf16[128,1536]{1,0:T(8,128)(2,1)S(1)}, u32[]{:S(2)}, u32[]{:S(2)}) %collective-permute-start.18) | collective-permute-done | bytes 393248 | tf_op jit(solution)/shard_map/ppermute | solution.py:103
  54.2 0.1 block_sum.4
  54.3 2.4 %collective-permute-start.19 = (bf16[128,1536]{1,0:T(8,128)(2,1)S(1)}, bf16[128,1536]{1,0:T(8,128)(2,1)S(1)}, u32[]{:S(2)}, u32[]{:S(2)}) collective-permute-start(bf16[128,1536]{1,0:T(8,128)(2,1)S(1)} %block_sum.4), channel_id=1, source_target_pairs={{0,16},{8,24},{16,0},{24,8},{1,17},{9,25},{17,1},{25,9},{2,18},{10... | collective-permute-start | bytes 1179656 | tf_op jit(solution)/shard_map/ppermute | solution.py:103
  56.7 0.0 collective-permute-done.15.refs_0_
  56.7 1.3 %collective-permute-start.21 = (bf16[128,1536]{1,0:T(8,128)(2,1)S(1)}, bf16[128,1536]{1,0:T(8,128)(2,1)S(1)}, u32[]{:S(2)}, u32[]{:S(2)}) collective-permute-start(bf16[128,1536]{1,0:T(8,128)(2,1)S(1)} %block_sum.5), channel_id=1, source_target_pairs={{0,8},{8,0},{16,24},{24,16},{1,9},{9,1},{17,25},{25,17},{2,10},{10... | collective-permute-start | bytes 1179656 | tf_op jit(solution)/shard_map/ppermute | solution.py:103
  58.0 15.7 %collective-permute-done.19.refs_1_ = bf16[128,1536]{1,0:T(8,128)(2,1)S(1)} collective-permute-done((bf16[128,1536]{1,0:T(8,128)(2,1)S(1)}, bf16[128,1536]{1,0:T(8,128)(2,1)S(1)}, u32[]{:S(2)}, u32[]{:S(2)}) %collective-permute-start.19) | collective-permute-done | bytes 393248 | tf_op jit(solution)/shard_map/ppermute | solution.py:103
  73.7 0.0 collective-permute-done.21.refs_2_
  73.7 0.8 gradient_sum.1
  74.5 1.8 %collective-permute-start.22 = (f32[128,128]{1,0:T(8,128)S(1)}, f32[128,128]{1,0:T(8,128)S(1)}, u32[]{:S(2)}, u32[]{:S(2)}) collective-permute-start(f32[128,128]{1,0:T(8,128)S(1)} %get-tuple-element.69.gram), channel_id=1, source_target_pairs={{0,2},{1,3},{2,0},{3,1},{4,6},{5,7},{6,4},{7,5},{8,10},{9,11},{10,... | collective-permute-start | bytes 196616 | tf_op jit(solution)/shard_map/ppermute | solution.py:103
  76.3 1.8 %key_value_sum.1 = (bf16[128,2048]{1,0:T(8,128)(2,1)}, bf16[128,2048]{1,0:T(8,128)(2,1)}) custom-call(s32[1,8]{1,0:T(1,128)S(1)} %copy-done.4, f32[128,2048]{1,0:T(8,128)S(1)} %get-tuple-element.43.dko, f32[128,2048]{1,0:T(8,128)S(1)} %get-tuple-element.44.dvo, bf16[2,128,2048]{2,1,0:T(8,128)(2,1)S(1)} %collective-permute-done.7.mate, ...), custom_call_target="tpu_custom_call" | custom-call | flops 1572864 | bytes 5242880 | tf_op jit(solution)/shard_map/key_value_sum/pallas_call | solution.py:442
  78.1 0.0 collective-permute-done.22.gram_other
  78.1 3.1 %newton_schulz.1 = (f32[128,384]{1,0:T(8,128)S(1)}, bf16[128,384]{1,0:T(8,128)(2,1)S(1)}, bf16[128,384]{1,0:T(8,128)(2,1)S(1)}, bf16[128,384]{1,0:T(8,128)(2,1)S(1)}) custom-call(f32[128,1536]{1,0:T(8,128)S(1)} %get-tuple-element.68.x, f32[128,128]{1,0:T(8,128)S(1)} %get-tuple-element.69.gram, f32[128,128]{1,0:T(8,128)S(1)} %collective-permute-done.22.gram_other), custom_call_target="tpu_custom_call" | custom-call | flops 301989888 | bytes 1572864 | tf_op jit(solution)/shard_map/newton_schulz/pallas_call | solution.py:473
  81.3 2.6 %collective-permute-start.23 = (bf16[128,384]{1,0:T(8,128)(2,1)S(1)}, bf16[128,384]{1,0:T(8,128)(2,1)S(1)}, u32[]{:S(2)}, u32[]{:S(2)}) collective-permute-start(bf16[128,384]{1,0:T(8,128)(2,1)S(1)} %get-tuple-element.71), channel_id=1, source_target_pairs={{0,1},{1,0},{2,3},{3,2},{4,5},{5,4},{6,7},{7,6},{8,9},{9,8},{10,11... | collective-permute-start | bytes 294920 | tf_op jit(solution)/shard_map/ppermute | solution.py:103
  83.9 1.7 %collective-permute-start.24 = (bf16[128,384]{1,0:T(8,128)(2,1)S(1)}, bf16[128,384]{1,0:T(8,128)(2,1)S(1)}, u32[]{:S(2)}, u32[]{:S(2)}) collective-permute-start(bf16[128,384]{1,0:T(8,128)(2,1)S(1)} %get-tuple-element.72), channel_id=1, source_target_pairs={{0,4},{1,5},{2,6},{3,7},{4,0},{5,1},{6,2},{7,3},{8,12},{9,13},{10,... | collective-permute-start | bytes 294920 | tf_op jit(solution)/shard_map/ppermute | solution.py:103
  85.6 0.0 collective-permute-start.25
  85.7 3.0 %collective-permute-done.24.refs_2_ = bf16[128,384]{1,0:T(8,128)(2,1)S(1)} collective-permute-done((bf16[128,384]{1,0:T(8,128)(2,1)S(1)}, bf16[128,384]{1,0:T(8,128)(2,1)S(1)}, u32[]{:S(2)}, u32[]{:S(2)}) %collective-permute-start.24) | collective-permute-done | bytes 98336 | tf_op jit(solution)/shard_map/ppermute | solution.py:103
  88.7 2.1 %collective-permute-done.25.refs_3_ = bf16[128,384]{1,0:T(8,128)(2,1)S(1)} collective-permute-done((bf16[128,384]{1,0:T(8,128)(2,1)S(1)}, bf16[128,384]{1,0:T(8,128)(2,1)S(1)}, u32[]{:S(2)}, u32[]{:S(2)}) %collective-permute-start.25) | collective-permute-done | bytes 98336 | tf_op jit(solution)/shard_map/ppermute | solution.py:103
  90.8 0.9 %update_rows.1 = f32[512,384]{1,0:T(8,128)} custom-call(f32[128,384]{1,0:T(8,128)S(1)} %get-tuple-element.70.refs_0_, bf16[128,384]{1,0:T(8,128)(2,1)S(1)} %collective-permute-done.23.refs_1_, bf16[128,384]{1,0:T(8,128)(2,1)S(1)} %collective-permute-done.24.refs_2_, bf16[128,384]{1,0:T(8,128)(2,1)S(1)} %collective-permute-done.25.refs_3_), custom_call_target="tpu_custom_call" | custom-call | flops 1 | bytes 1572864 | tf_op jit(solution)/shard_map/update_rows/pallas_call | solution.py:485
  (18 shorter events, 0.1 us)
Async XLA Ops:
  0.6 7.5 %copy-start.1 = (bf16[1,1,128,2048]{3,2,1,0:T(8,128)(2,1)S(1)}, bf16[1,1,128,2048]{3,2,1,0:T(8,128)(2,1)}, u32[]{:S(2)}) copy-start(bf16[1,1,128,2048]{3,2,1,0:T(8,128)(2,1)} %param.7) | copy-start | bytes 1572868
  0.6 7.5 %copy-start.2 = (bf16[1,1,128,2048]{3,2,1,0:T(8,128)(2,1)S(1)}, bf16[1,1,128,2048]{3,2,1,0:T(8,128)(2,1)}, u32[]{:S(2)}) copy-start(bf16[1,1,128,2048]{3,2,1,0:T(8,128)(2,1)} %param.8) | copy-start | bytes 1572868
  0.7 11.1 %collective-permute-start.2 = (bf16[128,2048]{1,0:T(8,128)(2,1)}, bf16[128,2048]{1,0:T(8,128)(2,1)S(1)}, u32[]{:S(2)}, u32[]{:S(2)}) collective-permute-start(bf16[128,2048]{1,0:T(8,128)(2,1)} %bitcast.25), channel_id=1, source_target_pairs={{1,2},{3,4},{4,3},{6,5},{9,10},{11,12},{12,11},{14,13},{17,18},{19... | collective-permute-start | bytes 1572872 | tf_op jit(solution)/shard_map/ppermute | solution.py:297
  5.3 12.0 %collective-permute-start.3 = (bf16[128,2048]{1,0:T(8,128)(2,1)}, bf16[128,2048]{1,0:T(8,128)(2,1)S(1)}, u32[]{:S(2)}, u32[]{:S(2)}) collective-permute-start(bf16[128,2048]{1,0:T(8,128)(2,1)} %bitcast.29), channel_id=1, source_target_pairs={{1,2},{3,4},{4,3},{6,5},{9,10},{11,12},{12,11},{14,13},{17,18},{19... | collective-permute-start | bytes 1572872 | tf_op jit(solution)/shard_map/ppermute | solution.py:298
  6.7 13.5 %copy-start = (bf16[1,1,128,2048]{3,2,1,0:T(8,128)(2,1)S(1)}, bf16[1,1,128,2048]{3,2,1,0:T(8,128)(2,1)}, u32[]{:S(2)}) copy-start(bf16[1,1,128,2048]{3,2,1,0:T(8,128)(2,1)} %param.6) | copy-start | bytes 1572868
  6.7 13.5 %copy-start.4 = (s32[1,8]{1,0:T(1,128)S(1)}, s32[1,8]{1,0:T(1,128)}, u32[]{:S(2)}) copy-start(s32[1,8]{1,0:T(1,128)} %near_ref.5) | copy-start | bytes 100
  8.1 12.1 %collective-permute-start = (bf16[128,2048]{1,0:T(8,128)(2,1)S(1)}, bf16[128,2048]{1,0:T(8,128)(2,1)S(1)}, u32[]{:S(2)}, u32[]{:S(2)}) collective-permute-start(bf16[128,2048]{1,0:T(8,128)(2,1)S(1)} %bitcast.26), channel_id=1, source_target_pairs={{0,1},{1,0},{2,3},{3,2},{4,5},{5,4},{6,7},{7,6},{8,9},{9,8},{10,11... | collective-permute-start | bytes 1572872 | tf_op jit(solution)/shard_map/ppermute | solution.py:103
  8.2 12.0 %collective-permute-start.1 = (bf16[128,2048]{1,0:T(8,128)(2,1)S(1)}, bf16[128,2048]{1,0:T(8,128)(2,1)S(1)}, u32[]{:S(2)}, u32[]{:S(2)}) collective-permute-start(bf16[128,2048]{1,0:T(8,128)(2,1)S(1)} %bitcast.30), channel_id=1, source_target_pairs={{0,1},{1,0},{2,3},{3,2},{4,5},{5,4},{6,7},{7,6},{8,9},{9,8},{10,11... | collective-permute-start | bytes 1572872 | tf_op jit(solution)/shard_map/ppermute | solution.py:103
  8.7 18.7 %collective-permute-start.4 = (bf16[128,1536]{1,0:T(8,128)(2,1)S(1)}, bf16[128,1536]{1,0:T(8,128)(2,1)S(1)}, u32[]{:S(2)}, u32[]{:S(2)}) collective-permute-start(bf16[128,1536]{1,0:T(8,128)(2,1)S(1)} %get-tuple-element.81), channel_id=1, source_target_pairs={{0,4},{1,5},{2,6},{3,7},{4,0},{5,1},{6,2},{7,3},{8,12},{9,13},{10,... | collective-permute-start | bytes 1179656 | tf_op jit(solution)/shard_map/ppermute | solution.py:103
  17.3 12.5 %collective-permute-start.5 = (bf16[128,1536]{1,0:T(8,128)(2,1)S(1)}, bf16[128,1536]{1,0:T(8,128)(2,1)S(1)}, u32[]{:S(2)}, u32[]{:S(2)}) collective-permute-start(bf16[128,1536]{1,0:T(8,128)(2,1)S(1)} %pad_maximum_fusion.1), channel_id=1, source_target_pairs={{0,2},{1,3},{2,0},{3,1},{4,6},{5,7},{6,4},{7,5},{8,10},{9,11},{10,... | collective-permute-start | bytes 1179656 | tf_op jit(solution)/shard_map/ppermute | solution.py:103
  20.2 3.2 %copy-start.3 = (bf16[1,1,128,2048]{3,2,1,0:T(8,128)(2,1)S(1)}, bf16[1,1,128,2048]{3,2,1,0:T(8,128)(2,1)}, u32[]{:S(2)}) copy-start(bf16[1,1,128,2048]{3,2,1,0:T(8,128)(2,1)} %param.9) | copy-start | bytes 1572868
  22.5 9.6 %collective-permute-start.11 = (bf16[2,512,128]{2,1,0:T(8,128)(2,1)S(1)}, bf16[2,512,128]{2,1,0:T(8,128)(2,1)S(1)}, u32[]{:S(2)}, u32[]{:S(2)}) collective-permute-start(bf16[2,512,128]{2,1,0:T(8,128)(2,1)S(1)} %get-tuple-element.78), channel_id=1, source_target_pairs={{0,4},{1,5},{2,6},{3,7},{4,0},{5,1},{6,2},{7,3},{8,12},{9,13},{10,... | collective-permute-start | bytes 786440 | tf_op jit(solution)/shard_map/ppermute | solution.py:103
  22.6 16.7 %collective-permute-start.10 = (bf16[2,512,128]{2,1,0:T(8,128)(2,1)S(1)}, bf16[2,512,128]{2,1,0:T(8,128)(2,1)S(1)}, u32[]{:S(2)}, u32[]{:S(2)}) collective-permute-start(bf16[2,512,128]{2,1,0:T(8,128)(2,1)S(1)} %get-tuple-element.60.refs_0_), channel_id=1, source_target_pairs={{0,2},{1,3},{2,0},{3,1},{4,6},{5,7},{6,4},{7,5},{8,10},{9,11},{10,... | collective-permute-start | bytes 786440 | tf_op jit(solution)/shard_map/ppermute | solution.py:103
  29.9 5.2 %collective-permute-start.6 = (bf16[1,128,768]{2,1,0:T(8,128)(2,1)S(1)}, bf16[1,128,768]{2,1,0:T(8,128)(2,1)S(1)}, u32[]{:S(2)}, u32[]{:S(2)}) collective-permute-start(bf16[1,128,768]{2,1,0:T(8,128)(2,1)S(1)} %get-tuple-element.83), channel_id=1, source_target_pairs={{0,4},{1,5},{2,6},{3,7},{4,0},{5,1},{6,2},{7,3},{8,12},{9,13},{10,... | collective-permute-start | bytes 589832 | tf_op jit(solution)/shard_map/ppermute | solution.py:103
  29.9 9.3 %collective-permute-start.14 = (bf16[1,128,768]{2,1,0:T(8,128)(2,1)S(1)}, bf16[1,128,768]{2,1,0:T(8,128)(2,1)S(1)}, u32[]{:S(2)}, u32[]{:S(2)}) collective-permute-start(bf16[1,128,768]{2,1,0:T(8,128)(2,1)S(1)} %get-tuple-element.82), channel_id=1, source_target_pairs={{0,4},{1,5},{2,6},{3,7},{4,0},{5,1},{6,2},{7,3},{8,12},{9,13},{10,... | collective-permute-start | bytes 589832 | tf_op jit(solution)/shard_map/ppermute | solution.py:103
  32.1 7.2 %collective-permute-start.12 = (bf16[1,512,128]{2,1,0:T(8,128)(2,1)S(1)}, bf16[1,512,128]{2,1,0:T(8,128)(2,1)S(1)}, u32[]{:S(2)}, u32[]{:S(2)}) collective-permute-start(bf16[1,512,128]{2,1,0:T(8,128)(2,1)S(1)} %get-tuple-element.85), channel_id=1, source_target_pairs={{0,2},{1,3},{2,0},{3,1},{4,6},{5,7},{6,4},{7,5},{8,10},{9,11},{10,... | collective-permute-start | bytes 393224 | tf_op jit(solution)/shard_map/ppermute | solution.py:103
  34.4 5.9 %collective-permute-start.13 = (bf16[1,512,128]{2,1,0:T(8,128)(2,1)S(1)}, bf16[1,512,128]{2,1,0:T(8,128)(2,1)S(1)}, u32[]{:S(2)}, u32[]{:S(2)}) collective-permute-start(bf16[1,512,128]{2,1,0:T(8,128)(2,1)S(1)} %get-tuple-element.84), channel_id=1, source_target_pairs={{0,2},{1,3},{2,0},{3,1},{4,6},{5,7},{6,4},{7,5},{8,10},{9,11},{10,... | collective-permute-start | bytes 393224 | tf_op jit(solution)/shard_map/ppermute | solution.py:103
  35.0 21.7 %collective-permute-start.7 = (bf16[2,128,2048]{2,1,0:T(8,128)(2,1)S(1)}, bf16[2,128,2048]{2,1,0:T(8,128)(2,1)S(1)}, u32[]{:S(2)}, u32[]{:S(2)}) collective-permute-start(bf16[2,128,2048]{2,1,0:T(8,128)(2,1)S(1)} %get-tuple-element.48), channel_id=1, source_target_pairs={{0,1},{1,0},{2,3},{3,2},{4,5},{5,4},{6,7},{7,6},{8,9},{9,8},{10,11... | collective-permute-start | bytes 3145736 | tf_op jit(solution)/shard_map/ppermute | solution.py:103
  41.0 2.8 %collective-permute-start.16 = (bf16[1,128,1536]{2,1,0:T(8,128)(2,1)S(1)}, bf16[1,128,1536]{2,1,0:T(8,128)(2,1)S(1)}, u32[]{:S(2)}, u32[]{:S(2)}) collective-permute-start(bf16[1,128,1536]{2,1,0:T(8,128)(2,1)S(1)} %get-tuple-element.59), channel_id=1, source_target_pairs={{0,1},{1,0},{2,3},{3,2},{4,5},{5,4},{6,7},{7,6},{8,9},{9,8},{10,11... | collective-permute-start | bytes 1179656 | tf_op jit(solution)/shard_map/ppermute | solution.py:103
  43.0 4.2 %collective-permute-start.20 = (bf16[1,128,1536]{2,1,0:T(8,128)(2,1)S(1)}, bf16[1,128,1536]{2,1,0:T(8,128)(2,1)S(1)}, u32[]{:S(2)}, u32[]{:S(2)}) collective-permute-start(bf16[1,128,1536]{2,1,0:T(8,128)(2,1)S(1)} %get-tuple-element.65), channel_id=1, source_target_pairs={{0,1},{1,0},{2,3},{3,2},{4,5},{5,4},{6,7},{7,6},{8,9},{9,8},{10,11... | collective-permute-start | bytes 1179656 | tf_op jit(solution)/shard_map/ppermute | solution.py:103
  43.8 10.4 %collective-permute-start.18 = (bf16[128,1536]{1,0:T(8,128)(2,1)S(1)}, bf16[128,1536]{1,0:T(8,128)(2,1)S(1)}, u32[]{:S(2)}, u32[]{:S(2)}) collective-permute-start(bf16[128,1536]{1,0:T(8,128)(2,1)S(1)} %block_sum.3), channel_id=1, source_target_pairs={{0,8},{8,0},{16,24},{24,16},{1,9},{9,1},{17,25},{25,17},{2,10},{10... | collective-permute-start | bytes 1179656 | tf_op jit(solution)/shard_map/ppermute | solution.py:103
  45.7 2.7 %collective-permute-start.17 = (bf16[1,128,1536]{2,1,0:T(8,128)(2,1)S(1)}, bf16[1,128,1536]{2,1,0:T(8,128)(2,1)S(1)}, u32[]{:S(2)}, u32[]{:S(2)}) collective-permute-start(bf16[1,128,1536]{2,1,0:T(8,128)(2,1)S(1)} %get-tuple-element.63), channel_id=1, source_target_pairs={{0,1},{1,0},{2,3},{3,2},{4,5},{5,4},{6,7},{7,6},{8,9},{9,8},{10,11... | collective-permute-start | bytes 1179656 | tf_op jit(solution)/shard_map/ppermute | solution.py:103
  47.1 9.6 %collective-permute-start.15 = (bf16[1,128,1536]{2,1,0:T(8,128)(2,1)S(1)}, bf16[1,128,1536]{2,1,0:T(8,128)(2,1)S(1)}, u32[]{:S(2)}, u32[]{:S(2)}) collective-permute-start(bf16[1,128,1536]{2,1,0:T(8,128)(2,1)S(1)} %get-tuple-element.57), channel_id=1, source_target_pairs={{0,1},{1,0},{2,3},{3,2},{4,5},{5,4},{6,7},{7,6},{8,9},{9,8},{10,11... | collective-permute-start | bytes 1179656 | tf_op jit(solution)/shard_map/ppermute | solution.py:103
  47.2 29.1 %collective-permute-start.8 = (bf16[128,2048]{1,0:T(8,128)(2,1)S(1)}, bf16[128,2048]{1,0:T(8,128)(2,1)S(1)}, u32[]{:S(2)}, u32[]{:S(2)}) collective-permute-start(bf16[128,2048]{1,0:T(8,128)(2,1)S(1)} %get-tuple-element.50), channel_id=1, source_target_pairs={{3,4},{5,6},{2,1},{4,3},{11,12},{13,14},{10,9},{12,11},{19,20},{21... | collective-permute-start | bytes 1572872 | tf_op jit(solution)/shard_map/ppermute | solution.py:432
  48.5 27.8 %collective-permute-start.9 = (bf16[128,2048]{1,0:T(8,128)(2,1)S(1)}, bf16[128,2048]{1,0:T(8,128)(2,1)S(1)}, u32[]{:S(2)}, u32[]{:S(2)}) collective-permute-start(bf16[128,2048]{1,0:T(8,128)(2,1)S(1)} %get-tuple-element.52), channel_id=1, source_target_pairs={{3,4},{5,6},{2,1},{4,3},{11,12},{13,14},{10,9},{12,11},{19,20},{21... | collective-permute-start | bytes 1572872 | tf_op jit(solution)/shard_map/ppermute | solution.py:433
  54.3 19.4 %collective-permute-start.19 = (bf16[128,1536]{1,0:T(8,128)(2,1)S(1)}, bf16[128,1536]{1,0:T(8,128)(2,1)S(1)}, u32[]{:S(2)}, u32[]{:S(2)}) collective-permute-start(bf16[128,1536]{1,0:T(8,128)(2,1)S(1)} %block_sum.4), channel_id=1, source_target_pairs={{0,16},{8,24},{16,0},{24,8},{1,17},{9,25},{17,1},{25,9},{2,18},{10... | collective-permute-start | bytes 1179656 | tf_op jit(solution)/shard_map/ppermute | solution.py:103
  56.7 17.0 %collective-permute-start.21 = (bf16[128,1536]{1,0:T(8,128)(2,1)S(1)}, bf16[128,1536]{1,0:T(8,128)(2,1)S(1)}, u32[]{:S(2)}, u32[]{:S(2)}) collective-permute-start(bf16[128,1536]{1,0:T(8,128)(2,1)S(1)} %block_sum.5), channel_id=1, source_target_pairs={{0,8},{8,0},{16,24},{24,16},{1,9},{9,1},{17,25},{25,17},{2,10},{10... | collective-permute-start | bytes 1179656 | tf_op jit(solution)/shard_map/ppermute | solution.py:103
  74.5 3.6 %collective-permute-start.22 = (f32[128,128]{1,0:T(8,128)S(1)}, f32[128,128]{1,0:T(8,128)S(1)}, u32[]{:S(2)}, u32[]{:S(2)}) collective-permute-start(f32[128,128]{1,0:T(8,128)S(1)} %get-tuple-element.69.gram), channel_id=1, source_target_pairs={{0,2},{1,3},{2,0},{3,1},{4,6},{5,7},{6,4},{7,5},{8,10},{9,11},{10,... | collective-permute-start | bytes 196616 | tf_op jit(solution)/shard_map/ppermute | solution.py:103
  81.3 4.4 %collective-permute-start.23 = (bf16[128,384]{1,0:T(8,128)(2,1)S(1)}, bf16[128,384]{1,0:T(8,128)(2,1)S(1)}, u32[]{:S(2)}, u32[]{:S(2)}) collective-permute-start(bf16[128,384]{1,0:T(8,128)(2,1)S(1)} %get-tuple-element.71), channel_id=1, source_target_pairs={{0,1},{1,0},{2,3},{3,2},{4,5},{5,4},{6,7},{7,6},{8,9},{9,8},{10,11... | collective-permute-start | bytes 294920 | tf_op jit(solution)/shard_map/ppermute | solution.py:103
  83.9 4.8 %collective-permute-start.24 = (bf16[128,384]{1,0:T(8,128)(2,1)S(1)}, bf16[128,384]{1,0:T(8,128)(2,1)S(1)}, u32[]{:S(2)}, u32[]{:S(2)}) collective-permute-start(bf16[128,384]{1,0:T(8,128)(2,1)S(1)} %get-tuple-element.72), channel_id=1, source_target_pairs={{0,4},{1,5},{2,6},{3,7},{4,0},{5,1},{6,2},{7,3},{8,12},{9,13},{10,... | collective-permute-start | bytes 294920 | tf_op jit(solution)/shard_map/ppermute | solution.py:103
  85.6 5.1 %collective-permute-start.25 = (bf16[128,384]{1,0:T(8,128)(2,1)S(1)}, bf16[128,384]{1,0:T(8,128)(2,1)S(1)}, u32[]{:S(2)}, u32[]{:S(2)}) collective-permute-start(bf16[128,384]{1,0:T(8,128)(2,1)S(1)} %get-tuple-element.73), channel_id=1, source_target_pairs={{0,5},{1,4},{2,7},{3,6},{4,1},{5,0},{6,3},{7,2},{8,13},{9,12},{10,... | collective-permute-start | bytes 294920 | tf_op jit(solution)/shard_map/ppermute | solution.py:103

commit v16 on v15

--- a/solution.py
+++ b/solution.py
@@ -62,10 +62,10 @@
     return high, middle, (rest - middle.astype(f32)).astype(bf16)
 
 
-def square_dot(a, b):
+def split_dot(a, b):
     a_high, a_middle, a_low = a
     b_high, b_middle, b_low = b
-    size = a_high.shape[0]
+    size = b_high.shape[1]
     left = jnp.concatenate([a_high, a_middle], 1)
     right = jnp.concatenate(
         [jnp.concatenate([b_high, b_high], 0), jnp.concatenate([b_middle, b_middle], 0)], 1
@@ -190,13 +190,14 @@
         out[...] = (total + jnp.where(from_other, beyond[...].astype(f32), 0.0)).astype(bf16)
 
 
-def product_kernel(counts, layers, *refs):
+def product_kernel(counts, layers, cores, *refs):
     att = list(refs[: sum(counts)])
-    cols, *outs, for_mate, gathered = refs[sum(counts) :]
+    cols, *outs, gathered = refs[sum(counts) :]
+    owns, for_mate = outs[: len(layers) * (0 in cores)], outs[-1]
     for t, count in enumerate(counts):
         at = slice(t * HEAD_DIM, (t + 1) * HEAD_DIM)
         parts, att = att[:count], att[count:]
-        for core in range(2):
+        for core in cores:
             part, row = (parts[0], core) if count == 1 else (parts[core], 0)
             for n, i in enumerate(layers):
                 block = part[row, i * HEAD_DIM : (i + 1) * HEAD_DIM, :]
@@ -205,10 +206,12 @@
     step = 512 if width % 512 == 0 else width
     for c in range(0, width, step):
         block = cols[:, :, c : c + step].reshape(tokens, step)
-        for n, out in enumerate(outs):
+        for n in range(len(layers)):
             rows = slice(n * HEAD_DIM, (n + 1) * HEAD_DIM)
-            out[:, c : c + step] = dot_n(gathered[0, rows, :], block)
-            for_mate[n, :, c : c + step] = dot_n(gathered[1, rows, :], block).astype(bf16)
+            if 0 in cores:
+                owns[n][:, c : c + step] = dot_n(gathered[0, rows, :], block)
+            if 1 in cores:
+                for_mate[n, :, c : c + step] = dot_n(gathered[1, rows, :], block).astype(bf16)
 
 
 def piece(ref, lead, start, size):
@@ -246,11 +249,11 @@
     p = None
     for turn in range(NS_STEPS):
         a_parts = parts_of(a)
-        q = coeff_a * eye + coeff_b * a + coeff_c * square_dot(a_parts, a_parts)
+        q = coeff_a * eye + coeff_b * a + coeff_c * split_dot(a_parts, a_parts)
         q_parts = parts_of(q)
-        p = q if p is None else square_dot(q_parts, parts_of(p))
+        p = q if p is None else split_dot(q_parts, parts_of(p))
         if turn + 1 < NS_STEPS:
-            a = square_dot(parts_of(square_dot(q_parts, a_parts)), q_parts)
+            a = split_dot(parts_of(split_dot(q_parts, a_parts)), q_parts)
     return p, inverse
 
 
@@ -258,7 +261,9 @@
     mine = plan.row_part(lax.axis_index("seq"))
     p, inverse = polynomial(gram[...] + gram_other[...])
     p = p * (inverse * factor)
+    p_parts = parts_of(p)
     width = outs[0].shape[1]
+    wide = width % HEAD_DIM == 0
     for j in range(plan.per_target):
         if width % HEAD_DIM == 0:
             block = x[:, pl.ds(pl.multiple_of((mine ^ j) * width, width), width)]
@@ -267,11 +272,13 @@
             for r in range(plan.per_target):
                 part = x[:, r * width : (r + 1) * width]
                 block = jnp.where((mine ^ j) == r, part, block)
-        outs[j][...] = exact(p, block).astype(outs[j].dtype)
+        piece_out = split_dot(p_parts, parts_of(block)) if wide else exact(p, block)
+        outs[j][...] = piece_out.astype(outs[j].dtype)
 
 
 def place_kernel(plan, *refs):
     *parts, out = refs
+    parts = parts[::-1]
     mine = plan.row_part(lax.axis_index("seq"))
     for j, part in enumerate(parts):
         at = pl.ds(pl.multiple_of((mine ^ j) * HEAD_DIM, HEAD_DIM), HEAD_DIM)
@@ -377,22 +384,33 @@
         held.append(jnp.concatenate([high_columns[high - 1][None], rest], 0))
     held = jnp.concatenate(held, 0)
 
-    def product(name, layers, *operands):
-        *blocks, for_mate = pl.pallas_call(
-            functools.partial(product_kernel, counts, layers),
-            out_shape=[struct((HEAD_DIM, mine_width), f32)] * len(layers)
-            + [struct((len(layers), HEAD_DIM, mine_width), bf16)],
+    def product(name, layers, cores, *operands):
+        shapes = [struct((HEAD_DIM, mine_width), f32)] * (len(layers) * (0 in cores))
+        shapes += [struct((len(layers), HEAD_DIM, mine_width), bf16)] * (1 in cores)
+        return pl.pallas_call(
+            functools.partial(product_kernel, counts, layers, cores),
+            out_shape=shapes,
             in_specs=whole(len(pairs) + 1),
-            out_specs=whole(len(layers) + 1),
+            out_specs=whole(len(shapes)),
             scratch_shapes=[pltpu.VMEM((2, len(layers) * HEAD_DIM, plan.pairs * tile), bf16)],
             compiler_params=params(),
             cost_estimate=cost(
-                2 * len(layers) * HEAD_DIM * n * tile * mine_width, n * tile * mine_width
+                len(cores) * len(layers) * HEAD_DIM * n * tile * mine_width,
+                n * tile * mine_width,
             ),
             name=name,
         )(*operands)
+
+    def swapped(layers, blocks, for_mate):
         mate = shift(for_mate, "seq", 1)
-        return {i: [(block, None, 0), (mate, k, 0)] for k, (i, block) in enumerate(zip(layers, blocks))}
+        return {
+            i: [(block, None, 0), (mate, k, 0)]
+            for k, (i, block) in enumerate(zip(layers, blocks, strict=True))
+        }
+
+    def product_pair(name, layers, *operands):
+        *blocks, for_mate = product(name, layers, (0, 1), *operands)
+        return swapped(layers, blocks, for_mate)
 
     def added(parts, start, size):
         return pl.pallas_call(
@@ -407,12 +425,14 @@
 
     first = [i for i in range(m - 1, 1, -1) if i & 1]
     middle = [i for i in range(m - 1, 1, -1) if not i & 1]
-    blocks = product("product_first", first, after(pairs[0], dq), *pairs[1:], held)
+    (for_mate,) = product("product_mate", first, (1,), after(pairs[0], dq), *pairs[1:], held)
+    own_first = product("product_first", first, (0,), after(pairs[0], for_mate), *pairs[1:], held)
+    blocks = swapped(first, own_first, for_mate)
     going = {i: added(blocks[i], 0, mine_width) for i in first}
-    blocks |= product("product_middle", middle, after(pairs[0], *going.values()), *pairs[1:], held)
-
-    blocks |= product("product_near", [1], after(pairs[0], dq), *pairs[1:], held)
-    blocks |= product("product_own", [0], after(pairs[0], dq), *pairs[1:], held)
+    blocks |= product_pair("product_middle", middle, after(pairs[0], *going.values()), *pairs[1:], held)
+
+    blocks |= product_pair("product_near", [1], after(pairs[0], dq), *pairs[1:], held)
+    blocks |= product_pair("product_own", [0], after(pairs[0], dq), *pairs[1:], held)
 
     extra = {i: [] for i in range(m)}
     sent = []
@@ -490,7 +510,7 @@
         compiler_params=params(),
         cost_estimate=cost(1, 8 * per * HEAD_DIM * slot),
         name="update_rows",
-    )(*pieces)
+    )(*reversed(pieces))
 
     shape = query_tiles.shape
     return dq.reshape(shape), dk.reshape(shape), dv.reshape(shape), update

time: 92.3 us -> 91.7 us (level)
  waiting for transfers between devices: 36.1 us -> 35 us
    ppermute x22, waiting for transfers between devices: 30.4 us -> 29.2 us  [shift(): lax.ppermute(value, axis, [(i, i ^ mask) for i in range(lax.axis_size(axi...]
    pallas_call x4 -> x5, Pallas kernels: 2.38 us -> 2.53 us  [product(): pl.pallas_call(functools.partial(product_kernel, counts, layers, cores),...]
where the time goes in v16:
time: 91.7 us; the launch traced here: 90.8 us
  starting transfers between devices  37.7 us (41%)
  waiting for transfers between devices  35 us (38%)
  Pallas kernels  15.5 us (17%)
  local copies, waits for them, and re-layouts  1.43 us (2%)
  between operations  0.93 us (1%)
    ppermute x22, waiting for transfers between devices, shift(): lax.ppermute(value, axis, [(i, i ^ mask) for i in range(lax.axis_size(axi...  29.2 us
    ppermute x22, starting transfers between devices, shift(): lax.ppermute(value, axis, [(i, i ^ mask) for i in range(lax.axis_size(axi...  29 us
    ppermute x1, waiting for transfers between devices, local(): value_next = lax.ppermute(value, 'seq', takes)  5.62 us
    ppermute x1, starting transfers between devices, local(): key_next = lax.ppermute(key, 'seq', takes)  4.67 us
    pallas_call x1, Pallas kernels, local(): pl.pallas_call(backward_kernel, out_shape=[struct((tile, width), bf16), s...  3.97 us
    pallas_call x1, Pallas kernels, local(): pl.pallas_call(functools.partial(update_kernel, plan, factor), out_shape=...  2.87 us
    pallas_call x5, Pallas kernels, product(): pl.pallas_call(functools.partial(product_kernel, counts, layers, cores),...  2.53 us
    pallas_call x1, Pallas kernels, local(): pl.pallas_call(functools.partial(forward_kernel, plan), out_shape=struct(...  2.3 us
  transfers between devices with their start and end apart: 26, of which 12 were waited for; matrix products, arithmetic and copies ran while one was open for 2% of the time, Pallas kernels for 13%

profile of v16, /device:TPU:1, one launch (start us, length us, event | category | flops | bytes accessed | tf_op | source)
XLA Modules:
  0.0 90.8 jit_solution(10480049381986184767)
XLA Ops:
  0.7 4.7 %collective-permute-start.2 = (bf16[128,2048]{1,0:T(8,128)(2,1)}, bf16[128,2048]{1,0:T(8,128)(2,1)S(1)}, u32[]{:S(2)}, u32[]{:S(2)}) collective-permute-start(bf16[128,2048]{1,0:T(8,128)(2,1)} %bitcast.25), channel_id=1, source_target_pairs={{1,2},{3,4},{4,3},{6,5},{9,10},{11,12},{12,11},{14,13},{17,18},{19... | collective-permute-start | bytes 1572872 | tf_op jit(solution)/shard_map/ppermute | solution.py:304
  5.3 1.3 %collective-permute-start.3 = (bf16[128,2048]{1,0:T(8,128)(2,1)}, bf16[128,2048]{1,0:T(8,128)(2,1)S(1)}, u32[]{:S(2)}, u32[]{:S(2)}) collective-permute-start(bf16[128,2048]{1,0:T(8,128)(2,1)} %bitcast.29), channel_id=1, source_target_pairs={{1,2},{3,4},{4,3},{6,5},{9,10},{11,12},{12,11},{14,13},{17,18},{19... | collective-permute-start | bytes 1572872 | tf_op jit(solution)/shard_map/ppermute | solution.py:305
  6.7 1.3 %dynamic-slice_bitcast_fusion.1 = (bf16[128,768]{1,0:T(8,128)(2,1)S(1)}, bf16[128,768]{1,0:T(8,128)(2,1)S(1)}, bf16[128,768]{1,0:T(8,128)(2,1)S(1)}, bf16[128,768]{1,0:T(8,128)(2,1)S(1)}) fusion(bf16[1,1,128,3072]{3,2,1,0:T(8,128)(2,1)} %param.10, s32[]{:T(128)S(6)} %select_n.14, s32[]{:T(128)S(6)} %select_n.13, s32[]{:T(128)S(6)} %select_n.12, s32[]{:T(128)S(6)} %select_n.15), kind=kLoop, calls=%fused_computation.6 | loop fusion | bytes 1572880 | tf_op jit(solution)/shard_map/dynamic_slice | solution.py:314
  8.0 0.1 fusion
  8.1 0.1 collective-permute-start
  8.2 0.5 collective-permute-start.1
  8.7 2.9 %collective-permute-start.4 = (bf16[128,1536]{1,0:T(8,128)(2,1)S(1)}, bf16[128,1536]{1,0:T(8,128)(2,1)S(1)}, u32[]{:S(2)}, u32[]{:S(2)}) collective-permute-start(bf16[128,1536]{1,0:T(8,128)(2,1)S(1)} %get-tuple-element.79), channel_id=1, source_target_pairs={{0,4},{1,5},{2,6},{3,7},{4,0},{5,1},{6,2},{7,3},{8,12},{9,13},{10,... | collective-permute-start | bytes 1179656 | tf_op jit(solution)/shard_map/ppermute | solution.py:103
  11.6 0.1 collective-permute-done.2.kn
  11.7 5.6 %collective-permute-done.3.vn = bf16[128,2048]{1,0:T(8,128)(2,1)S(1)} collective-permute-done((bf16[128,2048]{1,0:T(8,128)(2,1)}, bf16[128,2048]{1,0:T(8,128)(2,1)S(1)}, u32[]{:S(2)}, u32[]{:S(2)}) %collective-permute-start.3) | collective-permute-done | bytes 524320 | tf_op jit(solution)/shard_map/ppermute | solution.py:305
  17.3 2.8 %collective-permute-start.5 = (bf16[128,1536]{1,0:T(8,128)(2,1)S(1)}, bf16[128,1536]{1,0:T(8,128)(2,1)S(1)}, u32[]{:S(2)}, u32[]{:S(2)}) collective-permute-start(bf16[128,1536]{1,0:T(8,128)(2,1)S(1)} %pad_maximum_fusion.1), channel_id=1, source_target_pairs={{0,2},{1,3},{2,0},{3,1},{4,6},{5,7},{6,4},{7,5},{8,10},{9,11},{10,... | collective-permute-start | bytes 1179656 | tf_op jit(solution)/shard_map/ppermute | solution.py:103
  20.2 0.0 copy-start.3
  20.2 2.3 %attention_forward.1 = bf16[2,2,512,128]{3,2,1,0:T(8,128)(2,1)S(1)} custom-call(s32[1,8]{1,0:T(1,128)S(1)} %copy-done.4, bf16[128,2048]{1,0:T(8,128)(2,1)S(1)} %bitcast.23, bf16[128,2048]{1,0:T(8,128)(2,1)S(1)} %bitcast.27, bf16[128,2048]{1,0:T(8,128)(2,1)S(1)} %bitcast.31, bf16[128,2048]{1,0:T(8,128)(2,1)S(1)} %collective-permute-done.km, ...), custom_call_target="tpu_custom_call" | custom-call | flops 268435456 | bytes 4194304 | tf_op jit(solution)/shard_map/attention_forward/pallas_call | solution.py:333
  22.5 0.1 collective-permute-start.11
  22.6 0.8 collective-permute-start.10
  23.4 4.0 %attention_backward.1 = (bf16[128,2048]{1,0:T(8,128)(2,1)}, f32[128,2048]{1,0:T(8,128)S(1)}, f32[128,2048]{1,0:T(8,128)S(1)}, bf16[128,2048]{1,0:T(8,128)(2,1)S(...) custom-call(s32[1,8]{1,0:T(1,128)S(1)} %copy-done.4, bf16[128,2048]{1,0:T(8,128)(2,1)S(1)} %bitcast.24, ...), custom_call_target="tpu_custom_call" | custom-call | flops 1 | bytes 1 | tf_op jit(solution)/shard_map/attention_backward/pallas_call | solution.py:359
  27.4 0.0 collective-permute-done.4
  27.4 2.5 %collective-permute-done.5 = bf16[128,1536]{1,0:T(8,128)(2,1)S(1)} collective-permute-done((bf16[128,1536]{1,0:T(8,128)(2,1)S(1)}, bf16[128,1536]{1,0:T(8,128)(2,1)S(1)}, u32[]{:S(2)}, u32[]{:S(2)}) %collective-permute-start.5) | collective-permute-done | bytes 393248 | tf_op jit(solution)/shard_map/ppermute | solution.py:103
  29.9 0.1 collective-permute-start.6
  29.9 1.5 %collective-permute-start.14 = (bf16[1,128,768]{2,1,0:T(8,128)(2,1)S(1)}, bf16[1,128,768]{2,1,0:T(8,128)(2,1)S(1)}, u32[]{:S(2)}, u32[]{:S(2)}) collective-permute-start(bf16[1,128,768]{2,1,0:T(8,128)(2,1)S(1)} %get-tuple-element.80), channel_id=1, source_target_pairs={{0,4},{1,5},{2,6},{3,7},{4,0},{5,1},{6,2},{7,3},{8,12},{9,13},{10,... | collective-permute-start | bytes 589832 | tf_op jit(solution)/shard_map/ppermute | solution.py:103
  31.4 0.7 collective-permute-done.11.refs_2_
  32.1 2.3 %collective-permute-start.12 = (bf16[1,512,128]{2,1,0:T(8,128)(2,1)S(1)}, bf16[1,512,128]{2,1,0:T(8,128)(2,1)S(1)}, u32[]{:S(2)}, u32[]{:S(2)}) collective-permute-start(bf16[1,512,128]{2,1,0:T(8,128)(2,1)S(1)} %get-tuple-element.83), channel_id=1, source_target_pairs={{0,2},{1,3},{2,0},{3,1},{4,6},{5,7},{6,4},{7,5},{8,10},{9,11},{10,... | collective-permute-start | bytes 393224 | tf_op jit(solution)/shard_map/ppermute | solution.py:103
  34.4 0.1 collective-permute-start.13
  34.5 0.5 collective-permute-done.6
  35.0 4.1 %collective-permute-start.7 = (bf16[2,128,2048]{2,1,0:T(8,128)(2,1)S(1)}, bf16[2,128,2048]{2,1,0:T(8,128)(2,1)S(1)}, u32[]{:S(2)}, u32[]{:S(2)}) collective-permute-start(bf16[2,128,2048]{2,1,0:T(8,128)(2,1)S(1)} %get-tuple-element.47), channel_id=1, source_target_pairs={{0,1},{1,0},{2,3},{3,2},{4,5},{5,4},{6,7},{7,6},{8,9},{9,8},{10,11... | collective-permute-start | bytes 3145736 | tf_op jit(solution)/shard_map/ppermute | solution.py:103
  39.1 0.1 collective-permute-done.14
  39.2 0.1 maximum_maximum_fusion.refs_5_
  39.4 0.0 collective-permute-done.10.refs_1_
  39.4 0.0 collective-permute-done.12.refs_3_
  39.4 1.0 %collective-permute-done.13.refs_4_ = bf16[1,512,128]{2,1,0:T(8,128)(2,1)S(1)} collective-permute-done((bf16[1,512,128]{2,1,0:T(8,128)(2,1)S(1)}, bf16[1,512,128]{2,1,0:T(8,128)(2,1)S(1)}, u32[]{:S(2)}, u32[]{:S(2)}) %collective-permute-start.13) | collective-permute-done | bytes 131104 | tf_op jit(solution)/shard_map/ppermute | solution.py:103
  40.4 0.4 product_mate.1
  40.7 1.4 %collective-permute-start.16 = (bf16[1,128,1536]{2,1,0:T(8,128)(2,1)S(1)}, bf16[1,128,1536]{2,1,0:T(8,128)(2,1)S(1)}, u32[]{:S(2)}, u32[]{:S(2)}) collective-permute-start(bf16[1,128,1536]{2,1,0:T(8,128)(2,1)S(1)} %product_mate.1), channel_id=1, source_target_pairs={{0,1},{1,0},{2,3},{3,2},{4,5},{5,4},{6,7},{7,6},{8,9},{9,8},{10,11... | collective-permute-start | bytes 1179656 | tf_op jit(solution)/shard_map/ppermute | solution.py:103
  42.1 0.6 product_near.1
  42.7 0.1 collective-permute-start.20
  42.8 0.4 product_first.1.refs_0_
  43.2 0.3 collective-permute-done.16.refs_1_
  43.5 0.1 block_sum.3
  43.6 1.4 %collective-permute-start.18 = (bf16[128,1536]{1,0:T(8,128)(2,1)S(1)}, bf16[128,1536]{1,0:T(8,128)(2,1)S(1)}, u32[]{:S(2)}, u32[]{:S(2)}) collective-permute-start(bf16[128,1536]{1,0:T(8,128)(2,1)S(1)} %block_sum.3), channel_id=1, source_target_pairs={{0,8},{8,0},{16,24},{24,16},{1,9},{9,1},{17,25},{25,17},{2,10},{10... | collective-permute-start | bytes 1179656 | tf_op jit(solution)/shard_map/ppermute | solution.py:103
  44.9 0.6 product_middle.1
  45.5 0.7 collective-permute-start.17
  46.2 0.6 product_own.1
  46.8 0.1 collective-permute-start.15
  46.9 0.0 collective-permute-done.20.refs_1_
  46.9 1.3 %collective-permute-start.8 = (bf16[128,2048]{1,0:T(8,128)(2,1)S(1)}, bf16[128,2048]{1,0:T(8,128)(2,1)S(1)}, u32[]{:S(2)}, u32[]{:S(2)}) collective-permute-start(bf16[128,2048]{1,0:T(8,128)(2,1)S(1)} %get-tuple-element.49), channel_id=1, source_target_pairs={{3,4},{5,6},{2,1},{4,3},{11,12},{13,14},{10,9},{12,11},{19,20},{21... | collective-permute-start | bytes 1572872 | tf_op jit(solution)/shard_map/ppermute | solution.py:452
  48.2 0.0 collective-permute-done.17.refs_1_
  48.2 1.5 %collective-permute-start.9 = (bf16[128,2048]{1,0:T(8,128)(2,1)S(1)}, bf16[128,2048]{1,0:T(8,128)(2,1)S(1)}, u32[]{:S(2)}, u32[]{:S(2)}) collective-permute-start(bf16[128,2048]{1,0:T(8,128)(2,1)S(1)} %get-tuple-element.51), channel_id=1, source_target_pairs={{3,4},{5,6},{2,1},{4,3},{11,12},{13,14},{10,9},{12,11},{19,20},{21... | collective-permute-start | bytes 1572872 | tf_op jit(solution)/shard_map/ppermute | solution.py:453
  49.7 0.1 block_sum.5
  49.8 4.1 %collective-permute-done.18.refs_2_ = bf16[128,1536]{1,0:T(8,128)(2,1)S(1)} collective-permute-done((bf16[128,1536]{1,0:T(8,128)(2,1)S(1)}, bf16[128,1536]{1,0:T(8,128)(2,1)S(1)}, u32[]{:S(2)}, u32[]{:S(2)}) %collective-permute-start.18) | collective-permute-done | bytes 393248 | tf_op jit(solution)/shard_map/ppermute | solution.py:103
  54.0 0.1 block_sum.4
  54.1 2.4 %collective-permute-start.19 = (bf16[128,1536]{1,0:T(8,128)(2,1)S(1)}, bf16[128,1536]{1,0:T(8,128)(2,1)S(1)}, u32[]{:S(2)}, u32[]{:S(2)}) collective-permute-start(bf16[128,1536]{1,0:T(8,128)(2,1)S(1)} %block_sum.4), channel_id=1, source_target_pairs={{0,16},{8,24},{16,0},{24,8},{1,17},{9,25},{17,1},{25,9},{2,18},{10... | collective-permute-start | bytes 1179656 | tf_op jit(solution)/shard_map/ppermute | solution.py:103
  56.4 0.0 collective-permute-done.15.refs_0_
  56.5 1.3 %collective-permute-start.21 = (bf16[128,1536]{1,0:T(8,128)(2,1)S(1)}, bf16[128,1536]{1,0:T(8,128)(2,1)S(1)}, u32[]{:S(2)}, u32[]{:S(2)}) collective-permute-start(bf16[128,1536]{1,0:T(8,128)(2,1)S(1)} %block_sum.5), channel_id=1, source_target_pairs={{0,8},{8,0},{16,24},{24,16},{1,9},{9,1},{17,25},{25,17},{2,10},{10... | collective-permute-start | bytes 1179656 | tf_op jit(solution)/shard_map/ppermute | solution.py:103
  57.7 15.7 %collective-permute-done.19.refs_1_ = bf16[128,1536]{1,0:T(8,128)(2,1)S(1)} collective-permute-done((bf16[128,1536]{1,0:T(8,128)(2,1)S(1)}, bf16[128,1536]{1,0:T(8,128)(2,1)S(1)}, u32[]{:S(2)}, u32[]{:S(2)}) %collective-permute-start.19) | collective-permute-done | bytes 393248 | tf_op jit(solution)/shard_map/ppermute | solution.py:103
  73.5 0.0 collective-permute-done.21.refs_2_
  73.5 0.8 gradient_sum.1
  74.3 1.8 %collective-permute-start.22 = (f32[128,128]{1,0:T(8,128)S(1)}, f32[128,128]{1,0:T(8,128)S(1)}, u32[]{:S(2)}, u32[]{:S(2)}) collective-permute-start(f32[128,128]{1,0:T(8,128)S(1)} %get-tuple-element.67.gram), channel_id=1, source_target_pairs={{0,2},{1,3},{2,0},{3,1},{4,6},{5,7},{6,4},{7,5},{8,10},{9,11},{10,... | collective-permute-start | bytes 196616 | tf_op jit(solution)/shard_map/ppermute | solution.py:103
  76.1 0.0 collective-permute-done.8.kn
  76.1 0.0 collective-permute-done.9.vn
  76.1 1.8 %key_value_sum.1 = (bf16[128,2048]{1,0:T(8,128)(2,1)}, bf16[128,2048]{1,0:T(8,128)(2,1)}) custom-call(s32[1,8]{1,0:T(1,128)S(1)} %copy-done.4, f32[128,2048]{1,0:T(8,128)S(1)} %get-tuple-element.42.dko, f32[128,2048]{1,0:T(8,128)S(1)} %get-tuple-element.43.dvo, bf16[2,128,2048]{2,1,0:T(8,128)(2,1)S(1)} %collective-permute-done.7.mate, ...), custom_call_target="tpu_custom_call" | custom-call | flops 1572864 | bytes 5242880 | tf_op jit(solution)/shard_map/key_value_sum/pallas_call | solution.py:462
  77.9 2.9 %newton_schulz.1 = (f32[128,384]{1,0:T(8,128)S(1)}, bf16[128,384]{1,0:T(8,128)(2,1)S(1)}, bf16[128,384]{1,0:T(8,128)(2,1)S(1)}, bf16[128,384]{1,0:T(8,128)(2,1)S(1)}) custom-call(f32[128,1536]{1,0:T(8,128)S(1)} %get-tuple-element.66.x, f32[128,128]{1,0:T(8,128)S(1)} %get-tuple-element.67.gram, f32[128,128]{1,0:T(8,128)S(1)} %collective-permute-done.22.gram_other), custom_call_target="tpu_custom_call" | custom-call | flops 301989888 | bytes 1572864 | tf_op jit(solution)/shard_map/newton_schulz/pallas_call | solution.py:493
  80.8 4.3 %collective-permute-start.23 = (bf16[128,384]{1,0:T(8,128)(2,1)S(1)}, bf16[128,384]{1,0:T(8,128)(2,1)S(1)}, u32[]{:S(2)}, u32[]{:S(2)}) collective-permute-start(bf16[128,384]{1,0:T(8,128)(2,1)S(1)} %get-tuple-element.68), channel_id=1, source_target_pairs={{0,5},{1,4},{2,7},{3,6},{4,1},{5,0},{6,3},{7,2},{8,13},{9,12},{10,... | collective-permute-start | bytes 294920 | tf_op jit(solution)/shard_map/ppermute | solution.py:103
  85.0 0.5 collective-permute-start.25
  85.5 2.7 %collective-permute-done.23.refs_0_ = bf16[128,384]{1,0:T(8,128)(2,1)S(1)} collective-permute-done((bf16[128,384]{1,0:T(8,128)(2,1)S(1)}, bf16[128,384]{1,0:T(8,128)(2,1)S(1)}, u32[]{:S(2)}, u32[]{:S(2)}) %collective-permute-start.23) | collective-permute-done | bytes 98336 | tf_op jit(solution)/shard_map/ppermute | solution.py:103
  88.2 1.7 %collective-permute-done.24.refs_1_ = bf16[128,384]{1,0:T(8,128)(2,1)S(1)} collective-permute-done((bf16[128,384]{1,0:T(8,128)(2,1)S(1)}, bf16[128,384]{1,0:T(8,128)(2,1)S(1)}, u32[]{:S(2)}, u32[]{:S(2)}) %collective-permute-start.24) | collective-permute-done | bytes 98336 | tf_op jit(solution)/shard_map/ppermute | solution.py:103
  89.9 0.9 %update_rows.1 = f32[512,384]{1,0:T(8,128)} custom-call(bf16[128,384]{1,0:T(8,128)(2,1)S(1)} %collective-permute-done.23.refs_0_, bf16[128,384]{1,0:T(8,128)(2,1)S(1)} %collective-permute-done.24.refs_1_, bf16[128,384]{1,0:T(8,128)(2,1)S(1)} %collective-permute-done.25.refs_2_, f32[128,384]{1,0:T(8,128)S(1)} %get-tuple-element.71.refs_3_), custom_call_target="tpu_custom_call" | custom-call | flops 1 | bytes 1572864 | tf_op jit(solution)/shard_map/update_rows/pallas_call | solution.py:505
  (19 shorter events, 0.1 us)
Async XLA Ops:
  0.6 7.5 %copy-start.1 = (bf16[1,1,128,2048]{3,2,1,0:T(8,128)(2,1)S(1)}, bf16[1,1,128,2048]{3,2,1,0:T(8,128)(2,1)}, u32[]{:S(2)}) copy-start(bf16[1,1,128,2048]{3,2,1,0:T(8,128)(2,1)} %param.7) | copy-start | bytes 1572868
  0.6 7.5 %copy-start.2 = (bf16[1,1,128,2048]{3,2,1,0:T(8,128)(2,1)S(1)}, bf16[1,1,128,2048]{3,2,1,0:T(8,128)(2,1)}, u32[]{:S(2)}) copy-start(bf16[1,1,128,2048]{3,2,1,0:T(8,128)(2,1)} %param.8) | copy-start | bytes 1572868
  0.7 11.1 %collective-permute-start.2 = (bf16[128,2048]{1,0:T(8,128)(2,1)}, bf16[128,2048]{1,0:T(8,128)(2,1)S(1)}, u32[]{:S(2)}, u32[]{:S(2)}) collective-permute-start(bf16[128,2048]{1,0:T(8,128)(2,1)} %bitcast.25), channel_id=1, source_target_pairs={{1,2},{3,4},{4,3},{6,5},{9,10},{11,12},{12,11},{14,13},{17,18},{19... | collective-permute-start | bytes 1572872 | tf_op jit(solution)/shard_map/ppermute | solution.py:304
  5.3 12.0 %collective-permute-start.3 = (bf16[128,2048]{1,0:T(8,128)(2,1)}, bf16[128,2048]{1,0:T(8,128)(2,1)S(1)}, u32[]{:S(2)}, u32[]{:S(2)}) collective-permute-start(bf16[128,2048]{1,0:T(8,128)(2,1)} %bitcast.29), channel_id=1, source_target_pairs={{1,2},{3,4},{4,3},{6,5},{9,10},{11,12},{12,11},{14,13},{17,18},{19... | collective-permute-start | bytes 1572872 | tf_op jit(solution)/shard_map/ppermute | solution.py:305
  6.7 13.5 %copy-start = (bf16[1,1,128,2048]{3,2,1,0:T(8,128)(2,1)S(1)}, bf16[1,1,128,2048]{3,2,1,0:T(8,128)(2,1)}, u32[]{:S(2)}) copy-start(bf16[1,1,128,2048]{3,2,1,0:T(8,128)(2,1)} %param.6) | copy-start | bytes 1572868
  6.7 13.5 %copy-start.4 = (s32[1,8]{1,0:T(1,128)S(1)}, s32[1,8]{1,0:T(1,128)}, u32[]{:S(2)}) copy-start(s32[1,8]{1,0:T(1,128)} %near_ref.5) | copy-start | bytes 100
  8.1 12.1 %collective-permute-start = (bf16[128,2048]{1,0:T(8,128)(2,1)S(1)}, bf16[128,2048]{1,0:T(8,128)(2,1)S(1)}, u32[]{:S(2)}, u32[]{:S(2)}) collective-permute-start(bf16[128,2048]{1,0:T(8,128)(2,1)S(1)} %bitcast.26), channel_id=1, source_target_pairs={{0,1},{1,0},{2,3},{3,2},{4,5},{5,4},{6,7},{7,6},{8,9},{9,8},{10,11... | collective-permute-start | bytes 1572872 | tf_op jit(solution)/shard_map/ppermute | solution.py:103
  8.2 12.0 %collective-permute-start.1 = (bf16[128,2048]{1,0:T(8,128)(2,1)S(1)}, bf16[128,2048]{1,0:T(8,128)(2,1)S(1)}, u32[]{:S(2)}, u32[]{:S(2)}) collective-permute-start(bf16[128,2048]{1,0:T(8,128)(2,1)S(1)} %bitcast.30), channel_id=1, source_target_pairs={{0,1},{1,0},{2,3},{3,2},{4,5},{5,4},{6,7},{7,6},{8,9},{9,8},{10,11... | collective-permute-start | bytes 1572872 | tf_op jit(solution)/shard_map/ppermute | solution.py:103
  8.7 18.7 %collective-permute-start.4 = (bf16[128,1536]{1,0:T(8,128)(2,1)S(1)}, bf16[128,1536]{1,0:T(8,128)(2,1)S(1)}, u32[]{:S(2)}, u32[]{:S(2)}) collective-permute-start(bf16[128,1536]{1,0:T(8,128)(2,1)S(1)} %get-tuple-element.79), channel_id=1, source_target_pairs={{0,4},{1,5},{2,6},{3,7},{4,0},{5,1},{6,2},{7,3},{8,12},{9,13},{10,... | collective-permute-start | bytes 1179656 | tf_op jit(solution)/shard_map/ppermute | solution.py:103
  17.3 12.5 %collective-permute-start.5 = (bf16[128,1536]{1,0:T(8,128)(2,1)S(1)}, bf16[128,1536]{1,0:T(8,128)(2,1)S(1)}, u32[]{:S(2)}, u32[]{:S(2)}) collective-permute-start(bf16[128,1536]{1,0:T(8,128)(2,1)S(1)} %pad_maximum_fusion.1), channel_id=1, source_target_pairs={{0,2},{1,3},{2,0},{3,1},{4,6},{5,7},{6,4},{7,5},{8,10},{9,11},{10,... | collective-permute-start | bytes 1179656 | tf_op jit(solution)/shard_map/ppermute | solution.py:103
  20.2 3.2 %copy-start.3 = (bf16[1,1,128,2048]{3,2,1,0:T(8,128)(2,1)S(1)}, bf16[1,1,128,2048]{3,2,1,0:T(8,128)(2,1)}, u32[]{:S(2)}) copy-start(bf16[1,1,128,2048]{3,2,1,0:T(8,128)(2,1)} %param.9) | copy-start | bytes 1572868
  22.5 9.6 %collective-permute-start.11 = (bf16[2,512,128]{2,1,0:T(8,128)(2,1)S(1)}, bf16[2,512,128]{2,1,0:T(8,128)(2,1)S(1)}, u32[]{:S(2)}, u32[]{:S(2)}) collective-permute-start(bf16[2,512,128]{2,1,0:T(8,128)(2,1)S(1)} %get-tuple-element.76), channel_id=1, source_target_pairs={{0,4},{1,5},{2,6},{3,7},{4,0},{5,1},{6,2},{7,3},{8,12},{9,13},{10,... | collective-permute-start | bytes 786440 | tf_op jit(solution)/shard_map/ppermute | solution.py:103
  22.6 16.7 %collective-permute-start.10 = (bf16[2,512,128]{2,1,0:T(8,128)(2,1)S(1)}, bf16[2,512,128]{2,1,0:T(8,128)(2,1)S(1)}, u32[]{:S(2)}, u32[]{:S(2)}) collective-permute-start(bf16[2,512,128]{2,1,0:T(8,128)(2,1)S(1)} %get-tuple-element.58.refs_0_), channel_id=1, source_target_pairs={{0,2},{1,3},{2,0},{3,1},{4,6},{5,7},{6,4},{7,5},{8,10},{9,11},{10,... | collective-permute-start | bytes 786440 | tf_op jit(solution)/shard_map/ppermute | solution.py:103
  29.9 5.2 %collective-permute-start.6 = (bf16[1,128,768]{2,1,0:T(8,128)(2,1)S(1)}, bf16[1,128,768]{2,1,0:T(8,128)(2,1)S(1)}, u32[]{:S(2)}, u32[]{:S(2)}) collective-permute-start(bf16[1,128,768]{2,1,0:T(8,128)(2,1)S(1)} %get-tuple-element.81), channel_id=1, source_target_pairs={{0,4},{1,5},{2,6},{3,7},{4,0},{5,1},{6,2},{7,3},{8,12},{9,13},{10,... | collective-permute-start | bytes 589832 | tf_op jit(solution)/shard_map/ppermute | solution.py:103
  29.9 9.3 %collective-permute-start.14 = (bf16[1,128,768]{2,1,0:T(8,128)(2,1)S(1)}, bf16[1,128,768]{2,1,0:T(8,128)(2,1)S(1)}, u32[]{:S(2)}, u32[]{:S(2)}) collective-permute-start(bf16[1,128,768]{2,1,0:T(8,128)(2,1)S(1)} %get-tuple-element.80), channel_id=1, source_target_pairs={{0,4},{1,5},{2,6},{3,7},{4,0},{5,1},{6,2},{7,3},{8,12},{9,13},{10,... | collective-permute-start | bytes 589832 | tf_op jit(solution)/shard_map/ppermute | solution.py:103
  32.1 7.2 %collective-permute-start.12 = (bf16[1,512,128]{2,1,0:T(8,128)(2,1)S(1)}, bf16[1,512,128]{2,1,0:T(8,128)(2,1)S(1)}, u32[]{:S(2)}, u32[]{:S(2)}) collective-permute-start(bf16[1,512,128]{2,1,0:T(8,128)(2,1)S(1)} %get-tuple-element.83), channel_id=1, source_target_pairs={{0,2},{1,3},{2,0},{3,1},{4,6},{5,7},{6,4},{7,5},{8,10},{9,11},{10,... | collective-permute-start | bytes 393224 | tf_op jit(solution)/shard_map/ppermute | solution.py:103
  34.4 5.9 %collective-permute-start.13 = (bf16[1,512,128]{2,1,0:T(8,128)(2,1)S(1)}, bf16[1,512,128]{2,1,0:T(8,128)(2,1)S(1)}, u32[]{:S(2)}, u32[]{:S(2)}) collective-permute-start(bf16[1,512,128]{2,1,0:T(8,128)(2,1)S(1)} %get-tuple-element.82), channel_id=1, source_target_pairs={{0,2},{1,3},{2,0},{3,1},{4,6},{5,7},{6,4},{7,5},{8,10},{9,11},{10,... | collective-permute-start | bytes 393224 | tf_op jit(solution)/shard_map/ppermute | solution.py:103
  35.0 21.4 %collective-permute-start.7 = (bf16[2,128,2048]{2,1,0:T(8,128)(2,1)S(1)}, bf16[2,128,2048]{2,1,0:T(8,128)(2,1)S(1)}, u32[]{:S(2)}, u32[]{:S(2)}) collective-permute-start(bf16[2,128,2048]{2,1,0:T(8,128)(2,1)S(1)} %get-tuple-element.47), channel_id=1, source_target_pairs={{0,1},{1,0},{2,3},{3,2},{4,5},{5,4},{6,7},{7,6},{8,9},{9,8},{10,11... | collective-permute-start | bytes 3145736 | tf_op jit(solution)/shard_map/ppermute | solution.py:103
  40.7 2.8 %collective-permute-start.16 = (bf16[1,128,1536]{2,1,0:T(8,128)(2,1)S(1)}, bf16[1,128,1536]{2,1,0:T(8,128)(2,1)S(1)}, u32[]{:S(2)}, u32[]{:S(2)}) collective-permute-start(bf16[1,128,1536]{2,1,0:T(8,128)(2,1)S(1)} %product_mate.1), channel_id=1, source_target_pairs={{0,1},{1,0},{2,3},{3,2},{4,5},{5,4},{6,7},{7,6},{8,9},{9,8},{10,11... | collective-permute-start | bytes 1179656 | tf_op jit(solution)/shard_map/ppermute | solution.py:103
  42.7 4.2 %collective-permute-start.20 = (bf16[1,128,1536]{2,1,0:T(8,128)(2,1)S(1)}, bf16[1,128,1536]{2,1,0:T(8,128)(2,1)S(1)}, u32[]{:S(2)}, u32[]{:S(2)}) collective-permute-start(bf16[1,128,1536]{2,1,0:T(8,128)(2,1)S(1)} %get-tuple-element.63), channel_id=1, source_target_pairs={{0,1},{1,0},{2,3},{3,2},{4,5},{5,4},{6,7},{7,6},{8,9},{9,8},{10,11... | collective-permute-start | bytes 1179656 | tf_op jit(solution)/shard_map/ppermute | solution.py:103
  43.6 10.4 %collective-permute-start.18 = (bf16[128,1536]{1,0:T(8,128)(2,1)S(1)}, bf16[128,1536]{1,0:T(8,128)(2,1)S(1)}, u32[]{:S(2)}, u32[]{:S(2)}) collective-permute-start(bf16[128,1536]{1,0:T(8,128)(2,1)S(1)} %block_sum.3), channel_id=1, source_target_pairs={{0,8},{8,0},{16,24},{24,16},{1,9},{9,1},{17,25},{25,17},{2,10},{10... | collective-permute-start | bytes 1179656 | tf_op jit(solution)/shard_map/ppermute | solution.py:103
  45.5 2.7 %collective-permute-start.17 = (bf16[1,128,1536]{2,1,0:T(8,128)(2,1)S(1)}, bf16[1,128,1536]{2,1,0:T(8,128)(2,1)S(1)}, u32[]{:S(2)}, u32[]{:S(2)}) collective-permute-start(bf16[1,128,1536]{2,1,0:T(8,128)(2,1)S(1)} %get-tuple-element.61), channel_id=1, source_target_pairs={{0,1},{1,0},{2,3},{3,2},{4,5},{5,4},{6,7},{7,6},{8,9},{9,8},{10,11... | collective-permute-start | bytes 1179656 | tf_op jit(solution)/shard_map/ppermute | solution.py:103
  46.8 9.6 %collective-permute-start.15 = (bf16[1,128,1536]{2,1,0:T(8,128)(2,1)S(1)}, bf16[1,128,1536]{2,1,0:T(8,128)(2,1)S(1)}, u32[]{:S(2)}, u32[]{:S(2)}) collective-permute-start(bf16[1,128,1536]{2,1,0:T(8,128)(2,1)S(1)} %get-tuple-element.56), channel_id=1, source_target_pairs={{0,1},{1,0},{2,3},{3,2},{4,5},{5,4},{6,7},{7,6},{8,9},{9,8},{10,11... | collective-permute-start | bytes 1179656 | tf_op jit(solution)/shard_map/ppermute | solution.py:103
  46.9 29.1 %collective-permute-start.8 = (bf16[128,2048]{1,0:T(8,128)(2,1)S(1)}, bf16[128,2048]{1,0:T(8,128)(2,1)S(1)}, u32[]{:S(2)}, u32[]{:S(2)}) collective-permute-start(bf16[128,2048]{1,0:T(8,128)(2,1)S(1)} %get-tuple-element.49), channel_id=1, source_target_pairs={{3,4},{5,6},{2,1},{4,3},{11,12},{13,14},{10,9},{12,11},{19,20},{21... | collective-permute-start | bytes 1572872 | tf_op jit(solution)/shard_map/ppermute | solution.py:452
  48.2 27.8 %collective-permute-start.9 = (bf16[128,2048]{1,0:T(8,128)(2,1)S(1)}, bf16[128,2048]{1,0:T(8,128)(2,1)S(1)}, u32[]{:S(2)}, u32[]{:S(2)}) collective-permute-start(bf16[128,2048]{1,0:T(8,128)(2,1)S(1)} %get-tuple-element.51), channel_id=1, source_target_pairs={{3,4},{5,6},{2,1},{4,3},{11,12},{13,14},{10,9},{12,11},{19,20},{21... | collective-permute-start | bytes 1572872 | tf_op jit(solution)/shard_map/ppermute | solution.py:453
  54.1 19.4 %collective-permute-start.19 = (bf16[128,1536]{1,0:T(8,128)(2,1)S(1)}, bf16[128,1536]{1,0:T(8,128)(2,1)S(1)}, u32[]{:S(2)}, u32[]{:S(2)}) collective-permute-start(bf16[128,1536]{1,0:T(8,128)(2,1)S(1)} %block_sum.4), channel_id=1, source_target_pairs={{0,16},{8,24},{16,0},{24,8},{1,17},{9,25},{17,1},{25,9},{2,18},{10... | collective-permute-start | bytes 1179656 | tf_op jit(solution)/shard_map/ppermute | solution.py:103
  56.5 17.0 %collective-permute-start.21 = (bf16[128,1536]{1,0:T(8,128)(2,1)S(1)}, bf16[128,1536]{1,0:T(8,128)(2,1)S(1)}, u32[]{:S(2)}, u32[]{:S(2)}) collective-permute-start(bf16[128,1536]{1,0:T(8,128)(2,1)S(1)} %block_sum.5), channel_id=1, source_target_pairs={{0,8},{8,0},{16,24},{24,16},{1,9},{9,1},{17,25},{25,17},{2,10},{10... | collective-permute-start | bytes 1179656 | tf_op jit(solution)/shard_map/ppermute | solution.py:103
  74.3 3.6 %collective-permute-start.22 = (f32[128,128]{1,0:T(8,128)S(1)}, f32[128,128]{1,0:T(8,128)S(1)}, u32[]{:S(2)}, u32[]{:S(2)}) collective-permute-start(f32[128,128]{1,0:T(8,128)S(1)} %get-tuple-element.67.gram), channel_id=1, source_target_pairs={{0,2},{1,3},{2,0},{3,1},{4,6},{5,7},{6,4},{7,5},{8,10},{9,11},{10,... | collective-permute-start | bytes 196616 | tf_op jit(solution)/shard_map/ppermute | solution.py:103
  80.8 7.4 %collective-permute-start.23 = (bf16[128,384]{1,0:T(8,128)(2,1)S(1)}, bf16[128,384]{1,0:T(8,128)(2,1)S(1)}, u32[]{:S(2)}, u32[]{:S(2)}) collective-permute-start(bf16[128,384]{1,0:T(8,128)(2,1)S(1)} %get-tuple-element.68), channel_id=1, source_target_pairs={{0,5},{1,4},{2,7},{3,6},{4,1},{5,0},{6,3},{7,2},{8,13},{9,12},{10,... | collective-permute-start | bytes 294920 | tf_op jit(solution)/shard_map/ppermute | solution.py:103
  85.0 4.8 %collective-permute-start.24 = (bf16[128,384]{1,0:T(8,128)(2,1)S(1)}, bf16[128,384]{1,0:T(8,128)(2,1)S(1)}, u32[]{:S(2)}, u32[]{:S(2)}) collective-permute-start(bf16[128,384]{1,0:T(8,128)(2,1)S(1)} %get-tuple-element.69), channel_id=1, source_target_pairs={{0,4},{1,5},{2,6},{3,7},{4,0},{5,1},{6,2},{7,3},{8,12},{9,13},{10,... | collective-permute-start | bytes 294920 | tf_op jit(solution)/shard_map/ppermute | solution.py:103
  85.0 4.8 %collective-permute-start.25 = (bf16[128,384]{1,0:T(8,128)(2,1)S(1)}, bf16[128,384]{1,0:T(8,128)(2,1)S(1)}, u32[]{:S(2)}, u32[]{:S(2)}) collective-permute-start(bf16[128,384]{1,0:T(8,128)(2,1)S(1)} %get-tuple-element.70), channel_id=1, source_target_pairs={{0,1},{1,0},{2,3},{3,2},{4,5},{5,4},{6,7},{7,6},{8,9},{9,8},{10,11... | collective-permute-start | bytes 294920 | tf_op jit(solution)/shard_map/ppermute | solution.py:103

commit v17 on v16

--- a/solution.py
+++ b/solution.py
@@ -235,7 +235,12 @@
     for (lead, first), part in zip(spots, parts, strict=True):
         size = part.shape[-1]
         x[:, first : first + size] += piece(part, lead, 0, size)
-    gram[...] = exact(x[...], x[...], ((1,), (1,)))
+    high, middle, low = parts_of(x[...])
+    pair = jnp.concatenate([high, middle], 0)
+    size = gram.shape[0]
+    wide = dot_t(pair, pair)
+    cross = wide[:size, size:] + dot_t(high, low)
+    gram[...] = wide[:size, :size] + (wide[size:, size:] + (cross + cross.T))
 
 
 def polynomial(gram):

time: 91.7 us -> 91.5 us (level)
  no operation moved by 1% of the time
where the time goes in v17:
time: 91.5 us; the launch traced here: 90.6 us
  starting transfers between devices  37.5 us (41%)
  waiting for transfers between devices  35.1 us (38%)
  Pallas kernels  15.4 us (17%)
  local copies, waits for them, and re-layouts  1.43 us (2%)
  between operations  0.93 us (1%)
    ppermute x22, waiting for transfers between devices, shift(): lax.ppermute(value, axis, [(i, i ^ mask) for i in range(lax.axis_size(axi...  29.4 us
    ppermute x22, starting transfers between devices, shift(): lax.ppermute(value, axis, [(i, i ^ mask) for i in range(lax.axis_size(axi...  29 us
    ppermute x1, waiting for transfers between devices, local(): value_next = lax.ppermute(value, 'seq', takes)  5.62 us
    ppermute x1, starting transfers between devices, local(): key_next = lax.ppermute(key, 'seq', takes)  4.67 us
    pallas_call x1, Pallas kernels, local(): pl.pallas_call(backward_kernel, out_shape=[struct((tile, width), bf16), s...  3.97 us
    pallas_call x1, Pallas kernels, local(): pl.pallas_call(functools.partial(update_kernel, plan, factor), out_shape=...  2.89 us
    pallas_call x5, Pallas kernels, product(): pl.pallas_call(functools.partial(product_kernel, counts, layers, cores),...  2.52 us
    pallas_call x1, Pallas kernels, local(): pl.pallas_call(functools.partial(forward_kernel, plan), out_shape=struct(...  2.3 us
  transfers between devices with their start and end apart: 26, of which 12 were waited for; matrix products, arithmetic and copies ran while one was open for 2% of the time, Pallas kernels for 13%

profile of v17, /device:TPU:1, one launch (start us, length us, event | category | flops | bytes accessed | tf_op | source)
XLA Modules:
  0.0 90.6 jit_solution(128768515767424690)
XLA Ops:
  0.7 4.7 %collective-permute-start.2 = (bf16[128,2048]{1,0:T(8,128)(2,1)}, bf16[128,2048]{1,0:T(8,128)(2,1)S(1)}, u32[]{:S(2)}, u32[]{:S(2)}) collective-permute-start(bf16[128,2048]{1,0:T(8,128)(2,1)} %bitcast.25), channel_id=1, source_target_pairs={{1,2},{3,4},{4,3},{6,5},{9,10},{11,12},{12,11},{14,13},{17,18},{19... | collective-permute-start | bytes 1572872 | tf_op jit(solution)/shard_map/ppermute | solution.py:309
  5.3 1.3 %collective-permute-start.3 = (bf16[128,2048]{1,0:T(8,128)(2,1)}, bf16[128,2048]{1,0:T(8,128)(2,1)S(1)}, u32[]{:S(2)}, u32[]{:S(2)}) collective-permute-start(bf16[128,2048]{1,0:T(8,128)(2,1)} %bitcast.29), channel_id=1, source_target_pairs={{1,2},{3,4},{4,3},{6,5},{9,10},{11,12},{12,11},{14,13},{17,18},{19... | collective-permute-start | bytes 1572872 | tf_op jit(solution)/shard_map/ppermute | solution.py:310
  6.7 1.3 %dynamic-slice_bitcast_fusion.1 = (bf16[128,768]{1,0:T(8,128)(2,1)S(1)}, bf16[128,768]{1,0:T(8,128)(2,1)S(1)}, bf16[128,768]{1,0:T(8,128)(2,1)S(1)}, bf16[128,768]{1,0:T(8,128)(2,1)S(1)}) fusion(bf16[1,1,128,3072]{3,2,1,0:T(8,128)(2,1)} %param.10, s32[]{:T(128)S(6)} %select_n.14, s32[]{:T(128)S(6)} %select_n.13, s32[]{:T(128)S(6)} %select_n.12, s32[]{:T(128)S(6)} %select_n.15), kind=kLoop, calls=%fused_computation.6 | loop fusion | bytes 1572880 | tf_op jit(solution)/shard_map/dynamic_slice | solution.py:319
  8.0 0.1 fusion
  8.1 0.1 collective-permute-start
  8.2 0.5 collective-permute-start.1
  8.7 2.9 %collective-permute-start.4 = (bf16[128,1536]{1,0:T(8,128)(2,1)S(1)}, bf16[128,1536]{1,0:T(8,128)(2,1)S(1)}, u32[]{:S(2)}, u32[]{:S(2)}) collective-permute-start(bf16[128,1536]{1,0:T(8,128)(2,1)S(1)} %get-tuple-element.79), channel_id=1, source_target_pairs={{0,4},{1,5},{2,6},{3,7},{4,0},{5,1},{6,2},{7,3},{8,12},{9,13},{10,... | collective-permute-start | bytes 1179656 | tf_op jit(solution)/shard_map/ppermute | solution.py:103
  11.6 0.1 collective-permute-done.2.kn
  11.7 5.6 %collective-permute-done.3.vn = bf16[128,2048]{1,0:T(8,128)(2,1)S(1)} collective-permute-done((bf16[128,2048]{1,0:T(8,128)(2,1)}, bf16[128,2048]{1,0:T(8,128)(2,1)S(1)}, u32[]{:S(2)}, u32[]{:S(2)}) %collective-permute-start.3) | collective-permute-done | bytes 524320 | tf_op jit(solution)/shard_map/ppermute | solution.py:310
  17.3 2.8 %collective-permute-start.5 = (bf16[128,1536]{1,0:T(8,128)(2,1)S(1)}, bf16[128,1536]{1,0:T(8,128)(2,1)S(1)}, u32[]{:S(2)}, u32[]{:S(2)}) collective-permute-start(bf16[128,1536]{1,0:T(8,128)(2,1)S(1)} %pad_maximum_fusion.1), channel_id=1, source_target_pairs={{0,2},{1,3},{2,0},{3,1},{4,6},{5,7},{6,4},{7,5},{8,10},{9,11},{10,... | collective-permute-start | bytes 1179656 | tf_op jit(solution)/shard_map/ppermute | solution.py:103
  20.2 0.0 collective-permute-done.km
  20.2 0.0 collective-permute-done.1.vm
  20.2 0.0 copy-start.3
  20.2 2.3 %attention_forward.1 = bf16[2,2,512,128]{3,2,1,0:T(8,128)(2,1)S(1)} custom-call(s32[1,8]{1,0:T(1,128)S(1)} %copy-done.4, bf16[128,2048]{1,0:T(8,128)(2,1)S(1)} %bitcast.23, bf16[128,2048]{1,0:T(8,128)(2,1)S(1)} %bitcast.27, bf16[128,2048]{1,0:T(8,128)(2,1)S(1)} %bitcast.31, bf16[128,2048]{1,0:T(8,128)(2,1)S(1)} %collective-permute-done.km, ...), custom_call_target="tpu_custom_call" | custom-call | flops 268435456 | bytes 4194304 | tf_op jit(solution)/shard_map/attention_forward/pallas_call | solution.py:338
  22.5 0.1 collective-permute-start.11
  22.6 0.8 collective-permute-start.10
  23.4 4.0 %attention_backward.1 = (bf16[128,2048]{1,0:T(8,128)(2,1)}, f32[128,2048]{1,0:T(8,128)S(1)}, f32[128,2048]{1,0:T(8,128)S(1)}, bf16[128,2048]{1,0:T(8,128)(2,1)S(...) custom-call(s32[1,8]{1,0:T(1,128)S(1)} %copy-done.4, bf16[128,2048]{1,0:T(8,128)(2,1)S(1)} %bitcast.24, ...), custom_call_target="tpu_custom_call" | custom-call | flops 1 | bytes 1 | tf_op jit(solution)/shard_map/attention_backward/pallas_call | solution.py:364
  27.4 0.0 collective-permute-done.4
  27.4 2.5 %collective-permute-done.5 = bf16[128,1536]{1,0:T(8,128)(2,1)S(1)} collective-permute-done((bf16[128,1536]{1,0:T(8,128)(2,1)S(1)}, bf16[128,1536]{1,0:T(8,128)(2,1)S(1)}, u32[]{:S(2)}, u32[]{:S(2)}) %collective-permute-start.5) | collective-permute-done | bytes 393248 | tf_op jit(solution)/shard_map/ppermute | solution.py:103
  29.9 0.1 collective-permute-start.6
  29.9 1.5 %collective-permute-start.14 = (bf16[1,128,768]{2,1,0:T(8,128)(2,1)S(1)}, bf16[1,128,768]{2,1,0:T(8,128)(2,1)S(1)}, u32[]{:S(2)}, u32[]{:S(2)}) collective-permute-start(bf16[1,128,768]{2,1,0:T(8,128)(2,1)S(1)} %get-tuple-element.80), channel_id=1, source_target_pairs={{0,4},{1,5},{2,6},{3,7},{4,0},{5,1},{6,2},{7,3},{8,12},{9,13},{10,... | collective-permute-start | bytes 589832 | tf_op jit(solution)/shard_map/ppermute | solution.py:103
  31.4 0.7 collective-permute-done.11.refs_2_
  32.1 2.3 %collective-permute-start.12 = (bf16[1,512,128]{2,1,0:T(8,128)(2,1)S(1)}, bf16[1,512,128]{2,1,0:T(8,128)(2,1)S(1)}, u32[]{:S(2)}, u32[]{:S(2)}) collective-permute-start(bf16[1,512,128]{2,1,0:T(8,128)(2,1)S(1)} %get-tuple-element.83), channel_id=1, source_target_pairs={{0,2},{1,3},{2,0},{3,1},{4,6},{5,7},{6,4},{7,5},{8,10},{9,11},{10,... | collective-permute-start | bytes 393224 | tf_op jit(solution)/shard_map/ppermute | solution.py:103
  34.4 0.1 collective-permute-start.13
  34.5 0.5 collective-permute-done.6
  35.0 4.1 %collective-permute-start.7 = (bf16[2,128,2048]{2,1,0:T(8,128)(2,1)S(1)}, bf16[2,128,2048]{2,1,0:T(8,128)(2,1)S(1)}, u32[]{:S(2)}, u32[]{:S(2)}) collective-permute-start(bf16[2,128,2048]{2,1,0:T(8,128)(2,1)S(1)} %get-tuple-element.47), channel_id=1, source_target_pairs={{0,1},{1,0},{2,3},{3,2},{4,5},{5,4},{6,7},{7,6},{8,9},{9,8},{10,11... | collective-permute-start | bytes 3145736 | tf_op jit(solution)/shard_map/ppermute | solution.py:103
  39.1 0.1 collective-permute-done.14
  39.2 0.1 maximum_maximum_fusion.refs_5_
  39.4 0.0 collective-permute-done.10.refs_1_
  39.4 0.0 collective-permute-done.12.refs_3_
  39.4 1.0 %collective-permute-done.13.refs_4_ = bf16[1,512,128]{2,1,0:T(8,128)(2,1)S(1)} collective-permute-done((bf16[1,512,128]{2,1,0:T(8,128)(2,1)S(1)}, bf16[1,512,128]{2,1,0:T(8,128)(2,1)S(1)}, u32[]{:S(2)}, u32[]{:S(2)}) %collective-permute-start.13) | collective-permute-done | bytes 131104 | tf_op jit(solution)/shard_map/ppermute | solution.py:103
  40.4 0.4 product_mate.1
  40.7 1.4 %collective-permute-start.16 = (bf16[1,128,1536]{2,1,0:T(8,128)(2,1)S(1)}, bf16[1,128,1536]{2,1,0:T(8,128)(2,1)S(1)}, u32[]{:S(2)}, u32[]{:S(2)}) collective-permute-start(bf16[1,128,1536]{2,1,0:T(8,128)(2,1)S(1)} %product_mate.1), channel_id=1, source_target_pairs={{0,1},{1,0},{2,3},{3,2},{4,5},{5,4},{6,7},{7,6},{8,9},{9,8},{10,11... | collective-permute-start | bytes 1179656 | tf_op jit(solution)/shard_map/ppermute | solution.py:103
  42.1 0.6 product_near.1
  42.7 0.1 collective-permute-start.20
  42.8 0.4 product_first.1.refs_0_
  43.2 0.3 collective-permute-done.16.refs_1_
  43.5 0.1 block_sum.3
  43.6 1.4 %collective-permute-start.18 = (bf16[128,1536]{1,0:T(8,128)(2,1)S(1)}, bf16[128,1536]{1,0:T(8,128)(2,1)S(1)}, u32[]{:S(2)}, u32[]{:S(2)}) collective-permute-start(bf16[128,1536]{1,0:T(8,128)(2,1)S(1)} %block_sum.3), channel_id=1, source_target_pairs={{0,8},{8,0},{16,24},{24,16},{1,9},{9,1},{17,25},{25,17},{2,10},{10... | collective-permute-start | bytes 1179656 | tf_op jit(solution)/shard_map/ppermute | solution.py:103
  44.9 0.6 product_middle.1
  45.5 0.7 collective-permute-start.17
  46.2 0.6 product_own.1
  46.8 0.1 collective-permute-start.15
  46.9 0.0 collective-permute-done.20.refs_1_
  46.9 1.3 %collective-permute-start.8 = (bf16[128,2048]{1,0:T(8,128)(2,1)S(1)}, bf16[128,2048]{1,0:T(8,128)(2,1)S(1)}, u32[]{:S(2)}, u32[]{:S(2)}) collective-permute-start(bf16[128,2048]{1,0:T(8,128)(2,1)S(1)} %get-tuple-element.49), channel_id=1, source_target_pairs={{3,4},{5,6},{2,1},{4,3},{11,12},{13,14},{10,9},{12,11},{19,20},{21... | collective-permute-start | bytes 1572872 | tf_op jit(solution)/shard_map/ppermute | solution.py:457
  48.2 1.3 %collective-permute-start.9 = (bf16[128,2048]{1,0:T(8,128)(2,1)S(1)}, bf16[128,2048]{1,0:T(8,128)(2,1)S(1)}, u32[]{:S(2)}, u32[]{:S(2)}) collective-permute-start(bf16[128,2048]{1,0:T(8,128)(2,1)S(1)} %get-tuple-element.51), channel_id=1, source_target_pairs={{3,4},{5,6},{2,1},{4,3},{11,12},{13,14},{10,9},{12,11},{19,20},{21... | collective-permute-start | bytes 1572872 | tf_op jit(solution)/shard_map/ppermute | solution.py:458
  49.5 0.1 block_sum.5
  49.7 4.3 %collective-permute-done.18.refs_2_ = bf16[128,1536]{1,0:T(8,128)(2,1)S(1)} collective-permute-done((bf16[128,1536]{1,0:T(8,128)(2,1)S(1)}, bf16[128,1536]{1,0:T(8,128)(2,1)S(1)}, u32[]{:S(2)}, u32[]{:S(2)}) %collective-permute-start.18) | collective-permute-done | bytes 393248 | tf_op jit(solution)/shard_map/ppermute | solution.py:103
  53.9 0.1 block_sum.4
  54.1 2.4 %collective-permute-start.19 = (bf16[128,1536]{1,0:T(8,128)(2,1)S(1)}, bf16[128,1536]{1,0:T(8,128)(2,1)S(1)}, u32[]{:S(2)}, u32[]{:S(2)}) collective-permute-start(bf16[128,1536]{1,0:T(8,128)(2,1)S(1)} %block_sum.4), channel_id=1, source_target_pairs={{0,16},{8,24},{16,0},{24,8},{1,17},{9,25},{17,1},{25,9},{2,18},{10... | collective-permute-start | bytes 1179656 | tf_op jit(solution)/shard_map/ppermute | solution.py:103
  56.4 0.0 collective-permute-done.15.refs_0_
  56.5 0.0 collective-permute-done.7.mate
  56.5 1.3 %collective-permute-start.21 = (bf16[128,1536]{1,0:T(8,128)(2,1)S(1)}, bf16[128,1536]{1,0:T(8,128)(2,1)S(1)}, u32[]{:S(2)}, u32[]{:S(2)}) collective-permute-start(bf16[128,1536]{1,0:T(8,128)(2,1)S(1)} %block_sum.5), channel_id=1, source_target_pairs={{0,8},{8,0},{16,24},{24,16},{1,9},{9,1},{17,25},{25,17},{2,10},{10... | collective-permute-start | bytes 1179656 | tf_op jit(solution)/shard_map/ppermute | solution.py:103
  57.8 15.7 %collective-permute-done.19.refs_1_ = bf16[128,1536]{1,0:T(8,128)(2,1)S(1)} collective-permute-done((bf16[128,1536]{1,0:T(8,128)(2,1)S(1)}, bf16[128,1536]{1,0:T(8,128)(2,1)S(1)}, u32[]{:S(2)}, u32[]{:S(2)}) %collective-permute-start.19) | collective-permute-done | bytes 393248 | tf_op jit(solution)/shard_map/ppermute | solution.py:103
  73.5 0.6 gradient_sum.1
  74.1 1.8 %collective-permute-start.22 = (f32[128,128]{1,0:T(8,128)S(1)}, f32[128,128]{1,0:T(8,128)S(1)}, u32[]{:S(2)}, u32[]{:S(2)}) collective-permute-start(f32[128,128]{1,0:T(8,128)S(1)} %get-tuple-element.67.gram), channel_id=1, source_target_pairs={{0,2},{1,3},{2,0},{3,1},{4,6},{5,7},{6,4},{7,5},{8,10},{9,11},{10,... | collective-permute-start | bytes 196616 | tf_op jit(solution)/shard_map/ppermute | solution.py:103
  75.9 0.0 collective-permute-done.8.kn
  75.9 1.8 %key_value_sum.1 = (bf16[128,2048]{1,0:T(8,128)(2,1)}, bf16[128,2048]{1,0:T(8,128)(2,1)}) custom-call(s32[1,8]{1,0:T(1,128)S(1)} %copy-done.4, f32[128,2048]{1,0:T(8,128)S(1)} %get-tuple-element.42.dko, f32[128,2048]{1,0:T(8,128)S(1)} %get-tuple-element.43.dvo, bf16[2,128,2048]{2,1,0:T(8,128)(2,1)S(1)} %collective-permute-done.7.mate, ...), custom_call_target="tpu_custom_call" | custom-call | flops 1572864 | bytes 5242880 | tf_op jit(solution)/shard_map/key_value_sum/pallas_call | solution.py:467
  77.7 2.9 %newton_schulz.1 = (f32[128,384]{1,0:T(8,128)S(1)}, bf16[128,384]{1,0:T(8,128)(2,1)S(1)}, bf16[128,384]{1,0:T(8,128)(2,1)S(1)}, bf16[128,384]{1,0:T(8,128)(2,1)S(1)}) custom-call(f32[128,1536]{1,0:T(8,128)S(1)} %get-tuple-element.66.x, f32[128,128]{1,0:T(8,128)S(1)} %get-tuple-element.67.gram, f32[128,128]{1,0:T(8,128)S(1)} %collective-permute-done.22.gram_other), custom_call_target="tpu_custom_call" | custom-call | flops 301989888 | bytes 1572864 | tf_op jit(solution)/shard_map/newton_schulz/pallas_call | solution.py:498
  80.6 4.2 %collective-permute-start.23 = (bf16[128,384]{1,0:T(8,128)(2,1)S(1)}, bf16[128,384]{1,0:T(8,128)(2,1)S(1)}, u32[]{:S(2)}, u32[]{:S(2)}) collective-permute-start(bf16[128,384]{1,0:T(8,128)(2,1)S(1)} %get-tuple-element.68), channel_id=1, source_target_pairs={{0,5},{1,4},{2,7},{3,6},{4,1},{5,0},{6,3},{7,2},{8,13},{9,12},{10,... | collective-permute-start | bytes 294920 | tf_op jit(solution)/shard_map/ppermute | solution.py:103
  84.8 0.5 collective-permute-start.25
  85.3 2.7 %collective-permute-done.23.refs_0_ = bf16[128,384]{1,0:T(8,128)(2,1)S(1)} collective-permute-done((bf16[128,384]{1,0:T(8,128)(2,1)S(1)}, bf16[128,384]{1,0:T(8,128)(2,1)S(1)}, u32[]{:S(2)}, u32[]{:S(2)}) %collective-permute-start.23) | collective-permute-done | bytes 98336 | tf_op jit(solution)/shard_map/ppermute | solution.py:103
  88.0 1.7 %collective-permute-done.24.refs_1_ = bf16[128,384]{1,0:T(8,128)(2,1)S(1)} collective-permute-done((bf16[128,384]{1,0:T(8,128)(2,1)S(1)}, bf16[128,384]{1,0:T(8,128)(2,1)S(1)}, u32[]{:S(2)}, u32[]{:S(2)}) %collective-permute-start.24) | collective-permute-done | bytes 98336 | tf_op jit(solution)/shard_map/ppermute | solution.py:103
  89.7 0.9 %update_rows.1 = f32[512,384]{1,0:T(8,128)} custom-call(bf16[128,384]{1,0:T(8,128)(2,1)S(1)} %collective-permute-done.23.refs_0_, bf16[128,384]{1,0:T(8,128)(2,1)S(1)} %collective-permute-done.24.refs_1_, bf16[128,384]{1,0:T(8,128)(2,1)S(1)} %collective-permute-done.25.refs_2_, f32[128,384]{1,0:T(8,128)S(1)} %get-tuple-element.71.refs_3_), custom_call_target="tpu_custom_call" | custom-call | flops 1 | bytes 1572864 | tf_op jit(solution)/shard_map/update_rows/pallas_call | solution.py:510
  (19 shorter events, 0.1 us)
Async XLA Ops:
  0.6 7.5 %copy-start.1 = (bf16[1,1,128,2048]{3,2,1,0:T(8,128)(2,1)S(1)}, bf16[1,1,128,2048]{3,2,1,0:T(8,128)(2,1)}, u32[]{:S(2)}) copy-start(bf16[1,1,128,2048]{3,2,1,0:T(8,128)(2,1)} %param.7) | copy-start | bytes 1572868
  0.6 7.5 %copy-start.2 = (bf16[1,1,128,2048]{3,2,1,0:T(8,128)(2,1)S(1)}, bf16[1,1,128,2048]{3,2,1,0:T(8,128)(2,1)}, u32[]{:S(2)}) copy-start(bf16[1,1,128,2048]{3,2,1,0:T(8,128)(2,1)} %param.8) | copy-start | bytes 1572868
  0.7 11.1 %collective-permute-start.2 = (bf16[128,2048]{1,0:T(8,128)(2,1)}, bf16[128,2048]{1,0:T(8,128)(2,1)S(1)}, u32[]{:S(2)}, u32[]{:S(2)}) collective-permute-start(bf16[128,2048]{1,0:T(8,128)(2,1)} %bitcast.25), channel_id=1, source_target_pairs={{1,2},{3,4},{4,3},{6,5},{9,10},{11,12},{12,11},{14,13},{17,18},{19... | collective-permute-start | bytes 1572872 | tf_op jit(solution)/shard_map/ppermute | solution.py:309
  5.3 12.0 %collective-permute-start.3 = (bf16[128,2048]{1,0:T(8,128)(2,1)}, bf16[128,2048]{1,0:T(8,128)(2,1)S(1)}, u32[]{:S(2)}, u32[]{:S(2)}) collective-permute-start(bf16[128,2048]{1,0:T(8,128)(2,1)} %bitcast.29), channel_id=1, source_target_pairs={{1,2},{3,4},{4,3},{6,5},{9,10},{11,12},{12,11},{14,13},{17,18},{19... | collective-permute-start | bytes 1572872 | tf_op jit(solution)/shard_map/ppermute | solution.py:310
  6.7 13.5 %copy-start = (bf16[1,1,128,2048]{3,2,1,0:T(8,128)(2,1)S(1)}, bf16[1,1,128,2048]{3,2,1,0:T(8,128)(2,1)}, u32[]{:S(2)}) copy-start(bf16[1,1,128,2048]{3,2,1,0:T(8,128)(2,1)} %param.6) | copy-start | bytes 1572868
  6.7 13.5 %copy-start.4 = (s32[1,8]{1,0:T(1,128)S(1)}, s32[1,8]{1,0:T(1,128)}, u32[]{:S(2)}) copy-start(s32[1,8]{1,0:T(1,128)} %near_ref.5) | copy-start | bytes 100
  8.1 12.1 %collective-permute-start = (bf16[128,2048]{1,0:T(8,128)(2,1)S(1)}, bf16[128,2048]{1,0:T(8,128)(2,1)S(1)}, u32[]{:S(2)}, u32[]{:S(2)}) collective-permute-start(bf16[128,2048]{1,0:T(8,128)(2,1)S(1)} %bitcast.26), channel_id=1, source_target_pairs={{0,1},{1,0},{2,3},{3,2},{4,5},{5,4},{6,7},{7,6},{8,9},{9,8},{10,11... | collective-permute-start | bytes 1572872 | tf_op jit(solution)/shard_map/ppermute | solution.py:103
  8.2 12.0 %collective-permute-start.1 = (bf16[128,2048]{1,0:T(8,128)(2,1)S(1)}, bf16[128,2048]{1,0:T(8,128)(2,1)S(1)}, u32[]{:S(2)}, u32[]{:S(2)}) collective-permute-start(bf16[128,2048]{1,0:T(8,128)(2,1)S(1)} %bitcast.30), channel_id=1, source_target_pairs={{0,1},{1,0},{2,3},{3,2},{4,5},{5,4},{6,7},{7,6},{8,9},{9,8},{10,11... | collective-permute-start | bytes 1572872 | tf_op jit(solution)/shard_map/ppermute | solution.py:103
  8.7 18.7 %collective-permute-start.4 = (bf16[128,1536]{1,0:T(8,128)(2,1)S(1)}, bf16[128,1536]{1,0:T(8,128)(2,1)S(1)}, u32[]{:S(2)}, u32[]{:S(2)}) collective-permute-start(bf16[128,1536]{1,0:T(8,128)(2,1)S(1)} %get-tuple-element.79), channel_id=1, source_target_pairs={{0,4},{1,5},{2,6},{3,7},{4,0},{5,1},{6,2},{7,3},{8,12},{9,13},{10,... | collective-permute-start | bytes 1179656 | tf_op jit(solution)/shard_map/ppermute | solution.py:103
  17.3 12.5 %collective-permute-start.5 = (bf16[128,1536]{1,0:T(8,128)(2,1)S(1)}, bf16[128,1536]{1,0:T(8,128)(2,1)S(1)}, u32[]{:S(2)}, u32[]{:S(2)}) collective-permute-start(bf16[128,1536]{1,0:T(8,128)(2,1)S(1)} %pad_maximum_fusion.1), channel_id=1, source_target_pairs={{0,2},{1,3},{2,0},{3,1},{4,6},{5,7},{6,4},{7,5},{8,10},{9,11},{10,... | collective-permute-start | bytes 1179656 | tf_op jit(solution)/shard_map/ppermute | solution.py:103
  20.2 3.2 %copy-start.3 = (bf16[1,1,128,2048]{3,2,1,0:T(8,128)(2,1)S(1)}, bf16[1,1,128,2048]{3,2,1,0:T(8,128)(2,1)}, u32[]{:S(2)}) copy-start(bf16[1,1,128,2048]{3,2,1,0:T(8,128)(2,1)} %param.9) | copy-start | bytes 1572868
  22.5 9.6 %collective-permute-start.11 = (bf16[2,512,128]{2,1,0:T(8,128)(2,1)S(1)}, bf16[2,512,128]{2,1,0:T(8,128)(2,1)S(1)}, u32[]{:S(2)}, u32[]{:S(2)}) collective-permute-start(bf16[2,512,128]{2,1,0:T(8,128)(2,1)S(1)} %get-tuple-element.76), channel_id=1, source_target_pairs={{0,4},{1,5},{2,6},{3,7},{4,0},{5,1},{6,2},{7,3},{8,12},{9,13},{10,... | collective-permute-start | bytes 786440 | tf_op jit(solution)/shard_map/ppermute | solution.py:103
  22.6 16.7 %collective-permute-start.10 = (bf16[2,512,128]{2,1,0:T(8,128)(2,1)S(1)}, bf16[2,512,128]{2,1,0:T(8,128)(2,1)S(1)}, u32[]{:S(2)}, u32[]{:S(2)}) collective-permute-start(bf16[2,512,128]{2,1,0:T(8,128)(2,1)S(1)} %get-tuple-element.58.refs_0_), channel_id=1, source_target_pairs={{0,2},{1,3},{2,0},{3,1},{4,6},{5,7},{6,4},{7,5},{8,10},{9,11},{10,... | collective-permute-start | bytes 786440 | tf_op jit(solution)/shard_map/ppermute | solution.py:103
  29.9 5.2 %collective-permute-start.6 = (bf16[1,128,768]{2,1,0:T(8,128)(2,1)S(1)}, bf16[1,128,768]{2,1,0:T(8,128)(2,1)S(1)}, u32[]{:S(2)}, u32[]{:S(2)}) collective-permute-start(bf16[1,128,768]{2,1,0:T(8,128)(2,1)S(1)} %get-tuple-element.81), channel_id=1, source_target_pairs={{0,4},{1,5},{2,6},{3,7},{4,0},{5,1},{6,2},{7,3},{8,12},{9,13},{10,... | collective-permute-start | bytes 589832 | tf_op jit(solution)/shard_map/ppermute | solution.py:103
  29.9 9.3 %collective-permute-start.14 = (bf16[1,128,768]{2,1,0:T(8,128)(2,1)S(1)}, bf16[1,128,768]{2,1,0:T(8,128)(2,1)S(1)}, u32[]{:S(2)}, u32[]{:S(2)}) collective-permute-start(bf16[1,128,768]{2,1,0:T(8,128)(2,1)S(1)} %get-tuple-element.80), channel_id=1, source_target_pairs={{0,4},{1,5},{2,6},{3,7},{4,0},{5,1},{6,2},{7,3},{8,12},{9,13},{10,... | collective-permute-start | bytes 589832 | tf_op jit(solution)/shard_map/ppermute | solution.py:103
  32.1 7.2 %collective-permute-start.12 = (bf16[1,512,128]{2,1,0:T(8,128)(2,1)S(1)}, bf16[1,512,128]{2,1,0:T(8,128)(2,1)S(1)}, u32[]{:S(2)}, u32[]{:S(2)}) collective-permute-start(bf16[1,512,128]{2,1,0:T(8,128)(2,1)S(1)} %get-tuple-element.83), channel_id=1, source_target_pairs={{0,2},{1,3},{2,0},{3,1},{4,6},{5,7},{6,4},{7,5},{8,10},{9,11},{10,... | collective-permute-start | bytes 393224 | tf_op jit(solution)/shard_map/ppermute | solution.py:103
  34.4 5.9 %collective-permute-start.13 = (bf16[1,512,128]{2,1,0:T(8,128)(2,1)S(1)}, bf16[1,512,128]{2,1,0:T(8,128)(2,1)S(1)}, u32[]{:S(2)}, u32[]{:S(2)}) collective-permute-start(bf16[1,512,128]{2,1,0:T(8,128)(2,1)S(1)} %get-tuple-element.82), channel_id=1, source_target_pairs={{0,2},{1,3},{2,0},{3,1},{4,6},{5,7},{6,4},{7,5},{8,10},{9,11},{10,... | collective-permute-start | bytes 393224 | tf_op jit(solution)/shard_map/ppermute | solution.py:103
  35.0 21.4 %collective-permute-start.7 = (bf16[2,128,2048]{2,1,0:T(8,128)(2,1)S(1)}, bf16[2,128,2048]{2,1,0:T(8,128)(2,1)S(1)}, u32[]{:S(2)}, u32[]{:S(2)}) collective-permute-start(bf16[2,128,2048]{2,1,0:T(8,128)(2,1)S(1)} %get-tuple-element.47), channel_id=1, source_target_pairs={{0,1},{1,0},{2,3},{3,2},{4,5},{5,4},{6,7},{7,6},{8,9},{9,8},{10,11... | collective-permute-start | bytes 3145736 | tf_op jit(solution)/shard_map/ppermute | solution.py:103
  40.7 2.8 %collective-permute-start.16 = (bf16[1,128,1536]{2,1,0:T(8,128)(2,1)S(1)}, bf16[1,128,1536]{2,1,0:T(8,128)(2,1)S(1)}, u32[]{:S(2)}, u32[]{:S(2)}) collective-permute-start(bf16[1,128,1536]{2,1,0:T(8,128)(2,1)S(1)} %product_mate.1), channel_id=1, source_target_pairs={{0,1},{1,0},{2,3},{3,2},{4,5},{5,4},{6,7},{7,6},{8,9},{9,8},{10,11... | collective-permute-start | bytes 1179656 | tf_op jit(solution)/shard_map/ppermute | solution.py:103
  42.7 4.2 %collective-permute-start.20 = (bf16[1,128,1536]{2,1,0:T(8,128)(2,1)S(1)}, bf16[1,128,1536]{2,1,0:T(8,128)(2,1)S(1)}, u32[]{:S(2)}, u32[]{:S(2)}) collective-permute-start(bf16[1,128,1536]{2,1,0:T(8,128)(2,1)S(1)} %get-tuple-element.63), channel_id=1, source_target_pairs={{0,1},{1,0},{2,3},{3,2},{4,5},{5,4},{6,7},{7,6},{8,9},{9,8},{10,11... | collective-permute-start | bytes 1179656 | tf_op jit(solution)/shard_map/ppermute | solution.py:103
  43.6 10.4 %collective-permute-start.18 = (bf16[128,1536]{1,0:T(8,128)(2,1)S(1)}, bf16[128,1536]{1,0:T(8,128)(2,1)S(1)}, u32[]{:S(2)}, u32[]{:S(2)}) collective-permute-start(bf16[128,1536]{1,0:T(8,128)(2,1)S(1)} %block_sum.3), channel_id=1, source_target_pairs={{0,8},{8,0},{16,24},{24,16},{1,9},{9,1},{17,25},{25,17},{2,10},{10... | collective-permute-start | bytes 1179656 | tf_op jit(solution)/shard_map/ppermute | solution.py:103
  45.5 2.7 %collective-permute-start.17 = (bf16[1,128,1536]{2,1,0:T(8,128)(2,1)S(1)}, bf16[1,128,1536]{2,1,0:T(8,128)(2,1)S(1)}, u32[]{:S(2)}, u32[]{:S(2)}) collective-permute-start(bf16[1,128,1536]{2,1,0:T(8,128)(2,1)S(1)} %get-tuple-element.61), channel_id=1, source_target_pairs={{0,1},{1,0},{2,3},{3,2},{4,5},{5,4},{6,7},{7,6},{8,9},{9,8},{10,11... | collective-permute-start | bytes 1179656 | tf_op jit(solution)/shard_map/ppermute | solution.py:103
  46.8 9.6 %collective-permute-start.15 = (bf16[1,128,1536]{2,1,0:T(8,128)(2,1)S(1)}, bf16[1,128,1536]{2,1,0:T(8,128)(2,1)S(1)}, u32[]{:S(2)}, u32[]{:S(2)}) collective-permute-start(bf16[1,128,1536]{2,1,0:T(8,128)(2,1)S(1)} %get-tuple-element.56), channel_id=1, source_target_pairs={{0,1},{1,0},{2,3},{3,2},{4,5},{5,4},{6,7},{7,6},{8,9},{9,8},{10,11... | collective-permute-start | bytes 1179656 | tf_op jit(solution)/shard_map/ppermute | solution.py:103
  46.9 28.9 %collective-permute-start.8 = (bf16[128,2048]{1,0:T(8,128)(2,1)S(1)}, bf16[128,2048]{1,0:T(8,128)(2,1)S(1)}, u32[]{:S(2)}, u32[]{:S(2)}) collective-permute-start(bf16[128,2048]{1,0:T(8,128)(2,1)S(1)} %get-tuple-element.49), channel_id=1, source_target_pairs={{3,4},{5,6},{2,1},{4,3},{11,12},{13,14},{10,9},{12,11},{19,20},{21... | collective-permute-start | bytes 1572872 | tf_op jit(solution)/shard_map/ppermute | solution.py:457
  48.2 27.6 %collective-permute-start.9 = (bf16[128,2048]{1,0:T(8,128)(2,1)S(1)}, bf16[128,2048]{1,0:T(8,128)(2,1)S(1)}, u32[]{:S(2)}, u32[]{:S(2)}) collective-permute-start(bf16[128,2048]{1,0:T(8,128)(2,1)S(1)} %get-tuple-element.51), channel_id=1, source_target_pairs={{3,4},{5,6},{2,1},{4,3},{11,12},{13,14},{10,9},{12,11},{19,20},{21... | collective-permute-start | bytes 1572872 | tf_op jit(solution)/shard_map/ppermute | solution.py:458
  54.1 19.4 %collective-permute-start.19 = (bf16[128,1536]{1,0:T(8,128)(2,1)S(1)}, bf16[128,1536]{1,0:T(8,128)(2,1)S(1)}, u32[]{:S(2)}, u32[]{:S(2)}) collective-permute-start(bf16[128,1536]{1,0:T(8,128)(2,1)S(1)} %block_sum.4), channel_id=1, source_target_pairs={{0,16},{8,24},{16,0},{24,8},{1,17},{9,25},{17,1},{25,9},{2,18},{10... | collective-permute-start | bytes 1179656 | tf_op jit(solution)/shard_map/ppermute | solution.py:103
  56.5 17.0 %collective-permute-start.21 = (bf16[128,1536]{1,0:T(8,128)(2,1)S(1)}, bf16[128,1536]{1,0:T(8,128)(2,1)S(1)}, u32[]{:S(2)}, u32[]{:S(2)}) collective-permute-start(bf16[128,1536]{1,0:T(8,128)(2,1)S(1)} %block_sum.5), channel_id=1, source_target_pairs={{0,8},{8,0},{16,24},{24,16},{1,9},{9,1},{17,25},{25,17},{2,10},{10... | collective-permute-start | bytes 1179656 | tf_op jit(solution)/shard_map/ppermute | solution.py:103
  74.1 3.6 %collective-permute-start.22 = (f32[128,128]{1,0:T(8,128)S(1)}, f32[128,128]{1,0:T(8,128)S(1)}, u32[]{:S(2)}, u32[]{:S(2)}) collective-permute-start(f32[128,128]{1,0:T(8,128)S(1)} %get-tuple-element.67.gram), channel_id=1, source_target_pairs={{0,2},{1,3},{2,0},{3,1},{4,6},{5,7},{6,4},{7,5},{8,10},{9,11},{10,... | collective-permute-start | bytes 196616 | tf_op jit(solution)/shard_map/ppermute | solution.py:103
  80.6 7.4 %collective-permute-start.23 = (bf16[128,384]{1,0:T(8,128)(2,1)S(1)}, bf16[128,384]{1,0:T(8,128)(2,1)S(1)}, u32[]{:S(2)}, u32[]{:S(2)}) collective-permute-start(bf16[128,384]{1,0:T(8,128)(2,1)S(1)} %get-tuple-element.68), channel_id=1, source_target_pairs={{0,5},{1,4},{2,7},{3,6},{4,1},{5,0},{6,3},{7,2},{8,13},{9,12},{10,... | collective-permute-start | bytes 294920 | tf_op jit(solution)/shard_map/ppermute | solution.py:103
  84.8 4.8 %collective-permute-start.24 = (bf16[128,384]{1,0:T(8,128)(2,1)S(1)}, bf16[128,384]{1,0:T(8,128)(2,1)S(1)}, u32[]{:S(2)}, u32[]{:S(2)}) collective-permute-start(bf16[128,384]{1,0:T(8,128)(2,1)S(1)} %get-tuple-element.69), channel_id=1, source_target_pairs={{0,4},{1,5},{2,6},{3,7},{4,0},{5,1},{6,2},{7,3},{8,12},{9,13},{10,... | collective-permute-start | bytes 294920 | tf_op jit(solution)/shard_map/ppermute | solution.py:103
  84.8 4.8 %collective-permute-start.25 = (bf16[128,384]{1,0:T(8,128)(2,1)S(1)}, bf16[128,384]{1,0:T(8,128)(2,1)S(1)}, u32[]{:S(2)}, u32[]{:S(2)}) collective-permute-start(bf16[128,384]{1,0:T(8,128)(2,1)S(1)} %get-tuple-element.70), channel_id=1, source_target_pairs={{0,1},{1,0},{2,3},{3,2},{4,5},{5,4},{6,7},{7,6},{8,9},{9,8},{10,11... | collective-permute-start | bytes 294920 | tf_op jit(solution)/shard_map/ppermute | solution.py:103

commit v18 on v17

--- a/solution.py
+++ b/solution.py
@@ -282,12 +282,20 @@
 
 
 def place_kernel(plan, *refs):
-    *parts, out = refs
+    *parts, out, turned, sems = refs
     parts = parts[::-1]
     mine = plan.row_part(lax.axis_index("seq"))
+    copies = []
     for j, part in enumerate(parts):
+        source = part
+        if j:
+            turned[j - 1] = part[...].astype(f32)
+            source = turned.at[j - 1]
         at = pl.ds(pl.multiple_of((mine ^ j) * HEAD_DIM, HEAD_DIM), HEAD_DIM)
-        out[at, :] = part[...].astype(f32)
+        copies.append(pltpu.make_async_copy(source, out.at[at, :], sems.at[j]))
+        copies[-1].start()
+    for copy in copies:
+        copy.wait()
 
 
 def local(query_tiles, key_tiles, value_tiles, attn_grad, proj_grad, neighbour):
@@ -511,7 +519,11 @@
         functools.partial(place_kernel, plan),
         out_shape=struct((per * HEAD_DIM, slot), f32),
         in_specs=whole(per),
-        out_specs=pl.BlockSpec(memory_space=pltpu.VMEM),
+        out_specs=pl.BlockSpec(memory_space=pl.ANY),
+        scratch_shapes=[
+            pltpu.VMEM((per - 1, HEAD_DIM, slot), f32),
+            pltpu.SemaphoreType.DMA((per,)),
+        ],
         compiler_params=params(),
         cost_estimate=cost(1, 8 * per * HEAD_DIM * slot),
         name="update_rows",

time: 91.5 us -> 91.5 us (level)
  no operation moved by 1% of the time
where the time goes in v18:
time: 91.5 us; the launch traced here: 90.6 us
  starting transfers between devices  37.5 us (41%)
  waiting for transfers between devices  35.1 us (38%)
  Pallas kernels  15.3 us (17%)
  local copies, waits for them, and re-layouts  1.43 us (2%)
  between operations  0.93 us (1%)
    ppermute x22, waiting for transfers between devices, shift(): lax.ppermute(value, axis, [(i, i ^ mask) for i in range(lax.axis_size(axi...  29.4 us
    ppermute x22, starting transfers between devices, shift(): lax.ppermute(value, axis, [(i, i ^ mask) for i in range(lax.axis_size(axi...  29 us
    ppermute x1, waiting for transfers between devices, local(): value_next = lax.ppermute(value, 'seq', takes)  5.62 us
    ppermute x1, starting transfers between devices, local(): key_next = lax.ppermute(key, 'seq', takes)  4.67 us
    pallas_call x1, Pallas kernels, local(): pl.pallas_call(backward_kernel, out_shape=[struct((tile, width), bf16), s...  3.97 us
    pallas_call x1, Pallas kernels, local(): pl.pallas_call(functools.partial(update_kernel, plan, factor), out_shape=...  2.89 us
    pallas_call x5, Pallas kernels, product(): pl.pallas_call(functools.partial(product_kernel, counts, layers, cores),...  2.52 us
    pallas_call x1, Pallas kernels, local(): pl.pallas_call(functools.partial(forward_kernel, plan), out_shape=struct(...  2.3 us
  transfers between devices with their start and end apart: 26, of which 12 were waited for; matrix products, arithmetic and copies ran while one was open for 2% of the time, Pallas kernels for 13%

profile of v18, /device:TPU:1, one launch (start us, length us, event | category | flops | bytes accessed | tf_op | source)
XLA Modules:
  0.0 90.6 jit_solution(10844650268369287829)
XLA Ops:
  0.7 4.7 %collective-permute-start.2 = (bf16[128,2048]{1,0:T(8,128)(2,1)}, bf16[128,2048]{1,0:T(8,128)(2,1)S(1)}, u32[]{:S(2)}, u32[]{:S(2)}) collective-permute-start(bf16[128,2048]{1,0:T(8,128)(2,1)} %bitcast.25), channel_id=1, source_target_pairs={{1,2},{3,4},{4,3},{6,5},{9,10},{11,12},{12,11},{14,13},{17,18},{19... | collective-permute-start | bytes 1572872 | tf_op jit(solution)/shard_map/ppermute | solution.py:317
  5.3 1.3 %collective-permute-start.3 = (bf16[128,2048]{1,0:T(8,128)(2,1)}, bf16[128,2048]{1,0:T(8,128)(2,1)S(1)}, u32[]{:S(2)}, u32[]{:S(2)}) collective-permute-start(bf16[128,2048]{1,0:T(8,128)(2,1)} %bitcast.29), channel_id=1, source_target_pairs={{1,2},{3,4},{4,3},{6,5},{9,10},{11,12},{12,11},{14,13},{17,18},{19... | collective-permute-start | bytes 1572872 | tf_op jit(solution)/shard_map/ppermute | solution.py:318
  6.7 1.3 %dynamic-slice_bitcast_fusion.1 = (bf16[128,768]{1,0:T(8,128)(2,1)S(1)}, bf16[128,768]{1,0:T(8,128)(2,1)S(1)}, bf16[128,768]{1,0:T(8,128)(2,1)S(1)}, bf16[128,768]{1,0:T(8,128)(2,1)S(1)}) fusion(bf16[1,1,128,3072]{3,2,1,0:T(8,128)(2,1)} %param.10, s32[]{:T(128)S(6)} %select_n.14, s32[]{:T(128)S(6)} %select_n.13, s32[]{:T(128)S(6)} %select_n.12, s32[]{:T(128)S(6)} %select_n.15), kind=kLoop, calls=%fused_computation.6 | loop fusion | bytes 1572880 | tf_op jit(solution)/shard_map/dynamic_slice | solution.py:327
  8.0 0.1 fusion
  8.1 0.1 collective-permute-start
  8.2 0.5 collective-permute-start.1
  8.7 2.9 %collective-permute-start.4 = (bf16[128,1536]{1,0:T(8,128)(2,1)S(1)}, bf16[128,1536]{1,0:T(8,128)(2,1)S(1)}, u32[]{:S(2)}, u32[]{:S(2)}) collective-permute-start(bf16[128,1536]{1,0:T(8,128)(2,1)S(1)} %get-tuple-element.79), channel_id=1, source_target_pairs={{0,4},{1,5},{2,6},{3,7},{4,0},{5,1},{6,2},{7,3},{8,12},{9,13},{10,... | collective-permute-start | bytes 1179656 | tf_op jit(solution)/shard_map/ppermute | solution.py:103
  11.6 0.1 collective-permute-done.2.kn
  11.7 5.6 %collective-permute-done.3.vn = bf16[128,2048]{1,0:T(8,128)(2,1)S(1)} collective-permute-done((bf16[128,2048]{1,0:T(8,128)(2,1)}, bf16[128,2048]{1,0:T(8,128)(2,1)S(1)}, u32[]{:S(2)}, u32[]{:S(2)}) %collective-permute-start.3) | collective-permute-done | bytes 524320 | tf_op jit(solution)/shard_map/ppermute | solution.py:318
  17.3 2.8 %collective-permute-start.5 = (bf16[128,1536]{1,0:T(8,128)(2,1)S(1)}, bf16[128,1536]{1,0:T(8,128)(2,1)S(1)}, u32[]{:S(2)}, u32[]{:S(2)}) collective-permute-start(bf16[128,1536]{1,0:T(8,128)(2,1)S(1)} %pad_maximum_fusion.1), channel_id=1, source_target_pairs={{0,2},{1,3},{2,0},{3,1},{4,6},{5,7},{6,4},{7,5},{8,10},{9,11},{10,... | collective-permute-start | bytes 1179656 | tf_op jit(solution)/shard_map/ppermute | solution.py:103
  20.2 0.0 collective-permute-done.km
  20.2 0.0 collective-permute-done.1.vm
  20.2 0.0 copy-start.3
  20.2 2.3 %attention_forward.1 = bf16[2,2,512,128]{3,2,1,0:T(8,128)(2,1)S(1)} custom-call(s32[1,8]{1,0:T(1,128)S(1)} %copy-done.4, bf16[128,2048]{1,0:T(8,128)(2,1)S(1)} %bitcast.23, bf16[128,2048]{1,0:T(8,128)(2,1)S(1)} %bitcast.27, bf16[128,2048]{1,0:T(8,128)(2,1)S(1)} %bitcast.31, bf16[128,2048]{1,0:T(8,128)(2,1)S(1)} %collective-permute-done.km, ...), custom_call_target="tpu_custom_call" | custom-call | flops 268435456 | bytes 4194304 | tf_op jit(solution)/shard_map/attention_forward/pallas_call | solution.py:346
  22.5 0.1 collective-permute-start.11
  22.6 0.8 collective-permute-start.10
  23.4 4.0 %attention_backward.1 = (bf16[128,2048]{1,0:T(8,128)(2,1)}, f32[128,2048]{1,0:T(8,128)S(1)}, f32[128,2048]{1,0:T(8,128)S(1)}, bf16[128,2048]{1,0:T(8,128)(2,1)S(...) custom-call(s32[1,8]{1,0:T(1,128)S(1)} %copy-done.4, bf16[128,2048]{1,0:T(8,128)(2,1)S(1)} %bitcast.24, ...), custom_call_target="tpu_custom_call" | custom-call | flops 1 | bytes 1 | tf_op jit(solution)/shard_map/attention_backward/pallas_call | solution.py:372
  27.4 2.5 %collective-permute-done.5 = bf16[128,1536]{1,0:T(8,128)(2,1)S(1)} collective-permute-done((bf16[128,1536]{1,0:T(8,128)(2,1)S(1)}, bf16[128,1536]{1,0:T(8,128)(2,1)S(1)}, u32[]{:S(2)}, u32[]{:S(2)}) %collective-permute-start.5) | collective-permute-done | bytes 393248 | tf_op jit(solution)/shard_map/ppermute | solution.py:103
  29.9 0.1 collective-permute-start.6
  29.9 1.5 %collective-permute-start.14 = (bf16[1,128,768]{2,1,0:T(8,128)(2,1)S(1)}, bf16[1,128,768]{2,1,0:T(8,128)(2,1)S(1)}, u32[]{:S(2)}, u32[]{:S(2)}) collective-permute-start(bf16[1,128,768]{2,1,0:T(8,128)(2,1)S(1)} %get-tuple-element.80), channel_id=1, source_target_pairs={{0,4},{1,5},{2,6},{3,7},{4,0},{5,1},{6,2},{7,3},{8,12},{9,13},{10,... | collective-permute-start | bytes 589832 | tf_op jit(solution)/shard_map/ppermute | solution.py:103
  31.4 0.7 collective-permute-done.11.refs_2_
  32.1 2.3 %collective-permute-start.12 = (bf16[1,512,128]{2,1,0:T(8,128)(2,1)S(1)}, bf16[1,512,128]{2,1,0:T(8,128)(2,1)S(1)}, u32[]{:S(2)}, u32[]{:S(2)}) collective-permute-start(bf16[1,512,128]{2,1,0:T(8,128)(2,1)S(1)} %get-tuple-element.83), channel_id=1, source_target_pairs={{0,2},{1,3},{2,0},{3,1},{4,6},{5,7},{6,4},{7,5},{8,10},{9,11},{10,... | collective-permute-start | bytes 393224 | tf_op jit(solution)/shard_map/ppermute | solution.py:103
  34.4 0.1 collective-permute-start.13
  34.5 0.5 collective-permute-done.6
  35.0 4.1 %collective-permute-start.7 = (bf16[2,128,2048]{2,1,0:T(8,128)(2,1)S(1)}, bf16[2,128,2048]{2,1,0:T(8,128)(2,1)S(1)}, u32[]{:S(2)}, u32[]{:S(2)}) collective-permute-start(bf16[2,128,2048]{2,1,0:T(8,128)(2,1)S(1)} %get-tuple-element.47), channel_id=1, source_target_pairs={{0,1},{1,0},{2,3},{3,2},{4,5},{5,4},{6,7},{7,6},{8,9},{9,8},{10,11... | collective-permute-start | bytes 3145736 | tf_op jit(solution)/shard_map/ppermute | solution.py:103
  39.1 0.1 collective-permute-done.14
  39.2 0.1 maximum_maximum_fusion.refs_5_
  39.4 0.0 collective-permute-done.12.refs_3_
  39.4 1.0 %collective-permute-done.13.refs_4_ = bf16[1,512,128]{2,1,0:T(8,128)(2,1)S(1)} collective-permute-done((bf16[1,512,128]{2,1,0:T(8,128)(2,1)S(1)}, bf16[1,512,128]{2,1,0:T(8,128)(2,1)S(1)}, u32[]{:S(2)}, u32[]{:S(2)}) %collective-permute-start.13) | collective-permute-done | bytes 131104 | tf_op jit(solution)/shard_map/ppermute | solution.py:103
  40.4 0.4 product_mate.1
  40.7 1.4 %collective-permute-start.16 = (bf16[1,128,1536]{2,1,0:T(8,128)(2,1)S(1)}, bf16[1,128,1536]{2,1,0:T(8,128)(2,1)S(1)}, u32[]{:S(2)}, u32[]{:S(2)}) collective-permute-start(bf16[1,128,1536]{2,1,0:T(8,128)(2,1)S(1)} %product_mate.1), channel_id=1, source_target_pairs={{0,1},{1,0},{2,3},{3,2},{4,5},{5,4},{6,7},{7,6},{8,9},{9,8},{10,11... | collective-permute-start | bytes 1179656 | tf_op jit(solution)/shard_map/ppermute | solution.py:103
  42.1 0.6 product_near.1
  42.7 0.1 collective-permute-start.20
  42.8 0.4 product_first.1.refs_0_
  43.2 0.3 collective-permute-done.16.refs_1_
  43.5 0.1 block_sum.3
  43.6 1.4 %collective-permute-start.18 = (bf16[128,1536]{1,0:T(8,128)(2,1)S(1)}, bf16[128,1536]{1,0:T(8,128)(2,1)S(1)}, u32[]{:S(2)}, u32[]{:S(2)}) collective-permute-start(bf16[128,1536]{1,0:T(8,128)(2,1)S(1)} %block_sum.3), channel_id=1, source_target_pairs={{0,8},{8,0},{16,24},{24,16},{1,9},{9,1},{17,25},{25,17},{2,10},{10... | collective-permute-start | bytes 1179656 | tf_op jit(solution)/shard_map/ppermute | solution.py:103
  44.9 0.6 product_middle.1
  45.5 0.7 collective-permute-start.17
  46.2 0.6 product_own.1
  46.8 0.1 collective-permute-start.15
  46.9 1.3 %collective-permute-start.8 = (bf16[128,2048]{1,0:T(8,128)(2,1)S(1)}, bf16[128,2048]{1,0:T(8,128)(2,1)S(1)}, u32[]{:S(2)}, u32[]{:S(2)}) collective-permute-start(bf16[128,2048]{1,0:T(8,128)(2,1)S(1)} %get-tuple-element.49), channel_id=1, source_target_pairs={{3,4},{5,6},{2,1},{4,3},{11,12},{13,14},{10,9},{12,11},{19,20},{21... | collective-permute-start | bytes 1572872 | tf_op jit(solution)/shard_map/ppermute | solution.py:465
  48.2 0.0 collective-permute-done.17.refs_1_
  48.2 1.3 %collective-permute-start.9 = (bf16[128,2048]{1,0:T(8,128)(2,1)S(1)}, bf16[128,2048]{1,0:T(8,128)(2,1)S(1)}, u32[]{:S(2)}, u32[]{:S(2)}) collective-permute-start(bf16[128,2048]{1,0:T(8,128)(2,1)S(1)} %get-tuple-element.51), channel_id=1, source_target_pairs={{3,4},{5,6},{2,1},{4,3},{11,12},{13,14},{10,9},{12,11},{19,20},{21... | collective-permute-start | bytes 1572872 | tf_op jit(solution)/shard_map/ppermute | solution.py:466
  49.5 0.1 block_sum.5
  49.7 4.3 %collective-permute-done.18.refs_2_ = bf16[128,1536]{1,0:T(8,128)(2,1)S(1)} collective-permute-done((bf16[128,1536]{1,0:T(8,128)(2,1)S(1)}, bf16[128,1536]{1,0:T(8,128)(2,1)S(1)}, u32[]{:S(2)}, u32[]{:S(2)}) %collective-permute-start.18) | collective-permute-done | bytes 393248 | tf_op jit(solution)/shard_map/ppermute | solution.py:103
  53.9 0.1 block_sum.4
  54.1 2.4 %collective-permute-start.19 = (bf16[128,1536]{1,0:T(8,128)(2,1)S(1)}, bf16[128,1536]{1,0:T(8,128)(2,1)S(1)}, u32[]{:S(2)}, u32[]{:S(2)}) collective-permute-start(bf16[128,1536]{1,0:T(8,128)(2,1)S(1)} %block_sum.4), channel_id=1, source_target_pairs={{0,16},{8,24},{16,0},{24,8},{1,17},{9,25},{17,1},{25,9},{2,18},{10... | collective-permute-start | bytes 1179656 | tf_op jit(solution)/shard_map/ppermute | solution.py:103
  56.4 0.0 collective-permute-done.15.refs_0_
  56.5 1.3 %collective-permute-start.21 = (bf16[128,1536]{1,0:T(8,128)(2,1)S(1)}, bf16[128,1536]{1,0:T(8,128)(2,1)S(1)}, u32[]{:S(2)}, u32[]{:S(2)}) collective-permute-start(bf16[128,1536]{1,0:T(8,128)(2,1)S(1)} %block_sum.5), channel_id=1, source_target_pairs={{0,8},{8,0},{16,24},{24,16},{1,9},{9,1},{17,25},{25,17},{2,10},{10... | collective-permute-start | bytes 1179656 | tf_op jit(solution)/shard_map/ppermute | solution.py:103
  57.8 15.7 %collective-permute-done.19.refs_1_ = bf16[128,1536]{1,0:T(8,128)(2,1)S(1)} collective-permute-done((bf16[128,1536]{1,0:T(8,128)(2,1)S(1)}, bf16[128,1536]{1,0:T(8,128)(2,1)S(1)}, u32[]{:S(2)}, u32[]{:S(2)}) %collective-permute-start.19) | collective-permute-done | bytes 393248 | tf_op jit(solution)/shard_map/ppermute | solution.py:103
  73.5 0.0 collective-permute-done.21.refs_2_
  73.5 0.6 gradient_sum.1
  74.1 1.8 %collective-permute-start.22 = (f32[128,128]{1,0:T(8,128)S(1)}, f32[128,128]{1,0:T(8,128)S(1)}, u32[]{:S(2)}, u32[]{:S(2)}) collective-permute-start(f32[128,128]{1,0:T(8,128)S(1)} %get-tuple-element.67.gram), channel_id=1, source_target_pairs={{0,2},{1,3},{2,0},{3,1},{4,6},{5,7},{6,4},{7,5},{8,10},{9,11},{10,... | collective-permute-start | bytes 196616 | tf_op jit(solution)/shard_map/ppermute | solution.py:103
  75.9 1.8 %key_value_sum.1 = (bf16[128,2048]{1,0:T(8,128)(2,1)}, bf16[128,2048]{1,0:T(8,128)(2,1)}) custom-call(s32[1,8]{1,0:T(1,128)S(1)} %copy-done.4, f32[128,2048]{1,0:T(8,128)S(1)} %get-tuple-element.42.dko, f32[128,2048]{1,0:T(8,128)S(1)} %get-tuple-element.43.dvo, bf16[2,128,2048]{2,1,0:T(8,128)(2,1)S(1)} %collective-permute-done.7.mate, ...), custom_call_target="tpu_custom_call" | custom-call | flops 1572864 | bytes 5242880 | tf_op jit(solution)/shard_map/key_value_sum/pallas_call | solution.py:475
  77.7 0.0 collective-permute-done.22.gram_other
  77.7 2.9 %newton_schulz.1 = (f32[128,384]{1,0:T(8,128)S(1)}, bf16[128,384]{1,0:T(8,128)(2,1)S(1)}, bf16[128,384]{1,0:T(8,128)(2,1)S(1)}, bf16[128,384]{1,0:T(8,128)(2,1)S(1)}) custom-call(f32[128,1536]{1,0:T(8,128)S(1)} %get-tuple-element.66.x, f32[128,128]{1,0:T(8,128)S(1)} %get-tuple-element.67.gram, f32[128,128]{1,0:T(8,128)S(1)} %collective-permute-done.22.gram_other), custom_call_target="tpu_custom_call" | custom-call | flops 301989888 | bytes 1572864 | tf_op jit(solution)/shard_map/newton_schulz/pallas_call | solution.py:506
  80.6 4.2 %collective-permute-start.23 = (bf16[128,384]{1,0:T(8,128)(2,1)S(1)}, bf16[128,384]{1,0:T(8,128)(2,1)S(1)}, u32[]{:S(2)}, u32[]{:S(2)}) collective-permute-start(bf16[128,384]{1,0:T(8,128)(2,1)S(1)} %get-tuple-element.68), channel_id=1, source_target_pairs={{0,5},{1,4},{2,7},{3,6},{4,1},{5,0},{6,3},{7,2},{8,13},{9,12},{10,... | collective-permute-start | bytes 294920 | tf_op jit(solution)/shard_map/ppermute | solution.py:103
  84.8 0.0 collective-permute-start.24
  84.8 0.5 collective-permute-start.25
  85.3 2.7 %collective-permute-done.23.refs_0_ = bf16[128,384]{1,0:T(8,128)(2,1)S(1)} collective-permute-done((bf16[128,384]{1,0:T(8,128)(2,1)S(1)}, bf16[128,384]{1,0:T(8,128)(2,1)S(1)}, u32[]{:S(2)}, u32[]{:S(2)}) %collective-permute-start.23) | collective-permute-done | bytes 98336 | tf_op jit(solution)/shard_map/ppermute | solution.py:103
  88.0 1.7 %collective-permute-done.24.refs_1_ = bf16[128,384]{1,0:T(8,128)(2,1)S(1)} collective-permute-done((bf16[128,384]{1,0:T(8,128)(2,1)S(1)}, bf16[128,384]{1,0:T(8,128)(2,1)S(1)}, u32[]{:S(2)}, u32[]{:S(2)}) %collective-permute-start.24) | collective-permute-done | bytes 98336 | tf_op jit(solution)/shard_map/ppermute | solution.py:103
  89.7 0.0 collective-permute-done.25.refs_2_
  89.7 0.9 %update_rows.1 = f32[512,384]{1,0:T(8,128)} custom-call(bf16[128,384]{1,0:T(8,128)(2,1)S(1)} %collective-permute-done.23.refs_0_, bf16[128,384]{1,0:T(8,128)(2,1)S(1)} %collective-permute-done.24.refs_1_, bf16[128,384]{1,0:T(8,128)(2,1)S(1)} %collective-permute-done.25.refs_2_, f32[128,384]{1,0:T(8,128)S(1)} %get-tuple-element.71.refs_3_), custom_call_target="tpu_custom_call" | custom-call | flops 1 | bytes 1572864 | tf_op jit(solution)/shard_map/update_rows/pallas_call | solution.py:518
  (19 shorter events, 0.1 us)
Async XLA Ops:
  0.6 7.5 %copy-start.1 = (bf16[1,1,128,2048]{3,2,1,0:T(8,128)(2,1)S(1)}, bf16[1,1,128,2048]{3,2,1,0:T(8,128)(2,1)}, u32[]{:S(2)}) copy-start(bf16[1,1,128,2048]{3,2,1,0:T(8,128)(2,1)} %param.7) | copy-start | bytes 1572868
  0.6 7.5 %copy-start.2 = (bf16[1,1,128,2048]{3,2,1,0:T(8,128)(2,1)S(1)}, bf16[1,1,128,2048]{3,2,1,0:T(8,128)(2,1)}, u32[]{:S(2)}) copy-start(bf16[1,1,128,2048]{3,2,1,0:T(8,128)(2,1)} %param.8) | copy-start | bytes 1572868
  0.7 11.1 %collective-permute-start.2 = (bf16[128,2048]{1,0:T(8,128)(2,1)}, bf16[128,2048]{1,0:T(8,128)(2,1)S(1)}, u32[]{:S(2)}, u32[]{:S(2)}) collective-permute-start(bf16[128,2048]{1,0:T(8,128)(2,1)} %bitcast.25), channel_id=1, source_target_pairs={{1,2},{3,4},{4,3},{6,5},{9,10},{11,12},{12,11},{14,13},{17,18},{19... | collective-permute-start | bytes 1572872 | tf_op jit(solution)/shard_map/ppermute | solution.py:317
  5.3 12.0 %collective-permute-start.3 = (bf16[128,2048]{1,0:T(8,128)(2,1)}, bf16[128,2048]{1,0:T(8,128)(2,1)S(1)}, u32[]{:S(2)}, u32[]{:S(2)}) collective-permute-start(bf16[128,2048]{1,0:T(8,128)(2,1)} %bitcast.29), channel_id=1, source_target_pairs={{1,2},{3,4},{4,3},{6,5},{9,10},{11,12},{12,11},{14,13},{17,18},{19... | collective-permute-start | bytes 1572872 | tf_op jit(solution)/shard_map/ppermute | solution.py:318
  6.7 13.5 %copy-start = (bf16[1,1,128,2048]{3,2,1,0:T(8,128)(2,1)S(1)}, bf16[1,1,128,2048]{3,2,1,0:T(8,128)(2,1)}, u32[]{:S(2)}) copy-start(bf16[1,1,128,2048]{3,2,1,0:T(8,128)(2,1)} %param.6) | copy-start | bytes 1572868
  6.7 13.5 %copy-start.4 = (s32[1,8]{1,0:T(1,128)S(1)}, s32[1,8]{1,0:T(1,128)}, u32[]{:S(2)}) copy-start(s32[1,8]{1,0:T(1,128)} %near_ref.5) | copy-start | bytes 100
  8.1 12.1 %collective-permute-start = (bf16[128,2048]{1,0:T(8,128)(2,1)S(1)}, bf16[128,2048]{1,0:T(8,128)(2,1)S(1)}, u32[]{:S(2)}, u32[]{:S(2)}) collective-permute-start(bf16[128,2048]{1,0:T(8,128)(2,1)S(1)} %bitcast.26), channel_id=1, source_target_pairs={{0,1},{1,0},{2,3},{3,2},{4,5},{5,4},{6,7},{7,6},{8,9},{9,8},{10,11... | collective-permute-start | bytes 1572872 | tf_op jit(solution)/shard_map/ppermute | solution.py:103
  8.2 12.0 %collective-permute-start.1 = (bf16[128,2048]{1,0:T(8,128)(2,1)S(1)}, bf16[128,2048]{1,0:T(8,128)(2,1)S(1)}, u32[]{:S(2)}, u32[]{:S(2)}) collective-permute-start(bf16[128,2048]{1,0:T(8,128)(2,1)S(1)} %bitcast.30), channel_id=1, source_target_pairs={{0,1},{1,0},{2,3},{3,2},{4,5},{5,4},{6,7},{7,6},{8,9},{9,8},{10,11... | collective-permute-start | bytes 1572872 | tf_op jit(solution)/shard_map/ppermute | solution.py:103
  8.7 18.7 %collective-permute-start.4 = (bf16[128,1536]{1,0:T(8,128)(2,1)S(1)}, bf16[128,1536]{1,0:T(8,128)(2,1)S(1)}, u32[]{:S(2)}, u32[]{:S(2)}) collective-permute-start(bf16[128,1536]{1,0:T(8,128)(2,1)S(1)} %get-tuple-element.79), channel_id=1, source_target_pairs={{0,4},{1,5},{2,6},{3,7},{4,0},{5,1},{6,2},{7,3},{8,12},{9,13},{10,... | collective-permute-start | bytes 1179656 | tf_op jit(solution)/shard_map/ppermute | solution.py:103
  17.3 12.5 %collective-permute-start.5 = (bf16[128,1536]{1,0:T(8,128)(2,1)S(1)}, bf16[128,1536]{1,0:T(8,128)(2,1)S(1)}, u32[]{:S(2)}, u32[]{:S(2)}) collective-permute-start(bf16[128,1536]{1,0:T(8,128)(2,1)S(1)} %pad_maximum_fusion.1), channel_id=1, source_target_pairs={{0,2},{1,3},{2,0},{3,1},{4,6},{5,7},{6,4},{7,5},{8,10},{9,11},{10,... | collective-permute-start | bytes 1179656 | tf_op jit(solution)/shard_map/ppermute | solution.py:103
  20.2 3.2 %copy-start.3 = (bf16[1,1,128,2048]{3,2,1,0:T(8,128)(2,1)S(1)}, bf16[1,1,128,2048]{3,2,1,0:T(8,128)(2,1)}, u32[]{:S(2)}) copy-start(bf16[1,1,128,2048]{3,2,1,0:T(8,128)(2,1)} %param.9) | copy-start | bytes 1572868
  22.5 9.6 %collective-permute-start.11 = (bf16[2,512,128]{2,1,0:T(8,128)(2,1)S(1)}, bf16[2,512,128]{2,1,0:T(8,128)(2,1)S(1)}, u32[]{:S(2)}, u32[]{:S(2)}) collective-permute-start(bf16[2,512,128]{2,1,0:T(8,128)(2,1)S(1)} %get-tuple-element.76), channel_id=1, source_target_pairs={{0,4},{1,5},{2,6},{3,7},{4,0},{5,1},{6,2},{7,3},{8,12},{9,13},{10,... | collective-permute-start | bytes 786440 | tf_op jit(solution)/shard_map/ppermute | solution.py:103
  22.6 16.7 %collective-permute-start.10 = (bf16[2,512,128]{2,1,0:T(8,128)(2,1)S(1)}, bf16[2,512,128]{2,1,0:T(8,128)(2,1)S(1)}, u32[]{:S(2)}, u32[]{:S(2)}) collective-permute-start(bf16[2,512,128]{2,1,0:T(8,128)(2,1)S(1)} %get-tuple-element.58.refs_0_), channel_id=1, source_target_pairs={{0,2},{1,3},{2,0},{3,1},{4,6},{5,7},{6,4},{7,5},{8,10},{9,11},{10,... | collective-permute-start | bytes 786440 | tf_op jit(solution)/shard_map/ppermute | solution.py:103
  29.9 5.2 %collective-permute-start.6 = (bf16[1,128,768]{2,1,0:T(8,128)(2,1)S(1)}, bf16[1,128,768]{2,1,0:T(8,128)(2,1)S(1)}, u32[]{:S(2)}, u32[]{:S(2)}) collective-permute-start(bf16[1,128,768]{2,1,0:T(8,128)(2,1)S(1)} %get-tuple-element.81), channel_id=1, source_target_pairs={{0,4},{1,5},{2,6},{3,7},{4,0},{5,1},{6,2},{7,3},{8,12},{9,13},{10,... | collective-permute-start | bytes 589832 | tf_op jit(solution)/shard_map/ppermute | solution.py:103
  29.9 9.3 %collective-permute-start.14 = (bf16[1,128,768]{2,1,0:T(8,128)(2,1)S(1)}, bf16[1,128,768]{2,1,0:T(8,128)(2,1)S(1)}, u32[]{:S(2)}, u32[]{:S(2)}) collective-permute-start(bf16[1,128,768]{2,1,0:T(8,128)(2,1)S(1)} %get-tuple-element.80), channel_id=1, source_target_pairs={{0,4},{1,5},{2,6},{3,7},{4,0},{5,1},{6,2},{7,3},{8,12},{9,13},{10,... | collective-permute-start | bytes 589832 | tf_op jit(solution)/shard_map/ppermute | solution.py:103
  32.1 7.2 %collective-permute-start.12 = (bf16[1,512,128]{2,1,0:T(8,128)(2,1)S(1)}, bf16[1,512,128]{2,1,0:T(8,128)(2,1)S(1)}, u32[]{:S(2)}, u32[]{:S(2)}) collective-permute-start(bf16[1,512,128]{2,1,0:T(8,128)(2,1)S(1)} %get-tuple-element.83), channel_id=1, source_target_pairs={{0,2},{1,3},{2,0},{3,1},{4,6},{5,7},{6,4},{7,5},{8,10},{9,11},{10,... | collective-permute-start | bytes 393224 | tf_op jit(solution)/shard_map/ppermute | solution.py:103
  34.4 5.9 %collective-permute-start.13 = (bf16[1,512,128]{2,1,0:T(8,128)(2,1)S(1)}, bf16[1,512,128]{2,1,0:T(8,128)(2,1)S(1)}, u32[]{:S(2)}, u32[]{:S(2)}) collective-permute-start(bf16[1,512,128]{2,1,0:T(8,128)(2,1)S(1)} %get-tuple-element.82), channel_id=1, source_target_pairs={{0,2},{1,3},{2,0},{3,1},{4,6},{5,7},{6,4},{7,5},{8,10},{9,11},{10,... | collective-permute-start | bytes 393224 | tf_op jit(solution)/shard_map/ppermute | solution.py:103
  35.0 21.4 %collective-permute-start.7 = (bf16[2,128,2048]{2,1,0:T(8,128)(2,1)S(1)}, bf16[2,128,2048]{2,1,0:T(8,128)(2,1)S(1)}, u32[]{:S(2)}, u32[]{:S(2)}) collective-permute-start(bf16[2,128,2048]{2,1,0:T(8,128)(2,1)S(1)} %get-tuple-element.47), channel_id=1, source_target_pairs={{0,1},{1,0},{2,3},{3,2},{4,5},{5,4},{6,7},{7,6},{8,9},{9,8},{10,11... | collective-permute-start | bytes 3145736 | tf_op jit(solution)/shard_map/ppermute | solution.py:103
  40.7 2.8 %collective-permute-start.16 = (bf16[1,128,1536]{2,1,0:T(8,128)(2,1)S(1)}, bf16[1,128,1536]{2,1,0:T(8,128)(2,1)S(1)}, u32[]{:S(2)}, u32[]{:S(2)}) collective-permute-start(bf16[1,128,1536]{2,1,0:T(8,128)(2,1)S(1)} %product_mate.1), channel_id=1, source_target_pairs={{0,1},{1,0},{2,3},{3,2},{4,5},{5,4},{6,7},{7,6},{8,9},{9,8},{10,11... | collective-permute-start | bytes 1179656 | tf_op jit(solution)/shard_map/ppermute | solution.py:103
  42.7 4.2 %collective-permute-start.20 = (bf16[1,128,1536]{2,1,0:T(8,128)(2,1)S(1)}, bf16[1,128,1536]{2,1,0:T(8,128)(2,1)S(1)}, u32[]{:S(2)}, u32[]{:S(2)}) collective-permute-start(bf16[1,128,1536]{2,1,0:T(8,128)(2,1)S(1)} %get-tuple-element.63), channel_id=1, source_target_pairs={{0,1},{1,0},{2,3},{3,2},{4,5},{5,4},{6,7},{7,6},{8,9},{9,8},{10,11... | collective-permute-start | bytes 1179656 | tf_op jit(solution)/shard_map/ppermute | solution.py:103
  43.6 10.4 %collective-permute-start.18 = (bf16[128,1536]{1,0:T(8,128)(2,1)S(1)}, bf16[128,1536]{1,0:T(8,128)(2,1)S(1)}, u32[]{:S(2)}, u32[]{:S(2)}) collective-permute-start(bf16[128,1536]{1,0:T(8,128)(2,1)S(1)} %block_sum.3), channel_id=1, source_target_pairs={{0,8},{8,0},{16,24},{24,16},{1,9},{9,1},{17,25},{25,17},{2,10},{10... | collective-permute-start | bytes 1179656 | tf_op jit(solution)/shard_map/ppermute | solution.py:103
  45.5 2.7 %collective-permute-start.17 = (bf16[1,128,1536]{2,1,0:T(8,128)(2,1)S(1)}, bf16[1,128,1536]{2,1,0:T(8,128)(2,1)S(1)}, u32[]{:S(2)}, u32[]{:S(2)}) collective-permute-start(bf16[1,128,1536]{2,1,0:T(8,128)(2,1)S(1)} %get-tuple-element.61), channel_id=1, source_target_pairs={{0,1},{1,0},{2,3},{3,2},{4,5},{5,4},{6,7},{7,6},{8,9},{9,8},{10,11... | collective-permute-start | bytes 1179656 | tf_op jit(solution)/shard_map/ppermute | solution.py:103
  46.8 9.6 %collective-permute-start.15 = (bf16[1,128,1536]{2,1,0:T(8,128)(2,1)S(1)}, bf16[1,128,1536]{2,1,0:T(8,128)(2,1)S(1)}, u32[]{:S(2)}, u32[]{:S(2)}) collective-permute-start(bf16[1,128,1536]{2,1,0:T(8,128)(2,1)S(1)} %get-tuple-element.56), channel_id=1, source_target_pairs={{0,1},{1,0},{2,3},{3,2},{4,5},{5,4},{6,7},{7,6},{8,9},{9,8},{10,11... | collective-permute-start | bytes 1179656 | tf_op jit(solution)/shard_map/ppermute | solution.py:103
  46.9 28.9 %collective-permute-start.8 = (bf16[128,2048]{1,0:T(8,128)(2,1)S(1)}, bf16[128,2048]{1,0:T(8,128)(2,1)S(1)}, u32[]{:S(2)}, u32[]{:S(2)}) collective-permute-start(bf16[128,2048]{1,0:T(8,128)(2,1)S(1)} %get-tuple-element.49), channel_id=1, source_target_pairs={{3,4},{5,6},{2,1},{4,3},{11,12},{13,14},{10,9},{12,11},{19,20},{21... | collective-permute-start | bytes 1572872 | tf_op jit(solution)/shard_map/ppermute | solution.py:465
  48.2 27.6 %collective-permute-start.9 = (bf16[128,2048]{1,0:T(8,128)(2,1)S(1)}, bf16[128,2048]{1,0:T(8,128)(2,1)S(1)}, u32[]{:S(2)}, u32[]{:S(2)}) collective-permute-start(bf16[128,2048]{1,0:T(8,128)(2,1)S(1)} %get-tuple-element.51), channel_id=1, source_target_pairs={{3,4},{5,6},{2,1},{4,3},{11,12},{13,14},{10,9},{12,11},{19,20},{21... | collective-permute-start | bytes 1572872 | tf_op jit(solution)/shard_map/ppermute | solution.py:466
  54.1 19.4 %collective-permute-start.19 = (bf16[128,1536]{1,0:T(8,128)(2,1)S(1)}, bf16[128,1536]{1,0:T(8,128)(2,1)S(1)}, u32[]{:S(2)}, u32[]{:S(2)}) collective-permute-start(bf16[128,1536]{1,0:T(8,128)(2,1)S(1)} %block_sum.4), channel_id=1, source_target_pairs={{0,16},{8,24},{16,0},{24,8},{1,17},{9,25},{17,1},{25,9},{2,18},{10... | collective-permute-start | bytes 1179656 | tf_op jit(solution)/shard_map/ppermute | solution.py:103
  56.5 17.0 %collective-permute-start.21 = (bf16[128,1536]{1,0:T(8,128)(2,1)S(1)}, bf16[128,1536]{1,0:T(8,128)(2,1)S(1)}, u32[]{:S(2)}, u32[]{:S(2)}) collective-permute-start(bf16[128,1536]{1,0:T(8,128)(2,1)S(1)} %block_sum.5), channel_id=1, source_target_pairs={{0,8},{8,0},{16,24},{24,16},{1,9},{9,1},{17,25},{25,17},{2,10},{10... | collective-permute-start | bytes 1179656 | tf_op jit(solution)/shard_map/ppermute | solution.py:103
  74.1 3.6 %collective-permute-start.22 = (f32[128,128]{1,0:T(8,128)S(1)}, f32[128,128]{1,0:T(8,128)S(1)}, u32[]{:S(2)}, u32[]{:S(2)}) collective-permute-start(f32[128,128]{1,0:T(8,128)S(1)} %get-tuple-element.67.gram), channel_id=1, source_target_pairs={{0,2},{1,3},{2,0},{3,1},{4,6},{5,7},{6,4},{7,5},{8,10},{9,11},{10,... | collective-permute-start | bytes 196616 | tf_op jit(solution)/shard_map/ppermute | solution.py:103
  80.6 7.4 %collective-permute-start.23 = (bf16[128,384]{1,0:T(8,128)(2,1)S(1)}, bf16[128,384]{1,0:T(8,128)(2,1)S(1)}, u32[]{:S(2)}, u32[]{:S(2)}) collective-permute-start(bf16[128,384]{1,0:T(8,128)(2,1)S(1)} %get-tuple-element.68), channel_id=1, source_target_pairs={{0,5},{1,4},{2,7},{3,6},{4,1},{5,0},{6,3},{7,2},{8,13},{9,12},{10,... | collective-permute-start | bytes 294920 | tf_op jit(solution)/shard_map/ppermute | solution.py:103
  84.8 4.8 %collective-permute-start.24 = (bf16[128,384]{1,0:T(8,128)(2,1)S(1)}, bf16[128,384]{1,0:T(8,128)(2,1)S(1)}, u32[]{:S(2)}, u32[]{:S(2)}) collective-permute-start(bf16[128,384]{1,0:T(8,128)(2,1)S(1)} %get-tuple-element.69), channel_id=1, source_target_pairs={{0,4},{1,5},{2,6},{3,7},{4,0},{5,1},{6,2},{7,3},{8,12},{9,13},{10,... | collective-permute-start | bytes 294920 | tf_op jit(solution)/shard_map/ppermute | solution.py:103
  84.8 4.8 %collective-permute-start.25 = (bf16[128,384]{1,0:T(8,128)(2,1)S(1)}, bf16[128,384]{1,0:T(8,128)(2,1)S(1)}, u32[]{:S(2)}, u32[]{:S(2)}) collective-permute-start(bf16[128,384]{1,0:T(8,128)(2,1)S(1)} %get-tuple-element.70), channel_id=1, source_target_pairs={{0,1},{1,0},{2,3},{3,2},{4,5},{5,4},{6,7},{7,6},{8,9},{9,8},{10,11... | collective-permute-start | bytes 294920 | tf_op jit(solution)/shard_map/ppermute | solution.py:103

commit v19 on v17

--- a/solution.py
+++ b/solution.py
@@ -229,8 +229,18 @@
     out[...] = total.astype(bf16)
 
 
-def gram_kernel(spots, own, *refs):
-    *parts, x, gram = refs
+def column_block(plan, x, part, width):
+    if width % HEAD_DIM == 0:
+        return x[:, pl.ds(pl.multiple_of(part * width, width), width)]
+    block = jnp.zeros((HEAD_DIM, width), f32)
+    for r in range(plan.per_target):
+        block = jnp.where(part == r, x[:, r * width : (r + 1) * width], block)
+    return block
+
+
+def gram_kernel(plan, spots, own, *refs):
+    parts = refs[: len(spots)]
+    *outs, gram, x = refs[len(spots) :]
     x[...] = own[...]
     for (lead, first), part in zip(spots, parts, strict=True):
         size = part.shape[-1]
@@ -241,6 +251,9 @@
     wide = dot_t(pair, pair)
     cross = wide[:size, size:] + dot_t(high, low)
     gram[...] = wide[:size, :size] + (wide[size:, size:] + (cross + cross.T))
+    mine = plan.row_part(lax.axis_index("seq"))
+    for j, out in enumerate(outs):
+        out[...] = column_block(plan, x, mine ^ j, out.shape[1]).astype(out.dtype)
 
 
 def polynomial(gram):
@@ -262,32 +275,19 @@
     return p, inverse
 
 
-def update_kernel(plan, factor, x, gram, gram_other, *outs):
+def polynomial_kernel(factor, gram, gram_other, out):
+    p, inverse = polynomial(gram[...] + gram_other[...])
+    out[...] = p * (inverse * factor)
+
+
+def update_kernel(plan, *refs):
+    *pairs, out = refs
     mine = plan.row_part(lax.axis_index("seq"))
-    p, inverse = polynomial(gram[...] + gram_other[...])
-    p = p * (inverse * factor)
-    p_parts = parts_of(p)
-    width = outs[0].shape[1]
-    wide = width % HEAD_DIM == 0
+    wide = out.shape[1] % HEAD_DIM == 0
     for j in range(plan.per_target):
-        if width % HEAD_DIM == 0:
-            block = x[:, pl.ds(pl.multiple_of((mine ^ j) * width, width), width)]
-        else:
-            block = jnp.zeros((HEAD_DIM, width), f32)
-            for r in range(plan.per_target):
-                part = x[:, r * width : (r + 1) * width]
-                block = jnp.where((mine ^ j) == r, part, block)
-        piece_out = split_dot(p_parts, parts_of(block)) if wide else exact(p, block)
-        outs[j][...] = piece_out.astype(outs[j].dtype)
-
-
-def place_kernel(plan, *refs):
-    *parts, out = refs
-    parts = parts[::-1]
-    mine = plan.row_part(lax.axis_index("seq"))
-    for j, part in enumerate(parts):
+        p, block = pairs[2 * j][...], pairs[2 * j + 1][...].astype(f32)
         at = pl.ds(pl.multiple_of((mine ^ j) * HEAD_DIM, HEAD_DIM), HEAD_DIM)
-        out[at, :] = part[...].astype(f32)
+        out[at, :] = split_dot(parts_of(p), parts_of(block)) if wide else exact(p, block)
 
 
 def local(query_tiles, key_tiles, value_tiles, attn_grad, proj_grad, neighbour):
@@ -479,11 +479,14 @@
         *far,
     )
 
-    x, gram = pl.pallas_call(
-        functools.partial(gram_kernel, [spot for _, *spot in came]),
-        out_shape=[struct((HEAD_DIM, mine_width), f32), struct((HEAD_DIM, HEAD_DIM), f32)],
+    *blocks_out, gram = pl.pallas_call(
+        functools.partial(gram_kernel, plan, [spot for _, *spot in came]),
+        out_shape=[struct((HEAD_DIM, slot), f32)]
+        + [struct((HEAD_DIM, slot), bf16)] * (per - 1)
+        + [struct((HEAD_DIM, HEAD_DIM), f32)],
         in_specs=whole(1 + len(came)),
-        out_specs=whole(2),
+        out_specs=whole(per + 1),
+        scratch_shapes=[pltpu.VMEM((HEAD_DIM, mine_width), f32)],
         compiler_params=params(),
         cost_estimate=cost(12 * HEAD_DIM * HEAD_DIM * mine_width, 14 * HEAD_DIM * mine_width),
         name="gradient_sum",
@@ -495,27 +498,29 @@
         gram_other = shift(gram, "seq", 2 << b)
 
     factor = 0.2 * depth**0.5
-    pieces = pl.pallas_call(
-        functools.partial(update_kernel, plan, factor),
-        out_shape=[struct((HEAD_DIM, slot), f32)] + [struct((HEAD_DIM, slot), bf16)] * (per - 1),
-        in_specs=whole(3),
-        out_specs=whole(per),
+    matrix = pl.BlockSpec(memory_space=pltpu.VMEM)
+    p = pl.pallas_call(
+        functools.partial(polynomial_kernel, factor),
+        out_shape=struct((HEAD_DIM, HEAD_DIM), f32),
+        in_specs=whole(2),
+        out_specs=matrix,
         compiler_params=params(),
         cost_estimate=cost(12 * HEAD_DIM * HEAD_DIM * mine_width, 8 * HEAD_DIM * mine_width),
         name="newton_schulz",
-    )(after(x, dk), gram, gram_other)
-    pieces = [pieces[0]] + [
-        shift(pieces[j], "seq", plan.row_mask(j)) for j in range(1, per)
-    ]
+    )(gram, gram_other)
+    moved = [shift(blocks_out[j], "seq", plan.row_mask(j)) for j in range(1, per)]
+    operands = [after(p, dk), blocks_out[0]]
+    for j in range(1, per):
+        operands += [shift(after(p, *moved), "seq", plan.row_mask(j)), moved[j - 1]]
     update = pl.pallas_call(
-        functools.partial(place_kernel, plan),
+        functools.partial(update_kernel, plan),
         out_shape=struct((per * HEAD_DIM, slot), f32),
-        in_specs=whole(per),
-        out_specs=pl.BlockSpec(memory_space=pltpu.VMEM),
+        in_specs=whole(2 * per),
+        out_specs=matrix,
         compiler_params=params(),
         cost_estimate=cost(1, 8 * per * HEAD_DIM * slot),
         name="update_rows",
-    )(*reversed(pieces))
+    )(*operands)
 
     shape = query_tiles.shape
     return dq.reshape(shape), dk.reshape(shape), dv.reshape(shape), update

time: 91.5 us -> 98.7 us (1.079)
  waiting for transfers between devices: 35.1 us -> 43.2 us
    ppermute x22 -> x25, waiting for transfers between devices: 29.4 us -> 37.5 us  [shift(): lax.ppermute(value, axis, [(i, i ^ mask) for i in range(lax.axis_size(axi...]
    ppermute x22 -> x25, starting transfers between devices: 29 us -> 28.5 us  [shift(): lax.ppermute(value, axis, [(i, i ^ mask) for i in range(lax.axis_size(axi...]
  transfers between devices with their start and end apart: 26 -> 29, of which waited for: 12 -> 14; matrix products, arithmetic and copies ran while one was open for 2% -> 2% of each run, Pallas kernels for 13% -> 14%
where the time goes in v19:
time: 98.7 us; the launch traced here: 98.4 us
  waiting for transfers between devices  43.2 us (44%)
  starting transfers between devices  37.2 us (38%)
  Pallas kernels  15.4 us (16%)
  local copies, waits for them, and re-layouts  1.43 us (1%)
    ppermute x25, waiting for transfers between devices, shift(): lax.ppermute(value, axis, [(i, i ^ mask) for i in range(lax.axis_size(axi...  37.5 us
    ppermute x25, starting transfers between devices, shift(): lax.ppermute(value, axis, [(i, i ^ mask) for i in range(lax.axis_size(axi...  28.5 us
    ppermute x1, waiting for transfers between devices, local(): value_next = lax.ppermute(value, 'seq', takes)  5.62 us
    ppermute x1, starting transfers between devices, local(): key_next = lax.ppermute(key, 'seq', takes)  4.67 us
    pallas_call x1, Pallas kernels, local(): pl.pallas_call(backward_kernel, out_shape=[struct((tile, width), bf16), s...  3.9 us
    pallas_call x5, Pallas kernels, product(): pl.pallas_call(functools.partial(product_kernel, counts, layers, cores),...  2.53 us
    pallas_call x1, Pallas kernels, local(): pl.pallas_call(functools.partial(polynomial_kernel, factor), out_shape=st...  2.42 us
    pallas_call x1, Pallas kernels, local(): pl.pallas_call(functools.partial(forward_kernel, plan), out_shape=struct(...  2.3 us
  transfers between devices with their start and end apart: 29, of which 14 were waited for; matrix products, arithmetic and copies ran while one was open for 2% of the time, Pallas kernels for 14%

profile of v19, /device:TPU:1, one launch (start us, length us, event | category | flops | bytes accessed | tf_op | source)
XLA Modules:
  0.0 98.4 jit_solution(3090116117185564953)
XLA Ops:
  0.7 4.7 %collective-permute-start.2 = (bf16[128,2048]{1,0:T(8,128)(2,1)}, bf16[128,2048]{1,0:T(8,128)(2,1)S(1)}, u32[]{:S(2)}, u32[]{:S(2)}) collective-permute-start(bf16[128,2048]{1,0:T(8,128)(2,1)} %bitcast.25), channel_id=1, source_target_pairs={{1,2},{3,4},{4,3},{6,5},{9,10},{11,12},{12,11},{14,13},{17,18},{19... | collective-permute-start | bytes 1572872 | tf_op jit(solution)/shard_map/ppermute | solution.py:309
  5.3 1.3 %collective-permute-start.3 = (bf16[128,2048]{1,0:T(8,128)(2,1)}, bf16[128,2048]{1,0:T(8,128)(2,1)S(1)}, u32[]{:S(2)}, u32[]{:S(2)}) collective-permute-start(bf16[128,2048]{1,0:T(8,128)(2,1)} %bitcast.29), channel_id=1, source_target_pairs={{1,2},{3,4},{4,3},{6,5},{9,10},{11,12},{12,11},{14,13},{17,18},{19... | collective-permute-start | bytes 1572872 | tf_op jit(solution)/shard_map/ppermute | solution.py:310
  6.7 1.3 %dynamic-slice_bitcast_fusion.1 = (bf16[128,768]{1,0:T(8,128)(2,1)S(1)}, bf16[128,768]{1,0:T(8,128)(2,1)S(1)}, bf16[128,768]{1,0:T(8,128)(2,1)S(1)}, bf16[128,768]{1,0:T(8,128)(2,1)S(1)}) fusion(bf16[1,1,128,3072]{3,2,1,0:T(8,128)(2,1)} %param.10, s32[]{:T(128)S(6)} %select_n.14, s32[]{:T(128)S(6)} %select_n.13, s32[]{:T(128)S(6)} %select_n.12, s32[]{:T(128)S(6)} %select_n.15), kind=kLoop, calls=%fused_computation.6 | loop fusion | bytes 1572880 | tf_op jit(solution)/shard_map/dynamic_slice | solution.py:319
  8.0 0.1 fusion
  8.1 0.1 collective-permute-start
  8.2 0.5 collective-permute-start.1
  8.7 2.9 %collective-permute-start.4 = (bf16[128,1536]{1,0:T(8,128)(2,1)S(1)}, bf16[128,1536]{1,0:T(8,128)(2,1)S(1)}, u32[]{:S(2)}, u32[]{:S(2)}) collective-permute-start(bf16[128,1536]{1,0:T(8,128)(2,1)S(1)} %get-tuple-element.79), channel_id=1, source_target_pairs={{0,4},{1,5},{2,6},{3,7},{4,0},{5,1},{6,2},{7,3},{8,12},{9,13},{10,... | collective-permute-start | bytes 1179656 | tf_op jit(solution)/shard_map/ppermute | solution.py:103
  11.6 0.1 collective-permute-done.2.kn
  11.7 5.6 %collective-permute-done.3.vn = bf16[128,2048]{1,0:T(8,128)(2,1)S(1)} collective-permute-done((bf16[128,2048]{1,0:T(8,128)(2,1)}, bf16[128,2048]{1,0:T(8,128)(2,1)S(1)}, u32[]{:S(2)}, u32[]{:S(2)}) %collective-permute-start.3) | collective-permute-done | bytes 524320 | tf_op jit(solution)/shard_map/ppermute | solution.py:310
  17.3 2.8 %collective-permute-start.5 = (bf16[128,1536]{1,0:T(8,128)(2,1)S(1)}, bf16[128,1536]{1,0:T(8,128)(2,1)S(1)}, u32[]{:S(2)}, u32[]{:S(2)}) collective-permute-start(bf16[128,1536]{1,0:T(8,128)(2,1)S(1)} %pad_maximum_fusion.1), channel_id=1, source_target_pairs={{0,2},{1,3},{2,0},{3,1},{4,6},{5,7},{6,4},{7,5},{8,10},{9,11},{10,... | collective-permute-start | bytes 1179656 | tf_op jit(solution)/shard_map/ppermute | solution.py:103
  20.2 0.0 copy-start.3
  20.2 2.3 %attention_forward.1 = bf16[2,2,512,128]{3,2,1,0:T(8,128)(2,1)S(1)} custom-call(s32[1,8]{1,0:T(1,128)S(1)} %copy-done.4, bf16[128,2048]{1,0:T(8,128)(2,1)S(1)} %bitcast.23, bf16[128,2048]{1,0:T(8,128)(2,1)S(1)} %bitcast.27, bf16[128,2048]{1,0:T(8,128)(2,1)S(1)} %bitcast.31, bf16[128,2048]{1,0:T(8,128)(2,1)S(1)} %collective-permute-done.km, ...), custom_call_target="tpu_custom_call" | custom-call | flops 268435456 | bytes 4194304 | tf_op jit(solution)/shard_map/attention_forward/pallas_call | solution.py:338
  22.5 0.1 collective-permute-start.11
  22.6 0.8 collective-permute-start.10
  23.4 3.9 %attention_backward.1 = (bf16[128,2048]{1,0:T(8,128)(2,1)}, f32[128,2048]{1,0:T(8,128)S(1)}, f32[128,2048]{1,0:T(8,128)S(1)}, bf16[128,2048]{1,0:T(8,128)(2,1)S(...) custom-call(s32[1,8]{1,0:T(1,128)S(1)} %copy-done.4, bf16[128,2048]{1,0:T(8,128)(2,1)S(1)} %bitcast.24, ...), custom_call_target="tpu_custom_call" | custom-call | flops 1 | bytes 1 | tf_op jit(solution)/shard_map/attention_backward/pallas_call | solution.py:364
  27.3 0.0 collective-permute-done.4
  27.3 2.5 %collective-permute-done.5 = bf16[128,1536]{1,0:T(8,128)(2,1)S(1)} collective-permute-done((bf16[128,1536]{1,0:T(8,128)(2,1)S(1)}, bf16[128,1536]{1,0:T(8,128)(2,1)S(1)}, u32[]{:S(2)}, u32[]{:S(2)}) %collective-permute-start.5) | collective-permute-done | bytes 393248 | tf_op jit(solution)/shard_map/ppermute | solution.py:103
  29.9 0.1 collective-permute-start.6
  29.9 1.5 %collective-permute-start.14 = (bf16[1,128,768]{2,1,0:T(8,128)(2,1)S(1)}, bf16[1,128,768]{2,1,0:T(8,128)(2,1)S(1)}, u32[]{:S(2)}, u32[]{:S(2)}) collective-permute-start(bf16[1,128,768]{2,1,0:T(8,128)(2,1)S(1)} %get-tuple-element.80), channel_id=1, source_target_pairs={{0,4},{1,5},{2,6},{3,7},{4,0},{5,1},{6,2},{7,3},{8,12},{9,13},{10,... | collective-permute-start | bytes 589832 | tf_op jit(solution)/shard_map/ppermute | solution.py:103
  31.4 0.7 collective-permute-done.11.refs_2_
  32.1 2.3 %collective-permute-start.12 = (bf16[1,512,128]{2,1,0:T(8,128)(2,1)S(1)}, bf16[1,512,128]{2,1,0:T(8,128)(2,1)S(1)}, u32[]{:S(2)}, u32[]{:S(2)}) collective-permute-start(bf16[1,512,128]{2,1,0:T(8,128)(2,1)S(1)} %get-tuple-element.83), channel_id=1, source_target_pairs={{0,2},{1,3},{2,0},{3,1},{4,6},{5,7},{6,4},{7,5},{8,10},{9,11},{10,... | collective-permute-start | bytes 393224 | tf_op jit(solution)/shard_map/ppermute | solution.py:103
  34.4 0.1 collective-permute-start.13
  34.5 0.5 collective-permute-done.6
  35.0 4.1 %collective-permute-start.7 = (bf16[2,128,2048]{2,1,0:T(8,128)(2,1)S(1)}, bf16[2,128,2048]{2,1,0:T(8,128)(2,1)S(1)}, u32[]{:S(2)}, u32[]{:S(2)}) collective-permute-start(bf16[2,128,2048]{2,1,0:T(8,128)(2,1)S(1)} %get-tuple-element.47), channel_id=1, source_target_pairs={{0,1},{1,0},{2,3},{3,2},{4,5},{5,4},{6,7},{7,6},{8,9},{9,8},{10,11... | collective-permute-start | bytes 3145736 | tf_op jit(solution)/shard_map/ppermute | solution.py:103
  39.1 0.1 collective-permute-done.14
  39.2 0.1 maximum_maximum_fusion.refs_5_
  39.4 0.0 collective-permute-done.12.refs_3_
  39.4 1.0 collective-permute-done.13.refs_4_
  40.4 0.4 product_mate.1
  40.7 1.4 %collective-permute-start.16 = (bf16[1,128,1536]{2,1,0:T(8,128)(2,1)S(1)}, bf16[1,128,1536]{2,1,0:T(8,128)(2,1)S(1)}, u32[]{:S(2)}, u32[]{:S(2)}) collective-permute-start(bf16[1,128,1536]{2,1,0:T(8,128)(2,1)S(1)} %product_mate.1), channel_id=1, source_target_pairs={{0,1},{1,0},{2,3},{3,2},{4,5},{5,4},{6,7},{7,6},{8,9},{9,8},{10,11... | collective-permute-start | bytes 1179656 | tf_op jit(solution)/shard_map/ppermute | solution.py:103
  42.1 0.6 product_near.1
  42.7 0.1 collective-permute-start.20
  42.8 0.4 product_first.1.refs_0_
  43.2 0.3 collective-permute-done.16.refs_1_
  43.5 0.1 block_sum.3
  43.6 1.4 %collective-permute-start.18 = (bf16[128,1536]{1,0:T(8,128)(2,1)S(1)}, bf16[128,1536]{1,0:T(8,128)(2,1)S(1)}, u32[]{:S(2)}, u32[]{:S(2)}) collective-permute-start(bf16[128,1536]{1,0:T(8,128)(2,1)S(1)} %block_sum.3), channel_id=1, source_target_pairs={{0,8},{8,0},{16,24},{24,16},{1,9},{9,1},{17,25},{25,17},{2,10},{10... | collective-permute-start | bytes 1179656 | tf_op jit(solution)/shard_map/ppermute | solution.py:103
  44.9 0.6 product_middle.1
  45.5 0.7 collective-permute-start.17
  46.2 0.6 product_own.1
  46.8 0.1 collective-permute-start.15
  46.9 0.0 collective-permute-done.20.refs_1_
  46.9 0.1 block_sum.5
  47.0 0.5 collective-permute-done.17.refs_1_
  47.6 6.4 %collective-permute-done.18.refs_2_ = bf16[128,1536]{1,0:T(8,128)(2,1)S(1)} collective-permute-done((bf16[128,1536]{1,0:T(8,128)(2,1)S(1)}, bf16[128,1536]{1,0:T(8,128)(2,1)S(1)}, u32[]{:S(2)}, u32[]{:S(2)}) %collective-permute-start.18) | collective-permute-done | bytes 393248 | tf_op jit(solution)/shard_map/ppermute | solution.py:103
  54.0 0.1 block_sum.4
  54.1 2.4 %collective-permute-start.19 = (bf16[128,1536]{1,0:T(8,128)(2,1)S(1)}, bf16[128,1536]{1,0:T(8,128)(2,1)S(1)}, u32[]{:S(2)}, u32[]{:S(2)}) collective-permute-start(bf16[128,1536]{1,0:T(8,128)(2,1)S(1)} %block_sum.4), channel_id=1, source_target_pairs={{0,16},{8,24},{16,0},{24,8},{1,17},{9,25},{17,1},{25,9},{2,18},{10... | collective-permute-start | bytes 1179656 | tf_op jit(solution)/shard_map/ppermute | solution.py:103
  56.5 1.3 %collective-permute-start.21 = (bf16[128,1536]{1,0:T(8,128)(2,1)S(1)}, bf16[128,1536]{1,0:T(8,128)(2,1)S(1)}, u32[]{:S(2)}, u32[]{:S(2)}) collective-permute-start(bf16[128,1536]{1,0:T(8,128)(2,1)S(1)} %block_sum.5), channel_id=1, source_target_pairs={{0,8},{8,0},{16,24},{24,16},{1,9},{9,1},{17,25},{25,17},{2,10},{10... | collective-permute-start | bytes 1179656 | tf_op jit(solution)/shard_map/ppermute | solution.py:103
  57.7 1.3 %collective-permute-start.8 = (bf16[128,2048]{1,0:T(8,128)(2,1)S(1)}, bf16[128,2048]{1,0:T(8,128)(2,1)S(1)}, u32[]{:S(2)}, u32[]{:S(2)}) collective-permute-start(bf16[128,2048]{1,0:T(8,128)(2,1)S(1)} %get-tuple-element.49), channel_id=1, source_target_pairs={{3,4},{5,6},{2,1},{4,3},{11,12},{13,14},{10,9},{12,11},{19,20},{21... | collective-permute-start | bytes 1572872 | tf_op jit(solution)/shard_map/ppermute | solution.py:457
  59.0 1.5 %collective-permute-start.9 = (bf16[128,2048]{1,0:T(8,128)(2,1)S(1)}, bf16[128,2048]{1,0:T(8,128)(2,1)S(1)}, u32[]{:S(2)}, u32[]{:S(2)}) collective-permute-start(bf16[128,2048]{1,0:T(8,128)(2,1)S(1)} %get-tuple-element.51), channel_id=1, source_target_pairs={{3,4},{5,6},{2,1},{4,3},{11,12},{13,14},{10,9},{12,11},{19,20},{21... | collective-permute-start | bytes 1572872 | tf_op jit(solution)/shard_map/ppermute | solution.py:458
  60.5 12.9 %collective-permute-done.19.refs_1_ = bf16[128,1536]{1,0:T(8,128)(2,1)S(1)} collective-permute-done((bf16[128,1536]{1,0:T(8,128)(2,1)S(1)}, bf16[128,1536]{1,0:T(8,128)(2,1)S(1)}, u32[]{:S(2)}, u32[]{:S(2)}) %collective-permute-start.19) | collective-permute-done | bytes 393248 | tf_op jit(solution)/shard_map/ppermute | solution.py:103
  73.5 0.0 collective-permute-done.21.refs_2_
  73.5 0.7 gradient_sum.1
  74.2 1.8 %collective-permute-start.22 = (f32[128,128]{1,0:T(8,128)S(1)}, f32[128,128]{1,0:T(8,128)S(1)}, u32[]{:S(2)}, u32[]{:S(2)}) collective-permute-start(f32[128,128]{1,0:T(8,128)S(1)} %get-tuple-element.65.gram), channel_id=1, source_target_pairs={{0,2},{1,3},{2,0},{3,1},{4,6},{5,7},{6,4},{7,5},{8,10},{9,11},{10,... | collective-permute-start | bytes 196616 | tf_op jit(solution)/shard_map/ppermute | solution.py:103
  75.9 2.1 %collective-permute-start.23 = (bf16[128,384]{1,0:T(8,128)(2,1)S(1)}, bf16[128,384]{1,0:T(8,128)(2,1)S(1)}, u32[]{:S(2)}, u32[]{:S(2)}) collective-permute-start(bf16[128,384]{1,0:T(8,128)(2,1)S(1)} %get-tuple-element.68), channel_id=1, source_target_pairs={{0,1},{1,0},{2,3},{3,2},{4,5},{5,4},{6,7},{7,6},{8,9},{9,8},{10,11... | collective-permute-start | bytes 294920 | tf_op jit(solution)/shard_map/ppermute | solution.py:103
  78.0 0.0 collective-permute-start.24
  78.0 9.4 %collective-permute-done.22.gram_other = f32[128,128]{1,0:T(8,128)S(1)} collective-permute-done((f32[128,128]{1,0:T(8,128)S(1)}, f32[128,128]{1,0:T(8,128)S(1)}, u32[]{:S(2)}, u32[]{:S(2)}) %collective-permute-start.22) | collective-permute-done | bytes 65568 | tf_op jit(solution)/shard_map/ppermute | solution.py:103
  87.5 2.4 %newton_schulz.1.refs_0_ = f32[128,128]{1,0:T(8,128)S(1)} custom-call(f32[128,128]{1,0:T(8,128)S(1)} %get-tuple-element.65.gram, f32[128,128]{1,0:T(8,128)S(1)} %collective-permute-done.22.gram_other), custom_call_target="tpu_custom_call" | custom-call | flops 301989888 | bytes 1572864 | tf_op jit(solution)/shard_map/newton_schulz/pallas_call | solution.py:502
  89.9 0.0 collective-permute-done.23.refs_3_
  89.9 1.6 %collective-permute-done.25.refs_7_ = bf16[128,384]{1,0:T(8,128)(2,1)S(1)} collective-permute-done((bf16[128,384]{1,0:T(8,128)(2,1)S(1)}, bf16[128,384]{1,0:T(8,128)(2,1)S(1)}, u32[]{:S(2)}, u32[]{:S(2)}) %collective-permute-start.25) | collective-permute-done | bytes 98336 | tf_op jit(solution)/shard_map/ppermute | solution.py:103
  91.5 0.8 collective-permute-start.27
  92.4 1.3 %collective-permute-start.28 = (f32[128,128]{1,0:T(8,128)S(1)}, f32[128,128]{1,0:T(8,128)S(1)}, u32[]{:S(2)}, u32[]{:S(2)}) collective-permute-start(f32[128,128]{1,0:T(8,128)S(1)} %newton_schulz.1.refs_0_), channel_id=1, source_target_pairs={{0,5},{1,4},{2,7},{3,6},{4,1},{5,0},{6,3},{7,2},{8,13},{9,12},{10,... | collective-permute-start | bytes 196616 | tf_op jit(solution)/shard_map/ppermute | solution.py:103
  93.7 1.8 %key_value_sum.1 = (bf16[128,2048]{1,0:T(8,128)(2,1)}, bf16[128,2048]{1,0:T(8,128)(2,1)}) custom-call(s32[1,8]{1,0:T(1,128)S(1)} %copy-done.4, f32[128,2048]{1,0:T(8,128)S(1)} %get-tuple-element.42.dko, f32[128,2048]{1,0:T(8,128)S(1)} %get-tuple-element.43.dvo, bf16[2,128,2048]{2,1,0:T(8,128)(2,1)S(1)} %collective-permute-done.7.mate, ...), custom_call_target="tpu_custom_call" | custom-call | flops 1572864 | bytes 5242880 | tf_op jit(solution)/shard_map/key_value_sum/pallas_call | solution.py:467
  95.5 1.5 %collective-permute-done.28.refs_6_ = f32[128,128]{1,0:T(8,128)S(1)} collective-permute-done((f32[128,128]{1,0:T(8,128)S(1)}, f32[128,128]{1,0:T(8,128)S(1)}, u32[]{:S(2)}, u32[]{:S(2)}) %collective-permute-start.28) | collective-permute-done | bytes 65568 | tf_op jit(solution)/shard_map/ppermute | solution.py:103
  97.0 1.4 %update_rows.1 = f32[512,384]{1,0:T(8,128)} custom-call(f32[128,128]{1,0:T(8,128)S(1)} %newton_schulz.1.refs_0_, f32[128,384]{1,0:T(8,128)S(1)} %get-tuple-element.67.refs_1_, f32[128,128]{1,0:T(8,128)S(1)} %collective-permute-done.26.refs_2_, bf16[128,384]{1,0:T(8,128)(2,1)S(1)} %collective-permute-done.23.refs_3_, ...), custom_call_target="tpu_custom_call" | custom-call | flops 1 | bytes 1572864 | tf_op jit(solution)/shard_map/update_rows/pallas_call | solution.py:515
  (25 shorter events, 0.2 us)
Async XLA Ops:
  0.6 7.5 %copy-start.1 = (bf16[1,1,128,2048]{3,2,1,0:T(8,128)(2,1)S(1)}, bf16[1,1,128,2048]{3,2,1,0:T(8,128)(2,1)}, u32[]{:S(2)}) copy-start(bf16[1,1,128,2048]{3,2,1,0:T(8,128)(2,1)} %param.7) | copy-start | bytes 1572868
  0.6 7.5 %copy-start.2 = (bf16[1,1,128,2048]{3,2,1,0:T(8,128)(2,1)S(1)}, bf16[1,1,128,2048]{3,2,1,0:T(8,128)(2,1)}, u32[]{:S(2)}) copy-start(bf16[1,1,128,2048]{3,2,1,0:T(8,128)(2,1)} %param.8) | copy-start | bytes 1572868
  0.7 11.1 %collective-permute-start.2 = (bf16[128,2048]{1,0:T(8,128)(2,1)}, bf16[128,2048]{1,0:T(8,128)(2,1)S(1)}, u32[]{:S(2)}, u32[]{:S(2)}) collective-permute-start(bf16[128,2048]{1,0:T(8,128)(2,1)} %bitcast.25), channel_id=1, source_target_pairs={{1,2},{3,4},{4,3},{6,5},{9,10},{11,12},{12,11},{14,13},{17,18},{19... | collective-permute-start | bytes 1572872 | tf_op jit(solution)/shard_map/ppermute | solution.py:309
  5.3 12.0 %collective-permute-start.3 = (bf16[128,2048]{1,0:T(8,128)(2,1)}, bf16[128,2048]{1,0:T(8,128)(2,1)S(1)}, u32[]{:S(2)}, u32[]{:S(2)}) collective-permute-start(bf16[128,2048]{1,0:T(8,128)(2,1)} %bitcast.29), channel_id=1, source_target_pairs={{1,2},{3,4},{4,3},{6,5},{9,10},{11,12},{12,11},{14,13},{17,18},{19... | collective-permute-start | bytes 1572872 | tf_op jit(solution)/shard_map/ppermute | solution.py:310
  6.7 13.5 %copy-start = (bf16[1,1,128,2048]{3,2,1,0:T(8,128)(2,1)S(1)}, bf16[1,1,128,2048]{3,2,1,0:T(8,128)(2,1)}, u32[]{:S(2)}) copy-start(bf16[1,1,128,2048]{3,2,1,0:T(8,128)(2,1)} %param.6) | copy-start | bytes 1572868
  6.7 13.5 %copy-start.4 = (s32[1,8]{1,0:T(1,128)S(1)}, s32[1,8]{1,0:T(1,128)}, u32[]{:S(2)}) copy-start(s32[1,8]{1,0:T(1,128)} %near_ref.5) | copy-start | bytes 100
  8.1 12.1 %collective-permute-start = (bf16[128,2048]{1,0:T(8,128)(2,1)S(1)}, bf16[128,2048]{1,0:T(8,128)(2,1)S(1)}, u32[]{:S(2)}, u32[]{:S(2)}) collective-permute-start(bf16[128,2048]{1,0:T(8,128)(2,1)S(1)} %bitcast.26), channel_id=1, source_target_pairs={{0,1},{1,0},{2,3},{3,2},{4,5},{5,4},{6,7},{7,6},{8,9},{9,8},{10,11... | collective-permute-start | bytes 1572872 | tf_op jit(solution)/shard_map/ppermute | solution.py:103
  8.2 12.0 %collective-permute-start.1 = (bf16[128,2048]{1,0:T(8,128)(2,1)S(1)}, bf16[128,2048]{1,0:T(8,128)(2,1)S(1)}, u32[]{:S(2)}, u32[]{:S(2)}) collective-permute-start(bf16[128,2048]{1,0:T(8,128)(2,1)S(1)} %bitcast.30), channel_id=1, source_target_pairs={{0,1},{1,0},{2,3},{3,2},{4,5},{5,4},{6,7},{7,6},{8,9},{9,8},{10,11... | collective-permute-start | bytes 1572872 | tf_op jit(solution)/shard_map/ppermute | solution.py:103
  8.7 18.6 %collective-permute-start.4 = (bf16[128,1536]{1,0:T(8,128)(2,1)S(1)}, bf16[128,1536]{1,0:T(8,128)(2,1)S(1)}, u32[]{:S(2)}, u32[]{:S(2)}) collective-permute-start(bf16[128,1536]{1,0:T(8,128)(2,1)S(1)} %get-tuple-element.79), channel_id=1, source_target_pairs={{0,4},{1,5},{2,6},{3,7},{4,0},{5,1},{6,2},{7,3},{8,12},{9,13},{10,... | collective-permute-start | bytes 1179656 | tf_op jit(solution)/shard_map/ppermute | solution.py:103
  17.3 12.5 %collective-permute-start.5 = (bf16[128,1536]{1,0:T(8,128)(2,1)S(1)}, bf16[128,1536]{1,0:T(8,128)(2,1)S(1)}, u32[]{:S(2)}, u32[]{:S(2)}) collective-permute-start(bf16[128,1536]{1,0:T(8,128)(2,1)S(1)} %pad_maximum_fusion.1), channel_id=1, source_target_pairs={{0,2},{1,3},{2,0},{3,1},{4,6},{5,7},{6,4},{7,5},{8,10},{9,11},{10,... | collective-permute-start | bytes 1179656 | tf_op jit(solution)/shard_map/ppermute | solution.py:103
  20.2 3.2 %copy-start.3 = (bf16[1,1,128,2048]{3,2,1,0:T(8,128)(2,1)S(1)}, bf16[1,1,128,2048]{3,2,1,0:T(8,128)(2,1)}, u32[]{:S(2)}) copy-start(bf16[1,1,128,2048]{3,2,1,0:T(8,128)(2,1)} %param.9) | copy-start | bytes 1572868
  22.5 9.6 %collective-permute-start.11 = (bf16[2,512,128]{2,1,0:T(8,128)(2,1)S(1)}, bf16[2,512,128]{2,1,0:T(8,128)(2,1)S(1)}, u32[]{:S(2)}, u32[]{:S(2)}) collective-permute-start(bf16[2,512,128]{2,1,0:T(8,128)(2,1)S(1)} %get-tuple-element.76), channel_id=1, source_target_pairs={{0,4},{1,5},{2,6},{3,7},{4,0},{5,1},{6,2},{7,3},{8,12},{9,13},{10,... | collective-permute-start | bytes 786440 | tf_op jit(solution)/shard_map/ppermute | solution.py:103
  22.6 16.7 %collective-permute-start.10 = (bf16[2,512,128]{2,1,0:T(8,128)(2,1)S(1)}, bf16[2,512,128]{2,1,0:T(8,128)(2,1)S(1)}, u32[]{:S(2)}, u32[]{:S(2)}) collective-permute-start(bf16[2,512,128]{2,1,0:T(8,128)(2,1)S(1)} %get-tuple-element.58.refs_0_), channel_id=1, source_target_pairs={{0,2},{1,3},{2,0},{3,1},{4,6},{5,7},{6,4},{7,5},{8,10},{9,11},{10,... | collective-permute-start | bytes 786440 | tf_op jit(solution)/shard_map/ppermute | solution.py:103
  29.9 5.2 %collective-permute-start.6 = (bf16[1,128,768]{2,1,0:T(8,128)(2,1)S(1)}, bf16[1,128,768]{2,1,0:T(8,128)(2,1)S(1)}, u32[]{:S(2)}, u32[]{:S(2)}) collective-permute-start(bf16[1,128,768]{2,1,0:T(8,128)(2,1)S(1)} %get-tuple-element.81), channel_id=1, source_target_pairs={{0,4},{1,5},{2,6},{3,7},{4,0},{5,1},{6,2},{7,3},{8,12},{9,13},{10,... | collective-permute-start | bytes 589832 | tf_op jit(solution)/shard_map/ppermute | solution.py:103
  29.9 9.3 %collective-permute-start.14 = (bf16[1,128,768]{2,1,0:T(8,128)(2,1)S(1)}, bf16[1,128,768]{2,1,0:T(8,128)(2,1)S(1)}, u32[]{:S(2)}, u32[]{:S(2)}) collective-permute-start(bf16[1,128,768]{2,1,0:T(8,128)(2,1)S(1)} %get-tuple-element.80), channel_id=1, source_target_pairs={{0,4},{1,5},{2,6},{3,7},{4,0},{5,1},{6,2},{7,3},{8,12},{9,13},{10,... | collective-permute-start | bytes 589832 | tf_op jit(solution)/shard_map/ppermute | solution.py:103
  32.1 7.2 %collective-permute-start.12 = (bf16[1,512,128]{2,1,0:T(8,128)(2,1)S(1)}, bf16[1,512,128]{2,1,0:T(8,128)(2,1)S(1)}, u32[]{:S(2)}, u32[]{:S(2)}) collective-permute-start(bf16[1,512,128]{2,1,0:T(8,128)(2,1)S(1)} %get-tuple-element.83), channel_id=1, source_target_pairs={{0,2},{1,3},{2,0},{3,1},{4,6},{5,7},{6,4},{7,5},{8,10},{9,11},{10,... | collective-permute-start | bytes 393224 | tf_op jit(solution)/shard_map/ppermute | solution.py:103
  34.4 5.9 %collective-permute-start.13 = (bf16[1,512,128]{2,1,0:T(8,128)(2,1)S(1)}, bf16[1,512,128]{2,1,0:T(8,128)(2,1)S(1)}, u32[]{:S(2)}, u32[]{:S(2)}) collective-permute-start(bf16[1,512,128]{2,1,0:T(8,128)(2,1)S(1)} %get-tuple-element.82), channel_id=1, source_target_pairs={{0,2},{1,3},{2,0},{3,1},{4,6},{5,7},{6,4},{7,5},{8,10},{9,11},{10,... | collective-permute-start | bytes 393224 | tf_op jit(solution)/shard_map/ppermute | solution.py:103
  35.0 21.4 %collective-permute-start.7 = (bf16[2,128,2048]{2,1,0:T(8,128)(2,1)S(1)}, bf16[2,128,2048]{2,1,0:T(8,128)(2,1)S(1)}, u32[]{:S(2)}, u32[]{:S(2)}) collective-permute-start(bf16[2,128,2048]{2,1,0:T(8,128)(2,1)S(1)} %get-tuple-element.47), channel_id=1, source_target_pairs={{0,1},{1,0},{2,3},{3,2},{4,5},{5,4},{6,7},{7,6},{8,9},{9,8},{10,11... | collective-permute-start | bytes 3145736 | tf_op jit(solution)/shard_map/ppermute | solution.py:103
  40.7 2.8 %collective-permute-start.16 = (bf16[1,128,1536]{2,1,0:T(8,128)(2,1)S(1)}, bf16[1,128,1536]{2,1,0:T(8,128)(2,1)S(1)}, u32[]{:S(2)}, u32[]{:S(2)}) collective-permute-start(bf16[1,128,1536]{2,1,0:T(8,128)(2,1)S(1)} %product_mate.1), channel_id=1, source_target_pairs={{0,1},{1,0},{2,3},{3,2},{4,5},{5,4},{6,7},{7,6},{8,9},{9,8},{10,11... | collective-permute-start | bytes 1179656 | tf_op jit(solution)/shard_map/ppermute | solution.py:103
  42.7 4.2 %collective-permute-start.20 = (bf16[1,128,1536]{2,1,0:T(8,128)(2,1)S(1)}, bf16[1,128,1536]{2,1,0:T(8,128)(2,1)S(1)}, u32[]{:S(2)}, u32[]{:S(2)}) collective-permute-start(bf16[1,128,1536]{2,1,0:T(8,128)(2,1)S(1)} %get-tuple-element.63), channel_id=1, source_target_pairs={{0,1},{1,0},{2,3},{3,2},{4,5},{5,4},{6,7},{7,6},{8,9},{9,8},{10,11... | collective-permute-start | bytes 1179656 | tf_op jit(solution)/shard_map/ppermute | solution.py:103
  43.6 10.4 %collective-permute-start.18 = (bf16[128,1536]{1,0:T(8,128)(2,1)S(1)}, bf16[128,1536]{1,0:T(8,128)(2,1)S(1)}, u32[]{:S(2)}, u32[]{:S(2)}) collective-permute-start(bf16[128,1536]{1,0:T(8,128)(2,1)S(1)} %block_sum.3), channel_id=1, source_target_pairs={{0,8},{8,0},{16,24},{24,16},{1,9},{9,1},{17,25},{25,17},{2,10},{10... | collective-permute-start | bytes 1179656 | tf_op jit(solution)/shard_map/ppermute | solution.py:103
  45.5 2.1 %collective-permute-start.17 = (bf16[1,128,1536]{2,1,0:T(8,128)(2,1)S(1)}, bf16[1,128,1536]{2,1,0:T(8,128)(2,1)S(1)}, u32[]{:S(2)}, u32[]{:S(2)}) collective-permute-start(bf16[1,128,1536]{2,1,0:T(8,128)(2,1)S(1)} %get-tuple-element.61), channel_id=1, source_target_pairs={{0,1},{1,0},{2,3},{3,2},{4,5},{5,4},{6,7},{7,6},{8,9},{9,8},{10,11... | collective-permute-start | bytes 1179656 | tf_op jit(solution)/shard_map/ppermute | solution.py:103
  46.8 9.6 %collective-permute-start.15 = (bf16[1,128,1536]{2,1,0:T(8,128)(2,1)S(1)}, bf16[1,128,1536]{2,1,0:T(8,128)(2,1)S(1)}, u32[]{:S(2)}, u32[]{:S(2)}) collective-permute-start(bf16[1,128,1536]{2,1,0:T(8,128)(2,1)S(1)} %get-tuple-element.56), channel_id=1, source_target_pairs={{0,1},{1,0},{2,3},{3,2},{4,5},{5,4},{6,7},{7,6},{8,9},{9,8},{10,11... | collective-permute-start | bytes 1179656 | tf_op jit(solution)/shard_map/ppermute | solution.py:103
  54.1 19.4 %collective-permute-start.19 = (bf16[128,1536]{1,0:T(8,128)(2,1)S(1)}, bf16[128,1536]{1,0:T(8,128)(2,1)S(1)}, u32[]{:S(2)}, u32[]{:S(2)}) collective-permute-start(bf16[128,1536]{1,0:T(8,128)(2,1)S(1)} %block_sum.4), channel_id=1, source_target_pairs={{0,16},{8,24},{16,0},{24,8},{1,17},{9,25},{17,1},{25,9},{2,18},{10... | collective-permute-start | bytes 1179656 | tf_op jit(solution)/shard_map/ppermute | solution.py:103
  56.5 17.0 %collective-permute-start.21 = (bf16[128,1536]{1,0:T(8,128)(2,1)S(1)}, bf16[128,1536]{1,0:T(8,128)(2,1)S(1)}, u32[]{:S(2)}, u32[]{:S(2)}) collective-permute-start(bf16[128,1536]{1,0:T(8,128)(2,1)S(1)} %block_sum.5), channel_id=1, source_target_pairs={{0,8},{8,0},{16,24},{24,16},{1,9},{9,1},{17,25},{25,17},{2,10},{10... | collective-permute-start | bytes 1179656 | tf_op jit(solution)/shard_map/ppermute | solution.py:103
  57.7 35.9 %collective-permute-start.8 = (bf16[128,2048]{1,0:T(8,128)(2,1)S(1)}, bf16[128,2048]{1,0:T(8,128)(2,1)S(1)}, u32[]{:S(2)}, u32[]{:S(2)}) collective-permute-start(bf16[128,2048]{1,0:T(8,128)(2,1)S(1)} %get-tuple-element.49), channel_id=1, source_target_pairs={{3,4},{5,6},{2,1},{4,3},{11,12},{13,14},{10,9},{12,11},{19,20},{21... | collective-permute-start | bytes 1572872 | tf_op jit(solution)/shard_map/ppermute | solution.py:457
  59.0 34.6 %collective-permute-start.9 = (bf16[128,2048]{1,0:T(8,128)(2,1)S(1)}, bf16[128,2048]{1,0:T(8,128)(2,1)S(1)}, u32[]{:S(2)}, u32[]{:S(2)}) collective-permute-start(bf16[128,2048]{1,0:T(8,128)(2,1)S(1)} %get-tuple-element.51), channel_id=1, source_target_pairs={{3,4},{5,6},{2,1},{4,3},{11,12},{13,14},{10,9},{12,11},{19,20},{21... | collective-permute-start | bytes 1572872 | tf_op jit(solution)/shard_map/ppermute | solution.py:458
  74.2 13.3 %collective-permute-start.22 = (f32[128,128]{1,0:T(8,128)S(1)}, f32[128,128]{1,0:T(8,128)S(1)}, u32[]{:S(2)}, u32[]{:S(2)}) collective-permute-start(f32[128,128]{1,0:T(8,128)S(1)} %get-tuple-element.65.gram), channel_id=1, source_target_pairs={{0,2},{1,3},{2,0},{3,1},{4,6},{5,7},{6,4},{7,5},{8,10},{9,11},{10,... | collective-permute-start | bytes 196616 | tf_op jit(solution)/shard_map/ppermute | solution.py:103
  75.9 14.0 %collective-permute-start.23 = (bf16[128,384]{1,0:T(8,128)(2,1)S(1)}, bf16[128,384]{1,0:T(8,128)(2,1)S(1)}, u32[]{:S(2)}, u32[]{:S(2)}) collective-permute-start(bf16[128,384]{1,0:T(8,128)(2,1)S(1)} %get-tuple-element.68), channel_id=1, source_target_pairs={{0,1},{1,0},{2,3},{3,2},{4,5},{5,4},{6,7},{7,6},{8,9},{9,8},{10,11... | collective-permute-start | bytes 294920 | tf_op jit(solution)/shard_map/ppermute | solution.py:103
  78.0 11.9 %collective-permute-start.24 = (bf16[128,384]{1,0:T(8,128)(2,1)S(1)}, bf16[128,384]{1,0:T(8,128)(2,1)S(1)}, u32[]{:S(2)}, u32[]{:S(2)}) collective-permute-start(bf16[128,384]{1,0:T(8,128)(2,1)S(1)} %get-tuple-element.69), channel_id=1, source_target_pairs={{0,4},{1,5},{2,6},{3,7},{4,0},{5,1},{6,2},{7,3},{8,12},{9,13},{10,... | collective-permute-start | bytes 294920 | tf_op jit(solution)/shard_map/ppermute | solution.py:103
  87.5 4.0 %collective-permute-start.25 = (bf16[128,384]{1,0:T(8,128)(2,1)S(1)}, bf16[128,384]{1,0:T(8,128)(2,1)S(1)}, u32[]{:S(2)}, u32[]{:S(2)}) collective-permute-start(bf16[128,384]{1,0:T(8,128)(2,1)S(1)} %get-tuple-element.70), channel_id=1, source_target_pairs={{0,5},{1,4},{2,7},{3,6},{4,1},{5,0},{6,3},{7,2},{8,13},{9,12},{10,... | collective-permute-start | bytes 294920 | tf_op jit(solution)/shard_map/ppermute | solution.py:103
  91.5 4.0 %collective-permute-start.26 = (f32[128,128]{1,0:T(8,128)S(1)}, f32[128,128]{1,0:T(8,128)S(1)}, u32[]{:S(2)}, u32[]{:S(2)}) collective-permute-start(f32[128,128]{1,0:T(8,128)S(1)} %newton_schulz.1.refs_0_), channel_id=1, source_target_pairs={{0,1},{1,0},{2,3},{3,2},{4,5},{5,4},{6,7},{7,6},{8,9},{9,8},{10,11... | collective-permute-start | bytes 196616 | tf_op jit(solution)/shard_map/ppermute | solution.py:103
  91.5 4.0 %collective-permute-start.27 = (f32[128,128]{1,0:T(8,128)S(1)}, f32[128,128]{1,0:T(8,128)S(1)}, u32[]{:S(2)}, u32[]{:S(2)}) collective-permute-start(f32[128,128]{1,0:T(8,128)S(1)} %newton_schulz.1.refs_0_), channel_id=1, source_target_pairs={{0,4},{1,5},{2,6},{3,7},{4,0},{5,1},{6,2},{7,3},{8,12},{9,13},{10,... | collective-permute-start | bytes 196616 | tf_op jit(solution)/shard_map/ppermute | solution.py:103
  92.4 4.7 %collective-permute-start.28 = (f32[128,128]{1,0:T(8,128)S(1)}, f32[128,128]{1,0:T(8,128)S(1)}, u32[]{:S(2)}, u32[]{:S(2)}) collective-permute-start(f32[128,128]{1,0:T(8,128)S(1)} %newton_schulz.1.refs_0_), channel_id=1, source_target_pairs={{0,5},{1,4},{2,7},{3,6},{4,1},{5,0},{6,3},{7,2},{8,13},{9,12},{10,... | collective-permute-start | bytes 196616 | tf_op jit(solution)/shard_map/ppermute | solution.py:103

commit v20 on v19

--- a/solution.py
+++ b/solution.py
@@ -507,9 +507,9 @@
         compiler_params=params(),
         cost_estimate=cost(12 * HEAD_DIM * HEAD_DIM * mine_width, 8 * HEAD_DIM * mine_width),
         name="newton_schulz",
-    )(gram, gram_other)
+    )(after(gram, dk), gram_other)
     moved = [shift(blocks_out[j], "seq", plan.row_mask(j)) for j in range(1, per)]
-    operands = [after(p, dk), blocks_out[0]]
+    operands = [p, blocks_out[0]]
     for j in range(1, per):
         operands += [shift(after(p, *moved), "seq", plan.row_mask(j)), moved[j - 1]]
     update = pl.pallas_call(

time: 98.7 us -> 92.5 us (0.937)
  waiting for transfers between devices: 43.2 us -> 34.7 us
  starting transfers between devices: 37.2 us -> 39.3 us
    ppermute x25, waiting for transfers between devices: 37.5 us -> 29 us  [shift(): lax.ppermute(value, axis, [(i, i ^ mask) for i in range(lax.axis_size(axi...]
    ppermute x25, starting transfers between devices: 28.5 us -> 30.6 us  [shift(): lax.ppermute(value, axis, [(i, i ^ mask) for i in range(lax.axis_size(axi...]
  transfers between devices with their start and end apart: 29 -> 29, of which waited for: 14 -> 13; matrix products, arithmetic and copies ran while one was open for 2% -> 2% of each run, Pallas kernels for 14% -> 15%
where the time goes in v20:
time: 92.5 us; the launch traced here: 92 us
  starting transfers between devices  39.3 us (42%)
  waiting for transfers between devices  34.7 us (38%)
  Pallas kernels  15.4 us (17%)
  local copies, waits for them, and re-layouts  1.43 us (2%)
  between operations  0.95 us (1%)
    ppermute x25, starting transfers between devices, shift(): lax.ppermute(value, axis, [(i, i ^ mask) for i in range(lax.axis_size(axi...  30.6 us
    ppermute x25, waiting for transfers between devices, shift(): lax.ppermute(value, axis, [(i, i ^ mask) for i in range(lax.axis_size(axi...  29 us
    ppermute x1, waiting for transfers between devices, local(): value_next = lax.ppermute(value, 'seq', takes)  5.62 us
    ppermute x1, starting transfers between devices, local(): key_next = lax.ppermute(key, 'seq', takes)  4.67 us
    pallas_call x1, Pallas kernels, local(): pl.pallas_call(backward_kernel, out_shape=[struct((tile, width), bf16), s...  3.9 us
    pallas_call x5, Pallas kernels, product(): pl.pallas_call(functools.partial(product_kernel, counts, layers, cores),...  2.53 us
    pallas_call x1, Pallas kernels, local(): pl.pallas_call(functools.partial(polynomial_kernel, factor), out_shape=st...  2.42 us
    pallas_call x1, Pallas kernels, local(): pl.pallas_call(functools.partial(forward_kernel, plan), out_shape=struct(...  2.3 us
  transfers between devices with their start and end apart: 29, of which 13 were waited for; matrix products, arithmetic and copies ran while one was open for 2% of the time, Pallas kernels for 15%

profile of v20, /device:TPU:1, one launch (start us, length us, event | category | flops | bytes accessed | tf_op | source)
XLA Modules:
  0.0 92.0 jit_solution(4439690662721986856)
XLA Ops:
  0.7 4.7 %collective-permute-start.2 = (bf16[128,2048]{1,0:T(8,128)(2,1)}, bf16[128,2048]{1,0:T(8,128)(2,1)S(1)}, u32[]{:S(2)}, u32[]{:S(2)}) collective-permute-start(bf16[128,2048]{1,0:T(8,128)(2,1)} %bitcast.25), channel_id=1, source_target_pairs={{1,2},{3,4},{4,3},{6,5},{9,10},{11,12},{12,11},{14,13},{17,18},{19... | collective-permute-start | bytes 1572872 | tf_op jit(solution)/shard_map/ppermute | solution.py:309
  5.3 1.3 %collective-permute-start.3 = (bf16[128,2048]{1,0:T(8,128)(2,1)}, bf16[128,2048]{1,0:T(8,128)(2,1)S(1)}, u32[]{:S(2)}, u32[]{:S(2)}) collective-permute-start(bf16[128,2048]{1,0:T(8,128)(2,1)} %bitcast.29), channel_id=1, source_target_pairs={{1,2},{3,4},{4,3},{6,5},{9,10},{11,12},{12,11},{14,13},{17,18},{19... | collective-permute-start | bytes 1572872 | tf_op jit(solution)/shard_map/ppermute | solution.py:310
  6.7 1.3 %dynamic-slice_bitcast_fusion.1 = (bf16[128,768]{1,0:T(8,128)(2,1)S(1)}, bf16[128,768]{1,0:T(8,128)(2,1)S(1)}, bf16[128,768]{1,0:T(8,128)(2,1)S(1)}, bf16[128,768]{1,0:T(8,128)(2,1)S(1)}) fusion(bf16[1,1,128,3072]{3,2,1,0:T(8,128)(2,1)} %param.10, s32[]{:T(128)S(6)} %select_n.14, s32[]{:T(128)S(6)} %select_n.13, s32[]{:T(128)S(6)} %select_n.12, s32[]{:T(128)S(6)} %select_n.15), kind=kLoop, calls=%fused_computation.6 | loop fusion | bytes 1572880 | tf_op jit(solution)/shard_map/dynamic_slice | solution.py:319
  8.0 0.1 fusion
  8.1 0.1 collective-permute-start
  8.2 0.5 collective-permute-start.1
  8.7 2.9 %collective-permute-start.4 = (bf16[128,1536]{1,0:T(8,128)(2,1)S(1)}, bf16[128,1536]{1,0:T(8,128)(2,1)S(1)}, u32[]{:S(2)}, u32[]{:S(2)}) collective-permute-start(bf16[128,1536]{1,0:T(8,128)(2,1)S(1)} %get-tuple-element.79), channel_id=1, source_target_pairs={{0,4},{1,5},{2,6},{3,7},{4,0},{5,1},{6,2},{7,3},{8,12},{9,13},{10,... | collective-permute-start | bytes 1179656 | tf_op jit(solution)/shard_map/ppermute | solution.py:103
  11.6 0.1 collective-permute-done.2.kn
  11.7 5.6 %collective-permute-done.3.vn = bf16[128,2048]{1,0:T(8,128)(2,1)S(1)} collective-permute-done((bf16[128,2048]{1,0:T(8,128)(2,1)}, bf16[128,2048]{1,0:T(8,128)(2,1)S(1)}, u32[]{:S(2)}, u32[]{:S(2)}) %collective-permute-start.3) | collective-permute-done | bytes 524320 | tf_op jit(solution)/shard_map/ppermute | solution.py:310
  17.3 2.8 %collective-permute-start.5 = (bf16[128,1536]{1,0:T(8,128)(2,1)S(1)}, bf16[128,1536]{1,0:T(8,128)(2,1)S(1)}, u32[]{:S(2)}, u32[]{:S(2)}) collective-permute-start(bf16[128,1536]{1,0:T(8,128)(2,1)S(1)} %pad_maximum_fusion.1), channel_id=1, source_target_pairs={{0,2},{1,3},{2,0},{3,1},{4,6},{5,7},{6,4},{7,5},{8,10},{9,11},{10,... | collective-permute-start | bytes 1179656 | tf_op jit(solution)/shard_map/ppermute | solution.py:103
  20.2 0.0 collective-permute-done.km
  20.2 0.0 collective-permute-done.1.vm
  20.2 0.0 copy-start.3
  20.2 2.3 %attention_forward.1 = bf16[2,2,512,128]{3,2,1,0:T(8,128)(2,1)S(1)} custom-call(s32[1,8]{1,0:T(1,128)S(1)} %copy-done.4, bf16[128,2048]{1,0:T(8,128)(2,1)S(1)} %bitcast.23, bf16[128,2048]{1,0:T(8,128)(2,1)S(1)} %bitcast.27, bf16[128,2048]{1,0:T(8,128)(2,1)S(1)} %bitcast.31, bf16[128,2048]{1,0:T(8,128)(2,1)S(1)} %collective-permute-done.km, ...), custom_call_target="tpu_custom_call" | custom-call | flops 268435456 | bytes 4194304 | tf_op jit(solution)/shard_map/attention_forward/pallas_call | solution.py:338
  22.5 0.1 collective-permute-start.11
  22.6 0.8 collective-permute-start.10
  23.4 3.9 %attention_backward.1 = (bf16[128,2048]{1,0:T(8,128)(2,1)}, f32[128,2048]{1,0:T(8,128)S(1)}, f32[128,2048]{1,0:T(8,128)S(1)}, bf16[128,2048]{1,0:T(8,128)(2,1)S(...) custom-call(s32[1,8]{1,0:T(1,128)S(1)} %copy-done.4, bf16[128,2048]{1,0:T(8,128)(2,1)S(1)} %bitcast.24, ...), custom_call_target="tpu_custom_call" | custom-call | flops 1 | bytes 1 | tf_op jit(solution)/shard_map/attention_backward/pallas_call | solution.py:364
  27.3 0.0 collective-permute-done.4
  27.3 2.5 %collective-permute-done.5 = bf16[128,1536]{1,0:T(8,128)(2,1)S(1)} collective-permute-done((bf16[128,1536]{1,0:T(8,128)(2,1)S(1)}, bf16[128,1536]{1,0:T(8,128)(2,1)S(1)}, u32[]{:S(2)}, u32[]{:S(2)}) %collective-permute-start.5) | collective-permute-done | bytes 393248 | tf_op jit(solution)/shard_map/ppermute | solution.py:103
  29.9 0.1 collective-permute-start.6
  29.9 1.5 %collective-permute-start.14 = (bf16[1,128,768]{2,1,0:T(8,128)(2,1)S(1)}, bf16[1,128,768]{2,1,0:T(8,128)(2,1)S(1)}, u32[]{:S(2)}, u32[]{:S(2)}) collective-permute-start(bf16[1,128,768]{2,1,0:T(8,128)(2,1)S(1)} %get-tuple-element.80), channel_id=1, source_target_pairs={{0,4},{1,5},{2,6},{3,7},{4,0},{5,1},{6,2},{7,3},{8,12},{9,13},{10,... | collective-permute-start | bytes 589832 | tf_op jit(solution)/shard_map/ppermute | solution.py:103
  31.4 0.7 collective-permute-done.11.refs_2_
  32.1 2.3 %collective-permute-start.12 = (bf16[1,512,128]{2,1,0:T(8,128)(2,1)S(1)}, bf16[1,512,128]{2,1,0:T(8,128)(2,1)S(1)}, u32[]{:S(2)}, u32[]{:S(2)}) collective-permute-start(bf16[1,512,128]{2,1,0:T(8,128)(2,1)S(1)} %get-tuple-element.83), channel_id=1, source_target_pairs={{0,2},{1,3},{2,0},{3,1},{4,6},{5,7},{6,4},{7,5},{8,10},{9,11},{10,... | collective-permute-start | bytes 393224 | tf_op jit(solution)/shard_map/ppermute | solution.py:103
  34.4 0.1 collective-permute-start.13
  34.5 0.5 collective-permute-done.6
  35.0 4.1 %collective-permute-start.7 = (bf16[2,128,2048]{2,1,0:T(8,128)(2,1)S(1)}, bf16[2,128,2048]{2,1,0:T(8,128)(2,1)S(1)}, u32[]{:S(2)}, u32[]{:S(2)}) collective-permute-start(bf16[2,128,2048]{2,1,0:T(8,128)(2,1)S(1)} %get-tuple-element.47), channel_id=1, source_target_pairs={{0,1},{1,0},{2,3},{3,2},{4,5},{5,4},{6,7},{7,6},{8,9},{9,8},{10,11... | collective-permute-start | bytes 3145736 | tf_op jit(solution)/shard_map/ppermute | solution.py:103
  39.1 0.1 collective-permute-done.14
  39.2 0.1 maximum_maximum_fusion.refs_5_
  39.4 0.0 collective-permute-done.10.refs_1_
  39.4 1.0 %collective-permute-done.13.refs_4_ = bf16[1,512,128]{2,1,0:T(8,128)(2,1)S(1)} collective-permute-done((bf16[1,512,128]{2,1,0:T(8,128)(2,1)S(1)}, bf16[1,512,128]{2,1,0:T(8,128)(2,1)S(1)}, u32[]{:S(2)}, u32[]{:S(2)}) %collective-permute-start.13) | collective-permute-done | bytes 131104 | tf_op jit(solution)/shard_map/ppermute | solution.py:103
  40.4 0.4 product_mate.1
  40.7 1.4 %collective-permute-start.16 = (bf16[1,128,1536]{2,1,0:T(8,128)(2,1)S(1)}, bf16[1,128,1536]{2,1,0:T(8,128)(2,1)S(1)}, u32[]{:S(2)}, u32[]{:S(2)}) collective-permute-start(bf16[1,128,1536]{2,1,0:T(8,128)(2,1)S(1)} %product_mate.1), channel_id=1, source_target_pairs={{0,1},{1,0},{2,3},{3,2},{4,5},{5,4},{6,7},{7,6},{8,9},{9,8},{10,11... | collective-permute-start | bytes 1179656 | tf_op jit(solution)/shard_map/ppermute | solution.py:103
  42.1 0.6 product_near.1
  42.7 0.1 collective-permute-start.20
  42.8 0.4 product_first.1.refs_0_
  43.2 0.3 collective-permute-done.16.refs_1_
  43.5 0.1 block_sum.3
  43.6 1.4 %collective-permute-start.18 = (bf16[128,1536]{1,0:T(8,128)(2,1)S(1)}, bf16[128,1536]{1,0:T(8,128)(2,1)S(1)}, u32[]{:S(2)}, u32[]{:S(2)}) collective-permute-start(bf16[128,1536]{1,0:T(8,128)(2,1)S(1)} %block_sum.3), channel_id=1, source_target_pairs={{0,8},{8,0},{16,24},{24,16},{1,9},{9,1},{17,25},{25,17},{2,10},{10... | collective-permute-start | bytes 1179656 | tf_op jit(solution)/shard_map/ppermute | solution.py:103
  44.9 0.6 product_middle.1
  45.5 0.7 collective-permute-start.17
  46.2 0.6 product_own.1
  46.8 0.1 collective-permute-start.15
  46.9 1.3 %collective-permute-start.8 = (bf16[128,2048]{1,0:T(8,128)(2,1)S(1)}, bf16[128,2048]{1,0:T(8,128)(2,1)S(1)}, u32[]{:S(2)}, u32[]{:S(2)}) collective-permute-start(bf16[128,2048]{1,0:T(8,128)(2,1)S(1)} %get-tuple-element.49), channel_id=1, source_target_pairs={{3,4},{5,6},{2,1},{4,3},{11,12},{13,14},{10,9},{12,11},{19,20},{21... | collective-permute-start | bytes 1572872 | tf_op jit(solution)/shard_map/ppermute | solution.py:457
  48.2 1.5 %collective-permute-start.9 = (bf16[128,2048]{1,0:T(8,128)(2,1)S(1)}, bf16[128,2048]{1,0:T(8,128)(2,1)S(1)}, u32[]{:S(2)}, u32[]{:S(2)}) collective-permute-start(bf16[128,2048]{1,0:T(8,128)(2,1)S(1)} %get-tuple-element.51), channel_id=1, source_target_pairs={{3,4},{5,6},{2,1},{4,3},{11,12},{13,14},{10,9},{12,11},{19,20},{21... | collective-permute-start | bytes 1572872 | tf_op jit(solution)/shard_map/ppermute | solution.py:458
  49.7 0.1 block_sum.5
  49.8 4.1 %collective-permute-done.18.refs_2_ = bf16[128,1536]{1,0:T(8,128)(2,1)S(1)} collective-permute-done((bf16[128,1536]{1,0:T(8,128)(2,1)S(1)}, bf16[128,1536]{1,0:T(8,128)(2,1)S(1)}, u32[]{:S(2)}, u32[]{:S(2)}) %collective-permute-start.18) | collective-permute-done | bytes 393248 | tf_op jit(solution)/shard_map/ppermute | solution.py:103
  54.0 0.1 block_sum.4
  54.1 2.4 %collective-permute-start.19 = (bf16[128,1536]{1,0:T(8,128)(2,1)S(1)}, bf16[128,1536]{1,0:T(8,128)(2,1)S(1)}, u32[]{:S(2)}, u32[]{:S(2)}) collective-permute-start(bf16[128,1536]{1,0:T(8,128)(2,1)S(1)} %block_sum.4), channel_id=1, source_target_pairs={{0,16},{8,24},{16,0},{24,8},{1,17},{9,25},{17,1},{25,9},{2,18},{10... | collective-permute-start | bytes 1179656 | tf_op jit(solution)/shard_map/ppermute | solution.py:103
  56.5 1.3 %collective-permute-start.21 = (bf16[128,1536]{1,0:T(8,128)(2,1)S(1)}, bf16[128,1536]{1,0:T(8,128)(2,1)S(1)}, u32[]{:S(2)}, u32[]{:S(2)}) collective-permute-start(bf16[128,1536]{1,0:T(8,128)(2,1)S(1)} %block_sum.5), channel_id=1, source_target_pairs={{0,8},{8,0},{16,24},{24,16},{1,9},{9,1},{17,25},{25,17},{2,10},{10... | collective-permute-start | bytes 1179656 | tf_op jit(solution)/shard_map/ppermute | solution.py:103
  57.7 15.7 %collective-permute-done.19.refs_1_ = bf16[128,1536]{1,0:T(8,128)(2,1)S(1)} collective-permute-done((bf16[128,1536]{1,0:T(8,128)(2,1)S(1)}, bf16[128,1536]{1,0:T(8,128)(2,1)S(1)}, u32[]{:S(2)}, u32[]{:S(2)}) %collective-permute-start.19) | collective-permute-done | bytes 393248 | tf_op jit(solution)/shard_map/ppermute | solution.py:103
  73.5 0.7 gradient_sum.1
  74.2 1.9 %collective-permute-start.23 = (bf16[128,384]{1,0:T(8,128)(2,1)S(1)}, bf16[128,384]{1,0:T(8,128)(2,1)S(1)}, u32[]{:S(2)}, u32[]{:S(2)}) collective-permute-start(bf16[128,384]{1,0:T(8,128)(2,1)S(1)} %get-tuple-element.68), channel_id=1, source_target_pairs={{0,1},{1,0},{2,3},{3,2},{4,5},{5,4},{6,7},{7,6},{8,9},{9,8},{10,11... | collective-permute-start | bytes 294920 | tf_op jit(solution)/shard_map/ppermute | solution.py:103
  76.1 1.7 %collective-permute-start.24 = (bf16[128,384]{1,0:T(8,128)(2,1)S(1)}, bf16[128,384]{1,0:T(8,128)(2,1)S(1)}, u32[]{:S(2)}, u32[]{:S(2)}) collective-permute-start(bf16[128,384]{1,0:T(8,128)(2,1)S(1)} %get-tuple-element.69), channel_id=1, source_target_pairs={{0,4},{1,5},{2,6},{3,7},{4,0},{5,1},{6,2},{7,3},{8,12},{9,13},{10,... | collective-permute-start | bytes 294920 | tf_op jit(solution)/shard_map/ppermute | solution.py:103
  77.8 0.0 collective-permute-start.25
  77.8 1.6 %collective-permute-start.22 = (f32[128,128]{1,0:T(8,128)S(1)}, f32[128,128]{1,0:T(8,128)S(1)}, u32[]{:S(2)}, u32[]{:S(2)}) collective-permute-start(f32[128,128]{1,0:T(8,128)S(1)} %get-tuple-element.66.gram), channel_id=1, source_target_pairs={{0,2},{1,3},{2,0},{3,1},{4,6},{5,7},{6,4},{7,5},{8,10},{9,11},{10,... | collective-permute-start | bytes 196616 | tf_op jit(solution)/shard_map/ppermute | solution.py:103
  79.5 1.8 %key_value_sum.1 = (bf16[128,2048]{1,0:T(8,128)(2,1)}, bf16[128,2048]{1,0:T(8,128)(2,1)}) custom-call(s32[1,8]{1,0:T(1,128)S(1)} %copy-done.4, f32[128,2048]{1,0:T(8,128)S(1)} %get-tuple-element.42.dko, f32[128,2048]{1,0:T(8,128)S(1)} %get-tuple-element.43.dvo, bf16[2,128,2048]{2,1,0:T(8,128)(2,1)S(1)} %collective-permute-done.7.mate, ...), custom_call_target="tpu_custom_call" | custom-call | flops 1572864 | bytes 5242880 | tf_op jit(solution)/shard_map/key_value_sum/pallas_call | solution.py:467
  81.3 0.2 collective-permute-done.22.gram_other
  81.5 2.4 %newton_schulz.1.refs_0_ = f32[128,128]{1,0:T(8,128)S(1)} custom-call(f32[128,128]{1,0:T(8,128)S(1)} %get-tuple-element.66.gram, f32[128,128]{1,0:T(8,128)S(1)} %collective-permute-done.22.gram_other), custom_call_target="tpu_custom_call" | custom-call | flops 301989888 | bytes 1572864 | tf_op jit(solution)/shard_map/newton_schulz/pallas_call | solution.py:502
  84.0 1.1 %collective-permute-start.26 = (f32[128,128]{1,0:T(8,128)S(1)}, f32[128,128]{1,0:T(8,128)S(1)}, u32[]{:S(2)}, u32[]{:S(2)}) collective-permute-start(f32[128,128]{1,0:T(8,128)S(1)} %newton_schulz.1.refs_0_), channel_id=1, source_target_pairs={{0,1},{1,0},{2,3},{3,2},{4,5},{5,4},{6,7},{7,6},{8,9},{9,8},{10,11... | collective-permute-start | bytes 196616 | tf_op jit(solution)/shard_map/ppermute | solution.py:103
  85.0 1.5 %collective-permute-start.27 = (f32[128,128]{1,0:T(8,128)S(1)}, f32[128,128]{1,0:T(8,128)S(1)}, u32[]{:S(2)}, u32[]{:S(2)}) collective-permute-start(f32[128,128]{1,0:T(8,128)S(1)} %newton_schulz.1.refs_0_), channel_id=1, source_target_pairs={{0,4},{1,5},{2,6},{3,7},{4,0},{5,1},{6,2},{7,3},{8,12},{9,13},{10,... | collective-permute-start | bytes 196616 | tf_op jit(solution)/shard_map/ppermute | solution.py:103
  86.5 0.2 collective-permute-start.28
  86.8 2.0 %collective-permute-done.27.refs_4_ = f32[128,128]{1,0:T(8,128)S(1)} collective-permute-done((f32[128,128]{1,0:T(8,128)S(1)}, f32[128,128]{1,0:T(8,128)S(1)}, u32[]{:S(2)}, u32[]{:S(2)}) %collective-permute-start.27) | collective-permute-done | bytes 65568 | tf_op jit(solution)/shard_map/ppermute | solution.py:103
  88.7 1.9 %collective-permute-done.28.refs_6_ = f32[128,128]{1,0:T(8,128)S(1)} collective-permute-done((f32[128,128]{1,0:T(8,128)S(1)}, f32[128,128]{1,0:T(8,128)S(1)}, u32[]{:S(2)}, u32[]{:S(2)}) %collective-permute-start.28) | collective-permute-done | bytes 65568 | tf_op jit(solution)/shard_map/ppermute | solution.py:103
  90.6 1.4 %update_rows.1 = f32[512,384]{1,0:T(8,128)} custom-call(f32[128,128]{1,0:T(8,128)S(1)} %newton_schulz.1.refs_0_, f32[128,384]{1,0:T(8,128)S(1)} %get-tuple-element.67.refs_1_, f32[128,128]{1,0:T(8,128)S(1)} %collective-permute-done.26.refs_2_, bf16[128,384]{1,0:T(8,128)(2,1)S(1)} %collective-permute-done.23.refs_3_, ...), custom_call_target="tpu_custom_call" | custom-call | flops 1 | bytes 1572864 | tf_op jit(solution)/shard_map/update_rows/pallas_call | solution.py:515
  (25 shorter events, 0.2 us)
Async XLA Ops:
  0.6 7.5 %copy-start.1 = (bf16[1,1,128,2048]{3,2,1,0:T(8,128)(2,1)S(1)}, bf16[1,1,128,2048]{3,2,1,0:T(8,128)(2,1)}, u32[]{:S(2)}) copy-start(bf16[1,1,128,2048]{3,2,1,0:T(8,128)(2,1)} %param.7) | copy-start | bytes 1572868
  0.6 7.5 %copy-start.2 = (bf16[1,1,128,2048]{3,2,1,0:T(8,128)(2,1)S(1)}, bf16[1,1,128,2048]{3,2,1,0:T(8,128)(2,1)}, u32[]{:S(2)}) copy-start(bf16[1,1,128,2048]{3,2,1,0:T(8,128)(2,1)} %param.8) | copy-start | bytes 1572868
  0.7 11.1 %collective-permute-start.2 = (bf16[128,2048]{1,0:T(8,128)(2,1)}, bf16[128,2048]{1,0:T(8,128)(2,1)S(1)}, u32[]{:S(2)}, u32[]{:S(2)}) collective-permute-start(bf16[128,2048]{1,0:T(8,128)(2,1)} %bitcast.25), channel_id=1, source_target_pairs={{1,2},{3,4},{4,3},{6,5},{9,10},{11,12},{12,11},{14,13},{17,18},{19... | collective-permute-start | bytes 1572872 | tf_op jit(solution)/shard_map/ppermute | solution.py:309
  5.3 12.0 %collective-permute-start.3 = (bf16[128,2048]{1,0:T(8,128)(2,1)}, bf16[128,2048]{1,0:T(8,128)(2,1)S(1)}, u32[]{:S(2)}, u32[]{:S(2)}) collective-permute-start(bf16[128,2048]{1,0:T(8,128)(2,1)} %bitcast.29), channel_id=1, source_target_pairs={{1,2},{3,4},{4,3},{6,5},{9,10},{11,12},{12,11},{14,13},{17,18},{19... | collective-permute-start | bytes 1572872 | tf_op jit(solution)/shard_map/ppermute | solution.py:310
  6.7 13.5 %copy-start = (bf16[1,1,128,2048]{3,2,1,0:T(8,128)(2,1)S(1)}, bf16[1,1,128,2048]{3,2,1,0:T(8,128)(2,1)}, u32[]{:S(2)}) copy-start(bf16[1,1,128,2048]{3,2,1,0:T(8,128)(2,1)} %param.6) | copy-start | bytes 1572868
  6.7 13.5 %copy-start.4 = (s32[1,8]{1,0:T(1,128)S(1)}, s32[1,8]{1,0:T(1,128)}, u32[]{:S(2)}) copy-start(s32[1,8]{1,0:T(1,128)} %near_ref.5) | copy-start | bytes 100
  8.1 12.1 %collective-permute-start = (bf16[128,2048]{1,0:T(8,128)(2,1)S(1)}, bf16[128,2048]{1,0:T(8,128)(2,1)S(1)}, u32[]{:S(2)}, u32[]{:S(2)}) collective-permute-start(bf16[128,2048]{1,0:T(8,128)(2,1)S(1)} %bitcast.26), channel_id=1, source_target_pairs={{0,1},{1,0},{2,3},{3,2},{4,5},{5,4},{6,7},{7,6},{8,9},{9,8},{10,11... | collective-permute-start | bytes 1572872 | tf_op jit(solution)/shard_map/ppermute | solution.py:103
  8.2 12.0 %collective-permute-start.1 = (bf16[128,2048]{1,0:T(8,128)(2,1)S(1)}, bf16[128,2048]{1,0:T(8,128)(2,1)S(1)}, u32[]{:S(2)}, u32[]{:S(2)}) collective-permute-start(bf16[128,2048]{1,0:T(8,128)(2,1)S(1)} %bitcast.30), channel_id=1, source_target_pairs={{0,1},{1,0},{2,3},{3,2},{4,5},{5,4},{6,7},{7,6},{8,9},{9,8},{10,11... | collective-permute-start | bytes 1572872 | tf_op jit(solution)/shard_map/ppermute | solution.py:103
  8.7 18.6 %collective-permute-start.4 = (bf16[128,1536]{1,0:T(8,128)(2,1)S(1)}, bf16[128,1536]{1,0:T(8,128)(2,1)S(1)}, u32[]{:S(2)}, u32[]{:S(2)}) collective-permute-start(bf16[128,1536]{1,0:T(8,128)(2,1)S(1)} %get-tuple-element.79), channel_id=1, source_target_pairs={{0,4},{1,5},{2,6},{3,7},{4,0},{5,1},{6,2},{7,3},{8,12},{9,13},{10,... | collective-permute-start | bytes 1179656 | tf_op jit(solution)/shard_map/ppermute | solution.py:103
  17.3 12.5 %collective-permute-start.5 = (bf16[128,1536]{1,0:T(8,128)(2,1)S(1)}, bf16[128,1536]{1,0:T(8,128)(2,1)S(1)}, u32[]{:S(2)}, u32[]{:S(2)}) collective-permute-start(bf16[128,1536]{1,0:T(8,128)(2,1)S(1)} %pad_maximum_fusion.1), channel_id=1, source_target_pairs={{0,2},{1,3},{2,0},{3,1},{4,6},{5,7},{6,4},{7,5},{8,10},{9,11},{10,... | collective-permute-start | bytes 1179656 | tf_op jit(solution)/shard_map/ppermute | solution.py:103
  20.2 3.2 %copy-start.3 = (bf16[1,1,128,2048]{3,2,1,0:T(8,128)(2,1)S(1)}, bf16[1,1,128,2048]{3,2,1,0:T(8,128)(2,1)}, u32[]{:S(2)}) copy-start(bf16[1,1,128,2048]{3,2,1,0:T(8,128)(2,1)} %param.9) | copy-start | bytes 1572868
  22.5 9.6 %collective-permute-start.11 = (bf16[2,512,128]{2,1,0:T(8,128)(2,1)S(1)}, bf16[2,512,128]{2,1,0:T(8,128)(2,1)S(1)}, u32[]{:S(2)}, u32[]{:S(2)}) collective-permute-start(bf16[2,512,128]{2,1,0:T(8,128)(2,1)S(1)} %get-tuple-element.76), channel_id=1, source_target_pairs={{0,4},{1,5},{2,6},{3,7},{4,0},{5,1},{6,2},{7,3},{8,12},{9,13},{10,... | collective-permute-start | bytes 786440 | tf_op jit(solution)/shard_map/ppermute | solution.py:103
  22.6 16.7 %collective-permute-start.10 = (bf16[2,512,128]{2,1,0:T(8,128)(2,1)S(1)}, bf16[2,512,128]{2,1,0:T(8,128)(2,1)S(1)}, u32[]{:S(2)}, u32[]{:S(2)}) collective-permute-start(bf16[2,512,128]{2,1,0:T(8,128)(2,1)S(1)} %get-tuple-element.58.refs_0_), channel_id=1, source_target_pairs={{0,2},{1,3},{2,0},{3,1},{4,6},{5,7},{6,4},{7,5},{8,10},{9,11},{10,... | collective-permute-start | bytes 786440 | tf_op jit(solution)/shard_map/ppermute | solution.py:103
  29.9 5.2 %collective-permute-start.6 = (bf16[1,128,768]{2,1,0:T(8,128)(2,1)S(1)}, bf16[1,128,768]{2,1,0:T(8,128)(2,1)S(1)}, u32[]{:S(2)}, u32[]{:S(2)}) collective-permute-start(bf16[1,128,768]{2,1,0:T(8,128)(2,1)S(1)} %get-tuple-element.81), channel_id=1, source_target_pairs={{0,4},{1,5},{2,6},{3,7},{4,0},{5,1},{6,2},{7,3},{8,12},{9,13},{10,... | collective-permute-start | bytes 589832 | tf_op jit(solution)/shard_map/ppermute | solution.py:103
  29.9 9.3 %collective-permute-start.14 = (bf16[1,128,768]{2,1,0:T(8,128)(2,1)S(1)}, bf16[1,128,768]{2,1,0:T(8,128)(2,1)S(1)}, u32[]{:S(2)}, u32[]{:S(2)}) collective-permute-start(bf16[1,128,768]{2,1,0:T(8,128)(2,1)S(1)} %get-tuple-element.80), channel_id=1, source_target_pairs={{0,4},{1,5},{2,6},{3,7},{4,0},{5,1},{6,2},{7,3},{8,12},{9,13},{10,... | collective-permute-start | bytes 589832 | tf_op jit(solution)/shard_map/ppermute | solution.py:103
  32.1 7.2 %collective-permute-start.12 = (bf16[1,512,128]{2,1,0:T(8,128)(2,1)S(1)}, bf16[1,512,128]{2,1,0:T(8,128)(2,1)S(1)}, u32[]{:S(2)}, u32[]{:S(2)}) collective-permute-start(bf16[1,512,128]{2,1,0:T(8,128)(2,1)S(1)} %get-tuple-element.83), channel_id=1, source_target_pairs={{0,2},{1,3},{2,0},{3,1},{4,6},{5,7},{6,4},{7,5},{8,10},{9,11},{10,... | collective-permute-start | bytes 393224 | tf_op jit(solution)/shard_map/ppermute | solution.py:103
  34.4 5.9 %collective-permute-start.13 = (bf16[1,512,128]{2,1,0:T(8,128)(2,1)S(1)}, bf16[1,512,128]{2,1,0:T(8,128)(2,1)S(1)}, u32[]{:S(2)}, u32[]{:S(2)}) collective-permute-start(bf16[1,512,128]{2,1,0:T(8,128)(2,1)S(1)} %get-tuple-element.82), channel_id=1, source_target_pairs={{0,2},{1,3},{2,0},{3,1},{4,6},{5,7},{6,4},{7,5},{8,10},{9,11},{10,... | collective-permute-start | bytes 393224 | tf_op jit(solution)/shard_map/ppermute | solution.py:103
  35.0 21.4 %collective-permute-start.7 = (bf16[2,128,2048]{2,1,0:T(8,128)(2,1)S(1)}, bf16[2,128,2048]{2,1,0:T(8,128)(2,1)S(1)}, u32[]{:S(2)}, u32[]{:S(2)}) collective-permute-start(bf16[2,128,2048]{2,1,0:T(8,128)(2,1)S(1)} %get-tuple-element.47), channel_id=1, source_target_pairs={{0,1},{1,0},{2,3},{3,2},{4,5},{5,4},{6,7},{7,6},{8,9},{9,8},{10,11... | collective-permute-start | bytes 3145736 | tf_op jit(solution)/shard_map/ppermute | solution.py:103
  40.7 2.8 %collective-permute-start.16 = (bf16[1,128,1536]{2,1,0:T(8,128)(2,1)S(1)}, bf16[1,128,1536]{2,1,0:T(8,128)(2,1)S(1)}, u32[]{:S(2)}, u32[]{:S(2)}) collective-permute-start(bf16[1,128,1536]{2,1,0:T(8,128)(2,1)S(1)} %product_mate.1), channel_id=1, source_target_pairs={{0,1},{1,0},{2,3},{3,2},{4,5},{5,4},{6,7},{7,6},{8,9},{9,8},{10,11... | collective-permute-start | bytes 1179656 | tf_op jit(solution)/shard_map/ppermute | solution.py:103
  42.7 4.2 %collective-permute-start.20 = (bf16[1,128,1536]{2,1,0:T(8,128)(2,1)S(1)}, bf16[1,128,1536]{2,1,0:T(8,128)(2,1)S(1)}, u32[]{:S(2)}, u32[]{:S(2)}) collective-permute-start(bf16[1,128,1536]{2,1,0:T(8,128)(2,1)S(1)} %get-tuple-element.63), channel_id=1, source_target_pairs={{0,1},{1,0},{2,3},{3,2},{4,5},{5,4},{6,7},{7,6},{8,9},{9,8},{10,11... | collective-permute-start | bytes 1179656 | tf_op jit(solution)/shard_map/ppermute | solution.py:103
  43.6 10.4 %collective-permute-start.18 = (bf16[128,1536]{1,0:T(8,128)(2,1)S(1)}, bf16[128,1536]{1,0:T(8,128)(2,1)S(1)}, u32[]{:S(2)}, u32[]{:S(2)}) collective-permute-start(bf16[128,1536]{1,0:T(8,128)(2,1)S(1)} %block_sum.3), channel_id=1, source_target_pairs={{0,8},{8,0},{16,24},{24,16},{1,9},{9,1},{17,25},{25,17},{2,10},{10... | collective-permute-start | bytes 1179656 | tf_op jit(solution)/shard_map/ppermute | solution.py:103
  45.5 2.7 %collective-permute-start.17 = (bf16[1,128,1536]{2,1,0:T(8,128)(2,1)S(1)}, bf16[1,128,1536]{2,1,0:T(8,128)(2,1)S(1)}, u32[]{:S(2)}, u32[]{:S(2)}) collective-permute-start(bf16[1,128,1536]{2,1,0:T(8,128)(2,1)S(1)} %get-tuple-element.61), channel_id=1, source_target_pairs={{0,1},{1,0},{2,3},{3,2},{4,5},{5,4},{6,7},{7,6},{8,9},{9,8},{10,11... | collective-permute-start | bytes 1179656 | tf_op jit(solution)/shard_map/ppermute | solution.py:103
  46.8 9.6 %collective-permute-start.15 = (bf16[1,128,1536]{2,1,0:T(8,128)(2,1)S(1)}, bf16[1,128,1536]{2,1,0:T(8,128)(2,1)S(1)}, u32[]{:S(2)}, u32[]{:S(2)}) collective-permute-start(bf16[1,128,1536]{2,1,0:T(8,128)(2,1)S(1)} %get-tuple-element.56), channel_id=1, source_target_pairs={{0,1},{1,0},{2,3},{3,2},{4,5},{5,4},{6,7},{7,6},{8,9},{9,8},{10,11... | collective-permute-start | bytes 1179656 | tf_op jit(solution)/shard_map/ppermute | solution.py:103
  46.9 30.9 %collective-permute-start.8 = (bf16[128,2048]{1,0:T(8,128)(2,1)S(1)}, bf16[128,2048]{1,0:T(8,128)(2,1)S(1)}, u32[]{:S(2)}, u32[]{:S(2)}) collective-permute-start(bf16[128,2048]{1,0:T(8,128)(2,1)S(1)} %get-tuple-element.49), channel_id=1, source_target_pairs={{3,4},{5,6},{2,1},{4,3},{11,12},{13,14},{10,9},{12,11},{19,20},{21... | collective-permute-start | bytes 1572872 | tf_op jit(solution)/shard_map/ppermute | solution.py:457
  48.2 31.2 %collective-permute-start.9 = (bf16[128,2048]{1,0:T(8,128)(2,1)S(1)}, bf16[128,2048]{1,0:T(8,128)(2,1)S(1)}, u32[]{:S(2)}, u32[]{:S(2)}) collective-permute-start(bf16[128,2048]{1,0:T(8,128)(2,1)S(1)} %get-tuple-element.51), channel_id=1, source_target_pairs={{3,4},{5,6},{2,1},{4,3},{11,12},{13,14},{10,9},{12,11},{19,20},{21... | collective-permute-start | bytes 1572872 | tf_op jit(solution)/shard_map/ppermute | solution.py:458
  54.1 19.4 %collective-permute-start.19 = (bf16[128,1536]{1,0:T(8,128)(2,1)S(1)}, bf16[128,1536]{1,0:T(8,128)(2,1)S(1)}, u32[]{:S(2)}, u32[]{:S(2)}) collective-permute-start(bf16[128,1536]{1,0:T(8,128)(2,1)S(1)} %block_sum.4), channel_id=1, source_target_pairs={{0,16},{8,24},{16,0},{24,8},{1,17},{9,25},{17,1},{25,9},{2,18},{10... | collective-permute-start | bytes 1179656 | tf_op jit(solution)/shard_map/ppermute | solution.py:103
  56.5 17.0 %collective-permute-start.21 = (bf16[128,1536]{1,0:T(8,128)(2,1)S(1)}, bf16[128,1536]{1,0:T(8,128)(2,1)S(1)}, u32[]{:S(2)}, u32[]{:S(2)}) collective-permute-start(bf16[128,1536]{1,0:T(8,128)(2,1)S(1)} %block_sum.5), channel_id=1, source_target_pairs={{0,8},{8,0},{16,24},{24,16},{1,9},{9,1},{17,25},{25,17},{2,10},{10... | collective-permute-start | bytes 1179656 | tf_op jit(solution)/shard_map/ppermute | solution.py:103
  74.2 9.8 %collective-permute-start.23 = (bf16[128,384]{1,0:T(8,128)(2,1)S(1)}, bf16[128,384]{1,0:T(8,128)(2,1)S(1)}, u32[]{:S(2)}, u32[]{:S(2)}) collective-permute-start(bf16[128,384]{1,0:T(8,128)(2,1)S(1)} %get-tuple-element.68), channel_id=1, source_target_pairs={{0,1},{1,0},{2,3},{3,2},{4,5},{5,4},{6,7},{7,6},{8,9},{9,8},{10,11... | collective-permute-start | bytes 294920 | tf_op jit(solution)/shard_map/ppermute | solution.py:103
  76.1 7.9 %collective-permute-start.24 = (bf16[128,384]{1,0:T(8,128)(2,1)S(1)}, bf16[128,384]{1,0:T(8,128)(2,1)S(1)}, u32[]{:S(2)}, u32[]{:S(2)}) collective-permute-start(bf16[128,384]{1,0:T(8,128)(2,1)S(1)} %get-tuple-element.69), channel_id=1, source_target_pairs={{0,4},{1,5},{2,6},{3,7},{4,0},{5,1},{6,2},{7,3},{8,12},{9,13},{10,... | collective-permute-start | bytes 294920 | tf_op jit(solution)/shard_map/ppermute | solution.py:103
  77.8 6.2 %collective-permute-start.25 = (bf16[128,384]{1,0:T(8,128)(2,1)S(1)}, bf16[128,384]{1,0:T(8,128)(2,1)S(1)}, u32[]{:S(2)}, u32[]{:S(2)}) collective-permute-start(bf16[128,384]{1,0:T(8,128)(2,1)S(1)} %get-tuple-element.70), channel_id=1, source_target_pairs={{0,5},{1,4},{2,7},{3,6},{4,1},{5,0},{6,3},{7,2},{8,13},{9,12},{10,... | collective-permute-start | bytes 294920 | tf_op jit(solution)/shard_map/ppermute | solution.py:103
  77.8 3.7 %collective-permute-start.22 = (f32[128,128]{1,0:T(8,128)S(1)}, f32[128,128]{1,0:T(8,128)S(1)}, u32[]{:S(2)}, u32[]{:S(2)}) collective-permute-start(f32[128,128]{1,0:T(8,128)S(1)} %get-tuple-element.66.gram), channel_id=1, source_target_pairs={{0,2},{1,3},{2,0},{3,1},{4,6},{5,7},{6,4},{7,5},{8,10},{9,11},{10,... | collective-permute-start | bytes 196616 | tf_op jit(solution)/shard_map/ppermute | solution.py:103
  84.0 2.8 %collective-permute-start.26 = (f32[128,128]{1,0:T(8,128)S(1)}, f32[128,128]{1,0:T(8,128)S(1)}, u32[]{:S(2)}, u32[]{:S(2)}) collective-permute-start(f32[128,128]{1,0:T(8,128)S(1)} %newton_schulz.1.refs_0_), channel_id=1, source_target_pairs={{0,1},{1,0},{2,3},{3,2},{4,5},{5,4},{6,7},{7,6},{8,9},{9,8},{10,11... | collective-permute-start | bytes 196616 | tf_op jit(solution)/shard_map/ppermute | solution.py:103
  85.0 3.7 %collective-permute-start.27 = (f32[128,128]{1,0:T(8,128)S(1)}, f32[128,128]{1,0:T(8,128)S(1)}, u32[]{:S(2)}, u32[]{:S(2)}) collective-permute-start(f32[128,128]{1,0:T(8,128)S(1)} %newton_schulz.1.refs_0_), channel_id=1, source_target_pairs={{0,4},{1,5},{2,6},{3,7},{4,0},{5,1},{6,2},{7,3},{8,12},{9,13},{10,... | collective-permute-start | bytes 196616 | tf_op jit(solution)/shard_map/ppermute | solution.py:103
  86.5 4.0 %collective-permute-start.28 = (f32[128,128]{1,0:T(8,128)S(1)}, f32[128,128]{1,0:T(8,128)S(1)}, u32[]{:S(2)}, u32[]{:S(2)}) collective-permute-start(f32[128,128]{1,0:T(8,128)S(1)} %newton_schulz.1.refs_0_), channel_id=1, source_target_pairs={{0,5},{1,4},{2,7},{3,6},{4,1},{5,0},{6,3},{7,2},{8,13},{9,12},{10,... | collective-permute-start | bytes 196616 | tf_op jit(solution)/shard_map/ppermute | solution.py:103
